TPU v7x, 32 devices: a whole 2x2x4 slice. The times are simulated.
32 devices in a mesh: runs: 2 (over x), xb: 8 (over z, y), yb: 2 (over core).
Axes of the slice: x: 2, y: 2, z: 4, core: 2. Of those that a mesh axis runs over, the one named last changes fastest.
Arguments:
- state: float32 [64, 3, 256, 256], P(('runs', 'xb', 'yb')), parts along dimension 0, may hold values from -12 to 12, as said below
- bed: float32 [64, 256, 256], P(('runs', 'xb', 'yb')), parts along dimension 0, may hold values from 0 to 1.5
- manning: float32 [64, 256, 256], P(('runs', 'xb', 'yb')), parts along dimension 0, may hold values from 0.02 to 0.3
- neighbours: int32 [64, 4], P('runs'), parts along dimension 0, may hold values from -1 to 31, as said below
- wet: int32 [3, 64], P(None, 'runs'), parts along dimension 1, may hold values from 0 to 1
- moves: int32 [3, 32], P(None, 'runs'), parts along dimension 1, may hold values from 0 to 1
Outputs:
- final: float32 [64, 3, 256, 256], P(('runs', 'xb', 'yb')), parts along dimension 0
There are 2 independent parts, one for each index of `runs`. A program takes and returns all parts, laid end to end along the dimension named above; each array names one. Nothing has to cross between parts.
Inputs may be any that keep to these rules, and one draw needn't show every extreme that they name: `state`: component 0 is the depth h, positive; components 1 and 2 are momenta with magnitude below 1.5 h. `neighbours`: the tiles form a grid of 8 by 4 tiles, entries 0 to 3 naming the tile to the west, east, south and north; the device of xb index i and yb index j starts with the 1 by 2 block of x-blocks i * 1 onward and y-blocks j * 2 onward, in any order within it.
All inputs are finite; a program needn't handle non-finite values.
Results may differ from a plain program's by a relative error of at most 0.00002.
Values sent between devices are 32-bit elements; how exact they have to be, the bound alone decides.
No kernel may reach another device: no remote copies, remote signals or barrier semaphores. Data moves between devices by JAX's collectives and lax.ppermute only.
A program may use at most 64 MiB of HBM per device.

v0:
```python
import jax
import jax.numpy as jnp
from jax import lax
from jax.sharding import PartitionSpec as P

STEPS = 3


GRAVITY = 9.81
SPACING = 5.0
COURANT = 0.2
OPPOSITE = (1, 0, 3, 2)
MIRROR = (
    (1.0, -1.0, 1.0, 1.0),
    (1.0, -1.0, 1.0, 1.0),
    (1.0, 1.0, -1.0, 1.0),
    (1.0, 1.0, -1.0, 1.0),
)


def shifted(value, axis, steps):
    count = lax.axis_size(axis)
    pairs = [(source, (source + steps) % count) for source in range(count)]
    return lax.ppermute(value, axis, pairs)


def physical(fields, normal):
    depth = fields[0]
    push_x = fields[1]
    push_y = fields[2]
    vel_x = push_x / depth
    vel_y = push_y / depth
    celerity = jnp.sqrt(GRAVITY * depth)
    pressure = 0.5 * GRAVITY * depth * depth
    if normal == 0:
        flux = jnp.stack([push_x, push_x * vel_x + pressure, push_x * vel_y])
        speed = jnp.abs(vel_x) + celerity
    else:
        flux = jnp.stack([push_y, push_y * vel_x, push_y * vel_y + pressure])
        speed = jnp.abs(vel_y) + celerity
    return (flux, speed)


def sweep(fields, lower, upper, axis, normal):
    extended = jnp.concatenate(
        [jnp.expand_dims(lower, axis + 1), fields, jnp.expand_dims(upper, axis + 1)], axis=axis + 1
    )
    count = extended.shape[axis + 1]
    left = lax.slice_in_dim(extended, 0, count - 1, axis=axis + 1)
    right = lax.slice_in_dim(extended, 1, count, axis=axis + 1)
    flux_left, speed_left = physical(left, normal)
    flux_right, speed_right = physical(right, normal)
    wave = jnp.maximum(speed_left, speed_right)
    face = 0.5 * (flux_left + flux_right) - 0.5 * wave * (right[:3] - left[:3])
    change = lax.slice_in_dim(face, 1, count - 1, axis=axis + 1) - lax.slice_in_dim(
        face, 0, count - 2, axis=axis + 1
    )
    ground = extended[3]
    slope = (
        lax.slice_in_dim(ground, 2, count, axis=axis)
        - lax.slice_in_dim(ground, 0, count - 2, axis=axis)
    ) / (2.0 * SPACING)
    return (change, slope)


def advance(tile, ground, rough, ghost, delta):
    fields = jnp.concatenate([tile, ground[None]], 0)
    change_x, slope_x = sweep(fields, ghost[0], ghost[1], 0, 0)
    change_y, slope_y = sweep(fields, ghost[2], ghost[3], 1, 1)
    ratio = delta / SPACING
    change = change_x + change_y
    depth = tile[0] - ratio * change[0]
    push_x = tile[1] - ratio * change[1] - delta * GRAVITY * tile[0] * slope_x
    push_y = tile[2] - ratio * change[2] - delta * GRAVITY * tile[0] * slope_y
    vel_x = push_x / depth
    vel_y = push_y / depth
    drag = (
        GRAVITY
        * rough
        * rough
        * jnp.sqrt(vel_x * vel_x + vel_y * vel_y)
        / (depth * jnp.cbrt(depth))
    )
    factor = 1.0 / (1.0 + delta * drag)
    return jnp.stack([depth, push_x * factor, push_y * factor])


def fastest_cell(tile):
    depth = tile[0]
    return jnp.max(
        jnp.maximum(jnp.abs(tile[1] / depth), jnp.abs(tile[2] / depth)) + jnp.sqrt(GRAVITY * depth)
    )


def boundary_lines(state, bed):
    planes = [state[:, 0], state[:, 1], state[:, 2], bed]
    west = jnp.stack([plane[:, 0, :] for plane in planes], 1)
    east = jnp.stack([plane[:, -1, :] for plane in planes], 1)
    south = jnp.stack([plane[:, :, 0] for plane in planes], 1)
    north = jnp.stack([plane[:, :, -1] for plane in planes], 1)
    return jnp.stack([west, east, south, north], 1)


def ghost_lines(lines, table, found, valid):
    flat = table.reshape(-1, table.shape[2], table.shape[3])
    facing = found * 4 + jnp.array(OPPOSITE, jnp.int32)[None, :]
    fetched = jnp.take(flat, facing, axis=0)
    mirrored = lines * jnp.array(MIRROR, lines.dtype)[None, :, :, None]
    return jnp.where(valid[:, :, None, None], fetched, mirrored)


def routes(choose, width_x, width_y, local):
    device_rank = jnp.arange(width_x * width_y, dtype=jnp.int32)
    target = (device_rank // width_y + 1) % width_x * width_y + device_rank % width_y
    source = device_rank * local + choose
    arrival = target * local + jnp.take(choose, target)
    return (source, arrival)


def invert_order(held):
    count = held.shape[0]
    ranks = jnp.arange(count, dtype=jnp.int32)
    hit = held[:, None] == ranks[None, :]
    return jnp.sum(jnp.where(hit, ranks[:, None], 0), axis=0)


def assign_slots(base, index, values):
    count = base.shape[0]
    ranks = jnp.arange(count, dtype=jnp.int32)
    hit = index[:, None] == ranks[None, :]
    landed = jnp.any(hit, axis=0)
    picked = jnp.sum(jnp.where(hit, values[:, None], 0), axis=0)
    return jnp.where(landed, picked, base)


def fastest(state, flag_row, owned):
    flags = jnp.take(flag_row, owned)
    speeds = jax.vmap(fastest_cell)(state)
    return lax.pmax(jnp.max(jnp.where(flags > 0, speeds, 0.0)), ("xb", "yb"))


def body(state, bed, manning, neighbours, wet, moves):
    local = state.shape[0]
    width_x = lax.axis_size("xb")
    width_y = lax.axis_size("yb")
    slots = local * width_x * width_y
    column = lax.axis_index("xb")
    device = column * width_y + lax.axis_index("yb")
    held = jnp.arange(slots, dtype=jnp.int32)
    tracked = jnp.arange(slots, dtype=jnp.int32)
    owned = lax.dynamic_slice_in_dim(held, device * local, local)
    top = fastest(state, wet[0], owned)
    for step in range(STEPS):
        delta = COURANT * SPACING / top
        place = invert_order(held)
        lines = boundary_lines(state, bed)
        pair = lax.all_gather(lines, "yb", axis=0, tiled=True)
        reach = step + 1
        pieces = {0: pair}
        for sign in (1, -1):
            moving = pair
            for offset in range(1, reach + 1):
                moving = shifted(moving, "xb", -sign)
                pieces[sign * offset] = moving
        table = jnp.concatenate([pieces[offset] for offset in range(-reach, reach + 1)], 0)
        near = jnp.take(neighbours, owned, axis=0)
        valid = near >= 0
        found_slot = jnp.take(place, jnp.maximum(near, 0))
        owner = found_slot // local
        distance = (owner // width_y - column + width_x) % width_x
        distance = jnp.where(distance > reach, distance - width_x, distance)
        found = ((distance + reach) * width_y + owner % width_y) * local + found_slot % local
        found = jnp.where(valid, found, 0)
        ghosts = ghost_lines(lines, table, found, valid)
        flags = jnp.take(wet[step], owned)
        fresh = jax.vmap(advance, in_axes=(0, 0, 0, 0, None))(state, bed, manning, ghosts, delta)
        state = jnp.where(flags[:, None, None, None] > 0, fresh, state)
        if step + 1 < STEPS:
            source, arrival = routes(moves[step], width_x, width_y, local)
            tracked = assign_slots(tracked, arrival, jnp.take(tracked, source))
            pick = jnp.take(moves[step], device)
            leaving = jnp.concatenate(
                [
                    lax.dynamic_index_in_dim(state, pick, 0, keepdims=False),
                    lax.dynamic_index_in_dim(bed, pick, 0, keepdims=True),
                    lax.dynamic_index_in_dim(manning, pick, 0, keepdims=True),
                ],
                0,
            )
            arriving = shifted(leaving, "xb", 1)
            state = lax.dynamic_update_index_in_dim(state, arriving[:3], pick, 0)
            bed = lax.dynamic_update_index_in_dim(bed, arriving[3], pick, 0)
            manning = lax.dynamic_update_index_in_dim(manning, arriving[4], pick, 0)
            held = tracked
            owned = lax.dynamic_slice_in_dim(held, device * local, local)
            top = fastest(state, wet[step + 1], owned)
    return state


def solution(mesh):
    placed = (
        P(("runs", "xb", "yb"), None, None, None),
        P(("runs", "xb", "yb"), None, None),
        P(("runs", "xb", "yb"), None, None),
        P("runs", None),
        P(None, "runs"),
        P(None, "runs"),
    )
    return jax.shard_map(
        body,
        mesh=mesh,
        in_specs=placed,
        out_specs=P(("runs", "xb", "yb"), None, None, None),
        check_vma=False,
    )
```

profile of v0, /device:TPU:0, one launch (start us, length us, event | category | flops | bytes accessed | tf_op | source)
XLA Modules:
  0.0 297.0 jit_solution(9755070677387082492)
XLA Ops:
  0.7 1.2 copy.261
  2.0 2.1 copy.251
  7.0 2.0 all_gather.9
  8.9 5.9 %collective-permute-start.1 = (f32[4,4,4,256]{3,2,0,1:T(4,128)S(1)}, f32[4,4,4,256]{3,2,0,1:T(4,128)}, u32[]{:S(2)}, u32[]{:S(2)}) collective-permute-start(f32[4,4,4,256]{3,2,0,1:T(4,128)S(1)} %all_gather.9), channel_id=1, source_target_pairs={{0,14},{2,0},{4,2},{6,4},{8,6},{10,8},{12,10},{14,12},{1,15},{3,1}... | collective-permute-start | bytes 196616 | tf_op jit(solution)/shard_map/ppermute | solution.py:24
  28.3 1.3 select_reduce_fusion.6
  29.5 34.0 %pmax.21 = f32[]{:T(128)} all-reduce(f32[]{:T(128)} %get-tuple-element.53), channel_id=1, replica_groups=mesh['runs'=2,'xb'=8,'yb'=2] {'xb','yb'}, use_global_device_ids=true, to_apply=%region_6.10 | all-reduce | flops 1 | bytes 8 | tf_op jit(solution)/shard_map/pmax | solution.py:139
  67.2 1.3 copy.268
  68.6 1.4 copy.267
  70.0 1.5 fusion.48
  81.5 28.5 %collective-permute-done.2 = f32[5,256,256]{1,2,0:T(8,128)} collective-permute-done((f32[5,256,256]{1,2,0:T(8,128)}, f32[5,256,256]{1,2,0:T(8,128)}, u32[]{:S(2)}, u32[]{:S(2)}) %collective-permute-start.2) | collective-permute-done | bytes 1310752 | tf_op jit(solution)/shard_map/ppermute | solution.py:24
  112.2 30.3 %pmax.22 = f32[]{:T(128)} all-reduce(f32[]{:T(128)} %get-tuple-element.44), channel_id=1, replica_groups=mesh['runs'=2,'xb'=8,'yb'=2] {'xb','yb'}, use_global_device_ids=true, to_apply=%region_10.16 | all-reduce | flops 1 | bytes 8 | tf_op jit(solution)/shard_map/pmax | solution.py:139
  155.7 1.9 all_gather.10
  157.6 2.0 collective-permute-start.3
  159.6 5.0 %collective-permute-done.3 = f32[4,4,4,256]{3,2,1,0:T(4,128)S(1)} collective-permute-done((f32[4,4,4,256]{3,2,1,0:T(4,128)S(1)}, f32[4,4,4,256]{3,2,1,0:T(4,128)S(1)}, u32[]{:S(2)}, u32[]{:S(2)}) %collective-permute-start.3) | collective-permute-done | bytes 65568 | tf_op jit(solution)/shard_map/ppermute | solution.py:24
  165.3 4.7 %collective-permute-start.6 = (f32[4,4,4,256]{3,2,1,0:T(4,128)S(1)}, f32[4,4,4,256]{3,2,1,0:T(4,128)S(1)}, u32[]{:S(2)}, u32[]{:S(2)}) collective-permute-start(f32[4,4,4,256]{3,2,1,0:T(4,128)S(1)} %collective-permute-done.5), channel_id=1, source_target_pairs={{0,14},{2,0},{4,2},{6,4},{8,6},{10,8},{12,10},{14,12},{1,15},{3,1}... | collective-permute-start | bytes 196616 | tf_op jit(solution)/shard_map/ppermute | solution.py:24
  170.0 1.5 collective-permute-done.4
  172.7 1.5 gather_fusion.1
  174.4 1.3 copy.295
  175.7 1.4 copy.294
  177.1 1.5 fusion.42
  187.9 31.1 %collective-permute-done.7 = f32[5,256,256]{1,2,0:T(8,128)} collective-permute-done((f32[5,256,256]{1,2,0:T(8,128)}, f32[5,256,256]{1,2,0:T(8,128)}, u32[]{:S(2)}, u32[]{:S(2)}) %collective-permute-start.7) | collective-permute-done | bytes 1310752 | tf_op jit(solution)/shard_map/ppermute | solution.py:24
  229.9 1.9 all_gather.11
  231.8 4.7 %collective-permute-start.11 = (f32[4,4,4,256]{3,2,0,1:T(4,128)S(1)}, f32[4,4,4,256]{3,2,0,1:T(4,128)S(1)}, u32[]{:S(2)}, u32[]{:S(2)}) collective-permute-start(f32[4,4,4,256]{3,2,0,1:T(4,128)S(1)} %all_gather.11), channel_id=1, source_target_pairs={{0,14},{2,0},{4,2},{6,4},{8,6},{10,8},{12,10},{14,12},{1,15},{3,1}... | collective-permute-start | bytes 196616 | tf_op jit(solution)/shard_map/ppermute | solution.py:24
  236.5 2.2 collective-permute-done.8
  239.1 4.7 %collective-permute-start.12 = (f32[4,4,4,256]{3,2,0,1:T(4,128)S(1)}, f32[4,4,4,256]{3,2,0,1:T(4,128)S(1)}, u32[]{:S(2)}, u32[]{:S(2)}) collective-permute-start(f32[4,4,4,256]{3,2,0,1:T(4,128)S(1)} %collective-permute-done.11), channel_id=1, source_target_pairs={{0,14},{2,0},{4,2},{6,4},{8,6},{10,8},{12,10},{14,12},{1,15},{3,1}... | collective-permute-start | bytes 196616 | tf_op jit(solution)/shard_map/ppermute | solution.py:24
  243.8 1.9 collective-permute-done.9
  246.3 32.1 %pmax.23 = f32[]{:T(128)} all-reduce(f32[]{:T(128)} %get-tuple-element.35), channel_id=1, replica_groups=mesh['runs'=2,'xb'=8,'yb'=2] {'xb','yb'}, use_global_device_ids=true, to_apply=%region_14.20 | all-reduce | flops 1 | bytes 8 | tf_op jit(solution)/shard_map/pmax | solution.py:139
  279.5 4.1 %collective-permute-done.13 = f32[4,4,4,256]{3,2,0,1:T(4,128)S(1)} collective-permute-done((f32[4,4,4,256]{3,2,0,1:T(4,128)S(1)}, f32[4,4,4,256]{3,2,0,1:T(4,128)S(1)}, u32[]{:S(2)}, u32[]{:S(2)}) %collective-permute-start.13) | collective-permute-done | bytes 65568 | tf_op jit(solution)/shard_map/ppermute | solution.py:24
  284.4 1.3 copy.319
  285.7 1.4 copy.318
  287.2 1.5 fusion.36
  295.4 1.6 copy.326
  (288 shorter events, 73.3 us)
Async XLA Ops:
  2.0 71.9 %copy-start = (f32[2,256,256]{1,2,0:T(8,128)}, f32[2,256,256]{1,2,0:T(8,128)S(1)}, u32[]{:S(2)}) copy-start(f32[2,256,256]{1,2,0:T(8,128)S(1)} %copy.261) | copy-start | bytes 1572868
  4.3 10.6 %copy-start.22 = (s32[3,16]{1,0:T(4,128)S(1)}, s32[3,16]{1,0:T(4,128)}, u32[]{:S(2)}) copy-start(s32[3,16]{1,0:T(4,128)} %param.27) | copy-start | bytes 580
  6.8 13.4 %copy-start.23 = (s32[3,32]{1,0:T(4,128)S(1)}, s32[3,32]{1,0:T(4,128)}, u32[]{:S(2)}) copy-start(s32[3,32]{1,0:T(4,128)} %param.26) | copy-start | bytes 1156
  6.8 13.5 %copy-start.19 = (s32[32,4]{0,1:T(4,128)S(1)}, s32[32,4]{0,1:T(4,128)}, u32[]{:S(2)}) copy-start(s32[32,4]{0,1:T(4,128)} %param.25) | copy-start | bytes 1540
  8.9 55.9 %collective-permute-start.1 = (f32[4,4,4,256]{3,2,0,1:T(4,128)S(1)}, f32[4,4,4,256]{3,2,0,1:T(4,128)}, u32[]{:S(2)}, u32[]{:S(2)}) collective-permute-start(f32[4,4,4,256]{3,2,0,1:T(4,128)S(1)} %all_gather.9), channel_id=1, source_target_pairs={{0,14},{2,0},{4,2},{6,4},{8,6},{10,8},{12,10},{14,12},{1,15},{3,1}... | collective-permute-start | bytes 196616 | tf_op jit(solution)/shard_map/ppermute | solution.py:24
  14.9 50.0 %collective-permute-start = (f32[4,4,4,256]{3,2,0,1:T(4,128)S(1)}, f32[4,4,4,256]{3,2,0,1:T(4,128)}, u32[]{:S(2)}, u32[]{:S(2)}) collective-permute-start(f32[4,4,4,256]{3,2,0,1:T(4,128)S(1)} %all_gather.9), channel_id=1, source_target_pairs={{0,2},{2,4},{4,6},{6,8},{8,10},{10,12},{12,14},{14,0},{1,3},{3,5},... | collective-permute-start | bytes 196616 | tf_op jit(solution)/shard_map/ppermute | solution.py:24
  20.1 5.7 %copy-start.26 = (s32[4]{0:T(128)S(1)}, s32[4]{0:T(128)}, u32[]{:S(2)}) copy-start(s32[4]{0:T(128)} %constant.353.clone) | copy-start | bytes 52
  20.2 7.0 %copy-start.16 = (f32[2,256,256]{2,1,0:T(8,128)S(1)}, f32[2,256,256]{2,1,0:T(8,128)}, u32[]{:S(2)}) copy-start(f32[2,256,256]{2,1,0:T(8,128)} %param.24) | copy-start | bytes 1572868
  25.0 41.4 %copy-start.18 = (f32[4,4]{1,0:T(4,128)S(1)}, f32[4,4]{1,0:T(4,128)}, u32[]{:S(2)}) copy-start(f32[4,4]{1,0:T(4,128)} %constant.354.clone) | copy-start | bytes 196
  27.5 49.2 %copy-start.4 = (f32[2,256,256]{1,2,0:T(8,128)}, f32[2,256,256]{1,2,0:T(8,128)S(1)}, u32[]{:S(2)}) copy-start(f32[2,256,256]{1,2,0:T(8,128)S(1)} %copy.273) | copy-start | bytes 1572868
  78.2 3.2 %copy-start.25 = (s32[2,4]{1,0:T(2,128)S(1)}, s32[2,4]{1,0:T(2,128)}, u32[]{:S(2)}) copy-start(s32[2,4]{1,0:T(2,128)} %get-tuple-element.203) | copy-start | bytes 100
  80.0 63.2 %copy-start.1 = (f32[2,256,256]{1,2,0:T(8,128)S(1)}, f32[2,256,256]{1,2,0:T(8,128)}, u32[]{:S(2)}) copy-start(f32[2,256,256]{1,2,0:T(8,128)} %copy-done) | copy-start | bytes 1572868
  80.0 63.2 %copy-start.5 = (f32[2,256,256]{1,2,0:T(8,128)S(1)}, f32[2,256,256]{1,2,0:T(8,128)}, u32[]{:S(2)}) copy-start(f32[2,256,256]{1,2,0:T(8,128)} %copy-done.4) | copy-start | bytes 1572868
  80.0 30.0 %collective-permute-start.2 = (f32[5,256,256]{1,2,0:T(8,128)}, f32[5,256,256]{1,2,0:T(8,128)}, u32[]{:S(2)}, u32[]{:S(2)}) collective-permute-start(f32[5,256,256]{1,2,0:T(8,128)} %pad_maximum_fusion.6), channel_id=1, source_target_pairs={{0,2},{2,4},{4,6},{6,8},{8,10},{10,12},{12,14},{14,0},{1,3},{3,5},... | collective-permute-start | bytes 3932168 | tf_op jit(solution)/shard_map/ppermute | solution.py:24
  144.2 36.8 %copy-start.2 = (f32[2,256,256]{1,2,0:T(8,128)}, f32[2,256,256]{1,2,0:T(8,128)S(1)}, u32[]{:S(2)}) copy-start(f32[2,256,256]{1,2,0:T(8,128)S(1)} %get-tuple-element.125) | copy-start | bytes 1572868
  144.2 39.6 %copy-start.6 = (f32[2,256,256]{1,2,0:T(8,128)}, f32[2,256,256]{1,2,0:T(8,128)S(1)}, u32[]{:S(2)}) copy-start(f32[2,256,256]{1,2,0:T(8,128)S(1)} %get-tuple-element.124) | copy-start | bytes 1572868
  148.0 26.3 %copy-start.20 = (pred[2,4]{1,0:T(4,128)(4,1)S(1)}, pred[2,4]{1,0:T(4,128)(4,1)}, u32[]{:S(2)}) copy-start(pred[2,4]{1,0:T(4,128)(4,1)} %get-tuple-element.201) | copy-start | bytes 28
  148.0 26.3 %copy-start.21 = (pred[2,4]{1,0:T(4,128)(4,1)S(1)}, pred[2,4]{1,0:T(4,128)(4,1)}, u32[]{:S(2)}) copy-start(pred[2,4]{1,0:T(4,128)(4,1)} %get-tuple-element.202) | copy-start | bytes 28
  157.5 7.8 %collective-permute-start.5 = (f32[4,4,4,256]{3,2,1,0:T(4,128)S(1)}, f32[4,4,4,256]{3,2,1,0:T(4,128)S(1)}, u32[]{:S(2)}, u32[]{:S(2)}) collective-permute-start(f32[4,4,4,256]{3,2,1,0:T(4,128)S(1)} %all_gather.10), channel_id=1, source_target_pairs={{0,14},{2,0},{4,2},{6,4},{8,6},{10,8},{12,10},{14,12},{1,15},{3,1}... | collective-permute-start | bytes 196616 | tf_op jit(solution)/shard_map/ppermute | solution.py:24
  157.6 7.0 %collective-permute-start.3 = (f32[4,4,4,256]{3,2,1,0:T(4,128)S(1)}, f32[4,4,4,256]{3,2,1,0:T(4,128)S(1)}, u32[]{:S(2)}, u32[]{:S(2)}) collective-permute-start(f32[4,4,4,256]{3,2,1,0:T(4,128)S(1)} %all_gather.10), channel_id=1, source_target_pairs={{0,2},{2,4},{4,6},{6,8},{8,10},{10,12},{12,14},{14,0},{1,3},{3,5},... | collective-permute-start | bytes 196616 | tf_op jit(solution)/shard_map/ppermute | solution.py:24
  164.6 7.0 %collective-permute-start.4 = (f32[4,4,4,256]{3,2,1,0:T(4,128)S(1)}, f32[4,4,4,256]{3,2,1,0:T(4,128)S(1)}, u32[]{:S(2)}, u32[]{:S(2)}) collective-permute-start(f32[4,4,4,256]{3,2,1,0:T(4,128)S(1)} %collective-permute-done.3), channel_id=1, source_target_pairs={{0,2},{2,4},{4,6},{6,8},{8,10},{10,12},{12,14},{14,0},{1,3},{3,5},... | collective-permute-start | bytes 196616 | tf_op jit(solution)/shard_map/ppermute | solution.py:24
  165.3 6.6 %collective-permute-start.6 = (f32[4,4,4,256]{3,2,1,0:T(4,128)S(1)}, f32[4,4,4,256]{3,2,1,0:T(4,128)S(1)}, u32[]{:S(2)}, u32[]{:S(2)}) collective-permute-start(f32[4,4,4,256]{3,2,1,0:T(4,128)S(1)} %collective-permute-done.5), channel_id=1, source_target_pairs={{0,14},{2,0},{4,2},{6,4},{8,6},{10,8},{12,10},{14,12},{1,15},{3,1}... | collective-permute-start | bytes 196616 | tf_op jit(solution)/shard_map/ppermute | solution.py:24
  185.4 2.4 copy-start.24
  185.4 33.6 %copy-start.3 = (f32[2,256,256]{1,2,0:T(8,128)S(1)}, f32[2,256,256]{1,2,0:T(8,128)}, u32[]{:S(2)}) copy-start(f32[2,256,256]{1,2,0:T(8,128)} %copy-done.2) | copy-start | bytes 1572868
  185.4 33.6 %copy-start.7 = (f32[2,256,256]{1,2,0:T(8,128)S(1)}, f32[2,256,256]{1,2,0:T(8,128)}, u32[]{:S(2)}) copy-start(f32[2,256,256]{1,2,0:T(8,128)} %copy-done.6) | copy-start | bytes 1572868
  187.2 31.8 %collective-permute-start.7 = (f32[5,256,256]{1,2,0:T(8,128)}, f32[5,256,256]{1,2,0:T(8,128)}, u32[]{:S(2)}, u32[]{:S(2)}) collective-permute-start(f32[5,256,256]{1,2,0:T(8,128)} %pad_maximum_fusion.7), channel_id=1, source_target_pairs={{0,2},{2,4},{4,6},{6,8},{8,10},{10,12},{12,14},{14,0},{1,3},{3,5},... | collective-permute-start | bytes 3932168 | tf_op jit(solution)/shard_map/ppermute | solution.py:24
  231.8 7.0 %collective-permute-start.8 = (f32[4,4,4,256]{3,2,0,1:T(4,128)S(1)}, f32[4,4,4,256]{3,2,0,1:T(4,128)S(1)}, u32[]{:S(2)}, u32[]{:S(2)}) collective-permute-start(f32[4,4,4,256]{3,2,0,1:T(4,128)S(1)} %all_gather.11), channel_id=1, source_target_pairs={{0,2},{2,4},{4,6},{6,8},{8,10},{10,12},{12,14},{14,0},{1,3},{3,5},... | collective-permute-start | bytes 196616 | tf_op jit(solution)/shard_map/ppermute | solution.py:24
  231.8 7.3 %collective-permute-start.11 = (f32[4,4,4,256]{3,2,0,1:T(4,128)S(1)}, f32[4,4,4,256]{3,2,0,1:T(4,128)S(1)}, u32[]{:S(2)}, u32[]{:S(2)}) collective-permute-start(f32[4,4,4,256]{3,2,0,1:T(4,128)S(1)} %all_gather.11), channel_id=1, source_target_pairs={{0,14},{2,0},{4,2},{6,4},{8,6},{10,8},{12,10},{14,12},{1,15},{3,1}... | collective-permute-start | bytes 196616 | tf_op jit(solution)/shard_map/ppermute | solution.py:24
  238.7 7.0 %collective-permute-start.9 = (f32[4,4,4,256]{3,2,0,1:T(4,128)S(1)}, f32[4,4,4,256]{3,2,0,1:T(4,128)S(1)}, u32[]{:S(2)}, u32[]{:S(2)}) collective-permute-start(f32[4,4,4,256]{3,2,0,1:T(4,128)S(1)} %collective-permute-done.8), channel_id=1, source_target_pairs={{0,2},{2,4},{4,6},{6,8},{8,10},{10,12},{12,14},{14,0},{1,3},{3,5},... | collective-permute-start | bytes 196616 | tf_op jit(solution)/shard_map/ppermute | solution.py:24
  239.1 40.0 %collective-permute-start.12 = (f32[4,4,4,256]{3,2,0,1:T(4,128)S(1)}, f32[4,4,4,256]{3,2,0,1:T(4,128)S(1)}, u32[]{:S(2)}, u32[]{:S(2)}) collective-permute-start(f32[4,4,4,256]{3,2,0,1:T(4,128)S(1)} %collective-permute-done.11), channel_id=1, source_target_pairs={{0,14},{2,0},{4,2},{6,4},{8,6},{10,8},{12,10},{14,12},{1,15},{3,1}... | collective-permute-start | bytes 196616 | tf_op jit(solution)/shard_map/ppermute | solution.py:24
  245.7 33.7 %collective-permute-start.10 = (f32[4,4,4,256]{3,2,0,1:T(4,128)S(1)}, f32[4,4,4,256]{3,2,0,1:T(4,128)S(1)}, u32[]{:S(2)}, u32[]{:S(2)}) collective-permute-start(f32[4,4,4,256]{3,2,0,1:T(4,128)S(1)} %collective-permute-done.9), channel_id=1, source_target_pairs={{0,2},{2,4},{4,6},{6,8},{8,10},{10,12},{12,14},{14,0},{1,3},{3,5},... | collective-permute-start | bytes 196616 | tf_op jit(solution)/shard_map/ppermute | solution.py:24
  279.1 4.5 %collective-permute-start.13 = (f32[4,4,4,256]{3,2,0,1:T(4,128)S(1)}, f32[4,4,4,256]{3,2,0,1:T(4,128)S(1)}, u32[]{:S(2)}, u32[]{:S(2)}) collective-permute-start(f32[4,4,4,256]{3,2,0,1:T(4,128)S(1)} %collective-permute-done.12), channel_id=1, source_target_pairs={{0,14},{2,0},{4,2},{6,4},{8,6},{10,8},{12,10},{14,12},{1,15},{3,1}... | collective-permute-start | bytes 196616 | tf_op jit(solution)/shard_map/ppermute | solution.py:24
  (9 other events, 12.3 us)
where the time goes:
time: 298 us; the launch traced here: 297 us
  blocking collectives  102 us (34%)
  waiting for transfers between devices  74.7 us (25%)
  local copies, waits for them, and re-layouts  59 us (20%)
  other arithmetic  34.2 us (11%)
  starting transfers between devices  22.4 us (8%)
  between operations  4.63 us (2%)
    pmax x3, blocking collectives, fastest(): return lax.pmax(jnp.max(jnp.where(flags > 0, speeds, 0.0)), ('xb', 'yb'))  96.4 us
    ppermute x14, waiting for transfers between devices, shifted(): return lax.ppermute(value, axis, pairs)  74.7 us
    ppermute x14, starting transfers between devices, shifted(): return lax.ppermute(value, axis, pairs)  22.4 us
    slice x22, local copies, waits for them, and re-layouts, boundary_lines(): west = jnp.stack([plane[:, 0, :] for plane in planes], 1)  16.8 us
    unnamed x68, local copies, waits for them, and re-layouts  6.08 us
    slice x11, local copies, waits for them, and re-layouts, boundary_lines(): east = jnp.stack([plane[:, -1, :] for plane in planes], 1)  6.06 us
  transfers between devices with their start and end apart: 14, of which 8 were waited for; matrix products, arithmetic and copies ran while one was open for 6% of the time, Pallas kernels for 0%

commit v1 on v0

v1 whole, which is shorter than its diff:
```python
import functools

import jax
import jax.numpy as jnp
from jax import lax
from jax.experimental import pallas as pl
from jax.experimental.pallas import tpu as pltpu
from jax.sharding import PartitionSpec as P

STEPS = 3
GRAVITY = 9.81
ROOT_G = GRAVITY**0.5
SPACING = 5.0
COURANT = 0.2
ROWS = 32
LANES = 128
TILE = 256
VMEM_BYTES = 24 * 1024 * 1024
SLOT_LOW, WALL_WEST, WALL_EAST, WALL_OUTER, WET, MOVE = 0, 1, 3, 5, 7, 13
CONTROLS = 16


def shifted(value, axis, steps):
    count = lax.axis_size(axis)
    pairs = [(source, (source + steps) % count) for source in range(count)]
    return lax.ppermute(value, axis, pairs)


def cell(h, hu, hv):
    root = lax.rsqrt(h)
    inverse = root * root
    u = hu * inverse
    v = hv * inverse
    celerity = ROOT_G * (h * root)
    pressure = (0.5 * GRAVITY) * (h * h)
    cross = hu * v
    speed_x = jnp.abs(u) + celerity
    speed_y = jnp.abs(v) + celerity
    along_x = (h, hu, hv, hu * u + pressure, cross, speed_x)
    along_y = (h, hv, hu, hv * v + pressure, cross, speed_y)
    return along_x, along_y


def face(left, right):
    wave = jnp.maximum(left[5], right[5])
    return (
        (left[1] + right[1]) - wave * (right[0] - left[0]),
        (left[3] + right[3]) - wave * (right[1] - left[1]),
        (left[4] + right[4]) - wave * (right[2] - left[2]),
    )


def flag(ctl, index):
    return ctl[index] > 0


def slot_of(ctl, position):
    low = ctl[SLOT_LOW]
    return low if position == 0 else 1 - low


def lines_out(ctl, upper, state, bed, west, east, pack):
    for position in range(2):
        slot = slot_of(ctl, position)
        for field in range(4):
            row = position * 4 + field
            if field < 3:
                west[row : row + 1, :] = state[slot, field, 0:1, :]
                east[row : row + 1, :] = state[slot, field, TILE - 1 : TILE, :]
            else:
                west[row : row + 1, :] = bed[slot, 0:1, :]
                east[row : row + 1, :] = bed[slot, TILE - 1 : TILE, :]
    is_upper = upper.astype(jnp.int32)
    slot = jnp.where(upper > 0, ctl[SLOT_LOW], 1 - ctl[SLOT_LOW])
    start = pl.multiple_of((1 - is_upper) * LANES, LANES)
    turn = 1 + is_upper * (LANES - 2)
    lane = lax.broadcasted_iota(jnp.int32, (TILE, LANES), 1)
    group = lax.rem(lane + is_upper, LANES) // 32
    packed = None
    for field in range(4):
        if field < 3:
            block = state[slot, field, :, pl.ds(start, LANES)]
        else:
            block = bed[slot, :, pl.ds(start, LANES)]
        turned = pltpu.roll(block, lax.rem(turn + 32 * field, LANES), 1)
        packed = turned if field == 0 else jnp.where(group == field, turned, packed)
    pack[...] = packed


def opening(state, bed, neighbours, wet, moves, place, west, east, pack, fast, ctl):
    device = place[0]
    upper = place[1]
    first = device * 2
    low = jnp.where(neighbours[first, 3] == first + 1, 0, 1)
    ctl[SLOT_LOW] = low
    for position in range(2):
        slot = low if position == 0 else 1 - low
        tile = first + slot
        ctl[WALL_WEST + position] = (neighbours[tile, 0] < 0).astype(jnp.int32)
        ctl[WALL_EAST + position] = (neighbours[tile, 1] < 0).astype(jnp.int32)
        ctl[WALL_OUTER + position] = (neighbours[tile, 2 + position] < 0).astype(jnp.int32)
        for step in range(STEPS):
            ctl[WET + 2 * step + position] = wet[step, tile]
    for step in range(STEPS):
        ctl[MOVE + step] = moves[step, device]
    lines_out(ctl, upper, state, bed, west, east, pack)

    total = jnp.zeros((ROWS, TILE), jnp.float32)
    for position in range(2):
        slot = slot_of(ctl, position)

        def group(index, best, slot=slot):
            rows = pl.ds(pl.multiple_of(index * ROWS, ROWS), ROWS)
            along_x, along_y = cell(*(state[slot, field, rows, :] for field in range(3)))
            return jnp.maximum(best, jnp.maximum(along_x[5], along_y[5]))

        best = lax.fori_loop(0, TILE // ROWS, group, jnp.zeros((ROWS, TILE), jnp.float32))
        total = jnp.maximum(total, jnp.where(flag(ctl, WET + position), best, 0.0))
    fast[...] = jnp.broadcast_to(jnp.max(total, keepdims=True), fast.shape)


def rates(ctl, state, bed, from_west, from_east, from_pack, rate):
    row_ids = lax.broadcasted_iota(jnp.int32, (ROWS, TILE), 0)
    lane = lax.broadcasted_iota(jnp.int32, (ROWS, LANES), 1)
    last = TILE // ROWS - 1
    for position in range(2):
        slot = slot_of(ctl, position)
        other = 1 - slot
        outer = flag(ctl, WALL_OUTER + position)
        wall_west = flag(ctl, WALL_WEST + position)
        wall_east = flag(ctl, WALL_EAST + position)

        def field_ref(which, field):
            return bed.at[which] if field == 3 else state.at[which, field]

        def ghost_row(received, wall, edge):
            out = []
            for field in range(4):
                own = field_ref(slot, field)[edge : edge + 1, :]
                if field == 1:
                    own = -own
                row = position * 4 + field
                line = jnp.where(wall, own, received[row : row + 1, :])
                out.append(jnp.broadcast_to(line, (8, TILE)))
            return out

        ghost_west = ghost_row(from_west, wall_west, 0)
        ghost_east = ghost_row(from_east, wall_east, TILE - 1)
        first_rows = [field_ref(slot, field)[0:8, :] for field in range(3)]
        left, _ = cell(*ghost_west[:3])
        right, _ = cell(*first_rows)
        start = tuple(part[0:1, :] for part in face(left, right)) + (ghost_west[3][0:1, :],)

        def group(index, carry):
            base = pl.multiple_of(index * ROWS, ROWS)
            rows = pl.ds(base, ROWS)
            after = pl.ds(pl.multiple_of(jnp.minimum(base + ROWS, TILE - 8), 8), 8)
            at_end = index == last
            fields = []
            for field in range(4):
                ref = field_ref(slot, field)
                following = jnp.where(at_end, ghost_east[field], ref[after, :])
                fields.append(jnp.concatenate([ref[rows, :], following], 0))
            cells_x, cells_y = cell(*fields[:3])

            def down(value):
                return pltpu.roll(value, ROWS + 7, 0)[:ROWS]

            here = tuple(value[:ROWS] for value in cells_x)
            faces = face(here, tuple(down(value) for value in cells_x))
            turned = tuple(pltpu.roll(value, 1, 0) for value in faces)
            change_x = tuple(
                value - jnp.where(row_ids == 0, before, moved)
                for value, before, moved in zip(faces, carry[:3], turned)
            )
            ground = fields[3][:ROWS]
            ground_up = pltpu.roll(ground, 1, 0)
            slope_x = down(fields[3]) - jnp.where(row_ids == 0, carry[3], ground_up)
            carried = tuple(value[0:1, :] for value in turned) + (ground_up[0:1, :],)

            inner_lane = LANES - 1 if position == 0 else 0
            inner_cols = slice(0, LANES) if position == 0 else slice(LANES, TILE)
            inner_turn = LANES - 1 if position == 0 else 1
            outer_cols = inner_cols
            packed = from_pack[rows, :]
            ghosts = []
            for field in range(4):
                inner = pltpu.roll(field_ref(other, field)[rows, inner_cols], inner_turn, 1)
                own = fields[field][:ROWS, outer_cols]
                if field == 2:
                    own = -own
                received = packed if field == 0 else pltpu.roll(packed, LANES - 32 * field, 1)
                ghosts.append(
                    jnp.where(lane == inner_lane, inner, jnp.where(outer, own, received))
                )
            _, ghost_y = cell(*ghosts[:3])
            low = tuple(value[:ROWS, :LANES] for value in cells_y)
            high = tuple(value[:ROWS, LANES:] for value in cells_y)

            def right_of(low_part, high_part, ghost_part):
                turned_low = pltpu.roll(low_part, LANES - 1, 1)
                turned_high = pltpu.roll(high_part, LANES - 1, 1)
                return (
                    jnp.where(lane == LANES - 1, turned_high, turned_low),
                    jnp.where(lane == LANES - 1, ghost_part, turned_high),
                )

            pairs = [right_of(a, b, c) for a, b, c in zip(low, high, ghost_y)]
            faces_low = face(low, tuple(pair[0] for pair in pairs))
            faces_high = face(high, tuple(pair[1] for pair in pairs))
            faces_edge = face(ghost_y, low)
            change_y = []
            for a, b, c in zip(faces_low, faces_high, faces_edge):
                turned_a = pltpu.roll(a, 1, 1)
                turned_b = pltpu.roll(b, 1, 1)
                change_y.append(
                    jnp.concatenate(
                        [
                            a - jnp.where(lane == 0, c, turned_a),
                            b - jnp.where(lane == 0, turned_a, turned_b),
                        ],
                        1,
                    )
                )
            ground_low = ground[:, :LANES]
            ground_high = ground[:, LANES:]
            north = right_of(ground_low, ground_high, ghosts[3])
            turned_low = pltpu.roll(ground_low, 1, 1)
            turned_high = pltpu.roll(ground_high, 1, 1)
            slope_y = jnp.concatenate(
                [
                    north[0] - jnp.where(lane == 0, ghosts[3], turned_low),
                    north[1] - jnp.where(lane == 0, turned_low, turned_high),
                ],
                1,
            )
            weight = (GRAVITY / (2.0 * SPACING)) * fields[0][:ROWS]
            scale = 0.5 / SPACING
            rate[slot, 0, rows, :] = scale * (change_x[0] + change_y[0])
            rate[slot, 1, rows, :] = scale * (change_x[1] + change_y[2]) + weight * slope_x
            rate[slot, 2, rows, :] = scale * (change_x[2] + change_y[1]) + weight * slope_y
            return carried

        lax.fori_loop(0, TILE // ROWS, group, start)


def update_tile(ctl, step, position, delta, state, manning, rate, fresh):
    slot = slot_of(ctl, position)
    wet_now = flag(ctl, WET + 2 * step + position)

    def group(index, best):
        rows = pl.ds(pl.multiple_of(index * ROWS, ROWS), ROWS)
        h0, hu0, hv0 = (state[slot, field, rows, :] for field in range(3))
        h = h0 - delta * rate[slot, 0, rows, :]
        hu = hu0 - delta * rate[slot, 1, rows, :]
        hv = hv0 - delta * rate[slot, 2, rows, :]
        rough = manning[slot, rows, :]
        inverse = 1.0 / h
        u = hu * inverse
        v = hv * inverse
        speed = jnp.sqrt(u * u + v * v)
        power = jnp.exp((-4.0 / 3.0) * jnp.log(jnp.abs(h)))
        drag = (GRAVITY * delta) * (rough * rough) * (speed * power)
        factor = 1.0 / (1.0 + drag)
        hu = hu * factor
        hv = hv * factor
        h = jnp.where(wet_now, h, h0)
        hu = jnp.where(wet_now, hu, hu0)
        hv = jnp.where(wet_now, hv, hv0)
        fresh[slot, 0, rows, :] = h
        fresh[slot, 1, rows, :] = hu
        fresh[slot, 2, rows, :] = hv
        if step + 1 < STEPS:
            along_x, along_y = cell(h, hu, hv)
            best = jnp.maximum(best, jnp.maximum(along_x[5], along_y[5]))
        return best

    best = lax.fori_loop(0, TILE // ROWS, group, jnp.zeros((ROWS, TILE), jnp.float32))
    if step + 1 < STEPS:
        best = jnp.where(flag(ctl, WET + 2 * step + 2 + position), best, 0.0)
    return best


def update(step, ctl, place, tops, state, bed, manning, rate, *outs):
    delta = (COURANT * SPACING) / jnp.max(tops[...], keepdims=True)
    fresh = outs[0]
    best = jnp.maximum(
        update_tile(ctl, step, 0, delta, state, manning, rate, fresh),
        update_tile(ctl, step, 1, delta, state, manning, rate, fresh),
    )
    if step + 1 < STEPS:
        _, west, east, pack, fast = outs
        lines_out(ctl, place[1], fresh, bed, west, east, pack)
        fast[...] = jnp.broadcast_to(jnp.max(best, keepdims=True), fast.shape)


def vmem():
    return pl.BlockSpec(memory_space=pltpu.VMEM)


def smem():
    return pl.BlockSpec(memory_space=pltpu.SMEM)


def call(kernel, outs, out_specs, in_specs, flops):
    return pl.pallas_call(
        kernel,
        out_shape=outs,
        in_specs=in_specs,
        out_specs=out_specs,
        compiler_params=pltpu.CompilerParams(vmem_limit_bytes=VMEM_BYTES),
        cost_estimate=pl.CostEstimate(flops=flops, bytes_accessed=4 << 20, transcendentals=0),
    )


def f32(*shape):
    return jax.ShapeDtypeStruct(shape, jnp.float32)


LINES = (f32(8, TILE), f32(8, TILE), f32(TILE, LANES), f32(8, LANES))


def exchange(west, east, pack):
    from_west = shifted(east, "xb", 1)
    from_east = shifted(west, "xb", -1)
    from_pack = shifted(pack, "yb", 1)
    return from_west, from_east, from_pack


def body(state, bed, manning, neighbours, wet, moves):
    width_y = lax.axis_size("yb")
    upper = lax.axis_index("yb")
    device = lax.axis_index("xb") * width_y + upper
    place = jnp.stack([device, upper]).astype(jnp.int32)
    shape = f32(*state.shape)
    west, east, pack, fast, ctl = call(
        opening,
        LINES + (jax.ShapeDtypeStruct((CONTROLS,), jnp.int32),),
        (vmem(),) * 4 + (smem(),),
        [vmem(), vmem(), smem(), smem(), smem(), smem()],
        4 << 20,
    )(state, bed, neighbours, wet, moves, place)
    for step in range(STEPS):
        got = exchange(west, east, pack)
        tops = lax.all_gather(fast, ("xb", "yb"), axis=0, tiled=True)
        rate = call(rates, shape, vmem(), [smem()] + [vmem()] * 5, 16 << 20)(ctl, state, bed, *got)
        more = step + 1 < STEPS
        outs = call(
            functools.partial(update, step),
            (shape,) + LINES if more else (shape,),
            (vmem(),) * (5 if more else 1),
            [smem(), smem()] + [vmem()] * 5,
            8 << 20,
        )(ctl, place, tops, state, bed, manning, rate)
        state = outs[0]
        if more:
            _, west, east, pack, fast = outs
    one, two = ctl[MOVE], ctl[MOVE + 1]
    again = one == two
    leaving = lax.dynamic_index_in_dim(state, one, 0, keepdims=False)
    staying = lax.dynamic_index_in_dim(state, 1 - one, 0, keepdims=False)
    arrived = shifted(leaving, "xb", 1)
    arrived_next = shifted(jnp.where(again, arrived, staying), "xb", 1)
    remains = jnp.where(again, staying, arrived)
    is_first = two == 0
    return jnp.stack(
        [jnp.where(is_first, arrived_next, remains), jnp.where(is_first, remains, arrived_next)]
    )


def solution(mesh):
    placed = (
        P(("runs", "xb", "yb"), None, None, None),
        P(("runs", "xb", "yb"), None, None),
        P(("runs", "xb", "yb"), None, None),
        P("runs", None),
        P(None, "runs"),
        P(None, "runs"),
    )
    return jax.shard_map(
        body,
        mesh=mesh,
        in_specs=placed,
        out_specs=P(("runs", "xb", "yb"), None, None, None),
        check_vma=False,
    )
```

time: 298 us -> 151 us (0.51)
  local copies, waits for them, and re-layouts: 59 us -> 8.72 us
  blocking collectives: 102 us -> 53.7 us
  waiting for transfers between devices: 74.7 us -> 39.6 us
  other arithmetic: 34.2 us -> 3.59 us
  Pallas kernels: 0 us -> 21.5 us
  starting transfers between devices: 22.4 us -> 18.5 us
    pmax x3 -> x0, blocking collectives: 96.4 us -> none  [fastest(): return lax.pmax(jnp.max(jnp.where(flags > 0, speeds, 0.0)), ('xb', 'yb'))]
    all_gather x3, blocking collectives: 5.67 us -> 53.7 us  [body(): tops = lax.all_gather(fast, ('xb', 'yb'), axis=0, tiled=True)]
    ppermute x14 -> x11, waiting for transfers between devices: 74.7 us -> 39.6 us  [shifted(): return lax.ppermute(value, axis, pairs)]
    slice x33 -> x1, local copies, waits for them, and re-layouts: 22.9 us -> 0.65 us  [body(): one, two = (ctl[MOVE], ctl[MOVE + 1])]
    pallas_call x0 -> x7, Pallas kernels: none -> 21.5 us  [the longest x3 14 us: body(): call(rates, shape, vmem(), [smem()] + [vmem()] * 5, 16 << 20)]
    gather x19 -> x0, local copies, waits for them, and re-layouts: 11.6 us -> none  [the longest x3 2.7 us: ghost_lines(): fetched = jnp.take(flat, facing, axis=0)]
    squeeze x22 -> x1, local copies, waits for them, and re-layouts: 8.78 us -> 0.94 us  [body(): leaving = lax.dynamic_index_in_dim(state, one, 0, keepdims=False)]
    concatenate x9 -> x0, other arithmetic: 7.59 us -> none  [the longest x6 4.36 us: sweep(): jnp.concatenate([jnp.expand_dims(lower, axis + 1), fields, jnp.expand_dim...]
  transfers between devices with their start and end apart: 14 -> 11, of which waited for: 8 -> 2; matrix products, arithmetic and copies ran while one was open for 6% -> 0% of each run, Pallas kernels for 0% -> 0%
where the time goes in v1:
time: 151 us
  blocking collectives  53.7 us (36%)
  waiting for transfers between devices  39.6 us (26%)
  Pallas kernels  21.5 us (14%)
  starting transfers between devices  18.5 us (12%)
  local copies, waits for them, and re-layouts  8.72 us (6%)
  between operations  5.12 us (3%)
  other arithmetic  3.59 us (2%)
    all_gather x3, blocking collectives, body(): tops = lax.all_gather(fast, ('xb', 'yb'), axis=0, tiled=True)  53.7 us
    ppermute x11, waiting for transfers between devices, shifted(): return lax.ppermute(value, axis, pairs)  39.6 us
    ppermute x11, starting transfers between devices, shifted(): return lax.ppermute(value, axis, pairs)  18.5 us
    pallas_call x3, Pallas kernels, body(): call(rates, shape, vmem(), [smem()] + [vmem()] * 5, 16 << 20)  14 us
    unnamed x17, local copies, waits for them, and re-layouts  7.13 us
    pallas_call x3, Pallas kernels, body(): call(functools.partial(update, step), (shape,) + LINES if more else (shap...  5.45 us
  transfers between devices with their start and end apart: 11, of which 2 were waited for; matrix products, arithmetic and copies ran while one was open for 0% of the time, Pallas kernels for 0%

profile of v1, /device:TPU:0, one launch (start us, length us, event | category | flops | bytes accessed | tf_op | source)
XLA Modules:
  0.0 150.8 jit_solution(7939988393593004332)
XLA Ops:
  0.0 0.8 copy.7.neighbours
  0.8 1.0 copy-done
  1.9 1.4 copy-done.2
  3.3 0.7 copy-done.6
  4.0 0.7 copy-done.7
  4.7 2.0 %shard_map.64 = (f32[8,256]{1,0:T(8,128)S(1)}, f32[8,256]{1,0:T(8,128)S(1)}, f32[256,128]{1,0:T(8,128)S(1)}, f32[8,128]{1,0:T(8,128)S(1)}, s32[16]{0:T(128)S(1)}) custom-call(f32[2,3,256,256]{3,2,1,0:T(8,128)S(1)} %copy-done.2, f32[2,256,256]{2,1,0:T(8,128)S(1)} %copy-done, s32[32,4]{1,0:T(8,128)S(1)} %copy.7.neighbours, s32[3,32]{1,0:T(4,128)S(1)} %copy-done.6, ...), custom_call_target="tpu_custom_call" | custom-call | flops 4194304 | bytes 4194304 | tf_op jit(solution)/shard_map/pallas_call | solution.py:336
  6.7 0.5 collective-permute-start.2
  7.2 2.6 %collective-permute-start = (f32[8,256]{1,0:T(8,128)S(1)}, f32[8,256]{1,0:T(8,128)S(1)}, u32[]{:S(2)}, u32[]{:S(2)}) collective-permute-start(f32[8,256]{1,0:T(8,128)S(1)} %get-tuple-element.22), channel_id=1, source_target_pairs={{0,2},{2,4},{4,6},{6,8},{8,10},{10,12},{12,14},{14,0},{1,3},{3,5},... | collective-permute-start | bytes 24584 | tf_op jit(solution)/shard_map/ppermute | solution.py:26
  9.8 3.1 %collective-permute-start.1 = (f32[8,256]{1,0:T(8,128)S(1)}, f32[8,256]{1,0:T(8,128)S(1)}, u32[]{:S(2)}, u32[]{:S(2)}) collective-permute-start(f32[8,256]{1,0:T(8,128)S(1)} %get-tuple-element.23), channel_id=1, source_target_pairs={{0,14},{2,0},{4,2},{6,4},{8,6},{10,8},{12,10},{14,12},{1,15},{3,1}... | collective-permute-start | bytes 24584 | tf_op jit(solution)/shard_map/ppermute | solution.py:26
  12.9 19.2 %all_gather.9.tops = f32[128,128]{1,0:T(8,128)S(1)} all-gather(f32[8,128]{1,0:T(8,128)S(1)} %get-tuple-element.21), channel_id=1, replica_groups=mesh['runs'=2,'xb'=8,'yb'=2] {'xb','yb'}, dimensions={0}, use_global_device_ids=true | all-gather | bytes 69632 | tf_op jit(solution)/shard_map/all_gather | solution.py:345
  32.1 4.7 %shard_map.65.rate = f32[2,3,256,256]{3,2,1,0:T(8,128)S(1)} custom-call(s32[16]{0:T(128)S(1)} %get-tuple-element.20.ctl, f32[2,3,256,256]{3,2,1,0:T(8,128)S(1)} %copy-done.2, f32[2,256,256]{2,1,0:T(8,128)S(1)} %copy-done, f32[8,256]{1,0:T(8,128)S(1)} %collective-permute-done.from_west, f32[8,256]{1,0:T(8,128)S(1)} %collective-permute-done.1.from_east, ...), custom_call_target="tpu_custom_call" | custom-call | flops 16777216 | bytes 4194304 | tf_op jit(solution)/shard_map/pallas_call | solution.py:346
  36.8 2.0 %shard_map.66 = (f32[2,3,256,256]{3,2,1,0:T(8,128)S(1)}, f32[8,256]{1,0:T(8,128)S(1)}, f32[8,256]{1,0:T(8,128)S(1)}, f32[256,128]{1,0:T(8,128)S(1)}, f32[8,128]{1,0:T(8,128)S(1)}) custom-call(s32[16]{0:T(128)S(1)} %get-tuple-element.20.ctl, s32[2]{0:T(128)S(1)} %pad_add_fusion.place, f32[128,128]{1,0:T(8,128)S(1)} %all_gather.9.tops, ...), custom_call_target="tpu_custom_call" | custom-call | flops 8388608 | bytes 4194304 | tf_op jit(solution)/shard_map/pallas_call | solution.py:348
  38.8 0.4 collective-permute-start.5
  39.3 4.6 %collective-permute-start.4 = (f32[8,256]{1,0:T(8,128)S(1)}, f32[8,256]{1,0:T(8,128)S(1)}, u32[]{:S(2)}, u32[]{:S(2)}) collective-permute-start(f32[8,256]{1,0:T(8,128)S(1)} %get-tuple-element.28), channel_id=1, source_target_pairs={{0,14},{2,0},{4,2},{6,4},{8,6},{10,8},{12,10},{14,12},{1,15},{3,1}... | collective-permute-start | bytes 24584 | tf_op jit(solution)/shard_map/ppermute | solution.py:26
  43.9 17.3 %all_gather.10.tops = f32[128,128]{1,0:T(8,128)S(1)} all-gather(f32[8,128]{1,0:T(8,128)S(1)} %get-tuple-element.25), channel_id=1, replica_groups=mesh['runs'=2,'xb'=8,'yb'=2] {'xb','yb'}, dimensions={0}, use_global_device_ids=true | all-gather | bytes 69632 | tf_op jit(solution)/shard_map/all_gather | solution.py:345
  61.2 4.7 %shard_map.67.rate = f32[2,3,256,256]{3,2,1,0:T(8,128)S(1)} custom-call(s32[16]{0:T(128)S(1)} %get-tuple-element.20.ctl, f32[2,3,256,256]{3,2,1,0:T(8,128)S(1)} %get-tuple-element.26.state, f32[2,256,256]{2,1,0:T(8,128)S(1)} %copy-done.1, f32[8,256]{1,0:T(8,128)S(1)} %collective-permute-done.3.from_west, f32[8,256]{1,0:T(8,128)S(1)} %collective-permute-done.4.from_east, ...), custom_call_target="tpu_custom_call" | custom-call | flops 16777216 | bytes 4194304 | tf_op jit(solution)/shard_map/pallas_call | solution.py:346
  66.0 2.0 %shard_map.68 = (f32[2,3,256,256]{3,2,1,0:T(8,128)S(1)}, f32[8,256]{1,0:T(8,128)S(1)}, f32[8,256]{1,0:T(8,128)S(1)}, f32[256,128]{1,0:T(8,128)S(1)}, f32[8,128]{1,0:T(8,128)S(1)}) custom-call(s32[16]{0:T(128)S(1)} %get-tuple-element.20.ctl, s32[2]{0:T(128)S(1)} %pad_add_fusion.place, f32[128,128]{1,0:T(8,128)S(1)} %all_gather.10.tops, ...), custom_call_target="tpu_custom_call" | custom-call | flops 8388608 | bytes 4194304 | tf_op jit(solution)/shard_map/pallas_call | solution.py:348
  68.4 0.6 fusion
  70.9 2.0 %collective-permute-start.6 = (f32[8,256]{1,0:T(8,128)S(1)}, f32[8,256]{1,0:T(8,128)S(1)}, u32[]{:S(2)}, u32[]{:S(2)}) collective-permute-start(f32[8,256]{1,0:T(8,128)S(1)} %get-tuple-element.32), channel_id=1, source_target_pairs={{0,2},{2,4},{4,6},{6,8},{8,10},{10,12},{12,14},{14,0},{1,3},{3,5},... | collective-permute-start | bytes 24584 | tf_op jit(solution)/shard_map/ppermute | solution.py:26
  72.9 2.7 %collective-permute-start.7 = (f32[8,256]{1,0:T(8,128)S(1)}, f32[8,256]{1,0:T(8,128)S(1)}, u32[]{:S(2)}, u32[]{:S(2)}) collective-permute-start(f32[8,256]{1,0:T(8,128)S(1)} %get-tuple-element.33), channel_id=1, source_target_pairs={{0,14},{2,0},{4,2},{6,4},{8,6},{10,8},{12,10},{14,12},{1,15},{3,1}... | collective-permute-start | bytes 24584 | tf_op jit(solution)/shard_map/ppermute | solution.py:26
  75.7 17.3 %all_gather.11.tops = f32[128,128]{1,0:T(8,128)S(1)} all-gather(f32[8,128]{1,0:T(8,128)S(1)} %get-tuple-element.30), channel_id=1, replica_groups=mesh['runs'=2,'xb'=8,'yb'=2] {'xb','yb'}, dimensions={0}, use_global_device_ids=true | all-gather | bytes 69632 | tf_op jit(solution)/shard_map/all_gather | solution.py:345
  93.0 4.7 %shard_map.69.rate = f32[2,3,256,256]{3,2,1,0:T(8,128)S(1)} custom-call(s32[16]{0:T(128)S(1)} %get-tuple-element.20.ctl, f32[2,3,256,256]{3,2,1,0:T(8,128)S(1)} %get-tuple-element.31.state, f32[2,256,256]{2,1,0:T(8,128)S(1)} %copy-done.1, f32[8,256]{1,0:T(8,128)S(1)} %collective-permute-done.6.from_west, f32[8,256]{1,0:T(8,128)S(1)} %collective-permute-done.7.from_east, ...), custom_call_target="tpu_custom_call" | custom-call | flops 16777216 | bytes 4194304 | tf_op jit(solution)/shard_map/pallas_call | solution.py:346
  97.6 1.1 copy-done.3
  98.8 1.4 copy-done.4
  100.2 1.5 shard_map.70
  101.7 0.9 dynamic-slice_bitcast_fusion
  102.6 2.0 %collective-permute-start.9 = (f32[3,256,256]{2,1,0:T(8,128)}, f32[3,256,256]{2,1,0:T(8,128)S(1)}, u32[]{:S(2)}, u32[]{:S(2)}) collective-permute-start(f32[3,256,256]{2,1,0:T(8,128)} %dynamic-slice_bitcast_fusion), channel_id=1, source_target_pairs={{0,2},{2,4},{4,6},{6,8},{8,10},{10,12},{12,14},{14,0},{1,3},{3,5},... | collective-permute-start | bytes 2359304 | tf_op jit(solution)/shard_map/ppermute | solution.py:26
  107.1 18.2 %collective-permute-done.9 = f32[3,256,256]{2,1,0:T(8,128)S(1)} collective-permute-done((f32[3,256,256]{2,1,0:T(8,128)}, f32[3,256,256]{2,1,0:T(8,128)S(1)}, u32[]{:S(2)}, u32[]{:S(2)}) %collective-permute-start.9) | collective-permute-done | bytes 786464 | tf_op jit(solution)/shard_map/ppermute | solution.py:26
  125.3 1.0 bitcast_select_fusion.1
  126.9 21.4 %collective-permute-done.10 = f32[3,256,256]{2,1,0:T(8,128)} collective-permute-done((f32[3,256,256]{2,1,0:T(8,128)}, f32[3,256,256]{2,1,0:T(8,128)}, u32[]{:S(2)}, u32[]{:S(2)}) %collective-permute-start.10) | collective-permute-done | bytes 786464 | tf_op jit(solution)/shard_map/ppermute | solution.py:26
  148.3 1.3 select_bitcast_fusion.1
  149.6 1.2 pad_maximum_fusion
  (23 shorter events, 0.6 us)
Async XLA Ops:
  0.8 1.0 copy-start
  1.9 1.4 copy-start.2
  3.3 0.7 copy-start.6
  4.0 0.7 copy-start.7
  6.7 25.4 %collective-permute-start.2 = (f32[256,128]{1,0:T(8,128)S(1)}, f32[256,128]{1,0:T(8,128)S(1)}, u32[]{:S(2)}, u32[]{:S(2)}) collective-permute-start(f32[256,128]{1,0:T(8,128)S(1)} %get-tuple-element.24), channel_id=1, source_target_pairs={{0,1},{1,0},{2,3},{3,2},{4,5},{5,4},{6,7},{7,6},{8,9},{9,8},{10,11... | collective-permute-start | bytes 393224 | tf_op jit(solution)/shard_map/ppermute | solution.py:26
  7.2 24.9 %collective-permute-start = (f32[8,256]{1,0:T(8,128)S(1)}, f32[8,256]{1,0:T(8,128)S(1)}, u32[]{:S(2)}, u32[]{:S(2)}) collective-permute-start(f32[8,256]{1,0:T(8,128)S(1)} %get-tuple-element.22), channel_id=1, source_target_pairs={{0,2},{2,4},{4,6},{6,8},{8,10},{10,12},{12,14},{14,0},{1,3},{3,5},... | collective-permute-start | bytes 24584 | tf_op jit(solution)/shard_map/ppermute | solution.py:26
  9.8 22.3 %collective-permute-start.1 = (f32[8,256]{1,0:T(8,128)S(1)}, f32[8,256]{1,0:T(8,128)S(1)}, u32[]{:S(2)}, u32[]{:S(2)}) collective-permute-start(f32[8,256]{1,0:T(8,128)S(1)} %get-tuple-element.23), channel_id=1, source_target_pairs={{0,14},{2,0},{4,2},{6,4},{8,6},{10,8},{12,10},{14,12},{1,15},{3,1}... | collective-permute-start | bytes 24584 | tf_op jit(solution)/shard_map/ppermute | solution.py:26
  32.1 4.7 %copy-start.5 = (f32[2,256,256]{2,1,0:T(8,128)S(1)}, f32[2,256,256]{2,1,0:T(8,128)}, u32[]{:S(2)}) copy-start(f32[2,256,256]{2,1,0:T(8,128)} %manning.5) | copy-start | bytes 1572868
  36.8 24.4 %copy-start.1 = (f32[2,256,256]{2,1,0:T(8,128)S(1)}, f32[2,256,256]{2,1,0:T(8,128)}, u32[]{:S(2)}) copy-start(f32[2,256,256]{2,1,0:T(8,128)} %bed.13) | copy-start | bytes 1572868
  38.8 22.4 %collective-permute-start.5 = (f32[256,128]{1,0:T(8,128)S(1)}, f32[256,128]{1,0:T(8,128)S(1)}, u32[]{:S(2)}, u32[]{:S(2)}) collective-permute-start(f32[256,128]{1,0:T(8,128)S(1)} %get-tuple-element.29), channel_id=1, source_target_pairs={{0,1},{1,0},{2,3},{3,2},{4,5},{5,4},{6,7},{7,6},{8,9},{9,8},{10,11... | collective-permute-start | bytes 393224 | tf_op jit(solution)/shard_map/ppermute | solution.py:26
  39.2 22.0 %collective-permute-start.3 = (f32[8,256]{1,0:T(8,128)S(1)}, f32[8,256]{1,0:T(8,128)S(1)}, u32[]{:S(2)}, u32[]{:S(2)}) collective-permute-start(f32[8,256]{1,0:T(8,128)S(1)} %get-tuple-element.27), channel_id=1, source_target_pairs={{0,2},{2,4},{4,6},{6,8},{8,10},{10,12},{12,14},{14,0},{1,3},{3,5},... | collective-permute-start | bytes 24584 | tf_op jit(solution)/shard_map/ppermute | solution.py:26
  39.3 21.9 %collective-permute-start.4 = (f32[8,256]{1,0:T(8,128)S(1)}, f32[8,256]{1,0:T(8,128)S(1)}, u32[]{:S(2)}, u32[]{:S(2)}) collective-permute-start(f32[8,256]{1,0:T(8,128)S(1)} %get-tuple-element.28), channel_id=1, source_target_pairs={{0,14},{2,0},{4,2},{6,4},{8,6},{10,8},{12,10},{14,12},{1,15},{3,1}... | collective-permute-start | bytes 24584 | tf_op jit(solution)/shard_map/ppermute | solution.py:26
  67.9 25.0 %collective-permute-start.8 = (f32[256,128]{1,0:T(8,128)S(1)}, f32[256,128]{1,0:T(8,128)S(1)}, u32[]{:S(2)}, u32[]{:S(2)}) collective-permute-start(f32[256,128]{1,0:T(8,128)S(1)} %get-tuple-element.34), channel_id=1, source_target_pairs={{0,1},{1,0},{2,3},{3,2},{4,5},{5,4},{6,7},{7,6},{8,9},{9,8},{10,11... | collective-permute-start | bytes 393224 | tf_op jit(solution)/shard_map/ppermute | solution.py:26
  70.9 22.1 %collective-permute-start.6 = (f32[8,256]{1,0:T(8,128)S(1)}, f32[8,256]{1,0:T(8,128)S(1)}, u32[]{:S(2)}, u32[]{:S(2)}) collective-permute-start(f32[8,256]{1,0:T(8,128)S(1)} %get-tuple-element.32), channel_id=1, source_target_pairs={{0,2},{2,4},{4,6},{6,8},{8,10},{10,12},{12,14},{14,0},{1,3},{3,5},... | collective-permute-start | bytes 24584 | tf_op jit(solution)/shard_map/ppermute | solution.py:26
  72.9 20.0 %collective-permute-start.7 = (f32[8,256]{1,0:T(8,128)S(1)}, f32[8,256]{1,0:T(8,128)S(1)}, u32[]{:S(2)}, u32[]{:S(2)}) collective-permute-start(f32[8,256]{1,0:T(8,128)S(1)} %get-tuple-element.33), channel_id=1, source_target_pairs={{0,14},{2,0},{4,2},{6,4},{8,6},{10,8},{12,10},{14,12},{1,15},{3,1}... | collective-permute-start | bytes 24584 | tf_op jit(solution)/shard_map/ppermute | solution.py:26
  97.6 1.1 copy-start.3
  98.8 1.4 copy-start.4
  102.6 22.7 %collective-permute-start.9 = (f32[3,256,256]{2,1,0:T(8,128)}, f32[3,256,256]{2,1,0:T(8,128)S(1)}, u32[]{:S(2)}, u32[]{:S(2)}) collective-permute-start(f32[3,256,256]{2,1,0:T(8,128)} %dynamic-slice_bitcast_fusion), channel_id=1, source_target_pairs={{0,2},{2,4},{4,6},{6,8},{8,10},{10,12},{12,14},{14,0},{1,3},{3,5},... | collective-permute-start | bytes 2359304 | tf_op jit(solution)/shard_map/ppermute | solution.py:26
  126.3 22.0 %collective-permute-start.10 = (f32[3,256,256]{2,1,0:T(8,128)}, f32[3,256,256]{2,1,0:T(8,128)}, u32[]{:S(2)}, u32[]{:S(2)}) collective-permute-start(f32[3,256,256]{2,1,0:T(8,128)} %bitcast_select_fusion.1), channel_id=1, source_target_pairs={{0,2},{2,4},{4,6},{6,8},{8,10},{10,12},{12,14},{14,0},{1,3},{3,5},... | collective-permute-start | bytes 2359304 | tf_op jit(solution)/shard_map/ppermute | solution.py:26

commit v2 on v1

--- a/solution.py
+++ b/solution.py
@@ -87,9 +87,25 @@
     pack[...] = packed
 
 
-def opening(state, bed, neighbours, wet, moves, place, west, east, pack, fast, ctl):
-    device = place[0]
-    upper = place[1]
+def copy_all(pairs, sems):
+    copies = [pltpu.make_async_copy(src, dst, sems.at[k]) for k, (src, dst) in enumerate(pairs)]
+    for copy in copies:
+        copy.start()
+    return copies
+
+
+def opening(
+    state_in, bed_in, neighbours_in, wet_in, moves_in,
+    west, east, pack, fast, ctl,
+    state, bed, neighbours, wet, moves, sems,
+):
+    small = ((neighbours_in, neighbours), (wet_in, wet), (moves_in, moves))
+    pieces = [(state_in.at[slot], state.at[slot]) for slot in range(2)]
+    copies = copy_all(small + tuple(pieces) + ((bed_in, bed),), sems)
+    upper = lax.axis_index("yb")
+    device = lax.axis_index("xb") * 2 + upper
+    for copy in copies[:3]:
+        copy.wait()
     first = device * 2
     low = jnp.where(neighbours[first, 3] == first + 1, 0, 1)
     ctl[SLOT_LOW] = low
@@ -103,11 +119,10 @@
             ctl[WET + 2 * step + position] = wet[step, tile]
     for step in range(STEPS):
         ctl[MOVE + step] = moves[step, device]
-    lines_out(ctl, upper, state, bed, west, east, pack)
 
     total = jnp.zeros((ROWS, TILE), jnp.float32)
-    for position in range(2):
-        slot = slot_of(ctl, position)
+    for slot in range(2):
+        copies[3 + slot].wait()
 
         def group(index, best, slot=slot):
             rows = pl.ds(pl.multiple_of(index * ROWS, ROWS), ROWS)
@@ -115,8 +130,10 @@
             return jnp.maximum(best, jnp.maximum(along_x[5], along_y[5]))
 
         best = lax.fori_loop(0, TILE // ROWS, group, jnp.zeros((ROWS, TILE), jnp.float32))
-        total = jnp.maximum(total, jnp.where(flag(ctl, WET + position), best, 0.0))
+        total = jnp.maximum(total, jnp.where(wet[0, first + slot] > 0, best, 0.0))
     fast[...] = jnp.broadcast_to(jnp.max(total, keepdims=True), fast.shape)
+    copies[5].wait()
+    lines_out(ctl, upper, state, bed, west, east, pack)
 
 
 def rates(ctl, state, bed, from_west, from_east, from_pack, rate):
@@ -281,7 +298,7 @@
     return best
 
 
-def update(step, ctl, place, tops, state, bed, manning, rate, *outs):
+def update(step, ctl, tops, state, bed, manning, rate, *outs):
     delta = (COURANT * SPACING) / jnp.max(tops[...], keepdims=True)
     fresh = outs[0]
     best = jnp.maximum(
@@ -290,8 +307,46 @@
     )
     if step + 1 < STEPS:
         _, west, east, pack, fast = outs
-        lines_out(ctl, place[1], fresh, bed, west, east, pack)
+        lines_out(ctl, lax.axis_index("yb"), fresh, bed, west, east, pack)
         fast[...] = jnp.broadcast_to(jnp.max(best, keepdims=True), fast.shape)
+    else:
+        outs[1][...] = fresh[ctl[MOVE]]
+
+
+def second_leaving(ctl, state, arrived, leaving, sems):
+    again = ctl[MOVE] == ctl[MOVE + 1]
+
+    @pl.when(again)
+    def _():
+        pltpu.make_async_copy(arrived, leaving, sems.at[0]).start()
+
+    @pl.when(jnp.logical_not(again))
+    def _():
+        pltpu.make_async_copy(state.at[1 - ctl[MOVE]], leaving, sems.at[0]).start()
+
+    pltpu.make_async_copy(arrived, leaving, sems.at[0]).wait()
+
+
+def keep_rest(ctl, state, arrived, out, sems):
+    rest = out.at[1 - ctl[MOVE + 1]]
+    again = ctl[MOVE] == ctl[MOVE + 1]
+
+    @pl.when(again)
+    def _():
+        pltpu.make_async_copy(state.at[1 - ctl[MOVE]], rest, sems.at[0]).start()
+
+    @pl.when(jnp.logical_not(again))
+    def _():
+        pltpu.make_async_copy(arrived, rest, sems.at[0]).start()
+
+    pltpu.make_async_copy(arrived, rest, sems.at[0]).wait()
+
+
+def keep_last(ctl, arrived, before, out, sems):
+    del before
+    copy = pltpu.make_async_copy(arrived, out.at[ctl[MOVE + 1]], sems.at[0])
+    copy.start()
+    copy.wait()
 
 
 def vmem():
@@ -302,9 +357,15 @@
     return pl.BlockSpec(memory_space=pltpu.SMEM)
 
 
-def call(kernel, outs, out_specs, in_specs, flops):
+def anywhere():
+    return pl.BlockSpec(memory_space=pl.ANY)
+
+
+def call(kernel, outs, out_specs, in_specs, flops, scratch=(), aliases=None):
     return pl.pallas_call(
         kernel,
+        scratch_shapes=scratch,
+        input_output_aliases=aliases or {},
         out_shape=outs,
         in_specs=in_specs,
         out_specs=out_specs,
@@ -327,45 +388,63 @@
     return from_west, from_east, from_pack
 
 
+def spread(fast):
+    tops = lax.all_gather(fast, "yb", axis=0, tiled=True)
+    count = lax.axis_size("xb")
+    reach = 1
+    while reach < count:
+        pairs = [[k, k + reach] for k in range(count) if k // reach % 2 == 0]
+        tops = lax.all_gather(tops, "xb", axis=0, axis_index_groups=pairs, tiled=True)
+        reach *= 2
+    return tops
+
+
 def body(state, bed, manning, neighbours, wet, moves):
-    width_y = lax.axis_size("yb")
-    upper = lax.axis_index("yb")
-    device = lax.axis_index("xb") * width_y + upper
-    place = jnp.stack([device, upper]).astype(jnp.int32)
     shape = f32(*state.shape)
+    tile_shape = f32(*state.shape[1:])
+    sem = [pltpu.SemaphoreType.DMA((1,))]
     west, east, pack, fast, ctl = call(
         opening,
         LINES + (jax.ShapeDtypeStruct((CONTROLS,), jnp.int32),),
         (vmem(),) * 4 + (smem(),),
-        [vmem(), vmem(), smem(), smem(), smem(), smem()],
+        [anywhere()] * 5,
         4 << 20,
-    )(state, bed, neighbours, wet, moves, place)
+        [
+            pltpu.VMEM(state.shape, jnp.float32),
+            pltpu.VMEM(bed.shape, jnp.float32),
+            pltpu.SMEM(neighbours.shape, jnp.int32),
+            pltpu.SMEM(wet.shape, jnp.int32),
+            pltpu.SMEM(moves.shape, jnp.int32),
+            pltpu.SemaphoreType.DMA((6,)),
+        ],
+    )(state, bed, neighbours, wet, moves)
     for step in range(STEPS):
         got = exchange(west, east, pack)
-        tops = lax.all_gather(fast, ("xb", "yb"), axis=0, tiled=True)
+        tops = spread(fast)
         rate = call(rates, shape, vmem(), [smem()] + [vmem()] * 5, 16 << 20)(ctl, state, bed, *got)
         more = step + 1 < STEPS
+        extra = LINES if more else (tile_shape,)
         outs = call(
             functools.partial(update, step),
-            (shape,) + LINES if more else (shape,),
-            (vmem(),) * (5 if more else 1),
-            [smem(), smem()] + [vmem()] * 5,
+            (shape,) + extra,
+            (vmem(),) * (1 + len(extra)),
+            [smem()] + [vmem()] * 5,
             8 << 20,
-        )(ctl, place, tops, state, bed, manning, rate)
+        )(ctl, tops, state, bed, manning, rate)
         state = outs[0]
         if more:
             _, west, east, pack, fast = outs
-    one, two = ctl[MOVE], ctl[MOVE + 1]
-    again = one == two
-    leaving = lax.dynamic_index_in_dim(state, one, 0, keepdims=False)
-    staying = lax.dynamic_index_in_dim(state, 1 - one, 0, keepdims=False)
-    arrived = shifted(leaving, "xb", 1)
-    arrived_next = shifted(jnp.where(again, arrived, staying), "xb", 1)
-    remains = jnp.where(again, staying, arrived)
-    is_first = two == 0
-    return jnp.stack(
-        [jnp.where(is_first, arrived_next, remains), jnp.where(is_first, remains, arrived_next)]
-    )
+    arrived = shifted(outs[1], "xb", 1)
+    leaving = call(
+        second_leaving, tile_shape, anywhere(), [smem(), anywhere(), anywhere()], 1 << 20, sem
+    )(ctl, state, arrived)
+    arrived_next = shifted(leaving, "xb", 1)
+    final = call(
+        keep_rest, shape, anywhere(), [smem(), anywhere(), anywhere()], 1 << 20, sem
+    )(ctl, state, arrived)
+    return call(
+        keep_last, shape, anywhere(), [smem(), anywhere(), anywhere()], 1 << 20, sem, {2: 0}
+    )(ctl, arrived_next, final)
 
 
 def solution(mesh):

time: 151 us -> 130 us (0.86)
  blocking collectives: 53.7 us -> 48 us
  between operations: 5.12 us -> 0.17 us
  local copies, waits for them, and re-layouts: 8.72 us -> 4.58 us
  waiting for transfers between devices: 39.6 us -> 35.5 us
  Pallas kernels: 21.5 us -> 25.2 us
  other arithmetic: 3.59 us -> 0 us
  starting transfers between devices: 18.5 us -> 16 us
    all_gather x3 -> x12, blocking collectives: 53.7 us -> 48 us  [the longest x9 42.7 us: spread(): lax.all_gather(tops, 'xb', axis=0, axis_index_groups=pairs, tiled=True)]
    ppermute x11, waiting for transfers between devices: 39.6 us -> 35.5 us  [shifted(): return lax.ppermute(value, axis, pairs)]
    pallas_call x3 -> x6, Pallas kernels: 5.45 us -> 8.95 us  [the longest x3 5.46 us: body(): call(functools.partial(update, step), (shape,) + extra, (vmem(),) * (1 +...]
    another operation x3 -> x0, other arithmetic: 2.61 us -> none  [the longest x2 2.53 us: body(): jnp.stack([jnp.where(is_first, arrived_next, remains), jnp.where(is_first...]
    unnamed x17 -> x13, local copies, waits for them, and re-layouts: 7.13 us -> 4.58 us
    ppermute x11, starting transfers between devices: 18.5 us -> 16 us  [shifted(): return lax.ppermute(value, axis, pairs)]
  transfers between devices with their start and end apart: 11 -> 11, of which waited for: 2 -> 2; matrix products, arithmetic and copies ran while one was open for 0% -> 0% of each run, Pallas kernels for 0% -> 1%
where the time goes in v2:
time: 130 us
  blocking collectives  48 us (37%)
  waiting for transfers between devices  35.5 us (27%)
  Pallas kernels  25.2 us (19%)
  starting transfers between devices  16 us (12%)
  local copies, waits for them, and re-layouts  4.58 us (4%)
    all_gather x9, blocking collectives, spread(): lax.all_gather(tops, 'xb', axis=0, axis_index_groups=pairs, tiled=True)  42.7 us
    ppermute x11, waiting for transfers between devices, shifted(): return lax.ppermute(value, axis, pairs)  35.5 us
    ppermute x11, starting transfers between devices, shifted(): return lax.ppermute(value, axis, pairs)  16 us
    pallas_call x3, Pallas kernels, body(): call(rates, shape, vmem(), [smem()] + [vmem()] * 5, 16 << 20)  14.1 us
    pallas_call x3, Pallas kernels, body(): call(functools.partial(update, step), (shape,) + extra, (vmem(),) * (1 +...  5.46 us
    all_gather x3, blocking collectives, spread(): tops = lax.all_gather(fast, 'yb', axis=0, tiled=True)  5.35 us
    unnamed x13, local copies, waits for them, and re-layouts  4.58 us
  transfers between devices with their start and end apart: 11, of which 2 were waited for; matrix products, arithmetic and copies ran while one was open for 0% of the time, Pallas kernels for 1%

profile of v2, /device:TPU:0, one launch (start us, length us, event | category | flops | bytes accessed | tf_op | source)
XLA Modules:
  0.0 129.5 jit_solution(15301732405733701723)
XLA Ops:
  0.0 0.8 copy.8.neighbours_in
  0.8 1.0 copy-done
  1.8 1.4 %copy-done.2 = f32[2,3,256,256]{3,2,1,0:T(8,128)S(1)} copy-done((f32[2,3,256,256]{3,2,1,0:T(8,128)S(1)}, f32[2,3,256,256]{3,2,1,0:T(8,128)}, u32[]{:S(2)}) %copy-start.2) | copy-done | bytes 1572888
  3.2 0.7 copy-done.4
  3.9 0.7 copy-done.5
  4.6 2.1 %shard_map.64 = (f32[8,256]{1,0:T(8,128)S(1)}, f32[8,256]{1,0:T(8,128)S(1)}, f32[256,128]{1,0:T(8,128)S(1)}, f32[8,128]{1,0:T(8,128)S(1)}, s32[16]{0:T(128)S(1)}) custom-call(f32[2,3,256,256]{3,2,1,0:T(8,128)S(1)} %copy-done.2, f32[2,256,256]{2,1,0:T(8,128)S(1)} %copy-done, s32[32,4]{1,0:T(8,128)S(1)} %copy.8.neighbours_in, s32[3,32]{1,0:T(4,128)S(1)} %copy-done.4, ...), custom_call_target="tpu_custom_call" | custom-call | flops 4194304 | bytes 4194304 | tf_op jit(solution)/shard_map/pallas_call | solution.py:406
  7.2 2.6 %collective-permute-start = (f32[8,256]{1,0:T(8,128)S(1)}, f32[8,256]{1,0:T(8,128)S(1)}, u32[]{:S(2)}, u32[]{:S(2)}) collective-permute-start(f32[8,256]{1,0:T(8,128)S(1)} %get-tuple-element.24), channel_id=1, source_target_pairs={{0,2},{2,4},{4,6},{6,8},{8,10},{10,12},{12,14},{14,0},{1,3},{3,5},... | collective-permute-start | bytes 24584 | tf_op jit(solution)/shard_map/ppermute | solution.py:26
  9.8 3.1 %collective-permute-start.1 = (f32[8,256]{1,0:T(8,128)S(1)}, f32[8,256]{1,0:T(8,128)S(1)}, u32[]{:S(2)}, u32[]{:S(2)}) collective-permute-start(f32[8,256]{1,0:T(8,128)S(1)} %get-tuple-element.25), channel_id=1, source_target_pairs={{0,14},{2,0},{4,2},{6,4},{8,6},{10,8},{12,10},{14,12},{1,15},{3,1}... | collective-permute-start | bytes 24584 | tf_op jit(solution)/shard_map/ppermute | solution.py:26
  12.9 1.8 %all_gather.36 = f32[16,128]{1,0:T(8,128)S(1)} all-gather(f32[8,128]{1,0:T(8,128)S(1)} %get-tuple-element.23), channel_id=1, replica_groups=mesh['runs'=2,'xb'=8,'yb'=2] {'yb'}, dimensions={0}, use_global_device_ids=true | all-gather | bytes 12288 | tf_op jit(solution)/shard_map/all_gather | solution.py:392
  14.7 4.4 %all_gather.37 = f32[32,128]{1,0:T(8,128)S(1)} all-gather(f32[16,128]{1,0:T(8,128)S(1)} %all_gather.36), channel_id=1, replica_groups={{0,2},{4,6},{8,10},{12,14},{1,3},{5,7},{9,11},{13,15},{16,18},{20,22},{..., dimensions={0}, use_global_device_ids=true | all-gather | bytes 24576 | tf_op jit(solution)/shard_map/all_gather | solution.py:397
  19.1 4.4 %all_gather.38 = f32[64,128]{1,0:T(8,128)S(1)} all-gather(f32[32,128]{1,0:T(8,128)S(1)} %all_gather.37), channel_id=1, replica_groups={{0,4},{2,6},{8,12},{10,14},{1,5},{3,7},{9,13},{11,15},{16,20},{18,22},{..., dimensions={0}, use_global_device_ids=true | all-gather | bytes 49152 | tf_op jit(solution)/shard_map/all_gather | solution.py:397
  23.5 5.5 %all_gather.39.tops = f32[128,128]{1,0:T(8,128)S(1)} all-gather(f32[64,128]{1,0:T(8,128)S(1)} %all_gather.38), channel_id=1, replica_groups={{0,8},{2,10},{4,12},{6,14},{1,9},{3,11},{5,13},{7,15},{16,24},{18,26},{..., dimensions={0}, use_global_device_ids=true | all-gather | bytes 98304 | tf_op jit(solution)/shard_map/all_gather | solution.py:397
  29.0 4.7 %shard_map.65.rate = f32[2,3,256,256]{3,2,1,0:T(8,128)S(1)} custom-call(s32[16]{0:T(128)S(1)} %get-tuple-element.22.ctl, f32[2,3,256,256]{3,2,1,0:T(8,128)S(1)} %copy-done.2, f32[2,256,256]{2,1,0:T(8,128)S(1)} %copy-done, f32[8,256]{1,0:T(8,128)S(1)} %collective-permute-done.from_west, f32[8,256]{1,0:T(8,128)S(1)} %collective-permute-done.1.from_east, ...), custom_call_target="tpu_custom_call" | custom-call | flops 16777216 | bytes 4194304 | tf_op jit(solution)/shard_map/pallas_call | solution.py:424
  33.7 2.0 %shard_map.66 = (f32[2,3,256,256]{3,2,1,0:T(8,128)S(1)}, f32[8,256]{1,0:T(8,128)S(1)}, f32[8,256]{1,0:T(8,128)S(1)}, f32[256,128]{1,0:T(8,128)S(1)}, f32[8,128]{1,0:T(8,128)S(1)}) custom-call(s32[16]{0:T(128)S(1)} %get-tuple-element.22.ctl, f32[128,128]{1,0:T(8,128)S(1)} %all_gather.39.tops, f32[2,3,256,256]{3,2,1,0:T(8,128)S(1)} %copy-done.2, ...), custom_call_target="tpu_custom_call" | custom-call | flops 8388608 | bytes 4194304 | tf_op jit(solution)/shard_map/pallas_call | solution.py:427
  36.1 4.5 %collective-permute-start.4 = (f32[8,256]{1,0:T(8,128)S(1)}, f32[8,256]{1,0:T(8,128)S(1)}, u32[]{:S(2)}, u32[]{:S(2)}) collective-permute-start(f32[8,256]{1,0:T(8,128)S(1)} %get-tuple-element.30), channel_id=1, source_target_pairs={{0,14},{2,0},{4,2},{6,4},{8,6},{10,8},{12,10},{14,12},{1,15},{3,1}... | collective-permute-start | bytes 24584 | tf_op jit(solution)/shard_map/ppermute | solution.py:26
  40.5 1.8 %all_gather.40 = f32[16,128]{1,0:T(8,128)S(1)} all-gather(f32[8,128]{1,0:T(8,128)S(1)} %get-tuple-element.27), channel_id=1, replica_groups=mesh['runs'=2,'xb'=8,'yb'=2] {'yb'}, dimensions={0}, use_global_device_ids=true | all-gather | bytes 12288 | tf_op jit(solution)/shard_map/all_gather | solution.py:392
  42.3 4.4 %all_gather.41 = f32[32,128]{1,0:T(8,128)S(1)} all-gather(f32[16,128]{1,0:T(8,128)S(1)} %all_gather.40), channel_id=1, replica_groups={{0,2},{4,6},{8,10},{12,14},{1,3},{5,7},{9,11},{13,15},{16,18},{20,22},{..., dimensions={0}, use_global_device_ids=true | all-gather | bytes 24576 | tf_op jit(solution)/shard_map/all_gather | solution.py:397
  46.6 4.4 %all_gather.42 = f32[64,128]{1,0:T(8,128)S(1)} all-gather(f32[32,128]{1,0:T(8,128)S(1)} %all_gather.41), channel_id=1, replica_groups={{0,4},{2,6},{8,12},{10,14},{1,5},{3,7},{9,13},{11,15},{16,20},{18,22},{..., dimensions={0}, use_global_device_ids=true | all-gather | bytes 49152 | tf_op jit(solution)/shard_map/all_gather | solution.py:397
  51.1 5.5 %all_gather.43.tops = f32[128,128]{1,0:T(8,128)S(1)} all-gather(f32[64,128]{1,0:T(8,128)S(1)} %all_gather.42), channel_id=1, replica_groups={{0,8},{2,10},{4,12},{6,14},{1,9},{3,11},{5,13},{7,15},{16,24},{18,26},{..., dimensions={0}, use_global_device_ids=true | all-gather | bytes 98304 | tf_op jit(solution)/shard_map/all_gather | solution.py:397
  56.6 4.7 %shard_map.67.rate = f32[2,3,256,256]{3,2,1,0:T(8,128)S(1)} custom-call(s32[16]{0:T(128)S(1)} %get-tuple-element.22.ctl, f32[2,3,256,256]{3,2,1,0:T(8,128)S(1)} %get-tuple-element.28.state, f32[2,256,256]{2,1,0:T(8,128)S(1)} %copy-done.1, f32[8,256]{1,0:T(8,128)S(1)} %collective-permute-done.3.from_west, f32[8,256]{1,0:T(8,128)S(1)} %collective-permute-done.4.from_east, ...), custom_call_target="tpu_custom_call" | custom-call | flops 16777216 | bytes 4194304 | tf_op jit(solution)/shard_map/pallas_call | solution.py:424
  61.3 2.0 %shard_map.68 = (f32[2,3,256,256]{3,2,1,0:T(8,128)S(1)}, f32[8,256]{1,0:T(8,128)S(1)}, f32[8,256]{1,0:T(8,128)S(1)}, f32[256,128]{1,0:T(8,128)S(1)}, f32[8,128]{1,0:T(8,128)S(1)}) custom-call(s32[16]{0:T(128)S(1)} %get-tuple-element.22.ctl, f32[128,128]{1,0:T(8,128)S(1)} %all_gather.43.tops, f32[2,3,256,256]{3,2,1,0:T(8,128)S(1)} %get-tuple-element.28.state, ...), custom_call_target="tpu_custom_call" | custom-call | flops 8388608 | bytes 4194304 | tf_op jit(solution)/shard_map/pallas_call | solution.py:427
  63.4 4.7 %collective-permute-start.7 = (f32[8,256]{1,0:T(8,128)S(1)}, f32[8,256]{1,0:T(8,128)S(1)}, u32[]{:S(2)}, u32[]{:S(2)}) collective-permute-start(f32[8,256]{1,0:T(8,128)S(1)} %get-tuple-element.35), channel_id=1, source_target_pairs={{0,14},{2,0},{4,2},{6,4},{8,6},{10,8},{12,10},{14,12},{1,15},{3,1}... | collective-permute-start | bytes 24584 | tf_op jit(solution)/shard_map/ppermute | solution.py:26
  68.1 1.8 %all_gather.44 = f32[16,128]{1,0:T(8,128)S(1)} all-gather(f32[8,128]{1,0:T(8,128)S(1)} %get-tuple-element.32), channel_id=1, replica_groups=mesh['runs'=2,'xb'=8,'yb'=2] {'yb'}, dimensions={0}, use_global_device_ids=true | all-gather | bytes 12288 | tf_op jit(solution)/shard_map/all_gather | solution.py:392
  69.9 4.4 %all_gather.45 = f32[32,128]{1,0:T(8,128)S(1)} all-gather(f32[16,128]{1,0:T(8,128)S(1)} %all_gather.44), channel_id=1, replica_groups={{0,2},{4,6},{8,10},{12,14},{1,3},{5,7},{9,11},{13,15},{16,18},{20,22},{..., dimensions={0}, use_global_device_ids=true | all-gather | bytes 24576 | tf_op jit(solution)/shard_map/all_gather | solution.py:397
  74.2 4.4 %all_gather.46 = f32[64,128]{1,0:T(8,128)S(1)} all-gather(f32[32,128]{1,0:T(8,128)S(1)} %all_gather.45), channel_id=1, replica_groups={{0,4},{2,6},{8,12},{10,14},{1,5},{3,7},{9,13},{11,15},{16,20},{18,22},{..., dimensions={0}, use_global_device_ids=true | all-gather | bytes 49152 | tf_op jit(solution)/shard_map/all_gather | solution.py:397
  78.6 5.5 %all_gather.47.tops = f32[128,128]{1,0:T(8,128)S(1)} all-gather(f32[64,128]{1,0:T(8,128)S(1)} %all_gather.46), channel_id=1, replica_groups={{0,8},{2,10},{4,12},{6,14},{1,9},{3,11},{5,13},{7,15},{16,24},{18,26},{..., dimensions={0}, use_global_device_ids=true | all-gather | bytes 98304 | tf_op jit(solution)/shard_map/all_gather | solution.py:397
  84.1 4.7 %shard_map.69.rate = f32[2,3,256,256]{3,2,1,0:T(8,128)S(1)} custom-call(s32[16]{0:T(128)S(1)} %get-tuple-element.22.ctl, f32[2,3,256,256]{3,2,1,0:T(8,128)S(1)} %get-tuple-element.33.state, f32[2,256,256]{2,1,0:T(8,128)S(1)} %copy-done.1, f32[8,256]{1,0:T(8,128)S(1)} %collective-permute-done.6.from_west, f32[8,256]{1,0:T(8,128)S(1)} %collective-permute-done.7.from_east, ...), custom_call_target="tpu_custom_call" | custom-call | flops 16777216 | bytes 4194304 | tf_op jit(solution)/shard_map/pallas_call | solution.py:424
  88.8 1.5 %shard_map.70 = (f32[2,3,256,256]{3,2,1,0:T(8,128)S(1)}, f32[3,256,256]{2,1,0:T(8,128)S(1)}) custom-call(s32[16]{0:T(128)S(1)} %get-tuple-element.22.ctl, f32[128,128]{1,0:T(8,128)S(1)} %all_gather.47.tops, f32[2,3,256,256]{3,2,1,0:T(8,128)S(1)} %get-tuple-element.33.state, f32[2,256,256]{2,1,0:T(8,128)S(1)} %copy-done.1, f32[2,256,256]{2,1,0:T(8,128)S(1)} %copy-done.3, ...), custom_call_target="tpu_custom_call" | custom-call | flops 8388608 | bytes 4194304 | tf_op jit(solution)/shard_map/pallas_call | solution.py:427
  90.5 18.9 %collective-permute-done.9.arrived = f32[3,256,256]{2,1,0:T(8,128)S(1)} collective-permute-done((f32[3,256,256]{2,1,0:T(8,128)S(1)}, f32[3,256,256]{2,1,0:T(8,128)S(1)}, u32[]{:S(2)}, u32[]{:S(2)}) %collective-permute-start.9) | collective-permute-done | bytes 786464 | tf_op jit(solution)/shard_map/ppermute | solution.py:26
  110.1 1.4 %shard_map.72.before = f32[2,3,256,256]{3,2,1,0:T(8,128)} custom-call(s32[16]{0:T(128)S(1)} %get-tuple-element.22.ctl, f32[2,3,256,256]{3,2,1,0:T(8,128)S(1)} %get-tuple-element.37.state, f32[3,256,256]{2,1,0:T(8,128)S(1)} %collective-permute-done.9.arrived), custom_call_target="tpu_custom_call" | custom-call | flops 1048576 | bytes 4194304 | tf_op jit(solution)/shard_map/pallas_call | solution.py:442
  111.5 16.6 %collective-permute-done.10.arrived = f32[3,256,256]{2,1,0:T(8,128)S(1)} collective-permute-done((f32[3,256,256]{2,1,0:T(8,128)S(1)}, f32[3,256,256]{2,1,0:T(8,128)S(1)}, u32[]{:S(2)}, u32[]{:S(2)}) %collective-permute-start.10) | collective-permute-done | bytes 786464 | tf_op jit(solution)/shard_map/ppermute | solution.py:26
  128.1 1.4 %shard_map.73 = f32[2,3,256,256]{3,2,1,0:T(8,128)} custom-call(s32[16]{0:T(128)S(1)} %get-tuple-element.22.ctl, f32[3,256,256]{2,1,0:T(8,128)S(1)} %collective-permute-done.10.arrived, f32[2,3,256,256]{3,2,1,0:T(8,128)} %shard_map.72.before), custom_call_target="tpu_custom_call", output_to_operand_aliasing={{}: (2, {})} | custom-call | flops 1048576 | bytes 4194304 | tf_op jit(solution)/shard_map/pallas_call | solution.py:445
  (25 shorter events, 1.8 us)
Async XLA Ops:
  0.8 1.0 copy-start
  1.8 1.4 %copy-start.2 = (f32[2,3,256,256]{3,2,1,0:T(8,128)S(1)}, f32[2,3,256,256]{3,2,1,0:T(8,128)}, u32[]{:S(2)}) copy-start(f32[2,3,256,256]{3,2,1,0:T(8,128)} %state.3) | copy-start | bytes 4718596
  3.2 0.7 copy-start.4
  3.9 0.7 copy-start.5
  6.7 22.2 %collective-permute-start.2 = (f32[256,128]{1,0:T(8,128)S(1)}, f32[256,128]{1,0:T(8,128)S(1)}, u32[]{:S(2)}, u32[]{:S(2)}) collective-permute-start(f32[256,128]{1,0:T(8,128)S(1)} %get-tuple-element.26), channel_id=1, source_target_pairs={{0,1},{1,0},{2,3},{3,2},{4,5},{5,4},{6,7},{7,6},{8,9},{9,8},{10,11... | collective-permute-start | bytes 393224 | tf_op jit(solution)/shard_map/ppermute | solution.py:26
  7.2 21.7 %collective-permute-start = (f32[8,256]{1,0:T(8,128)S(1)}, f32[8,256]{1,0:T(8,128)S(1)}, u32[]{:S(2)}, u32[]{:S(2)}) collective-permute-start(f32[8,256]{1,0:T(8,128)S(1)} %get-tuple-element.24), channel_id=1, source_target_pairs={{0,2},{2,4},{4,6},{6,8},{8,10},{10,12},{12,14},{14,0},{1,3},{3,5},... | collective-permute-start | bytes 24584 | tf_op jit(solution)/shard_map/ppermute | solution.py:26
  9.8 19.1 %collective-permute-start.1 = (f32[8,256]{1,0:T(8,128)S(1)}, f32[8,256]{1,0:T(8,128)S(1)}, u32[]{:S(2)}, u32[]{:S(2)}) collective-permute-start(f32[8,256]{1,0:T(8,128)S(1)} %get-tuple-element.25), channel_id=1, source_target_pairs={{0,14},{2,0},{4,2},{6,4},{8,6},{10,8},{12,10},{14,12},{1,15},{3,1}... | collective-permute-start | bytes 24584 | tf_op jit(solution)/shard_map/ppermute | solution.py:26
  29.0 4.7 %copy-start.3 = (f32[2,256,256]{2,1,0:T(8,128)S(1)}, f32[2,256,256]{2,1,0:T(8,128)}, u32[]{:S(2)}) copy-start(f32[2,256,256]{2,1,0:T(8,128)} %manning.5) | copy-start | bytes 1572868
  33.7 22.9 %copy-start.1 = (f32[2,256,256]{2,1,0:T(8,128)S(1)}, f32[2,256,256]{2,1,0:T(8,128)}, u32[]{:S(2)}) copy-start(f32[2,256,256]{2,1,0:T(8,128)} %bed.11) | copy-start | bytes 1572868
  35.7 20.9 %collective-permute-start.5 = (f32[256,128]{1,0:T(8,128)S(1)}, f32[256,128]{1,0:T(8,128)S(1)}, u32[]{:S(2)}, u32[]{:S(2)}) collective-permute-start(f32[256,128]{1,0:T(8,128)S(1)} %get-tuple-element.31), channel_id=1, source_target_pairs={{0,1},{1,0},{2,3},{3,2},{4,5},{5,4},{6,7},{7,6},{8,9},{9,8},{10,11... | collective-permute-start | bytes 393224 | tf_op jit(solution)/shard_map/ppermute | solution.py:26
  35.7 20.8 %collective-permute-start.3 = (f32[8,256]{1,0:T(8,128)S(1)}, f32[8,256]{1,0:T(8,128)S(1)}, u32[]{:S(2)}, u32[]{:S(2)}) collective-permute-start(f32[8,256]{1,0:T(8,128)S(1)} %get-tuple-element.29), channel_id=1, source_target_pairs={{0,2},{2,4},{4,6},{6,8},{8,10},{10,12},{12,14},{14,0},{1,3},{3,5},... | collective-permute-start | bytes 24584 | tf_op jit(solution)/shard_map/ppermute | solution.py:26
  36.1 20.5 %collective-permute-start.4 = (f32[8,256]{1,0:T(8,128)S(1)}, f32[8,256]{1,0:T(8,128)S(1)}, u32[]{:S(2)}, u32[]{:S(2)}) collective-permute-start(f32[8,256]{1,0:T(8,128)S(1)} %get-tuple-element.30), channel_id=1, source_target_pairs={{0,14},{2,0},{4,2},{6,4},{8,6},{10,8},{12,10},{14,12},{1,15},{3,1}... | collective-permute-start | bytes 24584 | tf_op jit(solution)/shard_map/ppermute | solution.py:26
  63.2 20.9 %collective-permute-start.8 = (f32[256,128]{1,0:T(8,128)S(1)}, f32[256,128]{1,0:T(8,128)S(1)}, u32[]{:S(2)}, u32[]{:S(2)}) collective-permute-start(f32[256,128]{1,0:T(8,128)S(1)} %get-tuple-element.36), channel_id=1, source_target_pairs={{0,1},{1,0},{2,3},{3,2},{4,5},{5,4},{6,7},{7,6},{8,9},{9,8},{10,11... | collective-permute-start | bytes 393224 | tf_op jit(solution)/shard_map/ppermute | solution.py:26
  63.3 20.8 %collective-permute-start.6 = (f32[8,256]{1,0:T(8,128)S(1)}, f32[8,256]{1,0:T(8,128)S(1)}, u32[]{:S(2)}, u32[]{:S(2)}) collective-permute-start(f32[8,256]{1,0:T(8,128)S(1)} %get-tuple-element.34), channel_id=1, source_target_pairs={{0,2},{2,4},{4,6},{6,8},{8,10},{10,12},{12,14},{14,0},{1,3},{3,5},... | collective-permute-start | bytes 24584 | tf_op jit(solution)/shard_map/ppermute | solution.py:26
  63.4 20.7 %collective-permute-start.7 = (f32[8,256]{1,0:T(8,128)S(1)}, f32[8,256]{1,0:T(8,128)S(1)}, u32[]{:S(2)}, u32[]{:S(2)}) collective-permute-start(f32[8,256]{1,0:T(8,128)S(1)} %get-tuple-element.35), channel_id=1, source_target_pairs={{0,14},{2,0},{4,2},{6,4},{8,6},{10,8},{12,10},{14,12},{1,15},{3,1}... | collective-permute-start | bytes 24584 | tf_op jit(solution)/shard_map/ppermute | solution.py:26
  90.4 19.0 %collective-permute-start.9 = (f32[3,256,256]{2,1,0:T(8,128)S(1)}, f32[3,256,256]{2,1,0:T(8,128)S(1)}, u32[]{:S(2)}, u32[]{:S(2)}) collective-permute-start(f32[3,256,256]{2,1,0:T(8,128)S(1)} %get-tuple-element.38), channel_id=1, source_target_pairs={{0,2},{2,4},{4,6},{6,8},{8,10},{10,12},{12,14},{14,0},{1,3},{3,5},... | collective-permute-start | bytes 2359304 | tf_op jit(solution)/shard_map/ppermute | solution.py:26
  110.0 18.1 %collective-permute-start.10 = (f32[3,256,256]{2,1,0:T(8,128)S(1)}, f32[3,256,256]{2,1,0:T(8,128)S(1)}, u32[]{:S(2)}, u32[]{:S(2)}) collective-permute-start(f32[3,256,256]{2,1,0:T(8,128)S(1)} %shard_map.71), channel_id=1, source_target_pairs={{0,2},{2,4},{4,6},{6,8},{8,10},{10,12},{12,14},{14,0},{1,3},{3,5},... | collective-permute-start | bytes 2359304 | tf_op jit(solution)/shard_map/ppermute | solution.py:26

commit v3 on v2

--- a/solution.py
+++ b/solution.py
@@ -20,9 +20,11 @@
 CONTROLS = 16
 
 
-def shifted(value, axis, steps):
+def shifted(value, axis, steps, around=True):
     count = lax.axis_size(axis)
     pairs = [(source, (source + steps) % count) for source in range(count)]
+    if not around:
+        pairs = [pair for pair in pairs if abs(pair[0] - pair[1]) == abs(steps)]
     return lax.ppermute(value, axis, pairs)
 
 
@@ -378,34 +380,30 @@
     return jax.ShapeDtypeStruct(shape, jnp.float32)
 
 
-LINES = (f32(8, TILE), f32(8, TILE), f32(TILE, LANES), f32(8, LANES))
+def line_shapes():
+    devices = lax.axis_size("xb") * lax.axis_size("yb")
+    return f32(8, TILE), f32(8, TILE), f32(TILE, LANES), f32(8 * devices, LANES)
 
 
 def exchange(west, east, pack):
-    from_west = shifted(east, "xb", 1)
-    from_east = shifted(west, "xb", -1)
+    from_west = shifted(east, "xb", 1, False)
+    from_east = shifted(west, "xb", -1, False)
     from_pack = shifted(pack, "yb", 1)
     return from_west, from_east, from_pack
 
 
 def spread(fast):
-    tops = lax.all_gather(fast, "yb", axis=0, tiled=True)
-    count = lax.axis_size("xb")
-    reach = 1
-    while reach < count:
-        pairs = [[k, k + reach] for k in range(count) if k // reach % 2 == 0]
-        tops = lax.all_gather(tops, "xb", axis=0, axis_index_groups=pairs, tiled=True)
-        reach *= 2
-    return tops
+    return lax.all_to_all(fast, ("xb", "yb"), split_axis=0, concat_axis=0, tiled=True)
 
 
 def body(state, bed, manning, neighbours, wet, moves):
     shape = f32(*state.shape)
     tile_shape = f32(*state.shape[1:])
+    lines = line_shapes()
     sem = [pltpu.SemaphoreType.DMA((1,))]
     west, east, pack, fast, ctl = call(
         opening,
-        LINES + (jax.ShapeDtypeStruct((CONTROLS,), jnp.int32),),
+        lines + (jax.ShapeDtypeStruct((CONTROLS,), jnp.int32),),
         (vmem(),) * 4 + (smem(),),
         [anywhere()] * 5,
         4 << 20,
@@ -423,7 +421,7 @@
         tops = spread(fast)
         rate = call(rates, shape, vmem(), [smem()] + [vmem()] * 5, 16 << 20)(ctl, state, bed, *got)
         more = step + 1 < STEPS
-        extra = LINES if more else (tile_shape,)
+        extra = lines if more else (tile_shape,)
         outs = call(
             functools.partial(update, step),
             (shape,) + extra,

time: 130 us -> 131 us (level)
  blocking collectives: 48 us -> 0 us
  starting transfers between devices: 16 us -> 36.7 us
  waiting for transfers between devices: 35.5 us -> 49.7 us
  local copies, waits for them, and re-layouts: 4.58 us -> 17.4 us
    all_gather x12 -> x0, blocking collectives: 48 us -> none  [the longest x9 42.7 us: spread(): lax.all_gather(tops, 'xb', axis=0, axis_index_groups=pairs, tiled=True)]
    all_to_all x0 -> x3, starting transfers between devices: none -> 18.4 us  [spread(): lax.all_to_all(fast, ('xb', 'yb'), split_axis=0, concat_axis=0, tiled=True)]
    ppermute x11, waiting for transfers between devices: 35.5 us -> 49.7 us  [shifted(): return lax.ppermute(value, axis, pairs)]
    unnamed x13 -> x39, local copies, waits for them, and re-layouts: 4.58 us -> 17.4 us
    ppermute x11, starting transfers between devices: 16 us -> 18.3 us  [shifted(): return lax.ppermute(value, axis, pairs)]
  transfers between devices with their start and end apart: 11 -> 14, of which waited for: 2 -> 5; matrix products, arithmetic and copies ran while one was open for 0% -> 0% of each run, Pallas kernels for 1% -> 12%
where the time goes in v3:
time: 131 us; the launch traced here: 130 us
  waiting for transfers between devices  49.7 us (38%)
  starting transfers between devices  36.7 us (28%)
  Pallas kernels  26.4 us (20%)
  local copies, waits for them, and re-layouts  17.4 us (13%)
    ppermute x11, waiting for transfers between devices, shifted(): return lax.ppermute(value, axis, pairs)  49.7 us
    all_to_all x3, starting transfers between devices, spread(): lax.all_to_all(fast, ('xb', 'yb'), split_axis=0, concat_axis=0, tiled=True)  18.4 us
    ppermute x11, starting transfers between devices, shifted(): return lax.ppermute(value, axis, pairs)  18.3 us
    unnamed x39, local copies, waits for them, and re-layouts  17.4 us
    pallas_call x3, Pallas kernels, body(): call(rates, shape, vmem(), [smem()] + [vmem()] * 5, 16 << 20)  14.1 us
    pallas_call x3, Pallas kernels, body(): call(functools.partial(update, step), (shape,) + extra, (vmem(),) * (1 +...  6.64 us
  transfers between devices with their start and end apart: 14, of which 5 were waited for; matrix products, arithmetic and copies ran while one was open for 0% of the time, Pallas kernels for 12%

profile of v3, /device:TPU:0, one launch (start us, length us, event | category | flops | bytes accessed | tf_op | source)
XLA Modules:
  0.0 130.4 jit_solution(7676169116286192025)
XLA Ops:
  1.8 1.4 %copy-done.2 = f32[2,3,256,256]{3,2,1,0:T(8,128)S(1)} copy-done((f32[2,3,256,256]{3,2,1,0:T(8,128)S(1)}, f32[2,3,256,256]{3,2,1,0:T(8,128)}, u32[]{:S(2)}) %copy-start.2) | copy-done | bytes 1572888
  4.6 2.2 %shard_map.64 = (f32[8,256]{1,0:T(8,128)S(1)}, f32[8,256]{1,0:T(8,128)S(1)}, f32[256,128]{1,0:T(8,128)S(1)}, f32[128,128]{1,0:T(8,128)}, s32[16]{0:T(128)S(1)}) custom-call(f32[2,3,256,256]{3,2,1,0:T(8,128)S(1)} %copy-done.2, f32[2,256,256]{2,1,0:T(8,128)S(1)} %copy-done, s32[32,4]{1,0:T(8,128)S(1)} %copy.8.neighbours_in, s32[3,32]{1,0:T(4,128)S(1)} %copy-done.17, ...), custom_call_target="tpu_custom_call" | custom-call | flops 4194304 | bytes 4194304 | tf_op jit(solution)/shard_map/pallas_call | solution.py:404
  7.3 7.0 %all-to-all-start = ((f32[16,8,128]{2,1,0:T(8,128)}), f32[16,8,128]{2,1,0:T(8,128)S(1)}, u32[]{:S(2)}, u32[]{:S(2)}) async-start(f32[16,8,128]{2,1,0:T(8,128)} %bitcast), calls=%async_computation | async-start | bytes 131072 | tf_op jit(solution)/shard_map/all_to_all | solution.py:396
  14.3 3.8 %collective-permute-start = (f32[8,256]{1,0:T(8,128)S(1)}, f32[8,256]{1,0:T(8,128)S(1)}, u32[]{:S(2)}, u32[]{:S(2)}) collective-permute-start(f32[8,256]{1,0:T(8,128)S(1)} %get-tuple-element.24), channel_id=1, source_target_pairs={{0,2},{2,4},{4,6},{6,8},{8,10},{10,12},{12,14},{1,3},{3,5},{5,7},{... | collective-permute-start | bytes 24584 | tf_op jit(solution)/shard_map/ppermute | solution.py:28
  18.2 1.3 collective-permute-start.1
  19.5 4.2 %collective-permute-done.1.from_east = f32[8,256]{1,0:T(8,128)S(1)} collective-permute-done((f32[8,256]{1,0:T(8,128)S(1)}, f32[8,256]{1,0:T(8,128)S(1)}, u32[]{:S(2)}, u32[]{:S(2)}) %collective-permute-start.1) | collective-permute-done | bytes 8224 | tf_op jit(solution)/shard_map/ppermute | solution.py:28
  23.7 4.7 %shard_map.65.rate = f32[2,3,256,256]{3,2,1,0:T(8,128)S(1)} custom-call(s32[16]{0:T(128)S(1)} %get-tuple-element.22.ctl, f32[2,3,256,256]{3,2,1,0:T(8,128)S(1)} %copy-done.3, f32[2,256,256]{2,1,0:T(8,128)S(1)} %copy-done.1, f32[8,256]{1,0:T(8,128)S(1)} %collective-permute-done.from_west, f32[8,256]{1,0:T(8,128)S(1)} %collective-permute-done.1.from_east, ...), custom_call_target="tpu_custom_call" | custom-call | flops 16777216 | bytes 4194304 | tf_op jit(solution)/shard_map/pallas_call | solution.py:422
  29.6 1.4 %copy-done.13 = f32[2,3,256,256]{3,2,1,0:T(8,128)S(1)} copy-done((f32[2,3,256,256]{3,2,1,0:T(8,128)S(1)}, f32[2,3,256,256]{3,2,1,0:T(8,128)}, u32[]{:S(2)}) %copy-start.13) | copy-done | bytes 1572888
  31.0 2.6 %shard_map.66 = (f32[2,3,256,256]{3,2,1,0:T(8,128)S(1)}, f32[8,256]{1,0:T(8,128)S(1)}, f32[8,256]{1,0:T(8,128)S(1)}, f32[256,128]{1,0:T(8,128)S(1)}, f32[128,128]{1,0:T(8,128)}) custom-call(s32[16]{0:T(128)S(1)} %get-tuple-element.22.ctl, f32[128,128]{1,0:T(8,128)S(1)} %bitcast.7, f32[2,3,256,256]{3,2,1,0:T(8,128)S(1)} %copy-done.3, ...), custom_call_target="tpu_custom_call" | custom-call | flops 8388608 | bytes 4194304 | tf_op jit(solution)/shard_map/pallas_call | solution.py:425
  34.7 5.7 %all-to-all-start.1 = ((f32[16,8,128]{2,1,0:T(8,128)}), f32[16,8,128]{2,1,0:T(8,128)S(1)}, u32[]{:S(2)}, u32[]{:S(2)}) async-start(f32[16,8,128]{2,1,0:T(8,128)} %bitcast.2), calls=%async_computation.1 | async-start | bytes 131072 | tf_op jit(solution)/shard_map/all_to_all | solution.py:396
  40.3 3.8 %collective-permute-start.3 = (f32[8,256]{1,0:T(8,128)S(1)}, f32[8,256]{1,0:T(8,128)S(1)}, u32[]{:S(2)}, u32[]{:S(2)}) collective-permute-start(f32[8,256]{1,0:T(8,128)S(1)} %get-tuple-element.29), channel_id=1, source_target_pairs={{0,2},{2,4},{4,6},{6,8},{8,10},{10,12},{12,14},{1,3},{3,5},{5,7},{... | collective-permute-start | bytes 24584 | tf_op jit(solution)/shard_map/ppermute | solution.py:28
  44.2 1.3 collective-permute-start.4
  45.5 4.2 %collective-permute-done.4.from_east = f32[8,256]{1,0:T(8,128)S(1)} collective-permute-done((f32[8,256]{1,0:T(8,128)S(1)}, f32[8,256]{1,0:T(8,128)S(1)}, u32[]{:S(2)}, u32[]{:S(2)}) %collective-permute-start.4) | collective-permute-done | bytes 8224 | tf_op jit(solution)/shard_map/ppermute | solution.py:28
  49.7 1.4 %copy-done.5 = f32[2,3,256,256]{3,2,1,0:T(8,128)S(1)} copy-done((f32[2,3,256,256]{3,2,1,0:T(8,128)S(1)}, f32[2,3,256,256]{3,2,1,0:T(8,128)}, u32[]{:S(2)}) %copy-start.5) | copy-done | bytes 1572888
  51.1 4.7 %shard_map.67.rate = f32[2,3,256,256]{3,2,1,0:T(8,128)S(1)} custom-call(s32[16]{0:T(128)S(1)} %get-tuple-element.22.ctl, f32[2,3,256,256]{3,2,1,0:T(8,128)S(1)} %copy-done.5, f32[2,256,256]{2,1,0:T(8,128)S(1)} %copy-done.1, f32[8,256]{1,0:T(8,128)S(1)} %collective-permute-done.3.from_west, f32[8,256]{1,0:T(8,128)S(1)} %collective-permute-done.4.from_east, ...), custom_call_target="tpu_custom_call" | custom-call | flops 16777216 | bytes 4194304 | tf_op jit(solution)/shard_map/pallas_call | solution.py:422
  55.8 1.2 copy-done.10
  57.0 1.4 %copy-done.11 = f32[2,3,256,256]{3,2,1,0:T(8,128)S(1)} copy-done((f32[2,3,256,256]{3,2,1,0:T(8,128)S(1)}, f32[2,3,256,256]{3,2,1,0:T(8,128)}, u32[]{:S(2)}) %copy-start.11) | copy-done | bytes 1572888
  58.4 2.6 %shard_map.68 = (f32[2,3,256,256]{3,2,1,0:T(8,128)S(1)}, f32[8,256]{1,0:T(8,128)S(1)}, f32[8,256]{1,0:T(8,128)S(1)}, f32[256,128]{1,0:T(8,128)S(1)}, f32[128,128]{1,0:T(8,128)}) custom-call(s32[16]{0:T(128)S(1)} %get-tuple-element.22.ctl, f32[128,128]{1,0:T(8,128)S(1)} %bitcast.6, f32[2,3,256,256]{3,2,1,0:T(8,128)S(1)} %copy-done.6, ...), custom_call_target="tpu_custom_call" | custom-call | flops 8388608 | bytes 4194304 | tf_op jit(solution)/shard_map/pallas_call | solution.py:425
  62.1 5.7 %all-to-all-start.2 = ((f32[16,8,128]{2,1,0:T(8,128)}), f32[16,8,128]{2,1,0:T(8,128)S(1)}, u32[]{:S(2)}, u32[]{:S(2)}) async-start(f32[16,8,128]{2,1,0:T(8,128)} %bitcast.4), calls=%async_computation.2 | async-start | bytes 131072 | tf_op jit(solution)/shard_map/all_to_all | solution.py:396
  67.8 3.8 %collective-permute-start.6 = (f32[8,256]{1,0:T(8,128)S(1)}, f32[8,256]{1,0:T(8,128)S(1)}, u32[]{:S(2)}, u32[]{:S(2)}) collective-permute-start(f32[8,256]{1,0:T(8,128)S(1)} %get-tuple-element.34), channel_id=1, source_target_pairs={{0,2},{2,4},{4,6},{6,8},{8,10},{10,12},{12,14},{1,3},{3,5},{5,7},{... | collective-permute-start | bytes 24584 | tf_op jit(solution)/shard_map/ppermute | solution.py:28
  71.6 1.3 collective-permute-start.7
  73.0 4.2 %collective-permute-done.7.from_east = f32[8,256]{1,0:T(8,128)S(1)} collective-permute-done((f32[8,256]{1,0:T(8,128)S(1)}, f32[8,256]{1,0:T(8,128)S(1)}, u32[]{:S(2)}, u32[]{:S(2)}) %collective-permute-start.7) | collective-permute-done | bytes 8224 | tf_op jit(solution)/shard_map/ppermute | solution.py:28
  77.2 1.4 %copy-done.8 = f32[2,3,256,256]{3,2,1,0:T(8,128)S(1)} copy-done((f32[2,3,256,256]{3,2,1,0:T(8,128)S(1)}, f32[2,3,256,256]{3,2,1,0:T(8,128)}, u32[]{:S(2)}) %copy-start.8) | copy-done | bytes 1572888
  78.6 4.7 %shard_map.69.rate = f32[2,3,256,256]{3,2,1,0:T(8,128)S(1)} custom-call(s32[16]{0:T(128)S(1)} %get-tuple-element.22.ctl, f32[2,3,256,256]{3,2,1,0:T(8,128)S(1)} %copy-done.8, f32[2,256,256]{2,1,0:T(8,128)S(1)} %copy-done.1, f32[8,256]{1,0:T(8,128)S(1)} %collective-permute-done.6.from_west, f32[8,256]{1,0:T(8,128)S(1)} %collective-permute-done.7.from_east, ...), custom_call_target="tpu_custom_call" | custom-call | flops 16777216 | bytes 4194304 | tf_op jit(solution)/shard_map/pallas_call | solution.py:422
  83.3 1.2 copy-done.14
  84.5 1.4 %copy-done.15 = f32[2,3,256,256]{3,2,1,0:T(8,128)S(1)} copy-done((f32[2,3,256,256]{3,2,1,0:T(8,128)S(1)}, f32[2,3,256,256]{3,2,1,0:T(8,128)}, u32[]{:S(2)}) %copy-start.15) | copy-done | bytes 1572888
  85.9 1.5 %shard_map.70 = (f32[2,3,256,256]{3,2,1,0:T(8,128)S(1)}, f32[3,256,256]{2,1,0:T(8,128)S(1)}) custom-call(s32[16]{0:T(128)S(1)} %get-tuple-element.22.ctl, f32[128,128]{1,0:T(8,128)S(1)} %bitcast.8, f32[2,3,256,256]{3,2,1,0:T(8,128)S(1)} %copy-done.9, f32[2,256,256]{2,1,0:T(8,128)S(1)} %copy-done.1, f32[2,256,256]{2,1,0:T(8,128)S(1)} %copy-done.16, ...), custom_call_target="tpu_custom_call" | custom-call | flops 8388608 | bytes 4194304 | tf_op jit(solution)/shard_map/pallas_call | solution.py:425
  87.5 2.4 %collective-permute-start.9 = (f32[3,256,256]{2,1,0:T(8,128)S(1)}, f32[3,256,256]{2,1,0:T(8,128)S(1)}, u32[]{:S(2)}, u32[]{:S(2)}) collective-permute-start(f32[3,256,256]{2,1,0:T(8,128)S(1)} %get-tuple-element.38), channel_id=1, source_target_pairs={{0,2},{2,4},{4,6},{6,8},{8,10},{10,12},{12,14},{14,0},{1,3},{3,5},... | collective-permute-start | bytes 2359304 | tf_op jit(solution)/shard_map/ppermute | solution.py:28
  89.9 18.5 %collective-permute-done.9.arrived = f32[3,256,256]{2,1,0:T(8,128)S(1)} collective-permute-done((f32[3,256,256]{2,1,0:T(8,128)S(1)}, f32[3,256,256]{2,1,0:T(8,128)S(1)}, u32[]{:S(2)}, u32[]{:S(2)}) %collective-permute-start.9) | collective-permute-done | bytes 786464 | tf_op jit(solution)/shard_map/ppermute | solution.py:28
  109.1 1.4 %shard_map.72.before = f32[2,3,256,256]{3,2,1,0:T(8,128)} custom-call(s32[16]{0:T(128)S(1)} %get-tuple-element.22.ctl, f32[2,3,256,256]{3,2,1,0:T(8,128)S(1)} %get-tuple-element.37.state, f32[3,256,256]{2,1,0:T(8,128)S(1)} %collective-permute-done.9.arrived), custom_call_target="tpu_custom_call" | custom-call | flops 1048576 | bytes 4194304 | tf_op jit(solution)/shard_map/pallas_call | solution.py:440
  110.5 18.5 %collective-permute-done.10.arrived = f32[3,256,256]{2,1,0:T(8,128)S(1)} collective-permute-done((f32[3,256,256]{2,1,0:T(8,128)S(1)}, f32[3,256,256]{2,1,0:T(8,128)S(1)}, u32[]{:S(2)}, u32[]{:S(2)}) %collective-permute-start.10) | collective-permute-done | bytes 786464 | tf_op jit(solution)/shard_map/ppermute | solution.py:28
  129.0 1.4 %shard_map.73 = f32[2,3,256,256]{3,2,1,0:T(8,128)} custom-call(s32[16]{0:T(128)S(1)} %get-tuple-element.22.ctl, f32[3,256,256]{2,1,0:T(8,128)S(1)} %collective-permute-done.10.arrived, f32[2,3,256,256]{3,2,1,0:T(8,128)} %shard_map.72.before), custom_call_target="tpu_custom_call", output_to_operand_aliasing={{}: (2, {})} | custom-call | flops 1048576 | bytes 4194304 | tf_op jit(solution)/shard_map/pallas_call | solution.py:443
  (45 shorter events, 8.0 us)
Async XLA Ops:
  0.8 1.0 copy-start
  1.8 1.4 %copy-start.2 = (f32[2,3,256,256]{3,2,1,0:T(8,128)S(1)}, f32[2,3,256,256]{3,2,1,0:T(8,128)}, u32[]{:S(2)}) copy-start(f32[2,3,256,256]{3,2,1,0:T(8,128)} %state.3) | copy-start | bytes 4718596
  3.2 0.7 copy-start.17
  4.6 19.1 %copy-start.1 = (f32[2,256,256]{2,1,0:T(8,128)S(1)}, f32[2,256,256]{2,1,0:T(8,128)}, u32[]{:S(2)}) copy-start(f32[2,256,256]{2,1,0:T(8,128)} %bed.11) | copy-start | bytes 1572868
  4.6 19.1 %copy-start.3 = (f32[2,3,256,256]{3,2,1,0:T(8,128)S(1)}, f32[2,3,256,256]{3,2,1,0:T(8,128)}, u32[]{:S(2)}) copy-start(f32[2,3,256,256]{3,2,1,0:T(8,128)} %state.3) | copy-start | bytes 4718596
  6.8 16.9 %collective-permute-start.2 = (f32[256,128]{1,0:T(8,128)S(1)}, f32[256,128]{1,0:T(8,128)S(1)}, u32[]{:S(2)}, u32[]{:S(2)}) collective-permute-start(f32[256,128]{1,0:T(8,128)S(1)} %get-tuple-element.26), channel_id=1, source_target_pairs={{0,1},{1,0},{2,3},{3,2},{4,5},{5,4},{6,7},{7,6},{8,9},{9,8},{10,11... | collective-permute-start | bytes 393224 | tf_op jit(solution)/shard_map/ppermute | solution.py:28
  7.3 22.3 %all-to-all-start = ((f32[16,8,128]{2,1,0:T(8,128)}), f32[16,8,128]{2,1,0:T(8,128)S(1)}, u32[]{:S(2)}, u32[]{:S(2)}) async-start(f32[16,8,128]{2,1,0:T(8,128)} %bitcast), calls=%async_computation | async-start | bytes 131072 | tf_op jit(solution)/shard_map/all_to_all | solution.py:396
  14.3 5.2 %collective-permute-start = (f32[8,256]{1,0:T(8,128)S(1)}, f32[8,256]{1,0:T(8,128)S(1)}, u32[]{:S(2)}, u32[]{:S(2)}) collective-permute-start(f32[8,256]{1,0:T(8,128)S(1)} %get-tuple-element.24), channel_id=1, source_target_pairs={{0,2},{2,4},{4,6},{6,8},{8,10},{10,12},{12,14},{1,3},{3,5},{5,7},{... | collective-permute-start | bytes 24584 | tf_op jit(solution)/shard_map/ppermute | solution.py:28
  18.2 5.5 %collective-permute-start.1 = (f32[8,256]{1,0:T(8,128)S(1)}, f32[8,256]{1,0:T(8,128)S(1)}, u32[]{:S(2)}, u32[]{:S(2)}) collective-permute-start(f32[8,256]{1,0:T(8,128)S(1)} %get-tuple-element.25), channel_id=1, source_target_pairs={{2,0},{4,2},{6,4},{8,6},{10,8},{12,10},{14,12},{3,1},{5,3},{7,5},{... | collective-permute-start | bytes 24584 | tf_op jit(solution)/shard_map/ppermute | solution.py:28
  23.7 5.8 %copy-start.16 = (f32[2,256,256]{2,1,0:T(8,128)S(1)}, f32[2,256,256]{2,1,0:T(8,128)}, u32[]{:S(2)}) copy-start(f32[2,256,256]{2,1,0:T(8,128)} %manning.5) | copy-start | bytes 1572868
  28.4 1.1 copy-start.12
  29.5 1.4 %copy-start.13 = (f32[2,3,256,256]{3,2,1,0:T(8,128)S(1)}, f32[2,3,256,256]{3,2,1,0:T(8,128)}, u32[]{:S(2)}) copy-start(f32[2,3,256,256]{3,2,1,0:T(8,128)} %copy-done.12) | copy-start | bytes 4718596
  33.5 1.1 copy-start.4
  34.7 15.0 %collective-permute-start.5 = (f32[256,128]{1,0:T(8,128)S(1)}, f32[256,128]{1,0:T(8,128)S(1)}, u32[]{:S(2)}, u32[]{:S(2)}) collective-permute-start(f32[256,128]{1,0:T(8,128)S(1)} %get-tuple-element.31), channel_id=1, source_target_pairs={{0,1},{1,0},{2,3},{3,2},{4,5},{5,4},{6,7},{7,6},{8,9},{9,8},{10,11... | collective-permute-start | bytes 393224 | tf_op jit(solution)/shard_map/ppermute | solution.py:28
  34.7 22.4 %all-to-all-start.1 = ((f32[16,8,128]{2,1,0:T(8,128)}), f32[16,8,128]{2,1,0:T(8,128)S(1)}, u32[]{:S(2)}, u32[]{:S(2)}) async-start(f32[16,8,128]{2,1,0:T(8,128)} %bitcast.2), calls=%async_computation.1 | async-start | bytes 131072 | tf_op jit(solution)/shard_map/all_to_all | solution.py:396
  40.3 5.2 %collective-permute-start.3 = (f32[8,256]{1,0:T(8,128)S(1)}, f32[8,256]{1,0:T(8,128)S(1)}, u32[]{:S(2)}, u32[]{:S(2)}) collective-permute-start(f32[8,256]{1,0:T(8,128)S(1)} %get-tuple-element.29), channel_id=1, source_target_pairs={{0,2},{2,4},{4,6},{6,8},{8,10},{10,12},{12,14},{1,3},{3,5},{5,7},{... | collective-permute-start | bytes 24584 | tf_op jit(solution)/shard_map/ppermute | solution.py:28
  44.2 5.5 %collective-permute-start.4 = (f32[8,256]{1,0:T(8,128)S(1)}, f32[8,256]{1,0:T(8,128)S(1)}, u32[]{:S(2)}, u32[]{:S(2)}) collective-permute-start(f32[8,256]{1,0:T(8,128)S(1)} %get-tuple-element.30), channel_id=1, source_target_pairs={{2,0},{4,2},{6,4},{8,6},{10,8},{12,10},{14,12},{3,1},{5,3},{7,5},{... | collective-permute-start | bytes 24584 | tf_op jit(solution)/shard_map/ppermute | solution.py:28
  49.7 1.4 %copy-start.5 = (f32[2,3,256,256]{3,2,1,0:T(8,128)S(1)}, f32[2,3,256,256]{3,2,1,0:T(8,128)}, u32[]{:S(2)}) copy-start(f32[2,3,256,256]{3,2,1,0:T(8,128)} %copy-done.4) | copy-start | bytes 4718596
  51.1 5.9 %copy-start.6 = (f32[2,3,256,256]{3,2,1,0:T(8,128)S(1)}, f32[2,3,256,256]{3,2,1,0:T(8,128)}, u32[]{:S(2)}) copy-start(f32[2,3,256,256]{3,2,1,0:T(8,128)} %copy-done.4) | copy-start | bytes 4718596
  55.8 1.2 copy-start.10
  57.0 1.4 %copy-start.11 = (f32[2,3,256,256]{3,2,1,0:T(8,128)S(1)}, f32[2,3,256,256]{3,2,1,0:T(8,128)}, u32[]{:S(2)}) copy-start(f32[2,3,256,256]{3,2,1,0:T(8,128)} %copy-done.10) | copy-start | bytes 4718596
  61.0 1.1 copy-start.7
  62.1 15.0 %collective-permute-start.8 = (f32[256,128]{1,0:T(8,128)S(1)}, f32[256,128]{1,0:T(8,128)S(1)}, u32[]{:S(2)}, u32[]{:S(2)}) collective-permute-start(f32[256,128]{1,0:T(8,128)S(1)} %get-tuple-element.36), channel_id=1, source_target_pairs={{0,1},{1,0},{2,3},{3,2},{4,5},{5,4},{6,7},{7,6},{8,9},{9,8},{10,11... | collective-permute-start | bytes 393224 | tf_op jit(solution)/shard_map/ppermute | solution.py:28
  62.1 22.4 %all-to-all-start.2 = ((f32[16,8,128]{2,1,0:T(8,128)}), f32[16,8,128]{2,1,0:T(8,128)S(1)}, u32[]{:S(2)}, u32[]{:S(2)}) async-start(f32[16,8,128]{2,1,0:T(8,128)} %bitcast.4), calls=%async_computation.2 | async-start | bytes 131072 | tf_op jit(solution)/shard_map/all_to_all | solution.py:396
  67.8 5.2 %collective-permute-start.6 = (f32[8,256]{1,0:T(8,128)S(1)}, f32[8,256]{1,0:T(8,128)S(1)}, u32[]{:S(2)}, u32[]{:S(2)}) collective-permute-start(f32[8,256]{1,0:T(8,128)S(1)} %get-tuple-element.34), channel_id=1, source_target_pairs={{0,2},{2,4},{4,6},{6,8},{8,10},{10,12},{12,14},{1,3},{3,5},{5,7},{... | collective-permute-start | bytes 24584 | tf_op jit(solution)/shard_map/ppermute | solution.py:28
  71.6 5.5 %collective-permute-start.7 = (f32[8,256]{1,0:T(8,128)S(1)}, f32[8,256]{1,0:T(8,128)S(1)}, u32[]{:S(2)}, u32[]{:S(2)}) collective-permute-start(f32[8,256]{1,0:T(8,128)S(1)} %get-tuple-element.35), channel_id=1, source_target_pairs={{2,0},{4,2},{6,4},{8,6},{10,8},{12,10},{14,12},{3,1},{5,3},{7,5},{... | collective-permute-start | bytes 24584 | tf_op jit(solution)/shard_map/ppermute | solution.py:28
  77.2 1.4 %copy-start.8 = (f32[2,3,256,256]{3,2,1,0:T(8,128)S(1)}, f32[2,3,256,256]{3,2,1,0:T(8,128)}, u32[]{:S(2)}) copy-start(f32[2,3,256,256]{3,2,1,0:T(8,128)} %copy-done.7) | copy-start | bytes 4718596
  78.6 5.9 %copy-start.9 = (f32[2,3,256,256]{3,2,1,0:T(8,128)S(1)}, f32[2,3,256,256]{3,2,1,0:T(8,128)}, u32[]{:S(2)}) copy-start(f32[2,3,256,256]{3,2,1,0:T(8,128)} %copy-done.7) | copy-start | bytes 4718596
  83.3 1.2 copy-start.14
  84.5 1.4 %copy-start.15 = (f32[2,3,256,256]{3,2,1,0:T(8,128)S(1)}, f32[2,3,256,256]{3,2,1,0:T(8,128)}, u32[]{:S(2)}) copy-start(f32[2,3,256,256]{3,2,1,0:T(8,128)} %copy-done.14) | copy-start | bytes 4718596
  87.5 20.9 %collective-permute-start.9 = (f32[3,256,256]{2,1,0:T(8,128)S(1)}, f32[3,256,256]{2,1,0:T(8,128)S(1)}, u32[]{:S(2)}, u32[]{:S(2)}) collective-permute-start(f32[3,256,256]{2,1,0:T(8,128)S(1)} %get-tuple-element.38), channel_id=1, source_target_pairs={{0,2},{2,4},{4,6},{6,8},{8,10},{10,12},{12,14},{14,0},{1,3},{3,5},... | collective-permute-start | bytes 2359304 | tf_op jit(solution)/shard_map/ppermute | solution.py:28
  109.0 20.0 %collective-permute-start.10 = (f32[3,256,256]{2,1,0:T(8,128)S(1)}, f32[3,256,256]{2,1,0:T(8,128)S(1)}, u32[]{:S(2)}, u32[]{:S(2)}) collective-permute-start(f32[3,256,256]{2,1,0:T(8,128)S(1)} %shard_map.71), channel_id=1, source_target_pairs={{0,2},{2,4},{4,6},{6,8},{8,10},{10,12},{12,14},{14,0},{1,3},{3,5},... | collective-permute-start | bytes 2359304 | tf_op jit(solution)/shard_map/ppermute | solution.py:28
  (1 other events, 0.7 us)

commit v4 on v3

v4 whole, which is shorter than its diff:
```python
import functools

import jax
import jax.numpy as jnp
from jax import lax
from jax.experimental import pallas as pl
from jax.experimental.pallas import tpu as pltpu
from jax.sharding import PartitionSpec as P

STEPS = 3
GRAVITY = 9.81
ROOT_G = GRAVITY**0.5
SPACING = 5.0
COURANT = 0.2
ROWS = 32
LANES = 128
TILE = 256
VMEM_BYTES = 24 * 1024 * 1024
SLOT_LOW, WALL_WEST, WALL_EAST, WALL_OUTER, WET, MOVE = 0, 1, 3, 5, 7, 13
CONTROLS = 16
CHUNKS = 4
TOP = 6
SCALE = 0.5 / SPACING
SLOPE = GRAVITY / (2.0 * SPACING)


def shifted(value, axis, steps, around=True):
    count = lax.axis_size(axis)
    pairs = [(source, (source + steps) % count) for source in range(count)]
    if not around:
        pairs = [pair for pair in pairs if abs(pair[0] - pair[1]) == abs(steps)]
    return lax.ppermute(value, axis, pairs)


def cell(h, hu, hv):
    root = lax.rsqrt(h)
    inverse = root * root
    u = hu * inverse
    v = hv * inverse
    celerity = ROOT_G * (h * root)
    pressure = (0.5 * GRAVITY) * (h * h)
    cross = hu * v
    speed_x = jnp.abs(u) + celerity
    speed_y = jnp.abs(v) + celerity
    along_x = (h, hu, hv, hu * u + pressure, cross, speed_x)
    along_y = (h, hv, hu, hv * v + pressure, cross, speed_y)
    return along_x, along_y


def face(left, right):
    wave = jnp.maximum(left[5], right[5])
    return (
        (left[1] + right[1]) - wave * (right[0] - left[0]),
        (left[3] + right[3]) - wave * (right[1] - left[1]),
        (left[4] + right[4]) - wave * (right[2] - left[2]),
    )


def slot_of(ctl, position):
    low = ctl[SLOT_LOW]
    return low if position == 0 else 1 - low


def flag(ctl, index):
    return ctl[index] > 0


def start_all(pairs, sems, first=0):
    copies = [
        pltpu.make_async_copy(src, dst, sems.at[first + k]) for k, (src, dst) in enumerate(pairs)
    ]
    for copy in copies:
        copy.start()
    return copies


def wait_all(copies):
    for copy in copies:
        copy.wait()


def sublanes(width=TILE):
    return lax.broadcasted_iota(jnp.int32, (8, width), 0)


def stacked(lines, base):
    row = sublanes()
    for index, line in enumerate(lines):
        base = jnp.where(row == index, jnp.broadcast_to(line, (8, TILE)), base)
    return base


def messages(ctl, state, bed, fastest, out, columns):
    upper = lax.axis_index("yb")
    column = lax.axis_index("xb")
    last = lax.axis_size("xb") - 1
    devices = 2 * (last + 1)
    block = out.shape[0] // devices
    device = column * 2 + upper
    top = jnp.broadcast_to(fastest, (8, TILE))
    for peer in range(devices):
        out[peer * block : peer * block + 8, :] = top
    row = sublanes()

    def edge(line):
        rows = slice(line, line + 1)
        slots = [slot_of(ctl, position) for position in range(2)]
        fields = [state[slot, field, rows, :] for slot in slots for field in range(3)]
        return stacked(fields, top), [bed[slot, rows, :] for slot in slots] if bed is not None else None

    for inside, peer, line in (
        (column > 0, device - 2, 0),
        (column < last, device + 2, TILE - 1),
    ):

        @pl.when(inside)
        def _(peer=peer, line=line):
            lines, ground = edge(line)
            start = pl.multiple_of(peer * block, 8)
            out[pl.ds(start, 8), :] = lines
            if ground:
                out[pl.ds(pl.multiple_of(start + 8, 8), 8), :] = stacked(ground, top)

    slot = jnp.where(upper > 0, ctl[SLOT_LOW], 1 - ctl[SLOT_LOW])
    begin = pl.multiple_of((1 - upper) * LANES, LANES)
    lane = lax.broadcasted_iota(jnp.int32, (TILE, LANES), 1)
    packed = None
    for field in range(4 if bed is not None else 3):
        if field < 3:
            part = state[slot, field, :, pl.ds(begin, LANES)]
        else:
            part = bed[slot, :, pl.ds(begin, LANES)]
        turned = pltpu.roll(part, field + 1 - upper, 1)
        packed = turned if field == 0 else jnp.where(lane == field, turned, packed)
    lines = jnp.transpose(packed)[:8]
    columns[...] = lines
    start = pl.multiple_of((device + 1 - 2 * upper) * block, 8)
    out[pl.ds(start, 8), :] = jnp.where(row == TOP, top, lines)


def opening(
    state_in, bed_in, neighbours_in, wet_in, moves_in,
    out, columns, ctl,
    state, bed, neighbours, wet, moves, sems,
):
    copies = start_all(
        (
            (neighbours_in, neighbours),
            (wet_in, wet),
            (moves_in, moves),
            (state_in.at[0], state.at[0]),
            (state_in.at[1], state.at[1]),
            (bed_in, bed),
        ),
        sems,
    )
    device = lax.axis_index("xb") * 2 + lax.axis_index("yb")
    wait_all(copies[:3])
    first = device * 2
    low = jnp.where(neighbours[first, 3] == first + 1, 0, 1)
    ctl[SLOT_LOW] = low
    for position in range(2):
        slot = low if position == 0 else 1 - low
        tile = first + slot
        ctl[WALL_WEST + position] = (neighbours[tile, 0] < 0).astype(jnp.int32)
        ctl[WALL_EAST + position] = (neighbours[tile, 1] < 0).astype(jnp.int32)
        ctl[WALL_OUTER + position] = (neighbours[tile, 2 + position] < 0).astype(jnp.int32)
    for step in range(STEPS):
        for slot in range(2):
            ctl[WET + 2 * step + slot] = wet[step, first + slot]
        ctl[MOVE + step] = moves[step, device]

    total = jnp.zeros((ROWS, TILE), jnp.float32)
    for slot in range(2):
        copies[3 + slot].wait()

        def group(index, best, slot=slot):
            rows = pl.ds(pl.multiple_of(index * ROWS, ROWS), ROWS)
            along_x, along_y = cell(*(state[slot, field, rows, :] for field in range(3)))
            return jnp.maximum(best, jnp.maximum(along_x[5], along_y[5]))

        best = lax.fori_loop(0, TILE // ROWS, group, jnp.zeros((ROWS, TILE), jnp.float32))
        total = jnp.maximum(total, jnp.where(wet[0, first + slot] > 0, best, 0.0))
    copies[5].wait()
    messages(ctl, state, bed, jnp.max(total, keepdims=True), out, columns)


def rates(ctl, state_in, bed_in, rate_out, state, bed, rate, sems):
    row_ids = lax.broadcasted_iota(jnp.int32, (ROWS, TILE), 0)
    lane = lax.broadcasted_iota(jnp.int32, (ROWS, LANES), 1)
    row8 = sublanes()
    last = TILE // ROWS - 1
    chunk = TILE // CHUNKS
    incoming = []
    for part in range(CHUNKS):
        rows = slice(part * chunk, (part + 1) * chunk)
        incoming.append(
            start_all(
                (
                    (state_in.at[:, :, rows], state.at[:, :, rows]),
                    (bed_in.at[:, rows], bed.at[:, rows]),
                ),
                sems,
                2 * part,
            )
        )
    wait_all(incoming[0])
    outgoing = []

    def field_ref(which, field):
        return bed.at[which] if field == 3 else state.at[which, field]

    def opening_faces(position):
        slot = slot_of(ctl, position)
        keep = jnp.where(flag(ctl, WALL_WEST + position), 1.0, 0.0)
        first = [field_ref(slot, field)[0:8, :] for field in range(4)]
        right, _ = cell(*first[:3])
        left, _ = cell(first[0], -first[1], first[2])
        return tuple(keep * part[0:1, :] for part in face(left, right)) + (keep * first[3][0:1, :],)

    def group_of(position):
        slot = slot_of(ctl, position)
        other = 1 - slot
        keep_outer = jnp.where(flag(ctl, WALL_OUTER + position), 1.0, 0.0)
        keep_east = jnp.where(flag(ctl, WALL_EAST + position), 1.0, 0.0)
        inner_lane = LANES - 1 if position == 0 else 0
        outer_lane = LANES - 1 - inner_lane
        inner_cols = slice(0, LANES) if position == 0 else slice(LANES, TILE)
        inner_turn = LANES - 1 if position == 0 else 1

        def group(index, carry):
            base = pl.multiple_of(index * ROWS, ROWS)
            rows = pl.ds(base, ROWS)
            after = pl.ds(pl.multiple_of(jnp.minimum(base + ROWS, TILE - 8), 8), 8)
            at_end = index == last
            fields = []
            for field in range(4):
                ref = field_ref(slot, field)
                block = ref[rows, :]
                mirrored = jnp.broadcast_to(block[ROWS - 1 : ROWS], (8, TILE))
                if field == 1:
                    mirrored = -mirrored
                if field == 3:
                    mirrored = keep_east * mirrored
                fields.append(
                    jnp.concatenate([block, jnp.where(at_end, mirrored, ref[after, :])], 0)
                )
            cells_x, cells_y = cell(*fields[:3])

            def down(value):
                return pltpu.roll(value, ROWS + 7, 0)[:ROWS]

            here = tuple(value[:ROWS] for value in cells_x)
            keep = jnp.where(row8 == 7, jnp.where(at_end, keep_east, 1.0), 1.0)
            faces = tuple(
                jnp.concatenate([value[: ROWS - 8], value[ROWS - 8 :] * keep], 0)
                for value in face(here, tuple(down(value) for value in cells_x))
            )
            turned = tuple(pltpu.roll(value, 1, 0) for value in faces)
            change_x = tuple(
                value - jnp.where(row_ids == 0, before, moved)
                for value, before, moved in zip(faces, carry[:3], turned)
            )
            ground = fields[3][:ROWS]
            ground_up = pltpu.roll(ground, 1, 0)
            slope_x = down(fields[3]) - jnp.where(row_ids == 0, carry[3], ground_up)
            carried = tuple(value[0:1, :] for value in turned) + (ground_up[0:1, :],)

            ghosts = []
            for field in range(4):
                inner = pltpu.roll(field_ref(other, field)[rows, inner_cols], inner_turn, 1)
                own = fields[field][:ROWS, inner_cols]
                if field == 2:
                    own = -own
                if field == 3:
                    own = keep_outer * own
                ghosts.append(jnp.where(lane == inner_lane, inner, own))
            _, ghost_y = cell(*ghosts[:3])
            low = tuple(value[:ROWS, :LANES] for value in cells_y)
            high = tuple(value[:ROWS, LANES:] for value in cells_y)

            def right_of(low_part, high_part, ghost_part):
                turned_low = pltpu.roll(low_part, LANES - 1, 1)
                turned_high = pltpu.roll(high_part, LANES - 1, 1)
                return (
                    jnp.where(lane == LANES - 1, turned_high, turned_low),
                    jnp.where(lane == LANES - 1, ghost_part, turned_high),
                )

            pairs = [right_of(a, b, c) for a, b, c in zip(low, high, ghost_y)]
            faces_low = face(low, tuple(pair[0] for pair in pairs))
            faces_high = face(high, tuple(pair[1] for pair in pairs))
            faces_edge = face(ghost_y, low)
            if position == 0:
                faces_edge = tuple(keep_outer * value for value in faces_edge)
            else:
                keep_lane = jnp.where(lane == outer_lane, keep_outer, 1.0)
                faces_high = tuple(keep_lane * value for value in faces_high)
            change_y = []
            for a, b, c in zip(faces_low, faces_high, faces_edge):
                turned_a = pltpu.roll(a, 1, 1)
                turned_b = pltpu.roll(b, 1, 1)
                change_y.append(
                    jnp.concatenate(
                        [
                            a - jnp.where(lane == 0, c, turned_a),
                            b - jnp.where(lane == 0, turned_a, turned_b),
                        ],
                        1,
                    )
                )
            ground_low = ground[:, :LANES]
            ground_high = ground[:, LANES:]
            north = right_of(ground_low, ground_high, ghosts[3])
            turned_low = pltpu.roll(ground_low, 1, 1)
            turned_high = pltpu.roll(ground_high, 1, 1)
            slope_y = jnp.concatenate(
                [
                    north[0] - jnp.where(lane == 0, ghosts[3], turned_low),
                    north[1] - jnp.where(lane == 0, turned_low, turned_high),
                ],
                1,
            )
            weight = SLOPE * fields[0][:ROWS]
            rate[slot, 0, rows, :] = SCALE * (change_x[0] + change_y[0])
            rate[slot, 1, rows, :] = SCALE * (change_x[1] + change_y[2]) + weight * slope_x
            rate[slot, 2, rows, :] = SCALE * (change_x[2] + change_y[1]) + weight * slope_y
            return carried

        return group

    carries = [opening_faces(position) for position in range(2)]
    groups = [group_of(position) for position in range(2)]
    per_chunk = chunk // ROWS
    for part in range(CHUNKS):
        if part + 1 < CHUNKS:
            wait_all(incoming[part + 1])
        for position in range(2):
            carries[position] = lax.fori_loop(
                part * per_chunk, (part + 1) * per_chunk, groups[position], carries[position]
            )
        rows = slice(part * chunk, (part + 1) * chunk)
        outgoing += start_all(
            ((rate.at[:, :, rows], rate_out.at[:, :, rows]),), sems, 2 * CHUNKS + part
        )
    wait_all(outgoing)


def correct_rows(ctl, slot, got, ground, block, state, rate, bottom):
    position = jnp.where(ctl[SLOT_LOW] == slot, 0, 1)
    device = lax.axis_index("xb") * 2 + lax.axis_index("yb")
    wall = WALL_WEST if bottom else WALL_EAST

    @pl.when(jnp.logical_not(flag(ctl, wall + position)))
    def _():
        peer = device - 2 if bottom else device + 2
        lines = got[pl.ds(pl.multiple_of(peer * block, 8), 8), :]
        grounds = ground[pl.ds(pl.multiple_of(peer * 16 + 8, 8), 8), :]

        def line(value, offset):
            picked = jnp.where(
                position == 0, value[offset : offset + 1, :], value[offset + 3 : offset + 4, :]
            )
            return jnp.broadcast_to(picked, (8, TILE))

        ghost, _ = cell(*(line(lines, field) for field in range(3)))
        ghost_ground = jnp.where(position == 0, grounds[0:1, :], grounds[1:2, :])
        rows = slice(0, 8) if bottom else slice(TILE - 8, TILE)
        own = [state[slot, field, rows, :] for field in range(3)]
        here, _ = cell(*own)
        fluxes = face(ghost, here) if bottom else face(here, ghost)
        push = SCALE * fluxes[1] + (SLOPE * own[0]) * ghost_ground
        row = sublanes()
        sign = -1.0 if bottom else 1.0
        chosen = row == (0 if bottom else 7)
        for field, value in enumerate((SCALE * fluxes[0], push, SCALE * fluxes[2])):
            rate[slot, field, rows, :] += jnp.where(chosen, sign * value, 0.0)


def column_fix(got, ground, block, columns, bed_columns):
    upper = lax.axis_index("yb")
    device = lax.axis_index("xb") * 2 + upper
    peer = device + 1 - 2 * upper
    lines = got[pl.ds(pl.multiple_of(peer * block, 8), 8), :]
    ghost_ground = ground[pl.ds(pl.multiple_of(peer * 16, 8), 8), :][3:4]
    del bed_columns
    mine = columns[...]
    _, ghost = cell(lines[0:1], lines[1:2], lines[2:3])
    _, own = cell(mine[0:1], mine[1:2], mine[2:3])
    low = upper == 0
    left = tuple(jnp.where(low, a, b) for a, b in zip(own, ghost))
    right = tuple(jnp.where(low, b, a) for a, b in zip(own, ghost))
    fluxes = face(left, right)
    sign = jnp.where(low, 1.0, -1.0)
    push = SCALE * fluxes[1] + (SLOPE * mine[0:1]) * ghost_ground
    block8 = stacked(
        [sign * SCALE * fluxes[0], sign * SCALE * fluxes[2], sign * push],
        jnp.zeros((8, TILE), jnp.float32),
    )
    return jnp.transpose(
        jnp.concatenate([block8, jnp.zeros((LANES - 8, TILE), jnp.float32)], 0)
    )


def update(step, ctl, got, ground, columns, state_in, manning_in, rate_in, *rest):
    more = step + 1 < STEPS
    if more:
        fresh_out, out, columns_out = rest[:3]
        rest = rest[3:]
    else:
        fresh_out, leaving = rest[:2]
        rest = rest[2:]
    state, manning, rate, fresh, sems = rest
    half = TILE // 2
    parts = [(slot, slice(k * half, (k + 1) * half)) for slot in range(2) for k in range(2)]
    incoming = []
    for index, (slot, rows) in enumerate(parts):
        incoming.append(
            start_all(
                (
                    (rate_in.at[slot, :, rows], rate.at[slot, :, rows]),
                    (state_in.at[slot, :, rows], state.at[slot, :, rows]),
                    (manning_in.at[slot, rows], manning.at[slot, rows]),
                ),
                sems,
                3 * index,
            )
        )
    upper = lax.axis_index("yb")
    devices = 2 * lax.axis_size("xb")
    block = got.shape[0] // devices
    tops = got[0:8, :]
    for peer in range(1, devices):
        tops = jnp.maximum(tops, got[peer * block : peer * block + 8, :])
    delta = (COURANT * SPACING) / tops[TOP : TOP + 1, :]
    fix = column_fix(got, ground, block, columns, None)
    facing = jnp.where(upper > 0, ctl[SLOT_LOW], 1 - ctl[SLOT_LOW])
    begin = pl.multiple_of((1 - upper) * LANES, LANES)
    target = (1 - upper) * (LANES - 1)
    lane = lax.broadcasted_iota(jnp.int32, (half, LANES), 1)
    total = jnp.zeros((ROWS, TILE), jnp.float32)
    outgoing = []
    for index, (slot, part_rows) in enumerate(parts):
        wait_all(incoming[index])
        bottom = index % 2 == 0
        correct_rows(ctl, slot, got, ground, block, state, rate, bottom)

        @pl.when(facing == slot)
        def _(slot=slot, part_rows=part_rows):
            for field in range(3):
                turned = pltpu.roll(
                    fix[part_rows], lax.rem(target + LANES - field, LANES), 1
                )
                rate[slot, field, part_rows, pl.ds(begin, LANES)] += jnp.where(
                    lane == target, turned, 0.0
                )

        wet_now = flag(ctl, WET + 2 * step + slot)

        def group(index, best, slot=slot, wet_now=wet_now):
            rows = pl.ds(pl.multiple_of(index * ROWS, ROWS), ROWS)
            h0, hu0, hv0 = (state[slot, field, rows, :] for field in range(3))
            h = h0 - delta * rate[slot, 0, rows, :]
            hu = hu0 - delta * rate[slot, 1, rows, :]
            hv = hv0 - delta * rate[slot, 2, rows, :]
            rough = manning[slot, rows, :]
            inverse = 1.0 / h
            u = hu * inverse
            v = hv * inverse
            speed = jnp.sqrt(u * u + v * v)
            power = jnp.exp((-4.0 / 3.0) * jnp.log(jnp.abs(h)))
            drag = (GRAVITY * delta) * (rough * rough) * (speed * power)
            factor = 1.0 / (1.0 + drag)
            hu = hu * factor
            hv = hv * factor
            h = jnp.where(wet_now, h, h0)
            hu = jnp.where(wet_now, hu, hu0)
            hv = jnp.where(wet_now, hv, hv0)
            fresh[slot, 0, rows, :] = h
            fresh[slot, 1, rows, :] = hu
            fresh[slot, 2, rows, :] = hv
            if more:
                along_x, along_y = cell(h, hu, hv)
                best = jnp.maximum(best, jnp.maximum(along_x[5], along_y[5]))
            return best

        best = lax.fori_loop(
            part_rows.start // ROWS,
            part_rows.stop // ROWS,
            group,
            jnp.zeros((ROWS, TILE), jnp.float32),
        )
        if more:
            best = jnp.where(flag(ctl, WET + 2 * step + 2 + slot), best, 0.0)
            total = jnp.maximum(total, best)
        outgoing += start_all(
            ((fresh.at[slot, :, part_rows], fresh_out.at[slot, :, part_rows]),), sems, 12 + index
        )
    if more:
        messages(ctl, fresh, None, jnp.max(total, keepdims=True), out, columns_out)
    else:
        outgoing += start_all(((fresh.at[ctl[MOVE]], leaving),), sems, 16)
    wait_all(outgoing)


def second_leaving(ctl, state, arrived, leaving, sems):
    again = ctl[MOVE] == ctl[MOVE + 1]

    @pl.when(again)
    def _():
        pltpu.make_async_copy(arrived, leaving, sems.at[0]).start()

    @pl.when(jnp.logical_not(again))
    def _():
        pltpu.make_async_copy(state.at[1 - ctl[MOVE]], leaving, sems.at[0]).start()

    pltpu.make_async_copy(arrived, leaving, sems.at[0]).wait()


def keep_rest(ctl, state, arrived, out, sems):
    rest = out.at[1 - ctl[MOVE + 1]]
    again = ctl[MOVE] == ctl[MOVE + 1]

    @pl.when(again)
    def _():
        pltpu.make_async_copy(state.at[1 - ctl[MOVE]], rest, sems.at[0]).start()

    @pl.when(jnp.logical_not(again))
    def _():
        pltpu.make_async_copy(arrived, rest, sems.at[0]).start()

    pltpu.make_async_copy(arrived, rest, sems.at[0]).wait()


def keep_last(ctl, arrived, before, out, sems):
    del before
    copy = pltpu.make_async_copy(arrived, out.at[ctl[MOVE + 1]], sems.at[0])
    copy.start()
    copy.wait()


def vmem():
    return pl.BlockSpec(memory_space=pltpu.VMEM)


def smem():
    return pl.BlockSpec(memory_space=pltpu.SMEM)


def hbm():
    return pl.BlockSpec(memory_space=pltpu.HBM)


def anywhere():
    return pl.BlockSpec(memory_space=pl.ANY)


def call(kernel, outs, out_specs, in_specs, flops, scratch=(), aliases=None):
    return pl.pallas_call(
        kernel,
        scratch_shapes=scratch,
        input_output_aliases=aliases or {},
        out_shape=outs,
        in_specs=in_specs,
        out_specs=out_specs,
        compiler_params=pltpu.CompilerParams(vmem_limit_bytes=VMEM_BYTES),
        cost_estimate=pl.CostEstimate(flops=flops, bytes_accessed=4 << 20, transcendentals=0),
    )


def f32(*shape):
    return jax.ShapeDtypeStruct(shape, jnp.float32)


def spread(fast):
    return lax.all_to_all(fast, ("xb", "yb"), split_axis=0, concat_axis=0, tiled=True)


def body(state, bed, manning, neighbours, wet, moves):
    shape = f32(*state.shape)
    tile_shape = f32(*state.shape[1:])
    devices = lax.axis_size("xb") * lax.axis_size("yb")
    sem = [pltpu.SemaphoreType.DMA((1,))]
    whole = pltpu.VMEM(state.shape, jnp.float32)
    part = pltpu.VMEM(bed.shape, jnp.float32)
    out, columns, ctl = call(
        opening,
        (
            f32(16 * devices, TILE),
            f32(8, TILE),
            jax.ShapeDtypeStruct((CONTROLS,), jnp.int32),
        ),
        (vmem(), vmem(), smem()),
        [hbm()] * 5,
        4 << 20,
        [
            whole,
            part,
            pltpu.SMEM(neighbours.shape, jnp.int32),
            pltpu.SMEM(wet.shape, jnp.int32),
            pltpu.SMEM(moves.shape, jnp.int32),
            pltpu.SemaphoreType.DMA((6,)),
        ],
    )(state, bed, neighbours, wet, moves)
    ground = None
    for step in range(STEPS):
        got = spread(out)
        ground = got if step == 0 else ground
        rate = call(
            rates,
            shape,
            hbm(),
            [smem(), hbm(), hbm()],
            16 << 20,
            [whole, part, whole, pltpu.SemaphoreType.DMA((3 * CHUNKS,))],
        )(ctl, state, bed)
        more = step + 1 < STEPS
        extra = (f32(8 * devices, TILE), f32(8, TILE)) if more else (tile_shape,)
        outs = call(
            functools.partial(update, step),
            (shape,) + extra,
            (hbm(), vmem(), vmem()) if more else (hbm(), hbm()),
            [smem(), vmem(), vmem(), vmem(), hbm(), hbm(), hbm()],
            8 << 20,
            [whole, part, whole, whole, pltpu.SemaphoreType.DMA((17,))],
        )(ctl, got, ground, columns, state, manning, rate)
        state = outs[0]
        if more:
            _, out, columns = outs
    arrived = shifted(outs[1], "xb", 1)
    leaving = call(
        second_leaving, tile_shape, anywhere(), [smem(), anywhere(), anywhere()], 1 << 20, sem
    )(ctl, state, arrived)
    arrived_next = shifted(leaving, "xb", 1)
    final = call(
        keep_rest, shape, anywhere(), [smem(), anywhere(), anywhere()], 1 << 20, sem
    )(ctl, state, arrived)
    return call(
        keep_last, shape, anywhere(), [smem(), anywhere(), anywhere()], 1 << 20, sem, {2: 0}
    )(ctl, arrived_next, final)


def solution(mesh):
    placed = (
        P(("runs", "xb", "yb"), None, None, None),
        P(("runs", "xb", "yb"), None, None),
        P(("runs", "xb", "yb"), None, None),
        P("runs", None),
        P(None, "runs"),
        P(None, "runs"),
    )
    return jax.shard_map(
        body,
        mesh=mesh,
        in_specs=placed,
        out_specs=P(("runs", "xb", "yb"), None, None, None),
        check_vma=False,
    )
```

time: 131 us -> 114 us (0.87)
  starting transfers between devices: 36.7 us -> 17.4 us
  Pallas kernels: 26.4 us -> 34.6 us
  waiting for transfers between devices: 49.7 us -> 45.2 us
    ppermute x11 -> x2, starting transfers between devices: 18.3 us -> 0.58 us  [shifted(): return lax.ppermute(value, axis, pairs)]
    ppermute x11 -> x2, waiting for transfers between devices: 49.7 us -> 40.1 us  [shifted(): return lax.ppermute(value, axis, pairs)]
    pallas_call x7, Pallas kernels: 22.9 us -> 31.1 us  [the longest x3 15.8 us: body(): call(rates, shape, hbm(), [smem(), hbm(), hbm()], 16 << 20, [whole, part,...]
    all_to_all x3, waiting for transfers between devices: 0.01 us -> 5.09 us  [spread(): lax.all_to_all(fast, ('xb', 'yb'), split_axis=0, concat_axis=0, tiled=True)]
    all_to_all x3, starting transfers between devices: 18.4 us -> 16.9 us  [spread(): lax.all_to_all(fast, ('xb', 'yb'), split_axis=0, concat_axis=0, tiled=True)]
    unnamed x39 -> x33, local copies, waits for them, and re-layouts: 17.4 us -> 16.2 us
  transfers between devices with their start and end apart: 14 -> 5, of which waited for: 5 -> 4; matrix products, arithmetic and copies ran while one was open for 0% -> 0% of each run, Pallas kernels for 12% -> 15%
where the time goes in v4:
time: 114 us
  waiting for transfers between devices  45.2 us (40%)
  Pallas kernels  34.6 us (30%)
  starting transfers between devices  17.4 us (15%)
  local copies, waits for them, and re-layouts  16.2 us (14%)
    ppermute x2, waiting for transfers between devices, shifted(): return lax.ppermute(value, axis, pairs)  40.1 us
    all_to_all x3, starting transfers between devices, spread(): lax.all_to_all(fast, ('xb', 'yb'), split_axis=0, concat_axis=0, tiled=True)  16.9 us
    unnamed x33, local copies, waits for them, and re-layouts  16.2 us
    pallas_call x3, Pallas kernels, body(): call(rates, shape, hbm(), [smem(), hbm(), hbm()], 16 << 20, [whole, part,...  15.8 us
    pallas_call x3, Pallas kernels, body(): call(functools.partial(update, step), (shape,) + extra, (hbm(), vmem(), v...  12.9 us
    all_to_all x3, waiting for transfers between devices, spread(): lax.all_to_all(fast, ('xb', 'yb'), split_axis=0, concat_axis=0, tiled=True)  5.09 us
    pallas_call x1, Pallas kernels, body(): call(opening, (f32(16 * devices, TILE), f32(8, TILE), jax.ShapeDtypeStruc...  2.37 us
  transfers between devices with their start and end apart: 5, of which 4 were waited for; matrix products, arithmetic and copies ran while one was open for 0% of the time, Pallas kernels for 15%

profile of v4, /device:TPU:0, one launch (start us, length us, event | category | flops | bytes accessed | tf_op | source)
XLA Modules:
  0.0 113.7 jit_solution(17121943822841501299)
XLA Ops:
  0.0 0.8 copy.8.neighbours_in
  0.8 1.4 %copy-done = f32[2,3,256,256]{3,2,1,0:T(8,128)S(1)} copy-done((f32[2,3,256,256]{3,2,1,0:T(8,128)S(1)}, f32[2,3,256,256]{3,2,1,0:T(8,128)}, u32[]{:S(2)}) %copy-start) | copy-done | bytes 1572888
  2.2 1.0 copy-done.2
  3.2 0.7 copy-done.14
  3.9 0.7 copy-done.15
  4.6 2.4 %shard_map.64 = (f32[256,256]{1,0:T(8,128)}, f32[8,256]{1,0:T(8,128)S(1)}, s32[16]{0:T(128)S(1)}) custom-call(f32[2,3,256,256]{3,2,1,0:T(8,128)S(1)} %copy-done, f32[2,256,256]{2,1,0:T(8,128)S(1)} %copy-done.2, s32[32,4]{1,0:T(8,128)S(1)} %copy.8.neighbours_in, s32[3,32]{1,0:T(4,128)S(1)} %copy-done.14, s32[3,16]{1,0:T(4,128)S(1)} %copy-done.15), custom_call_target="tpu_custom_call" | custom-call | flops 4194304 | bytes 4194304 | tf_op jit(solution)/shard_map/pallas_call | solution.py:586
  7.0 7.4 %all-to-all-start = ((f32[16,16,256]{2,1,0:T(8,128)}), f32[16,16,256]{2,1,0:T(8,128)S(1)}, u32[]{:S(2)}, u32[]{:S(2)}) async-start(f32[16,16,256]{2,1,0:T(8,128)} %bitcast), calls=%async_computation | async-start | bytes 524288 | tf_op jit(solution)/shard_map/all_to_all | solution.py:576
  14.4 5.3 %shard_map.65.rate_in = f32[2,3,256,256]{3,2,1,0:T(8,128)S(1)} custom-call(s32[16]{0:T(128)S(1)} %get-tuple-element.16.ctl, f32[2,3,256,256]{3,2,1,0:T(8,128)S(1)} %copy-done.1, f32[2,256,256]{2,1,0:T(8,128)S(1)} %copy-done.3), custom_call_target="tpu_custom_call" | custom-call | flops 16777216 | bytes 4194304 | tf_op jit(solution)/shard_map/pallas_call | solution.py:609
  19.7 1.1 copy-done.11
  20.8 3.6 %all-to-all-done = f32[16,16,256]{2,1,0:T(8,128)S(1)} async-done(((f32[16,16,256]{2,1,0:T(8,128)}), f32[16,16,256]{2,1,0:T(8,128)S(1)}, u32[]{:S(2)}, u32[]{:S(2)}) %all-to-all-start) | async-done | bytes 262176 | tf_op jit(solution)/shard_map/all_to_all | solution.py:576
  24.4 1.4 %copy-done.12 = f32[2,3,256,256]{3,2,1,0:T(8,128)S(1)} copy-done((f32[2,3,256,256]{3,2,1,0:T(8,128)S(1)}, f32[2,3,256,256]{3,2,1,0:T(8,128)}, u32[]{:S(2)}) %copy-start.12) | copy-done | bytes 1572888
  25.8 4.7 %shard_map.66 = (f32[2,3,256,256]{3,2,1,0:T(8,128)S(1)}, f32[128,256]{1,0:T(8,128)}, f32[8,256]{1,0:T(8,128)S(1)}) custom-call(s32[16]{0:T(128)S(1)} %get-tuple-element.16.ctl, f32[256,256]{1,0:T(8,128)S(1)} %bitcast.6, f32[256,256]{1,0:T(8,128)S(1)} %bitcast.7, f32[8,256]{1,0:T(8,128)S(1)} %get-tuple-element.18.columns, f32[2,3,256,256]{3,2,1,0:T(8,128)S(1)} %copy-done.1, ...), custom_call_target="tpu_custom_call" | custom-call | flops 8388608 | bytes 4194304 | tf_op jit(solution)/shard_map/pallas_call | solution.py:619
  30.5 1.1 copy-done.4
  31.7 3.5 %all-to-all-start.1 = ((f32[16,8,256]{2,1,0:T(8,128)}), f32[16,8,256]{2,1,0:T(8,128)S(1)}, u32[]{:S(2)}, u32[]{:S(2)}) async-start(f32[16,8,256]{2,1,0:T(8,128)} %bitcast.2), calls=%async_computation.1 | async-start | bytes 262144 | tf_op jit(solution)/shard_map/all_to_all | solution.py:576
  35.2 1.4 %copy-done.5 = f32[2,3,256,256]{3,2,1,0:T(8,128)S(1)} copy-done((f32[2,3,256,256]{3,2,1,0:T(8,128)S(1)}, f32[2,3,256,256]{3,2,1,0:T(8,128)}, u32[]{:S(2)}) %copy-start.5) | copy-done | bytes 1572888
  36.6 5.3 %shard_map.67.rate_in = f32[2,3,256,256]{3,2,1,0:T(8,128)S(1)} custom-call(s32[16]{0:T(128)S(1)} %get-tuple-element.16.ctl, f32[2,3,256,256]{3,2,1,0:T(8,128)S(1)} %copy-done.5, f32[2,256,256]{2,1,0:T(8,128)S(1)} %copy-done.3), custom_call_target="tpu_custom_call" | custom-call | flops 16777216 | bytes 4194304 | tf_op jit(solution)/shard_map/pallas_call | solution.py:609
  41.9 1.2 %copy-done.7 = f32[2,3,256,256]{3,2,1,0:T(8,128)} copy-done((f32[2,3,256,256]{3,2,1,0:T(8,128)}, f32[2,3,256,256]{3,2,1,0:T(8,128)S(1)}, u32[]{:S(2)}) %copy-start.7) | copy-done | bytes 1572888
  43.1 1.4 %copy-done.6 = f32[2,3,256,256]{3,2,1,0:T(8,128)S(1)} copy-done((f32[2,3,256,256]{3,2,1,0:T(8,128)S(1)}, f32[2,3,256,256]{3,2,1,0:T(8,128)}, u32[]{:S(2)}) %copy-start.6) | copy-done | bytes 1572888
  44.5 1.4 %copy-done.8 = f32[2,3,256,256]{3,2,1,0:T(8,128)S(1)} copy-done((f32[2,3,256,256]{3,2,1,0:T(8,128)S(1)}, f32[2,3,256,256]{3,2,1,0:T(8,128)}, u32[]{:S(2)}) %copy-start.8) | copy-done | bytes 1572888
  45.9 4.7 %shard_map.68 = (f32[2,3,256,256]{3,2,1,0:T(8,128)S(1)}, f32[128,256]{1,0:T(8,128)}, f32[8,256]{1,0:T(8,128)S(1)}) custom-call(s32[16]{0:T(128)S(1)} %get-tuple-element.16.ctl, f32[128,256]{1,0:T(8,128)S(1)} %bitcast.10, f32[256,256]{1,0:T(8,128)S(1)} %bitcast.8, f32[8,256]{1,0:T(8,128)S(1)} %get-tuple-element.20.columns, f32[2,3,256,256]{3,2,1,0:T(8,128)S(1)} %copy-done.6, ...), custom_call_target="tpu_custom_call" | custom-call | flops 8388608 | bytes 4194304 | tf_op jit(solution)/shard_map/pallas_call | solution.py:619
  50.6 6.0 %all-to-all-start.2 = ((f32[16,8,256]{2,1,0:T(8,128)}), f32[16,8,256]{2,1,0:T(8,128)S(1)}, u32[]{:S(2)}, u32[]{:S(2)}) async-start(f32[16,8,256]{2,1,0:T(8,128)} %bitcast.4), calls=%async_computation.2 | async-start | bytes 262144 | tf_op jit(solution)/shard_map/all_to_all | solution.py:576
  56.6 5.3 %shard_map.69.rate_in = f32[2,3,256,256]{3,2,1,0:T(8,128)S(1)} custom-call(s32[16]{0:T(128)S(1)} %get-tuple-element.16.ctl, f32[2,3,256,256]{3,2,1,0:T(8,128)S(1)} %get-tuple-element.24.state_in, f32[2,256,256]{2,1,0:T(8,128)S(1)} %copy-done.3), custom_call_target="tpu_custom_call" | custom-call | flops 16777216 | bytes 4194304 | tf_op jit(solution)/shard_map/pallas_call | solution.py:609
  61.9 1.1 copy-done.9
  63.0 1.5 %all-to-all-done.2 = f32[16,8,256]{2,1,0:T(8,128)S(1)} async-done(((f32[16,8,256]{2,1,0:T(8,128)}), f32[16,8,256]{2,1,0:T(8,128)S(1)}, u32[]{:S(2)}, u32[]{:S(2)}) %all-to-all-start.2) | async-done | bytes 131104 | tf_op jit(solution)/shard_map/all_to_all | solution.py:576
  64.5 1.4 %copy-done.10 = f32[2,3,256,256]{3,2,1,0:T(8,128)S(1)} copy-done((f32[2,3,256,256]{3,2,1,0:T(8,128)S(1)}, f32[2,3,256,256]{3,2,1,0:T(8,128)}, u32[]{:S(2)}) %copy-start.10) | copy-done | bytes 1572888
  65.9 3.5 %shard_map.70 = (f32[2,3,256,256]{3,2,1,0:T(8,128)S(1)}, f32[3,256,256]{2,1,0:T(8,128)S(1)}) custom-call(s32[16]{0:T(128)S(1)} %get-tuple-element.16.ctl, f32[128,256]{1,0:T(8,128)S(1)} %bitcast.11, f32[256,256]{1,0:T(8,128)S(1)} %bitcast.9, f32[8,256]{1,0:T(8,128)S(1)} %get-tuple-element.23.columns, f32[2,3,256,256]{3,2,1,0:T(8,128)S(1)} %get-tuple-element.24.state_in, ...), custom_call_target="tpu_custom_call" | custom-call | flops 8388608 | bytes 4194304 | tf_op jit(solution)/shard_map/pallas_call | solution.py:619
  69.5 0.5 collective-permute-start
  70.0 21.0 %collective-permute-done.arrived = f32[3,256,256]{2,1,0:T(8,128)S(1)} collective-permute-done((f32[3,256,256]{2,1,0:T(8,128)S(1)}, f32[3,256,256]{2,1,0:T(8,128)S(1)}, u32[]{:S(2)}, u32[]{:S(2)}) %collective-permute-start) | collective-permute-done | bytes 786464 | tf_op jit(solution)/shard_map/ppermute | solution.py:32
  91.0 0.6 shard_map.71
  91.7 1.4 %shard_map.72.before = f32[2,3,256,256]{3,2,1,0:T(8,128)} custom-call(s32[16]{0:T(128)S(1)} %get-tuple-element.16.ctl, f32[2,3,256,256]{3,2,1,0:T(8,128)S(1)} %get-tuple-element.25.state, f32[3,256,256]{2,1,0:T(8,128)S(1)} %collective-permute-done.arrived), custom_call_target="tpu_custom_call" | custom-call | flops 1048576 | bytes 4194304 | tf_op jit(solution)/shard_map/pallas_call | solution.py:635
  93.1 19.1 %collective-permute-done.1.arrived = f32[3,256,256]{2,1,0:T(8,128)S(1)} collective-permute-done((f32[3,256,256]{2,1,0:T(8,128)S(1)}, f32[3,256,256]{2,1,0:T(8,128)S(1)}, u32[]{:S(2)}, u32[]{:S(2)}) %collective-permute-start.1) | collective-permute-done | bytes 786464 | tf_op jit(solution)/shard_map/ppermute | solution.py:32
  112.2 1.4 %shard_map.73 = f32[2,3,256,256]{3,2,1,0:T(8,128)} custom-call(s32[16]{0:T(128)S(1)} %get-tuple-element.16.ctl, f32[3,256,256]{2,1,0:T(8,128)S(1)} %collective-permute-done.1.arrived, f32[2,3,256,256]{3,2,1,0:T(8,128)} %shard_map.72.before), custom_call_target="tpu_custom_call", output_to_operand_aliasing={{}: (2, {})} | custom-call | flops 1048576 | bytes 4194304 | tf_op jit(solution)/shard_map/pallas_call | solution.py:638
  (21 shorter events, 0.1 us)
Async XLA Ops:
  0.8 1.4 %copy-start = (f32[2,3,256,256]{3,2,1,0:T(8,128)S(1)}, f32[2,3,256,256]{3,2,1,0:T(8,128)}, u32[]{:S(2)}) copy-start(f32[2,3,256,256]{3,2,1,0:T(8,128)} %state_in.5) | copy-start | bytes 4718596
  2.2 1.0 copy-start.2
  3.2 0.7 copy-start.14
  3.9 0.7 copy-start.15
  4.6 9.8 %copy-start.1 = (f32[2,3,256,256]{3,2,1,0:T(8,128)S(1)}, f32[2,3,256,256]{3,2,1,0:T(8,128)}, u32[]{:S(2)}) copy-start(f32[2,3,256,256]{3,2,1,0:T(8,128)} %state_in.5) | copy-start | bytes 4718596
  4.6 9.8 %copy-start.3 = (f32[2,256,256]{2,1,0:T(8,128)S(1)}, f32[2,256,256]{2,1,0:T(8,128)}, u32[]{:S(2)}) copy-start(f32[2,256,256]{2,1,0:T(8,128)} %bed_in.7) | copy-start | bytes 1572868
  7.0 17.4 %all-to-all-start = ((f32[16,16,256]{2,1,0:T(8,128)}), f32[16,16,256]{2,1,0:T(8,128)S(1)}, u32[]{:S(2)}, u32[]{:S(2)}) async-start(f32[16,16,256]{2,1,0:T(8,128)} %bitcast), calls=%async_computation | async-start | bytes 524288 | tf_op jit(solution)/shard_map/all_to_all | solution.py:576
  14.4 10.0 %copy-start.13 = (f32[2,256,256]{2,1,0:T(8,128)S(1)}, f32[2,256,256]{2,1,0:T(8,128)}, u32[]{:S(2)}) copy-start(f32[2,256,256]{2,1,0:T(8,128)} %manning_in.5) | copy-start | bytes 1572868
  19.7 1.1 %copy-start.11 = (f32[2,3,256,256]{3,2,1,0:T(8,128)}, f32[2,3,256,256]{3,2,1,0:T(8,128)S(1)}, u32[]{:S(2)}) copy-start(f32[2,3,256,256]{3,2,1,0:T(8,128)S(1)} %shard_map.65.rate_in) | copy-start | bytes 4718596
  24.4 1.4 %copy-start.12 = (f32[2,3,256,256]{3,2,1,0:T(8,128)S(1)}, f32[2,3,256,256]{3,2,1,0:T(8,128)}, u32[]{:S(2)}) copy-start(f32[2,3,256,256]{3,2,1,0:T(8,128)} %copy-done.11) | copy-start | bytes 4718596
  30.5 1.1 %copy-start.4 = (f32[2,3,256,256]{3,2,1,0:T(8,128)}, f32[2,3,256,256]{3,2,1,0:T(8,128)S(1)}, u32[]{:S(2)}) copy-start(f32[2,3,256,256]{3,2,1,0:T(8,128)S(1)} %get-tuple-element.21.state_in) | copy-start | bytes 4718596
  31.7 11.4 %all-to-all-start.1 = ((f32[16,8,256]{2,1,0:T(8,128)}), f32[16,8,256]{2,1,0:T(8,128)S(1)}, u32[]{:S(2)}, u32[]{:S(2)}) async-start(f32[16,8,256]{2,1,0:T(8,128)} %bitcast.2), calls=%async_computation.1 | async-start | bytes 262144 | tf_op jit(solution)/shard_map/all_to_all | solution.py:576
  35.2 1.4 %copy-start.5 = (f32[2,3,256,256]{3,2,1,0:T(8,128)S(1)}, f32[2,3,256,256]{3,2,1,0:T(8,128)}, u32[]{:S(2)}) copy-start(f32[2,3,256,256]{3,2,1,0:T(8,128)} %copy-done.4) | copy-start | bytes 4718596
  41.9 1.2 %copy-start.7 = (f32[2,3,256,256]{3,2,1,0:T(8,128)}, f32[2,3,256,256]{3,2,1,0:T(8,128)S(1)}, u32[]{:S(2)}) copy-start(f32[2,3,256,256]{3,2,1,0:T(8,128)S(1)} %shard_map.67.rate_in) | copy-start | bytes 4718596
  43.1 1.4 %copy-start.6 = (f32[2,3,256,256]{3,2,1,0:T(8,128)S(1)}, f32[2,3,256,256]{3,2,1,0:T(8,128)}, u32[]{:S(2)}) copy-start(f32[2,3,256,256]{3,2,1,0:T(8,128)} %copy-done.4) | copy-start | bytes 4718596
  44.5 1.4 %copy-start.8 = (f32[2,3,256,256]{3,2,1,0:T(8,128)S(1)}, f32[2,3,256,256]{3,2,1,0:T(8,128)}, u32[]{:S(2)}) copy-start(f32[2,3,256,256]{3,2,1,0:T(8,128)} %copy-done.7) | copy-start | bytes 4718596
  50.6 13.9 %all-to-all-start.2 = ((f32[16,8,256]{2,1,0:T(8,128)}), f32[16,8,256]{2,1,0:T(8,128)S(1)}, u32[]{:S(2)}, u32[]{:S(2)}) async-start(f32[16,8,256]{2,1,0:T(8,128)} %bitcast.4), calls=%async_computation.2 | async-start | bytes 262144 | tf_op jit(solution)/shard_map/all_to_all | solution.py:576
  61.9 1.1 %copy-start.9 = (f32[2,3,256,256]{3,2,1,0:T(8,128)}, f32[2,3,256,256]{3,2,1,0:T(8,128)S(1)}, u32[]{:S(2)}) copy-start(f32[2,3,256,256]{3,2,1,0:T(8,128)S(1)} %shard_map.69.rate_in) | copy-start | bytes 4718596
  64.5 1.4 %copy-start.10 = (f32[2,3,256,256]{3,2,1,0:T(8,128)S(1)}, f32[2,3,256,256]{3,2,1,0:T(8,128)}, u32[]{:S(2)}) copy-start(f32[2,3,256,256]{3,2,1,0:T(8,128)} %copy-done.9) | copy-start | bytes 4718596
  69.5 21.5 %collective-permute-start = (f32[3,256,256]{2,1,0:T(8,128)S(1)}, f32[3,256,256]{2,1,0:T(8,128)S(1)}, u32[]{:S(2)}, u32[]{:S(2)}) collective-permute-start(f32[3,256,256]{2,1,0:T(8,128)S(1)} %get-tuple-element.26), channel_id=1, source_target_pairs={{0,2},{2,4},{4,6},{6,8},{8,10},{10,12},{12,14},{14,0},{1,3},{3,5},... | collective-permute-start | bytes 2359304 | tf_op jit(solution)/shard_map/ppermute | solution.py:32
  91.6 20.6 %collective-permute-start.1 = (f32[3,256,256]{2,1,0:T(8,128)S(1)}, f32[3,256,256]{2,1,0:T(8,128)S(1)}, u32[]{:S(2)}, u32[]{:S(2)}) collective-permute-start(f32[3,256,256]{2,1,0:T(8,128)S(1)} %shard_map.71), channel_id=1, source_target_pairs={{0,2},{2,4},{4,6},{6,8},{8,10},{10,12},{12,14},{14,0},{1,3},{3,5},... | collective-permute-start | bytes 2359304 | tf_op jit(solution)/shard_map/ppermute | solution.py:32

commit v5 on v4

--- a/solution.py
+++ b/solution.py
@@ -15,7 +15,7 @@
 ROWS = 32
 LANES = 128
 TILE = 256
-VMEM_BYTES = 24 * 1024 * 1024
+VMEM_BYTES = 60 * 1024 * 1024
 SLOT_LOW, WALL_WEST, WALL_EAST, WALL_OUTER, WET, MOVE = 0, 1, 3, 5, 7, 13
 CONTROLS = 16
 CHUNKS = 4
@@ -157,14 +157,14 @@
     device = lax.axis_index("xb") * 2 + lax.axis_index("yb")
     wait_all(copies[:3])
     first = device * 2
-    low = jnp.where(neighbours[first, 3] == first + 1, 0, 1)
+    low = jnp.where(neighbours[3, first] == first + 1, 0, 1)
     ctl[SLOT_LOW] = low
     for position in range(2):
         slot = low if position == 0 else 1 - low
         tile = first + slot
-        ctl[WALL_WEST + position] = (neighbours[tile, 0] < 0).astype(jnp.int32)
-        ctl[WALL_EAST + position] = (neighbours[tile, 1] < 0).astype(jnp.int32)
-        ctl[WALL_OUTER + position] = (neighbours[tile, 2 + position] < 0).astype(jnp.int32)
+        ctl[WALL_WEST + position] = (neighbours[0, tile] < 0).astype(jnp.int32)
+        ctl[WALL_EAST + position] = (neighbours[1, tile] < 0).astype(jnp.int32)
+        ctl[WALL_OUTER + position] = (neighbours[2 + position, tile] < 0).astype(jnp.int32)
     for step in range(STEPS):
         for slot in range(2):
             ctl[WET + 2 * step + slot] = wet[step, first + slot]
@@ -555,7 +555,7 @@
     return pl.BlockSpec(memory_space=pl.ANY)
 
 
-def call(kernel, outs, out_specs, in_specs, flops, scratch=(), aliases=None):
+def call(kernel, outs, out_specs, in_specs, flops, scratch=(), aliases=None, room=VMEM_BYTES):
     return pl.pallas_call(
         kernel,
         scratch_shapes=scratch,
@@ -563,7 +563,7 @@
         out_shape=outs,
         in_specs=in_specs,
         out_specs=out_specs,
-        compiler_params=pltpu.CompilerParams(vmem_limit_bytes=VMEM_BYTES),
+        compiler_params=pltpu.CompilerParams(vmem_limit_bytes=room),
         cost_estimate=pl.CostEstimate(flops=flops, bytes_accessed=4 << 20, transcendentals=0),
     )
 
@@ -596,12 +596,12 @@
         [
             whole,
             part,
-            pltpu.SMEM(neighbours.shape, jnp.int32),
+            pltpu.SMEM(neighbours.shape[::-1], jnp.int32),
             pltpu.SMEM(wet.shape, jnp.int32),
             pltpu.SMEM(moves.shape, jnp.int32),
             pltpu.SemaphoreType.DMA((6,)),
         ],
-    )(state, bed, neighbours, wet, moves)
+    )(state, bed, neighbours.T, wet, moves)
     ground = None
     for step in range(STEPS):
         got = spread(out)
@@ -629,14 +629,14 @@
             _, out, columns = outs
     arrived = shifted(outs[1], "xb", 1)
     leaving = call(
-        second_leaving, tile_shape, anywhere(), [smem(), anywhere(), anywhere()], 1 << 20, sem
+        second_leaving, tile_shape, anywhere(), [smem(), anywhere(), anywhere()], 1 << 20, sem, room=1 << 20
     )(ctl, state, arrived)
     arrived_next = shifted(leaving, "xb", 1)
     final = call(
-        keep_rest, shape, anywhere(), [smem(), anywhere(), anywhere()], 1 << 20, sem
+        keep_rest, shape, anywhere(), [smem(), anywhere(), anywhere()], 1 << 20, sem, room=1 << 20
     )(ctl, state, arrived)
     return call(
-        keep_last, shape, anywhere(), [smem(), anywhere(), anywhere()], 1 << 20, sem, {2: 0}
+        keep_last, shape, anywhere(), [smem(), anywhere(), anywhere()], 1 << 20, sem, {2: 0}, 1 << 20
     )(ctl, arrived_next, final)
 
 

time: 114 us -> 107 us (0.939)
  local copies, waits for them, and re-layouts: 16.2 us -> 4.14 us
  Pallas kernels: 34.6 us -> 40.8 us
    unnamed x33 -> x12, local copies, waits for them, and re-layouts: 16.2 us -> 4.14 us
    pallas_call x3, Pallas kernels: 15.8 us -> 19.9 us  [body(): call(rates, shape, hbm(), [smem(), hbm(), hbm()], 16 << 20, [whole, part,...]
    pallas_call x3, Pallas kernels: 12.9 us -> 14.7 us  [body(): call(functools.partial(update, step), (shape,) + extra, (hbm(), vmem(), v...]
    all_to_all x3, starting transfers between devices: 16.9 us -> 15.7 us  [spread(): lax.all_to_all(fast, ('xb', 'yb'), split_axis=0, concat_axis=0, tiled=True)]
  transfers between devices with their start and end apart: 5 -> 5, of which waited for: 4 -> 5; matrix products, arithmetic and copies ran while one was open for 0% -> 0% of each run, Pallas kernels for 15% -> 20%
where the time goes in v5:
time: 107 us
  waiting for transfers between devices  45.2 us (42%)
  Pallas kernels  40.8 us (38%)
  starting transfers between devices  16.4 us (15%)
  local copies, waits for them, and re-layouts  4.14 us (4%)
    ppermute x2, waiting for transfers between devices, shifted(): return lax.ppermute(value, axis, pairs)  39.3 us
    pallas_call x3, Pallas kernels, body(): call(rates, shape, hbm(), [smem(), hbm(), hbm()], 16 << 20, [whole, part,...  19.9 us
    all_to_all x3, starting transfers between devices, spread(): lax.all_to_all(fast, ('xb', 'yb'), split_axis=0, concat_axis=0, tiled=True)  15.7 us
    pallas_call x3, Pallas kernels, body(): call(functools.partial(update, step), (shape,) + extra, (hbm(), vmem(), v...  14.7 us
    all_to_all x3, waiting for transfers between devices, spread(): lax.all_to_all(fast, ('xb', 'yb'), split_axis=0, concat_axis=0, tiled=True)  5.91 us
    unnamed x12, local copies, waits for them, and re-layouts  4.14 us
    pallas_call x1, Pallas kernels, body(): call(opening, (f32(16 * devices, TILE), f32(8, TILE), jax.ShapeDtypeStruc...  2.69 us
  transfers between devices with their start and end apart: 5, of which 5 were waited for; matrix products, arithmetic and copies ran while one was open for 0% of the time, Pallas kernels for 20%

profile of v5, /device:TPU:0, one launch (start us, length us, event | category | flops | bytes accessed | tf_op | source)
XLA Modules:
  0.0 106.8 jit_solution(3588090623942657851)
XLA Ops:
  0.0 2.7 %shard_map.64 = (f32[256,256]{1,0:T(8,128)}, f32[8,256]{1,0:T(8,128)}, s32[16]{0:T(128)}) custom-call(f32[2,3,256,256]{3,2,1,0:T(8,128)} %state_in.5, f32[2,256,256]{2,1,0:T(8,128)} %bed_in.7, s32[4,32]{1,0:T(4,128)} %bitcast.16, s32[3,32]{1,0:T(4,128)} %wet_in.1, s32[3,16]{1,0:T(4,128)} %moves_in.1), custom_call_target="tpu_custom_call" | custom-call | flops 4194304 | bytes 4194304 | tf_op jit(solution)/shard_map/pallas_call | solution.py:586
  2.7 7.4 %all-to-all-start = ((f32[16,16,256]{2,1,0:T(8,128)}), f32[16,16,256]{2,1,0:T(8,128)S(1)}, u32[]{:S(2)}, u32[]{:S(2)}) async-start(f32[16,16,256]{2,1,0:T(8,128)} %bitcast.13), calls=%async_computation | async-start | bytes 524288 | tf_op jit(solution)/shard_map/all_to_all | solution.py:576
  10.1 6.6 %shard_map.65.rate_in = f32[2,3,256,256]{3,2,1,0:T(8,128)} custom-call(s32[16]{0:T(128)} %get-tuple-element.16.ctl, f32[2,3,256,256]{3,2,1,0:T(8,128)} %state_in.5, f32[2,256,256]{2,1,0:T(8,128)} %bed_in.7), custom_call_target="tpu_custom_call" | custom-call | flops 16777216 | bytes 4194304 | tf_op jit(solution)/shard_map/pallas_call | solution.py:609
  16.8 3.4 %all-to-all-done = f32[16,16,256]{2,1,0:T(8,128)S(1)} async-done(((f32[16,16,256]{2,1,0:T(8,128)}), f32[16,16,256]{2,1,0:T(8,128)S(1)}, u32[]{:S(2)}, u32[]{:S(2)}) %all-to-all-start) | async-done | bytes 262176 | tf_op jit(solution)/shard_map/all_to_all | solution.py:576
  20.1 0.0 copy-start.3
  20.1 0.7 copy-done.3
  20.8 5.1 %shard_map.66 = (f32[2,3,256,256]{3,2,1,0:T(8,128)}, f32[128,256]{1,0:T(8,128)}, f32[8,256]{1,0:T(8,128)}) custom-call(s32[16]{0:T(128)} %get-tuple-element.16.ctl, f32[256,256]{1,0:T(8,128)} %bitcast.7, f32[256,256]{1,0:T(8,128)} %bitcast.8, f32[8,256]{1,0:T(8,128)} %get-tuple-element.18.columns, f32[2,3,256,256]{3,2,1,0:T(8,128)} %state_in.5, ...), custom_call_target="tpu_custom_call" | custom-call | flops 8388608 | bytes 4194304 | tf_op jit(solution)/shard_map/pallas_call | solution.py:619
  26.0 3.5 %all-to-all-start.1 = ((f32[16,8,256]{2,1,0:T(8,128)}), f32[16,8,256]{2,1,0:T(8,128)S(1)}, u32[]{:S(2)}, u32[]{:S(2)}) async-start(f32[16,8,256]{2,1,0:T(8,128)} %bitcast.15), calls=%async_computation.1 | async-start | bytes 262144 | tf_op jit(solution)/shard_map/all_to_all | solution.py:576
  29.5 6.6 %shard_map.67.rate_in = f32[2,3,256,256]{3,2,1,0:T(8,128)} custom-call(s32[16]{0:T(128)} %get-tuple-element.16.ctl, f32[2,3,256,256]{3,2,1,0:T(8,128)} %get-tuple-element.21.state_in, f32[2,256,256]{2,1,0:T(8,128)} %bed_in.7), custom_call_target="tpu_custom_call" | custom-call | flops 16777216 | bytes 4194304 | tf_op jit(solution)/shard_map/pallas_call | solution.py:609
  36.2 1.2 %all-to-all-done.1 = f32[16,8,256]{2,1,0:T(8,128)S(1)} async-done(((f32[16,8,256]{2,1,0:T(8,128)}), f32[16,8,256]{2,1,0:T(8,128)S(1)}, u32[]{:S(2)}, u32[]{:S(2)}) %all-to-all-start.1) | async-done | bytes 131104 | tf_op jit(solution)/shard_map/all_to_all | solution.py:576
  37.4 0.0 copy-start.4
  37.4 0.7 copy-done.4
  38.1 5.1 %shard_map.68 = (f32[2,3,256,256]{3,2,1,0:T(8,128)}, f32[128,256]{1,0:T(8,128)}, f32[8,256]{1,0:T(8,128)}) custom-call(s32[16]{0:T(128)} %get-tuple-element.16.ctl, f32[128,256]{1,0:T(8,128)} %bitcast.11, f32[256,256]{1,0:T(8,128)} %bitcast.9, f32[8,256]{1,0:T(8,128)} %get-tuple-element.20.columns, f32[2,3,256,256]{3,2,1,0:T(8,128)} %get-tuple-element.21.state_in, ...), custom_call_target="tpu_custom_call" | custom-call | flops 8388608 | bytes 4194304 | tf_op jit(solution)/shard_map/pallas_call | solution.py:619
  43.1 4.8 %all-to-all-start.2 = ((f32[16,8,256]{2,1,0:T(8,128)}), f32[16,8,256]{2,1,0:T(8,128)S(1)}, u32[]{:S(2)}, u32[]{:S(2)}) async-start(f32[16,8,256]{2,1,0:T(8,128)} %bitcast.14), calls=%async_computation.2 | async-start | bytes 262144 | tf_op jit(solution)/shard_map/all_to_all | solution.py:576
  47.9 6.6 %shard_map.69.rate_in = f32[2,3,256,256]{3,2,1,0:T(8,128)} custom-call(s32[16]{0:T(128)} %get-tuple-element.16.ctl, f32[2,3,256,256]{3,2,1,0:T(8,128)} %get-tuple-element.24.state_in, f32[2,256,256]{2,1,0:T(8,128)} %bed_in.7), custom_call_target="tpu_custom_call" | custom-call | flops 16777216 | bytes 4194304 | tf_op jit(solution)/shard_map/pallas_call | solution.py:609
  54.6 1.3 %all-to-all-done.2 = f32[16,8,256]{2,1,0:T(8,128)S(1)} async-done(((f32[16,8,256]{2,1,0:T(8,128)}), f32[16,8,256]{2,1,0:T(8,128)S(1)}, u32[]{:S(2)}, u32[]{:S(2)}) %all-to-all-start.2) | async-done | bytes 131104 | tf_op jit(solution)/shard_map/all_to_all | solution.py:576
  55.8 0.0 copy-start.5
  55.8 0.6 copy-done.5
  56.5 0.0 copy-start.2
  56.5 4.5 %shard_map.70 = (f32[2,3,256,256]{3,2,1,0:T(8,128)}, f32[3,256,256]{2,1,0:T(8,128)}) custom-call(s32[16]{0:T(128)} %get-tuple-element.16.ctl, f32[128,256]{1,0:T(8,128)} %bitcast.12, f32[256,256]{1,0:T(8,128)} %bitcast.10, f32[8,256]{1,0:T(8,128)} %get-tuple-element.23.columns, f32[2,3,256,256]{3,2,1,0:T(8,128)} %get-tuple-element.24.state_in, ...), custom_call_target="tpu_custom_call" | custom-call | flops 8388608 | bytes 4194304 | tf_op jit(solution)/shard_map/pallas_call | solution.py:619
  61.0 0.7 collective-permute-start
  61.7 21.0 %collective-permute-done.arrived = f32[3,256,256]{2,1,0:T(8,128)S(1)} collective-permute-done((f32[3,256,256]{2,1,0:T(8,128)}, f32[3,256,256]{2,1,0:T(8,128)S(1)}, u32[]{:S(2)}, u32[]{:S(2)}) %collective-permute-start) | collective-permute-done | bytes 786464 | tf_op jit(solution)/shard_map/ppermute | solution.py:32
  82.7 0.0 copy-done.2
  82.7 0.0 copy-start
  82.7 1.4 %copy-done = f32[2,3,256,256]{3,2,1,0:T(8,128)S(1)} copy-done((f32[2,3,256,256]{3,2,1,0:T(8,128)S(1)}, f32[2,3,256,256]{3,2,1,0:T(8,128)}, u32[]{:S(2)}) %copy-start) | copy-done | bytes 1572888
  84.1 0.0 copy-start.1
  84.1 0.6 shard_map.71
  84.8 0.1 collective-permute-start.1
  84.8 0.7 copy-done.1
  85.6 1.4 %shard_map.72.before = f32[2,3,256,256]{3,2,1,0:T(8,128)} custom-call(s32[16]{0:T(128)S(1)} %copy-done.2, f32[2,3,256,256]{3,2,1,0:T(8,128)S(1)} %copy-done.1, f32[3,256,256]{2,1,0:T(8,128)S(1)} %collective-permute-done.arrived), custom_call_target="tpu_custom_call" | custom-call | flops 1048576 | bytes 4194304 | tf_op jit(solution)/shard_map/pallas_call | solution.py:635
  87.0 18.3 %collective-permute-done.1.arrived = f32[3,256,256]{2,1,0:T(8,128)S(1)} collective-permute-done((f32[3,256,256]{2,1,0:T(8,128)S(1)}, f32[3,256,256]{2,1,0:T(8,128)S(1)}, u32[]{:S(2)}, u32[]{:S(2)}) %collective-permute-start.1) | collective-permute-done | bytes 786464 | tf_op jit(solution)/shard_map/ppermute | solution.py:32
  105.3 1.4 %shard_map.73 = f32[2,3,256,256]{3,2,1,0:T(8,128)} custom-call(s32[16]{0:T(128)S(1)} %copy-done.2, f32[3,256,256]{2,1,0:T(8,128)S(1)} %collective-permute-done.1.arrived, f32[2,3,256,256]{3,2,1,0:T(8,128)} %shard_map.72.before), custom_call_target="tpu_custom_call", output_to_operand_aliasing={{}: (2, {})} | custom-call | flops 1048576 | bytes 4194304 | tf_op jit(solution)/shard_map/pallas_call | solution.py:638
Async XLA Ops:
  2.7 17.4 %all-to-all-start = ((f32[16,16,256]{2,1,0:T(8,128)}), f32[16,16,256]{2,1,0:T(8,128)S(1)}, u32[]{:S(2)}, u32[]{:S(2)}) async-start(f32[16,16,256]{2,1,0:T(8,128)} %bitcast.13), calls=%async_computation | async-start | bytes 524288 | tf_op jit(solution)/shard_map/all_to_all | solution.py:576
  20.1 0.7 copy-start.3
  26.0 11.4 %all-to-all-start.1 = ((f32[16,8,256]{2,1,0:T(8,128)}), f32[16,8,256]{2,1,0:T(8,128)S(1)}, u32[]{:S(2)}, u32[]{:S(2)}) async-start(f32[16,8,256]{2,1,0:T(8,128)} %bitcast.15), calls=%async_computation.1 | async-start | bytes 262144 | tf_op jit(solution)/shard_map/all_to_all | solution.py:576
  37.4 0.7 copy-start.4
  43.1 12.7 %all-to-all-start.2 = ((f32[16,8,256]{2,1,0:T(8,128)}), f32[16,8,256]{2,1,0:T(8,128)S(1)}, u32[]{:S(2)}, u32[]{:S(2)}) async-start(f32[16,8,256]{2,1,0:T(8,128)} %bitcast.14), calls=%async_computation.2 | async-start | bytes 262144 | tf_op jit(solution)/shard_map/all_to_all | solution.py:576
  55.8 0.6 copy-start.5
  56.5 26.2 %copy-start.2 = (s32[16]{0:T(128)S(1)}, s32[16]{0:T(128)}, u32[]{:S(2)}) copy-start(s32[16]{0:T(128)} %get-tuple-element.16.ctl) | copy-start | bytes 196
  61.0 21.7 %collective-permute-start = (f32[3,256,256]{2,1,0:T(8,128)}, f32[3,256,256]{2,1,0:T(8,128)S(1)}, u32[]{:S(2)}, u32[]{:S(2)}) collective-permute-start(f32[3,256,256]{2,1,0:T(8,128)} %get-tuple-element.26), channel_id=1, source_target_pairs={{0,2},{2,4},{4,6},{6,8},{8,10},{10,12},{12,14},{14,0},{1,3},{3,5},... | collective-permute-start | bytes 2359304 | tf_op jit(solution)/shard_map/ppermute | solution.py:32
  82.7 1.4 %copy-start = (f32[2,3,256,256]{3,2,1,0:T(8,128)S(1)}, f32[2,3,256,256]{3,2,1,0:T(8,128)}, u32[]{:S(2)}) copy-start(f32[2,3,256,256]{3,2,1,0:T(8,128)} %get-tuple-element.25.state) | copy-start | bytes 4718596
  84.1 1.4 %copy-start.1 = (f32[2,3,256,256]{3,2,1,0:T(8,128)S(1)}, f32[2,3,256,256]{3,2,1,0:T(8,128)}, u32[]{:S(2)}) copy-start(f32[2,3,256,256]{3,2,1,0:T(8,128)} %get-tuple-element.25.state) | copy-start | bytes 4718596
  84.8 20.6 %collective-permute-start.1 = (f32[3,256,256]{2,1,0:T(8,128)S(1)}, f32[3,256,256]{2,1,0:T(8,128)S(1)}, u32[]{:S(2)}, u32[]{:S(2)}) collective-permute-start(f32[3,256,256]{2,1,0:T(8,128)S(1)} %shard_map.71), channel_id=1, source_target_pairs={{0,2},{2,4},{4,6},{6,8},{8,10},{10,12},{12,14},{14,0},{1,3},{3,5},... | collective-permute-start | bytes 2359304 | tf_op jit(solution)/shard_map/ppermute | solution.py:32

commit v6 on v5

--- a/solution.py
+++ b/solution.py
@@ -17,7 +17,10 @@
 TILE = 256
 VMEM_BYTES = 60 * 1024 * 1024
 SLOT_LOW, WALL_WEST, WALL_EAST, WALL_OUTER, WET, MOVE = 0, 1, 3, 5, 7, 13
-CONTROLS = 16
+WET_FIRST, WET_SECOND = 16, 19
+CONTROLS = 24
+EARLY = 192
+LATE = TILE - EARLY + 16
 CHUNKS = 4
 TOP = 6
 SCALE = 0.5 / SPACING
@@ -139,8 +142,8 @@
 
 
 def opening(
-    state_in, bed_in, neighbours_in, wet_in, moves_in,
-    out, columns, ctl,
+    state_in, bed_in, manning_in, neighbours_in, wet_in, moves_in,
+    out, columns, ctl, leaving,
     state, bed, neighbours, wet, moves, sems,
 ):
     copies = start_all(
@@ -169,6 +172,22 @@
         for slot in range(2):
             ctl[WET + 2 * step + slot] = wet[step, first + slot]
         ctl[MOVE + step] = moves[step, device]
+    early = early_copies(moves[0, device], state_in, bed_in, manning_in, leaving, sems, 6)
+    for copy in early:
+        copy.start()
+    count = lax.axis_size("xb")
+    upper = lax.axis_index("yb")
+    column = lax.axis_index("xb")
+    source = lax.rem(column + count - 1, count) * 2 + upper
+    before = lax.rem(column + count - 2, count) * 2 + upper
+    again = moves[0, source] == moves[1, source]
+    tile_first = source * 2 + moves[0, source]
+    tile_second = jnp.where(
+        again, before * 2 + moves[0, before], source * 2 + 1 - moves[0, source]
+    )
+    for step in range(STEPS):
+        ctl[WET_FIRST + step] = wet[step, tile_first]
+        ctl[WET_SECOND + step] = wet[step, tile_second]
 
     total = jnp.zeros((ROWS, TILE), jnp.float32)
     for slot in range(2):
@@ -183,6 +202,47 @@
         total = jnp.maximum(total, jnp.where(wet[0, first + slot] > 0, best, 0.0))
     copies[5].wait()
     messages(ctl, state, bed, jnp.max(total, keepdims=True), out, columns)
+    wait_all(early)
+
+
+def early_copies(slot, state_in, bed_in, manning_in, leaving, sems, first):
+    rows = slice(0, EARLY)
+    pairs = (
+        (state_in.at[slot, :, rows], leaving.at[0:3]),
+        (bed_in.at[slot, rows], leaving.at[3]),
+        (manning_in.at[slot, rows], leaving.at[4]),
+    )
+    return [
+        pltpu.make_async_copy(src, dst, sems.at[first + k]) for k, (src, dst) in enumerate(pairs)
+    ]
+
+
+def rates_and_leaving(
+    ctl, state_in, bed_in, state_first, manning_in, arrived, rate_out, leaving,
+    state, bed, rate, sems, moving,
+):
+    again = ctl[MOVE] == ctl[MOVE + 1]
+    passed = pltpu.make_async_copy(arrived, leaving, moving.at[0])
+    own = early_copies(1 - ctl[MOVE], state_first, bed_in, manning_in, leaving, moving, 1)
+
+    @pl.when(again)
+    def _():
+        passed.start()
+
+    @pl.when(jnp.logical_not(again))
+    def _():
+        for copy in own:
+            copy.start()
+
+    rates(ctl, state_in, bed_in, rate_out, state, bed, rate, sems)
+
+    @pl.when(again)
+    def _():
+        passed.wait()
+
+    @pl.when(jnp.logical_not(again))
+    def _():
+        wait_all(own)
 
 
 def rates(ctl, state_in, bed_in, rate_out, state, bed, rate, sems):
@@ -346,6 +406,192 @@
     wait_all(outgoing)
 
 
+def moved_on(old, slopes, rough, delta, wet_now):
+    h, hu, hv = (value - delta * slope for value, slope in zip(old, slopes))
+    inverse = 1.0 / h
+    u = hu * inverse
+    v = hv * inverse
+    speed = jnp.sqrt(u * u + v * v)
+    power = jnp.exp((-4.0 / 3.0) * jnp.log(jnp.abs(h)))
+    drag = (GRAVITY * delta) * (rough * rough) * (speed * power)
+    factor = 1.0 / (1.0 + drag)
+    fresh = (h, hu * factor, hv * factor)
+    return tuple(jnp.where(wet_now, new, value) for new, value in zip(fresh, old))
+
+
+def repeat_steps(ctl, wet_from, deltas, early, work, other, sems):
+    chunk = EARLY // 3
+    incoming = []
+    for part in range(3):
+        rows = slice(part * chunk, (part + 1) * chunk)
+        incoming += start_all(((early.at[:, rows], work.at[:, rows]),), sems, part)
+    row_ids = lax.broadcasted_iota(jnp.int32, (ROWS, TILE), 0)
+    lane = lax.broadcasted_iota(jnp.int32, (ROWS, LANES), 1)
+    start = tuple(jnp.zeros((1, TILE), jnp.float32) for _ in range(4))
+
+    def halves(value):
+        return value[:, :LANES], value[:, LANES:]
+
+    def right_of(value):
+        low, high = (pltpu.roll(part, LANES - 1, 1) for part in halves(value))
+        return jnp.concatenate([jnp.where(lane == LANES - 1, high, low), high], 1)
+
+    def left_of(value):
+        low, high = (pltpu.roll(part, 1, 1) for part in halves(value))
+        return jnp.concatenate([low, jnp.where(lane == 0, low, high)], 1)
+
+    def down(value):
+        return pltpu.roll(value, ROWS + 7, 0)[:ROWS]
+
+    for step in range(STEPS):
+        source, target = (work, other) if step % 2 == 0 else (other, work)
+        delta = deltas[step][0:1, :]
+        wet_now = flag(ctl, wet_from + step)
+
+        def group(index, carry, source=source, target=target, delta=delta, wet_now=wet_now):
+            base = pl.multiple_of(index * ROWS, ROWS)
+            rows = pl.ds(base, ROWS)
+            after = pl.ds(pl.multiple_of(jnp.minimum(base + ROWS, EARLY - 8), 8), 8)
+            refs = [source.at[field] for field in range(3)] + [work.at[3]]
+            fields = [jnp.concatenate([ref[rows, :], ref[after, :]], 0) for ref in refs]
+            cells_x, cells_y = cell(*fields[:3])
+            here_x = tuple(value[:ROWS] for value in cells_x)
+            here_y = tuple(value[:ROWS] for value in cells_y)
+            faces_x = face(here_x, tuple(down(value) for value in cells_x))
+            turned = tuple(pltpu.roll(value, 1, 0) for value in faces_x)
+            change_x = tuple(
+                value - jnp.where(row_ids == 0, before, moved)
+                for value, before, moved in zip(faces_x, carry[:3], turned)
+            )
+            ground = fields[3][:ROWS]
+            ground_up = pltpu.roll(ground, 1, 0)
+            slope_x = down(fields[3]) - jnp.where(row_ids == 0, carry[3], ground_up)
+            carried = tuple(value[0:1, :] for value in turned) + (ground_up[0:1, :],)
+            faces_y = face(here_y, tuple(right_of(value) for value in here_y))
+            change_y = tuple(value - left_of(value) for value in faces_y)
+            slope_y = right_of(ground) - left_of(ground)
+            old = tuple(value[:ROWS] for value in fields[:3])
+            weight = SLOPE * old[0]
+            slopes = (
+                SCALE * (change_x[0] + change_y[0]),
+                SCALE * (change_x[1] + change_y[2]) + weight * slope_x,
+                SCALE * (change_x[2] + change_y[1]) + weight * slope_y,
+            )
+            for field, value in enumerate(
+                moved_on(old, slopes, work[4, rows, :], delta, wet_now)
+            ):
+                target[field, rows, :] = value
+            return carried
+
+        per_chunk = chunk // ROWS
+        if step == 0:
+            carry = start
+            incoming[0].wait()
+            for part in range(3):
+                if part < 2:
+                    incoming[part + 1].wait()
+                carry = lax.fori_loop(part * per_chunk, (part + 1) * per_chunk, group, carry)
+        else:
+            lax.fori_loop(0, EARLY // ROWS, group, start)
+
+
+def late_rows(tile, late):
+    row = sublanes()
+    kept = EARLY - 8
+    lane = lax.broadcasted_iota(jnp.int32, (8, LANES), 1)
+    for field in range(3):
+        late[field, 0:8, :] = jnp.where(
+            row < 3, tile[field, 0:8, :], tile[field, kept : kept + 8, :]
+        )
+        late[field, 8 : TILE - kept, :] = tile[field, kept + 8 :, :]
+        packed = [None, None]
+        for block in range(EARLY // 8):
+            rows = slice(8 * block, 8 * block + 8)
+            sides = jnp.where(lane < 64, tile[field, rows, :LANES], tile[field, rows, LANES:])
+            turned = pltpu.roll(sides, (3 + 8 * block) % LANES, 1)
+            which = block // 16
+            packed[which] = (
+                turned
+                if packed[which] is None
+                else jnp.where(lane // 8 == block % 16, turned, packed[which])
+            )
+        late[field, TILE - kept :, :] = jnp.concatenate(packed, 1)
+
+
+def merge(late, early, tile):
+    row = sublanes()
+    kept = EARLY - 8
+    lane = lax.broadcasted_iota(jnp.int32, (8, LANES), 1)
+    for field in range(3):
+        first = late[field, 0:8, :]
+        for block in range(EARLY // 8):
+            rows = slice(8 * block, 8 * block + 8)
+            which = block // 16
+            packed = late[field, TILE - kept :, which * LANES : (which + 1) * LANES]
+            sides = pltpu.roll(packed, (-3 - 8 * block) % LANES, 1)
+            value = early[field, rows, :]
+            value = jnp.concatenate(
+                [
+                    jnp.where(lane < 3, sides, value[:, :LANES]),
+                    jnp.where(lane >= LANES - 3, sides, value[:, LANES:]),
+                ],
+                1,
+            )
+            if block == 0:
+                value = jnp.where(row < 3, first, value)
+            if block == EARLY // 8 - 1:
+                value = jnp.where(row < 5, value, first)
+            tile[field, rows, :] = value
+        tile[field, EARLY:, :] = late[field, 8 : TILE - kept, :]
+
+
+def repeat_second(ctl, delta0, delta1, delta2, early, tile, work, sems):
+    repeat_steps(ctl, WET_SECOND, (delta0, delta1, delta2), early, work, tile, sems)
+
+
+def repeat_first(
+    ctl, delta0, delta1, delta2, early, late, staying, out, work, other, tile, sems
+):
+    rest = out.at[1 - ctl[MOVE + 1]]
+    again = ctl[MOVE] == ctl[MOVE + 1]
+
+    @pl.when(again)
+    def _():
+        copy = pltpu.make_async_copy(staying, rest, sems.at[3])
+        copy.start()
+        copy.wait()
+
+    @pl.when(jnp.logical_not(again))
+    def _():
+        repeat_steps(ctl, WET_FIRST, (delta0, delta1, delta2), early, work, other, sems)
+        merge(late, other, tile)
+        copy = pltpu.make_async_copy(tile, rest, sems.at[3])
+        copy.start()
+        copy.wait()
+
+
+def finish(ctl, late, early, before, out, tile, sems):
+    del before
+    merge(late, early, tile)
+    copy = pltpu.make_async_copy(tile, out.at[ctl[MOVE + 1]], sems.at[0])
+    copy.start()
+    copy.wait()
+
+
+def second_late(ctl, arrived, own, leaving, sems):
+    again = ctl[MOVE] == ctl[MOVE + 1]
+
+    @pl.when(again)
+    def _():
+        pltpu.make_async_copy(arrived, leaving, sems.at[0]).start()
+
+    @pl.when(jnp.logical_not(again))
+    def _():
+        pltpu.make_async_copy(own, leaving, sems.at[0]).start()
+
+    pltpu.make_async_copy(arrived, leaving, sems.at[0]).wait()
+
+
 def correct_rows(ctl, slot, got, ground, block, state, rate, bottom):
     position = jnp.where(ctl[SLOT_LOW] == slot, 0, 1)
     device = lax.axis_index("xb") * 2 + lax.axis_index("yb")
@@ -405,11 +651,11 @@
 def update(step, ctl, got, ground, columns, state_in, manning_in, rate_in, *rest):
     more = step + 1 < STEPS
     if more:
-        fresh_out, out, columns_out = rest[:3]
-        rest = rest[3:]
+        fresh_out, out, columns_out, delta_out = rest[:4]
+        rest = rest[4:]
     else:
-        fresh_out, leaving = rest[:2]
-        rest = rest[2:]
+        staying, late_first, late_second, delta_out = rest[:4]
+        rest = rest[4:]
     state, manning, rate, fresh, sems = rest
     half = TILE // 2
     parts = [(slot, slice(k * half, (k + 1) * half)) for slot in range(2) for k in range(2)]
@@ -433,6 +679,7 @@
     for peer in range(1, devices):
         tops = jnp.maximum(tops, got[peer * block : peer * block + 8, :])
     delta = (COURANT * SPACING) / tops[TOP : TOP + 1, :]
+    delta_out[...] = jnp.broadcast_to(delta, (8, TILE))
     fix = column_fix(got, ground, block, columns, None)
     facing = jnp.where(upper > 0, ctl[SLOT_LOW], 1 - ctl[SLOT_LOW])
     begin = pl.multiple_of((1 - upper) * LANES, LANES)
@@ -459,23 +706,9 @@
 
         def group(index, best, slot=slot, wet_now=wet_now):
             rows = pl.ds(pl.multiple_of(index * ROWS, ROWS), ROWS)
-            h0, hu0, hv0 = (state[slot, field, rows, :] for field in range(3))
-            h = h0 - delta * rate[slot, 0, rows, :]
-            hu = hu0 - delta * rate[slot, 1, rows, :]
-            hv = hv0 - delta * rate[slot, 2, rows, :]
-            rough = manning[slot, rows, :]
-            inverse = 1.0 / h
-            u = hu * inverse
-            v = hv * inverse
-            speed = jnp.sqrt(u * u + v * v)
-            power = jnp.exp((-4.0 / 3.0) * jnp.log(jnp.abs(h)))
-            drag = (GRAVITY * delta) * (rough * rough) * (speed * power)
-            factor = 1.0 / (1.0 + drag)
-            hu = hu * factor
-            hv = hv * factor
-            h = jnp.where(wet_now, h, h0)
-            hu = jnp.where(wet_now, hu, hu0)
-            hv = jnp.where(wet_now, hv, hv0)
+            old = tuple(state[slot, field, rows, :] for field in range(3))
+            slopes = tuple(rate[slot, field, rows, :] for field in range(3))
+            h, hu, hv = moved_on(old, slopes, manning[slot, rows, :], delta, wet_now)
             fresh[slot, 0, rows, :] = h
             fresh[slot, 1, rows, :] = hu
             fresh[slot, 2, rows, :] = hv
@@ -493,50 +726,19 @@
         if more:
             best = jnp.where(flag(ctl, WET + 2 * step + 2 + slot), best, 0.0)
             total = jnp.maximum(total, best)
-        outgoing += start_all(
-            ((fresh.at[slot, :, part_rows], fresh_out.at[slot, :, part_rows]),), sems, 12 + index
-        )
+        if more:
+            outgoing += start_all(
+                ((fresh.at[slot, :, part_rows], fresh_out.at[slot, :, part_rows]),),
+                sems,
+                12 + index,
+            )
     if more:
         messages(ctl, fresh, None, jnp.max(total, keepdims=True), out, columns_out)
     else:
-        outgoing += start_all(((fresh.at[ctl[MOVE]], leaving),), sems, 16)
+        outgoing += start_all(((fresh.at[1 - ctl[MOVE]], staying),), sems, 16)
+        late_rows(fresh.at[ctl[MOVE]], late_first)
+        late_rows(fresh.at[1 - ctl[MOVE]], late_second)
     wait_all(outgoing)
-
-
-def second_leaving(ctl, state, arrived, leaving, sems):
-    again = ctl[MOVE] == ctl[MOVE + 1]
-
-    @pl.when(again)
-    def _():
-        pltpu.make_async_copy(arrived, leaving, sems.at[0]).start()
-
-    @pl.when(jnp.logical_not(again))
-    def _():
-        pltpu.make_async_copy(state.at[1 - ctl[MOVE]], leaving, sems.at[0]).start()
-
-    pltpu.make_async_copy(arrived, leaving, sems.at[0]).wait()
-
-
-def keep_rest(ctl, state, arrived, out, sems):
-    rest = out.at[1 - ctl[MOVE + 1]]
-    again = ctl[MOVE] == ctl[MOVE + 1]
-
-    @pl.when(again)
-    def _():
-        pltpu.make_async_copy(state.at[1 - ctl[MOVE]], rest, sems.at[0]).start()
-
-    @pl.when(jnp.logical_not(again))
-    def _():
-        pltpu.make_async_copy(arrived, rest, sems.at[0]).start()
-
-    pltpu.make_async_copy(arrived, rest, sems.at[0]).wait()
-
-
-def keep_last(ctl, arrived, before, out, sems):
-    del before
-    copy = pltpu.make_async_copy(arrived, out.at[ctl[MOVE + 1]], sems.at[0])
-    copy.start()
-    copy.wait()
 
 
 def vmem():
@@ -583,15 +785,19 @@
     sem = [pltpu.SemaphoreType.DMA((1,))]
     whole = pltpu.VMEM(state.shape, jnp.float32)
     part = pltpu.VMEM(bed.shape, jnp.float32)
-    out, columns, ctl = call(
+    early_shape = f32(5, EARLY, TILE)
+    late_shape = f32(3, LATE, TILE)
+    delta_shape = f32(8, TILE)
+    out, columns, ctl, leaving = call(
         opening,
         (
             f32(16 * devices, TILE),
             f32(8, TILE),
             jax.ShapeDtypeStruct((CONTROLS,), jnp.int32),
+            early_shape,
         ),
-        (vmem(), vmem(), smem()),
-        [hbm()] * 5,
+        (vmem(), vmem(), smem(), hbm()),
+        [hbm()] * 6,
         4 << 20,
         [
             whole,
@@ -599,45 +805,91 @@
             pltpu.SMEM(neighbours.shape[::-1], jnp.int32),
             pltpu.SMEM(wet.shape, jnp.int32),
             pltpu.SMEM(moves.shape, jnp.int32),
-            pltpu.SemaphoreType.DMA((6,)),
+            pltpu.SemaphoreType.DMA((9,)),
         ],
-    )(state, bed, neighbours.T, wet, moves)
+    )(state, bed, manning, neighbours.T, wet, moves)
+    early_first = shifted(leaving, "xb", 1)
+    state_first = state
     ground = None
+    deltas = []
     for step in range(STEPS):
         got = spread(out)
         ground = got if step == 0 else ground
-        rate = call(
-            rates,
-            shape,
-            hbm(),
-            [smem(), hbm(), hbm()],
-            16 << 20,
-            [whole, part, whole, pltpu.SemaphoreType.DMA((3 * CHUNKS,))],
-        )(ctl, state, bed)
-        more = step + 1 < STEPS
-        extra = (f32(8 * devices, TILE), f32(8, TILE)) if more else (tile_shape,)
+        scratch = [whole, part, whole, pltpu.SemaphoreType.DMA((3 * CHUNKS,))]
+        if step == 1:
+            rate, leaving = call(
+                rates_and_leaving,
+                (shape, early_shape),
+                (hbm(), hbm()),
+                [smem()] + [hbm()] * 5,
+                16 << 20,
+                scratch + [pltpu.SemaphoreType.DMA((4,))],
+            )(ctl, state, bed, state_first, manning, early_first)
+            early_second = shifted(leaving, "xb", 1)
+        else:
+            rate = call(rates, shape, hbm(), [smem(), hbm(), hbm()], 16 << 20, scratch)(
+                ctl, state, bed
+            )
+        if step + 1 < STEPS:
+            shapes = (shape, f32(8 * devices, TILE), f32(8, TILE), delta_shape)
+            places = (hbm(), vmem(), vmem(), vmem())
+        else:
+            shapes = (tile_shape, late_shape, late_shape, delta_shape)
+            places = (hbm(), vmem(), vmem(), vmem())
         outs = call(
             functools.partial(update, step),
-            (shape,) + extra,
-            (hbm(), vmem(), vmem()) if more else (hbm(), hbm()),
+            shapes,
+            places,
             [smem(), vmem(), vmem(), vmem(), hbm(), hbm(), hbm()],
             8 << 20,
             [whole, part, whole, whole, pltpu.SemaphoreType.DMA((17,))],
         )(ctl, got, ground, columns, state, manning, rate)
-        state = outs[0]
-        if more:
-            _, out, columns = outs
-    arrived = shifted(outs[1], "xb", 1)
+        deltas.append(outs[3])
+        if step + 1 < STEPS:
+            state, out, columns, _ = outs
+    staying, late_first, late_second, _ = outs
+    late_arrived = shifted(late_first, "xb", 1)
+    small = 8 << 20
+    early_work = pltpu.VMEM(early_shape.shape, jnp.float32)
+    early_state = f32(3, EARLY, TILE)
+    second = call(
+        repeat_second,
+        early_state,
+        vmem(),
+        [smem()] + [vmem()] * 3 + [hbm()],
+        8 << 20,
+        [early_work, pltpu.SemaphoreType.DMA((3,))],
+        room=small,
+    )(ctl, *deltas, early_second)
     leaving = call(
-        second_leaving, tile_shape, anywhere(), [smem(), anywhere(), anywhere()], 1 << 20, sem, room=1 << 20
-    )(ctl, state, arrived)
-    arrived_next = shifted(leaving, "xb", 1)
+        second_late, late_shape, anywhere(), [smem(), anywhere(), anywhere()], 1 << 20, sem,
+        room=1 << 20,
+    )(ctl, late_arrived, late_second)
+    late_next = shifted(leaving, "xb", 1)
     final = call(
-        keep_rest, shape, anywhere(), [smem(), anywhere(), anywhere()], 1 << 20, sem, room=1 << 20
-    )(ctl, state, arrived)
+        repeat_first,
+        shape,
+        hbm(),
+        [smem()] + [vmem()] * 3 + [hbm(), vmem(), hbm()],
+        8 << 20,
+        [
+            early_work,
+            pltpu.VMEM(early_state.shape, jnp.float32),
+            pltpu.VMEM(tile_shape.shape, jnp.float32),
+            pltpu.SemaphoreType.DMA((4,)),
+        ],
+        room=small,
+    )(ctl, *deltas, early_first, late_arrived, staying)
     return call(
-        keep_last, shape, anywhere(), [smem(), anywhere(), anywhere()], 1 << 20, sem, {2: 0}, 1 << 20
-    )(ctl, arrived_next, final)
+        finish,
+        shape,
+        hbm(),
+        [smem(), vmem(), vmem(), hbm()],
+        1 << 20,
+        [pltpu.VMEM(tile_shape.shape, jnp.float32)] + sem,
+        {3: 0},
+        room=small,
+    )(ctl, late_next, second, final)
 
 
 def solution(mesh):

time: 107 us -> 171 us (1.60)
  Pallas kernels: 40.8 us -> 107 us
  waiting for transfers between devices: 45.2 us -> 38.2 us
  starting transfers between devices: 16.4 us -> 19.1 us
    pallas_call x9 -> x10, Pallas kernels: 38.1 us -> 74.8 us  [the longest x1 31.7 us: body(): call(rates_and_leaving, (shape, early_shape), (hbm(), hbm()), [smem()] +...]
    pallas_call x1, Pallas kernels: 2.69 us -> 32.4 us  [body(): call(opening, (f32(16 * devices, TILE), f32(8, TILE), jax.ShapeDtypeStruc...]
    ppermute x2 -> x4, waiting for transfers between devices: 39.3 us -> 10.1 us  [shifted(): return lax.ppermute(value, axis, pairs)]
    all_to_all x3, waiting for transfers between devices: 5.91 us -> 28.1 us  [spread(): lax.all_to_all(fast, ('xb', 'yb'), split_axis=0, concat_axis=0, tiled=True)]
    ppermute x2 -> x4, starting transfers between devices: 0.75 us -> 5.82 us  [shifted(): return lax.ppermute(value, axis, pairs)]
    all_to_all x3, starting transfers between devices: 15.7 us -> 13.3 us  [spread(): lax.all_to_all(fast, ('xb', 'yb'), split_axis=0, concat_axis=0, tiled=True)]
    unnamed x12 -> x22, local copies, waits for them, and re-layouts: 4.14 us -> 5.76 us
  transfers between devices with their start and end apart: 5 -> 7, of which waited for: 5 -> 3; matrix products, arithmetic and copies ran while one was open for 0% -> 0% of each run, Pallas kernels for 20% -> 43%
where the time goes in v6:
time: 171 us; the launch traced here: 170 us
  Pallas kernels  107 us (63%)
  waiting for transfers between devices  38.2 us (22%)
  starting transfers between devices  19.1 us (11%)
  local copies, waits for them, and re-layouts  5.76 us (3%)
    pallas_call x1, Pallas kernels, body(): call(opening, (f32(16 * devices, TILE), f32(8, TILE), jax.ShapeDtypeStruc...  32.4 us
    pallas_call x1, Pallas kernels, body(): call(rates_and_leaving, (shape, early_shape), (hbm(), hbm()), [smem()] +...  31.7 us
    all_to_all x3, waiting for transfers between devices, spread(): lax.all_to_all(fast, ('xb', 'yb'), split_axis=0, concat_axis=0, tiled=True)  28.1 us
    pallas_call x3, Pallas kernels, body(): call(functools.partial(update, step), shapes, places, [smem(), vmem(), vm...  15.5 us
    pallas_call x2, Pallas kernels, body(): call(rates, shape, hbm(), [smem(), hbm(), hbm()], 16 << 20, scratch)  13.3 us
    all_to_all x3, starting transfers between devices, spread(): lax.all_to_all(fast, ('xb', 'yb'), split_axis=0, concat_axis=0, tiled=True)  13.3 us
    ppermute x4, waiting for transfers between devices, shifted(): return lax.ppermute(value, axis, pairs)  10.1 us
    pallas_call x1, Pallas kernels, body(): call(repeat_first, shape, hbm(), [smem()] + [vmem()] * 3 + [hbm(), vmem()...  6.47 us
  transfers between devices with their start and end apart: 7, of which 3 were waited for; matrix products, arithmetic and copies ran while one was open for 0% of the time, Pallas kernels for 43%

profile of v6, /device:TPU:0, one launch (start us, length us, event | category | flops | bytes accessed | tf_op | source)
XLA Modules:
  0.0 170.5 jit_solution(5788649875318226577)
XLA Ops:
  0.0 32.4 %shard_map.64 = (f32[256,256]{1,0:T(8,128)}, f32[8,256]{1,0:T(8,128)}, s32[24]{0:T(128)}, f32[5,192,256]{2,1,0:T(8,128)}) custom-call(f32[2,3,256,256]{3,2,1,0:T(8,128)} %state_first.1, f32[2,256,256]{2,1,0:T(8,128)} %bed_in.7, f32[2,256,256]{2,1,0:T(8,128)} %manning_in.9, s32[4,32]{1,0:T(4,128)} %bitcast.16, s32[3,32]{1,0:T(4,128)} %wet_in.1, s32[3,16]{1,0:T(4,128)} %moves_in.1), custom_call_target="tpu_custom_call" | custom-call | flops 4194304 | bytes 4194304 | tf_op jit(solution)/shard_map/pallas_call | solution.py:791
  32.5 3.0 %collective-permute-start = (f32[5,192,256]{2,1,0:T(8,128)}, f32[5,192,256]{2,1,0:T(8,128)S(1)}, u32[]{:S(2)}, u32[]{:S(2)}) collective-permute-start(f32[5,192,256]{2,1,0:T(8,128)} %get-tuple-element.29), channel_id=1, source_target_pairs={{0,2},{2,4},{4,6},{6,8},{8,10},{10,12},{12,14},{14,0},{1,3},{3,5},... | collective-permute-start | bytes 2949128 | tf_op jit(solution)/shard_map/ppermute | solution.py:35
  35.5 5.0 %all-to-all-start = ((f32[16,16,256]{2,1,0:T(8,128)}), f32[16,16,256]{2,1,0:T(8,128)S(1)}, u32[]{:S(2)}, u32[]{:S(2)}) async-start(f32[16,16,256]{2,1,0:T(8,128)} %bitcast.13), calls=%async_computation | async-start | bytes 524288 | tf_op jit(solution)/shard_map/all_to_all | solution.py:778
  40.5 6.6 %shard_map.65.rate_in = f32[2,3,256,256]{3,2,1,0:T(8,128)} custom-call(s32[24]{0:T(128)} %get-tuple-element.23.ctl, f32[2,3,256,256]{3,2,1,0:T(8,128)} %state_first.1, f32[2,256,256]{2,1,0:T(8,128)} %bed_in.7), custom_call_target="tpu_custom_call" | custom-call | flops 16777216 | bytes 4194304 | tf_op jit(solution)/shard_map/pallas_call | solution.py:830
  47.1 18.0 %all-to-all-done = f32[16,16,256]{2,1,0:T(8,128)S(1)} async-done(((f32[16,16,256]{2,1,0:T(8,128)}), f32[16,16,256]{2,1,0:T(8,128)S(1)}, u32[]{:S(2)}, u32[]{:S(2)}) %all-to-all-start) | async-done | bytes 262176 | tf_op jit(solution)/shard_map/all_to_all | solution.py:778
  65.1 0.7 copy-done.8
  65.8 5.1 %shard_map.66 = (f32[2,3,256,256]{3,2,1,0:T(8,128)}, f32[128,256]{1,0:T(8,128)}, f32[8,256]{1,0:T(8,128)}, f32[8,256]{1,0:T(8,128)}) custom-call(s32[24]{0:T(128)} %get-tuple-element.23.ctl, f32[256,256]{1,0:T(8,128)} %bitcast.7, f32[256,256]{1,0:T(8,128)} %bitcast.8, f32[8,256]{1,0:T(8,128)} %get-tuple-element.25.columns, f32[2,3,256,256]{3,2,1,0:T(8,128)} %state_first.1, ...), custom_call_target="tpu_custom_call" | custom-call | flops 8388608 | bytes 4194304 | tf_op jit(solution)/shard_map/pallas_call | solution.py:839
  71.0 3.5 %all-to-all-start.1 = ((f32[16,8,256]{2,1,0:T(8,128)}), f32[16,8,256]{2,1,0:T(8,128)S(1)}, u32[]{:S(2)}, u32[]{:S(2)}) async-start(f32[16,8,256]{2,1,0:T(8,128)} %bitcast.14), calls=%async_computation.1 | async-start | bytes 262144 | tf_op jit(solution)/shard_map/all_to_all | solution.py:778
  74.5 0.0 collective-permute-done.arrived.early
  74.5 1.0 copy-done
  75.5 31.7 %shard_map.67 = (f32[2,3,256,256]{3,2,1,0:T(8,128)}, f32[5,192,256]{2,1,0:T(8,128)}) custom-call(s32[24]{0:T(128)} %get-tuple-element.23.ctl, f32[2,3,256,256]{3,2,1,0:T(8,128)} %get-tuple-element.28.state_in, f32[2,256,256]{2,1,0:T(8,128)} %bed_in.7, f32[2,3,256,256]{3,2,1,0:T(8,128)} %state_first.1, f32[2,256,256]{2,1,0:T(8,128)} %manning_in.9, ...), custom_call_target="tpu_custom_call" | custom-call | flops 16777216 | bytes 4194304 | tf_op jit(solution)/shard_map/pallas_call | solution.py:820
  107.2 1.9 %collective-permute-start.3 = (f32[5,192,256]{2,1,0:T(8,128)}, f32[5,192,256]{2,1,0:T(8,128)S(1)}, u32[]{:S(2)}, u32[]{:S(2)}) collective-permute-start(f32[5,192,256]{2,1,0:T(8,128)} %get-tuple-element.39), channel_id=1, source_target_pairs={{0,2},{2,4},{4,6},{6,8},{8,10},{10,12},{12,14},{14,0},{1,3},{3,5},... | collective-permute-start | bytes 2949128 | tf_op jit(solution)/shard_map/ppermute | solution.py:35
  109.0 0.0 all-to-all-done.1
  109.0 0.7 copy-done.9
  109.7 5.1 %shard_map.68 = (f32[2,3,256,256]{3,2,1,0:T(8,128)}, f32[128,256]{1,0:T(8,128)}, f32[8,256]{1,0:T(8,128)}, f32[8,256]{1,0:T(8,128)}) custom-call(s32[24]{0:T(128)} %get-tuple-element.23.ctl, f32[128,256]{1,0:T(8,128)} %bitcast.11, f32[256,256]{1,0:T(8,128)} %bitcast.9, f32[8,256]{1,0:T(8,128)} %get-tuple-element.27.columns, ...), custom_call_target="tpu_custom_call" | custom-call | flops 8388608 | bytes 4194304 | tf_op jit(solution)/shard_map/pallas_call | solution.py:839
  114.8 4.8 %all-to-all-start.2 = ((f32[16,8,256]{2,1,0:T(8,128)}), f32[16,8,256]{2,1,0:T(8,128)S(1)}, u32[]{:S(2)}, u32[]{:S(2)}) async-start(f32[16,8,256]{2,1,0:T(8,128)} %bitcast.15), calls=%async_computation.2 | async-start | bytes 262144 | tf_op jit(solution)/shard_map/all_to_all | solution.py:778
  119.6 6.6 %shard_map.69.rate_in = f32[2,3,256,256]{3,2,1,0:T(8,128)} custom-call(s32[24]{0:T(128)} %get-tuple-element.23.ctl, f32[2,3,256,256]{3,2,1,0:T(8,128)} %get-tuple-element.33.state_in, f32[2,256,256]{2,1,0:T(8,128)} %bed_in.7), custom_call_target="tpu_custom_call" | custom-call | flops 16777216 | bytes 4194304 | tf_op jit(solution)/shard_map/pallas_call | solution.py:830
  126.2 10.2 %all-to-all-done.2 = f32[16,8,256]{2,1,0:T(8,128)S(1)} async-done(((f32[16,8,256]{2,1,0:T(8,128)}), f32[16,8,256]{2,1,0:T(8,128)S(1)}, u32[]{:S(2)}, u32[]{:S(2)}) %all-to-all-start.2) | async-done | bytes 131104 | tf_op jit(solution)/shard_map/all_to_all | solution.py:778
  136.4 0.6 copy-done.10
  137.1 5.2 %shard_map.70 = (f32[3,256,256]{2,1,0:T(8,128)}, f32[3,80,256]{2,1,0:T(8,128)}, f32[3,80,256]{2,1,0:T(8,128)}, f32[8,256]{1,0:T(8,128)}) custom-call(s32[24]{0:T(128)} %get-tuple-element.23.ctl, f32[128,256]{1,0:T(8,128)} %bitcast.12, f32[256,256]{1,0:T(8,128)} %bitcast.10, f32[8,256]{1,0:T(8,128)} %get-tuple-element.32.columns, ...), custom_call_target="tpu_custom_call" | custom-call | flops 8388608 | bytes 4194304 | tf_op jit(solution)/shard_map/pallas_call | solution.py:839
  142.3 0.9 collective-permute-start.1
  143.2 10.1 %collective-permute-done.1.arrived.late = f32[3,80,256]{2,1,0:T(8,128)S(1)} collective-permute-done((f32[3,80,256]{2,1,0:T(8,128)}, f32[3,80,256]{2,1,0:T(8,128)S(1)}, u32[]{:S(2)}, u32[]{:S(2)}) %collective-permute-start.1) | collective-permute-done | bytes 245792 | tf_op jit(solution)/shard_map/ppermute | solution.py:35
  153.2 0.9 copy-done.3
  154.2 0.9 shard_map.71
  155.1 0.1 collective-permute-start.2
  155.2 1.1 copy-done.2
  156.3 0.7 copy-done.7
  157.0 6.5 %shard_map.73.before = f32[2,3,256,256]{3,2,1,0:T(8,128)} custom-call(s32[24]{0:T(128)S(1)} %copy-done.4, f32[8,256]{1,0:T(8,128)S(1)} %copy-done.5, f32[8,256]{1,0:T(8,128)S(1)} %copy-done.6, f32[8,256]{1,0:T(8,128)S(1)} %copy-done.7, f32[5,192,256]{2,1,0:T(8,128)S(1)} %copy-done.1, f32[3,80,256]{2,1,0:T(8,128)S(1)} %collective-permute-done.1.arrived.late, ...), custom_call_target="tpu_custom_call" | custom-call | flops 8388608 | bytes 4194304 | tf_op jit(solution)/shard_map/pallas_call | solution.py:869
  163.5 0.0 collective-permute-done.3.early
  163.5 5.4 %shard_map.72.early = f32[3,192,256]{2,1,0:T(8,128)S(1)} custom-call(s32[24]{0:T(128)S(1)} %copy-done.4, f32[8,256]{1,0:T(8,128)S(1)} %copy-done.5, f32[8,256]{1,0:T(8,128)S(1)} %copy-done.6, f32[8,256]{1,0:T(8,128)S(1)} %copy-done.7, f32[5,192,256]{2,1,0:T(8,128)S(1)} %collective-permute-done.3.early), custom_call_target="tpu_custom_call" | custom-call | flops 8388608 | bytes 4194304 | tf_op jit(solution)/shard_map/pallas_call | solution.py:855
  168.9 0.0 collective-permute-done.2.late
  168.9 1.6 shard_map.74
  (15 shorter events, 0.0 us)
Async XLA Ops:
  32.5 42.0 %collective-permute-start = (f32[5,192,256]{2,1,0:T(8,128)}, f32[5,192,256]{2,1,0:T(8,128)S(1)}, u32[]{:S(2)}, u32[]{:S(2)}) collective-permute-start(f32[5,192,256]{2,1,0:T(8,128)} %get-tuple-element.29), channel_id=1, source_target_pairs={{0,2},{2,4},{4,6},{6,8},{8,10},{10,12},{12,14},{14,0},{1,3},{3,5},... | collective-permute-start | bytes 2949128 | tf_op jit(solution)/shard_map/ppermute | solution.py:35
  35.5 29.6 %all-to-all-start = ((f32[16,16,256]{2,1,0:T(8,128)}), f32[16,16,256]{2,1,0:T(8,128)S(1)}, u32[]{:S(2)}, u32[]{:S(2)}) async-start(f32[16,16,256]{2,1,0:T(8,128)} %bitcast.13), calls=%async_computation | async-start | bytes 524288 | tf_op jit(solution)/shard_map/all_to_all | solution.py:778
  65.1 0.7 copy-start.8
  71.0 38.1 %all-to-all-start.1 = ((f32[16,8,256]{2,1,0:T(8,128)}), f32[16,8,256]{2,1,0:T(8,128)S(1)}, u32[]{:S(2)}, u32[]{:S(2)}) async-start(f32[16,8,256]{2,1,0:T(8,128)} %bitcast.14), calls=%async_computation.1 | async-start | bytes 262144 | tf_op jit(solution)/shard_map/all_to_all | solution.py:778
  74.5 1.0 copy-start
  107.2 56.3 %collective-permute-start.3 = (f32[5,192,256]{2,1,0:T(8,128)}, f32[5,192,256]{2,1,0:T(8,128)S(1)}, u32[]{:S(2)}, u32[]{:S(2)}) collective-permute-start(f32[5,192,256]{2,1,0:T(8,128)} %get-tuple-element.39), channel_id=1, source_target_pairs={{0,2},{2,4},{4,6},{6,8},{8,10},{10,12},{12,14},{14,0},{1,3},{3,5},... | collective-permute-start | bytes 2949128 | tf_op jit(solution)/shard_map/ppermute | solution.py:35
  109.0 0.7 copy-start.9
  114.8 21.6 %all-to-all-start.2 = ((f32[16,8,256]{2,1,0:T(8,128)}), f32[16,8,256]{2,1,0:T(8,128)S(1)}, u32[]{:S(2)}, u32[]{:S(2)}) async-start(f32[16,8,256]{2,1,0:T(8,128)} %bitcast.15), calls=%async_computation.2 | async-start | bytes 262144 | tf_op jit(solution)/shard_map/all_to_all | solution.py:778
  136.4 0.7 copy-start.10
  137.0 16.2 %copy-start.4 = (s32[24]{0:T(128)S(1)}, s32[24]{0:T(128)}, u32[]{:S(2)}) copy-start(s32[24]{0:T(128)} %get-tuple-element.23.ctl) | copy-start | bytes 292
  137.0 18.1 %copy-start.1 = (f32[5,192,256]{2,1,0:T(8,128)S(1)}, f32[5,192,256]{2,1,0:T(8,128)}, u32[]{:S(2)}) copy-start(f32[5,192,256]{2,1,0:T(8,128)} %copy-done) | copy-start | bytes 2949124
  137.0 18.1 %copy-start.5 = (f32[8,256]{1,0:T(8,128)S(1)}, f32[8,256]{1,0:T(8,128)}, u32[]{:S(2)}) copy-start(f32[8,256]{1,0:T(8,128)} %get-tuple-element.36.delta0) | copy-start | bytes 24580
  137.0 18.1 %copy-start.6 = (f32[8,256]{1,0:T(8,128)S(1)}, f32[8,256]{1,0:T(8,128)}, u32[]{:S(2)}) copy-start(f32[8,256]{1,0:T(8,128)} %get-tuple-element.37.delta1) | copy-start | bytes 24580
  142.3 10.9 %collective-permute-start.1 = (f32[3,80,256]{2,1,0:T(8,128)}, f32[3,80,256]{2,1,0:T(8,128)S(1)}, u32[]{:S(2)}, u32[]{:S(2)}) collective-permute-start(f32[3,80,256]{2,1,0:T(8,128)} %get-tuple-element.34), channel_id=1, source_target_pairs={{0,2},{2,4},{4,6},{6,8},{8,10},{10,12},{12,14},{14,0},{1,3},{3,5},... | collective-permute-start | bytes 737288 | tf_op jit(solution)/shard_map/ppermute | solution.py:35
  153.2 0.9 copy-start.3
  155.1 13.9 %collective-permute-start.2 = (f32[3,80,256]{2,1,0:T(8,128)S(1)}, f32[3,80,256]{2,1,0:T(8,128)S(1)}, u32[]{:S(2)}, u32[]{:S(2)}) collective-permute-start(f32[3,80,256]{2,1,0:T(8,128)S(1)} %shard_map.71), channel_id=1, source_target_pairs={{0,2},{2,4},{4,6},{6,8},{8,10},{10,12},{12,14},{14,0},{1,3},{3,5},... | collective-permute-start | bytes 737288 | tf_op jit(solution)/shard_map/ppermute | solution.py:35
  155.1 1.1 copy-start.2
  156.3 0.7 copy-start.7

commit v7 on v6

--- a/solution.py
+++ b/solution.py
@@ -144,7 +144,7 @@
 def opening(
     state_in, bed_in, manning_in, neighbours_in, wet_in, moves_in,
     out, columns, ctl, leaving,
-    state, bed, neighbours, wet, moves, sems,
+    state, bed, manning, neighbours, wet, moves, sems,
 ):
     copies = start_all(
         (
@@ -172,9 +172,8 @@
         for slot in range(2):
             ctl[WET + 2 * step + slot] = wet[step, first + slot]
         ctl[MOVE + step] = moves[step, device]
-    early = early_copies(moves[0, device], state_in, bed_in, manning_in, leaving, sems, 6)
-    for copy in early:
-        copy.start()
+    moving = moves[0, device]
+    rough = start_all(((manning_in.at[moving, 0:EARLY], manning),), sems, 6)
     count = lax.axis_size("xb")
     upper = lax.axis_index("yb")
     column = lax.axis_index("xb")
@@ -201,48 +200,59 @@
         best = lax.fori_loop(0, TILE // ROWS, group, jnp.zeros((ROWS, TILE), jnp.float32))
         total = jnp.maximum(total, jnp.where(wet[0, first + slot] > 0, best, 0.0))
     copies[5].wait()
+    wait_all(rough)
+    early = start_all(
+        (
+            (state.at[moving, :, 0:EARLY], leaving.at[0:3]),
+            (bed.at[moving, 0:EARLY], leaving.at[3]),
+            (manning, leaving.at[4]),
+        ),
+        sems,
+        7,
+    )
     messages(ctl, state, bed, jnp.max(total, keepdims=True), out, columns)
     wait_all(early)
 
 
-def early_copies(slot, state_in, bed_in, manning_in, leaving, sems, first):
-    rows = slice(0, EARLY)
-    pairs = (
-        (state_in.at[slot, :, rows], leaving.at[0:3]),
-        (bed_in.at[slot, rows], leaving.at[3]),
-        (manning_in.at[slot, rows], leaving.at[4]),
-    )
-    return [
-        pltpu.make_async_copy(src, dst, sems.at[first + k]) for k, (src, dst) in enumerate(pairs)
-    ]
-
-
-def rates_and_leaving(
-    ctl, state_in, bed_in, state_first, manning_in, arrived, rate_out, leaving,
-    state, bed, rate, sems, moving,
+def pass_on(ctl_in, leaving, ctl, same):
+    del leaving, same
+    for index in range(CONTROLS):
+        ctl[index] = ctl_in[index]
+
+
+def second_early(
+    ctl_in, order, state_in, bed_in, manning_in, arrived, ctl, leaving, buffer, sems
 ):
-    again = ctl[MOVE] == ctl[MOVE + 1]
-    passed = pltpu.make_async_copy(arrived, leaving, moving.at[0])
-    own = early_copies(1 - ctl[MOVE], state_first, bed_in, manning_in, leaving, moving, 1)
-
-    @pl.when(again)
-    def _():
-        passed.start()
-
-    @pl.when(jnp.logical_not(again))
-    def _():
-        for copy in own:
-            copy.start()
-
-    rates(ctl, state_in, bed_in, rate_out, state, bed, rate, sems)
-
-    @pl.when(again)
-    def _():
-        passed.wait()
-
-    @pl.when(jnp.logical_not(again))
-    def _():
-        wait_all(own)
+    del order
+    for index in range(CONTROLS):
+        ctl[index] = ctl_in[index]
+    again = ctl_in[MOVE] == ctl_in[MOVE + 1]
+    other = 1 - ctl_in[MOVE]
+    parts = 3
+    size = EARLY // parts
+    chunks = [slice(part * size, (part + 1) * size) for part in range(parts)]
+    for part, rows in enumerate(chunks):
+
+        @pl.when(again)
+        def _(part=part, rows=rows):
+            pltpu.make_async_copy(arrived.at[:, rows], buffer.at[:, rows], sems.at[part]).start()
+
+        @pl.when(jnp.logical_not(again))
+        def _(part=part, rows=rows):
+            sem = sems.at[part]
+            pltpu.make_async_copy(
+                state_in.at[other, :, rows], buffer.at[0:3, rows], sem
+            ).start()
+            pltpu.make_async_copy(bed_in.at[other, rows], buffer.at[3, rows], sem).start()
+            pltpu.make_async_copy(manning_in.at[other, rows], buffer.at[4, rows], sem).start()
+
+    outgoing = []
+    for part, rows in enumerate(chunks):
+        pltpu.make_async_copy(arrived.at[:, rows], buffer.at[:, rows], sems.at[part]).wait()
+        outgoing += start_all(
+            ((buffer.at[:, rows], leaving.at[:, rows]),), sems, parts + part
+        )
+    wait_all(outgoing)
 
 
 def rates(ctl, state_in, bed_in, rate_out, state, bed, rate, sems):
@@ -545,8 +555,11 @@
         tile[field, EARLY:, :] = late[field, 8 : TILE - kept, :]
 
 
-def repeat_second(ctl, delta0, delta1, delta2, early, tile, work, sems):
+def repeat_second(ctl, delta0, delta1, delta2, early, out, work, tile, sems):
     repeat_steps(ctl, WET_SECOND, (delta0, delta1, delta2), early, work, tile, sems)
+    copy = pltpu.make_async_copy(tile, out, sems.at[0])
+    copy.start()
+    copy.wait()
 
 
 def repeat_first(
@@ -578,18 +591,22 @@
     copy.wait()
 
 
-def second_late(ctl, arrived, own, leaving, sems):
+def second_late(ctl, arrived, own, order, leaving, buffer, sems):
+    del order
     again = ctl[MOVE] == ctl[MOVE + 1]
 
     @pl.when(again)
     def _():
-        pltpu.make_async_copy(arrived, leaving, sems.at[0]).start()
+        pltpu.make_async_copy(arrived, buffer, sems.at[0]).start()
 
     @pl.when(jnp.logical_not(again))
     def _():
-        pltpu.make_async_copy(own, leaving, sems.at[0]).start()
-
-    pltpu.make_async_copy(arrived, leaving, sems.at[0]).wait()
+        pltpu.make_async_copy(own, buffer, sems.at[0]).start()
+
+    pltpu.make_async_copy(arrived, buffer, sems.at[0]).wait()
+    copy = pltpu.make_async_copy(buffer, leaving, sems.at[0])
+    copy.start()
+    copy.wait()
 
 
 def correct_rows(ctl, slot, got, ground, block, state, rate, bottom):
@@ -802,34 +819,45 @@
         [
             whole,
             part,
+            pltpu.VMEM((EARLY, TILE), jnp.float32),
             pltpu.SMEM(neighbours.shape[::-1], jnp.int32),
             pltpu.SMEM(wet.shape, jnp.int32),
             pltpu.SMEM(moves.shape, jnp.int32),
-            pltpu.SemaphoreType.DMA((9,)),
+            pltpu.SemaphoreType.DMA((10,)),
         ],
     )(state, bed, manning, neighbours.T, wet, moves)
-    early_first = shifted(leaving, "xb", 1)
+    controls = jax.ShapeDtypeStruct((CONTROLS,), jnp.int32)
+    early_work = pltpu.VMEM(early_shape.shape, jnp.float32)
     state_first = state
     ground = None
     deltas = []
     for step in range(STEPS):
         got = spread(out)
         ground = got if step == 0 else ground
-        scratch = [whole, part, whole, pltpu.SemaphoreType.DMA((3 * CHUNKS,))]
-        if step == 1:
-            rate, leaving = call(
-                rates_and_leaving,
-                (shape, early_shape),
-                (hbm(), hbm()),
+        if step == 0:
+            ctl, leaving = call(
+                pass_on, (controls, early_shape), (smem(), hbm()), [smem(), hbm()], 1 << 10,
+                aliases={1: 1},
+            )(ctl, leaving)
+            early_first = shifted(leaving, "xb", 1)
+        elif step == 1:
+            ctl, leaving = call(
+                second_early,
+                (controls, early_shape),
+                (smem(), hbm()),
                 [smem()] + [hbm()] * 5,
-                16 << 20,
-                scratch + [pltpu.SemaphoreType.DMA((4,))],
-            )(ctl, state, bed, state_first, manning, early_first)
+                1 << 10,
+                [early_work, pltpu.SemaphoreType.DMA((6,))],
+            )(ctl, deltas[0], state_first, bed, manning, early_first)
             early_second = shifted(leaving, "xb", 1)
-        else:
-            rate = call(rates, shape, hbm(), [smem(), hbm(), hbm()], 16 << 20, scratch)(
-                ctl, state, bed
-            )
+        rate = call(
+            rates,
+            shape,
+            hbm(),
+            [smem(), hbm(), hbm()],
+            16 << 20,
+            [whole, part, whole, pltpu.SemaphoreType.DMA((3 * CHUNKS,))],
+        )(ctl, state, bed)
         if step + 1 < STEPS:
             shapes = (shape, f32(8 * devices, TILE), f32(8, TILE), delta_shape)
             places = (hbm(), vmem(), vmem(), vmem())
@@ -849,22 +877,23 @@
             state, out, columns, _ = outs
     staying, late_first, late_second, _ = outs
     late_arrived = shifted(late_first, "xb", 1)
-    small = 8 << 20
-    early_work = pltpu.VMEM(early_shape.shape, jnp.float32)
     early_state = f32(3, EARLY, TILE)
     second = call(
         repeat_second,
         early_state,
-        vmem(),
+        hbm(),
         [smem()] + [vmem()] * 3 + [hbm()],
         8 << 20,
-        [early_work, pltpu.SemaphoreType.DMA((3,))],
-        room=small,
+        [early_work, pltpu.VMEM(early_state.shape, jnp.float32), pltpu.SemaphoreType.DMA((3,))],
     )(ctl, *deltas, early_second)
     leaving = call(
-        second_late, late_shape, anywhere(), [smem(), anywhere(), anywhere()], 1 << 20, sem,
-        room=1 << 20,
-    )(ctl, late_arrived, late_second)
+        second_late,
+        late_shape,
+        hbm(),
+        [smem(), hbm(), hbm(), hbm()],
+        1 << 10,
+        [pltpu.VMEM(late_shape.shape, jnp.float32)] + sem,
+    )(ctl, late_arrived, late_second, second)
     late_next = shifted(leaving, "xb", 1)
     final = call(
         repeat_first,
@@ -878,7 +907,6 @@
             pltpu.VMEM(tile_shape.shape, jnp.float32),
             pltpu.SemaphoreType.DMA((4,)),
         ],
-        room=small,
     )(ctl, *deltas, early_first, late_arrived, staying)
     return call(
         finish,
@@ -888,7 +916,6 @@
         1 << 20,
         [pltpu.VMEM(tile_shape.shape, jnp.float32)] + sem,
         {3: 0},
-        room=small,
     )(ctl, late_next, second, final)
 
 

time: 171 us -> 143 us (0.84)
  the two profiles are of different devices: /device:TPU:0 before, /device:TPU:1 now
where the time goes in v7:
time: 143 us; the launch traced here: 141 us
  Pallas kernels  81.4 us (57%)
  waiting for transfers between devices  33.9 us (24%)
  starting transfers between devices  20.6 us (14%)
  local copies, waits for them, and re-layouts  5.3 us (4%)
    all_to_all x3, waiting for transfers between devices, spread(): lax.all_to_all(fast, ('xb', 'yb'), split_axis=0, concat_axis=0, tiled=True)  33.9 us
    pallas_call x1, Pallas kernels, body(): call(repeat_first, shape, hbm(), [smem()] + [vmem()] * 3 + [hbm(), vmem()...  26 us
    pallas_call x3, Pallas kernels, body(): call(rates, shape, hbm(), [smem(), hbm(), hbm()], 16 << 20, [whole, part,...  19.9 us
    pallas_call x3, Pallas kernels, body(): call(functools.partial(update, step), shapes, places, [smem(), vmem(), vm...  15.4 us
    all_to_all x3, starting transfers between devices, spread(): lax.all_to_all(fast, ('xb', 'yb'), split_axis=0, concat_axis=0, tiled=True)  15.3 us
    pallas_call x1, Pallas kernels, body(): call(repeat_second, early_state, hbm(), [smem()] + [vmem()] * 3 + [hbm()]...  7.51 us
    ppermute x4, starting transfers between devices, shifted(): return lax.ppermute(value, axis, pairs)  5.3 us
    unnamed x14, local copies, waits for them, and re-layouts  5.3 us
  transfers between devices with their start and end apart: 7, of which 3 were waited for; matrix products, arithmetic and copies ran while one was open for 0% of the time, Pallas kernels for 49%

profile of v7, /device:TPU:1, one launch (start us, length us, event | category | flops | bytes accessed | tf_op | source)
XLA Modules:
  0.0 141.3 jit_solution(10462878223167088990)
XLA Ops:
  0.0 3.6 %shard_map.64 = (f32[256,256]{1,0:T(8,128)}, f32[8,256]{1,0:T(8,128)}, s32[24]{0:T(128)}, f32[5,192,256]{2,1,0:T(8,128)}) custom-call(f32[2,3,256,256]{3,2,1,0:T(8,128)} %state_in.7, f32[2,256,256]{2,1,0:T(8,128)} %bed_in.9, f32[2,256,256]{2,1,0:T(8,128)} %manning_in.9, s32[4,32]{1,0:T(4,128)} %bitcast.15, s32[3,32]{1,0:T(4,128)} %wet_in.1, s32[3,16]{1,0:T(4,128)} %moves_in.1), custom_call_target="tpu_custom_call" | custom-call | flops 4194304 | bytes 4194304 | tf_op jit(solution)/shard_map/pallas_call | solution.py:808
  3.7 1.2 shard_map.65
  4.9 2.1 %collective-permute-start = (f32[5,192,256]{2,1,0:T(8,128)}, f32[5,192,256]{2,1,0:T(8,128)S(1)}, u32[]{:S(2)}, u32[]{:S(2)}) collective-permute-start(f32[5,192,256]{2,1,0:T(8,128)} %get-tuple-element.31), channel_id=1, source_target_pairs={{0,2},{2,4},{4,6},{6,8},{8,10},{10,12},{12,14},{14,0},{1,3},{3,5},... | collective-permute-start | bytes 2949128 | tf_op jit(solution)/shard_map/ppermute | solution.py:35
  7.0 5.8 %all-to-all-start = ((f32[16,16,256]{2,1,0:T(8,128)}), f32[16,16,256]{2,1,0:T(8,128)S(1)}, u32[]{:S(2)}, u32[]{:S(2)}) async-start(f32[16,16,256]{2,1,0:T(8,128)} %bitcast.13), calls=%async_computation | async-start | bytes 524288 | tf_op jit(solution)/shard_map/all_to_all | solution.py:795
  12.8 6.6 %shard_map.66.rate_in = f32[2,3,256,256]{3,2,1,0:T(8,128)} custom-call(s32[24]{0:T(128)} %get-tuple-element.27.ctl.ctl_in, f32[2,3,256,256]{3,2,1,0:T(8,128)} %state_in.7, f32[2,256,256]{2,1,0:T(8,128)} %bed_in.9), custom_call_target="tpu_custom_call" | custom-call | flops 16777216 | bytes 4194304 | tf_op jit(solution)/shard_map/pallas_call | solution.py:853
  19.5 17.7 %all-to-all-done = f32[16,16,256]{2,1,0:T(8,128)S(1)} async-done(((f32[16,16,256]{2,1,0:T(8,128)}), f32[16,16,256]{2,1,0:T(8,128)S(1)}, u32[]{:S(2)}, u32[]{:S(2)}) %all-to-all-start) | async-done | bytes 262176 | tf_op jit(solution)/shard_map/all_to_all | solution.py:795
  37.1 0.7 copy-done
  37.9 5.1 %shard_map.67 = (f32[2,3,256,256]{3,2,1,0:T(8,128)}, f32[128,256]{1,0:T(8,128)}, f32[8,256]{1,0:T(8,128)}, f32[8,256]{1,0:T(8,128)}) custom-call(s32[24]{0:T(128)} %get-tuple-element.27.ctl.ctl_in, f32[256,256]{1,0:T(8,128)} %bitcast.7, f32[256,256]{1,0:T(8,128)} %bitcast.8, f32[8,256]{1,0:T(8,128)} %get-tuple-element.29.columns, ...), custom_call_target="tpu_custom_call" | custom-call | flops 8388608 | bytes 4194304 | tf_op jit(solution)/shard_map/pallas_call | solution.py:867
  43.0 0.0 collective-permute-done.arrived.early
  43.0 1.0 copy-done.1
  44.0 3.2 %shard_map.68 = (s32[24]{0:T(128)}, f32[5,192,256]{2,1,0:T(8,128)}) custom-call(s32[24]{0:T(128)} %get-tuple-element.27.ctl.ctl_in, f32[8,256]{1,0:T(8,128)} %get-tuple-element.30.order.delta0, f32[2,3,256,256]{3,2,1,0:T(8,128)} %state_in.7, f32[2,256,256]{2,1,0:T(8,128)} %bed_in.9, f32[2,256,256]{2,1,0:T(8,128)} %manning_in.9, f32[5,192,256]{2,1,0:T(8,128)} %copy-done.1), custom_call_target="tpu_custom_call" | custom-call | flops 1024 | bytes 4194304 | tf_op jit(solution)/shard_map/pallas_call | solution.py:844
  47.2 0.7 collective-permute-start.2
  47.9 5.8 %all-to-all-start.1 = ((f32[16,8,256]{2,1,0:T(8,128)}), f32[16,8,256]{2,1,0:T(8,128)S(1)}, u32[]{:S(2)}, u32[]{:S(2)}) async-start(f32[16,8,256]{2,1,0:T(8,128)} %bitcast.3), calls=%async_computation.1 | async-start | bytes 262144 | tf_op jit(solution)/shard_map/all_to_all | solution.py:795
  53.7 6.6 %shard_map.69.rate_in = f32[2,3,256,256]{3,2,1,0:T(8,128)} custom-call(s32[24]{0:T(128)} %get-tuple-element.32.ctl, f32[2,3,256,256]{3,2,1,0:T(8,128)} %get-tuple-element.35.state_in, f32[2,256,256]{2,1,0:T(8,128)} %bed_in.9), custom_call_target="tpu_custom_call" | custom-call | flops 16777216 | bytes 4194304 | tf_op jit(solution)/shard_map/pallas_call | solution.py:853
  60.3 15.9 %all-to-all-done.1 = f32[16,8,256]{2,1,0:T(8,128)S(1)} async-done(((f32[16,8,256]{2,1,0:T(8,128)}), f32[16,8,256]{2,1,0:T(8,128)S(1)}, u32[]{:S(2)}, u32[]{:S(2)}) %all-to-all-start.1) | async-done | bytes 131104 | tf_op jit(solution)/shard_map/all_to_all | solution.py:795
  76.2 0.7 copy-done.4
  76.9 5.1 %shard_map.70 = (f32[2,3,256,256]{3,2,1,0:T(8,128)}, f32[128,256]{1,0:T(8,128)}, f32[8,256]{1,0:T(8,128)}, f32[8,256]{1,0:T(8,128)}) custom-call(s32[24]{0:T(128)} %get-tuple-element.32.ctl, f32[128,256]{1,0:T(8,128)} %bitcast.11, f32[256,256]{1,0:T(8,128)} %bitcast.9, f32[8,256]{1,0:T(8,128)} %get-tuple-element.34.columns, ...), custom_call_target="tpu_custom_call" | custom-call | flops 8388608 | bytes 4194304 | tf_op jit(solution)/shard_map/pallas_call | solution.py:867
  82.0 3.7 %all-to-all-start.2 = ((f32[16,8,256]{2,1,0:T(8,128)}), f32[16,8,256]{2,1,0:T(8,128)S(1)}, u32[]{:S(2)}, u32[]{:S(2)}) async-start(f32[16,8,256]{2,1,0:T(8,128)} %bitcast.14), calls=%async_computation.2 | async-start | bytes 262144 | tf_op jit(solution)/shard_map/all_to_all | solution.py:795
  85.7 6.6 %shard_map.71.rate_in = f32[2,3,256,256]{3,2,1,0:T(8,128)} custom-call(s32[24]{0:T(128)} %get-tuple-element.32.ctl, f32[2,3,256,256]{3,2,1,0:T(8,128)} %get-tuple-element.38.state_in, f32[2,256,256]{2,1,0:T(8,128)} %bed_in.9), custom_call_target="tpu_custom_call" | custom-call | flops 16777216 | bytes 4194304 | tf_op jit(solution)/shard_map/pallas_call | solution.py:853
  92.3 0.3 all-to-all-done.2
  92.6 0.6 copy-done.5
  93.3 5.2 %shard_map.72 = (f32[3,256,256]{2,1,0:T(8,128)}, f32[3,80,256]{2,1,0:T(8,128)}, f32[3,80,256]{2,1,0:T(8,128)}, f32[8,256]{1,0:T(8,128)}) custom-call(s32[24]{0:T(128)} %get-tuple-element.32.ctl, f32[128,256]{1,0:T(8,128)} %bitcast.12, f32[256,256]{1,0:T(8,128)} %bitcast.10, f32[8,256]{1,0:T(8,128)} %get-tuple-element.37.columns, ...), custom_call_target="tpu_custom_call" | custom-call | flops 8388608 | bytes 4194304 | tf_op jit(solution)/shard_map/pallas_call | solution.py:867
  98.5 1.1 collective-permute-start.1
  99.6 0.0 collective-permute-done.2.early
  99.6 0.9 copy-done.2
  100.6 7.5 %shard_map.73.order.early = f32[3,192,256]{2,1,0:T(8,128)} custom-call(s32[24]{0:T(128)} %get-tuple-element.32.ctl, f32[8,256]{1,0:T(8,128)} %get-tuple-element.30.order.delta0, f32[8,256]{1,0:T(8,128)} %get-tuple-element.41.delta1, f32[8,256]{1,0:T(8,128)} %get-tuple-element.42.delta2, f32[5,192,256]{2,1,0:T(8,128)} %copy-done.2), custom_call_target="tpu_custom_call" | custom-call | flops 8388608 | bytes 4194304 | tf_op jit(solution)/shard_map/pallas_call | solution.py:881
  108.1 0.7 copy-done.3
  108.8 2.3 %shard_map.74 = f32[3,80,256]{2,1,0:T(8,128)} custom-call(s32[24]{0:T(128)} %get-tuple-element.32.ctl, f32[3,80,256]{2,1,0:T(8,128)} %copy-done.3, f32[3,80,256]{2,1,0:T(8,128)} %get-tuple-element.40.own, f32[3,192,256]{2,1,0:T(8,128)} %shard_map.73.order.early), custom_call_target="tpu_custom_call" | custom-call | flops 1024 | bytes 4194304 | tf_op jit(solution)/shard_map/pallas_call | solution.py:889
  111.1 1.3 collective-permute-start.3
  112.4 26.0 %shard_map.75.before = f32[2,3,256,256]{3,2,1,0:T(8,128)} custom-call(s32[24]{0:T(128)} %get-tuple-element.32.ctl, f32[8,256]{1,0:T(8,128)} %get-tuple-element.30.order.delta0, f32[8,256]{1,0:T(8,128)} %get-tuple-element.41.delta1, f32[8,256]{1,0:T(8,128)} %get-tuple-element.42.delta2, f32[5,192,256]{2,1,0:T(8,128)} %copy-done.1, f32[3,80,256]{2,1,0:T(8,128)} %copy-done.3, ...), custom_call_target="tpu_custom_call" | custom-call | flops 8388608 | bytes 4194304 | tf_op jit(solution)/shard_map/pallas_call | solution.py:898
  138.4 0.7 copy-done.6
  139.1 2.2 %shard_map.76 = f32[2,3,256,256]{3,2,1,0:T(8,128)} custom-call(s32[24]{0:T(128)} %get-tuple-element.32.ctl, f32[3,80,256]{2,1,0:T(8,128)} %copy-done.6, f32[3,192,256]{2,1,0:T(8,128)} %shard_map.73.order.early, f32[2,3,256,256]{3,2,1,0:T(8,128)} %shard_map.75.before), custom_call_target="tpu_custom_call", output_to_operand_aliasing={{}: (3, {})} | custom-call | flops 1048576 | bytes 4194304 | tf_op jit(solution)/shard_map/pallas_call | solution.py:911
  (9 shorter events, 0.0 us)
Async XLA Ops:
  4.9 38.1 %collective-permute-start = (f32[5,192,256]{2,1,0:T(8,128)}, f32[5,192,256]{2,1,0:T(8,128)S(1)}, u32[]{:S(2)}, u32[]{:S(2)}) collective-permute-start(f32[5,192,256]{2,1,0:T(8,128)} %get-tuple-element.31), channel_id=1, source_target_pairs={{0,2},{2,4},{4,6},{6,8},{8,10},{10,12},{12,14},{14,0},{1,3},{3,5},... | collective-permute-start | bytes 2949128 | tf_op jit(solution)/shard_map/ppermute | solution.py:35
  7.0 30.2 %all-to-all-start = ((f32[16,16,256]{2,1,0:T(8,128)}), f32[16,16,256]{2,1,0:T(8,128)S(1)}, u32[]{:S(2)}, u32[]{:S(2)}) async-start(f32[16,16,256]{2,1,0:T(8,128)} %bitcast.13), calls=%async_computation | async-start | bytes 524288 | tf_op jit(solution)/shard_map/all_to_all | solution.py:795
  37.1 0.7 copy-start
  43.0 1.0 copy-start.1
  47.2 52.5 %collective-permute-start.2 = (f32[5,192,256]{2,1,0:T(8,128)}, f32[5,192,256]{2,1,0:T(8,128)S(1)}, u32[]{:S(2)}, u32[]{:S(2)}) collective-permute-start(f32[5,192,256]{2,1,0:T(8,128)} %get-tuple-element.43), channel_id=1, source_target_pairs={{0,2},{2,4},{4,6},{6,8},{8,10},{10,12},{12,14},{14,0},{1,3},{3,5},... | collective-permute-start | bytes 2949128 | tf_op jit(solution)/shard_map/ppermute | solution.py:35
  47.9 28.3 %all-to-all-start.1 = ((f32[16,8,256]{2,1,0:T(8,128)}), f32[16,8,256]{2,1,0:T(8,128)S(1)}, u32[]{:S(2)}, u32[]{:S(2)}) async-start(f32[16,8,256]{2,1,0:T(8,128)} %bitcast.3), calls=%async_computation.1 | async-start | bytes 262144 | tf_op jit(solution)/shard_map/all_to_all | solution.py:795
  76.2 0.7 copy-start.4
  82.0 10.7 %all-to-all-start.2 = ((f32[16,8,256]{2,1,0:T(8,128)}), f32[16,8,256]{2,1,0:T(8,128)S(1)}, u32[]{:S(2)}, u32[]{:S(2)}) async-start(f32[16,8,256]{2,1,0:T(8,128)} %bitcast.14), calls=%async_computation.2 | async-start | bytes 262144 | tf_op jit(solution)/shard_map/all_to_all | solution.py:795
  92.6 0.6 copy-start.5
  98.5 9.6 %collective-permute-start.1 = (f32[3,80,256]{2,1,0:T(8,128)}, f32[3,80,256]{2,1,0:T(8,128)S(1)}, u32[]{:S(2)}, u32[]{:S(2)}) collective-permute-start(f32[3,80,256]{2,1,0:T(8,128)} %get-tuple-element.39), channel_id=1, source_target_pairs={{0,2},{2,4},{4,6},{6,8},{8,10},{10,12},{12,14},{14,0},{1,3},{3,5},... | collective-permute-start | bytes 737288 | tf_op jit(solution)/shard_map/ppermute | solution.py:35
  99.6 0.9 copy-start.2
  108.1 0.7 copy-start.3
  111.1 27.3 %collective-permute-start.3 = (f32[3,80,256]{2,1,0:T(8,128)}, f32[3,80,256]{2,1,0:T(8,128)S(1)}, u32[]{:S(2)}, u32[]{:S(2)}) collective-permute-start(f32[3,80,256]{2,1,0:T(8,128)} %shard_map.74), channel_id=1, source_target_pairs={{0,2},{2,4},{4,6},{6,8},{8,10},{10,12},{12,14},{14,0},{1,3},{3,5},... | collective-permute-start | bytes 737288 | tf_op jit(solution)/shard_map/ppermute | solution.py:35
  138.4 0.7 copy-start.6

commit v8 on v5

--- a/solution.py
+++ b/solution.py
@@ -18,7 +18,10 @@
 VMEM_BYTES = 60 * 1024 * 1024
 SLOT_LOW, WALL_WEST, WALL_EAST, WALL_OUTER, WET, MOVE = 0, 1, 3, 5, 7, 13
 CONTROLS = 16
-CHUNKS = 4
+CHUNKS = 8
+PARTS = 8
+HALF = TILE // 2
+STRIP = 16
 TOP = 6
 SCALE = 0.5 / SPACING
 SLOPE = GRAVITY / (2.0 * SPACING)
@@ -186,11 +189,13 @@
 
 
 def rates(ctl, state_in, bed_in, rate_out, state, bed, rate, sems):
-    row_ids = lax.broadcasted_iota(jnp.int32, (ROWS, TILE), 0)
-    lane = lax.broadcasted_iota(jnp.int32, (ROWS, LANES), 1)
-    row8 = sublanes()
-    last = TILE // ROWS - 1
+    width = 2 * TILE
+    row_ids = lax.broadcasted_iota(jnp.int32, (STRIP, width), 0)
+    row8 = sublanes(width)
+    lane = lax.broadcasted_iota(jnp.int32, (STRIP, LANES), 1)
+    last = TILE // STRIP - 1
     chunk = TILE // CHUNKS
+    slots = [slot_of(ctl, position) for position in range(2)]
     incoming = []
     for part in range(CHUNKS):
         rows = slice(part * chunk, (part + 1) * chunk)
@@ -204,141 +209,119 @@
                 2 * part,
             )
         )
+    keep_west, keep_east, keep_south, keep_north = (
+        jnp.where(flag(ctl, index), 1.0, 0.0)
+        for index in (WALL_WEST, WALL_EAST, WALL_OUTER, WALL_OUTER + 1)
+    )
+
+    def strip(field, rows):
+        if field == 3:
+            return jnp.concatenate([bed[slot, rows, :] for slot in slots], 1)
+        return jnp.concatenate([state[slot, field, rows, :] for slot in slots], 1)
+
+    def blocks(value):
+        return [value[:, k * LANES : (k + 1) * LANES] for k in range(4)]
+
+    def right_of(value, end=None):
+        turned = [pltpu.roll(part, LANES - 1, 1) for part in blocks(value)]
+        after = turned[1:] + [turned[3] if end is None else end]
+        return jnp.concatenate(
+            [
+                jnp.where(lane == LANES - 1, following, part)
+                if following is not part
+                else part
+                for part, following in zip(turned, after)
+            ],
+            1,
+        )
+
+    def left_of(value, end):
+        turned = [pltpu.roll(part, 1, 1) for part in blocks(value)]
+        before = [end] + turned[:3]
+        return jnp.concatenate(
+            [jnp.where(lane == 0, previous, part) for part, previous in zip(turned, before)], 1
+        )
+
+    def down(value):
+        return pltpu.roll(value, STRIP + 7, 0)[:STRIP]
+
+    def group(index, carry):
+        base = pl.multiple_of(index * STRIP, STRIP)
+        rows = pl.ds(base, STRIP)
+        after = pl.ds(pl.multiple_of(jnp.minimum(base + STRIP, TILE - 8), 8), 8)
+        at_end = index == last
+        fields = [
+            jnp.concatenate([strip(field, rows), strip(field, after)], 0) for field in range(3)
+        ]
+        cells_x, cells_y = cell(*fields)
+        here_x = tuple(value[:STRIP] for value in cells_x)
+        here_y = tuple(value[:STRIP] for value in cells_y)
+
+        ending = jnp.logical_and(row8 == 7, at_end)
+        faces = list(face(here_x, tuple(down(value) for value in cells_x)))
+        wall = keep_east * (2.0 * (here_x[3] + here_x[5] * here_x[1])[STRIP - 8 :])
+        for component, value in enumerate((0.0, wall, 0.0)):
+            upper = faces[component]
+            faces[component] = jnp.concatenate(
+                [upper[: STRIP - 8], jnp.where(ending, value, upper[STRIP - 8 :])], 0
+            )
+        turned = tuple(pltpu.roll(value, 1, 0) for value in faces)
+        change_x = tuple(
+            value - jnp.where(row_ids == 0, before, moved)
+            for value, before, moved in zip(faces, carry[:3], turned)
+        )
+        ground = strip(3, rows)
+        ground_after = jnp.where(
+            at_end,
+            jnp.broadcast_to(keep_east * ground[STRIP - 1 :], (8, width)),
+            strip(3, after),
+        )
+        ground_up = pltpu.roll(ground, 1, 0)
+        slope_x = down(jnp.concatenate([ground, ground_after], 0)) - jnp.where(
+            row_ids == 0, carry[3], ground_up
+        )
+        carried = tuple(value[0:1, :] for value in turned) + (ground_up[0:1, :],)
+
+        faces_y = list(face(here_y, tuple(right_of(value) for value in here_y)))
+        normal = here_y[3]
+        spread_y = here_y[5] * here_y[1]
+        north = keep_north * (2.0 * (normal + spread_y)[:, width - LANES :])
+        south = keep_south * (2.0 * (normal - spread_y)[:, :LANES])
+        change_y = []
+        for component, (high, low) in enumerate(((0.0, 0.0), (north, south), (0.0, 0.0))):
+            parts = blocks(faces_y[component])
+            parts[3] = jnp.where(lane == LANES - 1, high, parts[3])
+            value = jnp.concatenate(parts, 1)
+            change_y.append(value - left_of(value, low))
+        slope_y = right_of(ground, keep_north * ground[:, width - LANES :]) - left_of(
+            ground, keep_south * ground[:, :LANES]
+        )
+        weight = SLOPE * here_x[0]
+        results = (
+            SCALE * (change_x[0] + change_y[0]),
+            SCALE * (change_x[1] + change_y[2]) + weight * slope_x,
+            SCALE * (change_x[2] + change_y[1]) + weight * slope_y,
+        )
+        for field, value in enumerate(results):
+            for position, slot in enumerate(slots):
+                rate[slot, field, rows, :] = value[:, position * TILE : (position + 1) * TILE]
+        return carried
+
     wait_all(incoming[0])
+    top, _ = cell(*(strip(field, slice(0, 8)) for field in range(3)))
+    nothing = jnp.zeros((1, width), jnp.float32)
+    carry = (
+        nothing,
+        keep_west * (2.0 * (top[3] - top[5] * top[1])[0:1]),
+        nothing,
+        keep_west * strip(3, slice(0, 8))[0:1],
+    )
+    per_chunk = chunk // STRIP
     outgoing = []
-
-    def field_ref(which, field):
-        return bed.at[which] if field == 3 else state.at[which, field]
-
-    def opening_faces(position):
-        slot = slot_of(ctl, position)
-        keep = jnp.where(flag(ctl, WALL_WEST + position), 1.0, 0.0)
-        first = [field_ref(slot, field)[0:8, :] for field in range(4)]
-        right, _ = cell(*first[:3])
-        left, _ = cell(first[0], -first[1], first[2])
-        return tuple(keep * part[0:1, :] for part in face(left, right)) + (keep * first[3][0:1, :],)
-
-    def group_of(position):
-        slot = slot_of(ctl, position)
-        other = 1 - slot
-        keep_outer = jnp.where(flag(ctl, WALL_OUTER + position), 1.0, 0.0)
-        keep_east = jnp.where(flag(ctl, WALL_EAST + position), 1.0, 0.0)
-        inner_lane = LANES - 1 if position == 0 else 0
-        outer_lane = LANES - 1 - inner_lane
-        inner_cols = slice(0, LANES) if position == 0 else slice(LANES, TILE)
-        inner_turn = LANES - 1 if position == 0 else 1
-
-        def group(index, carry):
-            base = pl.multiple_of(index * ROWS, ROWS)
-            rows = pl.ds(base, ROWS)
-            after = pl.ds(pl.multiple_of(jnp.minimum(base + ROWS, TILE - 8), 8), 8)
-            at_end = index == last
-            fields = []
-            for field in range(4):
-                ref = field_ref(slot, field)
-                block = ref[rows, :]
-                mirrored = jnp.broadcast_to(block[ROWS - 1 : ROWS], (8, TILE))
-                if field == 1:
-                    mirrored = -mirrored
-                if field == 3:
-                    mirrored = keep_east * mirrored
-                fields.append(
-                    jnp.concatenate([block, jnp.where(at_end, mirrored, ref[after, :])], 0)
-                )
-            cells_x, cells_y = cell(*fields[:3])
-
-            def down(value):
-                return pltpu.roll(value, ROWS + 7, 0)[:ROWS]
-
-            here = tuple(value[:ROWS] for value in cells_x)
-            keep = jnp.where(row8 == 7, jnp.where(at_end, keep_east, 1.0), 1.0)
-            faces = tuple(
-                jnp.concatenate([value[: ROWS - 8], value[ROWS - 8 :] * keep], 0)
-                for value in face(here, tuple(down(value) for value in cells_x))
-            )
-            turned = tuple(pltpu.roll(value, 1, 0) for value in faces)
-            change_x = tuple(
-                value - jnp.where(row_ids == 0, before, moved)
-                for value, before, moved in zip(faces, carry[:3], turned)
-            )
-            ground = fields[3][:ROWS]
-            ground_up = pltpu.roll(ground, 1, 0)
-            slope_x = down(fields[3]) - jnp.where(row_ids == 0, carry[3], ground_up)
-            carried = tuple(value[0:1, :] for value in turned) + (ground_up[0:1, :],)
-
-            ghosts = []
-            for field in range(4):
-                inner = pltpu.roll(field_ref(other, field)[rows, inner_cols], inner_turn, 1)
-                own = fields[field][:ROWS, inner_cols]
-                if field == 2:
-                    own = -own
-                if field == 3:
-                    own = keep_outer * own
-                ghosts.append(jnp.where(lane == inner_lane, inner, own))
-            _, ghost_y = cell(*ghosts[:3])
-            low = tuple(value[:ROWS, :LANES] for value in cells_y)
-            high = tuple(value[:ROWS, LANES:] for value in cells_y)
-
-            def right_of(low_part, high_part, ghost_part):
-                turned_low = pltpu.roll(low_part, LANES - 1, 1)
-                turned_high = pltpu.roll(high_part, LANES - 1, 1)
-                return (
-                    jnp.where(lane == LANES - 1, turned_high, turned_low),
-                    jnp.where(lane == LANES - 1, ghost_part, turned_high),
-                )
-
-            pairs = [right_of(a, b, c) for a, b, c in zip(low, high, ghost_y)]
-            faces_low = face(low, tuple(pair[0] for pair in pairs))
-            faces_high = face(high, tuple(pair[1] for pair in pairs))
-            faces_edge = face(ghost_y, low)
-            if position == 0:
-                faces_edge = tuple(keep_outer * value for value in faces_edge)
-            else:
-                keep_lane = jnp.where(lane == outer_lane, keep_outer, 1.0)
-                faces_high = tuple(keep_lane * value for value in faces_high)
-            change_y = []
-            for a, b, c in zip(faces_low, faces_high, faces_edge):
-                turned_a = pltpu.roll(a, 1, 1)
-                turned_b = pltpu.roll(b, 1, 1)
-                change_y.append(
-                    jnp.concatenate(
-                        [
-                            a - jnp.where(lane == 0, c, turned_a),
-                            b - jnp.where(lane == 0, turned_a, turned_b),
-                        ],
-                        1,
-                    )
-                )
-            ground_low = ground[:, :LANES]
-            ground_high = ground[:, LANES:]
-            north = right_of(ground_low, ground_high, ghosts[3])
-            turned_low = pltpu.roll(ground_low, 1, 1)
-            turned_high = pltpu.roll(ground_high, 1, 1)
-            slope_y = jnp.concatenate(
-                [
-                    north[0] - jnp.where(lane == 0, ghosts[3], turned_low),
-                    north[1] - jnp.where(lane == 0, turned_low, turned_high),
-                ],
-                1,
-            )
-            weight = SLOPE * fields[0][:ROWS]
-            rate[slot, 0, rows, :] = SCALE * (change_x[0] + change_y[0])
-            rate[slot, 1, rows, :] = SCALE * (change_x[1] + change_y[2]) + weight * slope_x
-            rate[slot, 2, rows, :] = SCALE * (change_x[2] + change_y[1]) + weight * slope_y
-            return carried
-
-        return group
-
-    carries = [opening_faces(position) for position in range(2)]
-    groups = [group_of(position) for position in range(2)]
-    per_chunk = chunk // ROWS
     for part in range(CHUNKS):
         if part + 1 < CHUNKS:
             wait_all(incoming[part + 1])
-        for position in range(2):
-            carries[position] = lax.fori_loop(
-                part * per_chunk, (part + 1) * per_chunk, groups[position], carries[position]
-            )
+        carry = lax.fori_loop(part * per_chunk, (part + 1) * per_chunk, group, carry)
         rows = slice(part * chunk, (part + 1) * chunk)
         outgoing += start_all(
             ((rate.at[:, :, rows], rate_out.at[:, :, rows]),), sems, 2 * CHUNKS + part
@@ -402,17 +385,22 @@
     )
 
 
-def update(step, ctl, got, ground, columns, state_in, manning_in, rate_in, *rest):
+def update(step, ctl, got_in, ground_in, columns_in, state_in, manning_in, rate_in, *rest):
     more = step + 1 < STEPS
     if more:
-        fresh_out, out, columns_out = rest[:3]
+        fresh_out, out_to, columns_to = rest[:3]
         rest = rest[3:]
     else:
-        fresh_out, leaving = rest[:2]
-        rest = rest[2:]
-    state, manning, rate, fresh, sems = rest
-    half = TILE // 2
-    parts = [(slot, slice(k * half, (k + 1) * half)) for slot in range(2) for k in range(2)]
+        fresh_out, leaving_low, leaving_high = rest[:3]
+        rest = rest[3:]
+    state, manning, rate, fresh, got, ground, columns, out, columns_out, sems = rest
+    small = start_all(
+        ((got_in, got), (ground_in, ground), (columns_in, columns)), sems, 5 * PARTS
+    )
+    size = 2 * TILE // PARTS
+    parts = [
+        (slot, slice(k * size, (k + 1) * size)) for slot in range(2) for k in range(PARTS // 2)
+    ]
     incoming = []
     for index, (slot, rows) in enumerate(parts):
         incoming.append(
@@ -426,6 +414,7 @@
                 3 * index,
             )
         )
+    wait_all(small)
     upper = lax.axis_index("yb")
     devices = 2 * lax.axis_size("xb")
     block = got.shape[0] // devices
@@ -437,13 +426,15 @@
     facing = jnp.where(upper > 0, ctl[SLOT_LOW], 1 - ctl[SLOT_LOW])
     begin = pl.multiple_of((1 - upper) * LANES, LANES)
     target = (1 - upper) * (LANES - 1)
-    lane = lax.broadcasted_iota(jnp.int32, (half, LANES), 1)
+    lane = lax.broadcasted_iota(jnp.int32, (size, LANES), 1)
     total = jnp.zeros((ROWS, TILE), jnp.float32)
     outgoing = []
     for index, (slot, part_rows) in enumerate(parts):
         wait_all(incoming[index])
-        bottom = index % 2 == 0
-        correct_rows(ctl, slot, got, ground, block, state, rate, bottom)
+        if part_rows.start == 0:
+            correct_rows(ctl, slot, got, ground, block, state, rate, True)
+        if part_rows.stop == TILE:
+            correct_rows(ctl, slot, got, ground, block, state, rate, False)
 
         @pl.when(facing == slot)
         def _(slot=slot, part_rows=part_rows):
@@ -494,16 +485,24 @@
             best = jnp.where(flag(ctl, WET + 2 * step + 2 + slot), best, 0.0)
             total = jnp.maximum(total, best)
         outgoing += start_all(
-            ((fresh.at[slot, :, part_rows], fresh_out.at[slot, :, part_rows]),), sems, 12 + index
+            ((fresh.at[slot, :, part_rows], fresh_out.at[slot, :, part_rows]),),
+            sems,
+            3 * PARTS + index,
         )
     if more:
         messages(ctl, fresh, None, jnp.max(total, keepdims=True), out, columns_out)
+        outgoing += start_all(((out, out_to), (columns_out, columns_to)), sems, 4 * PARTS)
     else:
-        outgoing += start_all(((fresh.at[ctl[MOVE]], leaving),), sems, 16)
+        tile = fresh.at[ctl[MOVE]]
+        outgoing += start_all(
+            ((tile.at[:, :HALF], leaving_low), (tile.at[:, HALF:], leaving_high)),
+            sems,
+            4 * PARTS,
+        )
     wait_all(outgoing)
 
 
-def second_leaving(ctl, state, arrived, leaving, sems):
+def second_leaving(rows, ctl, state, arrived, leaving, sems):
     again = ctl[MOVE] == ctl[MOVE + 1]
 
     @pl.when(again)
@@ -512,29 +511,34 @@
 
     @pl.when(jnp.logical_not(again))
     def _():
-        pltpu.make_async_copy(state.at[1 - ctl[MOVE]], leaving, sems.at[0]).start()
+        other = state.at[1 - ctl[MOVE], :, rows]
+        pltpu.make_async_copy(other, leaving, sems.at[0]).start()
 
     pltpu.make_async_copy(arrived, leaving, sems.at[0]).wait()
 
 
-def keep_rest(ctl, state, arrived, out, sems):
+def keep_rest(ctl, state, arrived_low, arrived_high, out, sems):
     rest = out.at[1 - ctl[MOVE + 1]]
     again = ctl[MOVE] == ctl[MOVE + 1]
-
-    @pl.when(again)
-    def _():
-        pltpu.make_async_copy(state.at[1 - ctl[MOVE]], rest, sems.at[0]).start()
-
-    @pl.when(jnp.logical_not(again))
-    def _():
-        pltpu.make_async_copy(arrived, rest, sems.at[0]).start()
-
-    pltpu.make_async_copy(arrived, rest, sems.at[0]).wait()
-
-
-def keep_last(ctl, arrived, before, out, sems):
+    halves = ((slice(0, HALF), arrived_low), (slice(HALF, TILE), arrived_high))
+    for index, (rows, arrived) in enumerate(halves):
+
+        @pl.when(again)
+        def _(index=index, rows=rows):
+            kept = state.at[1 - ctl[MOVE], :, rows]
+            pltpu.make_async_copy(kept, rest.at[:, rows], sems.at[index]).start()
+
+        @pl.when(jnp.logical_not(again))
+        def _(index=index, rows=rows, arrived=arrived):
+            pltpu.make_async_copy(arrived, rest.at[:, rows], sems.at[index]).start()
+
+    for index, (rows, arrived) in enumerate(halves):
+        pltpu.make_async_copy(arrived, rest.at[:, rows], sems.at[index]).wait()
+
+
+def keep_last(rows, ctl, arrived, before, out, sems):
     del before
-    copy = pltpu.make_async_copy(arrived, out.at[ctl[MOVE + 1]], sems.at[0])
+    copy = pltpu.make_async_copy(arrived, out.at[ctl[MOVE + 1], :, rows], sems.at[0])
     copy.start()
     copy.wait()
 
@@ -578,7 +582,7 @@
 
 def body(state, bed, manning, neighbours, wet, moves):
     shape = f32(*state.shape)
-    tile_shape = f32(*state.shape[1:])
+    half_shape = f32(3, HALF, TILE)
     devices = lax.axis_size("xb") * lax.axis_size("yb")
     sem = [pltpu.SemaphoreType.DMA((1,))]
     whole = pltpu.VMEM(state.shape, jnp.float32)
@@ -615,29 +619,65 @@
             [whole, part, whole, pltpu.SemaphoreType.DMA((3 * CHUNKS,))],
         )(ctl, state, bed)
         more = step + 1 < STEPS
-        extra = (f32(8 * devices, TILE), f32(8, TILE)) if more else (tile_shape,)
+        extra = (f32(8 * devices, TILE), f32(8, TILE)) if more else (half_shape, half_shape)
         outs = call(
             functools.partial(update, step),
             (shape,) + extra,
-            (hbm(), vmem(), vmem()) if more else (hbm(), hbm()),
-            [smem(), vmem(), vmem(), vmem(), hbm(), hbm(), hbm()],
+            (hbm(),) * 3,
+            [smem()] + [hbm()] * 6,
             8 << 20,
-            [whole, part, whole, whole, pltpu.SemaphoreType.DMA((17,))],
+            [
+                whole,
+                part,
+                whole,
+                whole,
+                pltpu.VMEM(got.shape, jnp.float32),
+                pltpu.VMEM(ground.shape, jnp.float32),
+                pltpu.VMEM((8, TILE), jnp.float32),
+                pltpu.VMEM((8 * devices, TILE), jnp.float32),
+                pltpu.VMEM((8, TILE), jnp.float32),
+                pltpu.SemaphoreType.DMA((5 * PARTS + 3,)),
+            ],
         )(ctl, got, ground, columns, state, manning, rate)
         state = outs[0]
         if more:
             _, out, columns = outs
-    arrived = shifted(outs[1], "xb", 1)
-    leaving = call(
-        second_leaving, tile_shape, anywhere(), [smem(), anywhere(), anywhere()], 1 << 20, sem, room=1 << 20
-    )(ctl, state, arrived)
-    arrived_next = shifted(leaving, "xb", 1)
+    halves = (slice(0, HALF), slice(HALF, TILE))
+    room = 1 << 20
+    arrived = [shifted(leaving, "xb", 1) for leaving in outs[1:]]
+    arrived_next = []
+    for rows, got in zip(halves, arrived):
+        leaving = call(
+            functools.partial(second_leaving, rows),
+            half_shape,
+            anywhere(),
+            [smem(), anywhere(), anywhere()],
+            1 << 20,
+            sem,
+            room=room,
+        )(ctl, state, got)
+        arrived_next.append(shifted(leaving, "xb", 1))
     final = call(
-        keep_rest, shape, anywhere(), [smem(), anywhere(), anywhere()], 1 << 20, sem, room=1 << 20
-    )(ctl, state, arrived)
-    return call(
-        keep_last, shape, anywhere(), [smem(), anywhere(), anywhere()], 1 << 20, sem, {2: 0}, 1 << 20
-    )(ctl, arrived_next, final)
+        keep_rest,
+        shape,
+        hbm(),
+        [smem(), anywhere(), anywhere(), anywhere()],
+        1 << 20,
+        [pltpu.SemaphoreType.DMA((2,))],
+        room=room,
+    )(ctl, state, *arrived)
+    for rows, got in zip(halves, arrived_next):
+        final = call(
+            functools.partial(keep_last, rows),
+            shape,
+            hbm(),
+            [smem(), anywhere(), hbm()],
+            1 << 20,
+            sem,
+            {2: 0},
+            room=room,
+        )(ctl, got, final)
+    return final
 
 
 def solution(mesh):

time: 107 us -> 100 us (0.935)
  waiting for transfers between devices: 45.2 us -> 39.3 us
    ppermute x2 -> x4, waiting for transfers between devices: 39.3 us -> 31.3 us  [shifted(): return lax.ppermute(value, axis, pairs)]
    pallas_call x3, Pallas kernels: 19.9 us -> 17.9 us  [body(): call(rates, shape, hbm(), [smem(), hbm(), hbm()], 16 << 20, [whole, part,...]
    all_to_all x3, waiting for transfers between devices: 5.91 us -> 7.97 us  [spread(): lax.all_to_all(fast, ('xb', 'yb'), split_axis=0, concat_axis=0, tiled=True)]
    pallas_call x6 -> x8, Pallas kernels: 18.2 us -> 19.9 us  [the longest x3 14.4 us: body(): call(functools.partial(update, step), (shape,) + extra, (hbm(),) * 3, [sm...]
  transfers between devices with their start and end apart: 5 -> 7, of which waited for: 5 -> 7; matrix products, arithmetic and copies ran while one was open for 0% -> 0% of each run, Pallas kernels for 20% -> 22%
where the time goes in v8:
time: 100 us
  Pallas kernels  40.5 us (40%)
  waiting for transfers between devices  39.3 us (39%)
  starting transfers between devices  16.6 us (17%)
  local copies, waits for them, and re-layouts  3.42 us (3%)
    ppermute x4, waiting for transfers between devices, shifted(): return lax.ppermute(value, axis, pairs)  31.3 us
    pallas_call x3, Pallas kernels, body(): call(rates, shape, hbm(), [smem(), hbm(), hbm()], 16 << 20, [whole, part,...  17.9 us
    all_to_all x3, starting transfers between devices, spread(): lax.all_to_all(fast, ('xb', 'yb'), split_axis=0, concat_axis=0, tiled=True)  15 us
    pallas_call x3, Pallas kernels, body(): call(functools.partial(update, step), (shape,) + extra, (hbm(),) * 3, [sm...  14.4 us
    all_to_all x3, waiting for transfers between devices, spread(): lax.all_to_all(fast, ('xb', 'yb'), split_axis=0, concat_axis=0, tiled=True)  7.97 us
    unnamed x12, local copies, waits for them, and re-layouts  3.42 us
    pallas_call x1, Pallas kernels, body(): call(opening, (f32(16 * devices, TILE), f32(8, TILE), jax.ShapeDtypeStruc...  2.69 us
    pallas_call x2, Pallas kernels, body(): call(functools.partial(keep_last, rows), shape, hbm(), [smem(), anywhere(...  2.6 us
  transfers between devices with their start and end apart: 7, of which 7 were waited for; matrix products, arithmetic and copies ran while one was open for 0% of the time, Pallas kernels for 22%

profile of v8, /device:TPU:0, one launch (start us, length us, event | category | flops | bytes accessed | tf_op | source)
XLA Modules:
  0.0 100.0 jit_solution(5237608451309981801)
XLA Ops:
  0.0 2.7 %shard_map.64 = (f32[256,256]{1,0:T(8,128)}, f32[8,256]{1,0:T(8,128)}, s32[16]{0:T(128)}) custom-call(f32[2,3,256,256]{3,2,1,0:T(8,128)} %state_in.5, f32[2,256,256]{2,1,0:T(8,128)} %bed_in.7, s32[4,32]{1,0:T(4,128)} %bitcast.16, s32[3,32]{1,0:T(4,128)} %wet_in.1, s32[3,16]{1,0:T(4,128)} %moves_in.1), custom_call_target="tpu_custom_call" | custom-call | flops 4194304 | bytes 4194304 | tf_op jit(solution)/shard_map/pallas_call | solution.py:590
  2.7 7.4 %all-to-all-start = ((f32[16,16,256]{2,1,0:T(8,128)}), f32[16,16,256]{2,1,0:T(8,128)S(1)}, u32[]{:S(2)}, u32[]{:S(2)}) async-start(f32[16,16,256]{2,1,0:T(8,128)} %bitcast.13), calls=%async_computation | async-start | bytes 524288 | tf_op jit(solution)/shard_map/all_to_all | solution.py:580
  10.1 6.0 %shard_map.65.rate_in = f32[2,3,256,256]{3,2,1,0:T(8,128)} custom-call(s32[16]{0:T(128)} %get-tuple-element.17.ctl, f32[2,3,256,256]{3,2,1,0:T(8,128)} %state_in.5, f32[2,256,256]{2,1,0:T(8,128)} %bed_in.7), custom_call_target="tpu_custom_call" | custom-call | flops 16777216 | bytes 4194304 | tf_op jit(solution)/shard_map/pallas_call | solution.py:613
  16.1 4.1 %all-to-all-done = f32[16,16,256]{2,1,0:T(8,128)S(1)} async-done(((f32[16,16,256]{2,1,0:T(8,128)}), f32[16,16,256]{2,1,0:T(8,128)S(1)}, u32[]{:S(2)}, u32[]{:S(2)}) %all-to-all-start) | async-done | bytes 262176 | tf_op jit(solution)/shard_map/all_to_all | solution.py:580
  20.1 0.7 copy-done.3
  20.8 4.8 %shard_map.66 = (f32[2,3,256,256]{3,2,1,0:T(8,128)}, f32[128,256]{1,0:T(8,128)}, f32[8,256]{1,0:T(8,128)}) custom-call(s32[16]{0:T(128)} %get-tuple-element.17.ctl, f32[256,256]{1,0:T(8,128)} %bitcast.7, f32[256,256]{1,0:T(8,128)} %bitcast.8, f32[8,256]{1,0:T(8,128)} %get-tuple-element.19.columns_in, f32[2,3,256,256]{3,2,1,0:T(8,128)} %state_in.5, ...), custom_call_target="tpu_custom_call" | custom-call | flops 8388608 | bytes 4194304 | tf_op jit(solution)/shard_map/pallas_call | solution.py:623
  25.7 3.5 %all-to-all-start.1 = ((f32[16,8,256]{2,1,0:T(8,128)}), f32[16,8,256]{2,1,0:T(8,128)S(1)}, u32[]{:S(2)}, u32[]{:S(2)}) async-start(f32[16,8,256]{2,1,0:T(8,128)} %bitcast.15), calls=%async_computation.1 | async-start | bytes 262144 | tf_op jit(solution)/shard_map/all_to_all | solution.py:580
  29.2 6.0 %shard_map.67.rate_in = f32[2,3,256,256]{3,2,1,0:T(8,128)} custom-call(s32[16]{0:T(128)} %get-tuple-element.17.ctl, f32[2,3,256,256]{3,2,1,0:T(8,128)} %get-tuple-element.22.state_in, f32[2,256,256]{2,1,0:T(8,128)} %bed_in.7), custom_call_target="tpu_custom_call" | custom-call | flops 16777216 | bytes 4194304 | tf_op jit(solution)/shard_map/pallas_call | solution.py:613
  35.2 1.9 %all-to-all-done.1 = f32[16,8,256]{2,1,0:T(8,128)S(1)} async-done(((f32[16,8,256]{2,1,0:T(8,128)}), f32[16,8,256]{2,1,0:T(8,128)S(1)}, u32[]{:S(2)}, u32[]{:S(2)}) %all-to-all-start.1) | async-done | bytes 131104 | tf_op jit(solution)/shard_map/all_to_all | solution.py:580
  37.1 0.7 copy-done.5
  37.8 4.8 %shard_map.68 = (f32[2,3,256,256]{3,2,1,0:T(8,128)}, f32[128,256]{1,0:T(8,128)}, f32[8,256]{1,0:T(8,128)}) custom-call(s32[16]{0:T(128)} %get-tuple-element.17.ctl, f32[128,256]{1,0:T(8,128)} %bitcast.12, f32[256,256]{1,0:T(8,128)} %bitcast.9, f32[8,256]{1,0:T(8,128)} %get-tuple-element.21.columns_in, f32[2,3,256,256]{3,2,1,0:T(8,128)} %get-tuple-element.22.state_in, ...), custom_call_target="tpu_custom_call" | custom-call | flops 8388608 | bytes 4194304 | tf_op jit(solution)/shard_map/pallas_call | solution.py:623
  42.6 4.1 %all-to-all-start.2 = ((f32[16,8,256]{2,1,0:T(8,128)}), f32[16,8,256]{2,1,0:T(8,128)S(1)}, u32[]{:S(2)}, u32[]{:S(2)}) async-start(f32[16,8,256]{2,1,0:T(8,128)} %bitcast.14), calls=%async_computation.2 | async-start | bytes 262144 | tf_op jit(solution)/shard_map/all_to_all | solution.py:580
  46.7 6.0 %shard_map.69.rate_in = f32[2,3,256,256]{3,2,1,0:T(8,128)} custom-call(s32[16]{0:T(128)} %get-tuple-element.17.ctl, f32[2,3,256,256]{3,2,1,0:T(8,128)} %get-tuple-element.25.state_in, f32[2,256,256]{2,1,0:T(8,128)} %bed_in.7), custom_call_target="tpu_custom_call" | custom-call | flops 16777216 | bytes 4194304 | tf_op jit(solution)/shard_map/pallas_call | solution.py:613
  52.7 2.0 %all-to-all-done.2 = f32[16,8,256]{2,1,0:T(8,128)S(1)} async-done(((f32[16,8,256]{2,1,0:T(8,128)}), f32[16,8,256]{2,1,0:T(8,128)S(1)}, u32[]{:S(2)}, u32[]{:S(2)}) %all-to-all-start.2) | async-done | bytes 131104 | tf_op jit(solution)/shard_map/all_to_all | solution.py:580
  54.6 0.7 copy-done.4
  55.3 4.7 %shard_map.70 = (f32[2,3,256,256]{3,2,1,0:T(8,128)}, f32[3,128,256]{2,1,0:T(8,128)}, f32[3,128,256]{2,1,0:T(8,128)}) custom-call(s32[16]{0:T(128)} %get-tuple-element.17.ctl, f32[128,256]{1,0:T(8,128)} %bitcast.11, f32[256,256]{1,0:T(8,128)} %bitcast.10, f32[8,256]{1,0:T(8,128)} %get-tuple-element.24.columns_in, ...), custom_call_target="tpu_custom_call" | custom-call | flops 8388608 | bytes 4194304 | tf_op jit(solution)/shard_map/pallas_call | solution.py:623
  60.0 0.1 collective-permute-start.2
  60.1 1.5 %collective-permute-start = (f32[3,128,256]{2,1,0:T(8,128)}, f32[3,128,256]{2,1,0:T(8,128)S(1)}, u32[]{:S(2)}, u32[]{:S(2)}) collective-permute-start(f32[3,128,256]{2,1,0:T(8,128)} %get-tuple-element.27), channel_id=1, source_target_pairs={{0,2},{2,4},{4,6},{6,8},{8,10},{10,12},{12,14},{14,0},{1,3},{3,5},... | collective-permute-start | bytes 1179656 | tf_op jit(solution)/shard_map/ppermute | solution.py:35
  61.5 13.5 %collective-permute-done.2.arrived.arrived_low = f32[3,128,256]{2,1,0:T(8,128)S(1)} collective-permute-done((f32[3,128,256]{2,1,0:T(8,128)}, f32[3,128,256]{2,1,0:T(8,128)S(1)}, u32[]{:S(2)}, u32[]{:S(2)}) %collective-permute-start.2) | collective-permute-done | bytes 393248 | tf_op jit(solution)/shard_map/ppermute | solution.py:35
  75.0 0.0 copy-done.2
  75.0 1.4 %copy-done = f32[2,3,256,256]{3,2,1,0:T(8,128)S(1)} copy-done((f32[2,3,256,256]{3,2,1,0:T(8,128)S(1)}, f32[2,3,256,256]{3,2,1,0:T(8,128)}, u32[]{:S(2)}) %copy-start) | copy-done | bytes 1572888
  76.4 0.7 shard_map.72
  77.2 0.1 collective-permute-start.3
  77.3 6.2 %collective-permute-done.arrived.arrived_high = f32[3,128,256]{2,1,0:T(8,128)S(1)} collective-permute-done((f32[3,128,256]{2,1,0:T(8,128)}, f32[3,128,256]{2,1,0:T(8,128)S(1)}, u32[]{:S(2)}, u32[]{:S(2)}) %collective-permute-start) | collective-permute-done | bytes 393248 | tf_op jit(solution)/shard_map/ppermute | solution.py:35
  83.4 0.0 copy-done.1
  83.4 0.7 shard_map.71
  84.2 0.1 collective-permute-start.1
  84.3 1.4 %shard_map.73.before = f32[2,3,256,256]{3,2,1,0:T(8,128)} custom-call(s32[16]{0:T(128)S(1)} %copy-done.2, f32[2,3,256,256]{3,2,1,0:T(8,128)S(1)} %copy-done.1, f32[3,128,256]{2,1,0:T(8,128)S(1)} %collective-permute-done.2.arrived.arrived_low, f32[3,128,256]{2,1,0:T(8,128)S(1)} %collective-permute-done.arrived.arrived_high), custom_call_target="tpu_custom_call" | custom-call | flops 1048576 | bytes 4194304 | tf_op jit(solution)/shard_map/pallas_call | solution.py:660
  85.7 6.3 %collective-permute-done.3.arrived = f32[3,128,256]{2,1,0:T(8,128)S(1)} collective-permute-done((f32[3,128,256]{2,1,0:T(8,128)S(1)}, f32[3,128,256]{2,1,0:T(8,128)S(1)}, u32[]{:S(2)}, u32[]{:S(2)}) %collective-permute-start.3) | collective-permute-done | bytes 393248 | tf_op jit(solution)/shard_map/ppermute | solution.py:35
  92.0 1.3 %shard_map.74.before = f32[2,3,256,256]{3,2,1,0:T(8,128)} custom-call(s32[16]{0:T(128)S(1)} %copy-done.2, f32[3,128,256]{2,1,0:T(8,128)S(1)} %collective-permute-done.3.arrived, f32[2,3,256,256]{3,2,1,0:T(8,128)} %shard_map.73.before), custom_call_target="tpu_custom_call", output_to_operand_aliasing={{}: (2, {})} | custom-call | flops 1048576 | bytes 4194304 | tf_op jit(solution)/shard_map/pallas_call | solution.py:670
  93.3 5.4 %collective-permute-done.1.arrived = f32[3,128,256]{2,1,0:T(8,128)S(1)} collective-permute-done((f32[3,128,256]{2,1,0:T(8,128)S(1)}, f32[3,128,256]{2,1,0:T(8,128)S(1)}, u32[]{:S(2)}, u32[]{:S(2)}) %collective-permute-start.1) | collective-permute-done | bytes 393248 | tf_op jit(solution)/shard_map/ppermute | solution.py:35
  98.7 1.3 %shard_map.75 = f32[2,3,256,256]{3,2,1,0:T(8,128)} custom-call(s32[16]{0:T(128)S(1)} %copy-done.2, f32[3,128,256]{2,1,0:T(8,128)S(1)} %collective-permute-done.1.arrived, f32[2,3,256,256]{3,2,1,0:T(8,128)} %shard_map.74.before), custom_call_target="tpu_custom_call", output_to_operand_aliasing={{}: (2, {})} | custom-call | flops 1048576 | bytes 4194304 | tf_op jit(solution)/shard_map/pallas_call | solution.py:670
  (6 shorter events, 0.0 us)
Async XLA Ops:
  2.7 17.4 %all-to-all-start = ((f32[16,16,256]{2,1,0:T(8,128)}), f32[16,16,256]{2,1,0:T(8,128)S(1)}, u32[]{:S(2)}, u32[]{:S(2)}) async-start(f32[16,16,256]{2,1,0:T(8,128)} %bitcast.13), calls=%async_computation | async-start | bytes 524288 | tf_op jit(solution)/shard_map/all_to_all | solution.py:580
  20.1 0.7 copy-start.3
  25.7 11.4 %all-to-all-start.1 = ((f32[16,8,256]{2,1,0:T(8,128)}), f32[16,8,256]{2,1,0:T(8,128)S(1)}, u32[]{:S(2)}, u32[]{:S(2)}) async-start(f32[16,8,256]{2,1,0:T(8,128)} %bitcast.15), calls=%async_computation.1 | async-start | bytes 262144 | tf_op jit(solution)/shard_map/all_to_all | solution.py:580
  37.1 0.7 copy-start.5
  42.6 12.0 %all-to-all-start.2 = ((f32[16,8,256]{2,1,0:T(8,128)}), f32[16,8,256]{2,1,0:T(8,128)S(1)}, u32[]{:S(2)}, u32[]{:S(2)}) async-start(f32[16,8,256]{2,1,0:T(8,128)} %bitcast.14), calls=%async_computation.2 | async-start | bytes 262144 | tf_op jit(solution)/shard_map/all_to_all | solution.py:580
  54.6 0.7 copy-start.4
  55.3 19.7 %copy-start.2 = (s32[16]{0:T(128)S(1)}, s32[16]{0:T(128)}, u32[]{:S(2)}) copy-start(s32[16]{0:T(128)} %get-tuple-element.17.ctl) | copy-start | bytes 196
  60.0 15.0 %collective-permute-start.2 = (f32[3,128,256]{2,1,0:T(8,128)}, f32[3,128,256]{2,1,0:T(8,128)S(1)}, u32[]{:S(2)}, u32[]{:S(2)}) collective-permute-start(f32[3,128,256]{2,1,0:T(8,128)} %get-tuple-element.28), channel_id=1, source_target_pairs={{0,2},{2,4},{4,6},{6,8},{8,10},{10,12},{12,14},{14,0},{1,3},{3,5},... | collective-permute-start | bytes 1179656 | tf_op jit(solution)/shard_map/ppermute | solution.py:35
  60.1 23.4 %collective-permute-start = (f32[3,128,256]{2,1,0:T(8,128)}, f32[3,128,256]{2,1,0:T(8,128)S(1)}, u32[]{:S(2)}, u32[]{:S(2)}) collective-permute-start(f32[3,128,256]{2,1,0:T(8,128)} %get-tuple-element.27), channel_id=1, source_target_pairs={{0,2},{2,4},{4,6},{6,8},{8,10},{10,12},{12,14},{14,0},{1,3},{3,5},... | collective-permute-start | bytes 1179656 | tf_op jit(solution)/shard_map/ppermute | solution.py:35
  75.0 1.4 %copy-start = (f32[2,3,256,256]{3,2,1,0:T(8,128)S(1)}, f32[2,3,256,256]{3,2,1,0:T(8,128)}, u32[]{:S(2)}) copy-start(f32[2,3,256,256]{3,2,1,0:T(8,128)} %get-tuple-element.26.state) | copy-start | bytes 4718596
  76.4 7.0 %copy-start.1 = (f32[2,3,256,256]{3,2,1,0:T(8,128)S(1)}, f32[2,3,256,256]{3,2,1,0:T(8,128)}, u32[]{:S(2)}) copy-start(f32[2,3,256,256]{3,2,1,0:T(8,128)} %get-tuple-element.26.state) | copy-start | bytes 4718596
  77.2 14.8 %collective-permute-start.3 = (f32[3,128,256]{2,1,0:T(8,128)S(1)}, f32[3,128,256]{2,1,0:T(8,128)S(1)}, u32[]{:S(2)}, u32[]{:S(2)}) collective-permute-start(f32[3,128,256]{2,1,0:T(8,128)S(1)} %shard_map.72), channel_id=1, source_target_pairs={{0,2},{2,4},{4,6},{6,8},{8,10},{10,12},{12,14},{14,0},{1,3},{3,5},... | collective-permute-start | bytes 1179656 | tf_op jit(solution)/shard_map/ppermute | solution.py:35
  84.2 14.5 %collective-permute-start.1 = (f32[3,128,256]{2,1,0:T(8,128)S(1)}, f32[3,128,256]{2,1,0:T(8,128)S(1)}, u32[]{:S(2)}, u32[]{:S(2)}) collective-permute-start(f32[3,128,256]{2,1,0:T(8,128)S(1)} %shard_map.71), channel_id=1, source_target_pairs={{0,2},{2,4},{4,6},{6,8},{8,10},{10,12},{12,14},{14,0},{1,3},{3,5},... | collective-permute-start | bytes 1179656 | tf_op jit(solution)/shard_map/ppermute | solution.py:35

commit v9 on v8

--- a/solution.py
+++ b/solution.py
@@ -17,10 +17,13 @@
 TILE = 256
 VMEM_BYTES = 60 * 1024 * 1024
 SLOT_LOW, WALL_WEST, WALL_EAST, WALL_OUTER, WET, MOVE = 0, 1, 3, 5, 7, 13
-CONTROLS = 16
+WET_FIRST, WET_SECOND = 16, 19
+CONTROLS = 24
+EARLY = 96
+LATE = (TILE - EARLY + 16) // 2
+CUT = TILE - LATE
 CHUNKS = 8
 PARTS = 8
-HALF = TILE // 2
 STRIP = 16
 TOP = 6
 SCALE = 0.5 / SPACING
@@ -142,9 +145,9 @@
 
 
 def opening(
-    state_in, bed_in, neighbours_in, wet_in, moves_in,
-    out, columns, ctl,
-    state, bed, neighbours, wet, moves, sems,
+    state_in, bed_in, manning_in, neighbours_in, wet_in, moves_in,
+    out, columns, ctl, leaving,
+    state, bed, manning, neighbours, wet, moves, sems,
 ):
     copies = start_all(
         (
@@ -172,6 +175,21 @@
         for slot in range(2):
             ctl[WET + 2 * step + slot] = wet[step, first + slot]
         ctl[MOVE + step] = moves[step, device]
+    moving = moves[0, device]
+    rough = start_all(((manning_in.at[moving, 0:EARLY], manning),), sems, 6)
+    count = lax.axis_size("xb")
+    upper = lax.axis_index("yb")
+    column = lax.axis_index("xb")
+    source = lax.rem(column + count - 1, count) * 2 + upper
+    before = lax.rem(column + count - 2, count) * 2 + upper
+    again = moves[0, source] == moves[1, source]
+    tile_first = source * 2 + moves[0, source]
+    tile_second = jnp.where(
+        again, before * 2 + moves[0, before], source * 2 + 1 - moves[0, source]
+    )
+    for step in range(STEPS):
+        ctl[WET_FIRST + step] = wet[step, tile_first]
+        ctl[WET_SECOND + step] = wet[step, tile_second]
 
     total = jnp.zeros((ROWS, TILE), jnp.float32)
     for slot in range(2):
@@ -185,10 +203,64 @@
         best = lax.fori_loop(0, TILE // ROWS, group, jnp.zeros((ROWS, TILE), jnp.float32))
         total = jnp.maximum(total, jnp.where(wet[0, first + slot] > 0, best, 0.0))
     copies[5].wait()
+    wait_all(rough)
+    early = start_all(
+        (
+            (state.at[moving, :, 0:EARLY], leaving.at[0:3]),
+            (bed.at[moving, 0:EARLY], leaving.at[3]),
+            (manning, leaving.at[4]),
+        ),
+        sems,
+        7,
+    )
     messages(ctl, state, bed, jnp.max(total, keepdims=True), out, columns)
-
-
-def rates(ctl, state_in, bed_in, rate_out, state, bed, rate, sems):
+    wait_all(early)
+
+
+def hold(order, leaving, same):
+    del order, leaving, same
+
+
+class Passing:
+    def __init__(self, ctl, state_in, bed_in, manning_in, arrived, leaving, buffer, sems):
+        self.again = ctl[MOVE] == ctl[MOVE + 1]
+        self.other = 1 - ctl[MOVE]
+        self.refs = state_in, bed_in, manning_in, arrived, leaving, buffer, sems
+
+    def start(self):
+        state_in, bed_in, manning_in, arrived, _, buffer, sems = self.refs
+        rows = slice(0, EARLY)
+        sem = sems.at[0]
+
+        @pl.when(self.again)
+        def _():
+            pltpu.make_async_copy(arrived, buffer, sem).start()
+
+        @pl.when(jnp.logical_not(self.again))
+        def _():
+            pltpu.make_async_copy(state_in.at[self.other, :, rows], buffer.at[0:3], sem).start()
+            pltpu.make_async_copy(bed_in.at[self.other, rows], buffer.at[3], sem).start()
+            pltpu.make_async_copy(manning_in.at[self.other, rows], buffer.at[4], sem).start()
+
+    def middle(self):
+        _, _, _, arrived, leaving, buffer, sems = self.refs
+        pltpu.make_async_copy(arrived, buffer, sems.at[0]).wait()
+        pltpu.make_async_copy(buffer, leaving, sems.at[1]).start()
+
+    def end(self):
+        _, _, _, _, leaving, buffer, sems = self.refs
+        pltpu.make_async_copy(buffer, leaving, sems.at[1]).wait()
+
+
+def rates_and_leaving(
+    ctl, state_in, bed_in, state_first, manning_in, arrived, rate_out, leaving,
+    state, bed, rate, sems, buffer, moving,
+):
+    passing = Passing(ctl, state_first, bed_in, manning_in, arrived, leaving, buffer, moving)
+    rates(ctl, state_in, bed_in, rate_out, state, bed, rate, sems, passing)
+
+
+def rates(ctl, state_in, bed_in, rate_out, state, bed, rate, sems, passing=None):
     width = 2 * TILE
     row_ids = lax.broadcasted_iota(jnp.int32, (STRIP, width), 0)
     row8 = sublanes(width)
@@ -209,6 +281,8 @@
                 2 * part,
             )
         )
+    if passing:
+        passing.start()
     keep_west, keep_east, keep_south, keep_north = (
         jnp.where(flag(ctl, index), 1.0, 0.0)
         for index in (WALL_WEST, WALL_EAST, WALL_OUTER, WALL_OUTER + 1)
@@ -326,7 +400,208 @@
         outgoing += start_all(
             ((rate.at[:, :, rows], rate_out.at[:, :, rows]),), sems, 2 * CHUNKS + part
         )
+        if passing and part == CHUNKS // 2:
+            passing.middle()
     wait_all(outgoing)
+    if passing:
+        passing.end()
+
+
+def moved_on(old, slopes, rough, delta, wet_now):
+    h, hu, hv = (value - delta * slope for value, slope in zip(old, slopes))
+    inverse = 1.0 / h
+    u = hu * inverse
+    v = hv * inverse
+    speed = jnp.sqrt(u * u + v * v)
+    power = jnp.exp((-4.0 / 3.0) * jnp.log(jnp.abs(h)))
+    drag = (GRAVITY * delta) * (rough * rough) * (speed * power)
+    factor = 1.0 / (1.0 + drag)
+    fresh = (h, hu * factor, hv * factor)
+    return tuple(jnp.where(wet_now, new, value) for new, value in zip(fresh, old))
+
+
+def repeat_steps(ctl, wet_from, deltas, early, work, other, sems):
+    chunk = EARLY // 3
+    incoming = []
+    for part in range(3):
+        rows = slice(part * chunk, (part + 1) * chunk)
+        incoming += start_all(((early.at[:, rows], work.at[:, rows]),), sems, part)
+    row_ids = lax.broadcasted_iota(jnp.int32, (ROWS, TILE), 0)
+    lane = lax.broadcasted_iota(jnp.int32, (ROWS, LANES), 1)
+    start = tuple(jnp.zeros((1, TILE), jnp.float32) for _ in range(4))
+
+    def halves(value):
+        return value[:, :LANES], value[:, LANES:]
+
+    def right_of(value):
+        low, high = (pltpu.roll(part, LANES - 1, 1) for part in halves(value))
+        return jnp.concatenate([jnp.where(lane == LANES - 1, high, low), high], 1)
+
+    def left_of(value):
+        low, high = (pltpu.roll(part, 1, 1) for part in halves(value))
+        return jnp.concatenate([low, jnp.where(lane == 0, low, high)], 1)
+
+    def down(value):
+        return pltpu.roll(value, ROWS + 7, 0)[:ROWS]
+
+    for step in range(STEPS):
+        source, target = (work, other) if step % 2 == 0 else (other, work)
+        delta = deltas[step][0:1, :]
+        wet_now = flag(ctl, wet_from + step)
+
+        def group(index, carry, source=source, target=target, delta=delta, wet_now=wet_now):
+            base = pl.multiple_of(index * ROWS, ROWS)
+            rows = pl.ds(base, ROWS)
+            after = pl.ds(pl.multiple_of(jnp.minimum(base + ROWS, EARLY - 8), 8), 8)
+            refs = [source.at[field] for field in range(3)] + [work.at[3]]
+            fields = [jnp.concatenate([ref[rows, :], ref[after, :]], 0) for ref in refs]
+            cells_x, cells_y = cell(*fields[:3])
+            here_x = tuple(value[:ROWS] for value in cells_x)
+            here_y = tuple(value[:ROWS] for value in cells_y)
+            faces_x = face(here_x, tuple(down(value) for value in cells_x))
+            turned = tuple(pltpu.roll(value, 1, 0) for value in faces_x)
+            change_x = tuple(
+                value - jnp.where(row_ids == 0, before, moved)
+                for value, before, moved in zip(faces_x, carry[:3], turned)
+            )
+            ground = fields[3][:ROWS]
+            ground_up = pltpu.roll(ground, 1, 0)
+            slope_x = down(fields[3]) - jnp.where(row_ids == 0, carry[3], ground_up)
+            carried = tuple(value[0:1, :] for value in turned) + (ground_up[0:1, :],)
+            faces_y = face(here_y, tuple(right_of(value) for value in here_y))
+            change_y = tuple(value - left_of(value) for value in faces_y)
+            slope_y = right_of(ground) - left_of(ground)
+            old = tuple(value[:ROWS] for value in fields[:3])
+            weight = SLOPE * old[0]
+            slopes = (
+                SCALE * (change_x[0] + change_y[0]),
+                SCALE * (change_x[1] + change_y[2]) + weight * slope_x,
+                SCALE * (change_x[2] + change_y[1]) + weight * slope_y,
+            )
+            for field, value in enumerate(
+                moved_on(old, slopes, work[4, rows, :], delta, wet_now)
+            ):
+                target[field, rows, :] = value
+            return carried
+
+        per_chunk = chunk // ROWS
+        if step == 0:
+            carry = start
+            incoming[0].wait()
+            for part in range(3):
+                if part < 2:
+                    incoming[part + 1].wait()
+                carry = lax.fori_loop(part * per_chunk, (part + 1) * per_chunk, group, carry)
+        else:
+            lax.fori_loop(0, EARLY // ROWS, group, start)
+
+
+def late_rows(tile, late):
+    row = sublanes()
+    kept = EARLY - 8
+    lane = lax.broadcasted_iota(jnp.int32, (8, LANES), 1)
+    for field in range(3):
+        late[field, 0:8, :] = jnp.where(
+            row < 3, tile[field, 0:8, :], tile[field, kept : kept + 8, :]
+        )
+        packed = [jnp.zeros((8, LANES), jnp.float32)] * 2
+        for block in range(EARLY // 8):
+            rows = slice(8 * block, 8 * block + 8)
+            sides = jnp.where(lane < 64, tile[field, rows, :LANES], tile[field, rows, LANES:])
+            turned = pltpu.roll(sides, (3 + 8 * block) % LANES, 1)
+            which = block // 16
+            packed[which] = jnp.where(lane // 8 == block % 16, turned, packed[which])
+        late[field, 8:16, :] = jnp.concatenate(packed, 1)
+        late[field, 16:, :] = tile[field, EARLY:CUT, :]
+
+
+def merge(late, early, tile):
+    row = sublanes()
+    lane = lax.broadcasted_iota(jnp.int32, (8, LANES), 1)
+    for field in range(3):
+        first = late[field, 0:8, :]
+        for block in range(EARLY // 8):
+            rows = slice(8 * block, 8 * block + 8)
+            which = block // 16
+            packed = late[field, 8:16, which * LANES : (which + 1) * LANES]
+            sides = pltpu.roll(packed, (-3 - 8 * block) % LANES, 1)
+            value = early[field, rows, :]
+            value = jnp.concatenate(
+                [
+                    jnp.where(lane < 3, sides, value[:, :LANES]),
+                    jnp.where(lane >= LANES - 3, sides, value[:, LANES:]),
+                ],
+                1,
+            )
+            if block == 0:
+                value = jnp.where(row < 3, first, value)
+            if block == EARLY // 8 - 1:
+                value = jnp.where(row < 5, value, first)
+            tile[field, rows, :] = value
+        tile[field, EARLY:, :] = late[field, 16:, :]
+
+
+def repeat_second(ctl, delta0, delta1, delta2, early, out, work, tile, sems):
+    repeat_steps(ctl, WET_SECOND, (delta0, delta1, delta2), early, work, tile, sems)
+    copy = pltpu.make_async_copy(tile, out, sems.at[0])
+    copy.start()
+    copy.wait()
+
+
+def repeat_first(
+    ctl, delta0, delta1, delta2, early, late_in, plain_in, staying, out,
+    work, other, tile, late, sems,
+):
+    rest = out.at[1 - ctl[MOVE + 1]]
+    again = ctl[MOVE] == ctl[MOVE + 1]
+    low, high = tile.at[:, :CUT], tile.at[:, CUT:]
+
+    @pl.when(again)
+    def _():
+        copy = pltpu.make_async_copy(staying, tile, sems.at[3])
+        copy.start()
+        copy.wait()
+
+    @pl.when(jnp.logical_not(again))
+    def _():
+        copies = start_all(((late_in, late), (plain_in, high)), sems, 3)
+        repeat_steps(ctl, WET_FIRST, (delta0, delta1, delta2), early, work, other, sems)
+        wait_all(copies)
+        merge(late, other, low)
+
+    copy = pltpu.make_async_copy(tile, rest, sems.at[3])
+    copy.start()
+    copy.wait()
+
+
+def finish_low(ctl, late_in, early_in, before, out, late, early, tile, sems):
+    del before
+    wait_all(start_all(((late_in, late), (early_in, early)), sems))
+    merge(late, early, tile)
+    wait_all(start_all(((tile, out.at[ctl[MOVE + 1], :, 0:CUT]),), sems))
+
+
+def finish_high(ctl, plain_in, before, out, plain, sems):
+    del before
+    wait_all(start_all(((plain_in, plain),), sems))
+    wait_all(start_all(((plain, out.at[ctl[MOVE + 1], :, CUT:]),), sems))
+
+
+def second_late(is_low, ctl, arrived, own, order, leaving, buffer, sems):
+    del order
+    again = ctl[MOVE] == ctl[MOVE + 1]
+
+    @pl.when(again)
+    def _():
+        pltpu.make_async_copy(arrived, buffer, sems.at[0]).start()
+
+    @pl.when(jnp.logical_not(again))
+    def _():
+        source = own if is_low else own.at[:, CUT:]
+        pltpu.make_async_copy(source, buffer, sems.at[0]).start()
+
+    pltpu.make_async_copy(arrived, buffer, sems.at[0]).wait()
+    wait_all(start_all(((buffer, leaving),), sems))
 
 
 def correct_rows(ctl, slot, got, ground, block, state, rate, bottom):
@@ -388,11 +663,10 @@
 def update(step, ctl, got_in, ground_in, columns_in, state_in, manning_in, rate_in, *rest):
     more = step + 1 < STEPS
     if more:
-        fresh_out, out_to, columns_to = rest[:3]
-        rest = rest[3:]
+        fresh_out, out_to, columns_to, delta_out = rest[:4]
     else:
-        fresh_out, leaving_low, leaving_high = rest[:3]
-        rest = rest[3:]
+        staying, late_first, late_second, plain_first, delta_out = rest[:5]
+    rest = rest[4 if more else 5 :]
     state, manning, rate, fresh, got, ground, columns, out, columns_out, sems = rest
     small = start_all(
         ((got_in, got), (ground_in, ground), (columns_in, columns)), sems, 5 * PARTS
@@ -422,6 +696,7 @@
     for peer in range(1, devices):
         tops = jnp.maximum(tops, got[peer * block : peer * block + 8, :])
     delta = (COURANT * SPACING) / tops[TOP : TOP + 1, :]
+    delta_out[...] = jnp.broadcast_to(delta, (8, TILE))
     fix = column_fix(got, ground, block, columns, None)
     facing = jnp.where(upper > 0, ctl[SLOT_LOW], 1 - ctl[SLOT_LOW])
     begin = pl.multiple_of((1 - upper) * LANES, LANES)
@@ -450,23 +725,9 @@
 
         def group(index, best, slot=slot, wet_now=wet_now):
             rows = pl.ds(pl.multiple_of(index * ROWS, ROWS), ROWS)
-            h0, hu0, hv0 = (state[slot, field, rows, :] for field in range(3))
-            h = h0 - delta * rate[slot, 0, rows, :]
-            hu = hu0 - delta * rate[slot, 1, rows, :]
-            hv = hv0 - delta * rate[slot, 2, rows, :]
-            rough = manning[slot, rows, :]
-            inverse = 1.0 / h
-            u = hu * inverse
-            v = hv * inverse
-            speed = jnp.sqrt(u * u + v * v)
-            power = jnp.exp((-4.0 / 3.0) * jnp.log(jnp.abs(h)))
-            drag = (GRAVITY * delta) * (rough * rough) * (speed * power)
-            factor = 1.0 / (1.0 + drag)
-            hu = hu * factor
-            hv = hv * factor
-            h = jnp.where(wet_now, h, h0)
-            hu = jnp.where(wet_now, hu, hu0)
-            hv = jnp.where(wet_now, hv, hv0)
+            old = tuple(state[slot, field, rows, :] for field in range(3))
+            slopes = tuple(rate[slot, field, rows, :] for field in range(3))
+            h, hu, hv = moved_on(old, slopes, manning[slot, rows, :], delta, wet_now)
             fresh[slot, 0, rows, :] = h
             fresh[slot, 1, rows, :] = hu
             fresh[slot, 2, rows, :] = hv
@@ -484,63 +745,23 @@
         if more:
             best = jnp.where(flag(ctl, WET + 2 * step + 2 + slot), best, 0.0)
             total = jnp.maximum(total, best)
-        outgoing += start_all(
-            ((fresh.at[slot, :, part_rows], fresh_out.at[slot, :, part_rows]),),
-            sems,
-            3 * PARTS + index,
-        )
+        if more:
+            outgoing += start_all(
+                ((fresh.at[slot, :, part_rows], fresh_out.at[slot, :, part_rows]),),
+                sems,
+                3 * PARTS + index,
+            )
     if more:
         messages(ctl, fresh, None, jnp.max(total, keepdims=True), out, columns_out)
         outgoing += start_all(((out, out_to), (columns_out, columns_to)), sems, 4 * PARTS)
     else:
-        tile = fresh.at[ctl[MOVE]]
+        first, second = fresh.at[ctl[MOVE]], fresh.at[1 - ctl[MOVE]]
         outgoing += start_all(
-            ((tile.at[:, :HALF], leaving_low), (tile.at[:, HALF:], leaving_high)),
-            sems,
-            4 * PARTS,
-        )
+            ((first.at[:, CUT:], plain_first), (second, staying)), sems, 4 * PARTS
+        )
+        late_rows(first, late_first)
+        late_rows(second, late_second)
     wait_all(outgoing)
-
-
-def second_leaving(rows, ctl, state, arrived, leaving, sems):
-    again = ctl[MOVE] == ctl[MOVE + 1]
-
-    @pl.when(again)
-    def _():
-        pltpu.make_async_copy(arrived, leaving, sems.at[0]).start()
-
-    @pl.when(jnp.logical_not(again))
-    def _():
-        other = state.at[1 - ctl[MOVE], :, rows]
-        pltpu.make_async_copy(other, leaving, sems.at[0]).start()
-
-    pltpu.make_async_copy(arrived, leaving, sems.at[0]).wait()
-
-
-def keep_rest(ctl, state, arrived_low, arrived_high, out, sems):
-    rest = out.at[1 - ctl[MOVE + 1]]
-    again = ctl[MOVE] == ctl[MOVE + 1]
-    halves = ((slice(0, HALF), arrived_low), (slice(HALF, TILE), arrived_high))
-    for index, (rows, arrived) in enumerate(halves):
-
-        @pl.when(again)
-        def _(index=index, rows=rows):
-            kept = state.at[1 - ctl[MOVE], :, rows]
-            pltpu.make_async_copy(kept, rest.at[:, rows], sems.at[index]).start()
-
-        @pl.when(jnp.logical_not(again))
-        def _(index=index, rows=rows, arrived=arrived):
-            pltpu.make_async_copy(arrived, rest.at[:, rows], sems.at[index]).start()
-
-    for index, (rows, arrived) in enumerate(halves):
-        pltpu.make_async_copy(arrived, rest.at[:, rows], sems.at[index]).wait()
-
-
-def keep_last(rows, ctl, arrived, before, out, sems):
-    del before
-    copy = pltpu.make_async_copy(arrived, out.at[ctl[MOVE + 1], :, rows], sems.at[0])
-    copy.start()
-    copy.wait()
 
 
 def vmem():
@@ -582,48 +803,76 @@
 
 def body(state, bed, manning, neighbours, wet, moves):
     shape = f32(*state.shape)
-    half_shape = f32(3, HALF, TILE)
     devices = lax.axis_size("xb") * lax.axis_size("yb")
     sem = [pltpu.SemaphoreType.DMA((1,))]
     whole = pltpu.VMEM(state.shape, jnp.float32)
     part = pltpu.VMEM(bed.shape, jnp.float32)
-    out, columns, ctl = call(
+    tile_shape = f32(*state.shape[1:])
+    early_shape = f32(5, EARLY, TILE)
+    early_state = f32(3, EARLY, TILE)
+    late_shape = f32(3, LATE, TILE)
+    delta_shape = f32(8, TILE)
+
+    def buffer(like):
+        return pltpu.VMEM(like.shape, jnp.float32)
+
+    out, columns, ctl, leaving = call(
         opening,
         (
             f32(16 * devices, TILE),
             f32(8, TILE),
             jax.ShapeDtypeStruct((CONTROLS,), jnp.int32),
+            early_shape,
         ),
-        (vmem(), vmem(), smem()),
-        [hbm()] * 5,
+        (vmem(), vmem(), smem(), hbm()),
+        [hbm()] * 6,
         4 << 20,
         [
             whole,
             part,
+            pltpu.VMEM((EARLY, TILE), jnp.float32),
             pltpu.SMEM(neighbours.shape[::-1], jnp.int32),
             pltpu.SMEM(wet.shape, jnp.int32),
             pltpu.SMEM(moves.shape, jnp.int32),
-            pltpu.SemaphoreType.DMA((6,)),
+            pltpu.SemaphoreType.DMA((10,)),
         ],
-    )(state, bed, neighbours.T, wet, moves)
+    )(state, bed, manning, neighbours.T, wet, moves)
+    state_first = state
     ground = None
+    deltas = []
+    early = []
     for step in range(STEPS):
         got = spread(out)
         ground = got if step == 0 else ground
-        rate = call(
-            rates,
-            shape,
-            hbm(),
-            [smem(), hbm(), hbm()],
-            16 << 20,
-            [whole, part, whole, pltpu.SemaphoreType.DMA((3 * CHUNKS,))],
-        )(ctl, state, bed)
+        scratch = [whole, part, whole, pltpu.SemaphoreType.DMA((3 * CHUNKS,))]
+        if step == 1:
+            rate, leaving = call(
+                rates_and_leaving,
+                (shape, early_shape),
+                (hbm(), hbm()),
+                [smem()] + [hbm()] * 5,
+                16 << 20,
+                scratch + [buffer(early_shape), pltpu.SemaphoreType.DMA((2,))],
+            )(ctl, state, bed, state_first, manning, early[0])
+        else:
+            rate = call(rates, shape, hbm(), [smem(), hbm(), hbm()], 16 << 20, scratch)(
+                ctl, state, bed
+            )
         more = step + 1 < STEPS
-        extra = (f32(8 * devices, TILE), f32(8, TILE)) if more else (half_shape, half_shape)
+        if more:
+            leaving = call(
+                hold, early_shape, hbm(), [hbm(), hbm()], 1 << 10, aliases={1: 0}
+            )(got, leaving)
+            early.append(shifted(leaving, "xb", 1))
+            shapes = (shape, f32(8 * devices, TILE), f32(8, TILE), delta_shape)
+            places = (hbm(), hbm(), hbm(), vmem())
+        else:
+            shapes = (tile_shape, late_shape, late_shape, late_shape, delta_shape)
+            places = (hbm(), vmem(), vmem(), hbm(), vmem())
         outs = call(
             functools.partial(update, step),
-            (shape,) + extra,
-            (hbm(),) * 3,
+            shapes,
+            places,
             [smem()] + [hbm()] * 6,
             8 << 20,
             [
@@ -639,45 +888,77 @@
                 pltpu.SemaphoreType.DMA((5 * PARTS + 3,)),
             ],
         )(ctl, got, ground, columns, state, manning, rate)
-        state = outs[0]
+        deltas.append(outs[-1])
         if more:
-            _, out, columns = outs
-    halves = (slice(0, HALF), slice(HALF, TILE))
-    room = 1 << 20
-    arrived = [shifted(leaving, "xb", 1) for leaving in outs[1:]]
-    arrived_next = []
-    for rows, got in zip(halves, arrived):
+            state, out, columns, _ = outs
+    staying, late_first, late_second, plain_first, _ = outs
+    room = 16 << 20
+    late_arrived = shifted(late_first, "xb", 1)
+    plain_arrived = shifted(plain_first, "xb", 1)
+    second = call(
+        repeat_second,
+        early_state,
+        anywhere(),
+        [smem()] + [vmem()] * 3 + [anywhere()],
+        8 << 20,
+        [buffer(early_shape), buffer(early_state), pltpu.SemaphoreType.DMA((3,))],
+        room=room,
+    )(ctl, *deltas, early[1])
+
+    def pass_late(is_low, arrived, own):
         leaving = call(
-            functools.partial(second_leaving, rows),
-            half_shape,
+            functools.partial(second_late, is_low),
+            late_shape,
             anywhere(),
-            [smem(), anywhere(), anywhere()],
+            [smem(), anywhere(), anywhere(), anywhere()],
             1 << 20,
-            sem,
+            [buffer(late_shape)] + sem,
             room=room,
-        )(ctl, state, got)
-        arrived_next.append(shifted(leaving, "xb", 1))
+        )(ctl, arrived, own, second)
+        return shifted(leaving, "xb", 1)
+
+    late_next = pass_late(True, late_arrived, late_second)
+    plain_next = pass_late(False, plain_arrived, staying)
     final = call(
-        keep_rest,
+        repeat_first,
         shape,
         hbm(),
-        [smem(), anywhere(), anywhere(), anywhere()],
+        [smem()] + [vmem()] * 3 + [anywhere()] * 4,
+        8 << 20,
+        [
+            buffer(early_shape),
+            buffer(early_state),
+            buffer(tile_shape),
+            buffer(late_shape),
+            pltpu.SemaphoreType.DMA((5,)),
+        ],
+        room=room,
+    )(ctl, *deltas, early[0], late_arrived, plain_arrived, staying)
+    final = call(
+        finish_low,
+        shape,
+        hbm(),
+        [smem(), anywhere(), anywhere(), hbm()],
         1 << 20,
-        [pltpu.SemaphoreType.DMA((2,))],
+        [
+            buffer(late_shape),
+            buffer(early_state),
+            pltpu.VMEM((3, CUT, TILE), jnp.float32),
+            pltpu.SemaphoreType.DMA((2,)),
+        ],
+        {3: 0},
         room=room,
-    )(ctl, state, *arrived)
-    for rows, got in zip(halves, arrived_next):
-        final = call(
-            functools.partial(keep_last, rows),
-            shape,
-            hbm(),
-            [smem(), anywhere(), hbm()],
-            1 << 20,
-            sem,
-            {2: 0},
-            room=room,
-        )(ctl, got, final)
-    return final
+    )(ctl, late_next, second, final)
+    return call(
+        finish_high,
+        shape,
+        hbm(),
+        [smem(), anywhere(), hbm()],
+        1 << 20,
+        [buffer(late_shape)] + sem,
+        {2: 0},
+        room=room,
+    )(ctl, plain_next, final)
 
 
 def solution(mesh):

time: 100 us -> 103 us (1.030)
  waiting for transfers between devices: 39.3 us -> 16.1 us
  blocking collectives: 0 us -> 17.5 us
  Pallas kernels: 40.5 us -> 49.2 us
    all_to_all x0 -> x1, blocking collectives: none -> 17.5 us  [spread(): lax.all_to_all(fast, ('xb', 'yb'), split_axis=0, concat_axis=0, tiled=True)]
    ppermute x4 -> x6, waiting for transfers between devices: 31.3 us -> 14.5 us  [shifted(): return lax.ppermute(value, axis, pairs)]
    pallas_call x11 -> x14, Pallas kernels: 37.8 us -> 45.8 us  [the longest x3 16.5 us: body(): call(functools.partial(update, step), shapes, places, [smem()] + [hbm()]...]
    all_to_all x3 -> x2, waiting for transfers between devices: 7.97 us -> 1.62 us  [spread(): lax.all_to_all(fast, ('xb', 'yb'), split_axis=0, concat_axis=0, tiled=True)]
    all_to_all x3 -> x2, starting transfers between devices: 15 us -> 11 us  [spread(): lax.all_to_all(fast, ('xb', 'yb'), split_axis=0, concat_axis=0, tiled=True)]
    ppermute x4 -> x6, starting transfers between devices: 1.65 us -> 4.65 us  [shifted(): return lax.ppermute(value, axis, pairs)]
    unnamed x12 -> x22, local copies, waits for them, and re-layouts: 3.42 us -> 3.71 us
  transfers between devices with their start and end apart: 7 -> 8, of which waited for: 7 -> 7; matrix products, arithmetic and copies ran while one was open for 0% -> 0% of each run, Pallas kernels for 22% -> 38%
where the time goes in v9:
time: 103 us
  Pallas kernels  49.2 us (48%)
  blocking collectives  17.5 us (17%)
  waiting for transfers between devices  16.1 us (16%)
  starting transfers between devices  15.6 us (15%)
  local copies, waits for them, and re-layouts  3.71 us (4%)
    all_to_all x1, blocking collectives, spread(): lax.all_to_all(fast, ('xb', 'yb'), split_axis=0, concat_axis=0, tiled=True)  17.5 us
    pallas_call x3, Pallas kernels, body(): call(functools.partial(update, step), shapes, places, [smem()] + [hbm()]...  16.5 us
    ppermute x6, waiting for transfers between devices, shifted(): return lax.ppermute(value, axis, pairs)  14.5 us
    pallas_call x2, Pallas kernels, body(): call(rates, shape, hbm(), [smem(), hbm(), hbm()], 16 << 20, scratch)  11.9 us
    all_to_all x2, starting transfers between devices, spread(): lax.all_to_all(fast, ('xb', 'yb'), split_axis=0, concat_axis=0, tiled=True)  11 us
    pallas_call x1, Pallas kernels, body(): call(rates_and_leaving, (shape, early_shape), (hbm(), hbm()), [smem()] +...  5.98 us
    ppermute x6, starting transfers between devices, shifted(): return lax.ppermute(value, axis, pairs)  4.65 us
    pallas_call x1, Pallas kernels, body(): call(repeat_first, shape, hbm(), [smem()] + [vmem()] * 3 + [anywhere()] *...  4.14 us
  transfers between devices with their start and end apart: 8, of which 7 were waited for; matrix products, arithmetic and copies ran while one was open for 0% of the time, Pallas kernels for 38%

profile of v9, /device:TPU:0, one launch (start us, length us, event | category | flops | bytes accessed | tf_op | source)
XLA Modules:
  0.0 102.6 jit_solution(4009667161458749900)
XLA Ops:
  0.0 3.4 %shard_map.64 = (f32[256,256]{1,0:T(8,128)}, f32[8,256]{1,0:T(8,128)}, s32[24]{0:T(128)}, f32[5,96,256]{2,1,0:T(8,128)}) custom-call(f32[2,3,256,256]{3,2,1,0:T(8,128)} %state_first.1, f32[2,256,256]{2,1,0:T(8,128)} %bed_in.7, f32[2,256,256]{2,1,0:T(8,128)} %manning_in.9, s32[4,32]{1,0:T(4,128)} %bitcast.18, s32[3,32]{1,0:T(4,128)} %wet_in.1, s32[3,16]{1,0:T(4,128)} %moves_in.1), custom_call_target="tpu_custom_call" | custom-call | flops 4194304 | bytes 4194304 | tf_op jit(solution)/shard_map/pallas_call | solution.py:819
  3.4 17.5 %all_to_all.33 = f32[16,16,256]{2,1,0:T(8,128)} all-to-all(f32[16,16,256]{2,1,0:T(8,128)} %bitcast.15), channel_id=1, replica_groups=mesh['runs'=2,'xb'=8,'yb'=2] {'xb','yb'}, dimensions={0} | all-to-all | bytes 524288 | tf_op jit(solution)/shard_map/all_to_all | solution.py:801
  21.0 6.0 %shard_map.65.rate_in = f32[2,3,256,256]{3,2,1,0:T(8,128)} custom-call(s32[24]{0:T(128)} %get-tuple-element.24.ctl, f32[2,3,256,256]{3,2,1,0:T(8,128)} %state_first.1, f32[2,256,256]{2,1,0:T(8,128)} %bed_in.7), custom_call_target="tpu_custom_call" | custom-call | flops 16777216 | bytes 4194304 | tf_op jit(solution)/shard_map/pallas_call | solution.py:858
  27.0 5.6 %shard_map.66 = (f32[2,3,256,256]{3,2,1,0:T(8,128)}, f32[128,256]{1,0:T(8,128)}, f32[8,256]{1,0:T(8,128)}, f32[8,256]{1,0:T(8,128)}) custom-call(s32[24]{0:T(128)} %get-tuple-element.24.ctl, f32[256,256]{1,0:T(8,128)} %bitcast.8, f32[256,256]{1,0:T(8,128)} %bitcast.9, f32[8,256]{1,0:T(8,128)} %get-tuple-element.26.columns_in, ...), custom_call_target="tpu_custom_call" | custom-call | flops 8388608 | bytes 4194304 | tf_op jit(solution)/shard_map/pallas_call | solution.py:872
  32.5 6.1 %all-to-all-start.1 = ((f32[16,8,256]{2,1,0:T(8,128)}), f32[16,8,256]{2,1,0:T(8,128)S(1)}, u32[]{:S(2)}, u32[]{:S(2)}) async-start(f32[16,8,256]{2,1,0:T(8,128)} %bitcast.17), calls=%async_computation.1 | async-start | bytes 262144 | tf_op jit(solution)/shard_map/all_to_all | solution.py:801
  38.7 0.8 copy-done.1
  39.4 6.0 %shard_map.68 = (f32[2,3,256,256]{3,2,1,0:T(8,128)}, f32[5,96,256]{2,1,0:T(8,128)}) custom-call(s32[24]{0:T(128)} %get-tuple-element.24.ctl, f32[2,3,256,256]{3,2,1,0:T(8,128)} %get-tuple-element.29.state_in, f32[2,256,256]{2,1,0:T(8,128)} %bed_in.7, f32[2,3,256,256]{3,2,1,0:T(8,128)} %state_first.1, f32[2,256,256]{2,1,0:T(8,128)} %manning_in.9, ...), custom_call_target="tpu_custom_call" | custom-call | flops 16777216 | bytes 4194304 | tf_op jit(solution)/shard_map/pallas_call | solution.py:849
  45.4 1.2 %all-to-all-done.1 = f32[16,8,256]{2,1,0:T(8,128)S(1)} async-done(((f32[16,8,256]{2,1,0:T(8,128)}), f32[16,8,256]{2,1,0:T(8,128)S(1)}, u32[]{:S(2)}, u32[]{:S(2)}) %all-to-all-start.1) | async-done | bytes 131104 | tf_op jit(solution)/shard_map/all_to_all | solution.py:801
  46.6 0.6 copy-done.9
  47.2 5.4 %shard_map.69 = (f32[2,3,256,256]{3,2,1,0:T(8,128)}, f32[128,256]{1,0:T(8,128)}, f32[8,256]{1,0:T(8,128)}, f32[8,256]{1,0:T(8,128)}) custom-call(s32[24]{0:T(128)} %get-tuple-element.24.ctl, f32[128,256]{1,0:T(8,128)} %bitcast.12, f32[256,256]{1,0:T(8,128)} %bitcast.10, f32[8,256]{1,0:T(8,128)} %get-tuple-element.28.columns_in, ...), custom_call_target="tpu_custom_call" | custom-call | flops 8388608 | bytes 4194304 | tf_op jit(solution)/shard_map/pallas_call | solution.py:872
  52.7 4.9 %all-to-all-start.2 = ((f32[16,8,256]{2,1,0:T(8,128)}), f32[16,8,256]{2,1,0:T(8,128)S(1)}, u32[]{:S(2)}, u32[]{:S(2)}) async-start(f32[16,8,256]{2,1,0:T(8,128)} %bitcast.16), calls=%async_computation.2 | async-start | bytes 262144 | tf_op jit(solution)/shard_map/all_to_all | solution.py:801
  57.5 2.0 %collective-permute-start.2 = (f32[5,96,256]{2,1,0:T(8,128)}, f32[5,96,256]{2,1,0:T(8,128)S(1)}, u32[]{:S(2)}, u32[]{:S(2)}) collective-permute-start(f32[5,96,256]{2,1,0:T(8,128)} %shard_map.72), channel_id=1, source_target_pairs={{0,2},{2,4},{4,6},{6,8},{8,10},{10,12},{12,14},{14,0},{1,3},{3,5},... | collective-permute-start | bytes 1474568 | tf_op jit(solution)/shard_map/ppermute | solution.py:38
  59.5 6.0 %shard_map.70.rate_in = f32[2,3,256,256]{3,2,1,0:T(8,128)} custom-call(s32[24]{0:T(128)} %get-tuple-element.24.ctl, f32[2,3,256,256]{3,2,1,0:T(8,128)} %get-tuple-element.34.state_in, f32[2,256,256]{2,1,0:T(8,128)} %bed_in.7), custom_call_target="tpu_custom_call" | custom-call | flops 16777216 | bytes 4194304 | tf_op jit(solution)/shard_map/pallas_call | solution.py:858
  65.5 0.5 all-to-all-done.2
  65.9 0.6 copy-done.10
  66.6 5.5 %shard_map.71 = (f32[3,256,256]{2,1,0:T(8,128)}, f32[3,88,256]{2,1,0:T(8,128)}, f32[3,88,256]{2,1,0:T(8,128)}, f32[3,88,256]{2,1,0:T(8,128)}, f32[8,256]{1,0:T(8,128)}) custom-call(s32[24]{0:T(128)} %get-tuple-element.24.ctl, f32[128,256]{1,0:T(8,128)} %bitcast.14, f32[256,256]{1,0:T(8,128)} %bitcast.11, f32[8,256]{1,0:T(8,128)} %get-tuple-element.33.columns_in, ...), custom_call_target="tpu_custom_call" | custom-call | flops 8388608 | bytes 4194304 | tf_op jit(solution)/shard_map/pallas_call | solution.py:872
  72.1 1.1 %collective-permute-start.4 = (f32[3,88,256]{2,1,0:T(8,128)}, f32[3,88,256]{2,1,0:T(8,128)S(1)}, u32[]{:S(2)}, u32[]{:S(2)}) collective-permute-start(f32[3,88,256]{2,1,0:T(8,128)} %get-tuple-element.41), channel_id=1, source_target_pairs={{0,2},{2,4},{4,6},{6,8},{8,10},{10,12},{12,14},{14,0},{1,3},{3,5},... | collective-permute-start | bytes 811016 | tf_op jit(solution)/shard_map/ppermute | solution.py:38
  73.2 1.5 %collective-permute-start.1 = (f32[3,88,256]{2,1,0:T(8,128)}, f32[3,88,256]{2,1,0:T(8,128)S(1)}, u32[]{:S(2)}, u32[]{:S(2)}) collective-permute-start(f32[3,88,256]{2,1,0:T(8,128)} %get-tuple-element.35), channel_id=1, source_target_pairs={{0,2},{2,4},{4,6},{6,8},{8,10},{10,12},{12,14},{14,0},{1,3},{3,5},... | collective-permute-start | bytes 811016 | tf_op jit(solution)/shard_map/ppermute | solution.py:38
  74.7 1.3 %collective-permute-done.2.early = f32[5,96,256]{2,1,0:T(8,128)S(1)} collective-permute-done((f32[5,96,256]{2,1,0:T(8,128)}, f32[5,96,256]{2,1,0:T(8,128)S(1)}, u32[]{:S(2)}, u32[]{:S(2)}) %collective-permute-start.2) | collective-permute-done | bytes 491552 | tf_op jit(solution)/shard_map/ppermute | solution.py:38
  76.0 0.7 copy-done.7
  76.7 3.0 %shard_map.73.order.early_in = f32[3,96,256]{2,1,0:T(8,128)S(1)} custom-call(s32[24]{0:T(128)S(1)} %copy-done.4, f32[8,256]{1,0:T(8,128)S(1)} %copy-done.5, f32[8,256]{1,0:T(8,128)S(1)} %copy-done.6, f32[8,256]{1,0:T(8,128)S(1)} %copy-done.7, f32[5,96,256]{2,1,0:T(8,128)S(1)} %collective-permute-done.2.early), custom_call_target="tpu_custom_call" | custom-call | flops 8388608 | bytes 4194304 | tf_op jit(solution)/shard_map/pallas_call | solution.py:898
  79.7 4.8 %collective-permute-done.4.arrived.late_in = f32[3,88,256]{2,1,0:T(8,128)S(1)} collective-permute-done((f32[3,88,256]{2,1,0:T(8,128)}, f32[3,88,256]{2,1,0:T(8,128)S(1)}, u32[]{:S(2)}, u32[]{:S(2)}) %collective-permute-start.4) | collective-permute-done | bytes 270368 | tf_op jit(solution)/shard_map/ppermute | solution.py:38
  84.5 1.0 copy-done.3
  85.5 0.6 shard_map.75
  86.1 0.1 collective-permute-start.5
  86.2 2.8 %collective-permute-done.1.arrived.plain_in = f32[3,88,256]{2,1,0:T(8,128)S(1)} collective-permute-done((f32[3,88,256]{2,1,0:T(8,128)}, f32[3,88,256]{2,1,0:T(8,128)S(1)}, u32[]{:S(2)}, u32[]{:S(2)}) %collective-permute-start.1) | collective-permute-done | bytes 270368 | tf_op jit(solution)/shard_map/ppermute | solution.py:38
  89.0 0.7 shard_map.74
  89.8 4.1 %shard_map.76.before = f32[2,3,256,256]{3,2,1,0:T(8,128)} custom-call(s32[24]{0:T(128)S(1)} %copy-done.4, f32[8,256]{1,0:T(8,128)S(1)} %copy-done.5, f32[8,256]{1,0:T(8,128)S(1)} %copy-done.6, f32[8,256]{1,0:T(8,128)S(1)} %copy-done.8, f32[5,96,256]{2,1,0:T(8,128)S(1)} %copy-done.2, f32[3,88,256]{2,1,0:T(8,128)S(1)} %collective-permute-done.4.arrived.late_in, ...), custom_call_target="tpu_custom_call" | custom-call | flops 8388608 | bytes 4194304 | tf_op jit(solution)/shard_map/pallas_call | solution.py:922
  94.0 3.5 %collective-permute-done.5.late_in = f32[3,88,256]{2,1,0:T(8,128)S(1)} collective-permute-done((f32[3,88,256]{2,1,0:T(8,128)S(1)}, f32[3,88,256]{2,1,0:T(8,128)S(1)}, u32[]{:S(2)}, u32[]{:S(2)}) %collective-permute-start.5) | collective-permute-done | bytes 270368 | tf_op jit(solution)/shard_map/ppermute | solution.py:38
  97.5 1.5 %shard_map.77.before = f32[2,3,256,256]{3,2,1,0:T(8,128)} custom-call(s32[24]{0:T(128)S(1)} %copy-done.4, f32[3,88,256]{2,1,0:T(8,128)S(1)} %collective-permute-done.5.late_in, f32[3,96,256]{2,1,0:T(8,128)S(1)} %shard_map.73.order.early_in, f32[2,3,256,256]{3,2,1,0:T(8,128)} %shard_map.76.before), custom_call_target="tpu_custom_call", output_to_operand_aliasing={{}: (3, {})} | custom-call | flops 1048576 | bytes 4194304 | tf_op jit(solution)/shard_map/pallas_call | solution.py:937
  99.1 2.1 %collective-permute-done.3.plain_in = f32[3,88,256]{2,1,0:T(8,128)S(1)} collective-permute-done((f32[3,88,256]{2,1,0:T(8,128)S(1)}, f32[3,88,256]{2,1,0:T(8,128)S(1)}, u32[]{:S(2)}, u32[]{:S(2)}) %collective-permute-start.3) | collective-permute-done | bytes 270368 | tf_op jit(solution)/shard_map/ppermute | solution.py:38
  101.1 1.3 %shard_map.78 = f32[2,3,256,256]{3,2,1,0:T(8,128)} custom-call(s32[24]{0:T(128)S(1)} %copy-done.4, f32[3,88,256]{2,1,0:T(8,128)S(1)} %collective-permute-done.3.plain_in, f32[2,3,256,256]{3,2,1,0:T(8,128)} %shard_map.77.before), custom_call_target="tpu_custom_call", output_to_operand_aliasing={{}: (2, {})} | custom-call | flops 1048576 | bytes 4194304 | tf_op jit(solution)/shard_map/pallas_call | solution.py:952
  (22 shorter events, 0.1 us)
Async XLA Ops:
  21.0 17.7 %collective-permute-start = (f32[5,96,256]{2,1,0:T(8,128)}, f32[5,96,256]{2,1,0:T(8,128)S(1)}, u32[]{:S(2)}, u32[]{:S(2)}) collective-permute-start(f32[5,96,256]{2,1,0:T(8,128)} %shard_map.67), channel_id=1, source_target_pairs={{0,2},{2,4},{4,6},{6,8},{8,10},{10,12},{12,14},{14,0},{1,3},{3,5},... | collective-permute-start | bytes 1474568 | tf_op jit(solution)/shard_map/ppermute | solution.py:38
  32.5 14.1 %all-to-all-start.1 = ((f32[16,8,256]{2,1,0:T(8,128)}), f32[16,8,256]{2,1,0:T(8,128)S(1)}, u32[]{:S(2)}, u32[]{:S(2)}) async-start(f32[16,8,256]{2,1,0:T(8,128)} %bitcast.17), calls=%async_computation.1 | async-start | bytes 262144 | tf_op jit(solution)/shard_map/all_to_all | solution.py:801
  38.6 0.8 copy-start.1
  46.6 0.6 copy-start.9
  52.7 13.3 %all-to-all-start.2 = ((f32[16,8,256]{2,1,0:T(8,128)}), f32[16,8,256]{2,1,0:T(8,128)S(1)}, u32[]{:S(2)}, u32[]{:S(2)}) async-start(f32[16,8,256]{2,1,0:T(8,128)} %bitcast.16), calls=%async_computation.2 | async-start | bytes 262144 | tf_op jit(solution)/shard_map/all_to_all | solution.py:801
  57.5 18.5 %collective-permute-start.2 = (f32[5,96,256]{2,1,0:T(8,128)}, f32[5,96,256]{2,1,0:T(8,128)S(1)}, u32[]{:S(2)}, u32[]{:S(2)}) collective-permute-start(f32[5,96,256]{2,1,0:T(8,128)} %shard_map.72), channel_id=1, source_target_pairs={{0,2},{2,4},{4,6},{6,8},{8,10},{10,12},{12,14},{14,0},{1,3},{3,5},... | collective-permute-start | bytes 1474568 | tf_op jit(solution)/shard_map/ppermute | solution.py:38
  65.9 0.6 copy-start.10
  66.6 9.4 %copy-start.4 = (s32[24]{0:T(128)S(1)}, s32[24]{0:T(128)}, u32[]{:S(2)}) copy-start(s32[24]{0:T(128)} %get-tuple-element.24.ctl) | copy-start | bytes 292
  66.6 9.4 %copy-start.5 = (f32[8,256]{1,0:T(8,128)S(1)}, f32[8,256]{1,0:T(8,128)}, u32[]{:S(2)}) copy-start(f32[8,256]{1,0:T(8,128)} %get-tuple-element.37.delta0) | copy-start | bytes 24580
  66.6 9.4 %copy-start.6 = (f32[8,256]{1,0:T(8,128)S(1)}, f32[8,256]{1,0:T(8,128)}, u32[]{:S(2)}) copy-start(f32[8,256]{1,0:T(8,128)} %get-tuple-element.38.delta1) | copy-start | bytes 24580
  72.1 16.9 %copy-start = (f32[3,256,256]{2,1,0:T(8,128)S(1)}, f32[3,256,256]{2,1,0:T(8,128)}, u32[]{:S(2)}) copy-start(f32[3,256,256]{2,1,0:T(8,128)} %get-tuple-element.36.own.staying) | copy-start | bytes 2359300
  72.1 12.4 %collective-permute-start.4 = (f32[3,88,256]{2,1,0:T(8,128)}, f32[3,88,256]{2,1,0:T(8,128)S(1)}, u32[]{:S(2)}, u32[]{:S(2)}) collective-permute-start(f32[3,88,256]{2,1,0:T(8,128)} %get-tuple-element.41), channel_id=1, source_target_pairs={{0,2},{2,4},{4,6},{6,8},{8,10},{10,12},{12,14},{14,0},{1,3},{3,5},... | collective-permute-start | bytes 811016 | tf_op jit(solution)/shard_map/ppermute | solution.py:38
  73.2 15.8 %collective-permute-start.1 = (f32[3,88,256]{2,1,0:T(8,128)}, f32[3,88,256]{2,1,0:T(8,128)S(1)}, u32[]{:S(2)}, u32[]{:S(2)}) collective-permute-start(f32[3,88,256]{2,1,0:T(8,128)} %get-tuple-element.35), channel_id=1, source_target_pairs={{0,2},{2,4},{4,6},{6,8},{8,10},{10,12},{12,14},{14,0},{1,3},{3,5},... | collective-permute-start | bytes 811016 | tf_op jit(solution)/shard_map/ppermute | solution.py:38
  76.0 0.7 copy-start.7
  76.7 13.1 %copy-start.2 = (f32[5,96,256]{2,1,0:T(8,128)S(1)}, f32[5,96,256]{2,1,0:T(8,128)}, u32[]{:S(2)}) copy-start(f32[5,96,256]{2,1,0:T(8,128)} %copy-done.1) | copy-start | bytes 1474564
  84.5 1.0 copy-start.3
  85.5 4.3 %copy-start.8 = (f32[8,256]{1,0:T(8,128)S(1)}, f32[8,256]{1,0:T(8,128)}, u32[]{:S(2)}) copy-start(f32[8,256]{1,0:T(8,128)} %get-tuple-element.39.delta2) | copy-start | bytes 24580
  86.1 11.4 %collective-permute-start.5 = (f32[3,88,256]{2,1,0:T(8,128)S(1)}, f32[3,88,256]{2,1,0:T(8,128)S(1)}, u32[]{:S(2)}, u32[]{:S(2)}) collective-permute-start(f32[3,88,256]{2,1,0:T(8,128)S(1)} %shard_map.75), channel_id=1, source_target_pairs={{0,2},{2,4},{4,6},{6,8},{8,10},{10,12},{12,14},{14,0},{1,3},{3,5},... | collective-permute-start | bytes 811016 | tf_op jit(solution)/shard_map/ppermute | solution.py:38
  89.7 11.4 %collective-permute-start.3 = (f32[3,88,256]{2,1,0:T(8,128)S(1)}, f32[3,88,256]{2,1,0:T(8,128)S(1)}, u32[]{:S(2)}, u32[]{:S(2)}) collective-permute-start(f32[3,88,256]{2,1,0:T(8,128)S(1)} %shard_map.74), channel_id=1, source_target_pairs={{0,2},{2,4},{4,6},{6,8},{8,10},{10,12},{12,14},{14,0},{1,3},{3,5},... | collective-permute-start | bytes 811016 | tf_op jit(solution)/shard_map/ppermute | solution.py:38

commit v10 on v9

--- a/solution.py
+++ b/solution.py
@@ -19,9 +19,9 @@
 SLOT_LOW, WALL_WEST, WALL_EAST, WALL_OUTER, WET, MOVE = 0, 1, 3, 5, 7, 13
 WET_FIRST, WET_SECOND = 16, 19
 CONTROLS = 24
-EARLY = 96
-LATE = (TILE - EARLY + 16) // 2
-CUT = TILE - LATE
+EARLY = 160
+PIECES = ((0, 80), (80, 160))
+LATE = TILE - EARLY + 16
 CHUNKS = 8
 PARTS = 8
 STRIP = 16
@@ -217,18 +217,18 @@
     wait_all(early)
 
 
-def hold(order, leaving, same):
-    del order, leaving, same
-
-
 class Passing:
     def __init__(self, ctl, state_in, bed_in, manning_in, arrived, leaving, buffer, sems):
         self.again = ctl[MOVE] == ctl[MOVE + 1]
         self.other = 1 - ctl[MOVE]
-        self.refs = state_in, bed_in, manning_in, arrived, leaving, buffer, sems
+        self.refs = state_in, bed_in, manning_in, arrived, buffer, sems
+        self.outgoing = [
+            pltpu.make_async_copy(buffer.at[:, begin:end], piece, sems.at[1 + index])
+            for index, ((begin, end), piece) in enumerate(zip(PIECES, leaving))
+        ]
 
     def start(self):
-        state_in, bed_in, manning_in, arrived, _, buffer, sems = self.refs
+        state_in, bed_in, manning_in, arrived, buffer, sems = self.refs
         rows = slice(0, EARLY)
         sem = sems.at[0]
 
@@ -243,21 +243,28 @@
             pltpu.make_async_copy(manning_in.at[self.other, rows], buffer.at[4], sem).start()
 
     def middle(self):
-        _, _, _, arrived, leaving, buffer, sems = self.refs
+        _, _, _, arrived, buffer, sems = self.refs
         pltpu.make_async_copy(arrived, buffer, sems.at[0]).wait()
-        pltpu.make_async_copy(buffer, leaving, sems.at[1]).start()
+        for copy in self.outgoing:
+            copy.start()
 
     def end(self):
-        _, _, _, _, leaving, buffer, sems = self.refs
-        pltpu.make_async_copy(buffer, leaving, sems.at[1]).wait()
+        wait_all(self.outgoing)
 
 
 def rates_and_leaving(
-    ctl, state_in, bed_in, state_first, manning_in, arrived, rate_out, leaving,
+    ctl, state_in, bed_in, state_first, manning_in, arrived, rate_out, leaving_low, leaving_high,
     state, bed, rate, sems, buffer, moving,
 ):
-    passing = Passing(ctl, state_first, bed_in, manning_in, arrived, leaving, buffer, moving)
+    passing = Passing(
+        ctl, state_first, bed_in, manning_in, arrived, (leaving_low, leaving_high), buffer, moving
+    )
     rates(ctl, state_in, bed_in, rate_out, state, bed, rate, sems, passing)
+
+
+def rates_after(ctl, state_in, bed_in, order, *rest):
+    del order
+    rates(ctl, state_in, bed_in, *rest)
 
 
 def rates(ctl, state_in, bed_in, rate_out, state, bed, rate, sems, passing=None):
@@ -421,11 +428,12 @@
 
 
 def repeat_steps(ctl, wet_from, deltas, early, work, other, sems):
-    chunk = EARLY // 3
     incoming = []
-    for part in range(3):
-        rows = slice(part * chunk, (part + 1) * chunk)
-        incoming += start_all(((early.at[:, rows], work.at[:, rows]),), sems, part)
+    for ref in early:
+        begin = 0 if ref is early[0] else early[0].shape[1]
+        incoming += start_all(
+            ((ref, work.at[:, begin : begin + ref.shape[1]]),), sems, len(incoming)
+        )
     row_ids = lax.broadcasted_iota(jnp.int32, (ROWS, TILE), 0)
     lane = lax.broadcasted_iota(jnp.int32, (ROWS, LANES), 1)
     start = tuple(jnp.zeros((1, TILE), jnp.float32) for _ in range(4))
@@ -484,16 +492,9 @@
                 target[field, rows, :] = value
             return carried
 
-        per_chunk = chunk // ROWS
         if step == 0:
-            carry = start
-            incoming[0].wait()
-            for part in range(3):
-                if part < 2:
-                    incoming[part + 1].wait()
-                carry = lax.fori_loop(part * per_chunk, (part + 1) * per_chunk, group, carry)
-        else:
-            lax.fori_loop(0, EARLY // ROWS, group, start)
+            wait_all(incoming)
+        lax.fori_loop(0, EARLY // ROWS, group, start)
 
 
 def late_rows(tile, late):
@@ -512,7 +513,7 @@
             which = block // 16
             packed[which] = jnp.where(lane // 8 == block % 16, turned, packed[which])
         late[field, 8:16, :] = jnp.concatenate(packed, 1)
-        late[field, 16:, :] = tile[field, EARLY:CUT, :]
+        late[field, 16:, :] = tile[field, EARLY:, :]
 
 
 def merge(late, early, tile):
@@ -541,53 +542,39 @@
         tile[field, EARLY:, :] = late[field, 16:, :]
 
 
-def repeat_second(ctl, delta0, delta1, delta2, early, out, work, tile, sems):
-    repeat_steps(ctl, WET_SECOND, (delta0, delta1, delta2), early, work, tile, sems)
-    copy = pltpu.make_async_copy(tile, out, sems.at[0])
-    copy.start()
-    copy.wait()
+def repeat_second(ctl, delta0, delta1, delta2, low, high, out, work, tile, sems):
+    repeat_steps(ctl, WET_SECOND, (delta0, delta1, delta2), (low, high), work, tile, sems)
+    wait_all(start_all(((tile, out),), sems))
 
 
 def repeat_first(
-    ctl, delta0, delta1, delta2, early, late_in, plain_in, staying, out,
-    work, other, tile, late, sems,
+    ctl, delta0, delta1, delta2, early, late_in, staying, out, work, other, tile, late, sems
 ):
     rest = out.at[1 - ctl[MOVE + 1]]
     again = ctl[MOVE] == ctl[MOVE + 1]
-    low, high = tile.at[:, :CUT], tile.at[:, CUT:]
 
     @pl.when(again)
     def _():
-        copy = pltpu.make_async_copy(staying, tile, sems.at[3])
-        copy.start()
-        copy.wait()
+        wait_all(start_all(((staying, tile),), sems))
 
     @pl.when(jnp.logical_not(again))
     def _():
-        copies = start_all(((late_in, late), (plain_in, high)), sems, 3)
-        repeat_steps(ctl, WET_FIRST, (delta0, delta1, delta2), early, work, other, sems)
+        copies = start_all(((late_in, late),), sems, 1)
+        repeat_steps(ctl, WET_FIRST, (delta0, delta1, delta2), (early,), work, other, sems)
         wait_all(copies)
-        merge(late, other, low)
-
-    copy = pltpu.make_async_copy(tile, rest, sems.at[3])
-    copy.start()
-    copy.wait()
-
-
-def finish_low(ctl, late_in, early_in, before, out, late, early, tile, sems):
+        merge(late, other, tile)
+
+    wait_all(start_all(((tile, rest),), sems))
+
+
+def finish(ctl, late_in, early_in, before, out, late, early, tile, sems):
     del before
     wait_all(start_all(((late_in, late), (early_in, early)), sems))
     merge(late, early, tile)
-    wait_all(start_all(((tile, out.at[ctl[MOVE + 1], :, 0:CUT]),), sems))
-
-
-def finish_high(ctl, plain_in, before, out, plain, sems):
-    del before
-    wait_all(start_all(((plain_in, plain),), sems))
-    wait_all(start_all(((plain, out.at[ctl[MOVE + 1], :, CUT:]),), sems))
-
-
-def second_late(is_low, ctl, arrived, own, order, leaving, buffer, sems):
+    wait_all(start_all(((tile, out.at[ctl[MOVE + 1]]),), sems))
+
+
+def second_late(ctl, arrived, own, order, leaving, buffer, sems):
     del order
     again = ctl[MOVE] == ctl[MOVE + 1]
 
@@ -597,8 +584,7 @@
 
     @pl.when(jnp.logical_not(again))
     def _():
-        source = own if is_low else own.at[:, CUT:]
-        pltpu.make_async_copy(source, buffer, sems.at[0]).start()
+        pltpu.make_async_copy(own, buffer, sems.at[0]).start()
 
     pltpu.make_async_copy(arrived, buffer, sems.at[0]).wait()
     wait_all(start_all(((buffer, leaving),), sems))
@@ -665,9 +651,9 @@
     if more:
         fresh_out, out_to, columns_to, delta_out = rest[:4]
     else:
-        staying, late_first, late_second, plain_first, delta_out = rest[:5]
-    rest = rest[4 if more else 5 :]
-    state, manning, rate, fresh, got, ground, columns, out, columns_out, sems = rest
+        staying, late_first, late_second, delta_out = rest[:4]
+    rest = rest[4:]
+    state, manning, rate, fresh, got, ground, columns, out, columns_out, delta_keep, sems = rest
     small = start_all(
         ((got_in, got), (ground_in, ground), (columns_in, columns)), sems, 5 * PARTS
     )
@@ -696,14 +682,14 @@
     for peer in range(1, devices):
         tops = jnp.maximum(tops, got[peer * block : peer * block + 8, :])
     delta = (COURANT * SPACING) / tops[TOP : TOP + 1, :]
-    delta_out[...] = jnp.broadcast_to(delta, (8, TILE))
+    delta_keep[...] = jnp.broadcast_to(delta, (8, TILE))
+    outgoing = start_all(((delta_keep, delta_out),), sems, 5 * PARTS + 3)
     fix = column_fix(got, ground, block, columns, None)
     facing = jnp.where(upper > 0, ctl[SLOT_LOW], 1 - ctl[SLOT_LOW])
     begin = pl.multiple_of((1 - upper) * LANES, LANES)
     target = (1 - upper) * (LANES - 1)
     lane = lax.broadcasted_iota(jnp.int32, (size, LANES), 1)
     total = jnp.zeros((ROWS, TILE), jnp.float32)
-    outgoing = []
     for index, (slot, part_rows) in enumerate(parts):
         wait_all(incoming[index])
         if part_rows.start == 0:
@@ -756,9 +742,7 @@
         outgoing += start_all(((out, out_to), (columns_out, columns_to)), sems, 4 * PARTS)
     else:
         first, second = fresh.at[ctl[MOVE]], fresh.at[1 - ctl[MOVE]]
-        outgoing += start_all(
-            ((first.at[:, CUT:], plain_first), (second, staying)), sems, 4 * PARTS
-        )
+        outgoing += start_all(((second, staying),), sems, 4 * PARTS)
         late_rows(first, late_first)
         late_rows(second, late_second)
     wait_all(outgoing)
@@ -780,7 +764,9 @@
     return pl.BlockSpec(memory_space=pl.ANY)
 
 
-def call(kernel, outs, out_specs, in_specs, flops, scratch=(), aliases=None, room=VMEM_BYTES):
+def call(
+    kernel, outs, out_specs, in_specs, flops, scratch=(), aliases=None, room=VMEM_BYTES, moved=4
+):
     return pl.pallas_call(
         kernel,
         scratch_shapes=scratch,
@@ -789,7 +775,7 @@
         in_specs=in_specs,
         out_specs=out_specs,
         compiler_params=pltpu.CompilerParams(vmem_limit_bytes=room),
-        cost_estimate=pl.CostEstimate(flops=flops, bytes_accessed=4 << 20, transcendentals=0),
+        cost_estimate=pl.CostEstimate(flops=flops, bytes_accessed=moved << 20, transcendentals=0),
     )
 
 
@@ -840,35 +826,36 @@
     state_first = state
     ground = None
     deltas = []
-    early = []
     for step in range(STEPS):
         got = spread(out)
         ground = got if step == 0 else ground
         scratch = [whole, part, whole, pltpu.SemaphoreType.DMA((3 * CHUNKS,))]
-        if step == 1:
-            rate, leaving = call(
-                rates_and_leaving,
-                (shape, early_shape),
-                (hbm(), hbm()),
-                [smem()] + [hbm()] * 5,
-                16 << 20,
-                scratch + [buffer(early_shape), pltpu.SemaphoreType.DMA((2,))],
-            )(ctl, state, bed, state_first, manning, early[0])
-        else:
+        if step == 0:
+            early_first = shifted(leaving, "xb", 1)
             rate = call(rates, shape, hbm(), [smem(), hbm(), hbm()], 16 << 20, scratch)(
                 ctl, state, bed
             )
+        elif step == 1:
+            rate, *leaving = call(
+                rates_and_leaving,
+                (shape,) + tuple(f32(5, end - begin, TILE) for begin, end in PIECES),
+                (hbm(),) * 3,
+                [smem()] + [hbm()] * 5,
+                16 << 20,
+                scratch + [buffer(early_shape), pltpu.SemaphoreType.DMA((3,))],
+            )(ctl, state, bed, state_first, manning, early_first)
+            early_second = [shifted(piece, "xb", 1) for piece in leaving]
+        else:
+            rate = call(rates_after, shape, hbm(), [smem()] + [hbm()] * 3, 16 << 20, scratch)(
+                ctl, state, bed, early_second[0]
+            )
         more = step + 1 < STEPS
         if more:
-            leaving = call(
-                hold, early_shape, hbm(), [hbm(), hbm()], 1 << 10, aliases={1: 0}
-            )(got, leaving)
-            early.append(shifted(leaving, "xb", 1))
             shapes = (shape, f32(8 * devices, TILE), f32(8, TILE), delta_shape)
-            places = (hbm(), hbm(), hbm(), vmem())
+            places = (hbm(),) * 4
         else:
-            shapes = (tile_shape, late_shape, late_shape, late_shape, delta_shape)
-            places = (hbm(), vmem(), vmem(), hbm(), vmem())
+            shapes = (tile_shape, late_shape, late_shape, delta_shape)
+            places = (hbm(), vmem(), vmem(), hbm())
         outs = call(
             functools.partial(update, step),
             shapes,
@@ -885,57 +872,53 @@
                 pltpu.VMEM((8, TILE), jnp.float32),
                 pltpu.VMEM((8 * devices, TILE), jnp.float32),
                 pltpu.VMEM((8, TILE), jnp.float32),
-                pltpu.SemaphoreType.DMA((5 * PARTS + 3,)),
+                buffer(delta_shape),
+                pltpu.SemaphoreType.DMA((5 * PARTS + 4,)),
             ],
+            moved=9 if step == 0 else 4,
         )(ctl, got, ground, columns, state, manning, rate)
         deltas.append(outs[-1])
         if more:
             state, out, columns, _ = outs
-    staying, late_first, late_second, plain_first, _ = outs
+    staying, late_first, late_second, _ = outs
     room = 16 << 20
     late_arrived = shifted(late_first, "xb", 1)
-    plain_arrived = shifted(plain_first, "xb", 1)
     second = call(
         repeat_second,
         early_state,
         anywhere(),
-        [smem()] + [vmem()] * 3 + [anywhere()],
+        [smem()] + [vmem()] * 3 + [anywhere()] * 2,
         8 << 20,
-        [buffer(early_shape), buffer(early_state), pltpu.SemaphoreType.DMA((3,))],
+        [buffer(early_shape), buffer(early_state), pltpu.SemaphoreType.DMA((2,))],
         room=room,
-    )(ctl, *deltas, early[1])
-
-    def pass_late(is_low, arrived, own):
-        leaving = call(
-            functools.partial(second_late, is_low),
-            late_shape,
-            anywhere(),
-            [smem(), anywhere(), anywhere(), anywhere()],
-            1 << 20,
-            [buffer(late_shape)] + sem,
-            room=room,
-        )(ctl, arrived, own, second)
-        return shifted(leaving, "xb", 1)
-
-    late_next = pass_late(True, late_arrived, late_second)
-    plain_next = pass_late(False, plain_arrived, staying)
+    )(ctl, *deltas, *early_second)
+    leaving = call(
+        second_late,
+        late_shape,
+        anywhere(),
+        [smem(), anywhere(), anywhere(), anywhere()],
+        1 << 20,
+        [buffer(late_shape)] + sem,
+        room=room,
+    )(ctl, late_arrived, late_second, second)
+    late_next = shifted(leaving, "xb", 1)
     final = call(
         repeat_first,
         shape,
         hbm(),
-        [smem()] + [vmem()] * 3 + [anywhere()] * 4,
+        [smem()] + [vmem()] * 3 + [anywhere()] * 3,
         8 << 20,
         [
             buffer(early_shape),
             buffer(early_state),
             buffer(tile_shape),
             buffer(late_shape),
-            pltpu.SemaphoreType.DMA((5,)),
+            pltpu.SemaphoreType.DMA((2,)),
         ],
         room=room,
-    )(ctl, *deltas, early[0], late_arrived, plain_arrived, staying)
-    final = call(
-        finish_low,
+    )(ctl, *deltas, early_first, late_arrived, staying)
+    return call(
+        finish,
         shape,
         hbm(),
         [smem(), anywhere(), anywhere(), hbm()],
@@ -943,22 +926,12 @@
         [
             buffer(late_shape),
             buffer(early_state),
-            pltpu.VMEM((3, CUT, TILE), jnp.float32),
+            buffer(tile_shape),
             pltpu.SemaphoreType.DMA((2,)),
         ],
         {3: 0},
         room=room,
     )(ctl, late_next, second, final)
-    return call(
-        finish_high,
-        shape,
-        hbm(),
-        [smem(), anywhere(), hbm()],
-        1 << 20,
-        [buffer(late_shape)] + sem,
-        {2: 0},
-        room=room,
-    )(ctl, plain_next, final)
 
 
 def solution(mesh):

time: 103 us -> 105 us (1.019)
  blocking collectives: 17.5 us -> 0 us
  waiting for transfers between devices: 16.1 us -> 30.8 us
  starting transfers between devices: 15.6 us -> 21.4 us
  Pallas kernels: 49.2 us -> 46.3 us
  local copies, waits for them, and re-layouts: 3.71 us -> 5.36 us
    all_to_all x1 -> x0, blocking collectives: 17.5 us -> none  [spread(): lax.all_to_all(fast, ('xb', 'yb'), split_axis=0, concat_axis=0, tiled=True)]
    all_to_all x2 -> x3, waiting for transfers between devices: 1.62 us -> 15.1 us  [spread(): lax.all_to_all(fast, ('xb', 'yb'), split_axis=0, concat_axis=0, tiled=True)]
    pallas_call x2 -> x1, Pallas kernels: 11.9 us -> 5.96 us  [body(): call(rates, shape, hbm(), [smem(), hbm(), hbm()], 16 << 20, scratch)]
    pallas_call x7 -> x4, Pallas kernels: 10.1 us -> 14.8 us  [the longest x1 5.99 us: body(): call(rates_and_leaving, (shape,) + tuple((f32(5, end - begin, TILE) for b...]
    ppermute x6 -> x5, starting transfers between devices: 4.65 us -> 8.12 us  [shifted(): return lax.ppermute(value, axis, pairs)]
    pallas_call x1, Pallas kernels: 4.14 us -> 1.5 us  [body(): call(repeat_first, shape, hbm(), [smem()] + [vmem()] * 3 + [anywhere()] *...]
    all_to_all x2 -> x3, starting transfers between devices: 11 us -> 13.3 us  [spread(): lax.all_to_all(fast, ('xb', 'yb'), split_axis=0, concat_axis=0, tiled=True)]
    pallas_call x1, Pallas kernels: 3.03 us -> 4.96 us  [body(): call(repeat_second, early_state, anywhere(), [smem()] + [vmem()] * 3 + [a...]
  transfers between devices with their start and end apart: 8 -> 8, of which waited for: 7 -> 5; matrix products, arithmetic and copies ran while one was open for 0% -> 0% of each run, Pallas kernels for 38% -> 38%
where the time goes in v10:
time: 105 us; the launch traced here: 104 us
  Pallas kernels  46.3 us (44%)
  waiting for transfers between devices  30.8 us (29%)
  starting transfers between devices  21.4 us (20%)
  local copies, waits for them, and re-layouts  5.36 us (5%)
    ppermute x5, waiting for transfers between devices, shifted(): return lax.ppermute(value, axis, pairs)  15.6 us
    pallas_call x3, Pallas kernels, body(): call(functools.partial(update, step), shapes, places, [smem()] + [hbm()]...  15.5 us
    all_to_all x3, waiting for transfers between devices, spread(): lax.all_to_all(fast, ('xb', 'yb'), split_axis=0, concat_axis=0, tiled=True)  15.1 us
    all_to_all x3, starting transfers between devices, spread(): lax.all_to_all(fast, ('xb', 'yb'), split_axis=0, concat_axis=0, tiled=True)  13.3 us
    ppermute x5, starting transfers between devices, shifted(): return lax.ppermute(value, axis, pairs)  8.12 us
    pallas_call x1, Pallas kernels, body(): call(rates_and_leaving, (shape,) + tuple((f32(5, end - begin, TILE) for b...  5.99 us
    pallas_call x1, Pallas kernels, body(): call(rates, shape, hbm(), [smem(), hbm(), hbm()], 16 << 20, scratch)  5.96 us
    pallas_call x1, Pallas kernels, body(): call(rates_after, shape, hbm(), [smem()] + [hbm()] * 3, 16 << 20, scratch)  5.96 us
  transfers between devices with their start and end apart: 8, of which 5 were waited for; matrix products, arithmetic and copies ran while one was open for 0% of the time, Pallas kernels for 38%

profile of v10, /device:TPU:0, one launch (start us, length us, event | category | flops | bytes accessed | tf_op | source)
XLA Modules:
  0.0 104.0 jit_solution(15112338708736196727)
XLA Ops:
  0.0 3.6 %shard_map.64 = (f32[256,256]{1,0:T(8,128)}, f32[8,256]{1,0:T(8,128)}, s32[24]{0:T(128)}, f32[5,160,256]{2,1,0:T(8,128)}) custom-call(f32[2,3,256,256]{3,2,1,0:T(8,128)} %state_first.1, f32[2,256,256]{2,1,0:T(8,128)} %bed_in.7, f32[2,256,256]{2,1,0:T(8,128)} %manning_in.9, s32[4,32]{1,0:T(4,128)} %bitcast.16, s32[3,32]{1,0:T(4,128)} %wet_in.1, s32[3,16]{1,0:T(4,128)} %moves_in.1), custom_call_target="tpu_custom_call" | custom-call | flops 4194304 | bytes 4194304 | tf_op jit(solution)/shard_map/pallas_call | solution.py:805
  3.6 3.0 %collective-permute-start = (f32[5,160,256]{2,1,0:T(8,128)}, f32[5,160,256]{2,1,0:T(8,128)S(1)}, u32[]{:S(2)}, u32[]{:S(2)}) collective-permute-start(f32[5,160,256]{2,1,0:T(8,128)} %get-tuple-element.30), channel_id=1, source_target_pairs={{0,2},{2,4},{4,6},{6,8},{8,10},{10,12},{12,14},{14,0},{1,3},{3,5},... | collective-permute-start | bytes 2457608 | tf_op jit(solution)/shard_map/ppermute | solution.py:38
  6.6 5.0 %all-to-all-start = ((f32[16,16,256]{2,1,0:T(8,128)}), f32[16,16,256]{2,1,0:T(8,128)S(1)}, u32[]{:S(2)}, u32[]{:S(2)}) async-start(f32[16,16,256]{2,1,0:T(8,128)} %bitcast.13), calls=%async_computation | async-start | bytes 524288 | tf_op jit(solution)/shard_map/all_to_all | solution.py:787
  11.6 6.0 %shard_map.65.rate_in = f32[2,3,256,256]{3,2,1,0:T(8,128)} custom-call(s32[24]{0:T(128)} %get-tuple-element.24.ctl, f32[2,3,256,256]{3,2,1,0:T(8,128)} %state_first.1, f32[2,256,256]{2,1,0:T(8,128)} %bed_in.7), custom_call_target="tpu_custom_call" | custom-call | flops 16777216 | bytes 4194304 | tf_op jit(solution)/shard_map/pallas_call | solution.py:835
  17.6 15.1 %all-to-all-done = f32[16,16,256]{2,1,0:T(8,128)S(1)} async-done(((f32[16,16,256]{2,1,0:T(8,128)}), f32[16,16,256]{2,1,0:T(8,128)S(1)}, u32[]{:S(2)}, u32[]{:S(2)}) %all-to-all-start) | async-done | bytes 262176 | tf_op jit(solution)/shard_map/all_to_all | solution.py:787
  32.7 0.7 copy-done.10
  33.4 5.0 %shard_map.66 = (f32[2,3,256,256]{3,2,1,0:T(8,128)}, f32[128,256]{1,0:T(8,128)}, f32[8,256]{1,0:T(8,128)}, f32[8,256]{1,0:T(8,128)}) custom-call(s32[24]{0:T(128)} %get-tuple-element.24.ctl, f32[256,256]{1,0:T(8,128)} %bitcast.7, f32[256,256]{1,0:T(8,128)} %bitcast.8, f32[8,256]{1,0:T(8,128)} %get-tuple-element.26.columns_in, ...), custom_call_target="tpu_custom_call" | custom-call | flops 8388608 | bytes 9437184 | tf_op jit(solution)/shard_map/pallas_call | solution.py:859
  38.4 3.5 %all-to-all-start.1 = ((f32[16,8,256]{2,1,0:T(8,128)}), f32[16,8,256]{2,1,0:T(8,128)S(1)}, u32[]{:S(2)}, u32[]{:S(2)}) async-start(f32[16,8,256]{2,1,0:T(8,128)} %bitcast.14), calls=%async_computation.1 | async-start | bytes 262144 | tf_op jit(solution)/shard_map/all_to_all | solution.py:787
  41.9 0.9 copy-done
  42.8 6.0 %shard_map.67 = (f32[2,3,256,256]{3,2,1,0:T(8,128)}, f32[5,80,256]{2,1,0:T(8,128)}, f32[5,80,256]{2,1,0:T(8,128)}) custom-call(s32[24]{0:T(128)} %get-tuple-element.24.ctl, f32[2,3,256,256]{3,2,1,0:T(8,128)} %get-tuple-element.29.state_in, f32[2,256,256]{2,1,0:T(8,128)} %bed_in.7, f32[2,3,256,256]{3,2,1,0:T(8,128)} %state_first.1, ...), custom_call_target="tpu_custom_call" | custom-call | flops 16777216 | bytes 4194304 | tf_op jit(solution)/shard_map/pallas_call | solution.py:839
  48.8 1.9 %collective-permute-start.1 = (f32[5,80,256]{2,1,0:T(8,128)}, f32[5,80,256]{2,1,0:T(8,128)S(1)}, u32[]{:S(2)}, u32[]{:S(2)}) collective-permute-start(f32[5,80,256]{2,1,0:T(8,128)} %get-tuple-element.35), channel_id=1, source_target_pairs={{0,2},{2,4},{4,6},{6,8},{8,10},{10,12},{12,14},{14,0},{1,3},{3,5},... | collective-permute-start | bytes 1228808 | tf_op jit(solution)/shard_map/ppermute | solution.py:38
  50.7 0.0 all-to-all-done.1
  50.7 0.7 copy-done.11
  51.4 5.0 %shard_map.68 = (f32[2,3,256,256]{3,2,1,0:T(8,128)}, f32[128,256]{1,0:T(8,128)}, f32[8,256]{1,0:T(8,128)}, f32[8,256]{1,0:T(8,128)}) custom-call(s32[24]{0:T(128)} %get-tuple-element.24.ctl, f32[128,256]{1,0:T(8,128)} %bitcast.11, f32[256,256]{1,0:T(8,128)} %bitcast.9, f32[8,256]{1,0:T(8,128)} %get-tuple-element.28.columns_in, ...), custom_call_target="tpu_custom_call" | custom-call | flops 8388608 | bytes 4194304 | tf_op jit(solution)/shard_map/pallas_call | solution.py:859
  56.4 4.8 %all-to-all-start.2 = ((f32[16,8,256]{2,1,0:T(8,128)}), f32[16,8,256]{2,1,0:T(8,128)S(1)}, u32[]{:S(2)}, u32[]{:S(2)}) async-start(f32[16,8,256]{2,1,0:T(8,128)} %bitcast.15), calls=%async_computation.2 | async-start | bytes 262144 | tf_op jit(solution)/shard_map/all_to_all | solution.py:787
  61.2 2.0 %collective-permute-start.3 = (f32[5,80,256]{2,1,0:T(8,128)S(1)}, f32[5,80,256]{2,1,0:T(8,128)S(1)}, u32[]{:S(2)}, u32[]{:S(2)}) collective-permute-start(f32[5,80,256]{2,1,0:T(8,128)S(1)} %copy-done.13), channel_id=1, source_target_pairs={{0,2},{2,4},{4,6},{6,8},{8,10},{10,12},{12,14},{14,0},{1,3},{3,5},... | collective-permute-start | bytes 1228808 | tf_op jit(solution)/shard_map/ppermute | solution.py:38
  63.1 0.3 collective-permute-done.1.order.low
  63.5 0.8 copy-done.2
  64.2 6.0 %shard_map.69.rate_in = f32[2,3,256,256]{3,2,1,0:T(8,128)} custom-call(s32[24]{0:T(128)} %get-tuple-element.24.ctl, f32[2,3,256,256]{3,2,1,0:T(8,128)} %get-tuple-element.34.state_in, f32[2,256,256]{2,1,0:T(8,128)} %bed_in.7, f32[5,80,256]{2,1,0:T(8,128)} %copy-done.2), custom_call_target="tpu_custom_call" | custom-call | flops 16777216 | bytes 4194304 | tf_op jit(solution)/shard_map/pallas_call | solution.py:849
  70.2 0.6 copy-done.12
  70.9 5.5 %shard_map.70 = (f32[3,256,256]{2,1,0:T(8,128)}, f32[3,112,256]{2,1,0:T(8,128)}, f32[3,112,256]{2,1,0:T(8,128)}, f32[8,256]{1,0:T(8,128)}) custom-call(s32[24]{0:T(128)} %get-tuple-element.24.ctl, f32[128,256]{1,0:T(8,128)} %bitcast.12, f32[256,256]{1,0:T(8,128)} %bitcast.10, f32[8,256]{1,0:T(8,128)} %get-tuple-element.33.columns_in, ...), custom_call_target="tpu_custom_call" | custom-call | flops 8388608 | bytes 4194304 | tf_op jit(solution)/shard_map/pallas_call | solution.py:859
  76.4 1.2 %collective-permute-start.2 = (f32[3,112,256]{2,1,0:T(8,128)}, f32[3,112,256]{2,1,0:T(8,128)S(1)}, u32[]{:S(2)}, u32[]{:S(2)}) collective-permute-start(f32[3,112,256]{2,1,0:T(8,128)} %get-tuple-element.36), channel_id=1, source_target_pairs={{0,2},{2,4},{4,6},{6,8},{8,10},{10,12},{12,14},{14,0},{1,3},{3,5},... | collective-permute-start | bytes 1032200 | tf_op jit(solution)/shard_map/ppermute | solution.py:38
  77.6 0.2 collective-permute-done.3.high
  77.9 0.7 copy-done.9
  78.6 5.0 %shard_map.71.order.early_in = f32[3,160,256]{2,1,0:T(8,128)S(1)} custom-call(s32[24]{0:T(128)S(1)} %copy-done.6, f32[8,256]{1,0:T(8,128)S(1)} %copy-done.7, f32[8,256]{1,0:T(8,128)S(1)} %copy-done.8, f32[8,256]{1,0:T(8,128)S(1)} %copy-done.9, f32[5,80,256]{2,1,0:T(8,128)S(1)} %copy-done.3, f32[5,80,256]{2,1,0:T(8,128)S(1)} %collective-permute-done.3.high), custom_call_target="tpu_custom_call" | custom-call | flops 8388608 | bytes 4194304 | tf_op jit(solution)/shard_map/pallas_call | solution.py:886
  83.6 5.3 %collective-permute-done.2.arrived.late_in = f32[3,112,256]{2,1,0:T(8,128)S(1)} collective-permute-done((f32[3,112,256]{2,1,0:T(8,128)}, f32[3,112,256]{2,1,0:T(8,128)S(1)}, u32[]{:S(2)}, u32[]{:S(2)}) %collective-permute-start.2) | collective-permute-done | bytes 344096 | tf_op jit(solution)/shard_map/ppermute | solution.py:38
  88.9 1.0 copy-done.5
  89.9 0.8 shard_map.72
  90.7 0.1 collective-permute-start.4
  90.8 1.5 %shard_map.73.before = f32[2,3,256,256]{3,2,1,0:T(8,128)} custom-call(s32[24]{0:T(128)S(1)} %copy-done.6, f32[8,256]{1,0:T(8,128)S(1)} %copy-done.7, f32[8,256]{1,0:T(8,128)S(1)} %copy-done.8, f32[8,256]{1,0:T(8,128)S(1)} %copy-done.9, f32[5,160,256]{2,1,0:T(8,128)S(1)} %copy-done.1, f32[3,112,256]{2,1,0:T(8,128)S(1)} %collective-permute-done.2.arrived.late_in, ...), custom_call_target="tpu_custom_call" | custom-call | flops 8388608 | bytes 4194304 | tf_op jit(solution)/shard_map/pallas_call | solution.py:905
  92.3 9.7 %collective-permute-done.4.late_in = f32[3,112,256]{2,1,0:T(8,128)S(1)} collective-permute-done((f32[3,112,256]{2,1,0:T(8,128)S(1)}, f32[3,112,256]{2,1,0:T(8,128)S(1)}, u32[]{:S(2)}, u32[]{:S(2)}) %collective-permute-start.4) | collective-permute-done | bytes 344096 | tf_op jit(solution)/shard_map/ppermute | solution.py:38
  102.0 2.0 %shard_map.74 = f32[2,3,256,256]{3,2,1,0:T(8,128)} custom-call(s32[24]{0:T(128)S(1)} %copy-done.6, f32[3,112,256]{2,1,0:T(8,128)S(1)} %collective-permute-done.4.late_in, f32[3,160,256]{2,1,0:T(8,128)S(1)} %shard_map.71.order.early_in, f32[2,3,256,256]{3,2,1,0:T(8,128)} %shard_map.73.before), custom_call_target="tpu_custom_call", output_to_operand_aliasing={{}: (3, {})} | custom-call | flops 1048576 | bytes 4194304 | tf_op jit(solution)/shard_map/pallas_call | solution.py:920
  (23 shorter events, 0.0 us)
Async XLA Ops:
  3.6 38.3 %collective-permute-start = (f32[5,160,256]{2,1,0:T(8,128)}, f32[5,160,256]{2,1,0:T(8,128)S(1)}, u32[]{:S(2)}, u32[]{:S(2)}) collective-permute-start(f32[5,160,256]{2,1,0:T(8,128)} %get-tuple-element.30), channel_id=1, source_target_pairs={{0,2},{2,4},{4,6},{6,8},{8,10},{10,12},{12,14},{14,0},{1,3},{3,5},... | collective-permute-start | bytes 2457608 | tf_op jit(solution)/shard_map/ppermute | solution.py:38
  6.6 26.1 %all-to-all-start = ((f32[16,16,256]{2,1,0:T(8,128)}), f32[16,16,256]{2,1,0:T(8,128)S(1)}, u32[]{:S(2)}, u32[]{:S(2)}) async-start(f32[16,16,256]{2,1,0:T(8,128)} %bitcast.13), calls=%async_computation | async-start | bytes 524288 | tf_op jit(solution)/shard_map/all_to_all | solution.py:787
  32.7 0.7 copy-start.10
  38.4 12.3 %all-to-all-start.1 = ((f32[16,8,256]{2,1,0:T(8,128)}), f32[16,8,256]{2,1,0:T(8,128)S(1)}, u32[]{:S(2)}, u32[]{:S(2)}) async-start(f32[16,8,256]{2,1,0:T(8,128)} %bitcast.14), calls=%async_computation.1 | async-start | bytes 262144 | tf_op jit(solution)/shard_map/all_to_all | solution.py:787
  41.9 0.9 copy-start
  48.8 14.6 %collective-permute-start.1 = (f32[5,80,256]{2,1,0:T(8,128)}, f32[5,80,256]{2,1,0:T(8,128)S(1)}, u32[]{:S(2)}, u32[]{:S(2)}) collective-permute-start(f32[5,80,256]{2,1,0:T(8,128)} %get-tuple-element.35), channel_id=1, source_target_pairs={{0,2},{2,4},{4,6},{6,8},{8,10},{10,12},{12,14},{14,0},{1,3},{3,5},... | collective-permute-start | bytes 1228808 | tf_op jit(solution)/shard_map/ppermute | solution.py:38
  50.7 0.7 copy-start.11
  51.4 9.8 %copy-start.13 = (f32[5,80,256]{2,1,0:T(8,128)S(1)}, f32[5,80,256]{2,1,0:T(8,128)}, u32[]{:S(2)}) copy-start(f32[5,80,256]{2,1,0:T(8,128)} %get-tuple-element.41) | copy-start | bytes 1228804
  56.4 13.8 %all-to-all-start.2 = ((f32[16,8,256]{2,1,0:T(8,128)}), f32[16,8,256]{2,1,0:T(8,128)S(1)}, u32[]{:S(2)}, u32[]{:S(2)}) async-start(f32[16,8,256]{2,1,0:T(8,128)} %bitcast.15), calls=%async_computation.2 | async-start | bytes 262144 | tf_op jit(solution)/shard_map/all_to_all | solution.py:787
  61.2 16.7 %collective-permute-start.3 = (f32[5,80,256]{2,1,0:T(8,128)S(1)}, f32[5,80,256]{2,1,0:T(8,128)S(1)}, u32[]{:S(2)}, u32[]{:S(2)}) collective-permute-start(f32[5,80,256]{2,1,0:T(8,128)S(1)} %copy-done.13), channel_id=1, source_target_pairs={{0,2},{2,4},{4,6},{6,8},{8,10},{10,12},{12,14},{14,0},{1,3},{3,5},... | collective-permute-start | bytes 1228808 | tf_op jit(solution)/shard_map/ppermute | solution.py:38
  63.5 0.8 copy-start.2
  70.2 0.6 copy-start.12
  70.9 7.0 %copy-start.3 = (f32[5,80,256]{2,1,0:T(8,128)S(1)}, f32[5,80,256]{2,1,0:T(8,128)}, u32[]{:S(2)}) copy-start(f32[5,80,256]{2,1,0:T(8,128)} %copy-done.2) | copy-start | bytes 1228804
  70.9 7.0 %copy-start.6 = (s32[24]{0:T(128)S(1)}, s32[24]{0:T(128)}, u32[]{:S(2)}) copy-start(s32[24]{0:T(128)} %get-tuple-element.24.ctl) | copy-start | bytes 292
  70.9 7.0 %copy-start.7 = (f32[8,256]{1,0:T(8,128)S(1)}, f32[8,256]{1,0:T(8,128)}, u32[]{:S(2)}) copy-start(f32[8,256]{1,0:T(8,128)} %get-tuple-element.38.delta0) | copy-start | bytes 24580
  70.9 7.0 %copy-start.8 = (f32[8,256]{1,0:T(8,128)S(1)}, f32[8,256]{1,0:T(8,128)}, u32[]{:S(2)}) copy-start(f32[8,256]{1,0:T(8,128)} %get-tuple-element.39.delta1) | copy-start | bytes 24580
  76.4 14.4 %copy-start.1 = (f32[5,160,256]{2,1,0:T(8,128)S(1)}, f32[5,160,256]{2,1,0:T(8,128)}, u32[]{:S(2)}) copy-start(f32[5,160,256]{2,1,0:T(8,128)} %copy-done) | copy-start | bytes 2457604
  76.4 14.4 %copy-start.4 = (f32[3,256,256]{2,1,0:T(8,128)S(1)}, f32[3,256,256]{2,1,0:T(8,128)}, u32[]{:S(2)}) copy-start(f32[3,256,256]{2,1,0:T(8,128)} %get-tuple-element.42.staying) | copy-start | bytes 2359300
  76.4 12.5 %collective-permute-start.2 = (f32[3,112,256]{2,1,0:T(8,128)}, f32[3,112,256]{2,1,0:T(8,128)S(1)}, u32[]{:S(2)}, u32[]{:S(2)}) collective-permute-start(f32[3,112,256]{2,1,0:T(8,128)} %get-tuple-element.36), channel_id=1, source_target_pairs={{0,2},{2,4},{4,6},{6,8},{8,10},{10,12},{12,14},{14,0},{1,3},{3,5},... | collective-permute-start | bytes 1032200 | tf_op jit(solution)/shard_map/ppermute | solution.py:38
  77.9 0.7 copy-start.9
  88.9 1.0 copy-start.5
  90.7 11.3 %collective-permute-start.4 = (f32[3,112,256]{2,1,0:T(8,128)S(1)}, f32[3,112,256]{2,1,0:T(8,128)S(1)}, u32[]{:S(2)}, u32[]{:S(2)}) collective-permute-start(f32[3,112,256]{2,1,0:T(8,128)S(1)} %shard_map.72), channel_id=1, source_target_pairs={{0,2},{2,4},{4,6},{6,8},{8,10},{10,12},{12,14},{14,0},{1,3},{3,5},... | collective-permute-start | bytes 1032200 | tf_op jit(solution)/shard_map/ppermute | solution.py:38

commit v11 on v10

--- a/solution.py
+++ b/solution.py
@@ -19,8 +19,8 @@
 SLOT_LOW, WALL_WEST, WALL_EAST, WALL_OUTER, WET, MOVE = 0, 1, 3, 5, 7, 13
 WET_FIRST, WET_SECOND = 16, 19
 CONTROLS = 24
-EARLY = 160
-PIECES = ((0, 80), (80, 160))
+EARLY = 192
+PIECES = ((0, 96), (96, 192))
 LATE = TILE - EARLY + 16
 CHUNKS = 8
 PARTS = 8
@@ -191,19 +191,7 @@
         ctl[WET_FIRST + step] = wet[step, tile_first]
         ctl[WET_SECOND + step] = wet[step, tile_second]
 
-    total = jnp.zeros((ROWS, TILE), jnp.float32)
-    for slot in range(2):
-        copies[3 + slot].wait()
-
-        def group(index, best, slot=slot):
-            rows = pl.ds(pl.multiple_of(index * ROWS, ROWS), ROWS)
-            along_x, along_y = cell(*(state[slot, field, rows, :] for field in range(3)))
-            return jnp.maximum(best, jnp.maximum(along_x[5], along_y[5]))
-
-        best = lax.fori_loop(0, TILE // ROWS, group, jnp.zeros((ROWS, TILE), jnp.float32))
-        total = jnp.maximum(total, jnp.where(wet[0, first + slot] > 0, best, 0.0))
-    copies[5].wait()
-    wait_all(rough)
+    wait_all(copies[3:] + rough)
     early = start_all(
         (
             (state.at[moving, :, 0:EARLY], leaving.at[0:3]),
@@ -213,6 +201,16 @@
         sems,
         7,
     )
+    total = jnp.zeros((ROWS, TILE), jnp.float32)
+    for slot in range(2):
+
+        def group(index, best, slot=slot):
+            rows = pl.ds(pl.multiple_of(index * ROWS, ROWS), ROWS)
+            along_x, along_y = cell(*(state[slot, field, rows, :] for field in range(3)))
+            return jnp.maximum(best, jnp.maximum(along_x[5], along_y[5]))
+
+        best = lax.fori_loop(0, TILE // ROWS, group, jnp.zeros((ROWS, TILE), jnp.float32))
+        total = jnp.maximum(total, jnp.where(wet[0, first + slot] > 0, best, 0.0))
     messages(ctl, state, bed, jnp.max(total, keepdims=True), out, columns)
     wait_all(early)
 
@@ -542,20 +540,21 @@
         tile[field, EARLY:, :] = late[field, 16:, :]
 
 
-def repeat_second(ctl, delta0, delta1, delta2, low, high, out, work, tile, sems):
+def repeat_second(ctl, delta0, delta1, delta2, low, high, late, out, late_out, work, tile, sems):
+    near = start_all(((late, late_out),), sems, 2)
     repeat_steps(ctl, WET_SECOND, (delta0, delta1, delta2), (low, high), work, tile, sems)
-    wait_all(start_all(((tile, out),), sems))
+    wait_all(start_all(((tile, out),), sems) + near)
 
 
 def repeat_first(
-    ctl, delta0, delta1, delta2, early, late_in, staying, out, work, other, tile, late, sems
+    ctl, delta0, delta1, delta2, early, late_in, state, out, work, other, tile, late, sems
 ):
     rest = out.at[1 - ctl[MOVE + 1]]
     again = ctl[MOVE] == ctl[MOVE + 1]
 
     @pl.when(again)
     def _():
-        wait_all(start_all(((staying, tile),), sems))
+        wait_all(start_all(((state.at[1 - ctl[MOVE]], tile),), sems))
 
     @pl.when(jnp.logical_not(again))
     def _():
@@ -648,12 +647,10 @@
 
 def update(step, ctl, got_in, ground_in, columns_in, state_in, manning_in, rate_in, *rest):
     more = step + 1 < STEPS
-    if more:
-        fresh_out, out_to, columns_to, delta_out = rest[:4]
-    else:
-        staying, late_first, late_second, delta_out = rest[:4]
+    fresh_out, first_out, second_out, delta_out = rest[:4]
     rest = rest[4:]
-    state, manning, rate, fresh, got, ground, columns, out, columns_out, delta_keep, sems = rest
+    state, manning, rate, fresh, got, ground, columns, first, second, delta_keep, sems = rest
+    out, columns_out = late_first, late_second = first, second
     small = start_all(
         ((got_in, got), (ground_in, ground), (columns_in, columns)), sems, 5 * PARTS
     )
@@ -731,20 +728,19 @@
         if more:
             best = jnp.where(flag(ctl, WET + 2 * step + 2 + slot), best, 0.0)
             total = jnp.maximum(total, best)
-        if more:
-            outgoing += start_all(
-                ((fresh.at[slot, :, part_rows], fresh_out.at[slot, :, part_rows]),),
-                sems,
-                3 * PARTS + index,
-            )
+        outgoing += start_all(
+            ((fresh.at[slot, :, part_rows], fresh_out.at[slot, :, part_rows]),),
+            sems,
+            3 * PARTS + index,
+        )
     if more:
         messages(ctl, fresh, None, jnp.max(total, keepdims=True), out, columns_out)
-        outgoing += start_all(((out, out_to), (columns_out, columns_to)), sems, 4 * PARTS)
+        outgoing += start_all(((out, first_out), (columns_out, second_out)), sems, 4 * PARTS)
     else:
-        first, second = fresh.at[ctl[MOVE]], fresh.at[1 - ctl[MOVE]]
-        outgoing += start_all(((second, staying),), sems, 4 * PARTS)
-        late_rows(first, late_first)
-        late_rows(second, late_second)
+        late_rows(fresh.at[ctl[MOVE]], late_first)
+        outgoing += start_all(((late_first, first_out),), sems, 4 * PARTS)
+        late_rows(fresh.at[1 - ctl[MOVE]], late_second)
+        outgoing += start_all(((late_second, second_out),), sems, 4 * PARTS + 1)
     wait_all(outgoing)
 
 
@@ -851,15 +847,13 @@
             )
         more = step + 1 < STEPS
         if more:
-            shapes = (shape, f32(8 * devices, TILE), f32(8, TILE), delta_shape)
-            places = (hbm(),) * 4
+            shapes = f32(8 * devices, TILE), f32(8, TILE)
         else:
-            shapes = (tile_shape, late_shape, late_shape, delta_shape)
-            places = (hbm(), vmem(), vmem(), hbm())
+            shapes = late_shape, late_shape
         outs = call(
             functools.partial(update, step),
-            shapes,
-            places,
+            (shape,) + shapes + (delta_shape,),
+            (hbm(),) * 4,
             [smem()] + [hbm()] * 6,
             8 << 20,
             [
@@ -870,28 +864,27 @@
                 pltpu.VMEM(got.shape, jnp.float32),
                 pltpu.VMEM(ground.shape, jnp.float32),
                 pltpu.VMEM((8, TILE), jnp.float32),
-                pltpu.VMEM((8 * devices, TILE), jnp.float32),
-                pltpu.VMEM((8, TILE), jnp.float32),
+                buffer(shapes[0]),
+                buffer(shapes[1]),
                 buffer(delta_shape),
                 pltpu.SemaphoreType.DMA((5 * PARTS + 4,)),
             ],
-            moved=9 if step == 0 else 4,
+            moved=16 if step == 0 else 4,
         )(ctl, got, ground, columns, state, manning, rate)
         deltas.append(outs[-1])
-        if more:
-            state, out, columns, _ = outs
-    staying, late_first, late_second, _ = outs
+        state, out, columns, _ = outs
+    late_first, late_second = out, columns
     room = 16 << 20
     late_arrived = shifted(late_first, "xb", 1)
-    second = call(
+    second, late_second = call(
         repeat_second,
-        early_state,
-        anywhere(),
-        [smem()] + [vmem()] * 3 + [anywhere()] * 2,
+        (early_state, late_shape),
+        (anywhere(), vmem()),
+        [smem()] + [vmem()] * 3 + [anywhere()] * 3,
         8 << 20,
-        [buffer(early_shape), buffer(early_state), pltpu.SemaphoreType.DMA((2,))],
+        [buffer(early_shape), buffer(early_state), pltpu.SemaphoreType.DMA((3,))],
         room=room,
-    )(ctl, *deltas, *early_second)
+    )(ctl, *deltas, *early_second, late_second)
     leaving = call(
         second_late,
         late_shape,
@@ -916,7 +909,7 @@
             pltpu.SemaphoreType.DMA((2,)),
         ],
         room=room,
-    )(ctl, *deltas, early_first, late_arrived, staying)
+    )(ctl, *deltas, early_first, late_arrived, state)
     return call(
         finish,
         shape,

time: 105 us -> 123 us (1.17)
  waiting for transfers between devices: 30.8 us -> 50 us
    all_to_all x3, waiting for transfers between devices: 15.1 us -> 40.7 us  [spread(): lax.all_to_all(fast, ('xb', 'yb'), split_axis=0, concat_axis=0, tiled=True)]
    ppermute x5, waiting for transfers between devices: 15.6 us -> 9.28 us  [shifted(): return lax.ppermute(value, axis, pairs)]
    ppermute x5, starting transfers between devices: 8.12 us -> 6.82 us  [shifted(): return lax.ppermute(value, axis, pairs)]
    unnamed x28 -> x26, local copies, waits for them, and re-layouts: 5.36 us -> 5.36 us
  transfers between devices with their start and end apart: 8 -> 8, of which waited for: 5 -> 5; matrix products, arithmetic and copies ran while one was open for 0% -> 0% of each run, Pallas kernels for 38% -> 28%
where the time goes in v11:
time: 123 us
  waiting for transfers between devices  50 us (41%)
  Pallas kernels  46.7 us (38%)
  starting transfers between devices  20.5 us (17%)
  local copies, waits for them, and re-layouts  5.36 us (4%)
    all_to_all x3, waiting for transfers between devices, spread(): lax.all_to_all(fast, ('xb', 'yb'), split_axis=0, concat_axis=0, tiled=True)  40.7 us
    pallas_call x3, Pallas kernels, body(): call(functools.partial(update, step), (shape,) + shapes + (delta_shape,),...  14.5 us
    all_to_all x3, starting transfers between devices, spread(): lax.all_to_all(fast, ('xb', 'yb'), split_axis=0, concat_axis=0, tiled=True)  13.6 us
    ppermute x5, waiting for transfers between devices, shifted(): return lax.ppermute(value, axis, pairs)  9.28 us
    ppermute x5, starting transfers between devices, shifted(): return lax.ppermute(value, axis, pairs)  6.82 us
    pallas_call x1, Pallas kernels, body(): call(rates_and_leaving, (shape,) + tuple((f32(5, end - begin, TILE) for b...  5.99 us
    pallas_call x1, Pallas kernels, body(): call(rates, shape, hbm(), [smem(), hbm(), hbm()], 16 << 20, scratch)  5.96 us
    pallas_call x1, Pallas kernels, body(): call(rates_after, shape, hbm(), [smem()] + [hbm()] * 3, 16 << 20, scratch)  5.96 us
  transfers between devices with their start and end apart: 8, of which 5 were waited for; matrix products, arithmetic and copies ran while one was open for 0% of the time, Pallas kernels for 28%

profile of v11, /device:TPU:0, one launch (start us, length us, event | category | flops | bytes accessed | tf_op | source)
XLA Modules:
  0.0 122.8 jit_solution(6854694728846543467)
XLA Ops:
  0.0 3.6 %shard_map.64 = (f32[256,256]{1,0:T(8,128)}, f32[8,256]{1,0:T(8,128)}, s32[24]{0:T(128)}, f32[5,192,256]{2,1,0:T(8,128)}) custom-call(f32[2,3,256,256]{3,2,1,0:T(8,128)} %state_first.1, f32[2,256,256]{2,1,0:T(8,128)} %bed_in.7, f32[2,256,256]{2,1,0:T(8,128)} %manning_in.9, s32[4,32]{1,0:T(4,128)} %bitcast.15, s32[3,32]{1,0:T(4,128)} %wet_in.1, s32[3,16]{1,0:T(4,128)} %moves_in.1), custom_call_target="tpu_custom_call" | custom-call | flops 4194304 | bytes 4194304 | tf_op jit(solution)/shard_map/pallas_call | solution.py:801
  3.6 3.0 %collective-permute-start = (f32[5,192,256]{2,1,0:T(8,128)}, f32[5,192,256]{2,1,0:T(8,128)S(1)}, u32[]{:S(2)}, u32[]{:S(2)}) collective-permute-start(f32[5,192,256]{2,1,0:T(8,128)} %get-tuple-element.32), channel_id=1, source_target_pairs={{0,2},{2,4},{4,6},{6,8},{8,10},{10,12},{12,14},{14,0},{1,3},{3,5},... | collective-permute-start | bytes 2949128 | tf_op jit(solution)/shard_map/ppermute | solution.py:38
  6.7 5.0 %all-to-all-start = ((f32[16,16,256]{2,1,0:T(8,128)}), f32[16,16,256]{2,1,0:T(8,128)S(1)}, u32[]{:S(2)}, u32[]{:S(2)}) async-start(f32[16,16,256]{2,1,0:T(8,128)} %bitcast.13), calls=%async_computation | async-start | bytes 524288 | tf_op jit(solution)/shard_map/all_to_all | solution.py:783
  11.6 6.0 %shard_map.65.rate_in = f32[2,3,256,256]{3,2,1,0:T(8,128)} custom-call(s32[24]{0:T(128)} %get-tuple-element.26.ctl, f32[2,3,256,256]{3,2,1,0:T(8,128)} %state_first.1, f32[2,256,256]{2,1,0:T(8,128)} %bed_in.7), custom_call_target="tpu_custom_call" | custom-call | flops 16777216 | bytes 4194304 | tf_op jit(solution)/shard_map/pallas_call | solution.py:831
  17.6 18.6 %all-to-all-done = f32[16,16,256]{2,1,0:T(8,128)S(1)} async-done(((f32[16,16,256]{2,1,0:T(8,128)}), f32[16,16,256]{2,1,0:T(8,128)S(1)}, u32[]{:S(2)}, u32[]{:S(2)}) %all-to-all-start) | async-done | bytes 262176 | tf_op jit(solution)/shard_map/all_to_all | solution.py:783
  36.3 0.7 copy-done.10
  37.0 5.0 %shard_map.66 = (f32[2,3,256,256]{3,2,1,0:T(8,128)}, f32[128,256]{1,0:T(8,128)}, f32[8,256]{1,0:T(8,128)}, f32[8,256]{1,0:T(8,128)}) custom-call(s32[24]{0:T(128)} %get-tuple-element.26.ctl, f32[256,256]{1,0:T(8,128)} %bitcast.7, f32[256,256]{1,0:T(8,128)} %bitcast.8, f32[8,256]{1,0:T(8,128)} %get-tuple-element.28.columns_in, ...), custom_call_target="tpu_custom_call" | custom-call | flops 8388608 | bytes 16777216 | tf_op jit(solution)/shard_map/pallas_call | solution.py:853
  41.9 0.0 collective-permute-done.arrived.early
  42.0 0.9 copy-done
  42.9 6.0 %shard_map.67 = (f32[2,3,256,256]{3,2,1,0:T(8,128)}, f32[5,96,256]{2,1,0:T(8,128)}, f32[5,96,256]{2,1,0:T(8,128)}) custom-call(s32[24]{0:T(128)} %get-tuple-element.26.ctl, f32[2,3,256,256]{3,2,1,0:T(8,128)} %get-tuple-element.31.state_in, f32[2,256,256]{2,1,0:T(8,128)} %bed_in.7, f32[2,3,256,256]{3,2,1,0:T(8,128)} %state_first.1, ...), custom_call_target="tpu_custom_call" | custom-call | flops 16777216 | bytes 4194304 | tf_op jit(solution)/shard_map/pallas_call | solution.py:835
  48.9 1.0 collective-permute-start.1
  49.9 5.1 %all-to-all-start.1 = ((f32[16,8,256]{2,1,0:T(8,128)}), f32[16,8,256]{2,1,0:T(8,128)S(1)}, u32[]{:S(2)}, u32[]{:S(2)}) async-start(f32[16,8,256]{2,1,0:T(8,128)} %bitcast.3), calls=%async_computation.1 | async-start | bytes 262144 | tf_op jit(solution)/shard_map/all_to_all | solution.py:783
  55.1 1.9 %collective-permute-start.3 = (f32[5,96,256]{2,1,0:T(8,128)}, f32[5,96,256]{2,1,0:T(8,128)S(1)}, u32[]{:S(2)}, u32[]{:S(2)}) collective-permute-start(f32[5,96,256]{2,1,0:T(8,128)} %get-tuple-element.42), channel_id=1, source_target_pairs={{0,2},{2,4},{4,6},{6,8},{8,10},{10,12},{12,14},{14,0},{1,3},{3,5},... | collective-permute-start | bytes 1474568 | tf_op jit(solution)/shard_map/ppermute | solution.py:38
  57.0 21.0 %all-to-all-done.1 = f32[16,8,256]{2,1,0:T(8,128)S(1)} async-done(((f32[16,8,256]{2,1,0:T(8,128)}), f32[16,8,256]{2,1,0:T(8,128)S(1)}, u32[]{:S(2)}, u32[]{:S(2)}) %all-to-all-start.1) | async-done | bytes 131104 | tf_op jit(solution)/shard_map/all_to_all | solution.py:783
  78.0 0.6 copy-done.11
  78.6 4.8 %shard_map.68 = (f32[2,3,256,256]{3,2,1,0:T(8,128)}, f32[128,256]{1,0:T(8,128)}, f32[8,256]{1,0:T(8,128)}, f32[8,256]{1,0:T(8,128)}) custom-call(s32[24]{0:T(128)} %get-tuple-element.26.ctl, f32[128,256]{1,0:T(8,128)} %bitcast.11, f32[256,256]{1,0:T(8,128)} %bitcast.9, f32[8,256]{1,0:T(8,128)} %get-tuple-element.30.columns_in, ...), custom_call_target="tpu_custom_call" | custom-call | flops 8388608 | bytes 4194304 | tf_op jit(solution)/shard_map/pallas_call | solution.py:853
  83.5 3.5 %all-to-all-start.2 = ((f32[16,8,256]{2,1,0:T(8,128)}), f32[16,8,256]{2,1,0:T(8,128)S(1)}, u32[]{:S(2)}, u32[]{:S(2)}) async-start(f32[16,8,256]{2,1,0:T(8,128)} %bitcast.14), calls=%async_computation.2 | async-start | bytes 262144 | tf_op jit(solution)/shard_map/all_to_all | solution.py:783
  87.0 0.8 copy-done.2
  87.8 6.0 %shard_map.69.rate_in = f32[2,3,256,256]{3,2,1,0:T(8,128)} custom-call(s32[24]{0:T(128)} %get-tuple-element.26.ctl, f32[2,3,256,256]{3,2,1,0:T(8,128)} %get-tuple-element.36.state_in, f32[2,256,256]{2,1,0:T(8,128)} %bed_in.7, f32[5,96,256]{2,1,0:T(8,128)} %copy-done.2), custom_call_target="tpu_custom_call" | custom-call | flops 16777216 | bytes 4194304 | tf_op jit(solution)/shard_map/pallas_call | solution.py:845
  93.7 1.1 all-to-all-done.2
  94.9 0.7 copy-done.12
  95.5 4.7 %shard_map.70 = (f32[2,3,256,256]{3,2,1,0:T(8,128)}, f32[3,80,256]{2,1,0:T(8,128)}, f32[3,80,256]{2,1,0:T(8,128)}, f32[8,256]{1,0:T(8,128)}) custom-call(s32[24]{0:T(128)} %get-tuple-element.26.ctl, f32[128,256]{1,0:T(8,128)} %bitcast.12, f32[256,256]{1,0:T(8,128)} %bitcast.10, f32[8,256]{1,0:T(8,128)} %get-tuple-element.35.columns_in, ...), custom_call_target="tpu_custom_call" | custom-call | flops 8388608 | bytes 4194304 | tf_op jit(solution)/shard_map/pallas_call | solution.py:853
  100.2 0.8 collective-permute-start.2
  101.1 0.9 copy-done.5
  102.0 0.7 copy-done.9
  102.7 5.9 %shard_map.71 = (f32[3,192,256]{2,1,0:T(8,128)S(1)}, f32[3,80,256]{2,1,0:T(8,128)S(1)}) custom-call(s32[24]{0:T(128)S(1)} %copy-done.6, f32[8,256]{1,0:T(8,128)S(1)} %copy-done.7, f32[8,256]{1,0:T(8,128)S(1)} %copy-done.8, f32[8,256]{1,0:T(8,128)S(1)} %copy-done.9, f32[5,96,256]{2,1,0:T(8,128)S(1)} %copy-done.3, ...), custom_call_target="tpu_custom_call" | custom-call | flops 8388608 | bytes 4194304 | tf_op jit(solution)/shard_map/pallas_call | solution.py:879
  108.7 1.8 %collective-permute-done.2.arrived.late_in = f32[3,80,256]{2,1,0:T(8,128)S(1)} collective-permute-done((f32[3,80,256]{2,1,0:T(8,128)}, f32[3,80,256]{2,1,0:T(8,128)S(1)}, u32[]{:S(2)}, u32[]{:S(2)}) %collective-permute-start.2) | collective-permute-done | bytes 245792 | tf_op jit(solution)/shard_map/ppermute | solution.py:38
  110.5 1.2 shard_map.72
  111.7 0.1 collective-permute-start.4
  111.7 1.5 %shard_map.73.before = f32[2,3,256,256]{3,2,1,0:T(8,128)} custom-call(s32[24]{0:T(128)S(1)} %copy-done.6, f32[8,256]{1,0:T(8,128)S(1)} %copy-done.7, f32[8,256]{1,0:T(8,128)S(1)} %copy-done.8, f32[8,256]{1,0:T(8,128)S(1)} %copy-done.9, f32[5,192,256]{2,1,0:T(8,128)S(1)} %copy-done.1, f32[3,80,256]{2,1,0:T(8,128)S(1)} %collective-permute-done.2.arrived.late_in, ...), custom_call_target="tpu_custom_call" | custom-call | flops 8388608 | bytes 4194304 | tf_op jit(solution)/shard_map/pallas_call | solution.py:898
  113.3 7.5 %collective-permute-done.4.late_in = f32[3,80,256]{2,1,0:T(8,128)S(1)} collective-permute-done((f32[3,80,256]{2,1,0:T(8,128)S(1)}, f32[3,80,256]{2,1,0:T(8,128)S(1)}, u32[]{:S(2)}, u32[]{:S(2)}) %collective-permute-start.4) | collective-permute-done | bytes 245792 | tf_op jit(solution)/shard_map/ppermute | solution.py:38
  120.7 2.0 %shard_map.74 = f32[2,3,256,256]{3,2,1,0:T(8,128)} custom-call(s32[24]{0:T(128)S(1)} %copy-done.6, f32[3,80,256]{2,1,0:T(8,128)S(1)} %collective-permute-done.4.late_in, f32[3,192,256]{2,1,0:T(8,128)S(1)} %get-tuple-element.45.order.early_in, f32[2,3,256,256]{3,2,1,0:T(8,128)} %shard_map.73.before), custom_call_target="tpu_custom_call", output_to_operand_aliasing={{}: (3, {})} | custom-call | flops 1048576 | bytes 4194304 | tf_op jit(solution)/shard_map/pallas_call | solution.py:913
  (21 shorter events, 0.0 us)
Async XLA Ops:
  3.6 38.3 %collective-permute-start = (f32[5,192,256]{2,1,0:T(8,128)}, f32[5,192,256]{2,1,0:T(8,128)S(1)}, u32[]{:S(2)}, u32[]{:S(2)}) collective-permute-start(f32[5,192,256]{2,1,0:T(8,128)} %get-tuple-element.32), channel_id=1, source_target_pairs={{0,2},{2,4},{4,6},{6,8},{8,10},{10,12},{12,14},{14,0},{1,3},{3,5},... | collective-permute-start | bytes 2949128 | tf_op jit(solution)/shard_map/ppermute | solution.py:38
  6.7 29.6 %all-to-all-start = ((f32[16,16,256]{2,1,0:T(8,128)}), f32[16,16,256]{2,1,0:T(8,128)S(1)}, u32[]{:S(2)}, u32[]{:S(2)}) async-start(f32[16,16,256]{2,1,0:T(8,128)} %bitcast.13), calls=%async_computation | async-start | bytes 524288 | tf_op jit(solution)/shard_map/all_to_all | solution.py:783
  36.3 0.7 copy-start.10
  42.0 0.9 copy-start
  48.9 38.1 %collective-permute-start.1 = (f32[5,96,256]{2,1,0:T(8,128)}, f32[5,96,256]{2,1,0:T(8,128)S(1)}, u32[]{:S(2)}, u32[]{:S(2)}) collective-permute-start(f32[5,96,256]{2,1,0:T(8,128)} %get-tuple-element.37), channel_id=1, source_target_pairs={{0,2},{2,4},{4,6},{6,8},{8,10},{10,12},{12,14},{14,0},{1,3},{3,5},... | collective-permute-start | bytes 1474568 | tf_op jit(solution)/shard_map/ppermute | solution.py:38
  49.9 28.0 %all-to-all-start.1 = ((f32[16,8,256]{2,1,0:T(8,128)}), f32[16,8,256]{2,1,0:T(8,128)S(1)}, u32[]{:S(2)}, u32[]{:S(2)}) async-start(f32[16,8,256]{2,1,0:T(8,128)} %bitcast.3), calls=%async_computation.1 | async-start | bytes 262144 | tf_op jit(solution)/shard_map/all_to_all | solution.py:783
  55.1 46.0 %collective-permute-start.3 = (f32[5,96,256]{2,1,0:T(8,128)}, f32[5,96,256]{2,1,0:T(8,128)S(1)}, u32[]{:S(2)}, u32[]{:S(2)}) collective-permute-start(f32[5,96,256]{2,1,0:T(8,128)} %get-tuple-element.42), channel_id=1, source_target_pairs={{0,2},{2,4},{4,6},{6,8},{8,10},{10,12},{12,14},{14,0},{1,3},{3,5},... | collective-permute-start | bytes 1474568 | tf_op jit(solution)/shard_map/ppermute | solution.py:38
  78.0 0.6 copy-start.11
  83.5 11.4 %all-to-all-start.2 = ((f32[16,8,256]{2,1,0:T(8,128)}), f32[16,8,256]{2,1,0:T(8,128)S(1)}, u32[]{:S(2)}, u32[]{:S(2)}) async-start(f32[16,8,256]{2,1,0:T(8,128)} %bitcast.14), calls=%async_computation.2 | async-start | bytes 262144 | tf_op jit(solution)/shard_map/all_to_all | solution.py:783
  87.0 0.8 copy-start.2
  94.9 0.7 copy-start.12
  95.5 5.5 %copy-start.3 = (f32[5,96,256]{2,1,0:T(8,128)S(1)}, f32[5,96,256]{2,1,0:T(8,128)}, u32[]{:S(2)}) copy-start(f32[5,96,256]{2,1,0:T(8,128)} %copy-done.2) | copy-start | bytes 1474564
  95.5 5.5 %copy-start.6 = (s32[24]{0:T(128)S(1)}, s32[24]{0:T(128)}, u32[]{:S(2)}) copy-start(s32[24]{0:T(128)} %get-tuple-element.26.ctl) | copy-start | bytes 292
  95.5 5.5 %copy-start.7 = (f32[8,256]{1,0:T(8,128)S(1)}, f32[8,256]{1,0:T(8,128)}, u32[]{:S(2)}) copy-start(f32[8,256]{1,0:T(8,128)} %get-tuple-element.39.delta0) | copy-start | bytes 24580
  95.5 5.5 %copy-start.8 = (f32[8,256]{1,0:T(8,128)S(1)}, f32[8,256]{1,0:T(8,128)}, u32[]{:S(2)}) copy-start(f32[8,256]{1,0:T(8,128)} %get-tuple-element.40.delta1) | copy-start | bytes 24580
  100.2 11.5 %copy-start.1 = (f32[5,192,256]{2,1,0:T(8,128)S(1)}, f32[5,192,256]{2,1,0:T(8,128)}, u32[]{:S(2)}) copy-start(f32[5,192,256]{2,1,0:T(8,128)} %copy-done) | copy-start | bytes 2949124
  100.2 11.5 %copy-start.4 = (f32[2,3,256,256]{3,2,1,0:T(8,128)S(1)}, f32[2,3,256,256]{3,2,1,0:T(8,128)}, u32[]{:S(2)}) copy-start(f32[2,3,256,256]{3,2,1,0:T(8,128)} %get-tuple-element.46.state) | copy-start | bytes 4718596
  100.2 10.2 %collective-permute-start.2 = (f32[3,80,256]{2,1,0:T(8,128)}, f32[3,80,256]{2,1,0:T(8,128)S(1)}, u32[]{:S(2)}, u32[]{:S(2)}) collective-permute-start(f32[3,80,256]{2,1,0:T(8,128)} %get-tuple-element.38), channel_id=1, source_target_pairs={{0,2},{2,4},{4,6},{6,8},{8,10},{10,12},{12,14},{14,0},{1,3},{3,5},... | collective-permute-start | bytes 737288 | tf_op jit(solution)/shard_map/ppermute | solution.py:38
  101.1 0.9 copy-start.5
  102.0 0.7 copy-start.9
  111.7 9.1 %collective-permute-start.4 = (f32[3,80,256]{2,1,0:T(8,128)S(1)}, f32[3,80,256]{2,1,0:T(8,128)S(1)}, u32[]{:S(2)}, u32[]{:S(2)}) collective-permute-start(f32[3,80,256]{2,1,0:T(8,128)S(1)} %shard_map.72), channel_id=1, source_target_pairs={{0,2},{2,4},{4,6},{6,8},{8,10},{10,12},{12,14},{14,0},{1,3},{3,5},... | collective-permute-start | bytes 737288 | tf_op jit(solution)/shard_map/ppermute | solution.py:38

commit v12 on v11

--- a/solution.py
+++ b/solution.py
@@ -19,8 +19,8 @@
 SLOT_LOW, WALL_WEST, WALL_EAST, WALL_OUTER, WET, MOVE = 0, 1, 3, 5, 7, 13
 WET_FIRST, WET_SECOND = 16, 19
 CONTROLS = 24
-EARLY = 192
-PIECES = ((0, 96), (96, 192))
+EARLY = 160
+PIECES = ((0, 80), (80, 160))
 LATE = TILE - EARLY + 16
 CHUNKS = 8
 PARTS = 8
@@ -146,7 +146,7 @@
 
 def opening(
     state_in, bed_in, manning_in, neighbours_in, wet_in, moves_in,
-    out, columns, ctl, leaving,
+    out, columns, ctl, leaving_low, leaving_high,
     state, bed, manning, neighbours, wet, moves, sems,
 ):
     copies = start_all(
@@ -192,15 +192,17 @@
         ctl[WET_SECOND + step] = wet[step, tile_second]
 
     wait_all(copies[3:] + rough)
-    early = start_all(
-        (
-            (state.at[moving, :, 0:EARLY], leaving.at[0:3]),
-            (bed.at[moving, 0:EARLY], leaving.at[3]),
-            (manning, leaving.at[4]),
-        ),
-        sems,
-        7,
-    )
+    early = []
+    for (begin, end), leaving in zip(PIECES, (leaving_low, leaving_high)):
+        early += start_all(
+            (
+                (state.at[moving, :, begin:end], leaving.at[0:3]),
+                (bed.at[moving, begin:end], leaving.at[3]),
+                (manning.at[begin:end], leaving.at[4]),
+            ),
+            sems,
+            7 + len(early),
+        )
     total = jnp.zeros((ROWS, TILE), jnp.float32)
     for slot in range(2):
 
@@ -232,7 +234,8 @@
 
         @pl.when(self.again)
         def _():
-            pltpu.make_async_copy(arrived, buffer, sem).start()
+            for (begin, end), piece in zip(PIECES, arrived):
+                pltpu.make_async_copy(piece, buffer.at[:, begin:end], sem).start()
 
         @pl.when(jnp.logical_not(self.again))
         def _():
@@ -242,7 +245,8 @@
 
     def middle(self):
         _, _, _, arrived, buffer, sems = self.refs
-        pltpu.make_async_copy(arrived, buffer, sems.at[0]).wait()
+        for (begin, end), piece in zip(PIECES, arrived):
+            pltpu.make_async_copy(piece, buffer.at[:, begin:end], sems.at[0]).wait()
         for copy in self.outgoing:
             copy.start()
 
@@ -251,9 +255,11 @@
 
 
 def rates_and_leaving(
-    ctl, state_in, bed_in, state_first, manning_in, arrived, rate_out, leaving_low, leaving_high,
+    ctl, state_in, bed_in, state_first, manning_in, arrived_low, arrived_high,
+    rate_out, leaving_low, leaving_high,
     state, bed, rate, sems, buffer, moving,
 ):
+    arrived = arrived_low, arrived_high
     passing = Passing(
         ctl, state_first, bed_in, manning_in, arrived, (leaving_low, leaving_high), buffer, moving
     )
@@ -547,7 +553,7 @@
 
 
 def repeat_first(
-    ctl, delta0, delta1, delta2, early, late_in, state, out, work, other, tile, late, sems
+    ctl, delta0, delta1, delta2, low, high, late_in, state, out, work, other, tile, late, sems
 ):
     rest = out.at[1 - ctl[MOVE + 1]]
     again = ctl[MOVE] == ctl[MOVE + 1]
@@ -558,8 +564,8 @@
 
     @pl.when(jnp.logical_not(again))
     def _():
-        copies = start_all(((late_in, late),), sems, 1)
-        repeat_steps(ctl, WET_FIRST, (delta0, delta1, delta2), (early,), work, other, sems)
+        copies = start_all(((late_in, late),), sems, 2)
+        repeat_steps(ctl, WET_FIRST, (delta0, delta1, delta2), (low, high), work, other, sems)
         wait_all(copies)
         merge(late, other, tile)
 
@@ -798,15 +804,16 @@
     def buffer(like):
         return pltpu.VMEM(like.shape, jnp.float32)
 
-    out, columns, ctl, leaving = call(
+    piece_shapes = tuple(f32(5, end - begin, TILE) for begin, end in PIECES)
+    out, columns, ctl, *leaving = call(
         opening,
         (
             f32(16 * devices, TILE),
             f32(8, TILE),
             jax.ShapeDtypeStruct((CONTROLS,), jnp.int32),
-            early_shape,
-        ),
-        (vmem(), vmem(), smem(), hbm()),
+        )
+        + piece_shapes,
+        (vmem(), vmem(), smem(), hbm(), hbm()),
         [hbm()] * 6,
         4 << 20,
         [
@@ -816,7 +823,7 @@
             pltpu.SMEM(neighbours.shape[::-1], jnp.int32),
             pltpu.SMEM(wet.shape, jnp.int32),
             pltpu.SMEM(moves.shape, jnp.int32),
-            pltpu.SemaphoreType.DMA((10,)),
+            pltpu.SemaphoreType.DMA((13,)),
         ],
     )(state, bed, manning, neighbours.T, wet, moves)
     state_first = state
@@ -827,19 +834,19 @@
         ground = got if step == 0 else ground
         scratch = [whole, part, whole, pltpu.SemaphoreType.DMA((3 * CHUNKS,))]
         if step == 0:
-            early_first = shifted(leaving, "xb", 1)
+            early_first = [shifted(piece, "xb", 1) for piece in leaving]
             rate = call(rates, shape, hbm(), [smem(), hbm(), hbm()], 16 << 20, scratch)(
                 ctl, state, bed
             )
         elif step == 1:
             rate, *leaving = call(
                 rates_and_leaving,
-                (shape,) + tuple(f32(5, end - begin, TILE) for begin, end in PIECES),
+                (shape,) + piece_shapes,
                 (hbm(),) * 3,
-                [smem()] + [hbm()] * 5,
+                [smem()] + [hbm()] * 6,
                 16 << 20,
                 scratch + [buffer(early_shape), pltpu.SemaphoreType.DMA((3,))],
-            )(ctl, state, bed, state_first, manning, early_first)
+            )(ctl, state, bed, state_first, manning, *early_first)
             early_second = [shifted(piece, "xb", 1) for piece in leaving]
         else:
             rate = call(rates_after, shape, hbm(), [smem()] + [hbm()] * 3, 16 << 20, scratch)(
@@ -869,7 +876,7 @@
                 buffer(delta_shape),
                 pltpu.SemaphoreType.DMA((5 * PARTS + 4,)),
             ],
-            moved=16 if step == 0 else 4,
+            moved=4,
         )(ctl, got, ground, columns, state, manning, rate)
         deltas.append(outs[-1])
         state, out, columns, _ = outs
@@ -899,17 +906,17 @@
         repeat_first,
         shape,
         hbm(),
-        [smem()] + [vmem()] * 3 + [anywhere()] * 3,
+        [smem()] + [vmem()] * 3 + [anywhere()] * 4,
         8 << 20,
         [
             buffer(early_shape),
             buffer(early_state),
             buffer(tile_shape),
             buffer(late_shape),
-            pltpu.SemaphoreType.DMA((2,)),
+            pltpu.SemaphoreType.DMA((3,)),
         ],
         room=room,
-    )(ctl, *deltas, early_first, late_arrived, state)
+    )(ctl, *deltas, *early_first, late_arrived, state)
     return call(
         finish,
         shape,

time: 123 us -> 108 us (0.88)
  waiting for transfers between devices: 50 us -> 11.7 us
  starting transfers between devices: 20.5 us -> 39.8 us
  Pallas kernels: 46.7 us -> 49.9 us
    all_to_all x3, waiting for transfers between devices: 40.7 us -> 1.16 us  [spread(): lax.all_to_all(fast, ('xb', 'yb'), split_axis=0, concat_axis=0, tiled=True)]
    all_to_all x3, starting transfers between devices: 13.6 us -> 31.2 us  [spread(): lax.all_to_all(fast, ('xb', 'yb'), split_axis=0, concat_axis=0, tiled=True)]
    pallas_call x1, Pallas kernels: 1.51 us -> 5.82 us  [body(): call(repeat_first, shape, hbm(), [smem()] + [vmem()] * 3 + [anywhere()] *...]
    ppermute x5 -> x6, starting transfers between devices: 6.82 us -> 8.56 us  [shifted(): return lax.ppermute(value, axis, pairs)]
    ppermute x5 -> x6, waiting for transfers between devices: 9.28 us -> 10.6 us  [shifted(): return lax.ppermute(value, axis, pairs)]
    unnamed x26 -> x32, local copies, waits for them, and re-layouts: 5.36 us -> 5.34 us
  transfers between devices with their start and end apart: 8 -> 9, of which waited for: 5 -> 5; matrix products, arithmetic and copies ran while one was open for 0% -> 0% of each run, Pallas kernels for 28% -> 41%
where the time goes in v12:
time: 108 us; the launch traced here: 107 us
  Pallas kernels  49.9 us (46%)
  starting transfers between devices  39.8 us (37%)
  waiting for transfers between devices  11.7 us (11%)
  local copies, waits for them, and re-layouts  5.34 us (5%)
    all_to_all x3, starting transfers between devices, spread(): lax.all_to_all(fast, ('xb', 'yb'), split_axis=0, concat_axis=0, tiled=True)  31.2 us
    pallas_call x3, Pallas kernels, body(): call(functools.partial(update, step), (shape,) + shapes + (delta_shape,),...  14.7 us
    ppermute x6, waiting for transfers between devices, shifted(): return lax.ppermute(value, axis, pairs)  10.6 us
    ppermute x6, starting transfers between devices, shifted(): return lax.ppermute(value, axis, pairs)  8.56 us
    pallas_call x1, Pallas kernels, body(): call(rates_and_leaving, (shape,) + piece_shapes, (hbm(),) * 3, [smem()] +...  5.99 us
    pallas_call x1, Pallas kernels, body(): call(rates, shape, hbm(), [smem(), hbm(), hbm()], 16 << 20, scratch)  5.96 us
    pallas_call x1, Pallas kernels, body(): call(rates_after, shape, hbm(), [smem()] + [hbm()] * 3, 16 << 20, scratch)  5.96 us
    pallas_call x1, Pallas kernels, body(): call(repeat_first, shape, hbm(), [smem()] + [vmem()] * 3 + [anywhere()] *...  5.82 us
  transfers between devices with their start and end apart: 9, of which 5 were waited for; matrix products, arithmetic and copies ran while one was open for 0% of the time, Pallas kernels for 41%

profile of v12, /device:TPU:0, one launch (start us, length us, event | category | flops | bytes accessed | tf_op | source)
XLA Modules:
  0.0 107.0 jit_solution(11207710924476683605)
XLA Ops:
  0.0 3.6 %shard_map.64 = (f32[256,256]{1,0:T(8,128)}, f32[8,256]{1,0:T(8,128)}, s32[24]{0:T(128)}, f32[5,80,256]{2,1,0:T(8,128)}, f32[5,80,256]{2,1,0:T(8,128)}) custom-call(f32[2,3,256,256]{3,2,1,0:T(8,128)} %state_first.1, f32[2,256,256]{2,1,0:T(8,128)} %bed_in.7, f32[2,256,256]{2,1,0:T(8,128)} %manning_in.9, s32[4,32]{1,0:T(4,128)} %bitcast.16, s32[3,32]{1,0:T(4,128)} %wet_in.1, ...), custom_call_target="tpu_custom_call" | custom-call | flops 4194304 | bytes 4194304 | tf_op jit(solution)/shard_map/pallas_call | solution.py:808
  3.6 7.4 %all-to-all-start = ((f32[16,16,256]{2,1,0:T(8,128)}), f32[16,16,256]{2,1,0:T(8,128)S(1)}, u32[]{:S(2)}, u32[]{:S(2)}) async-start(f32[16,16,256]{2,1,0:T(8,128)} %bitcast.13), calls=%async_computation | async-start | bytes 524288 | tf_op jit(solution)/shard_map/all_to_all | solution.py:789
  11.0 1.9 %collective-permute-start = (f32[5,80,256]{2,1,0:T(8,128)}, f32[5,80,256]{2,1,0:T(8,128)S(1)}, u32[]{:S(2)}, u32[]{:S(2)}) collective-permute-start(f32[5,80,256]{2,1,0:T(8,128)} %get-tuple-element.33), channel_id=1, source_target_pairs={{0,2},{2,4},{4,6},{6,8},{8,10},{10,12},{12,14},{14,0},{1,3},{3,5},... | collective-permute-start | bytes 1228808 | tf_op jit(solution)/shard_map/ppermute | solution.py:38
  12.9 1.5 %collective-permute-start.1 = (f32[5,80,256]{2,1,0:T(8,128)}, f32[5,80,256]{2,1,0:T(8,128)S(1)}, u32[]{:S(2)}, u32[]{:S(2)}) collective-permute-start(f32[5,80,256]{2,1,0:T(8,128)} %get-tuple-element.34), channel_id=1, source_target_pairs={{0,2},{2,4},{4,6},{6,8},{8,10},{10,12},{12,14},{14,0},{1,3},{3,5},... | collective-permute-start | bytes 1228808 | tf_op jit(solution)/shard_map/ppermute | solution.py:38
  14.4 6.0 %shard_map.65.rate_in = f32[2,3,256,256]{3,2,1,0:T(8,128)} custom-call(s32[24]{0:T(128)} %get-tuple-element.27.ctl, f32[2,3,256,256]{3,2,1,0:T(8,128)} %state_first.1, f32[2,256,256]{2,1,0:T(8,128)} %bed_in.7), custom_call_target="tpu_custom_call" | custom-call | flops 16777216 | bytes 4194304 | tf_op jit(solution)/shard_map/pallas_call | solution.py:838
  20.4 1.2 %all-to-all-done = f32[16,16,256]{2,1,0:T(8,128)S(1)} async-done(((f32[16,16,256]{2,1,0:T(8,128)}), f32[16,16,256]{2,1,0:T(8,128)S(1)}, u32[]{:S(2)}, u32[]{:S(2)}) %all-to-all-start) | async-done | bytes 262176 | tf_op jit(solution)/shard_map/all_to_all | solution.py:789
  21.5 0.7 copy-done.12
  22.2 5.0 %shard_map.66 = (f32[2,3,256,256]{3,2,1,0:T(8,128)}, f32[128,256]{1,0:T(8,128)}, f32[8,256]{1,0:T(8,128)}, f32[8,256]{1,0:T(8,128)}) custom-call(s32[24]{0:T(128)} %get-tuple-element.27.ctl, f32[256,256]{1,0:T(8,128)} %bitcast.7, f32[256,256]{1,0:T(8,128)} %bitcast.8, f32[8,256]{1,0:T(8,128)} %get-tuple-element.29.columns_in, ...), custom_call_target="tpu_custom_call" | custom-call | flops 8388608 | bytes 4194304 | tf_op jit(solution)/shard_map/pallas_call | solution.py:860
  27.2 19.1 %all-to-all-start.1 = ((f32[16,8,256]{2,1,0:T(8,128)}), f32[16,8,256]{2,1,0:T(8,128)S(1)}, u32[]{:S(2)}, u32[]{:S(2)}) async-start(f32[16,8,256]{2,1,0:T(8,128)} %bitcast.14), calls=%async_computation.1 | async-start | bytes 262144 | tf_op jit(solution)/shard_map/all_to_all | solution.py:789
  46.4 0.7 copy-done.2
  47.1 0.1 copy-done.4
  47.2 6.0 %shard_map.67 = (f32[2,3,256,256]{3,2,1,0:T(8,128)}, f32[5,80,256]{2,1,0:T(8,128)}, f32[5,80,256]{2,1,0:T(8,128)}) custom-call(s32[24]{0:T(128)} %get-tuple-element.27.ctl, f32[2,3,256,256]{3,2,1,0:T(8,128)} %get-tuple-element.32.state_in, f32[2,256,256]{2,1,0:T(8,128)} %bed_in.7, f32[2,3,256,256]{3,2,1,0:T(8,128)} %state_first.1, ...), custom_call_target="tpu_custom_call" | custom-call | flops 16777216 | bytes 4194304 | tf_op jit(solution)/shard_map/pallas_call | solution.py:842
  53.2 2.0 %collective-permute-start.2 = (f32[5,80,256]{2,1,0:T(8,128)}, f32[5,80,256]{2,1,0:T(8,128)S(1)}, u32[]{:S(2)}, u32[]{:S(2)}) collective-permute-start(f32[5,80,256]{2,1,0:T(8,128)} %get-tuple-element.39), channel_id=1, source_target_pairs={{0,2},{2,4},{4,6},{6,8},{8,10},{10,12},{12,14},{14,0},{1,3},{3,5},... | collective-permute-start | bytes 1228808 | tf_op jit(solution)/shard_map/ppermute | solution.py:38
  55.2 0.7 copy-done.13
  55.9 5.0 %shard_map.68 = (f32[2,3,256,256]{3,2,1,0:T(8,128)}, f32[128,256]{1,0:T(8,128)}, f32[8,256]{1,0:T(8,128)}, f32[8,256]{1,0:T(8,128)}) custom-call(s32[24]{0:T(128)} %get-tuple-element.27.ctl, f32[128,256]{1,0:T(8,128)} %bitcast.11, f32[256,256]{1,0:T(8,128)} %bitcast.9, f32[8,256]{1,0:T(8,128)} %get-tuple-element.31.columns_in, ...), custom_call_target="tpu_custom_call" | custom-call | flops 8388608 | bytes 4194304 | tf_op jit(solution)/shard_map/pallas_call | solution.py:860
  60.8 4.7 %all-to-all-start.2 = ((f32[16,8,256]{2,1,0:T(8,128)}), f32[16,8,256]{2,1,0:T(8,128)S(1)}, u32[]{:S(2)}, u32[]{:S(2)}) async-start(f32[16,8,256]{2,1,0:T(8,128)} %bitcast.15), calls=%async_computation.2 | async-start | bytes 262144 | tf_op jit(solution)/shard_map/all_to_all | solution.py:789
  65.6 2.0 %collective-permute-start.4 = (f32[5,80,256]{2,1,0:T(8,128)S(1)}, f32[5,80,256]{2,1,0:T(8,128)S(1)}, u32[]{:S(2)}, u32[]{:S(2)}) collective-permute-start(f32[5,80,256]{2,1,0:T(8,128)S(1)} %copy-done.15), channel_id=1, source_target_pairs={{0,2},{2,4},{4,6},{6,8},{8,10},{10,12},{12,14},{14,0},{1,3},{3,5},... | collective-permute-start | bytes 1228808 | tf_op jit(solution)/shard_map/ppermute | solution.py:38
  67.5 0.4 collective-permute-done.2.order.low
  68.0 0.8 copy-done
  68.7 6.0 %shard_map.69.rate_in = f32[2,3,256,256]{3,2,1,0:T(8,128)} custom-call(s32[24]{0:T(128)} %get-tuple-element.27.ctl, f32[2,3,256,256]{3,2,1,0:T(8,128)} %get-tuple-element.38.state_in, f32[2,256,256]{2,1,0:T(8,128)} %bed_in.7, f32[5,80,256]{2,1,0:T(8,128)} %copy-done), custom_call_target="tpu_custom_call" | custom-call | flops 16777216 | bytes 4194304 | tf_op jit(solution)/shard_map/pallas_call | solution.py:852
  74.7 0.7 copy-done.14
  75.4 4.7 %shard_map.70 = (f32[2,3,256,256]{3,2,1,0:T(8,128)}, f32[3,112,256]{2,1,0:T(8,128)}, f32[3,112,256]{2,1,0:T(8,128)}, f32[8,256]{1,0:T(8,128)}) custom-call(s32[24]{0:T(128)} %get-tuple-element.27.ctl, f32[128,256]{1,0:T(8,128)} %bitcast.12, f32[256,256]{1,0:T(8,128)} %bitcast.10, f32[8,256]{1,0:T(8,128)} %get-tuple-element.37.columns_in, ...), custom_call_target="tpu_custom_call" | custom-call | flops 8388608 | bytes 4194304 | tf_op jit(solution)/shard_map/pallas_call | solution.py:860
  80.2 1.2 %collective-permute-start.3 = (f32[3,112,256]{2,1,0:T(8,128)}, f32[3,112,256]{2,1,0:T(8,128)S(1)}, u32[]{:S(2)}, u32[]{:S(2)}) collective-permute-start(f32[3,112,256]{2,1,0:T(8,128)} %get-tuple-element.40), channel_id=1, source_target_pairs={{0,2},{2,4},{4,6},{6,8},{8,10},{10,12},{12,14},{14,0},{1,3},{3,5},... | collective-permute-start | bytes 1032200 | tf_op jit(solution)/shard_map/ppermute | solution.py:38
  81.3 1.0 collective-permute-done.4.high
  82.3 1.0 copy-done.7
  83.3 0.7 copy-done.11
  84.0 5.1 %shard_map.71 = (f32[3,160,256]{2,1,0:T(8,128)S(1)}, f32[3,112,256]{2,1,0:T(8,128)S(1)}) custom-call(s32[24]{0:T(128)S(1)} %copy-done.8, f32[8,256]{1,0:T(8,128)S(1)} %copy-done.9, f32[8,256]{1,0:T(8,128)S(1)} %copy-done.10, f32[8,256]{1,0:T(8,128)S(1)} %copy-done.11, f32[5,80,256]{2,1,0:T(8,128)S(1)} %copy-done.1, ...), custom_call_target="tpu_custom_call" | custom-call | flops 8388608 | bytes 4194304 | tf_op jit(solution)/shard_map/pallas_call | solution.py:886
  89.1 3.7 %collective-permute-done.3.arrived.late_in = f32[3,112,256]{2,1,0:T(8,128)S(1)} collective-permute-done((f32[3,112,256]{2,1,0:T(8,128)}, f32[3,112,256]{2,1,0:T(8,128)S(1)}, u32[]{:S(2)}, u32[]{:S(2)}) %collective-permute-start.3) | collective-permute-done | bytes 344096 | tf_op jit(solution)/shard_map/ppermute | solution.py:38
  92.7 0.8 shard_map.72
  93.6 5.8 %shard_map.73.before = f32[2,3,256,256]{3,2,1,0:T(8,128)} custom-call(s32[24]{0:T(128)S(1)} %copy-done.8, f32[8,256]{1,0:T(8,128)S(1)} %copy-done.9, f32[8,256]{1,0:T(8,128)S(1)} %copy-done.10, f32[8,256]{1,0:T(8,128)S(1)} %copy-done.11, f32[5,80,256]{2,1,0:T(8,128)S(1)} %copy-done.3, f32[5,80,256]{2,1,0:T(8,128)S(1)} %copy-done.5, ...), custom_call_target="tpu_custom_call" | custom-call | flops 8388608 | bytes 4194304 | tf_op jit(solution)/shard_map/pallas_call | solution.py:905
  99.5 5.5 %collective-permute-done.5.late_in = f32[3,112,256]{2,1,0:T(8,128)S(1)} collective-permute-done((f32[3,112,256]{2,1,0:T(8,128)S(1)}, f32[3,112,256]{2,1,0:T(8,128)S(1)}, u32[]{:S(2)}, u32[]{:S(2)}) %collective-permute-start.5) | collective-permute-done | bytes 344096 | tf_op jit(solution)/shard_map/ppermute | solution.py:38
  105.0 2.0 %shard_map.74 = f32[2,3,256,256]{3,2,1,0:T(8,128)} custom-call(s32[24]{0:T(128)S(1)} %copy-done.8, f32[3,112,256]{2,1,0:T(8,128)S(1)} %collective-permute-done.5.late_in, f32[3,160,256]{2,1,0:T(8,128)S(1)} %get-tuple-element.47.order.early_in, f32[2,3,256,256]{3,2,1,0:T(8,128)} %shard_map.73.before), custom_call_target="tpu_custom_call", output_to_operand_aliasing={{}: (3, {})} | custom-call | flops 1048576 | bytes 4194304 | tf_op jit(solution)/shard_map/pallas_call | solution.py:920
  (29 shorter events, 0.1 us)
Async XLA Ops:
  3.6 17.9 %all-to-all-start = ((f32[16,16,256]{2,1,0:T(8,128)}), f32[16,16,256]{2,1,0:T(8,128)S(1)}, u32[]{:S(2)}, u32[]{:S(2)}) async-start(f32[16,16,256]{2,1,0:T(8,128)} %bitcast.13), calls=%async_computation | async-start | bytes 524288 | tf_op jit(solution)/shard_map/all_to_all | solution.py:789
  11.0 35.3 %collective-permute-start = (f32[5,80,256]{2,1,0:T(8,128)}, f32[5,80,256]{2,1,0:T(8,128)S(1)}, u32[]{:S(2)}, u32[]{:S(2)}) collective-permute-start(f32[5,80,256]{2,1,0:T(8,128)} %get-tuple-element.33), channel_id=1, source_target_pairs={{0,2},{2,4},{4,6},{6,8},{8,10},{10,12},{12,14},{14,0},{1,3},{3,5},... | collective-permute-start | bytes 1228808 | tf_op jit(solution)/shard_map/ppermute | solution.py:38
  12.9 33.4 %collective-permute-start.1 = (f32[5,80,256]{2,1,0:T(8,128)}, f32[5,80,256]{2,1,0:T(8,128)S(1)}, u32[]{:S(2)}, u32[]{:S(2)}) collective-permute-start(f32[5,80,256]{2,1,0:T(8,128)} %get-tuple-element.34), channel_id=1, source_target_pairs={{0,2},{2,4},{4,6},{6,8},{8,10},{10,12},{12,14},{14,0},{1,3},{3,5},... | collective-permute-start | bytes 1228808 | tf_op jit(solution)/shard_map/ppermute | solution.py:38
  21.5 0.7 copy-start.12
  27.2 28.0 %all-to-all-start.1 = ((f32[16,8,256]{2,1,0:T(8,128)}), f32[16,8,256]{2,1,0:T(8,128)S(1)}, u32[]{:S(2)}, u32[]{:S(2)}) async-start(f32[16,8,256]{2,1,0:T(8,128)} %bitcast.14), calls=%async_computation.1 | async-start | bytes 262144 | tf_op jit(solution)/shard_map/all_to_all | solution.py:789
  46.3 0.8 copy-start.2
  46.3 0.9 copy-start.4
  53.2 14.8 %collective-permute-start.2 = (f32[5,80,256]{2,1,0:T(8,128)}, f32[5,80,256]{2,1,0:T(8,128)S(1)}, u32[]{:S(2)}, u32[]{:S(2)}) collective-permute-start(f32[5,80,256]{2,1,0:T(8,128)} %get-tuple-element.39), channel_id=1, source_target_pairs={{0,2},{2,4},{4,6},{6,8},{8,10},{10,12},{12,14},{14,0},{1,3},{3,5},... | collective-permute-start | bytes 1228808 | tf_op jit(solution)/shard_map/ppermute | solution.py:38
  55.2 0.7 copy-start.13
  55.9 9.7 %copy-start.15 = (f32[5,80,256]{2,1,0:T(8,128)S(1)}, f32[5,80,256]{2,1,0:T(8,128)}, u32[]{:S(2)}) copy-start(f32[5,80,256]{2,1,0:T(8,128)} %get-tuple-element.44) | copy-start | bytes 1228804
  60.8 13.9 %all-to-all-start.2 = ((f32[16,8,256]{2,1,0:T(8,128)}), f32[16,8,256]{2,1,0:T(8,128)S(1)}, u32[]{:S(2)}, u32[]{:S(2)}) async-start(f32[16,8,256]{2,1,0:T(8,128)} %bitcast.15), calls=%async_computation.2 | async-start | bytes 262144 | tf_op jit(solution)/shard_map/all_to_all | solution.py:789
  65.6 16.7 %collective-permute-start.4 = (f32[5,80,256]{2,1,0:T(8,128)S(1)}, f32[5,80,256]{2,1,0:T(8,128)S(1)}, u32[]{:S(2)}, u32[]{:S(2)}) collective-permute-start(f32[5,80,256]{2,1,0:T(8,128)S(1)} %copy-done.15), channel_id=1, source_target_pairs={{0,2},{2,4},{4,6},{6,8},{8,10},{10,12},{12,14},{14,0},{1,3},{3,5},... | collective-permute-start | bytes 1228808 | tf_op jit(solution)/shard_map/ppermute | solution.py:38
  68.0 0.8 copy-start
  74.7 0.7 copy-start.14
  75.4 6.9 %copy-start.1 = (f32[5,80,256]{2,1,0:T(8,128)S(1)}, f32[5,80,256]{2,1,0:T(8,128)}, u32[]{:S(2)}) copy-start(f32[5,80,256]{2,1,0:T(8,128)} %copy-done) | copy-start | bytes 1228804
  75.4 6.9 %copy-start.8 = (s32[24]{0:T(128)S(1)}, s32[24]{0:T(128)}, u32[]{:S(2)}) copy-start(s32[24]{0:T(128)} %get-tuple-element.27.ctl) | copy-start | bytes 292
  75.4 6.9 %copy-start.9 = (f32[8,256]{1,0:T(8,128)S(1)}, f32[8,256]{1,0:T(8,128)}, u32[]{:S(2)}) copy-start(f32[8,256]{1,0:T(8,128)} %get-tuple-element.41.delta0) | copy-start | bytes 24580
  75.4 6.9 %copy-start.10 = (f32[8,256]{1,0:T(8,128)S(1)}, f32[8,256]{1,0:T(8,128)}, u32[]{:S(2)}) copy-start(f32[8,256]{1,0:T(8,128)} %get-tuple-element.42.delta1) | copy-start | bytes 24580
  80.1 13.5 %copy-start.3 = (f32[5,80,256]{2,1,0:T(8,128)S(1)}, f32[5,80,256]{2,1,0:T(8,128)}, u32[]{:S(2)}) copy-start(f32[5,80,256]{2,1,0:T(8,128)} %copy-done.2) | copy-start | bytes 1228804
  80.1 13.5 %copy-start.5 = (f32[5,80,256]{2,1,0:T(8,128)S(1)}, f32[5,80,256]{2,1,0:T(8,128)}, u32[]{:S(2)}) copy-start(f32[5,80,256]{2,1,0:T(8,128)} %copy-done.4) | copy-start | bytes 1228804
  80.1 13.5 %copy-start.6 = (f32[2,3,256,256]{3,2,1,0:T(8,128)S(1)}, f32[2,3,256,256]{3,2,1,0:T(8,128)}, u32[]{:S(2)}) copy-start(f32[2,3,256,256]{3,2,1,0:T(8,128)} %get-tuple-element.48.state) | copy-start | bytes 4718596
  80.2 12.6 %collective-permute-start.3 = (f32[3,112,256]{2,1,0:T(8,128)}, f32[3,112,256]{2,1,0:T(8,128)S(1)}, u32[]{:S(2)}, u32[]{:S(2)}) collective-permute-start(f32[3,112,256]{2,1,0:T(8,128)} %get-tuple-element.40), channel_id=1, source_target_pairs={{0,2},{2,4},{4,6},{6,8},{8,10},{10,12},{12,14},{14,0},{1,3},{3,5},... | collective-permute-start | bytes 1032200 | tf_op jit(solution)/shard_map/ppermute | solution.py:38
  82.3 1.0 copy-start.7
  83.3 0.7 copy-start.11
  93.5 11.5 %collective-permute-start.5 = (f32[3,112,256]{2,1,0:T(8,128)S(1)}, f32[3,112,256]{2,1,0:T(8,128)S(1)}, u32[]{:S(2)}, u32[]{:S(2)}) collective-permute-start(f32[3,112,256]{2,1,0:T(8,128)S(1)} %shard_map.72), channel_id=1, source_target_pairs={{0,2},{2,4},{4,6},{6,8},{8,10},{10,12},{12,14},{14,0},{1,3},{3,5},... | collective-permute-start | bytes 1032200 | tf_op jit(solution)/shard_map/ppermute | solution.py:38

commit v13 on v12

--- a/solution.py
+++ b/solution.py
@@ -19,8 +19,8 @@
 SLOT_LOW, WALL_WEST, WALL_EAST, WALL_OUTER, WET, MOVE = 0, 1, 3, 5, 7, 13
 WET_FIRST, WET_SECOND = 16, 19
 CONTROLS = 24
-EARLY = 160
-PIECES = ((0, 80), (80, 160))
+EARLY = 192
+PIECES = ((0, 96), (96, 192))
 LATE = TILE - EARLY + 16
 CHUNKS = 8
 PARTS = 8
@@ -101,18 +101,23 @@
     column = lax.axis_index("xb")
     last = lax.axis_size("xb") - 1
     devices = 2 * (last + 1)
-    block = out.shape[0] // devices
     device = column * 2 + upper
     top = jnp.broadcast_to(fastest, (8, TILE))
     for peer in range(devices):
-        out[peer * block : peer * block + 8, :] = top
+        out[peer * 8 : peer * 8 + 8, :TILE] = top
+        if bed is not None:
+            out[peer * 8 : peer * 8 + 8, TILE:] = top[:, :LANES]
     row = sublanes()
 
     def edge(line):
         rows = slice(line, line + 1)
-        slots = [slot_of(ctl, position) for position in range(2)]
-        fields = [state[slot, field, rows, :] for slot in slots for field in range(3)]
-        return stacked(fields, top), [bed[slot, rows, :] for slot in slots] if bed is not None else None
+        lines = []
+        for position in range(2):
+            slot = slot_of(ctl, position)
+            lines += [state[slot, field, rows, :] for field in range(3)]
+            if bed is not None:
+                lines.append(bed[slot, rows, :])
+        return stacked(lines, top)
 
     for inside, peer, line in (
         (column > 0, device - 2, 0),
@@ -121,11 +126,7 @@
 
         @pl.when(inside)
         def _(peer=peer, line=line):
-            lines, ground = edge(line)
-            start = pl.multiple_of(peer * block, 8)
-            out[pl.ds(start, 8), :] = lines
-            if ground:
-                out[pl.ds(pl.multiple_of(start + 8, 8), 8), :] = stacked(ground, top)
+            out[pl.ds(pl.multiple_of(peer * 8, 8), 8), :TILE] = edge(line)
 
     slot = jnp.where(upper > 0, ctl[SLOT_LOW], 1 - ctl[SLOT_LOW])
     begin = pl.multiple_of((1 - upper) * LANES, LANES)
@@ -140,8 +141,8 @@
         packed = turned if field == 0 else jnp.where(lane == field, turned, packed)
     lines = jnp.transpose(packed)[:8]
     columns[...] = lines
-    start = pl.multiple_of((device + 1 - 2 * upper) * block, 8)
-    out[pl.ds(start, 8), :] = jnp.where(row == TOP, top, lines)
+    start = pl.multiple_of((device + 1 - 2 * upper) * 8, 8)
+    out[pl.ds(start, 8), :TILE] = jnp.where(row == TOP, top, lines)
 
 
 def opening(
@@ -215,6 +216,10 @@
         total = jnp.maximum(total, jnp.where(wet[0, first + slot] > 0, best, 0.0))
     messages(ctl, state, bed, jnp.max(total, keepdims=True), out, columns)
     wait_all(early)
+
+
+def hold(order, leaving, same):
+    del order, leaving, same
 
 
 class Passing:
@@ -595,7 +600,7 @@
     wait_all(start_all(((buffer, leaving),), sems))
 
 
-def correct_rows(ctl, slot, got, ground, block, state, rate, bottom):
+def correct_rows(ctl, slot, got, ground, state, rate, bottom):
     position = jnp.where(ctl[SLOT_LOW] == slot, 0, 1)
     device = lax.axis_index("xb") * 2 + lax.axis_index("yb")
     wall = WALL_WEST if bottom else WALL_EAST
@@ -603,17 +608,20 @@
     @pl.when(jnp.logical_not(flag(ctl, wall + position)))
     def _():
         peer = device - 2 if bottom else device + 2
-        lines = got[pl.ds(pl.multiple_of(peer * block, 8), 8), :]
-        grounds = ground[pl.ds(pl.multiple_of(peer * 16 + 8, 8), 8), :]
-
-        def line(value, offset):
+        block = pl.ds(pl.multiple_of(peer * 8, 8), 8)
+        lines = got[block, :TILE]
+        grounds = ground[block, :TILE]
+        stride = 4 if got.shape[1] > TILE else 3
+
+        def line(offset):
+            other = offset + stride
             picked = jnp.where(
-                position == 0, value[offset : offset + 1, :], value[offset + 3 : offset + 4, :]
+                position == 0, lines[offset : offset + 1, :], lines[other : other + 1, :]
             )
             return jnp.broadcast_to(picked, (8, TILE))
 
-        ghost, _ = cell(*(line(lines, field) for field in range(3)))
-        ghost_ground = jnp.where(position == 0, grounds[0:1, :], grounds[1:2, :])
+        ghost, _ = cell(*(line(field) for field in range(3)))
+        ghost_ground = jnp.where(position == 0, grounds[3:4, :], grounds[7:8, :])
         rows = slice(0, 8) if bottom else slice(TILE - 8, TILE)
         own = [state[slot, field, rows, :] for field in range(3)]
         here, _ = cell(*own)
@@ -626,13 +634,13 @@
             rate[slot, field, rows, :] += jnp.where(chosen, sign * value, 0.0)
 
 
-def column_fix(got, ground, block, columns, bed_columns):
+def column_fix(got, ground, columns):
     upper = lax.axis_index("yb")
     device = lax.axis_index("xb") * 2 + upper
     peer = device + 1 - 2 * upper
-    lines = got[pl.ds(pl.multiple_of(peer * block, 8), 8), :]
-    ghost_ground = ground[pl.ds(pl.multiple_of(peer * 16, 8), 8), :][3:4]
-    del bed_columns
+    block = pl.ds(pl.multiple_of(peer * 8, 8), 8)
+    lines = got[block, :TILE]
+    ghost_ground = ground[block, :TILE][3:4]
     mine = columns[...]
     _, ghost = cell(lines[0:1], lines[1:2], lines[2:3])
     _, own = cell(mine[0:1], mine[1:2], mine[2:3])
@@ -680,14 +688,15 @@
     wait_all(small)
     upper = lax.axis_index("yb")
     devices = 2 * lax.axis_size("xb")
-    block = got.shape[0] // devices
-    tops = got[0:8, :]
+    begin = TILE if got.shape[1] > TILE else 0
+    tops = got[0:8, begin : begin + LANES]
     for peer in range(1, devices):
-        tops = jnp.maximum(tops, got[peer * block : peer * block + 8, :])
+        tops = jnp.maximum(tops, got[peer * 8 : peer * 8 + 8, begin : begin + LANES])
     delta = (COURANT * SPACING) / tops[TOP : TOP + 1, :]
+    delta = jnp.concatenate([delta, delta], 1)
     delta_keep[...] = jnp.broadcast_to(delta, (8, TILE))
     outgoing = start_all(((delta_keep, delta_out),), sems, 5 * PARTS + 3)
-    fix = column_fix(got, ground, block, columns, None)
+    fix = column_fix(got, ground, columns)
     facing = jnp.where(upper > 0, ctl[SLOT_LOW], 1 - ctl[SLOT_LOW])
     begin = pl.multiple_of((1 - upper) * LANES, LANES)
     target = (1 - upper) * (LANES - 1)
@@ -696,9 +705,9 @@
     for index, (slot, part_rows) in enumerate(parts):
         wait_all(incoming[index])
         if part_rows.start == 0:
-            correct_rows(ctl, slot, got, ground, block, state, rate, True)
+            correct_rows(ctl, slot, got, ground, state, rate, True)
         if part_rows.stop == TILE:
-            correct_rows(ctl, slot, got, ground, block, state, rate, False)
+            correct_rows(ctl, slot, got, ground, state, rate, False)
 
         @pl.when(facing == slot)
         def _(slot=slot, part_rows=part_rows):
@@ -808,7 +817,7 @@
     out, columns, ctl, *leaving = call(
         opening,
         (
-            f32(16 * devices, TILE),
+            f32(8 * devices, TILE + LANES),
             f32(8, TILE),
             jax.ShapeDtypeStruct((CONTROLS,), jnp.int32),
         )
@@ -834,10 +843,13 @@
         ground = got if step == 0 else ground
         scratch = [whole, part, whole, pltpu.SemaphoreType.DMA((3 * CHUNKS,))]
         if step == 0:
-            early_first = [shifted(piece, "xb", 1) for piece in leaving]
             rate = call(rates, shape, hbm(), [smem(), hbm(), hbm()], 16 << 20, scratch)(
                 ctl, state, bed
             )
+            leaving[1] = call(
+                hold, piece_shapes[1], hbm(), [hbm(), hbm()], 1 << 10, aliases={1: 0}
+            )(rate, leaving[1])
+            early_first = [shifted(piece, "xb", 1) for piece in leaving]
         elif step == 1:
             rate, *leaving = call(
                 rates_and_leaving,
@@ -876,7 +888,7 @@
                 buffer(delta_shape),
                 pltpu.SemaphoreType.DMA((5 * PARTS + 4,)),
             ],
-            moved=4,
+            moved=6,
         )(ctl, got, ground, columns, state, manning, rate)
         deltas.append(outs[-1])
         state, out, columns, _ = outs

time: 108 us -> 122 us (1.13)
  starting transfers between devices: 39.8 us -> 17 us
  blocking collectives: 0 us -> 21 us
  waiting for transfers between devices: 11.7 us -> 25.9 us
  Pallas kernels: 49.9 us -> 52.1 us
    all_to_all x3 -> x2, starting transfers between devices: 31.2 us -> 8.75 us  [spread(): lax.all_to_all(fast, ('xb', 'yb'), split_axis=0, concat_axis=0, tiled=True)]
    all_to_all x0 -> x1, blocking collectives: none -> 21 us  [spread(): lax.all_to_all(fast, ('xb', 'yb'), split_axis=0, concat_axis=0, tiled=True)]
    all_to_all x3 -> x2, waiting for transfers between devices: 1.16 us -> 22.1 us  [spread(): lax.all_to_all(fast, ('xb', 'yb'), split_axis=0, concat_axis=0, tiled=True)]
    ppermute x6, waiting for transfers between devices: 10.6 us -> 3.84 us  [shifted(): return lax.ppermute(value, axis, pairs)]
    unnamed x32 -> x30, local copies, waits for them, and re-layouts: 5.34 us -> 4.67 us
    pallas_call x1 -> x2, Pallas kernels: 3.59 us -> 3.62 us  [the longest x1 3.62 us: body(): call(opening, (f32(8 * devices, TILE + LANES), f32(8, TILE), jax.ShapeDty...]
  transfers between devices with their start and end apart: 9 -> 8, of which waited for: 5 -> 4; matrix products, arithmetic and copies ran while one was open for 0% -> 0% of each run, Pallas kernels for 41% -> 32%
where the time goes in v13:
time: 122 us; the launch traced here: 121 us
  Pallas kernels  52.1 us (43%)
  waiting for transfers between devices  25.9 us (21%)
  blocking collectives  21 us (17%)
  starting transfers between devices  17 us (14%)
  local copies, waits for them, and re-layouts  4.67 us (4%)
    all_to_all x2, waiting for transfers between devices, spread(): lax.all_to_all(fast, ('xb', 'yb'), split_axis=0, concat_axis=0, tiled=True)  22.1 us
    all_to_all x1, blocking collectives, spread(): lax.all_to_all(fast, ('xb', 'yb'), split_axis=0, concat_axis=0, tiled=True)  21 us
    pallas_call x3, Pallas kernels, body(): call(functools.partial(update, step), (shape,) + shapes + (delta_shape,),...  14.6 us
    all_to_all x2, starting transfers between devices, spread(): lax.all_to_all(fast, ('xb', 'yb'), split_axis=0, concat_axis=0, tiled=True)  8.75 us
    ppermute x6, starting transfers between devices, shifted(): return lax.ppermute(value, axis, pairs)  8.28 us
    pallas_call x1, Pallas kernels, body(): call(repeat_first, shape, hbm(), [smem()] + [vmem()] * 3 + [anywhere()] *...  6.86 us
    pallas_call x1, Pallas kernels, body(): call(rates_and_leaving, (shape,) + piece_shapes, (hbm(),) * 3, [smem()] +...  5.99 us
    pallas_call x1, Pallas kernels, body(): call(rates, shape, hbm(), [smem(), hbm(), hbm()], 16 << 20, scratch)  5.96 us
  transfers between devices with their start and end apart: 8, of which 4 were waited for; matrix products, arithmetic and copies ran while one was open for 0% of the time, Pallas kernels for 32%

profile of v13, /device:TPU:0, one launch (start us, length us, event | category | flops | bytes accessed | tf_op | source)
XLA Modules:
  0.0 121.0 jit_solution(3649014367245521290)
XLA Ops:
  0.0 3.6 %shard_map.64 = (f32[128,384]{1,0:T(8,128)}, f32[8,256]{1,0:T(8,128)}, s32[24]{0:T(128)}, f32[5,96,256]{2,1,0:T(8,128)}, f32[5,96,256]{2,1,0:T(8,128)}) custom-call(f32[2,3,256,256]{3,2,1,0:T(8,128)} %state_first.1, f32[2,256,256]{2,1,0:T(8,128)} %bed_in.7, f32[2,256,256]{2,1,0:T(8,128)} %manning_in.9, s32[4,32]{1,0:T(4,128)} %bitcast.15, s32[3,32]{1,0:T(4,128)} %wet_in.1, ...), custom_call_target="tpu_custom_call" | custom-call | flops 4194304 | bytes 4194304 | tf_op jit(solution)/shard_map/pallas_call | solution.py:817
  3.6 3.0 %collective-permute-start = (f32[5,96,256]{2,1,0:T(8,128)}, f32[5,96,256]{2,1,0:T(8,128)S(1)}, u32[]{:S(2)}, u32[]{:S(2)}) collective-permute-start(f32[5,96,256]{2,1,0:T(8,128)} %get-tuple-element.33), channel_id=1, source_target_pairs={{0,2},{2,4},{4,6},{6,8},{8,10},{10,12},{12,14},{14,0},{1,3},{3,5},... | collective-permute-start | bytes 1474568 | tf_op jit(solution)/shard_map/ppermute | solution.py:38
  6.6 6.0 %shard_map.65.rate_in.order = f32[2,3,256,256]{3,2,1,0:T(8,128)} custom-call(s32[24]{0:T(128)} %get-tuple-element.27.ctl, f32[2,3,256,256]{3,2,1,0:T(8,128)} %state_first.1, f32[2,256,256]{2,1,0:T(8,128)} %bed_in.7), custom_call_target="tpu_custom_call" | custom-call | flops 16777216 | bytes 4194304 | tf_op jit(solution)/shard_map/pallas_call | solution.py:846
  12.6 1.6 %collective-permute-start.1 = (f32[5,96,256]{2,1,0:T(8,128)}, f32[5,96,256]{2,1,0:T(8,128)S(1)}, u32[]{:S(2)}, u32[]{:S(2)}) collective-permute-start(f32[5,96,256]{2,1,0:T(8,128)} %shard_map.67), channel_id=1, source_target_pairs={{0,2},{2,4},{4,6},{6,8},{8,10},{10,12},{12,14},{14,0},{1,3},{3,5},... | collective-permute-start | bytes 1474568 | tf_op jit(solution)/shard_map/ppermute | solution.py:38
  14.2 21.0 %all_to_all.33 = f32[16,8,384]{2,1,0:T(8,128)} all-to-all(f32[16,8,384]{2,1,0:T(8,128)S(1)} %bitcast.13), channel_id=1, replica_groups=mesh['runs'=2,'xb'=8,'yb'=2] {'xb','yb'}, dimensions={0} | all-to-all | bytes 393216 | tf_op jit(solution)/shard_map/all_to_all | solution.py:798
  35.2 5.0 %shard_map.66 = (f32[2,3,256,256]{3,2,1,0:T(8,128)}, f32[128,256]{1,0:T(8,128)}, f32[8,256]{1,0:T(8,128)}, f32[8,256]{1,0:T(8,128)}) custom-call(s32[24]{0:T(128)} %get-tuple-element.27.ctl, f32[128,384]{1,0:T(8,128)} %bitcast.7, f32[128,384]{1,0:T(8,128)} %bitcast.8, f32[8,256]{1,0:T(8,128)} %get-tuple-element.29.columns_in, ...), custom_call_target="tpu_custom_call" | custom-call | flops 8388608 | bytes 6291456 | tf_op jit(solution)/shard_map/pallas_call | solution.py:872
  40.2 0.0 collective-permute-done.arrived_low.low
  40.3 0.8 copy-done.2
  41.0 0.1 copy-done.4
  41.2 6.0 %shard_map.68 = (f32[2,3,256,256]{3,2,1,0:T(8,128)}, f32[5,96,256]{2,1,0:T(8,128)}, f32[5,96,256]{2,1,0:T(8,128)}) custom-call(s32[24]{0:T(128)} %get-tuple-element.27.ctl, f32[2,3,256,256]{3,2,1,0:T(8,128)} %get-tuple-element.32.state_in, f32[2,256,256]{2,1,0:T(8,128)} %bed_in.7, f32[2,3,256,256]{3,2,1,0:T(8,128)} %state_first.1, ...), custom_call_target="tpu_custom_call" | custom-call | flops 16777216 | bytes 4194304 | tf_op jit(solution)/shard_map/pallas_call | solution.py:854
  47.2 0.9 collective-permute-start.2
  48.1 5.2 %all-to-all-start.1 = ((f32[16,8,256]{2,1,0:T(8,128)}), f32[16,8,256]{2,1,0:T(8,128)S(1)}, u32[]{:S(2)}, u32[]{:S(2)}) async-start(f32[16,8,256]{2,1,0:T(8,128)} %bitcast.3), calls=%async_computation.1 | async-start | bytes 262144 | tf_op jit(solution)/shard_map/all_to_all | solution.py:798
  53.3 1.9 %collective-permute-start.4 = (f32[5,96,256]{2,1,0:T(8,128)}, f32[5,96,256]{2,1,0:T(8,128)S(1)}, u32[]{:S(2)}, u32[]{:S(2)}) collective-permute-start(f32[5,96,256]{2,1,0:T(8,128)} %get-tuple-element.44), channel_id=1, source_target_pairs={{0,2},{2,4},{4,6},{6,8},{8,10},{10,12},{12,14},{14,0},{1,3},{3,5},... | collective-permute-start | bytes 1474568 | tf_op jit(solution)/shard_map/ppermute | solution.py:38
  55.3 21.0 %all-to-all-done.1 = f32[16,8,256]{2,1,0:T(8,128)S(1)} async-done(((f32[16,8,256]{2,1,0:T(8,128)}), f32[16,8,256]{2,1,0:T(8,128)S(1)}, u32[]{:S(2)}, u32[]{:S(2)}) %all-to-all-start.1) | async-done | bytes 131104 | tf_op jit(solution)/shard_map/all_to_all | solution.py:798
  76.2 0.7 copy-done.12
  76.9 4.9 %shard_map.69 = (f32[2,3,256,256]{3,2,1,0:T(8,128)}, f32[128,256]{1,0:T(8,128)}, f32[8,256]{1,0:T(8,128)}, f32[8,256]{1,0:T(8,128)}) custom-call(s32[24]{0:T(128)} %get-tuple-element.27.ctl, f32[128,256]{1,0:T(8,128)} %bitcast.11, f32[128,384]{1,0:T(8,128)} %bitcast.9, f32[8,256]{1,0:T(8,128)} %get-tuple-element.31.columns_in, ...), custom_call_target="tpu_custom_call" | custom-call | flops 8388608 | bytes 6291456 | tf_op jit(solution)/shard_map/pallas_call | solution.py:872
  81.8 3.5 %all-to-all-start.2 = ((f32[16,8,256]{2,1,0:T(8,128)}), f32[16,8,256]{2,1,0:T(8,128)S(1)}, u32[]{:S(2)}, u32[]{:S(2)}) async-start(f32[16,8,256]{2,1,0:T(8,128)} %bitcast.14), calls=%async_computation.2 | async-start | bytes 262144 | tf_op jit(solution)/shard_map/all_to_all | solution.py:798
  85.3 0.8 copy-done
  86.1 6.0 %shard_map.70.rate_in = f32[2,3,256,256]{3,2,1,0:T(8,128)} custom-call(s32[24]{0:T(128)} %get-tuple-element.27.ctl, f32[2,3,256,256]{3,2,1,0:T(8,128)} %get-tuple-element.38.state_in, f32[2,256,256]{2,1,0:T(8,128)} %bed_in.7, f32[5,96,256]{2,1,0:T(8,128)} %copy-done), custom_call_target="tpu_custom_call" | custom-call | flops 16777216 | bytes 4194304 | tf_op jit(solution)/shard_map/pallas_call | solution.py:864
  92.1 1.1 all-to-all-done.2
  93.2 0.7 copy-done.13
  93.9 4.7 %shard_map.71 = (f32[2,3,256,256]{3,2,1,0:T(8,128)}, f32[3,80,256]{2,1,0:T(8,128)}, f32[3,80,256]{2,1,0:T(8,128)}, f32[8,256]{1,0:T(8,128)}) custom-call(s32[24]{0:T(128)} %get-tuple-element.27.ctl, f32[128,256]{1,0:T(8,128)} %bitcast.12, f32[128,384]{1,0:T(8,128)} %bitcast.10, f32[8,256]{1,0:T(8,128)} %get-tuple-element.37.columns_in, ...), custom_call_target="tpu_custom_call" | custom-call | flops 8388608 | bytes 6291456 | tf_op jit(solution)/shard_map/pallas_call | solution.py:872
  98.6 0.8 collective-permute-start.3
  99.4 0.9 copy-done.7
  100.4 0.7 copy-done.11
  101.1 5.9 %shard_map.72 = (f32[3,192,256]{2,1,0:T(8,128)S(1)}, f32[3,80,256]{2,1,0:T(8,128)S(1)}) custom-call(s32[24]{0:T(128)S(1)} %copy-done.8, f32[8,256]{1,0:T(8,128)S(1)} %copy-done.9, f32[8,256]{1,0:T(8,128)S(1)} %copy-done.10, f32[8,256]{1,0:T(8,128)S(1)} %copy-done.11, f32[5,96,256]{2,1,0:T(8,128)S(1)} %copy-done.1, ...), custom_call_target="tpu_custom_call" | custom-call | flops 8388608 | bytes 4194304 | tf_op jit(solution)/shard_map/pallas_call | solution.py:898
  107.0 1.8 %collective-permute-done.3.arrived.late_in = f32[3,80,256]{2,1,0:T(8,128)S(1)} collective-permute-done((f32[3,80,256]{2,1,0:T(8,128)}, f32[3,80,256]{2,1,0:T(8,128)S(1)}, u32[]{:S(2)}, u32[]{:S(2)}) %collective-permute-start.3) | collective-permute-done | bytes 245792 | tf_op jit(solution)/shard_map/ppermute | solution.py:38
  108.8 1.2 shard_map.73
  110.0 0.1 collective-permute-start.5
  110.1 6.9 %shard_map.74.before = f32[2,3,256,256]{3,2,1,0:T(8,128)} custom-call(s32[24]{0:T(128)S(1)} %copy-done.8, f32[8,256]{1,0:T(8,128)S(1)} %copy-done.9, f32[8,256]{1,0:T(8,128)S(1)} %copy-done.10, f32[8,256]{1,0:T(8,128)S(1)} %copy-done.11, f32[5,96,256]{2,1,0:T(8,128)S(1)} %copy-done.3, f32[5,96,256]{2,1,0:T(8,128)S(1)} %copy-done.5, ...), custom_call_target="tpu_custom_call" | custom-call | flops 8388608 | bytes 4194304 | tf_op jit(solution)/shard_map/pallas_call | solution.py:917
  116.9 2.1 %collective-permute-done.5.late_in = f32[3,80,256]{2,1,0:T(8,128)S(1)} collective-permute-done((f32[3,80,256]{2,1,0:T(8,128)S(1)}, f32[3,80,256]{2,1,0:T(8,128)S(1)}, u32[]{:S(2)}, u32[]{:S(2)}) %collective-permute-start.5) | collective-permute-done | bytes 245792 | tf_op jit(solution)/shard_map/ppermute | solution.py:38
  119.0 2.0 %shard_map.75 = f32[2,3,256,256]{3,2,1,0:T(8,128)} custom-call(s32[24]{0:T(128)S(1)} %copy-done.8, f32[3,80,256]{2,1,0:T(8,128)S(1)} %collective-permute-done.5.late_in, f32[3,192,256]{2,1,0:T(8,128)S(1)} %get-tuple-element.47.order.early_in, f32[2,3,256,256]{3,2,1,0:T(8,128)} %shard_map.74.before), custom_call_target="tpu_custom_call", output_to_operand_aliasing={{}: (3, {})} | custom-call | flops 1048576 | bytes 4194304 | tf_op jit(solution)/shard_map/pallas_call | solution.py:932
  (27 shorter events, 0.1 us)
Async XLA Ops:
  3.6 36.6 %collective-permute-start = (f32[5,96,256]{2,1,0:T(8,128)}, f32[5,96,256]{2,1,0:T(8,128)S(1)}, u32[]{:S(2)}, u32[]{:S(2)}) collective-permute-start(f32[5,96,256]{2,1,0:T(8,128)} %get-tuple-element.33), channel_id=1, source_target_pairs={{0,2},{2,4},{4,6},{6,8},{8,10},{10,12},{12,14},{14,0},{1,3},{3,5},... | collective-permute-start | bytes 1474568 | tf_op jit(solution)/shard_map/ppermute | solution.py:38
  12.6 1.6 %copy-start.14 = (f32[128,384]{1,0:T(8,128)S(1)}, f32[128,384]{1,0:T(8,128)}, u32[]{:S(2)}) copy-start(f32[128,384]{1,0:T(8,128)} %get-tuple-element.28) | copy-start | bytes 589828
  12.6 27.6 %collective-permute-start.1 = (f32[5,96,256]{2,1,0:T(8,128)}, f32[5,96,256]{2,1,0:T(8,128)S(1)}, u32[]{:S(2)}, u32[]{:S(2)}) collective-permute-start(f32[5,96,256]{2,1,0:T(8,128)} %shard_map.67), channel_id=1, source_target_pairs={{0,2},{2,4},{4,6},{6,8},{8,10},{10,12},{12,14},{14,0},{1,3},{3,5},... | collective-permute-start | bytes 1474568 | tf_op jit(solution)/shard_map/ppermute | solution.py:38
  40.2 0.8 copy-start.2
  40.3 0.9 copy-start.4
  47.2 38.1 %collective-permute-start.2 = (f32[5,96,256]{2,1,0:T(8,128)}, f32[5,96,256]{2,1,0:T(8,128)S(1)}, u32[]{:S(2)}, u32[]{:S(2)}) collective-permute-start(f32[5,96,256]{2,1,0:T(8,128)} %get-tuple-element.39), channel_id=1, source_target_pairs={{0,2},{2,4},{4,6},{6,8},{8,10},{10,12},{12,14},{14,0},{1,3},{3,5},... | collective-permute-start | bytes 1474568 | tf_op jit(solution)/shard_map/ppermute | solution.py:38
  48.1 28.1 %all-to-all-start.1 = ((f32[16,8,256]{2,1,0:T(8,128)}), f32[16,8,256]{2,1,0:T(8,128)S(1)}, u32[]{:S(2)}, u32[]{:S(2)}) async-start(f32[16,8,256]{2,1,0:T(8,128)} %bitcast.3), calls=%async_computation.1 | async-start | bytes 262144 | tf_op jit(solution)/shard_map/all_to_all | solution.py:798
  53.3 46.0 %collective-permute-start.4 = (f32[5,96,256]{2,1,0:T(8,128)}, f32[5,96,256]{2,1,0:T(8,128)S(1)}, u32[]{:S(2)}, u32[]{:S(2)}) collective-permute-start(f32[5,96,256]{2,1,0:T(8,128)} %get-tuple-element.44), channel_id=1, source_target_pairs={{0,2},{2,4},{4,6},{6,8},{8,10},{10,12},{12,14},{14,0},{1,3},{3,5},... | collective-permute-start | bytes 1474568 | tf_op jit(solution)/shard_map/ppermute | solution.py:38
  76.2 0.7 copy-start.12
  81.8 11.4 %all-to-all-start.2 = ((f32[16,8,256]{2,1,0:T(8,128)}), f32[16,8,256]{2,1,0:T(8,128)S(1)}, u32[]{:S(2)}, u32[]{:S(2)}) async-start(f32[16,8,256]{2,1,0:T(8,128)} %bitcast.14), calls=%async_computation.2 | async-start | bytes 262144 | tf_op jit(solution)/shard_map/all_to_all | solution.py:798
  85.3 0.8 copy-start
  93.2 0.7 copy-start.13
  93.9 5.5 %copy-start.1 = (f32[5,96,256]{2,1,0:T(8,128)S(1)}, f32[5,96,256]{2,1,0:T(8,128)}, u32[]{:S(2)}) copy-start(f32[5,96,256]{2,1,0:T(8,128)} %copy-done) | copy-start | bytes 1474564
  93.9 5.5 %copy-start.8 = (s32[24]{0:T(128)S(1)}, s32[24]{0:T(128)}, u32[]{:S(2)}) copy-start(s32[24]{0:T(128)} %get-tuple-element.27.ctl) | copy-start | bytes 292
  93.9 5.5 %copy-start.9 = (f32[8,256]{1,0:T(8,128)S(1)}, f32[8,256]{1,0:T(8,128)}, u32[]{:S(2)}) copy-start(f32[8,256]{1,0:T(8,128)} %get-tuple-element.41.delta0) | copy-start | bytes 24580
  93.9 5.5 %copy-start.10 = (f32[8,256]{1,0:T(8,128)S(1)}, f32[8,256]{1,0:T(8,128)}, u32[]{:S(2)}) copy-start(f32[8,256]{1,0:T(8,128)} %get-tuple-element.42.delta1) | copy-start | bytes 24580
  98.6 11.5 %copy-start.3 = (f32[5,96,256]{2,1,0:T(8,128)S(1)}, f32[5,96,256]{2,1,0:T(8,128)}, u32[]{:S(2)}) copy-start(f32[5,96,256]{2,1,0:T(8,128)} %copy-done.2) | copy-start | bytes 1474564
  98.6 11.5 %copy-start.5 = (f32[5,96,256]{2,1,0:T(8,128)S(1)}, f32[5,96,256]{2,1,0:T(8,128)}, u32[]{:S(2)}) copy-start(f32[5,96,256]{2,1,0:T(8,128)} %copy-done.4) | copy-start | bytes 1474564
  98.6 11.5 %copy-start.6 = (f32[2,3,256,256]{3,2,1,0:T(8,128)S(1)}, f32[2,3,256,256]{3,2,1,0:T(8,128)}, u32[]{:S(2)}) copy-start(f32[2,3,256,256]{3,2,1,0:T(8,128)} %get-tuple-element.48.state) | copy-start | bytes 4718596
  98.6 10.2 %collective-permute-start.3 = (f32[3,80,256]{2,1,0:T(8,128)}, f32[3,80,256]{2,1,0:T(8,128)S(1)}, u32[]{:S(2)}, u32[]{:S(2)}) collective-permute-start(f32[3,80,256]{2,1,0:T(8,128)} %get-tuple-element.40), channel_id=1, source_target_pairs={{0,2},{2,4},{4,6},{6,8},{8,10},{10,12},{12,14},{14,0},{1,3},{3,5},... | collective-permute-start | bytes 737288 | tf_op jit(solution)/shard_map/ppermute | solution.py:38
  99.4 0.9 copy-start.7
  100.4 0.7 copy-start.11
  110.0 9.0 %collective-permute-start.5 = (f32[3,80,256]{2,1,0:T(8,128)S(1)}, f32[3,80,256]{2,1,0:T(8,128)S(1)}, u32[]{:S(2)}, u32[]{:S(2)}) collective-permute-start(f32[3,80,256]{2,1,0:T(8,128)S(1)} %shard_map.73), channel_id=1, source_target_pairs={{0,2},{2,4},{4,6},{6,8},{8,10},{10,12},{12,14},{14,0},{1,3},{3,5},... | collective-permute-start | bytes 737288 | tf_op jit(solution)/shard_map/ppermute | solution.py:38

commit v14 on v13

--- a/solution.py
+++ b/solution.py
@@ -19,8 +19,8 @@
 SLOT_LOW, WALL_WEST, WALL_EAST, WALL_OUTER, WET, MOVE = 0, 1, 3, 5, 7, 13
 WET_FIRST, WET_SECOND = 16, 19
 CONTROLS = 24
-EARLY = 192
-PIECES = ((0, 96), (96, 192))
+EARLY = 160
+PIECES = ((0, 88), (88, 160))
 LATE = TILE - EARLY + 16
 CHUNKS = 8
 PARTS = 8
@@ -888,7 +888,7 @@
                 buffer(delta_shape),
                 pltpu.SemaphoreType.DMA((5 * PARTS + 4,)),
             ],
-            moved=6,
+            moved=10,
         )(ctl, got, ground, columns, state, manning, rate)
         deltas.append(outs[-1])
         state, out, columns, _ = outs

time: 122 us -> 102 us (0.84)
  blocking collectives: 21 us -> 0 us
  starting transfers between devices: 17 us -> 22.5 us
  Pallas kernels: 52.1 us -> 49.8 us
  waiting for transfers between devices: 25.9 us -> 23.6 us
    all_to_all x1 -> x0, blocking collectives: 21 us -> none  [spread(): lax.all_to_all(fast, ('xb', 'yb'), split_axis=0, concat_axis=0, tiled=True)]
    all_to_all x2 -> x3, waiting for transfers between devices: 22.1 us -> 12 us  [spread(): lax.all_to_all(fast, ('xb', 'yb'), split_axis=0, concat_axis=0, tiled=True)]
    ppermute x6, waiting for transfers between devices: 3.84 us -> 11.6 us  [shifted(): return lax.ppermute(value, axis, pairs)]
    all_to_all x2 -> x3, starting transfers between devices: 8.75 us -> 13.3 us  [spread(): lax.all_to_all(fast, ('xb', 'yb'), split_axis=0, concat_axis=0, tiled=True)]
    unnamed x30 -> x32, local copies, waits for them, and re-layouts: 4.67 us -> 5.57 us
  transfers between devices with their start and end apart: 8 -> 9, of which waited for: 4 -> 5; matrix products, arithmetic and copies ran while one was open for 0% -> 0% of each run, Pallas kernels for 32% -> 43%
where the time goes in v14:
time: 102 us
  Pallas kernels  49.8 us (49%)
  waiting for transfers between devices  23.6 us (23%)
  starting transfers between devices  22.5 us (22%)
  local copies, waits for them, and re-layouts  5.57 us (5%)
    pallas_call x3, Pallas kernels, body(): call(functools.partial(update, step), (shape,) + shapes + (delta_shape,),...  14.6 us
    all_to_all x3, starting transfers between devices, spread(): lax.all_to_all(fast, ('xb', 'yb'), split_axis=0, concat_axis=0, tiled=True)  13.3 us
    all_to_all x3, waiting for transfers between devices, spread(): lax.all_to_all(fast, ('xb', 'yb'), split_axis=0, concat_axis=0, tiled=True)  12 us
    ppermute x6, waiting for transfers between devices, shifted(): return lax.ppermute(value, axis, pairs)  11.6 us
    ppermute x6, starting transfers between devices, shifted(): return lax.ppermute(value, axis, pairs)  9.26 us
    pallas_call x1, Pallas kernels, body(): call(rates_and_leaving, (shape,) + piece_shapes, (hbm(),) * 3, [smem()] +...  5.99 us
    pallas_call x1, Pallas kernels, body(): call(rates, shape, hbm(), [smem(), hbm(), hbm()], 16 << 20, scratch)  5.96 us
    pallas_call x1, Pallas kernels, body(): call(rates_after, shape, hbm(), [smem()] + [hbm()] * 3, 16 << 20, scratch)  5.96 us
  transfers between devices with their start and end apart: 9, of which 5 were waited for; matrix products, arithmetic and copies ran while one was open for 0% of the time, Pallas kernels for 43%

profile of v14, /device:TPU:0, one launch (start us, length us, event | category | flops | bytes accessed | tf_op | source)
XLA Modules:
  0.0 101.8 jit_solution(17994221978805954877)
XLA Ops:
  0.0 3.6 %shard_map.64 = (f32[128,384]{1,0:T(8,128)}, f32[8,256]{1,0:T(8,128)}, s32[24]{0:T(128)}, f32[5,88,256]{2,1,0:T(8,128)}, f32[5,72,256]{2,1,0:T(8,128)}) custom-call(f32[2,3,256,256]{3,2,1,0:T(8,128)} %state_first.1, f32[2,256,256]{2,1,0:T(8,128)} %bed_in.7, f32[2,256,256]{2,1,0:T(8,128)} %manning_in.9, s32[4,32]{1,0:T(4,128)} %bitcast.16, s32[3,32]{1,0:T(4,128)} %wet_in.1, ...), custom_call_target="tpu_custom_call" | custom-call | flops 4194304 | bytes 4194304 | tf_op jit(solution)/shard_map/pallas_call | solution.py:817
  3.6 3.0 %collective-permute-start = (f32[5,88,256]{2,1,0:T(8,128)}, f32[5,88,256]{2,1,0:T(8,128)S(1)}, u32[]{:S(2)}, u32[]{:S(2)}) collective-permute-start(f32[5,88,256]{2,1,0:T(8,128)} %get-tuple-element.33), channel_id=1, source_target_pairs={{0,2},{2,4},{4,6},{6,8},{8,10},{10,12},{12,14},{14,0},{1,3},{3,5},... | collective-permute-start | bytes 1351688 | tf_op jit(solution)/shard_map/ppermute | solution.py:38
  6.6 5.0 %all-to-all-start = ((f32[16,8,384]{2,1,0:T(8,128)}), f32[16,8,384]{2,1,0:T(8,128)S(1)}, u32[]{:S(2)}, u32[]{:S(2)}) async-start(f32[16,8,384]{2,1,0:T(8,128)} %bitcast.13), calls=%async_computation | async-start | bytes 393216 | tf_op jit(solution)/shard_map/all_to_all | solution.py:798
  11.6 6.0 %shard_map.65.rate_in.order = f32[2,3,256,256]{3,2,1,0:T(8,128)} custom-call(s32[24]{0:T(128)} %get-tuple-element.27.ctl, f32[2,3,256,256]{3,2,1,0:T(8,128)} %state_first.1, f32[2,256,256]{2,1,0:T(8,128)} %bed_in.7), custom_call_target="tpu_custom_call" | custom-call | flops 16777216 | bytes 4194304 | tf_op jit(solution)/shard_map/pallas_call | solution.py:846
  17.6 2.0 %collective-permute-start.1 = (f32[5,72,256]{2,1,0:T(8,128)}, f32[5,72,256]{2,1,0:T(8,128)S(1)}, u32[]{:S(2)}, u32[]{:S(2)}) collective-permute-start(f32[5,72,256]{2,1,0:T(8,128)} %shard_map.67), channel_id=1, source_target_pairs={{0,2},{2,4},{4,6},{6,8},{8,10},{10,12},{12,14},{14,0},{1,3},{3,5},... | collective-permute-start | bytes 1105928 | tf_op jit(solution)/shard_map/ppermute | solution.py:38
  19.5 12.0 %all-to-all-done = f32[16,8,384]{2,1,0:T(8,128)S(1)} async-done(((f32[16,8,384]{2,1,0:T(8,128)}), f32[16,8,384]{2,1,0:T(8,128)S(1)}, u32[]{:S(2)}, u32[]{:S(2)}) %all-to-all-start) | async-done | bytes 196640 | tf_op jit(solution)/shard_map/all_to_all | solution.py:798
  31.5 0.7 copy-done.12
  32.2 4.9 %shard_map.66 = (f32[2,3,256,256]{3,2,1,0:T(8,128)}, f32[128,256]{1,0:T(8,128)}, f32[8,256]{1,0:T(8,128)}, f32[8,256]{1,0:T(8,128)}) custom-call(s32[24]{0:T(128)} %get-tuple-element.27.ctl, f32[128,384]{1,0:T(8,128)} %bitcast.7, f32[128,384]{1,0:T(8,128)} %bitcast.8, f32[8,256]{1,0:T(8,128)} %get-tuple-element.29.columns_in, ...), custom_call_target="tpu_custom_call" | custom-call | flops 8388608 | bytes 10485760 | tf_op jit(solution)/shard_map/pallas_call | solution.py:872
  37.1 3.5 %all-to-all-start.1 = ((f32[16,8,256]{2,1,0:T(8,128)}), f32[16,8,256]{2,1,0:T(8,128)S(1)}, u32[]{:S(2)}, u32[]{:S(2)}) async-start(f32[16,8,256]{2,1,0:T(8,128)} %bitcast.14), calls=%async_computation.1 | async-start | bytes 262144 | tf_op jit(solution)/shard_map/all_to_all | solution.py:798
  40.7 0.7 copy-done.5
  41.4 0.2 copy-done.2
  41.6 6.0 %shard_map.68 = (f32[2,3,256,256]{3,2,1,0:T(8,128)}, f32[5,88,256]{2,1,0:T(8,128)}, f32[5,72,256]{2,1,0:T(8,128)}) custom-call(s32[24]{0:T(128)} %get-tuple-element.27.ctl, f32[2,3,256,256]{3,2,1,0:T(8,128)} %get-tuple-element.32.state_in, f32[2,256,256]{2,1,0:T(8,128)} %bed_in.7, f32[2,3,256,256]{3,2,1,0:T(8,128)} %state_first.1, ...), custom_call_target="tpu_custom_call" | custom-call | flops 16777216 | bytes 4194304 | tf_op jit(solution)/shard_map/pallas_call | solution.py:854
  47.6 1.9 %collective-permute-start.2 = (f32[5,88,256]{2,1,0:T(8,128)}, f32[5,88,256]{2,1,0:T(8,128)S(1)}, u32[]{:S(2)}, u32[]{:S(2)}) collective-permute-start(f32[5,88,256]{2,1,0:T(8,128)} %get-tuple-element.39), channel_id=1, source_target_pairs={{0,2},{2,4},{4,6},{6,8},{8,10},{10,12},{12,14},{14,0},{1,3},{3,5},... | collective-permute-start | bytes 1351688 | tf_op jit(solution)/shard_map/ppermute | solution.py:38
  49.5 0.7 copy-done.13
  50.1 5.0 %shard_map.69 = (f32[2,3,256,256]{3,2,1,0:T(8,128)}, f32[128,256]{1,0:T(8,128)}, f32[8,256]{1,0:T(8,128)}, f32[8,256]{1,0:T(8,128)}) custom-call(s32[24]{0:T(128)} %get-tuple-element.27.ctl, f32[128,256]{1,0:T(8,128)} %bitcast.11, f32[128,384]{1,0:T(8,128)} %bitcast.9, f32[8,256]{1,0:T(8,128)} %get-tuple-element.31.columns_in, ...), custom_call_target="tpu_custom_call" | custom-call | flops 8388608 | bytes 10485760 | tf_op jit(solution)/shard_map/pallas_call | solution.py:872
  55.1 4.8 %all-to-all-start.2 = ((f32[16,8,256]{2,1,0:T(8,128)}), f32[16,8,256]{2,1,0:T(8,128)S(1)}, u32[]{:S(2)}, u32[]{:S(2)}) async-start(f32[16,8,256]{2,1,0:T(8,128)} %bitcast.15), calls=%async_computation.2 | async-start | bytes 262144 | tf_op jit(solution)/shard_map/all_to_all | solution.py:798
  59.9 2.0 %collective-permute-start.4 = (f32[5,72,256]{2,1,0:T(8,128)S(1)}, f32[5,72,256]{2,1,0:T(8,128)S(1)}, u32[]{:S(2)}, u32[]{:S(2)}) collective-permute-start(f32[5,72,256]{2,1,0:T(8,128)S(1)} %copy-done.15), channel_id=1, source_target_pairs={{0,2},{2,4},{4,6},{6,8},{8,10},{10,12},{12,14},{14,0},{1,3},{3,5},... | collective-permute-start | bytes 1105928 | tf_op jit(solution)/shard_map/ppermute | solution.py:38
  61.9 1.2 %collective-permute-done.2.order.low = f32[5,88,256]{2,1,0:T(8,128)S(1)} collective-permute-done((f32[5,88,256]{2,1,0:T(8,128)}, f32[5,88,256]{2,1,0:T(8,128)S(1)}, u32[]{:S(2)}, u32[]{:S(2)}) %collective-permute-start.2) | collective-permute-done | bytes 450592 | tf_op jit(solution)/shard_map/ppermute | solution.py:38
  63.1 0.8 copy-done
  63.9 6.0 %shard_map.70.rate_in = f32[2,3,256,256]{3,2,1,0:T(8,128)} custom-call(s32[24]{0:T(128)} %get-tuple-element.27.ctl, f32[2,3,256,256]{3,2,1,0:T(8,128)} %get-tuple-element.38.state_in, f32[2,256,256]{2,1,0:T(8,128)} %bed_in.7, f32[5,88,256]{2,1,0:T(8,128)} %copy-done), custom_call_target="tpu_custom_call" | custom-call | flops 16777216 | bytes 4194304 | tf_op jit(solution)/shard_map/pallas_call | solution.py:864
  69.9 0.7 copy-done.14
  70.5 4.7 %shard_map.71 = (f32[2,3,256,256]{3,2,1,0:T(8,128)}, f32[3,112,256]{2,1,0:T(8,128)}, f32[3,112,256]{2,1,0:T(8,128)}, f32[8,256]{1,0:T(8,128)}) custom-call(s32[24]{0:T(128)} %get-tuple-element.27.ctl, f32[128,256]{1,0:T(8,128)} %bitcast.12, f32[128,384]{1,0:T(8,128)} %bitcast.10, f32[8,256]{1,0:T(8,128)} %get-tuple-element.37.columns_in, ...), custom_call_target="tpu_custom_call" | custom-call | flops 8388608 | bytes 10485760 | tf_op jit(solution)/shard_map/pallas_call | solution.py:872
  75.3 0.4 collective-permute-start.3
  75.7 0.1 collective-permute-done.4.high
  75.8 1.2 %copy-done.7 = f32[3,112,256]{2,1,0:T(8,128)S(1)} copy-done((f32[3,112,256]{2,1,0:T(8,128)S(1)}, f32[3,112,256]{2,1,0:T(8,128)}, u32[]{:S(2)}) %copy-start.7) | copy-done | bytes 344088
  77.0 0.7 copy-done.11
  77.7 5.1 %shard_map.72 = (f32[3,160,256]{2,1,0:T(8,128)S(1)}, f32[3,112,256]{2,1,0:T(8,128)S(1)}) custom-call(s32[24]{0:T(128)S(1)} %copy-done.8, f32[8,256]{1,0:T(8,128)S(1)} %copy-done.9, f32[8,256]{1,0:T(8,128)S(1)} %copy-done.10, f32[8,256]{1,0:T(8,128)S(1)} %copy-done.11, f32[5,88,256]{2,1,0:T(8,128)S(1)} %copy-done.1, ...), custom_call_target="tpu_custom_call" | custom-call | flops 8388608 | bytes 4194304 | tf_op jit(solution)/shard_map/pallas_call | solution.py:898
  82.8 5.0 %collective-permute-done.3.arrived.late_in = f32[3,112,256]{2,1,0:T(8,128)S(1)} collective-permute-done((f32[3,112,256]{2,1,0:T(8,128)}, f32[3,112,256]{2,1,0:T(8,128)S(1)}, u32[]{:S(2)}, u32[]{:S(2)}) %collective-permute-start.3) | collective-permute-done | bytes 344096 | tf_op jit(solution)/shard_map/ppermute | solution.py:38
  87.7 0.8 shard_map.73
  88.6 5.8 %shard_map.74.before = f32[2,3,256,256]{3,2,1,0:T(8,128)} custom-call(s32[24]{0:T(128)S(1)} %copy-done.8, f32[8,256]{1,0:T(8,128)S(1)} %copy-done.9, f32[8,256]{1,0:T(8,128)S(1)} %copy-done.10, f32[8,256]{1,0:T(8,128)S(1)} %copy-done.11, f32[5,88,256]{2,1,0:T(8,128)S(1)} %copy-done.3, f32[5,72,256]{2,1,0:T(8,128)S(1)} %copy-done.6, ...), custom_call_target="tpu_custom_call" | custom-call | flops 8388608 | bytes 4194304 | tf_op jit(solution)/shard_map/pallas_call | solution.py:917
  94.5 5.4 %collective-permute-done.5.late_in = f32[3,112,256]{2,1,0:T(8,128)S(1)} collective-permute-done((f32[3,112,256]{2,1,0:T(8,128)S(1)}, f32[3,112,256]{2,1,0:T(8,128)S(1)}, u32[]{:S(2)}, u32[]{:S(2)}) %collective-permute-start.5) | collective-permute-done | bytes 344096 | tf_op jit(solution)/shard_map/ppermute | solution.py:38
  99.8 2.0 %shard_map.75 = f32[2,3,256,256]{3,2,1,0:T(8,128)} custom-call(s32[24]{0:T(128)S(1)} %copy-done.8, f32[3,112,256]{2,1,0:T(8,128)S(1)} %collective-permute-done.5.late_in, f32[3,160,256]{2,1,0:T(8,128)S(1)} %get-tuple-element.47.order.early_in, f32[2,3,256,256]{3,2,1,0:T(8,128)} %shard_map.74.before), custom_call_target="tpu_custom_call", output_to_operand_aliasing={{}: (3, {})} | custom-call | flops 1048576 | bytes 4194304 | tf_op jit(solution)/shard_map/pallas_call | solution.py:932
  (30 shorter events, 0.1 us)
Async XLA Ops:
  3.6 37.1 %collective-permute-start = (f32[5,88,256]{2,1,0:T(8,128)}, f32[5,88,256]{2,1,0:T(8,128)S(1)}, u32[]{:S(2)}, u32[]{:S(2)}) collective-permute-start(f32[5,88,256]{2,1,0:T(8,128)} %get-tuple-element.33), channel_id=1, source_target_pairs={{0,2},{2,4},{4,6},{6,8},{8,10},{10,12},{12,14},{14,0},{1,3},{3,5},... | collective-permute-start | bytes 1351688 | tf_op jit(solution)/shard_map/ppermute | solution.py:38
  6.6 25.0 %all-to-all-start = ((f32[16,8,384]{2,1,0:T(8,128)}), f32[16,8,384]{2,1,0:T(8,128)S(1)}, u32[]{:S(2)}, u32[]{:S(2)}) async-start(f32[16,8,384]{2,1,0:T(8,128)} %bitcast.13), calls=%async_computation | async-start | bytes 393216 | tf_op jit(solution)/shard_map/all_to_all | solution.py:798
  17.6 23.1 %collective-permute-start.1 = (f32[5,72,256]{2,1,0:T(8,128)}, f32[5,72,256]{2,1,0:T(8,128)S(1)}, u32[]{:S(2)}, u32[]{:S(2)}) collective-permute-start(f32[5,72,256]{2,1,0:T(8,128)} %shard_map.67), channel_id=1, source_target_pairs={{0,2},{2,4},{4,6},{6,8},{8,10},{10,12},{12,14},{14,0},{1,3},{3,5},... | collective-permute-start | bytes 1105928 | tf_op jit(solution)/shard_map/ppermute | solution.py:38
  31.5 0.7 copy-start.12
  37.1 12.3 %all-to-all-start.1 = ((f32[16,8,256]{2,1,0:T(8,128)}), f32[16,8,256]{2,1,0:T(8,128)S(1)}, u32[]{:S(2)}, u32[]{:S(2)}) async-start(f32[16,8,256]{2,1,0:T(8,128)} %bitcast.14), calls=%async_computation.1 | async-start | bytes 262144 | tf_op jit(solution)/shard_map/all_to_all | solution.py:798
  40.7 0.7 copy-start.5
  40.7 0.9 copy-start.2
  47.6 15.5 %collective-permute-start.2 = (f32[5,88,256]{2,1,0:T(8,128)}, f32[5,88,256]{2,1,0:T(8,128)S(1)}, u32[]{:S(2)}, u32[]{:S(2)}) collective-permute-start(f32[5,88,256]{2,1,0:T(8,128)} %get-tuple-element.39), channel_id=1, source_target_pairs={{0,2},{2,4},{4,6},{6,8},{8,10},{10,12},{12,14},{14,0},{1,3},{3,5},... | collective-permute-start | bytes 1351688 | tf_op jit(solution)/shard_map/ppermute | solution.py:38
  49.5 0.7 copy-start.13
  50.1 9.8 %copy-start.15 = (f32[5,72,256]{2,1,0:T(8,128)S(1)}, f32[5,72,256]{2,1,0:T(8,128)}, u32[]{:S(2)}) copy-start(f32[5,72,256]{2,1,0:T(8,128)} %get-tuple-element.44) | copy-start | bytes 1105924
  55.1 14.7 %all-to-all-start.2 = ((f32[16,8,256]{2,1,0:T(8,128)}), f32[16,8,256]{2,1,0:T(8,128)S(1)}, u32[]{:S(2)}, u32[]{:S(2)}) async-start(f32[16,8,256]{2,1,0:T(8,128)} %bitcast.15), calls=%async_computation.2 | async-start | bytes 262144 | tf_op jit(solution)/shard_map/all_to_all | solution.py:798
  59.9 15.8 %collective-permute-start.4 = (f32[5,72,256]{2,1,0:T(8,128)S(1)}, f32[5,72,256]{2,1,0:T(8,128)S(1)}, u32[]{:S(2)}, u32[]{:S(2)}) collective-permute-start(f32[5,72,256]{2,1,0:T(8,128)S(1)} %copy-done.15), channel_id=1, source_target_pairs={{0,2},{2,4},{4,6},{6,8},{8,10},{10,12},{12,14},{14,0},{1,3},{3,5},... | collective-permute-start | bytes 1105928 | tf_op jit(solution)/shard_map/ppermute | solution.py:38
  63.1 0.8 copy-start
  69.8 0.7 copy-start.14
  70.5 5.2 %copy-start.1 = (f32[5,88,256]{2,1,0:T(8,128)S(1)}, f32[5,88,256]{2,1,0:T(8,128)}, u32[]{:S(2)}) copy-start(f32[5,88,256]{2,1,0:T(8,128)} %copy-done) | copy-start | bytes 1351684
  70.5 5.2 %copy-start.8 = (s32[24]{0:T(128)S(1)}, s32[24]{0:T(128)}, u32[]{:S(2)}) copy-start(s32[24]{0:T(128)} %get-tuple-element.27.ctl) | copy-start | bytes 292
  70.5 5.2 %copy-start.9 = (f32[8,256]{1,0:T(8,128)S(1)}, f32[8,256]{1,0:T(8,128)}, u32[]{:S(2)}) copy-start(f32[8,256]{1,0:T(8,128)} %get-tuple-element.41.delta0) | copy-start | bytes 24580
  70.5 5.2 %copy-start.10 = (f32[8,256]{1,0:T(8,128)S(1)}, f32[8,256]{1,0:T(8,128)}, u32[]{:S(2)}) copy-start(f32[8,256]{1,0:T(8,128)} %get-tuple-element.42.delta1) | copy-start | bytes 24580
  75.3 13.3 %copy-start.3 = (f32[5,88,256]{2,1,0:T(8,128)S(1)}, f32[5,88,256]{2,1,0:T(8,128)}, u32[]{:S(2)}) copy-start(f32[5,88,256]{2,1,0:T(8,128)} %copy-done.2) | copy-start | bytes 1351684
  75.3 13.3 %copy-start.4 = (f32[2,3,256,256]{3,2,1,0:T(8,128)S(1)}, f32[2,3,256,256]{3,2,1,0:T(8,128)}, u32[]{:S(2)}) copy-start(f32[2,3,256,256]{3,2,1,0:T(8,128)} %get-tuple-element.48.state) | copy-start | bytes 4718596
  75.3 13.3 %copy-start.6 = (f32[5,72,256]{2,1,0:T(8,128)S(1)}, f32[5,72,256]{2,1,0:T(8,128)}, u32[]{:S(2)}) copy-start(f32[5,72,256]{2,1,0:T(8,128)} %copy-done.5) | copy-start | bytes 1105924
  75.3 12.4 %collective-permute-start.3 = (f32[3,112,256]{2,1,0:T(8,128)}, f32[3,112,256]{2,1,0:T(8,128)S(1)}, u32[]{:S(2)}, u32[]{:S(2)}) collective-permute-start(f32[3,112,256]{2,1,0:T(8,128)} %get-tuple-element.40), channel_id=1, source_target_pairs={{0,2},{2,4},{4,6},{6,8},{8,10},{10,12},{12,14},{14,0},{1,3},{3,5},... | collective-permute-start | bytes 1032200 | tf_op jit(solution)/shard_map/ppermute | solution.py:38
  75.8 1.2 %copy-start.7 = (f32[3,112,256]{2,1,0:T(8,128)S(1)}, f32[3,112,256]{2,1,0:T(8,128)}, u32[]{:S(2)}) copy-start(f32[3,112,256]{2,1,0:T(8,128)} %get-tuple-element.45.late) | copy-start | bytes 1032196
  77.0 0.7 copy-start.11
  88.5 11.3 %collective-permute-start.5 = (f32[3,112,256]{2,1,0:T(8,128)S(1)}, f32[3,112,256]{2,1,0:T(8,128)S(1)}, u32[]{:S(2)}, u32[]{:S(2)}) collective-permute-start(f32[3,112,256]{2,1,0:T(8,128)S(1)} %shard_map.73), channel_id=1, source_target_pairs={{0,2},{2,4},{4,6},{6,8},{8,10},{10,12},{12,14},{14,0},{1,3},{3,5},... | collective-permute-start | bytes 1032200 | tf_op jit(solution)/shard_map/ppermute | solution.py:38

commit v15 on v14

--- a/solution.py
+++ b/solution.py
@@ -843,7 +843,7 @@
         ground = got if step == 0 else ground
         scratch = [whole, part, whole, pltpu.SemaphoreType.DMA((3 * CHUNKS,))]
         if step == 0:
-            rate = call(rates, shape, hbm(), [smem(), hbm(), hbm()], 16 << 20, scratch)(
+            rate = call(rates, shape, hbm(), [smem(), hbm(), hbm()], 0, scratch, moved=0)(
                 ctl, state, bed
             )
             leaving[1] = call(

time: 102 us -> 102 us (level)
  Pallas kernels: 49.8 us -> 45.5 us
  waiting for transfers between devices: 23.6 us -> 27.9 us
    pallas_call x1, Pallas kernels: 5.82 us -> 1.52 us  [body(): call(repeat_first, shape, hbm(), [smem()] + [vmem()] * 3 + [anywhere()] *...]
    ppermute x6, waiting for transfers between devices: 11.6 us -> 15.9 us  [shifted(): return lax.ppermute(value, axis, pairs)]
  transfers between devices with their start and end apart: 9 -> 9, of which waited for: 5 -> 5; matrix products, arithmetic and copies ran while one was open for 0% -> 0% of each run, Pallas kernels for 43% -> 38%
where the time goes in v15:
time: 102 us
  Pallas kernels  45.5 us (45%)
  waiting for transfers between devices  27.9 us (27%)
  starting transfers between devices  22.6 us (22%)
  local copies, waits for them, and re-layouts  5.57 us (5%)
    ppermute x6, waiting for transfers between devices, shifted(): return lax.ppermute(value, axis, pairs)  15.9 us
    pallas_call x3, Pallas kernels, body(): call(functools.partial(update, step), (shape,) + shapes + (delta_shape,),...  14.6 us
    all_to_all x3, starting transfers between devices, spread(): lax.all_to_all(fast, ('xb', 'yb'), split_axis=0, concat_axis=0, tiled=True)  13.3 us
    all_to_all x3, waiting for transfers between devices, spread(): lax.all_to_all(fast, ('xb', 'yb'), split_axis=0, concat_axis=0, tiled=True)  12 us
    ppermute x6, starting transfers between devices, shifted(): return lax.ppermute(value, axis, pairs)  9.29 us
    pallas_call x1, Pallas kernels, body(): call(rates_and_leaving, (shape,) + piece_shapes, (hbm(),) * 3, [smem()] +...  5.99 us
    pallas_call x1, Pallas kernels, body(): call(rates, shape, hbm(), [smem(), hbm(), hbm()], 0, scratch, moved=0)  5.96 us
    pallas_call x1, Pallas kernels, body(): call(rates_after, shape, hbm(), [smem()] + [hbm()] * 3, 16 << 20, scratch)  5.96 us
  transfers between devices with their start and end apart: 9, of which 5 were waited for; matrix products, arithmetic and copies ran while one was open for 0% of the time, Pallas kernels for 38%

profile of v15, /device:TPU:0, one launch (start us, length us, event | category | flops | bytes accessed | tf_op | source)
XLA Modules:
  0.0 101.8 jit_solution(17994221978805954877)
XLA Ops:
  0.0 3.6 %shard_map.64 = (f32[128,384]{1,0:T(8,128)}, f32[8,256]{1,0:T(8,128)}, s32[24]{0:T(128)}, f32[5,88,256]{2,1,0:T(8,128)}, f32[5,72,256]{2,1,0:T(8,128)}) custom-call(f32[2,3,256,256]{3,2,1,0:T(8,128)} %state_first.1, f32[2,256,256]{2,1,0:T(8,128)} %bed_in.7, f32[2,256,256]{2,1,0:T(8,128)} %manning_in.9, s32[4,32]{1,0:T(4,128)} %bitcast.16, s32[3,32]{1,0:T(4,128)} %wet_in.1, ...), custom_call_target="tpu_custom_call" | custom-call | flops 4194304 | bytes 4194304 | tf_op jit(solution)/shard_map/pallas_call | solution.py:817
  3.6 3.0 %collective-permute-start = (f32[5,88,256]{2,1,0:T(8,128)}, f32[5,88,256]{2,1,0:T(8,128)S(1)}, u32[]{:S(2)}, u32[]{:S(2)}) collective-permute-start(f32[5,88,256]{2,1,0:T(8,128)} %get-tuple-element.33), channel_id=1, source_target_pairs={{0,2},{2,4},{4,6},{6,8},{8,10},{10,12},{12,14},{14,0},{1,3},{3,5},... | collective-permute-start | bytes 1351688 | tf_op jit(solution)/shard_map/ppermute | solution.py:38
  6.6 5.0 %all-to-all-start = ((f32[16,8,384]{2,1,0:T(8,128)}), f32[16,8,384]{2,1,0:T(8,128)S(1)}, u32[]{:S(2)}, u32[]{:S(2)}) async-start(f32[16,8,384]{2,1,0:T(8,128)} %bitcast.13), calls=%async_computation | async-start | bytes 393216 | tf_op jit(solution)/shard_map/all_to_all | solution.py:798
  11.6 6.0 %shard_map.65.rate_in.order = f32[2,3,256,256]{3,2,1,0:T(8,128)} custom-call(s32[24]{0:T(128)} %get-tuple-element.27.ctl, f32[2,3,256,256]{3,2,1,0:T(8,128)} %state_first.1, f32[2,256,256]{2,1,0:T(8,128)} %bed_in.7), custom_call_target="tpu_custom_call" | custom-call | tf_op jit(solution)/shard_map/pallas_call | solution.py:846
  17.6 2.0 %collective-permute-start.1 = (f32[5,72,256]{2,1,0:T(8,128)}, f32[5,72,256]{2,1,0:T(8,128)S(1)}, u32[]{:S(2)}, u32[]{:S(2)}) collective-permute-start(f32[5,72,256]{2,1,0:T(8,128)} %shard_map.67), channel_id=1, source_target_pairs={{0,2},{2,4},{4,6},{6,8},{8,10},{10,12},{12,14},{14,0},{1,3},{3,5},... | collective-permute-start | bytes 1105928 | tf_op jit(solution)/shard_map/ppermute | solution.py:38
  19.5 12.0 %all-to-all-done = f32[16,8,384]{2,1,0:T(8,128)S(1)} async-done(((f32[16,8,384]{2,1,0:T(8,128)}), f32[16,8,384]{2,1,0:T(8,128)S(1)}, u32[]{:S(2)}, u32[]{:S(2)}) %all-to-all-start) | async-done | bytes 196640 | tf_op jit(solution)/shard_map/all_to_all | solution.py:798
  31.5 0.7 copy-done.12
  32.2 4.9 %shard_map.66 = (f32[2,3,256,256]{3,2,1,0:T(8,128)}, f32[128,256]{1,0:T(8,128)}, f32[8,256]{1,0:T(8,128)}, f32[8,256]{1,0:T(8,128)}) custom-call(s32[24]{0:T(128)} %get-tuple-element.27.ctl, f32[128,384]{1,0:T(8,128)} %bitcast.7, f32[128,384]{1,0:T(8,128)} %bitcast.8, f32[8,256]{1,0:T(8,128)} %get-tuple-element.29.columns_in, ...), custom_call_target="tpu_custom_call" | custom-call | flops 8388608 | bytes 10485760 | tf_op jit(solution)/shard_map/pallas_call | solution.py:872
  37.1 3.5 %all-to-all-start.1 = ((f32[16,8,256]{2,1,0:T(8,128)}), f32[16,8,256]{2,1,0:T(8,128)S(1)}, u32[]{:S(2)}, u32[]{:S(2)}) async-start(f32[16,8,256]{2,1,0:T(8,128)} %bitcast.14), calls=%async_computation.1 | async-start | bytes 262144 | tf_op jit(solution)/shard_map/all_to_all | solution.py:798
  40.7 0.7 copy-done.5
  41.4 0.2 copy-done.2
  41.6 6.0 %shard_map.68 = (f32[2,3,256,256]{3,2,1,0:T(8,128)}, f32[5,88,256]{2,1,0:T(8,128)}, f32[5,72,256]{2,1,0:T(8,128)}) custom-call(s32[24]{0:T(128)} %get-tuple-element.27.ctl, f32[2,3,256,256]{3,2,1,0:T(8,128)} %get-tuple-element.32.state_in, f32[2,256,256]{2,1,0:T(8,128)} %bed_in.7, f32[2,3,256,256]{3,2,1,0:T(8,128)} %state_first.1, ...), custom_call_target="tpu_custom_call" | custom-call | flops 16777216 | bytes 4194304 | tf_op jit(solution)/shard_map/pallas_call | solution.py:854
  47.6 1.9 %collective-permute-start.2 = (f32[5,88,256]{2,1,0:T(8,128)}, f32[5,88,256]{2,1,0:T(8,128)S(1)}, u32[]{:S(2)}, u32[]{:S(2)}) collective-permute-start(f32[5,88,256]{2,1,0:T(8,128)} %get-tuple-element.39), channel_id=1, source_target_pairs={{0,2},{2,4},{4,6},{6,8},{8,10},{10,12},{12,14},{14,0},{1,3},{3,5},... | collective-permute-start | bytes 1351688 | tf_op jit(solution)/shard_map/ppermute | solution.py:38
  49.5 0.7 copy-done.13
  50.1 5.0 %shard_map.69 = (f32[2,3,256,256]{3,2,1,0:T(8,128)}, f32[128,256]{1,0:T(8,128)}, f32[8,256]{1,0:T(8,128)}, f32[8,256]{1,0:T(8,128)}) custom-call(s32[24]{0:T(128)} %get-tuple-element.27.ctl, f32[128,256]{1,0:T(8,128)} %bitcast.11, f32[128,384]{1,0:T(8,128)} %bitcast.9, f32[8,256]{1,0:T(8,128)} %get-tuple-element.31.columns_in, ...), custom_call_target="tpu_custom_call" | custom-call | flops 8388608 | bytes 10485760 | tf_op jit(solution)/shard_map/pallas_call | solution.py:872
  55.1 4.8 %all-to-all-start.2 = ((f32[16,8,256]{2,1,0:T(8,128)}), f32[16,8,256]{2,1,0:T(8,128)S(1)}, u32[]{:S(2)}, u32[]{:S(2)}) async-start(f32[16,8,256]{2,1,0:T(8,128)} %bitcast.15), calls=%async_computation.2 | async-start | bytes 262144 | tf_op jit(solution)/shard_map/all_to_all | solution.py:798
  59.9 2.0 %collective-permute-start.4 = (f32[5,72,256]{2,1,0:T(8,128)S(1)}, f32[5,72,256]{2,1,0:T(8,128)S(1)}, u32[]{:S(2)}, u32[]{:S(2)}) collective-permute-start(f32[5,72,256]{2,1,0:T(8,128)S(1)} %copy-done.15), channel_id=1, source_target_pairs={{0,2},{2,4},{4,6},{6,8},{8,10},{10,12},{12,14},{14,0},{1,3},{3,5},... | collective-permute-start | bytes 1105928 | tf_op jit(solution)/shard_map/ppermute | solution.py:38
  61.9 1.2 %collective-permute-done.2.order.low = f32[5,88,256]{2,1,0:T(8,128)S(1)} collective-permute-done((f32[5,88,256]{2,1,0:T(8,128)}, f32[5,88,256]{2,1,0:T(8,128)S(1)}, u32[]{:S(2)}, u32[]{:S(2)}) %collective-permute-start.2) | collective-permute-done | bytes 450592 | tf_op jit(solution)/shard_map/ppermute | solution.py:38
  63.1 0.8 copy-done
  63.9 6.0 %shard_map.70.rate_in = f32[2,3,256,256]{3,2,1,0:T(8,128)} custom-call(s32[24]{0:T(128)} %get-tuple-element.27.ctl, f32[2,3,256,256]{3,2,1,0:T(8,128)} %get-tuple-element.38.state_in, f32[2,256,256]{2,1,0:T(8,128)} %bed_in.7, f32[5,88,256]{2,1,0:T(8,128)} %copy-done), custom_call_target="tpu_custom_call" | custom-call | flops 16777216 | bytes 4194304 | tf_op jit(solution)/shard_map/pallas_call | solution.py:864
  69.9 0.7 copy-done.14
  70.5 4.7 %shard_map.71 = (f32[2,3,256,256]{3,2,1,0:T(8,128)}, f32[3,112,256]{2,1,0:T(8,128)}, f32[3,112,256]{2,1,0:T(8,128)}, f32[8,256]{1,0:T(8,128)}) custom-call(s32[24]{0:T(128)} %get-tuple-element.27.ctl, f32[128,256]{1,0:T(8,128)} %bitcast.12, f32[128,384]{1,0:T(8,128)} %bitcast.10, f32[8,256]{1,0:T(8,128)} %get-tuple-element.37.columns_in, ...), custom_call_target="tpu_custom_call" | custom-call | flops 8388608 | bytes 10485760 | tf_op jit(solution)/shard_map/pallas_call | solution.py:872
  75.3 0.4 collective-permute-start.3
  75.8 1.2 %copy-done.7 = f32[3,112,256]{2,1,0:T(8,128)S(1)} copy-done((f32[3,112,256]{2,1,0:T(8,128)S(1)}, f32[3,112,256]{2,1,0:T(8,128)}, u32[]{:S(2)}) %copy-start.7) | copy-done | bytes 344088
  77.0 0.7 copy-done.11
  77.7 5.1 %shard_map.72 = (f32[3,160,256]{2,1,0:T(8,128)S(1)}, f32[3,112,256]{2,1,0:T(8,128)S(1)}) custom-call(s32[24]{0:T(128)S(1)} %copy-done.8, f32[8,256]{1,0:T(8,128)S(1)} %copy-done.9, f32[8,256]{1,0:T(8,128)S(1)} %copy-done.10, f32[8,256]{1,0:T(8,128)S(1)} %copy-done.11, f32[5,88,256]{2,1,0:T(8,128)S(1)} %copy-done.1, ...), custom_call_target="tpu_custom_call" | custom-call | flops 8388608 | bytes 4194304 | tf_op jit(solution)/shard_map/pallas_call | solution.py:898
  82.8 5.0 %collective-permute-done.3.arrived.late_in = f32[3,112,256]{2,1,0:T(8,128)S(1)} collective-permute-done((f32[3,112,256]{2,1,0:T(8,128)}, f32[3,112,256]{2,1,0:T(8,128)S(1)}, u32[]{:S(2)}, u32[]{:S(2)}) %collective-permute-start.3) | collective-permute-done | bytes 344096 | tf_op jit(solution)/shard_map/ppermute | solution.py:38
  87.7 0.8 shard_map.73
  88.5 0.1 collective-permute-start.5
  88.6 1.5 %shard_map.74.before = f32[2,3,256,256]{3,2,1,0:T(8,128)} custom-call(s32[24]{0:T(128)S(1)} %copy-done.8, f32[8,256]{1,0:T(8,128)S(1)} %copy-done.9, f32[8,256]{1,0:T(8,128)S(1)} %copy-done.10, f32[8,256]{1,0:T(8,128)S(1)} %copy-done.11, f32[5,88,256]{2,1,0:T(8,128)S(1)} %copy-done.3, f32[5,72,256]{2,1,0:T(8,128)S(1)} %copy-done.6, ...), custom_call_target="tpu_custom_call" | custom-call | flops 8388608 | bytes 4194304 | tf_op jit(solution)/shard_map/pallas_call | solution.py:917
  90.2 9.7 %collective-permute-done.5.late_in = f32[3,112,256]{2,1,0:T(8,128)S(1)} collective-permute-done((f32[3,112,256]{2,1,0:T(8,128)S(1)}, f32[3,112,256]{2,1,0:T(8,128)S(1)}, u32[]{:S(2)}, u32[]{:S(2)}) %collective-permute-start.5) | collective-permute-done | bytes 344096 | tf_op jit(solution)/shard_map/ppermute | solution.py:38
  99.8 2.0 %shard_map.75 = f32[2,3,256,256]{3,2,1,0:T(8,128)} custom-call(s32[24]{0:T(128)S(1)} %copy-done.8, f32[3,112,256]{2,1,0:T(8,128)S(1)} %collective-permute-done.5.late_in, f32[3,160,256]{2,1,0:T(8,128)S(1)} %get-tuple-element.47.order.early_in, f32[2,3,256,256]{3,2,1,0:T(8,128)} %shard_map.74.before), custom_call_target="tpu_custom_call", output_to_operand_aliasing={{}: (3, {})} | custom-call | flops 1048576 | bytes 4194304 | tf_op jit(solution)/shard_map/pallas_call | solution.py:932
  (30 shorter events, 0.1 us)
Async XLA Ops:
  3.6 37.1 %collective-permute-start = (f32[5,88,256]{2,1,0:T(8,128)}, f32[5,88,256]{2,1,0:T(8,128)S(1)}, u32[]{:S(2)}, u32[]{:S(2)}) collective-permute-start(f32[5,88,256]{2,1,0:T(8,128)} %get-tuple-element.33), channel_id=1, source_target_pairs={{0,2},{2,4},{4,6},{6,8},{8,10},{10,12},{12,14},{14,0},{1,3},{3,5},... | collective-permute-start | bytes 1351688 | tf_op jit(solution)/shard_map/ppermute | solution.py:38
  6.6 25.0 %all-to-all-start = ((f32[16,8,384]{2,1,0:T(8,128)}), f32[16,8,384]{2,1,0:T(8,128)S(1)}, u32[]{:S(2)}, u32[]{:S(2)}) async-start(f32[16,8,384]{2,1,0:T(8,128)} %bitcast.13), calls=%async_computation | async-start | bytes 393216 | tf_op jit(solution)/shard_map/all_to_all | solution.py:798
  17.6 23.1 %collective-permute-start.1 = (f32[5,72,256]{2,1,0:T(8,128)}, f32[5,72,256]{2,1,0:T(8,128)S(1)}, u32[]{:S(2)}, u32[]{:S(2)}) collective-permute-start(f32[5,72,256]{2,1,0:T(8,128)} %shard_map.67), channel_id=1, source_target_pairs={{0,2},{2,4},{4,6},{6,8},{8,10},{10,12},{12,14},{14,0},{1,3},{3,5},... | collective-permute-start | bytes 1105928 | tf_op jit(solution)/shard_map/ppermute | solution.py:38
  31.5 0.7 copy-start.12
  37.1 12.3 %all-to-all-start.1 = ((f32[16,8,256]{2,1,0:T(8,128)}), f32[16,8,256]{2,1,0:T(8,128)S(1)}, u32[]{:S(2)}, u32[]{:S(2)}) async-start(f32[16,8,256]{2,1,0:T(8,128)} %bitcast.14), calls=%async_computation.1 | async-start | bytes 262144 | tf_op jit(solution)/shard_map/all_to_all | solution.py:798
  40.7 0.7 copy-start.5
  40.7 0.9 copy-start.2
  47.6 15.5 %collective-permute-start.2 = (f32[5,88,256]{2,1,0:T(8,128)}, f32[5,88,256]{2,1,0:T(8,128)S(1)}, u32[]{:S(2)}, u32[]{:S(2)}) collective-permute-start(f32[5,88,256]{2,1,0:T(8,128)} %get-tuple-element.39), channel_id=1, source_target_pairs={{0,2},{2,4},{4,6},{6,8},{8,10},{10,12},{12,14},{14,0},{1,3},{3,5},... | collective-permute-start | bytes 1351688 | tf_op jit(solution)/shard_map/ppermute | solution.py:38
  49.5 0.7 copy-start.13
  50.1 9.8 %copy-start.15 = (f32[5,72,256]{2,1,0:T(8,128)S(1)}, f32[5,72,256]{2,1,0:T(8,128)}, u32[]{:S(2)}) copy-start(f32[5,72,256]{2,1,0:T(8,128)} %get-tuple-element.44) | copy-start | bytes 1105924
  55.1 14.7 %all-to-all-start.2 = ((f32[16,8,256]{2,1,0:T(8,128)}), f32[16,8,256]{2,1,0:T(8,128)S(1)}, u32[]{:S(2)}, u32[]{:S(2)}) async-start(f32[16,8,256]{2,1,0:T(8,128)} %bitcast.15), calls=%async_computation.2 | async-start | bytes 262144 | tf_op jit(solution)/shard_map/all_to_all | solution.py:798
  59.9 15.8 %collective-permute-start.4 = (f32[5,72,256]{2,1,0:T(8,128)S(1)}, f32[5,72,256]{2,1,0:T(8,128)S(1)}, u32[]{:S(2)}, u32[]{:S(2)}) collective-permute-start(f32[5,72,256]{2,1,0:T(8,128)S(1)} %copy-done.15), channel_id=1, source_target_pairs={{0,2},{2,4},{4,6},{6,8},{8,10},{10,12},{12,14},{14,0},{1,3},{3,5},... | collective-permute-start | bytes 1105928 | tf_op jit(solution)/shard_map/ppermute | solution.py:38
  63.1 0.8 copy-start
  69.8 0.7 copy-start.14
  70.5 5.2 %copy-start.1 = (f32[5,88,256]{2,1,0:T(8,128)S(1)}, f32[5,88,256]{2,1,0:T(8,128)}, u32[]{:S(2)}) copy-start(f32[5,88,256]{2,1,0:T(8,128)} %copy-done) | copy-start | bytes 1351684
  70.5 5.2 %copy-start.8 = (s32[24]{0:T(128)S(1)}, s32[24]{0:T(128)}, u32[]{:S(2)}) copy-start(s32[24]{0:T(128)} %get-tuple-element.27.ctl) | copy-start | bytes 292
  70.5 5.2 %copy-start.9 = (f32[8,256]{1,0:T(8,128)S(1)}, f32[8,256]{1,0:T(8,128)}, u32[]{:S(2)}) copy-start(f32[8,256]{1,0:T(8,128)} %get-tuple-element.41.delta0) | copy-start | bytes 24580
  70.5 5.2 %copy-start.10 = (f32[8,256]{1,0:T(8,128)S(1)}, f32[8,256]{1,0:T(8,128)}, u32[]{:S(2)}) copy-start(f32[8,256]{1,0:T(8,128)} %get-tuple-element.42.delta1) | copy-start | bytes 24580
  75.3 13.3 %copy-start.3 = (f32[5,88,256]{2,1,0:T(8,128)S(1)}, f32[5,88,256]{2,1,0:T(8,128)}, u32[]{:S(2)}) copy-start(f32[5,88,256]{2,1,0:T(8,128)} %copy-done.2) | copy-start | bytes 1351684
  75.3 13.3 %copy-start.4 = (f32[2,3,256,256]{3,2,1,0:T(8,128)S(1)}, f32[2,3,256,256]{3,2,1,0:T(8,128)}, u32[]{:S(2)}) copy-start(f32[2,3,256,256]{3,2,1,0:T(8,128)} %get-tuple-element.48.state) | copy-start | bytes 4718596
  75.3 13.3 %copy-start.6 = (f32[5,72,256]{2,1,0:T(8,128)S(1)}, f32[5,72,256]{2,1,0:T(8,128)}, u32[]{:S(2)}) copy-start(f32[5,72,256]{2,1,0:T(8,128)} %copy-done.5) | copy-start | bytes 1105924
  75.3 12.4 %collective-permute-start.3 = (f32[3,112,256]{2,1,0:T(8,128)}, f32[3,112,256]{2,1,0:T(8,128)S(1)}, u32[]{:S(2)}, u32[]{:S(2)}) collective-permute-start(f32[3,112,256]{2,1,0:T(8,128)} %get-tuple-element.40), channel_id=1, source_target_pairs={{0,2},{2,4},{4,6},{6,8},{8,10},{10,12},{12,14},{14,0},{1,3},{3,5},... | collective-permute-start | bytes 1032200 | tf_op jit(solution)/shard_map/ppermute | solution.py:38
  75.8 1.2 %copy-start.7 = (f32[3,112,256]{2,1,0:T(8,128)S(1)}, f32[3,112,256]{2,1,0:T(8,128)}, u32[]{:S(2)}) copy-start(f32[3,112,256]{2,1,0:T(8,128)} %get-tuple-element.45.late) | copy-start | bytes 1032196
  77.0 0.7 copy-start.11
  88.5 11.3 %collective-permute-start.5 = (f32[3,112,256]{2,1,0:T(8,128)S(1)}, f32[3,112,256]{2,1,0:T(8,128)S(1)}, u32[]{:S(2)}, u32[]{:S(2)}) collective-permute-start(f32[3,112,256]{2,1,0:T(8,128)S(1)} %shard_map.73), channel_id=1, source_target_pairs={{0,2},{2,4},{4,6},{6,8},{8,10},{10,12},{12,14},{14,0},{1,3},{3,5},... | collective-permute-start | bytes 1032200 | tf_op jit(solution)/shard_map/ppermute | solution.py:38

commit v16 on v15

--- a/solution.py
+++ b/solution.py
@@ -526,29 +526,33 @@
 
 
 def merge(late, early, tile):
+    for field in range(3):
+        merge_field(field, late, early, tile)
+
+
+def merge_field(field, late, early, tile):
     row = sublanes()
     lane = lax.broadcasted_iota(jnp.int32, (8, LANES), 1)
-    for field in range(3):
-        first = late[field, 0:8, :]
-        for block in range(EARLY // 8):
-            rows = slice(8 * block, 8 * block + 8)
-            which = block // 16
-            packed = late[field, 8:16, which * LANES : (which + 1) * LANES]
-            sides = pltpu.roll(packed, (-3 - 8 * block) % LANES, 1)
-            value = early[field, rows, :]
-            value = jnp.concatenate(
-                [
-                    jnp.where(lane < 3, sides, value[:, :LANES]),
-                    jnp.where(lane >= LANES - 3, sides, value[:, LANES:]),
-                ],
-                1,
-            )
-            if block == 0:
-                value = jnp.where(row < 3, first, value)
-            if block == EARLY // 8 - 1:
-                value = jnp.where(row < 5, value, first)
-            tile[field, rows, :] = value
-        tile[field, EARLY:, :] = late[field, 16:, :]
+    first = late[field, 0:8, :]
+    for block in range(EARLY // 8):
+        rows = slice(8 * block, 8 * block + 8)
+        which = block // 16
+        packed = late[field, 8:16, which * LANES : (which + 1) * LANES]
+        sides = pltpu.roll(packed, (-3 - 8 * block) % LANES, 1)
+        value = early[field, rows, :]
+        value = jnp.concatenate(
+            [
+                jnp.where(lane < 3, sides, value[:, :LANES]),
+                jnp.where(lane >= LANES - 3, sides, value[:, LANES:]),
+            ],
+            1,
+        )
+        if block == 0:
+            value = jnp.where(row < 3, first, value)
+        if block == EARLY // 8 - 1:
+            value = jnp.where(row < 5, value, first)
+        tile[field, rows, :] = value
+    tile[field, EARLY:, :] = late[field, 16:, :]
 
 
 def repeat_second(ctl, delta0, delta1, delta2, low, high, late, out, late_out, work, tile, sems):
@@ -577,27 +581,22 @@
     wait_all(start_all(((tile, rest),), sems))
 
 
-def finish(ctl, late_in, early_in, before, out, late, early, tile, sems):
+def finish(ctl, late, early, before, out, tile, sems):
     del before
-    wait_all(start_all(((late_in, late), (early_in, early)), sems))
-    merge(late, early, tile)
-    wait_all(start_all(((tile, out.at[ctl[MOVE + 1]]),), sems))
-
-
-def second_late(ctl, arrived, own, order, leaving, buffer, sems):
+    copies = []
+    for field in range(3):
+        merge_field(field, late, early, tile)
+        copies += start_all(
+            ((tile.at[field], out.at[ctl[MOVE + 1], field]),), sems, field
+        )
+    wait_all(copies)
+
+
+def second_late(ctl, arrived, own, order, leaving):
     del order
     again = ctl[MOVE] == ctl[MOVE + 1]
-
-    @pl.when(again)
-    def _():
-        pltpu.make_async_copy(arrived, buffer, sems.at[0]).start()
-
-    @pl.when(jnp.logical_not(again))
-    def _():
-        pltpu.make_async_copy(own, buffer, sems.at[0]).start()
-
-    pltpu.make_async_copy(arrived, buffer, sems.at[0]).wait()
-    wait_all(start_all(((buffer, leaving),), sems))
+    for field in range(3):
+        leaving[field] = jnp.where(again, arrived[field], own[field])
 
 
 def correct_rows(ctl, slot, got, ground, state, rate, bottom):
@@ -801,7 +800,6 @@
 def body(state, bed, manning, neighbours, wet, moves):
     shape = f32(*state.shape)
     devices = lax.axis_size("xb") * lax.axis_size("yb")
-    sem = [pltpu.SemaphoreType.DMA((1,))]
     whole = pltpu.VMEM(state.shape, jnp.float32)
     part = pltpu.VMEM(bed.shape, jnp.float32)
     tile_shape = f32(*state.shape[1:])
@@ -888,7 +886,7 @@
                 buffer(delta_shape),
                 pltpu.SemaphoreType.DMA((5 * PARTS + 4,)),
             ],
-            moved=10,
+            moved=14 if step == 0 else 10,
         )(ctl, got, ground, columns, state, manning, rate)
         deltas.append(outs[-1])
         state, out, columns, _ = outs
@@ -907,10 +905,9 @@
     leaving = call(
         second_late,
         late_shape,
-        anywhere(),
-        [smem(), anywhere(), anywhere(), anywhere()],
-        1 << 20,
-        [buffer(late_shape)] + sem,
+        vmem(),
+        [smem(), vmem(), vmem(), anywhere()],
+        1 << 10,
         room=room,
     )(ctl, late_arrived, late_second, second)
     late_next = shifted(leaving, "xb", 1)
@@ -933,14 +930,9 @@
         finish,
         shape,
         hbm(),
-        [smem(), anywhere(), anywhere(), hbm()],
+        [smem(), vmem(), vmem(), hbm()],
         1 << 20,
-        [
-            buffer(late_shape),
-            buffer(early_state),
-            buffer(tile_shape),
-            pltpu.SemaphoreType.DMA((2,)),
-        ],
+        [buffer(tile_shape), pltpu.SemaphoreType.DMA((3,))],
         {3: 0},
         room=room,
     )(ctl, late_next, second, final)

time: 102 us -> 102 us (level)
  waiting for transfers between devices: 27.9 us -> 23.6 us
  Pallas kernels: 45.5 us -> 49.1 us
    ppermute x6, waiting for transfers between devices: 15.9 us -> 11.6 us  [shifted(): return lax.ppermute(value, axis, pairs)]
    pallas_call x1, Pallas kernels: 1.52 us -> 5.82 us  [body(): call(repeat_first, shape, hbm(), [smem()] + [vmem()] * 3 + [anywhere()] *...]
  transfers between devices with their start and end apart: 9 -> 9, of which waited for: 5 -> 5; matrix products, arithmetic and copies ran while one was open for 0% -> 0% of each run, Pallas kernels for 38% -> 43%
where the time goes in v16:
time: 102 us; the launch traced here: 101 us
  Pallas kernels  49.1 us (48%)
  waiting for transfers between devices  23.6 us (23%)
  starting transfers between devices  22.6 us (22%)
  local copies, waits for them, and re-layouts  5.57 us (5%)
    pallas_call x3, Pallas kernels, body(): call(functools.partial(update, step), (shape,) + shapes + (delta_shape,),...  14.6 us
    all_to_all x3, starting transfers between devices, spread(): lax.all_to_all(fast, ('xb', 'yb'), split_axis=0, concat_axis=0, tiled=True)  13.3 us
    all_to_all x3, waiting for transfers between devices, spread(): lax.all_to_all(fast, ('xb', 'yb'), split_axis=0, concat_axis=0, tiled=True)  12 us
    ppermute x6, waiting for transfers between devices, shifted(): return lax.ppermute(value, axis, pairs)  11.6 us
    ppermute x6, starting transfers between devices, shifted(): return lax.ppermute(value, axis, pairs)  9.29 us
    pallas_call x1, Pallas kernels, body(): call(rates_and_leaving, (shape,) + piece_shapes, (hbm(),) * 3, [smem()] +...  5.99 us
    pallas_call x1, Pallas kernels, body(): call(rates, shape, hbm(), [smem(), hbm(), hbm()], 0, scratch, moved=0)  5.96 us
    pallas_call x1, Pallas kernels, body(): call(rates_after, shape, hbm(), [smem()] + [hbm()] * 3, 16 << 20, scratch)  5.96 us
  transfers between devices with their start and end apart: 9, of which 5 were waited for; matrix products, arithmetic and copies ran while one was open for 0% of the time, Pallas kernels for 43%

profile of v16, /device:TPU:0, one launch (start us, length us, event | category | flops | bytes accessed | tf_op | source)
XLA Modules:
  0.0 101.1 jit_solution(2823451578555659504)
XLA Ops:
  0.0 3.6 %shard_map.64 = (f32[128,384]{1,0:T(8,128)}, f32[8,256]{1,0:T(8,128)}, s32[24]{0:T(128)}, f32[5,88,256]{2,1,0:T(8,128)}, f32[5,72,256]{2,1,0:T(8,128)}) custom-call(f32[2,3,256,256]{3,2,1,0:T(8,128)} %state_first.1, f32[2,256,256]{2,1,0:T(8,128)} %bed_in.7, f32[2,256,256]{2,1,0:T(8,128)} %manning_in.9, s32[4,32]{1,0:T(4,128)} %bitcast.16, s32[3,32]{1,0:T(4,128)} %wet_in.1, ...), custom_call_target="tpu_custom_call" | custom-call | flops 4194304 | bytes 4194304 | tf_op jit(solution)/shard_map/pallas_call | solution.py:815
  3.6 3.0 %collective-permute-start = (f32[5,88,256]{2,1,0:T(8,128)}, f32[5,88,256]{2,1,0:T(8,128)S(1)}, u32[]{:S(2)}, u32[]{:S(2)}) collective-permute-start(f32[5,88,256]{2,1,0:T(8,128)} %get-tuple-element.33), channel_id=1, source_target_pairs={{0,2},{2,4},{4,6},{6,8},{8,10},{10,12},{12,14},{14,0},{1,3},{3,5},... | collective-permute-start | bytes 1351688 | tf_op jit(solution)/shard_map/ppermute | solution.py:38
  6.6 5.0 %all-to-all-start = ((f32[16,8,384]{2,1,0:T(8,128)}), f32[16,8,384]{2,1,0:T(8,128)S(1)}, u32[]{:S(2)}, u32[]{:S(2)}) async-start(f32[16,8,384]{2,1,0:T(8,128)} %bitcast.13), calls=%async_computation | async-start | bytes 393216 | tf_op jit(solution)/shard_map/all_to_all | solution.py:797
  11.6 6.0 %shard_map.65.rate_in.order = f32[2,3,256,256]{3,2,1,0:T(8,128)} custom-call(s32[24]{0:T(128)} %get-tuple-element.27.ctl, f32[2,3,256,256]{3,2,1,0:T(8,128)} %state_first.1, f32[2,256,256]{2,1,0:T(8,128)} %bed_in.7), custom_call_target="tpu_custom_call" | custom-call | tf_op jit(solution)/shard_map/pallas_call | solution.py:844
  17.6 2.0 %collective-permute-start.1 = (f32[5,72,256]{2,1,0:T(8,128)}, f32[5,72,256]{2,1,0:T(8,128)S(1)}, u32[]{:S(2)}, u32[]{:S(2)}) collective-permute-start(f32[5,72,256]{2,1,0:T(8,128)} %shard_map.67), channel_id=1, source_target_pairs={{0,2},{2,4},{4,6},{6,8},{8,10},{10,12},{12,14},{14,0},{1,3},{3,5},... | collective-permute-start | bytes 1105928 | tf_op jit(solution)/shard_map/ppermute | solution.py:38
  19.5 12.0 %all-to-all-done = f32[16,8,384]{2,1,0:T(8,128)S(1)} async-done(((f32[16,8,384]{2,1,0:T(8,128)}), f32[16,8,384]{2,1,0:T(8,128)S(1)}, u32[]{:S(2)}, u32[]{:S(2)}) %all-to-all-start) | async-done | bytes 196640 | tf_op jit(solution)/shard_map/all_to_all | solution.py:797
  31.5 0.7 copy-done.12
  32.2 4.9 %shard_map.66 = (f32[2,3,256,256]{3,2,1,0:T(8,128)}, f32[128,256]{1,0:T(8,128)}, f32[8,256]{1,0:T(8,128)}, f32[8,256]{1,0:T(8,128)}) custom-call(s32[24]{0:T(128)} %get-tuple-element.27.ctl, f32[128,384]{1,0:T(8,128)} %bitcast.7, f32[128,384]{1,0:T(8,128)} %bitcast.8, f32[8,256]{1,0:T(8,128)} %get-tuple-element.29.columns_in, ...), custom_call_target="tpu_custom_call" | custom-call | flops 8388608 | bytes 14680064 | tf_op jit(solution)/shard_map/pallas_call | solution.py:870
  37.1 3.5 %all-to-all-start.1 = ((f32[16,8,256]{2,1,0:T(8,128)}), f32[16,8,256]{2,1,0:T(8,128)S(1)}, u32[]{:S(2)}, u32[]{:S(2)}) async-start(f32[16,8,256]{2,1,0:T(8,128)} %bitcast.14), calls=%async_computation.1 | async-start | bytes 262144 | tf_op jit(solution)/shard_map/all_to_all | solution.py:797
  40.7 0.7 copy-done.5
  41.4 0.2 copy-done.2
  41.6 6.0 %shard_map.68 = (f32[2,3,256,256]{3,2,1,0:T(8,128)}, f32[5,88,256]{2,1,0:T(8,128)}, f32[5,72,256]{2,1,0:T(8,128)}) custom-call(s32[24]{0:T(128)} %get-tuple-element.27.ctl, f32[2,3,256,256]{3,2,1,0:T(8,128)} %get-tuple-element.32.state_in, f32[2,256,256]{2,1,0:T(8,128)} %bed_in.7, f32[2,3,256,256]{3,2,1,0:T(8,128)} %state_first.1, ...), custom_call_target="tpu_custom_call" | custom-call | flops 16777216 | bytes 4194304 | tf_op jit(solution)/shard_map/pallas_call | solution.py:852
  47.6 1.9 %collective-permute-start.2 = (f32[5,88,256]{2,1,0:T(8,128)}, f32[5,88,256]{2,1,0:T(8,128)S(1)}, u32[]{:S(2)}, u32[]{:S(2)}) collective-permute-start(f32[5,88,256]{2,1,0:T(8,128)} %get-tuple-element.39), channel_id=1, source_target_pairs={{0,2},{2,4},{4,6},{6,8},{8,10},{10,12},{12,14},{14,0},{1,3},{3,5},... | collective-permute-start | bytes 1351688 | tf_op jit(solution)/shard_map/ppermute | solution.py:38
  49.5 0.7 copy-done.13
  50.1 5.0 %shard_map.69 = (f32[2,3,256,256]{3,2,1,0:T(8,128)}, f32[128,256]{1,0:T(8,128)}, f32[8,256]{1,0:T(8,128)}, f32[8,256]{1,0:T(8,128)}) custom-call(s32[24]{0:T(128)} %get-tuple-element.27.ctl, f32[128,256]{1,0:T(8,128)} %bitcast.11, f32[128,384]{1,0:T(8,128)} %bitcast.9, f32[8,256]{1,0:T(8,128)} %get-tuple-element.31.columns_in, ...), custom_call_target="tpu_custom_call" | custom-call | flops 8388608 | bytes 10485760 | tf_op jit(solution)/shard_map/pallas_call | solution.py:870
  55.1 4.8 %all-to-all-start.2 = ((f32[16,8,256]{2,1,0:T(8,128)}), f32[16,8,256]{2,1,0:T(8,128)S(1)}, u32[]{:S(2)}, u32[]{:S(2)}) async-start(f32[16,8,256]{2,1,0:T(8,128)} %bitcast.15), calls=%async_computation.2 | async-start | bytes 262144 | tf_op jit(solution)/shard_map/all_to_all | solution.py:797
  59.9 2.0 %collective-permute-start.4 = (f32[5,72,256]{2,1,0:T(8,128)S(1)}, f32[5,72,256]{2,1,0:T(8,128)S(1)}, u32[]{:S(2)}, u32[]{:S(2)}) collective-permute-start(f32[5,72,256]{2,1,0:T(8,128)S(1)} %copy-done.15), channel_id=1, source_target_pairs={{0,2},{2,4},{4,6},{6,8},{8,10},{10,12},{12,14},{14,0},{1,3},{3,5},... | collective-permute-start | bytes 1105928 | tf_op jit(solution)/shard_map/ppermute | solution.py:38
  61.9 1.2 %collective-permute-done.2.order.low = f32[5,88,256]{2,1,0:T(8,128)S(1)} collective-permute-done((f32[5,88,256]{2,1,0:T(8,128)}, f32[5,88,256]{2,1,0:T(8,128)S(1)}, u32[]{:S(2)}, u32[]{:S(2)}) %collective-permute-start.2) | collective-permute-done | bytes 450592 | tf_op jit(solution)/shard_map/ppermute | solution.py:38
  63.1 0.8 copy-done
  63.9 6.0 %shard_map.70.rate_in = f32[2,3,256,256]{3,2,1,0:T(8,128)} custom-call(s32[24]{0:T(128)} %get-tuple-element.27.ctl, f32[2,3,256,256]{3,2,1,0:T(8,128)} %get-tuple-element.38.state_in, f32[2,256,256]{2,1,0:T(8,128)} %bed_in.7, f32[5,88,256]{2,1,0:T(8,128)} %copy-done), custom_call_target="tpu_custom_call" | custom-call | flops 16777216 | bytes 4194304 | tf_op jit(solution)/shard_map/pallas_call | solution.py:862
  69.9 0.7 copy-done.14
  70.5 4.7 %shard_map.71 = (f32[2,3,256,256]{3,2,1,0:T(8,128)}, f32[3,112,256]{2,1,0:T(8,128)}, f32[3,112,256]{2,1,0:T(8,128)}, f32[8,256]{1,0:T(8,128)}) custom-call(s32[24]{0:T(128)} %get-tuple-element.27.ctl, f32[128,256]{1,0:T(8,128)} %bitcast.12, f32[128,384]{1,0:T(8,128)} %bitcast.10, f32[8,256]{1,0:T(8,128)} %get-tuple-element.37.columns_in, ...), custom_call_target="tpu_custom_call" | custom-call | flops 8388608 | bytes 10485760 | tf_op jit(solution)/shard_map/pallas_call | solution.py:870
  75.3 0.4 collective-permute-start.3
  75.8 1.2 %copy-done.7 = f32[3,112,256]{2,1,0:T(8,128)S(1)} copy-done((f32[3,112,256]{2,1,0:T(8,128)S(1)}, f32[3,112,256]{2,1,0:T(8,128)}, u32[]{:S(2)}) %copy-start.7) | copy-done | bytes 344088
  77.0 0.7 copy-done.11
  77.7 5.1 %shard_map.72 = (f32[3,160,256]{2,1,0:T(8,128)S(1)}, f32[3,112,256]{2,1,0:T(8,128)S(1)}) custom-call(s32[24]{0:T(128)S(1)} %copy-done.8, f32[8,256]{1,0:T(8,128)S(1)} %copy-done.9, f32[8,256]{1,0:T(8,128)S(1)} %copy-done.10, f32[8,256]{1,0:T(8,128)S(1)} %copy-done.11, f32[5,88,256]{2,1,0:T(8,128)S(1)} %copy-done.1, ...), custom_call_target="tpu_custom_call" | custom-call | flops 8388608 | bytes 4194304 | tf_op jit(solution)/shard_map/pallas_call | solution.py:896
  82.8 5.0 %collective-permute-done.3.arrived.late_in = f32[3,112,256]{2,1,0:T(8,128)S(1)} collective-permute-done((f32[3,112,256]{2,1,0:T(8,128)}, f32[3,112,256]{2,1,0:T(8,128)S(1)}, u32[]{:S(2)}, u32[]{:S(2)}) %collective-permute-start.3) | collective-permute-done | bytes 344096 | tf_op jit(solution)/shard_map/ppermute | solution.py:38
  87.7 0.6 shard_map.73
  88.3 0.1 collective-permute-start.5
  88.4 5.8 %shard_map.74.before = f32[2,3,256,256]{3,2,1,0:T(8,128)} custom-call(s32[24]{0:T(128)S(1)} %copy-done.8, f32[8,256]{1,0:T(8,128)S(1)} %copy-done.9, f32[8,256]{1,0:T(8,128)S(1)} %copy-done.10, f32[8,256]{1,0:T(8,128)S(1)} %copy-done.11, f32[5,88,256]{2,1,0:T(8,128)S(1)} %copy-done.3, f32[5,72,256]{2,1,0:T(8,128)S(1)} %copy-done.6, ...), custom_call_target="tpu_custom_call" | custom-call | flops 8388608 | bytes 4194304 | tf_op jit(solution)/shard_map/pallas_call | solution.py:914
  94.2 5.4 %collective-permute-done.5.late = f32[3,112,256]{2,1,0:T(8,128)S(1)} collective-permute-done((f32[3,112,256]{2,1,0:T(8,128)S(1)}, f32[3,112,256]{2,1,0:T(8,128)S(1)}, u32[]{:S(2)}, u32[]{:S(2)}) %collective-permute-start.5) | collective-permute-done | bytes 344096 | tf_op jit(solution)/shard_map/ppermute | solution.py:38
  99.6 1.5 %shard_map.75 = f32[2,3,256,256]{3,2,1,0:T(8,128)} custom-call(s32[24]{0:T(128)S(1)} %copy-done.8, f32[3,112,256]{2,1,0:T(8,128)S(1)} %collective-permute-done.5.late, f32[3,160,256]{2,1,0:T(8,128)S(1)} %get-tuple-element.47.order.early, f32[2,3,256,256]{3,2,1,0:T(8,128)} %shard_map.74.before), custom_call_target="tpu_custom_call", output_to_operand_aliasing={{}: (3, {})} | custom-call | flops 1048576 | bytes 4194304 | tf_op jit(solution)/shard_map/pallas_call | solution.py:929
  (30 shorter events, 0.1 us)
Async XLA Ops:
  3.6 37.1 %collective-permute-start = (f32[5,88,256]{2,1,0:T(8,128)}, f32[5,88,256]{2,1,0:T(8,128)S(1)}, u32[]{:S(2)}, u32[]{:S(2)}) collective-permute-start(f32[5,88,256]{2,1,0:T(8,128)} %get-tuple-element.33), channel_id=1, source_target_pairs={{0,2},{2,4},{4,6},{6,8},{8,10},{10,12},{12,14},{14,0},{1,3},{3,5},... | collective-permute-start | bytes 1351688 | tf_op jit(solution)/shard_map/ppermute | solution.py:38
  6.6 25.0 %all-to-all-start = ((f32[16,8,384]{2,1,0:T(8,128)}), f32[16,8,384]{2,1,0:T(8,128)S(1)}, u32[]{:S(2)}, u32[]{:S(2)}) async-start(f32[16,8,384]{2,1,0:T(8,128)} %bitcast.13), calls=%async_computation | async-start | bytes 393216 | tf_op jit(solution)/shard_map/all_to_all | solution.py:797
  17.6 23.1 %collective-permute-start.1 = (f32[5,72,256]{2,1,0:T(8,128)}, f32[5,72,256]{2,1,0:T(8,128)S(1)}, u32[]{:S(2)}, u32[]{:S(2)}) collective-permute-start(f32[5,72,256]{2,1,0:T(8,128)} %shard_map.67), channel_id=1, source_target_pairs={{0,2},{2,4},{4,6},{6,8},{8,10},{10,12},{12,14},{14,0},{1,3},{3,5},... | collective-permute-start | bytes 1105928 | tf_op jit(solution)/shard_map/ppermute | solution.py:38
  31.5 0.7 copy-start.12
  37.1 12.3 %all-to-all-start.1 = ((f32[16,8,256]{2,1,0:T(8,128)}), f32[16,8,256]{2,1,0:T(8,128)S(1)}, u32[]{:S(2)}, u32[]{:S(2)}) async-start(f32[16,8,256]{2,1,0:T(8,128)} %bitcast.14), calls=%async_computation.1 | async-start | bytes 262144 | tf_op jit(solution)/shard_map/all_to_all | solution.py:797
  40.7 0.7 copy-start.5
  40.7 0.9 copy-start.2
  47.6 15.5 %collective-permute-start.2 = (f32[5,88,256]{2,1,0:T(8,128)}, f32[5,88,256]{2,1,0:T(8,128)S(1)}, u32[]{:S(2)}, u32[]{:S(2)}) collective-permute-start(f32[5,88,256]{2,1,0:T(8,128)} %get-tuple-element.39), channel_id=1, source_target_pairs={{0,2},{2,4},{4,6},{6,8},{8,10},{10,12},{12,14},{14,0},{1,3},{3,5},... | collective-permute-start | bytes 1351688 | tf_op jit(solution)/shard_map/ppermute | solution.py:38
  49.5 0.7 copy-start.13
  50.1 9.8 %copy-start.15 = (f32[5,72,256]{2,1,0:T(8,128)S(1)}, f32[5,72,256]{2,1,0:T(8,128)}, u32[]{:S(2)}) copy-start(f32[5,72,256]{2,1,0:T(8,128)} %get-tuple-element.44) | copy-start | bytes 1105924
  55.1 14.7 %all-to-all-start.2 = ((f32[16,8,256]{2,1,0:T(8,128)}), f32[16,8,256]{2,1,0:T(8,128)S(1)}, u32[]{:S(2)}, u32[]{:S(2)}) async-start(f32[16,8,256]{2,1,0:T(8,128)} %bitcast.15), calls=%async_computation.2 | async-start | bytes 262144 | tf_op jit(solution)/shard_map/all_to_all | solution.py:797
  59.9 15.8 %collective-permute-start.4 = (f32[5,72,256]{2,1,0:T(8,128)S(1)}, f32[5,72,256]{2,1,0:T(8,128)S(1)}, u32[]{:S(2)}, u32[]{:S(2)}) collective-permute-start(f32[5,72,256]{2,1,0:T(8,128)S(1)} %copy-done.15), channel_id=1, source_target_pairs={{0,2},{2,4},{4,6},{6,8},{8,10},{10,12},{12,14},{14,0},{1,3},{3,5},... | collective-permute-start | bytes 1105928 | tf_op jit(solution)/shard_map/ppermute | solution.py:38
  63.1 0.8 copy-start
  69.8 0.7 copy-start.14
  70.5 5.2 %copy-start.1 = (f32[5,88,256]{2,1,0:T(8,128)S(1)}, f32[5,88,256]{2,1,0:T(8,128)}, u32[]{:S(2)}) copy-start(f32[5,88,256]{2,1,0:T(8,128)} %copy-done) | copy-start | bytes 1351684
  70.5 5.2 %copy-start.8 = (s32[24]{0:T(128)S(1)}, s32[24]{0:T(128)}, u32[]{:S(2)}) copy-start(s32[24]{0:T(128)} %get-tuple-element.27.ctl) | copy-start | bytes 292
  70.5 5.2 %copy-start.9 = (f32[8,256]{1,0:T(8,128)S(1)}, f32[8,256]{1,0:T(8,128)}, u32[]{:S(2)}) copy-start(f32[8,256]{1,0:T(8,128)} %get-tuple-element.41.delta0) | copy-start | bytes 24580
  70.5 5.2 %copy-start.10 = (f32[8,256]{1,0:T(8,128)S(1)}, f32[8,256]{1,0:T(8,128)}, u32[]{:S(2)}) copy-start(f32[8,256]{1,0:T(8,128)} %get-tuple-element.42.delta1) | copy-start | bytes 24580
  75.3 13.1 %copy-start.3 = (f32[5,88,256]{2,1,0:T(8,128)S(1)}, f32[5,88,256]{2,1,0:T(8,128)}, u32[]{:S(2)}) copy-start(f32[5,88,256]{2,1,0:T(8,128)} %copy-done.2) | copy-start | bytes 1351684
  75.3 13.1 %copy-start.4 = (f32[2,3,256,256]{3,2,1,0:T(8,128)S(1)}, f32[2,3,256,256]{3,2,1,0:T(8,128)}, u32[]{:S(2)}) copy-start(f32[2,3,256,256]{3,2,1,0:T(8,128)} %get-tuple-element.48.state) | copy-start | bytes 4718596
  75.3 13.1 %copy-start.6 = (f32[5,72,256]{2,1,0:T(8,128)S(1)}, f32[5,72,256]{2,1,0:T(8,128)}, u32[]{:S(2)}) copy-start(f32[5,72,256]{2,1,0:T(8,128)} %copy-done.5) | copy-start | bytes 1105924
  75.3 12.4 %collective-permute-start.3 = (f32[3,112,256]{2,1,0:T(8,128)}, f32[3,112,256]{2,1,0:T(8,128)S(1)}, u32[]{:S(2)}, u32[]{:S(2)}) collective-permute-start(f32[3,112,256]{2,1,0:T(8,128)} %get-tuple-element.40), channel_id=1, source_target_pairs={{0,2},{2,4},{4,6},{6,8},{8,10},{10,12},{12,14},{14,0},{1,3},{3,5},... | collective-permute-start | bytes 1032200 | tf_op jit(solution)/shard_map/ppermute | solution.py:38
  75.8 1.2 %copy-start.7 = (f32[3,112,256]{2,1,0:T(8,128)S(1)}, f32[3,112,256]{2,1,0:T(8,128)}, u32[]{:S(2)}) copy-start(f32[3,112,256]{2,1,0:T(8,128)} %get-tuple-element.45.late) | copy-start | bytes 1032196
  77.0 0.7 copy-start.11
  88.3 11.3 %collective-permute-start.5 = (f32[3,112,256]{2,1,0:T(8,128)S(1)}, f32[3,112,256]{2,1,0:T(8,128)S(1)}, u32[]{:S(2)}, u32[]{:S(2)}) collective-permute-start(f32[3,112,256]{2,1,0:T(8,128)S(1)} %shard_map.73), channel_id=1, source_target_pairs={{0,2},{2,4},{4,6},{6,8},{8,10},{10,12},{12,14},{14,0},{1,3},{3,5},... | collective-permute-start | bytes 1032200 | tf_op jit(solution)/shard_map/ppermute | solution.py:38

commit v17 on v16

--- a/solution.py
+++ b/solution.py
@@ -19,8 +19,9 @@
 SLOT_LOW, WALL_WEST, WALL_EAST, WALL_OUTER, WET, MOVE = 0, 1, 3, 5, 7, 13
 WET_FIRST, WET_SECOND = 16, 19
 CONTROLS = 24
-EARLY = 160
-PIECES = ((0, 88), (88, 160))
+EARLY = 144
+PIECES = ((0, 80), (80, 144))
+AGAIN = 16
 LATE = TILE - EARLY + 16
 CHUNKS = 8
 PARTS = 8
@@ -443,8 +444,8 @@
         incoming += start_all(
             ((ref, work.at[:, begin : begin + ref.shape[1]]),), sems, len(incoming)
         )
-    row_ids = lax.broadcasted_iota(jnp.int32, (ROWS, TILE), 0)
-    lane = lax.broadcasted_iota(jnp.int32, (ROWS, LANES), 1)
+    row_ids = lax.broadcasted_iota(jnp.int32, (AGAIN, TILE), 0)
+    lane = lax.broadcasted_iota(jnp.int32, (AGAIN, LANES), 1)
     start = tuple(jnp.zeros((1, TILE), jnp.float32) for _ in range(4))
 
     def halves(value):
@@ -459,7 +460,7 @@
         return jnp.concatenate([low, jnp.where(lane == 0, low, high)], 1)
 
     def down(value):
-        return pltpu.roll(value, ROWS + 7, 0)[:ROWS]
+        return pltpu.roll(value, AGAIN + 7, 0)[:AGAIN]
 
     for step in range(STEPS):
         source, target = (work, other) if step % 2 == 0 else (other, work)
@@ -467,28 +468,28 @@
         wet_now = flag(ctl, wet_from + step)
 
         def group(index, carry, source=source, target=target, delta=delta, wet_now=wet_now):
-            base = pl.multiple_of(index * ROWS, ROWS)
-            rows = pl.ds(base, ROWS)
-            after = pl.ds(pl.multiple_of(jnp.minimum(base + ROWS, EARLY - 8), 8), 8)
+            base = pl.multiple_of(index * AGAIN, AGAIN)
+            rows = pl.ds(base, AGAIN)
+            after = pl.ds(pl.multiple_of(jnp.minimum(base + AGAIN, EARLY - 8), 8), 8)
             refs = [source.at[field] for field in range(3)] + [work.at[3]]
             fields = [jnp.concatenate([ref[rows, :], ref[after, :]], 0) for ref in refs]
             cells_x, cells_y = cell(*fields[:3])
-            here_x = tuple(value[:ROWS] for value in cells_x)
-            here_y = tuple(value[:ROWS] for value in cells_y)
+            here_x = tuple(value[:AGAIN] for value in cells_x)
+            here_y = tuple(value[:AGAIN] for value in cells_y)
             faces_x = face(here_x, tuple(down(value) for value in cells_x))
             turned = tuple(pltpu.roll(value, 1, 0) for value in faces_x)
             change_x = tuple(
                 value - jnp.where(row_ids == 0, before, moved)
                 for value, before, moved in zip(faces_x, carry[:3], turned)
             )
-            ground = fields[3][:ROWS]
+            ground = fields[3][:AGAIN]
             ground_up = pltpu.roll(ground, 1, 0)
             slope_x = down(fields[3]) - jnp.where(row_ids == 0, carry[3], ground_up)
             carried = tuple(value[0:1, :] for value in turned) + (ground_up[0:1, :],)
             faces_y = face(here_y, tuple(right_of(value) for value in here_y))
             change_y = tuple(value - left_of(value) for value in faces_y)
             slope_y = right_of(ground) - left_of(ground)
-            old = tuple(value[:ROWS] for value in fields[:3])
+            old = tuple(value[:AGAIN] for value in fields[:3])
             weight = SLOPE * old[0]
             slopes = (
                 SCALE * (change_x[0] + change_y[0]),
@@ -503,7 +504,7 @@
 
         if step == 0:
             wait_all(incoming)
-        lax.fori_loop(0, EARLY // ROWS, group, start)
+        lax.fori_loop(0, EARLY // AGAIN, group, start)
 
 
 def late_rows(tile, late):

time: 102 us -> 121 us (1.19)
  starting transfers between devices: 22.6 us -> 36.1 us
  waiting for transfers between devices: 23.6 us -> 26.7 us
  Pallas kernels: 49.1 us -> 52.1 us
    all_to_all x3, starting transfers between devices: 13.3 us -> 29 us  [spread(): lax.all_to_all(fast, ('xb', 'yb'), split_axis=0, concat_axis=0, tiled=True)]
    ppermute x6, waiting for transfers between devices: 11.6 us -> 26.7 us  [shifted(): return lax.ppermute(value, axis, pairs)]
    all_to_all x3, waiting for transfers between devices: 12 us -> 0.05 us  [spread(): lax.all_to_all(fast, ('xb', 'yb'), split_axis=0, concat_axis=0, tiled=True)]
    ppermute x6, starting transfers between devices: 9.29 us -> 7.09 us  [shifted(): return lax.ppermute(value, axis, pairs)]
    pallas_call x1, Pallas kernels: 5.82 us -> 7.43 us  [body(): call(repeat_first, shape, hbm(), [smem()] + [vmem()] * 3 + [anywhere()] *...]
    pallas_call x1, Pallas kernels: 5.09 us -> 6.64 us  [body(): call(repeat_second, (early_state, late_shape), (anywhere(), vmem()), [sme...]
    unnamed x32 -> x34, local copies, waits for them, and re-layouts: 5.57 us -> 5.31 us
  transfers between devices with their start and end apart: 9 -> 9, of which waited for: 5 -> 3; matrix products, arithmetic and copies ran while one was open for 0% -> 0% of each run, Pallas kernels for 43% -> 35%
where the time goes in v17:
time: 121 us
  Pallas kernels  52.1 us (43%)
  starting transfers between devices  36.1 us (30%)
  waiting for transfers between devices  26.7 us (22%)
  local copies, waits for them, and re-layouts  5.31 us (4%)
    all_to_all x3, starting transfers between devices, spread(): lax.all_to_all(fast, ('xb', 'yb'), split_axis=0, concat_axis=0, tiled=True)  29 us
    ppermute x6, waiting for transfers between devices, shifted(): return lax.ppermute(value, axis, pairs)  26.7 us
    pallas_call x3, Pallas kernels, body(): call(functools.partial(update, step), (shape,) + shapes + (delta_shape,),...  14.5 us
    pallas_call x1, Pallas kernels, body(): call(repeat_first, shape, hbm(), [smem()] + [vmem()] * 3 + [anywhere()] *...  7.43 us
    ppermute x6, starting transfers between devices, shifted(): return lax.ppermute(value, axis, pairs)  7.09 us
    pallas_call x1, Pallas kernels, body(): call(repeat_second, (early_state, late_shape), (anywhere(), vmem()), [sme...  6.64 us
    pallas_call x1, Pallas kernels, body(): call(rates_and_leaving, (shape,) + piece_shapes, (hbm(),) * 3, [smem()] +...  5.99 us
    pallas_call x1, Pallas kernels, body(): call(rates, shape, hbm(), [smem(), hbm(), hbm()], 0, scratch, moved=0)  5.96 us
  transfers between devices with their start and end apart: 9, of which 3 were waited for; matrix products, arithmetic and copies ran while one was open for 0% of the time, Pallas kernels for 35%

profile of v17, /device:TPU:0, one launch (start us, length us, event | category | flops | bytes accessed | tf_op | source)
XLA Modules:
  0.0 120.5 jit_solution(16028478702333612858)
XLA Ops:
  0.0 3.5 %shard_map.64 = (f32[128,384]{1,0:T(8,128)}, f32[8,256]{1,0:T(8,128)}, s32[24]{0:T(128)}, f32[5,80,256]{2,1,0:T(8,128)}, f32[5,64,256]{2,1,0:T(8,128)}) custom-call(f32[2,3,256,256]{3,2,1,0:T(8,128)} %state_first.1, f32[2,256,256]{2,1,0:T(8,128)} %bed_in.7, f32[2,256,256]{2,1,0:T(8,128)} %manning_in.9, s32[4,32]{1,0:T(4,128)} %bitcast.16, s32[3,32]{1,0:T(4,128)} %wet_in.1, ...), custom_call_target="tpu_custom_call" | custom-call | flops 4194304 | bytes 4194304 | tf_op jit(solution)/shard_map/pallas_call | solution.py:816
  3.5 7.4 %all-to-all-start = ((f32[16,8,384]{2,1,0:T(8,128)}), f32[16,8,384]{2,1,0:T(8,128)S(1)}, u32[]{:S(2)}, u32[]{:S(2)}) async-start(f32[16,8,384]{2,1,0:T(8,128)} %bitcast.13), calls=%async_computation | async-start | bytes 393216 | tf_op jit(solution)/shard_map/all_to_all | solution.py:798
  10.9 1.9 %collective-permute-start = (f32[5,80,256]{2,1,0:T(8,128)}, f32[5,80,256]{2,1,0:T(8,128)S(1)}, u32[]{:S(2)}, u32[]{:S(2)}) collective-permute-start(f32[5,80,256]{2,1,0:T(8,128)} %get-tuple-element.33), channel_id=1, source_target_pairs={{0,2},{2,4},{4,6},{6,8},{8,10},{10,12},{12,14},{14,0},{1,3},{3,5},... | collective-permute-start | bytes 1228808 | tf_op jit(solution)/shard_map/ppermute | solution.py:39
  12.9 6.0 %shard_map.65.rate_in.order = f32[2,3,256,256]{3,2,1,0:T(8,128)} custom-call(s32[24]{0:T(128)} %get-tuple-element.27.ctl, f32[2,3,256,256]{3,2,1,0:T(8,128)} %state_first.1, f32[2,256,256]{2,1,0:T(8,128)} %bed_in.7), custom_call_target="tpu_custom_call" | custom-call | tf_op jit(solution)/shard_map/pallas_call | solution.py:845
  18.8 1.5 %collective-permute-start.1 = (f32[5,64,256]{2,1,0:T(8,128)}, f32[5,64,256]{2,1,0:T(8,128)S(1)}, u32[]{:S(2)}, u32[]{:S(2)}) collective-permute-start(f32[5,64,256]{2,1,0:T(8,128)} %shard_map.67), channel_id=1, source_target_pairs={{0,2},{2,4},{4,6},{6,8},{8,10},{10,12},{12,14},{14,0},{1,3},{3,5},... | collective-permute-start | bytes 983048 | tf_op jit(solution)/shard_map/ppermute | solution.py:39
  20.4 0.0 all-to-all-done
  20.4 0.7 copy-done.13
  21.1 4.9 %shard_map.66 = (f32[2,3,256,256]{3,2,1,0:T(8,128)}, f32[128,256]{1,0:T(8,128)}, f32[8,256]{1,0:T(8,128)}, f32[8,256]{1,0:T(8,128)}) custom-call(s32[24]{0:T(128)} %get-tuple-element.27.ctl, f32[128,384]{1,0:T(8,128)} %bitcast.7, f32[128,384]{1,0:T(8,128)} %bitcast.8, f32[8,256]{1,0:T(8,128)} %get-tuple-element.29.columns_in, ...), custom_call_target="tpu_custom_call" | custom-call | flops 8388608 | bytes 14680064 | tf_op jit(solution)/shard_map/pallas_call | solution.py:871
  26.0 16.9 %all-to-all-start.1 = ((f32[16,8,256]{2,1,0:T(8,128)}), f32[16,8,256]{2,1,0:T(8,128)S(1)}, u32[]{:S(2)}, u32[]{:S(2)}) async-start(f32[16,8,256]{2,1,0:T(8,128)} %bitcast.14), calls=%async_computation.1 | async-start | bytes 262144 | tf_op jit(solution)/shard_map/all_to_all | solution.py:798
  42.9 0.7 copy-done.5
  43.6 0.1 copy-done
  43.8 6.0 %shard_map.68 = (f32[2,3,256,256]{3,2,1,0:T(8,128)}, f32[5,80,256]{2,1,0:T(8,128)}, f32[5,64,256]{2,1,0:T(8,128)}) custom-call(s32[24]{0:T(128)} %get-tuple-element.27.ctl, f32[2,3,256,256]{3,2,1,0:T(8,128)} %get-tuple-element.32.state_in, f32[2,256,256]{2,1,0:T(8,128)} %bed_in.7, f32[2,3,256,256]{3,2,1,0:T(8,128)} %state_first.1, ...), custom_call_target="tpu_custom_call" | custom-call | flops 16777216 | bytes 4194304 | tf_op jit(solution)/shard_map/pallas_call | solution.py:853
  49.8 2.0 %collective-permute-start.2 = (f32[5,80,256]{2,1,0:T(8,128)}, f32[5,80,256]{2,1,0:T(8,128)S(1)}, u32[]{:S(2)}, u32[]{:S(2)}) collective-permute-start(f32[5,80,256]{2,1,0:T(8,128)} %get-tuple-element.39), channel_id=1, source_target_pairs={{0,2},{2,4},{4,6},{6,8},{8,10},{10,12},{12,14},{14,0},{1,3},{3,5},... | collective-permute-start | bytes 1228808 | tf_op jit(solution)/shard_map/ppermute | solution.py:39
  51.8 0.7 copy-done.14
  52.4 4.9 %shard_map.69 = (f32[2,3,256,256]{3,2,1,0:T(8,128)}, f32[128,256]{1,0:T(8,128)}, f32[8,256]{1,0:T(8,128)}, f32[8,256]{1,0:T(8,128)}) custom-call(s32[24]{0:T(128)} %get-tuple-element.27.ctl, f32[128,256]{1,0:T(8,128)} %bitcast.11, f32[128,384]{1,0:T(8,128)} %bitcast.9, f32[8,256]{1,0:T(8,128)} %get-tuple-element.31.columns_in, ...), custom_call_target="tpu_custom_call" | custom-call | flops 8388608 | bytes 10485760 | tf_op jit(solution)/shard_map/pallas_call | solution.py:871
  57.3 4.7 %all-to-all-start.2 = ((f32[16,8,256]{2,1,0:T(8,128)}), f32[16,8,256]{2,1,0:T(8,128)S(1)}, u32[]{:S(2)}, u32[]{:S(2)}) async-start(f32[16,8,256]{2,1,0:T(8,128)} %bitcast.15), calls=%async_computation.2 | async-start | bytes 262144 | tf_op jit(solution)/shard_map/all_to_all | solution.py:798
  62.0 2.6 %collective-permute-done.2.order.low = f32[5,80,256]{2,1,0:T(8,128)S(1)} collective-permute-done((f32[5,80,256]{2,1,0:T(8,128)}, f32[5,80,256]{2,1,0:T(8,128)S(1)}, u32[]{:S(2)}, u32[]{:S(2)}) %collective-permute-start.2) | collective-permute-done | bytes 409632 | tf_op jit(solution)/shard_map/ppermute | solution.py:39
  64.6 0.8 copy-done.2
  65.3 6.0 %shard_map.70.rate_in = f32[2,3,256,256]{3,2,1,0:T(8,128)} custom-call(s32[24]{0:T(128)} %get-tuple-element.27.ctl, f32[2,3,256,256]{3,2,1,0:T(8,128)} %get-tuple-element.38.state_in, f32[2,256,256]{2,1,0:T(8,128)} %bed_in.7, f32[5,80,256]{2,1,0:T(8,128)} %copy-done.2), custom_call_target="tpu_custom_call" | custom-call | flops 16777216 | bytes 4194304 | tf_op jit(solution)/shard_map/pallas_call | solution.py:863
  71.3 0.6 copy-done.15
  72.0 4.8 %shard_map.71 = (f32[2,3,256,256]{3,2,1,0:T(8,128)}, f32[3,128,256]{2,1,0:T(8,128)}, f32[3,128,256]{2,1,0:T(8,128)}, f32[8,256]{1,0:T(8,128)}) custom-call(s32[24]{0:T(128)} %get-tuple-element.27.ctl, f32[128,256]{1,0:T(8,128)} %bitcast.12, f32[128,384]{1,0:T(8,128)} %bitcast.10, f32[8,256]{1,0:T(8,128)} %get-tuple-element.37.columns_in, ...), custom_call_target="tpu_custom_call" | custom-call | flops 8388608 | bytes 10485760 | tf_op jit(solution)/shard_map/pallas_call | solution.py:871
  76.7 0.1 collective-permute-start.3
  76.8 1.6 %collective-permute-start.4 = (f32[5,64,256]{2,1,0:T(8,128)S(1)}, f32[5,64,256]{2,1,0:T(8,128)S(1)}, u32[]{:S(2)}, u32[]{:S(2)}) collective-permute-start(f32[5,64,256]{2,1,0:T(8,128)S(1)} %copy-done.16), channel_id=1, source_target_pairs={{0,2},{2,4},{4,6},{6,8},{8,10},{10,12},{12,14},{14,0},{1,3},{3,5},... | collective-permute-start | bytes 983048 | tf_op jit(solution)/shard_map/ppermute | solution.py:39
  78.4 19.1 %collective-permute-done.4.high = f32[5,64,256]{2,1,0:T(8,128)S(1)} collective-permute-done((f32[5,64,256]{2,1,0:T(8,128)S(1)}, f32[5,64,256]{2,1,0:T(8,128)S(1)}, u32[]{:S(2)}, u32[]{:S(2)}) %collective-permute-start.4) | collective-permute-done | bytes 327712 | tf_op jit(solution)/shard_map/ppermute | solution.py:39
  97.5 1.0 copy-done.7
  98.5 0.7 copy-done.11
  99.2 6.6 %shard_map.72 = (f32[3,144,256]{2,1,0:T(8,128)S(1)}, f32[3,128,256]{2,1,0:T(8,128)S(1)}) custom-call(s32[24]{0:T(128)S(1)} %copy-done.8, f32[8,256]{1,0:T(8,128)S(1)} %copy-done.9, f32[8,256]{1,0:T(8,128)S(1)} %copy-done.10, f32[8,256]{1,0:T(8,128)S(1)} %copy-done.11, f32[5,80,256]{2,1,0:T(8,128)S(1)} %copy-done.3, ...), custom_call_target="tpu_custom_call" | custom-call | flops 8388608 | bytes 4194304 | tf_op jit(solution)/shard_map/pallas_call | solution.py:897
  105.8 0.6 shard_map.73
  106.4 0.1 collective-permute-start.5
  106.5 7.4 %shard_map.74.before = f32[2,3,256,256]{3,2,1,0:T(8,128)} custom-call(s32[24]{0:T(128)S(1)} %copy-done.8, f32[8,256]{1,0:T(8,128)S(1)} %copy-done.9, f32[8,256]{1,0:T(8,128)S(1)} %copy-done.10, f32[8,256]{1,0:T(8,128)S(1)} %copy-done.12, f32[5,80,256]{2,1,0:T(8,128)S(1)} %copy-done.1, f32[5,64,256]{2,1,0:T(8,128)S(1)} %copy-done.6, ...), custom_call_target="tpu_custom_call" | custom-call | flops 8388608 | bytes 4194304 | tf_op jit(solution)/shard_map/pallas_call | solution.py:915
  114.0 5.0 %collective-permute-done.5.late = f32[3,128,256]{2,1,0:T(8,128)S(1)} collective-permute-done((f32[3,128,256]{2,1,0:T(8,128)S(1)}, f32[3,128,256]{2,1,0:T(8,128)S(1)}, u32[]{:S(2)}, u32[]{:S(2)}) %collective-permute-start.5) | collective-permute-done | bytes 393248 | tf_op jit(solution)/shard_map/ppermute | solution.py:39
  119.0 1.5 %shard_map.75 = f32[2,3,256,256]{3,2,1,0:T(8,128)} custom-call(s32[24]{0:T(128)S(1)} %copy-done.8, f32[3,128,256]{2,1,0:T(8,128)S(1)} %collective-permute-done.5.late, f32[3,144,256]{2,1,0:T(8,128)S(1)} %get-tuple-element.47.order.early, f32[2,3,256,256]{3,2,1,0:T(8,128)} %shard_map.74.before), custom_call_target="tpu_custom_call", output_to_operand_aliasing={{}: (3, {})} | custom-call | flops 1048576 | bytes 4194304 | tf_op jit(solution)/shard_map/pallas_call | solution.py:930
  (32 shorter events, 0.1 us)
Async XLA Ops:
  3.5 16.9 %all-to-all-start = ((f32[16,8,384]{2,1,0:T(8,128)}), f32[16,8,384]{2,1,0:T(8,128)S(1)}, u32[]{:S(2)}, u32[]{:S(2)}) async-start(f32[16,8,384]{2,1,0:T(8,128)} %bitcast.13), calls=%async_computation | async-start | bytes 393216 | tf_op jit(solution)/shard_map/all_to_all | solution.py:798
  10.9 32.0 %collective-permute-start = (f32[5,80,256]{2,1,0:T(8,128)}, f32[5,80,256]{2,1,0:T(8,128)S(1)}, u32[]{:S(2)}, u32[]{:S(2)}) collective-permute-start(f32[5,80,256]{2,1,0:T(8,128)} %get-tuple-element.33), channel_id=1, source_target_pairs={{0,2},{2,4},{4,6},{6,8},{8,10},{10,12},{12,14},{14,0},{1,3},{3,5},... | collective-permute-start | bytes 1228808 | tf_op jit(solution)/shard_map/ppermute | solution.py:39
  18.8 24.0 %collective-permute-start.1 = (f32[5,64,256]{2,1,0:T(8,128)}, f32[5,64,256]{2,1,0:T(8,128)S(1)}, u32[]{:S(2)}, u32[]{:S(2)}) collective-permute-start(f32[5,64,256]{2,1,0:T(8,128)} %shard_map.67), channel_id=1, source_target_pairs={{0,2},{2,4},{4,6},{6,8},{8,10},{10,12},{12,14},{14,0},{1,3},{3,5},... | collective-permute-start | bytes 983048 | tf_op jit(solution)/shard_map/ppermute | solution.py:39
  20.4 0.7 copy-start.13
  26.0 25.8 %all-to-all-start.1 = ((f32[16,8,256]{2,1,0:T(8,128)}), f32[16,8,256]{2,1,0:T(8,128)S(1)}, u32[]{:S(2)}, u32[]{:S(2)}) async-start(f32[16,8,256]{2,1,0:T(8,128)} %bitcast.14), calls=%async_computation.1 | async-start | bytes 262144 | tf_op jit(solution)/shard_map/all_to_all | solution.py:798
  42.9 0.7 copy-start.5
  42.9 0.9 copy-start
  49.8 14.8 %collective-permute-start.2 = (f32[5,80,256]{2,1,0:T(8,128)}, f32[5,80,256]{2,1,0:T(8,128)S(1)}, u32[]{:S(2)}, u32[]{:S(2)}) collective-permute-start(f32[5,80,256]{2,1,0:T(8,128)} %get-tuple-element.39), channel_id=1, source_target_pairs={{0,2},{2,4},{4,6},{6,8},{8,10},{10,12},{12,14},{14,0},{1,3},{3,5},... | collective-permute-start | bytes 1228808 | tf_op jit(solution)/shard_map/ppermute | solution.py:39
  51.8 0.7 copy-start.14
  57.3 14.0 %all-to-all-start.2 = ((f32[16,8,256]{2,1,0:T(8,128)}), f32[16,8,256]{2,1,0:T(8,128)S(1)}, u32[]{:S(2)}, u32[]{:S(2)}) async-start(f32[16,8,256]{2,1,0:T(8,128)} %bitcast.15), calls=%async_computation.2 | async-start | bytes 262144 | tf_op jit(solution)/shard_map/all_to_all | solution.py:798
  64.6 0.8 copy-start.2
  71.3 0.7 copy-start.15
  71.9 4.9 %copy-start.16 = (f32[5,64,256]{2,1,0:T(8,128)S(1)}, f32[5,64,256]{2,1,0:T(8,128)}, u32[]{:S(2)}) copy-start(f32[5,64,256]{2,1,0:T(8,128)} %get-tuple-element.44) | copy-start | bytes 983044
  71.9 25.5 %copy-start.3 = (f32[5,80,256]{2,1,0:T(8,128)S(1)}, f32[5,80,256]{2,1,0:T(8,128)}, u32[]{:S(2)}) copy-start(f32[5,80,256]{2,1,0:T(8,128)} %copy-done.2) | copy-start | bytes 1228804
  71.9 25.5 %copy-start.8 = (s32[24]{0:T(128)S(1)}, s32[24]{0:T(128)}, u32[]{:S(2)}) copy-start(s32[24]{0:T(128)} %get-tuple-element.27.ctl) | copy-start | bytes 292
  71.9 25.5 %copy-start.9 = (f32[8,256]{1,0:T(8,128)S(1)}, f32[8,256]{1,0:T(8,128)}, u32[]{:S(2)}) copy-start(f32[8,256]{1,0:T(8,128)} %get-tuple-element.41.delta0) | copy-start | bytes 24580
  71.9 25.5 %copy-start.10 = (f32[8,256]{1,0:T(8,128)S(1)}, f32[8,256]{1,0:T(8,128)}, u32[]{:S(2)}) copy-start(f32[8,256]{1,0:T(8,128)} %get-tuple-element.42.delta1) | copy-start | bytes 24580
  76.7 29.8 %copy-start.1 = (f32[5,80,256]{2,1,0:T(8,128)S(1)}, f32[5,80,256]{2,1,0:T(8,128)}, u32[]{:S(2)}) copy-start(f32[5,80,256]{2,1,0:T(8,128)} %copy-done) | copy-start | bytes 1228804
  76.7 29.8 %copy-start.4 = (f32[2,3,256,256]{3,2,1,0:T(8,128)S(1)}, f32[2,3,256,256]{3,2,1,0:T(8,128)}, u32[]{:S(2)}) copy-start(f32[2,3,256,256]{3,2,1,0:T(8,128)} %get-tuple-element.48.state) | copy-start | bytes 4718596
  76.7 29.8 %copy-start.6 = (f32[5,64,256]{2,1,0:T(8,128)S(1)}, f32[5,64,256]{2,1,0:T(8,128)}, u32[]{:S(2)}) copy-start(f32[5,64,256]{2,1,0:T(8,128)} %copy-done.5) | copy-start | bytes 983044
  76.7 29.1 %collective-permute-start.3 = (f32[3,128,256]{2,1,0:T(8,128)}, f32[3,128,256]{2,1,0:T(8,128)S(1)}, u32[]{:S(2)}, u32[]{:S(2)}) collective-permute-start(f32[3,128,256]{2,1,0:T(8,128)} %get-tuple-element.40), channel_id=1, source_target_pairs={{0,2},{2,4},{4,6},{6,8},{8,10},{10,12},{12,14},{14,0},{1,3},{3,5},... | collective-permute-start | bytes 1179656 | tf_op jit(solution)/shard_map/ppermute | solution.py:39
  76.8 20.6 %collective-permute-start.4 = (f32[5,64,256]{2,1,0:T(8,128)S(1)}, f32[5,64,256]{2,1,0:T(8,128)S(1)}, u32[]{:S(2)}, u32[]{:S(2)}) collective-permute-start(f32[5,64,256]{2,1,0:T(8,128)S(1)} %copy-done.16), channel_id=1, source_target_pairs={{0,2},{2,4},{4,6},{6,8},{8,10},{10,12},{12,14},{14,0},{1,3},{3,5},... | collective-permute-start | bytes 983048 | tf_op jit(solution)/shard_map/ppermute | solution.py:39
  97.5 1.0 copy-start.7
  98.5 0.7 copy-start.11
  99.2 7.3 %copy-start.12 = (f32[8,256]{1,0:T(8,128)S(1)}, f32[8,256]{1,0:T(8,128)}, u32[]{:S(2)}) copy-start(f32[8,256]{1,0:T(8,128)} %get-tuple-element.43.delta2) | copy-start | bytes 24580
  106.4 12.6 %collective-permute-start.5 = (f32[3,128,256]{2,1,0:T(8,128)S(1)}, f32[3,128,256]{2,1,0:T(8,128)S(1)}, u32[]{:S(2)}, u32[]{:S(2)}) collective-permute-start(f32[3,128,256]{2,1,0:T(8,128)S(1)} %shard_map.73), channel_id=1, source_target_pairs={{0,2},{2,4},{4,6},{6,8},{8,10},{10,12},{12,14},{14,0},{1,3},{3,5},... | collective-permute-start | bytes 1179656 | tf_op jit(solution)/shard_map/ppermute | solution.py:39

commit v18 on v16

--- a/solution.py
+++ b/solution.py
@@ -218,8 +218,8 @@
     wait_all(early)
 
 
-def hold(order, leaving, same):
-    del order, leaving, same
+def hold(first, second, leaving, same):
+    del first, second, leaving, same
 
 
 class Passing:
@@ -845,8 +845,8 @@
                 ctl, state, bed
             )
             leaving[1] = call(
-                hold, piece_shapes[1], hbm(), [hbm(), hbm()], 1 << 10, aliases={1: 0}
-            )(rate, leaving[1])
+                hold, piece_shapes[1], hbm(), [hbm()] * 3, 1 << 10, aliases={2: 0}
+            )(rate, got, leaving[1])
             early_first = [shifted(piece, "xb", 1) for piece in leaving]
         elif step == 1:
             rate, *leaving = call(

time: 102 us -> 107 us (1.049)
  starting transfers between devices: 22.6 us -> 38 us
  waiting for transfers between devices: 23.6 us -> 13.8 us
    all_to_all x3, starting transfers between devices: 13.3 us -> 31.8 us  [spread(): lax.all_to_all(fast, ('xb', 'yb'), split_axis=0, concat_axis=0, tiled=True)]
    all_to_all x3, waiting for transfers between devices: 12 us -> 1.57 us  [spread(): lax.all_to_all(fast, ('xb', 'yb'), split_axis=0, concat_axis=0, tiled=True)]
    ppermute x6, starting transfers between devices: 9.29 us -> 6.21 us  [shifted(): return lax.ppermute(value, axis, pairs)]
  transfers between devices with their start and end apart: 9 -> 9, of which waited for: 5 -> 5; matrix products, arithmetic and copies ran while one was open for 0% -> 0% of each run, Pallas kernels for 43% -> 41%
where the time goes in v18:
time: 107 us
  Pallas kernels  49.1 us (46%)
  starting transfers between devices  38 us (36%)
  waiting for transfers between devices  13.8 us (13%)
  local copies, waits for them, and re-layouts  5.56 us (5%)
    all_to_all x3, starting transfers between devices, spread(): lax.all_to_all(fast, ('xb', 'yb'), split_axis=0, concat_axis=0, tiled=True)  31.8 us
    pallas_call x3, Pallas kernels, body(): call(functools.partial(update, step), (shape,) + shapes + (delta_shape,),...  14.6 us
    ppermute x6, waiting for transfers between devices, shifted(): return lax.ppermute(value, axis, pairs)  12.2 us
    ppermute x6, starting transfers between devices, shifted(): return lax.ppermute(value, axis, pairs)  6.21 us
    pallas_call x1, Pallas kernels, body(): call(rates_and_leaving, (shape,) + piece_shapes, (hbm(),) * 3, [smem()] +...  5.99 us
    pallas_call x1, Pallas kernels, body(): call(rates, shape, hbm(), [smem(), hbm(), hbm()], 0, scratch, moved=0)  5.96 us
    pallas_call x1, Pallas kernels, body(): call(rates_after, shape, hbm(), [smem()] + [hbm()] * 3, 16 << 20, scratch)  5.96 us
    pallas_call x1, Pallas kernels, body(): call(repeat_first, shape, hbm(), [smem()] + [vmem()] * 3 + [anywhere()] *...  5.82 us
  transfers between devices with their start and end apart: 9, of which 5 were waited for; matrix products, arithmetic and copies ran while one was open for 0% of the time, Pallas kernels for 41%

profile of v18, /device:TPU:0, one launch (start us, length us, event | category | flops | bytes accessed | tf_op | source)
XLA Modules:
  0.0 106.8 jit_solution(1280960313073479238)
XLA Ops:
  0.0 3.6 %shard_map.64 = (f32[128,384]{1,0:T(8,128)}, f32[8,256]{1,0:T(8,128)}, s32[24]{0:T(128)}, f32[5,88,256]{2,1,0:T(8,128)}, f32[5,72,256]{2,1,0:T(8,128)}) custom-call(f32[2,3,256,256]{3,2,1,0:T(8,128)} %state_first.1, f32[2,256,256]{2,1,0:T(8,128)} %bed_in.7, f32[2,256,256]{2,1,0:T(8,128)} %manning_in.9, s32[4,32]{1,0:T(4,128)} %bitcast.17, s32[3,32]{1,0:T(4,128)} %wet_in.1, ...), custom_call_target="tpu_custom_call" | custom-call | flops 4194304 | bytes 4194304 | tf_op jit(solution)/shard_map/pallas_call | solution.py:815
  3.6 7.4 %all-to-all-start = ((f32[16,8,384]{2,1,0:T(8,128)}), f32[16,8,384]{2,1,0:T(8,128)S(1)}, u32[]{:S(2)}, u32[]{:S(2)}) async-start(f32[16,8,384]{2,1,0:T(8,128)} %bitcast.14), calls=%async_computation | async-start | bytes 393216 | tf_op jit(solution)/shard_map/all_to_all | solution.py:797
  11.0 1.9 %collective-permute-start = (f32[5,88,256]{2,1,0:T(8,128)}, f32[5,88,256]{2,1,0:T(8,128)S(1)}, u32[]{:S(2)}, u32[]{:S(2)}) collective-permute-start(f32[5,88,256]{2,1,0:T(8,128)} %get-tuple-element.33), channel_id=1, source_target_pairs={{0,2},{2,4},{4,6},{6,8},{8,10},{10,12},{12,14},{14,0},{1,3},{3,5},... | collective-permute-start | bytes 1351688 | tf_op jit(solution)/shard_map/ppermute | solution.py:38
  12.9 6.0 %shard_map.65.rate_in.first = f32[2,3,256,256]{3,2,1,0:T(8,128)} custom-call(s32[24]{0:T(128)} %get-tuple-element.27.ctl, f32[2,3,256,256]{3,2,1,0:T(8,128)} %state_first.1, f32[2,256,256]{2,1,0:T(8,128)} %bed_in.7), custom_call_target="tpu_custom_call" | custom-call | tf_op jit(solution)/shard_map/pallas_call | solution.py:844
  18.9 1.6 %all-to-all-done = f32[16,8,384]{2,1,0:T(8,128)S(1)} async-done(((f32[16,8,384]{2,1,0:T(8,128)}), f32[16,8,384]{2,1,0:T(8,128)S(1)}, u32[]{:S(2)}, u32[]{:S(2)}) %all-to-all-start) | async-done | bytes 196640 | tf_op jit(solution)/shard_map/all_to_all | solution.py:797
  20.4 0.7 copy-done.12
  21.1 4.9 %shard_map.66 = (f32[2,3,256,256]{3,2,1,0:T(8,128)}, f32[128,256]{1,0:T(8,128)}, f32[8,256]{1,0:T(8,128)}, f32[8,256]{1,0:T(8,128)}) custom-call(s32[24]{0:T(128)} %get-tuple-element.27.ctl, f32[128,384]{1,0:T(8,128)} %bitcast.8, f32[128,384]{1,0:T(8,128)} %bitcast.9, f32[8,256]{1,0:T(8,128)} %get-tuple-element.29.columns_in, ...), custom_call_target="tpu_custom_call" | custom-call | flops 8388608 | bytes 14680064 | tf_op jit(solution)/shard_map/pallas_call | solution.py:870
  26.0 19.7 %all-to-all-start.1 = ((f32[16,8,256]{2,1,0:T(8,128)}), f32[16,8,256]{2,1,0:T(8,128)S(1)}, u32[]{:S(2)}, u32[]{:S(2)}) async-start(f32[16,8,256]{2,1,0:T(8,128)} %bitcast.15), calls=%async_computation.1 | async-start | bytes 262144 | tf_op jit(solution)/shard_map/all_to_all | solution.py:797
  45.8 0.8 copy-done.2
  46.5 0.1 copy-done.5
  46.7 6.0 %shard_map.68 = (f32[2,3,256,256]{3,2,1,0:T(8,128)}, f32[5,88,256]{2,1,0:T(8,128)}, f32[5,72,256]{2,1,0:T(8,128)}) custom-call(s32[24]{0:T(128)} %get-tuple-element.27.ctl, f32[2,3,256,256]{3,2,1,0:T(8,128)} %get-tuple-element.32.state_in, f32[2,256,256]{2,1,0:T(8,128)} %bed_in.7, f32[2,3,256,256]{3,2,1,0:T(8,128)} %state_first.1, ...), custom_call_target="tpu_custom_call" | custom-call | flops 16777216 | bytes 4194304 | tf_op jit(solution)/shard_map/pallas_call | solution.py:852
  52.7 2.0 %collective-permute-start.2 = (f32[5,88,256]{2,1,0:T(8,128)}, f32[5,88,256]{2,1,0:T(8,128)S(1)}, u32[]{:S(2)}, u32[]{:S(2)}) collective-permute-start(f32[5,88,256]{2,1,0:T(8,128)} %get-tuple-element.39), channel_id=1, source_target_pairs={{0,2},{2,4},{4,6},{6,8},{8,10},{10,12},{12,14},{14,0},{1,3},{3,5},... | collective-permute-start | bytes 1351688 | tf_op jit(solution)/shard_map/ppermute | solution.py:38
  54.7 0.7 copy-done.13
  55.3 5.0 %shard_map.69 = (f32[2,3,256,256]{3,2,1,0:T(8,128)}, f32[128,256]{1,0:T(8,128)}, f32[8,256]{1,0:T(8,128)}, f32[8,256]{1,0:T(8,128)}) custom-call(s32[24]{0:T(128)} %get-tuple-element.27.ctl, f32[128,256]{1,0:T(8,128)} %bitcast.12, f32[128,384]{1,0:T(8,128)} %bitcast.10, f32[8,256]{1,0:T(8,128)} %get-tuple-element.31.columns_in, ...), custom_call_target="tpu_custom_call" | custom-call | flops 8388608 | bytes 10485760 | tf_op jit(solution)/shard_map/pallas_call | solution.py:870
  60.3 4.7 %all-to-all-start.2 = ((f32[16,8,256]{2,1,0:T(8,128)}), f32[16,8,256]{2,1,0:T(8,128)S(1)}, u32[]{:S(2)}, u32[]{:S(2)}) async-start(f32[16,8,256]{2,1,0:T(8,128)} %bitcast.16), calls=%async_computation.2 | async-start | bytes 262144 | tf_op jit(solution)/shard_map/all_to_all | solution.py:797
  65.1 2.0 %collective-permute-start.4 = (f32[5,72,256]{2,1,0:T(8,128)S(1)}, f32[5,72,256]{2,1,0:T(8,128)S(1)}, u32[]{:S(2)}, u32[]{:S(2)}) collective-permute-start(f32[5,72,256]{2,1,0:T(8,128)S(1)} %copy-done.15), channel_id=1, source_target_pairs={{0,2},{2,4},{4,6},{6,8},{8,10},{10,12},{12,14},{14,0},{1,3},{3,5},... | collective-permute-start | bytes 1105928 | tf_op jit(solution)/shard_map/ppermute | solution.py:38
  67.0 1.3 %collective-permute-done.2.order.low = f32[5,88,256]{2,1,0:T(8,128)S(1)} collective-permute-done((f32[5,88,256]{2,1,0:T(8,128)}, f32[5,88,256]{2,1,0:T(8,128)S(1)}, u32[]{:S(2)}, u32[]{:S(2)}) %collective-permute-start.2) | collective-permute-done | bytes 450592 | tf_op jit(solution)/shard_map/ppermute | solution.py:38
  68.3 0.8 copy-done
  69.1 6.0 %shard_map.70.rate_in = f32[2,3,256,256]{3,2,1,0:T(8,128)} custom-call(s32[24]{0:T(128)} %get-tuple-element.27.ctl, f32[2,3,256,256]{3,2,1,0:T(8,128)} %get-tuple-element.38.state_in, f32[2,256,256]{2,1,0:T(8,128)} %bed_in.7, f32[5,88,256]{2,1,0:T(8,128)} %copy-done), custom_call_target="tpu_custom_call" | custom-call | flops 16777216 | bytes 4194304 | tf_op jit(solution)/shard_map/pallas_call | solution.py:862
  75.1 0.7 copy-done.14
  75.8 4.7 %shard_map.71 = (f32[2,3,256,256]{3,2,1,0:T(8,128)}, f32[3,112,256]{2,1,0:T(8,128)}, f32[3,112,256]{2,1,0:T(8,128)}, f32[8,256]{1,0:T(8,128)}) custom-call(s32[24]{0:T(128)} %get-tuple-element.27.ctl, f32[128,256]{1,0:T(8,128)} %bitcast.13, f32[128,384]{1,0:T(8,128)} %bitcast.11, f32[8,256]{1,0:T(8,128)} %get-tuple-element.37.columns_in, ...), custom_call_target="tpu_custom_call" | custom-call | flops 8388608 | bytes 10485760 | tf_op jit(solution)/shard_map/pallas_call | solution.py:870
  80.5 0.3 collective-permute-start.3
  80.8 0.1 collective-permute-done.4.high
  80.9 1.2 %copy-done.7 = f32[3,112,256]{2,1,0:T(8,128)S(1)} copy-done((f32[3,112,256]{2,1,0:T(8,128)S(1)}, f32[3,112,256]{2,1,0:T(8,128)}, u32[]{:S(2)}) %copy-start.7) | copy-done | bytes 344088
  82.1 0.7 copy-done.11
  82.8 5.1 %shard_map.72 = (f32[3,160,256]{2,1,0:T(8,128)S(1)}, f32[3,112,256]{2,1,0:T(8,128)S(1)}) custom-call(s32[24]{0:T(128)S(1)} %copy-done.8, f32[8,256]{1,0:T(8,128)S(1)} %copy-done.9, f32[8,256]{1,0:T(8,128)S(1)} %copy-done.10, f32[8,256]{1,0:T(8,128)S(1)} %copy-done.11, f32[5,88,256]{2,1,0:T(8,128)S(1)} %copy-done.1, ...), custom_call_target="tpu_custom_call" | custom-call | flops 8388608 | bytes 4194304 | tf_op jit(solution)/shard_map/pallas_call | solution.py:896
  87.9 5.3 %collective-permute-done.3.arrived.late_in = f32[3,112,256]{2,1,0:T(8,128)S(1)} collective-permute-done((f32[3,112,256]{2,1,0:T(8,128)}, f32[3,112,256]{2,1,0:T(8,128)S(1)}, u32[]{:S(2)}, u32[]{:S(2)}) %collective-permute-start.3) | collective-permute-done | bytes 344096 | tf_op jit(solution)/shard_map/ppermute | solution.py:38
  93.1 0.6 shard_map.73
  93.7 0.1 collective-permute-start.5
  93.8 5.8 %shard_map.74.before = f32[2,3,256,256]{3,2,1,0:T(8,128)} custom-call(s32[24]{0:T(128)S(1)} %copy-done.8, f32[8,256]{1,0:T(8,128)S(1)} %copy-done.9, f32[8,256]{1,0:T(8,128)S(1)} %copy-done.10, f32[8,256]{1,0:T(8,128)S(1)} %copy-done.11, f32[5,88,256]{2,1,0:T(8,128)S(1)} %copy-done.3, f32[5,72,256]{2,1,0:T(8,128)S(1)} %copy-done.6, ...), custom_call_target="tpu_custom_call" | custom-call | flops 8388608 | bytes 4194304 | tf_op jit(solution)/shard_map/pallas_call | solution.py:914
  99.7 5.6 %collective-permute-done.5.late = f32[3,112,256]{2,1,0:T(8,128)S(1)} collective-permute-done((f32[3,112,256]{2,1,0:T(8,128)S(1)}, f32[3,112,256]{2,1,0:T(8,128)S(1)}, u32[]{:S(2)}, u32[]{:S(2)}) %collective-permute-start.5) | collective-permute-done | bytes 344096 | tf_op jit(solution)/shard_map/ppermute | solution.py:38
  105.2 1.5 %shard_map.75 = f32[2,3,256,256]{3,2,1,0:T(8,128)} custom-call(s32[24]{0:T(128)S(1)} %copy-done.8, f32[3,112,256]{2,1,0:T(8,128)S(1)} %collective-permute-done.5.late, f32[3,160,256]{2,1,0:T(8,128)S(1)} %get-tuple-element.47.order.early, f32[2,3,256,256]{3,2,1,0:T(8,128)} %shard_map.74.before), custom_call_target="tpu_custom_call", output_to_operand_aliasing={{}: (3, {})} | custom-call | flops 1048576 | bytes 4194304 | tf_op jit(solution)/shard_map/pallas_call | solution.py:929
  (30 shorter events, 0.1 us)
Async XLA Ops:
  3.6 16.9 %all-to-all-start = ((f32[16,8,384]{2,1,0:T(8,128)}), f32[16,8,384]{2,1,0:T(8,128)S(1)}, u32[]{:S(2)}, u32[]{:S(2)}) async-start(f32[16,8,384]{2,1,0:T(8,128)} %bitcast.14), calls=%async_computation | async-start | bytes 393216 | tf_op jit(solution)/shard_map/all_to_all | solution.py:797
  11.0 34.8 %collective-permute-start = (f32[5,88,256]{2,1,0:T(8,128)}, f32[5,88,256]{2,1,0:T(8,128)S(1)}, u32[]{:S(2)}, u32[]{:S(2)}) collective-permute-start(f32[5,88,256]{2,1,0:T(8,128)} %get-tuple-element.33), channel_id=1, source_target_pairs={{0,2},{2,4},{4,6},{6,8},{8,10},{10,12},{12,14},{14,0},{1,3},{3,5},... | collective-permute-start | bytes 1351688 | tf_op jit(solution)/shard_map/ppermute | solution.py:38
  20.4 0.7 copy-start.12
  21.1 24.7 %collective-permute-start.1 = (f32[5,72,256]{2,1,0:T(8,128)}, f32[5,72,256]{2,1,0:T(8,128)S(1)}, u32[]{:S(2)}, u32[]{:S(2)}) collective-permute-start(f32[5,72,256]{2,1,0:T(8,128)} %shard_map.67), channel_id=1, source_target_pairs={{0,2},{2,4},{4,6},{6,8},{8,10},{10,12},{12,14},{14,0},{1,3},{3,5},... | collective-permute-start | bytes 1105928 | tf_op jit(solution)/shard_map/ppermute | solution.py:38
  26.0 28.6 %all-to-all-start.1 = ((f32[16,8,256]{2,1,0:T(8,128)}), f32[16,8,256]{2,1,0:T(8,128)S(1)}, u32[]{:S(2)}, u32[]{:S(2)}) async-start(f32[16,8,256]{2,1,0:T(8,128)} %bitcast.15), calls=%async_computation.1 | async-start | bytes 262144 | tf_op jit(solution)/shard_map/all_to_all | solution.py:797
  45.8 0.8 copy-start.2
  45.8 0.9 copy-start.5
  52.7 15.6 %collective-permute-start.2 = (f32[5,88,256]{2,1,0:T(8,128)}, f32[5,88,256]{2,1,0:T(8,128)S(1)}, u32[]{:S(2)}, u32[]{:S(2)}) collective-permute-start(f32[5,88,256]{2,1,0:T(8,128)} %get-tuple-element.39), channel_id=1, source_target_pairs={{0,2},{2,4},{4,6},{6,8},{8,10},{10,12},{12,14},{14,0},{1,3},{3,5},... | collective-permute-start | bytes 1351688 | tf_op jit(solution)/shard_map/ppermute | solution.py:38
  54.7 0.7 copy-start.13
  55.3 9.7 %copy-start.15 = (f32[5,72,256]{2,1,0:T(8,128)S(1)}, f32[5,72,256]{2,1,0:T(8,128)}, u32[]{:S(2)}) copy-start(f32[5,72,256]{2,1,0:T(8,128)} %get-tuple-element.44) | copy-start | bytes 1105924
  60.3 14.7 %all-to-all-start.2 = ((f32[16,8,256]{2,1,0:T(8,128)}), f32[16,8,256]{2,1,0:T(8,128)S(1)}, u32[]{:S(2)}, u32[]{:S(2)}) async-start(f32[16,8,256]{2,1,0:T(8,128)} %bitcast.16), calls=%async_computation.2 | async-start | bytes 262144 | tf_op jit(solution)/shard_map/all_to_all | solution.py:797
  65.1 15.8 %collective-permute-start.4 = (f32[5,72,256]{2,1,0:T(8,128)S(1)}, f32[5,72,256]{2,1,0:T(8,128)S(1)}, u32[]{:S(2)}, u32[]{:S(2)}) collective-permute-start(f32[5,72,256]{2,1,0:T(8,128)S(1)} %copy-done.15), channel_id=1, source_target_pairs={{0,2},{2,4},{4,6},{6,8},{8,10},{10,12},{12,14},{14,0},{1,3},{3,5},... | collective-permute-start | bytes 1105928 | tf_op jit(solution)/shard_map/ppermute | solution.py:38
  68.3 0.8 copy-start
  75.1 0.7 copy-start.14
  75.7 5.1 %copy-start.1 = (f32[5,88,256]{2,1,0:T(8,128)S(1)}, f32[5,88,256]{2,1,0:T(8,128)}, u32[]{:S(2)}) copy-start(f32[5,88,256]{2,1,0:T(8,128)} %copy-done) | copy-start | bytes 1351684
  75.7 5.1 %copy-start.8 = (s32[24]{0:T(128)S(1)}, s32[24]{0:T(128)}, u32[]{:S(2)}) copy-start(s32[24]{0:T(128)} %get-tuple-element.27.ctl) | copy-start | bytes 292
  75.7 5.1 %copy-start.9 = (f32[8,256]{1,0:T(8,128)S(1)}, f32[8,256]{1,0:T(8,128)}, u32[]{:S(2)}) copy-start(f32[8,256]{1,0:T(8,128)} %get-tuple-element.41.delta0) | copy-start | bytes 24580
  75.7 5.1 %copy-start.10 = (f32[8,256]{1,0:T(8,128)S(1)}, f32[8,256]{1,0:T(8,128)}, u32[]{:S(2)}) copy-start(f32[8,256]{1,0:T(8,128)} %get-tuple-element.42.delta1) | copy-start | bytes 24580
  80.5 13.3 %copy-start.3 = (f32[5,88,256]{2,1,0:T(8,128)S(1)}, f32[5,88,256]{2,1,0:T(8,128)}, u32[]{:S(2)}) copy-start(f32[5,88,256]{2,1,0:T(8,128)} %copy-done.2) | copy-start | bytes 1351684
  80.5 13.3 %copy-start.4 = (f32[2,3,256,256]{3,2,1,0:T(8,128)S(1)}, f32[2,3,256,256]{3,2,1,0:T(8,128)}, u32[]{:S(2)}) copy-start(f32[2,3,256,256]{3,2,1,0:T(8,128)} %get-tuple-element.48.state) | copy-start | bytes 4718596
  80.5 13.3 %copy-start.6 = (f32[5,72,256]{2,1,0:T(8,128)S(1)}, f32[5,72,256]{2,1,0:T(8,128)}, u32[]{:S(2)}) copy-start(f32[5,72,256]{2,1,0:T(8,128)} %copy-done.5) | copy-start | bytes 1105924
  80.5 12.6 %collective-permute-start.3 = (f32[3,112,256]{2,1,0:T(8,128)}, f32[3,112,256]{2,1,0:T(8,128)S(1)}, u32[]{:S(2)}, u32[]{:S(2)}) collective-permute-start(f32[3,112,256]{2,1,0:T(8,128)} %get-tuple-element.40), channel_id=1, source_target_pairs={{0,2},{2,4},{4,6},{6,8},{8,10},{10,12},{12,14},{14,0},{1,3},{3,5},... | collective-permute-start | bytes 1032200 | tf_op jit(solution)/shard_map/ppermute | solution.py:38
  80.9 1.2 %copy-start.7 = (f32[3,112,256]{2,1,0:T(8,128)S(1)}, f32[3,112,256]{2,1,0:T(8,128)}, u32[]{:S(2)}) copy-start(f32[3,112,256]{2,1,0:T(8,128)} %get-tuple-element.45.late) | copy-start | bytes 1032196
  82.1 0.7 copy-start.11
  93.7 11.5 %collective-permute-start.5 = (f32[3,112,256]{2,1,0:T(8,128)S(1)}, f32[3,112,256]{2,1,0:T(8,128)S(1)}, u32[]{:S(2)}, u32[]{:S(2)}) collective-permute-start(f32[3,112,256]{2,1,0:T(8,128)S(1)} %shard_map.73), channel_id=1, source_target_pairs={{0,2},{2,4},{4,6},{6,8},{8,10},{10,12},{12,14},{14,0},{1,3},{3,5},... | collective-permute-start | bytes 1032200 | tf_op jit(solution)/shard_map/ppermute | solution.py:38

commit v19 on v17

--- a/solution.py
+++ b/solution.py
@@ -20,7 +20,7 @@
 WET_FIRST, WET_SECOND = 16, 19
 CONTROLS = 24
 EARLY = 144
-PIECES = ((0, 80), (80, 144))
+PIECES = ((0, 72), (72, 144))
 AGAIN = 16
 LATE = TILE - EARLY + 16
 CHUNKS = 8
@@ -219,29 +219,28 @@
     wait_all(early)
 
 
-def hold(order, leaving, same):
-    del order, leaving, same
+def hold(first, second, leaving, same):
+    del first, second, leaving, same
 
 
 class Passing:
-    def __init__(self, ctl, state_in, bed_in, manning_in, arrived, leaving, buffer, sems):
+    def __init__(self, ctl, piece, state_in, bed_in, manning_in, arrived, leaving, buffer, sems):
         self.again = ctl[MOVE] == ctl[MOVE + 1]
         self.other = 1 - ctl[MOVE]
-        self.refs = state_in, bed_in, manning_in, arrived, buffer, sems
-        self.outgoing = [
-            pltpu.make_async_copy(buffer.at[:, begin:end], piece, sems.at[1 + index])
-            for index, ((begin, end), piece) in enumerate(zip(PIECES, leaving))
-        ]
+        self.rows = slice(*piece)
+        self.refs = state_in, bed_in, manning_in
+        self.incoming = pltpu.make_async_copy(arrived, buffer, sems.at[0])
+        self.outgoing = pltpu.make_async_copy(buffer, leaving, sems.at[1])
+        self.buffer = buffer
+        self.sem = sems.at[0]
 
     def start(self):
-        state_in, bed_in, manning_in, arrived, buffer, sems = self.refs
-        rows = slice(0, EARLY)
-        sem = sems.at[0]
+        state_in, bed_in, manning_in = self.refs
+        buffer, sem, rows = self.buffer, self.sem, self.rows
 
         @pl.when(self.again)
         def _():
-            for (begin, end), piece in zip(PIECES, arrived):
-                pltpu.make_async_copy(piece, buffer.at[:, begin:end], sem).start()
+            self.incoming.start()
 
         @pl.when(jnp.logical_not(self.again))
         def _():
@@ -250,26 +249,37 @@
             pltpu.make_async_copy(manning_in.at[self.other, rows], buffer.at[4], sem).start()
 
     def middle(self):
-        _, _, _, arrived, buffer, sems = self.refs
-        for (begin, end), piece in zip(PIECES, arrived):
-            pltpu.make_async_copy(piece, buffer.at[:, begin:end], sems.at[0]).wait()
-        for copy in self.outgoing:
-            copy.start()
+        self.incoming.wait()
+        self.outgoing.start()
 
     def end(self):
-        wait_all(self.outgoing)
+        self.outgoing.wait()
 
 
 def rates_and_leaving(
-    ctl, state_in, bed_in, state_first, manning_in, arrived_low, arrived_high,
-    rate_out, leaving_low, leaving_high,
+    ctl, state_in, bed_in, state_first, manning_in, arrived, rate_out, leaving,
     state, bed, rate, sems, buffer, moving,
 ):
-    arrived = arrived_low, arrived_high
     passing = Passing(
-        ctl, state_first, bed_in, manning_in, arrived, (leaving_low, leaving_high), buffer, moving
+        ctl, PIECES[0], state_first, bed_in, manning_in, arrived, leaving, buffer, moving
     )
     rates(ctl, state_in, bed_in, rate_out, state, bed, rate, sems, passing)
+
+
+def update_and_leaving(
+    step, ctl, got_in, ground_in, columns_in, state_in, manning_in, rate_in,
+    state_first, bed_in, arrived, fresh_out, first_out, second_out, delta_out, leaving, *rest
+):
+    *rest, buffer, moving = rest
+    passing = Passing(
+        ctl, PIECES[1], state_first, bed_in, manning_in, arrived, leaving, buffer, moving
+    )
+    passing.start()
+    update(
+        step, ctl, got_in, ground_in, columns_in, state_in, manning_in, rate_in,
+        fresh_out, first_out, second_out, delta_out, *rest, passing=passing,
+    )
+    passing.end()
 
 
 def rates_after(ctl, state_in, bed_in, order, *rest):
@@ -659,7 +669,9 @@
     )
 
 
-def update(step, ctl, got_in, ground_in, columns_in, state_in, manning_in, rate_in, *rest):
+def update(
+    step, ctl, got_in, ground_in, columns_in, state_in, manning_in, rate_in, *rest, passing=None
+):
     more = step + 1 < STEPS
     fresh_out, first_out, second_out, delta_out = rest[:4]
     rest = rest[4:]
@@ -748,6 +760,8 @@
             sems,
             3 * PARTS + index,
         )
+        if passing and index == PARTS // 2:
+            passing.middle()
     if more:
         messages(ctl, fresh, None, jnp.max(total, keepdims=True), out, columns_out)
         outgoing += start_all(((out, first_out), (columns_out, second_out)), sems, 4 * PARTS)
@@ -841,38 +855,40 @@
         got = spread(out)
         ground = got if step == 0 else ground
         scratch = [whole, part, whole, pltpu.SemaphoreType.DMA((3 * CHUNKS,))]
-        if step == 0:
-            rate = call(rates, shape, hbm(), [smem(), hbm(), hbm()], 0, scratch, moved=0)(
-                ctl, state, bed
-            )
-            leaving[1] = call(
-                hold, piece_shapes[1], hbm(), [hbm(), hbm()], 1 << 10, aliases={1: 0}
-            )(rate, leaving[1])
-            early_first = [shifted(piece, "xb", 1) for piece in leaving]
-        elif step == 1:
-            rate, *leaving = call(
+        piece_scratch = [buffer(piece_shapes[0]), pltpu.SemaphoreType.DMA((2,))]
+        if step == 1:
+            rate, leaving = call(
                 rates_and_leaving,
-                (shape,) + piece_shapes,
-                (hbm(),) * 3,
-                [smem()] + [hbm()] * 6,
+                (shape, piece_shapes[0]),
+                (hbm(),) * 2,
+                [smem()] + [hbm()] * 5,
                 16 << 20,
-                scratch + [buffer(early_shape), pltpu.SemaphoreType.DMA((3,))],
-            )(ctl, state, bed, state_first, manning, *early_first)
-            early_second = [shifted(piece, "xb", 1) for piece in leaving]
-        else:
+                scratch + piece_scratch,
+            )(ctl, state, bed, state_first, manning, early_first[0])
+            early_second = [shifted(leaving, "xb", 1)]
+        elif step == 2:
             rate = call(rates_after, shape, hbm(), [smem()] + [hbm()] * 3, 16 << 20, scratch)(
                 ctl, state, bed, early_second[0]
             )
+        else:
+            rate = call(rates, shape, hbm(), [smem(), hbm(), hbm()], 16 << 20, scratch)(
+                ctl, state, bed
+            )
+            held = call(
+                hold, piece_shapes[0], hbm(), [hbm()] * 3, 1 << 10, aliases={2: 0}
+            )(rate, got, leaving[0])
+            early_first = [shifted(held, "xb", 1)]
         more = step + 1 < STEPS
         if more:
             shapes = f32(8 * devices, TILE), f32(8, TILE)
         else:
             shapes = late_shape, late_shape
+        passing = step == 1
         outs = call(
-            functools.partial(update, step),
-            (shape,) + shapes + (delta_shape,),
-            (hbm(),) * 4,
-            [smem()] + [hbm()] * 6,
+            functools.partial(update_and_leaving if passing else update, step),
+            (shape,) + shapes + (delta_shape,) + ((piece_shapes[1],) if passing else ()),
+            (hbm(),) * (5 if passing else 4),
+            [smem()] + [hbm()] * (9 if passing else 6),
             8 << 20,
             [
                 whole,
@@ -886,11 +902,22 @@
                 buffer(shapes[1]),
                 buffer(delta_shape),
                 pltpu.SemaphoreType.DMA((5 * PARTS + 4,)),
-            ],
-            moved=14 if step == 0 else 10,
-        )(ctl, got, ground, columns, state, manning, rate)
-        deltas.append(outs[-1])
-        state, out, columns, _ = outs
+            ]
+            + (piece_scratch if passing else []),
+            moved=10,
+        )(
+            ctl, got, ground, columns, state, manning, rate,
+            *((state_first, bed, early_first[1]) if passing else ())
+        )
+        state, out, columns, delta, *passed = outs
+        deltas.append(delta)
+        if step == 0:
+            held = call(
+                hold, piece_shapes[1], hbm(), [hbm()] * 3, 1 << 10, aliases={2: 0}
+            )(delta, delta, leaving[1])
+            early_first.append(shifted(held, "xb", 1))
+        elif step == 1:
+            early_second.append(shifted(passed[0], "xb", 1))
     late_first, late_second = out, columns
     room = 16 << 20
     late_arrived = shifted(late_first, "xb", 1)

time: 121 us -> 112 us (0.926)
  starting transfers between devices: 36.1 us -> 20.3 us
  waiting for transfers between devices: 26.7 us -> 38.6 us
  Pallas kernels: 52.1 us -> 46.4 us
    all_to_all x3, starting transfers between devices: 29 us -> 17.3 us  [spread(): lax.all_to_all(fast, ('xb', 'yb'), split_axis=0, concat_axis=0, tiled=True)]
    all_to_all x3, waiting for transfers between devices: 0.05 us -> 6.36 us  [spread(): lax.all_to_all(fast, ('xb', 'yb'), split_axis=0, concat_axis=0, tiled=True)]
    pallas_call x1, Pallas kernels: 7.43 us -> 1.52 us  [body(): call(repeat_first, shape, hbm(), [smem()] + [vmem()] * 3 + [anywhere()] *...]
    ppermute x6, waiting for transfers between devices: 26.7 us -> 32.2 us  [shifted(): return lax.ppermute(value, axis, pairs)]
    ppermute x6, starting transfers between devices: 7.09 us -> 2.99 us  [shifted(): return lax.ppermute(value, axis, pairs)]
    pallas_call x6 -> x7, Pallas kernels: 26.4 us -> 26.6 us  [the longest x3 14.7 us: body(): call(functools.partial(update_and_leaving if passing else update, step),...]
    unnamed x34 -> x32, local copies, waits for them, and re-layouts: 5.31 us -> 5.38 us
  transfers between devices with their start and end apart: 9 -> 9, of which waited for: 3 -> 6; matrix products, arithmetic and copies ran while one was open for 0% -> 0% of each run, Pallas kernels for 35% -> 32%
where the time goes in v19:
time: 112 us; the launch traced here: 111 us
  Pallas kernels  46.4 us (41%)
  waiting for transfers between devices  38.6 us (34%)
  starting transfers between devices  20.3 us (18%)
  local copies, waits for them, and re-layouts  5.38 us (5%)
    ppermute x6, waiting for transfers between devices, shifted(): return lax.ppermute(value, axis, pairs)  32.2 us
    all_to_all x3, starting transfers between devices, spread(): lax.all_to_all(fast, ('xb', 'yb'), split_axis=0, concat_axis=0, tiled=True)  17.3 us
    pallas_call x3, Pallas kernels, body(): call(functools.partial(update_and_leaving if passing else update, step),...  14.7 us
    pallas_call x1, Pallas kernels, body(): call(repeat_second, (early_state, late_shape), (anywhere(), vmem()), [sme...  6.64 us
    all_to_all x3, waiting for transfers between devices, spread(): lax.all_to_all(fast, ('xb', 'yb'), split_axis=0, concat_axis=0, tiled=True)  6.36 us
    pallas_call x1, Pallas kernels, body(): call(rates_and_leaving, (shape, piece_shapes[0]), (hbm(),) * 2, [smem()]...  5.98 us
    pallas_call x1, Pallas kernels, body(): call(rates, shape, hbm(), [smem(), hbm(), hbm()], 16 << 20, scratch)  5.96 us
    pallas_call x1, Pallas kernels, body(): call(rates_after, shape, hbm(), [smem()] + [hbm()] * 3, 16 << 20, scratch)  5.96 us
  transfers between devices with their start and end apart: 9, of which 6 were waited for; matrix products, arithmetic and copies ran while one was open for 0% of the time, Pallas kernels for 32%

profile of v19, /device:TPU:0, one launch (start us, length us, event | category | flops | bytes accessed | tf_op | source)
XLA Modules:
  0.0 110.9 jit_solution(10193057272844185049)
XLA Ops:
  0.0 3.5 %shard_map.64 = (f32[128,384]{1,0:T(8,128)}, f32[8,256]{1,0:T(8,128)}, s32[24]{0:T(128)}, f32[5,72,256]{2,1,0:T(8,128)}, f32[5,72,256]{2,1,0:T(8,128)}) custom-call(f32[2,3,256,256]{3,2,1,0:T(8,128)} %state_first.3, f32[2,256,256]{2,1,0:T(8,128)} %bed_in.9, f32[2,256,256]{2,1,0:T(8,128)} %manning_in.9, s32[4,32]{1,0:T(4,128)} %bitcast.17, s32[3,32]{1,0:T(4,128)} %wet_in.1, ...), custom_call_target="tpu_custom_call" | custom-call | flops 4194304 | bytes 4194304 | tf_op jit(solution)/shard_map/pallas_call | solution.py:830
  3.5 7.4 %all-to-all-start = ((f32[16,8,384]{2,1,0:T(8,128)}), f32[16,8,384]{2,1,0:T(8,128)S(1)}, u32[]{:S(2)}, u32[]{:S(2)}) async-start(f32[16,8,384]{2,1,0:T(8,128)} %bitcast.14), calls=%async_computation | async-start | bytes 393216 | tf_op jit(solution)/shard_map/all_to_all | solution.py:812
  10.9 6.0 %shard_map.65.rate_in.first = f32[2,3,256,256]{3,2,1,0:T(8,128)} custom-call(s32[24]{0:T(128)} %get-tuple-element.27.ctl, f32[2,3,256,256]{3,2,1,0:T(8,128)} %state_first.3, f32[2,256,256]{2,1,0:T(8,128)} %bed_in.9), custom_call_target="tpu_custom_call" | custom-call | flops 16777216 | bytes 4194304 | tf_op jit(solution)/shard_map/pallas_call | solution.py:874
  16.9 3.0 %all-to-all-done = f32[16,8,384]{2,1,0:T(8,128)S(1)} async-done(((f32[16,8,384]{2,1,0:T(8,128)}), f32[16,8,384]{2,1,0:T(8,128)S(1)}, u32[]{:S(2)}, u32[]{:S(2)}) %all-to-all-start) | async-done | bytes 196640 | tf_op jit(solution)/shard_map/all_to_all | solution.py:812
  19.9 0.7 copy-done.12
  20.6 4.9 %shard_map.66 = (f32[2,3,256,256]{3,2,1,0:T(8,128)}, f32[128,256]{1,0:T(8,128)}, f32[8,256]{1,0:T(8,128)}, f32[8,256]{1,0:T(8,128)}) custom-call(s32[24]{0:T(128)} %get-tuple-element.27.ctl, f32[128,384]{1,0:T(8,128)} %bitcast.8, f32[128,384]{1,0:T(8,128)} %bitcast.9, f32[8,256]{1,0:T(8,128)} %get-tuple-element.29.columns_in, ...), custom_call_target="tpu_custom_call" | custom-call | flops 8388608 | bytes 10485760 | tf_op jit(solution)/shard_map/pallas_call | solution.py:887
  25.5 0.6 collective-permute-start.1
  26.1 6.1 %all-to-all-start.1 = ((f32[16,8,256]{2,1,0:T(8,128)}), f32[16,8,256]{2,1,0:T(8,128)S(1)}, u32[]{:S(2)}, u32[]{:S(2)}) async-start(f32[16,8,256]{2,1,0:T(8,128)} %bitcast.15), calls=%async_computation.1 | async-start | bytes 262144 | tf_op jit(solution)/shard_map/all_to_all | solution.py:812
  32.2 2.8 %collective-permute-done.arrived.low = f32[5,72,256]{2,1,0:T(8,128)S(1)} collective-permute-done((f32[5,72,256]{2,1,0:T(8,128)}, f32[5,72,256]{2,1,0:T(8,128)S(1)}, u32[]{:S(2)}, u32[]{:S(2)}) %collective-permute-start) | collective-permute-done | bytes 368672 | tf_op jit(solution)/shard_map/ppermute | solution.py:39
  35.0 0.8 copy-done.1
  35.8 6.0 %shard_map.68 = (f32[2,3,256,256]{3,2,1,0:T(8,128)}, f32[5,72,256]{2,1,0:T(8,128)}) custom-call(s32[24]{0:T(128)} %get-tuple-element.27.ctl, f32[2,3,256,256]{3,2,1,0:T(8,128)} %get-tuple-element.32.state_in, f32[2,256,256]{2,1,0:T(8,128)} %bed_in.9, f32[2,3,256,256]{3,2,1,0:T(8,128)} %state_first.3, f32[2,256,256]{2,1,0:T(8,128)} %manning_in.9, ...), custom_call_target="tpu_custom_call" | custom-call | flops 16777216 | bytes 4194304 | tf_op jit(solution)/shard_map/pallas_call | solution.py:860
  41.8 2.1 %all-to-all-done.1 = f32[16,8,256]{2,1,0:T(8,128)S(1)} async-done(((f32[16,8,256]{2,1,0:T(8,128)}), f32[16,8,256]{2,1,0:T(8,128)S(1)}, u32[]{:S(2)}, u32[]{:S(2)}) %all-to-all-start.1) | async-done | bytes 131104 | tf_op jit(solution)/shard_map/all_to_all | solution.py:812
  44.0 0.7 copy-done.13
  44.6 0.2 copy-done.3
  44.8 5.0 %shard_map.70 = (f32[2,3,256,256]{3,2,1,0:T(8,128)}, f32[128,256]{1,0:T(8,128)}, f32[8,256]{1,0:T(8,128)}, f32[8,256]{1,0:T(8,128)}, f32[5,72,256]{2,1,0:T(8,128)}) custom-call(s32[24]{0:T(128)} %get-tuple-element.27.ctl, f32[128,256]{1,0:T(8,128)} %bitcast.12, f32[128,384]{1,0:T(8,128)} %bitcast.10, f32[8,256]{1,0:T(8,128)} %get-tuple-element.31.columns_in, ...), custom_call_target="tpu_custom_call" | custom-call | flops 8388608 | bytes 10485760 | tf_op jit(solution)/shard_map/pallas_call | solution.py:887
  49.8 3.8 %all-to-all-start.2 = ((f32[16,8,256]{2,1,0:T(8,128)}), f32[16,8,256]{2,1,0:T(8,128)S(1)}, u32[]{:S(2)}, u32[]{:S(2)}) async-start(f32[16,8,256]{2,1,0:T(8,128)} %bitcast.16), calls=%async_computation.2 | async-start | bytes 262144 | tf_op jit(solution)/shard_map/all_to_all | solution.py:812
  53.7 0.7 copy-done.5
  54.4 6.0 %shard_map.71.rate_in = f32[2,3,256,256]{3,2,1,0:T(8,128)} custom-call(s32[24]{0:T(128)} %get-tuple-element.27.ctl, f32[2,3,256,256]{3,2,1,0:T(8,128)} %get-tuple-element.39.state_in, f32[2,256,256]{2,1,0:T(8,128)} %bed_in.9, f32[5,72,256]{2,1,0:T(8,128)} %copy-done.5), custom_call_target="tpu_custom_call" | custom-call | flops 16777216 | bytes 4194304 | tf_op jit(solution)/shard_map/pallas_call | solution.py:870
  60.4 1.2 %all-to-all-done.2 = f32[16,8,256]{2,1,0:T(8,128)S(1)} async-done(((f32[16,8,256]{2,1,0:T(8,128)}), f32[16,8,256]{2,1,0:T(8,128)S(1)}, u32[]{:S(2)}, u32[]{:S(2)}) %all-to-all-start.2) | async-done | bytes 131104 | tf_op jit(solution)/shard_map/all_to_all | solution.py:812
  61.6 0.6 copy-done.14
  62.3 4.8 %shard_map.72 = (f32[2,3,256,256]{3,2,1,0:T(8,128)}, f32[3,128,256]{2,1,0:T(8,128)}, f32[3,128,256]{2,1,0:T(8,128)}, f32[8,256]{1,0:T(8,128)}) custom-call(s32[24]{0:T(128)} %get-tuple-element.27.ctl, f32[128,256]{1,0:T(8,128)} %bitcast.13, f32[128,384]{1,0:T(8,128)} %bitcast.11, f32[8,256]{1,0:T(8,128)} %get-tuple-element.38.columns_in, ...), custom_call_target="tpu_custom_call" | custom-call | flops 8388608 | bytes 10485760 | tf_op jit(solution)/shard_map/pallas_call | solution.py:887
  67.1 0.8 collective-permute-start.3
  67.9 1.4 %collective-permute-start.4 = (f32[5,72,256]{2,1,0:T(8,128)S(1)}, f32[5,72,256]{2,1,0:T(8,128)S(1)}, u32[]{:S(2)}, u32[]{:S(2)}) collective-permute-start(f32[5,72,256]{2,1,0:T(8,128)S(1)} %copy-done.15), channel_id=1, source_target_pairs={{0,2},{2,4},{4,6},{6,8},{8,10},{10,12},{12,14},{14,0},{1,3},{3,5},... | collective-permute-start | bytes 1105928 | tf_op jit(solution)/shard_map/ppermute | solution.py:39
  69.3 18.9 %collective-permute-done.4.high = f32[5,72,256]{2,1,0:T(8,128)S(1)} collective-permute-done((f32[5,72,256]{2,1,0:T(8,128)S(1)}, f32[5,72,256]{2,1,0:T(8,128)S(1)}, u32[]{:S(2)}, u32[]{:S(2)}) %collective-permute-start.4) | collective-permute-done | bytes 368672 | tf_op jit(solution)/shard_map/ppermute | solution.py:39
  88.3 1.0 copy-done.7
  89.3 0.7 copy-done.11
  90.0 6.6 %shard_map.73 = (f32[3,144,256]{2,1,0:T(8,128)S(1)}, f32[3,128,256]{2,1,0:T(8,128)S(1)}) custom-call(s32[24]{0:T(128)S(1)} %copy-done.9, f32[8,256]{1,0:T(8,128)S(1)} %copy-done.8, f32[8,256]{1,0:T(8,128)S(1)} %copy-done.10, f32[8,256]{1,0:T(8,128)S(1)} %copy-done.11, f32[5,72,256]{2,1,0:T(8,128)S(1)} %copy-done.6, ...), custom_call_target="tpu_custom_call" | custom-call | flops 8388608 | bytes 4194304 | tf_op jit(solution)/shard_map/pallas_call | solution.py:924
  96.6 0.6 shard_map.74
  97.2 0.1 collective-permute-start.5
  97.3 1.5 %shard_map.75.before = f32[2,3,256,256]{3,2,1,0:T(8,128)} custom-call(s32[24]{0:T(128)S(1)} %copy-done.9, f32[8,256]{1,0:T(8,128)S(1)} %copy-done.8, f32[8,256]{1,0:T(8,128)S(1)} %copy-done.10, f32[8,256]{1,0:T(8,128)S(1)} %copy-done.11, f32[5,72,256]{2,1,0:T(8,128)S(1)} %copy-done.2, f32[5,72,256]{2,1,0:T(8,128)S(1)} %copy-done.4, ...), custom_call_target="tpu_custom_call" | custom-call | flops 8388608 | bytes 4194304 | tf_op jit(solution)/shard_map/pallas_call | solution.py:942
  98.9 10.5 %collective-permute-done.5.late = f32[3,128,256]{2,1,0:T(8,128)S(1)} collective-permute-done((f32[3,128,256]{2,1,0:T(8,128)S(1)}, f32[3,128,256]{2,1,0:T(8,128)S(1)}, u32[]{:S(2)}, u32[]{:S(2)}) %collective-permute-start.5) | collective-permute-done | bytes 393248 | tf_op jit(solution)/shard_map/ppermute | solution.py:39
  109.4 1.5 %shard_map.76 = f32[2,3,256,256]{3,2,1,0:T(8,128)} custom-call(s32[24]{0:T(128)S(1)} %copy-done.9, f32[3,128,256]{2,1,0:T(8,128)S(1)} %collective-permute-done.5.late, f32[3,144,256]{2,1,0:T(8,128)S(1)} %get-tuple-element.47.order.early, f32[2,3,256,256]{3,2,1,0:T(8,128)} %shard_map.75.before), custom_call_target="tpu_custom_call", output_to_operand_aliasing={{}: (3, {})} | custom-call | flops 1048576 | bytes 4194304 | tf_op jit(solution)/shard_map/pallas_call | solution.py:957
  (31 shorter events, 0.1 us)
Async XLA Ops:
  3.5 16.4 %all-to-all-start = ((f32[16,8,384]{2,1,0:T(8,128)}), f32[16,8,384]{2,1,0:T(8,128)S(1)}, u32[]{:S(2)}, u32[]{:S(2)}) async-start(f32[16,8,384]{2,1,0:T(8,128)} %bitcast.14), calls=%async_computation | async-start | bytes 393216 | tf_op jit(solution)/shard_map/all_to_all | solution.py:812
  19.9 0.7 copy-start.12
  20.6 14.4 %collective-permute-start = (f32[5,72,256]{2,1,0:T(8,128)}, f32[5,72,256]{2,1,0:T(8,128)S(1)}, u32[]{:S(2)}, u32[]{:S(2)}) collective-permute-start(f32[5,72,256]{2,1,0:T(8,128)} %shard_map.67), channel_id=1, source_target_pairs={{0,2},{2,4},{4,6},{6,8},{8,10},{10,12},{12,14},{14,0},{1,3},{3,5},... | collective-permute-start | bytes 1105928 | tf_op jit(solution)/shard_map/ppermute | solution.py:39
  25.5 18.5 %collective-permute-start.1 = (f32[5,72,256]{2,1,0:T(8,128)}, f32[5,72,256]{2,1,0:T(8,128)S(1)}, u32[]{:S(2)}, u32[]{:S(2)}) collective-permute-start(f32[5,72,256]{2,1,0:T(8,128)} %shard_map.69), channel_id=1, source_target_pairs={{0,2},{2,4},{4,6},{6,8},{8,10},{10,12},{12,14},{14,0},{1,3},{3,5},... | collective-permute-start | bytes 1105928 | tf_op jit(solution)/shard_map/ppermute | solution.py:39
  26.1 17.8 %all-to-all-start.1 = ((f32[16,8,256]{2,1,0:T(8,128)}), f32[16,8,256]{2,1,0:T(8,128)S(1)}, u32[]{:S(2)}, u32[]{:S(2)}) async-start(f32[16,8,256]{2,1,0:T(8,128)} %bitcast.15), calls=%async_computation.1 | async-start | bytes 262144 | tf_op jit(solution)/shard_map/all_to_all | solution.py:812
  35.0 0.8 copy-start.1
  41.8 11.9 %collective-permute-start.2 = (f32[5,72,256]{2,1,0:T(8,128)}, f32[5,72,256]{2,1,0:T(8,128)S(1)}, u32[]{:S(2)}, u32[]{:S(2)}) collective-permute-start(f32[5,72,256]{2,1,0:T(8,128)} %get-tuple-element.40), channel_id=1, source_target_pairs={{0,2},{2,4},{4,6},{6,8},{8,10},{10,12},{12,14},{14,0},{1,3},{3,5},... | collective-permute-start | bytes 1105928 | tf_op jit(solution)/shard_map/ppermute | solution.py:39
  44.0 0.7 copy-start.13
  44.0 0.8 copy-start.3
  49.8 11.8 %all-to-all-start.2 = ((f32[16,8,256]{2,1,0:T(8,128)}), f32[16,8,256]{2,1,0:T(8,128)S(1)}, u32[]{:S(2)}, u32[]{:S(2)}) async-start(f32[16,8,256]{2,1,0:T(8,128)} %bitcast.16), calls=%async_computation.2 | async-start | bytes 262144 | tf_op jit(solution)/shard_map/all_to_all | solution.py:812
  53.7 0.8 copy-start.5
  61.6 0.6 copy-start.14
  62.2 5.7 %copy-start.15 = (f32[5,72,256]{2,1,0:T(8,128)S(1)}, f32[5,72,256]{2,1,0:T(8,128)}, u32[]{:S(2)}) copy-start(f32[5,72,256]{2,1,0:T(8,128)} %get-tuple-element.44) | copy-start | bytes 1105924
  62.2 26.0 %copy-start.6 = (f32[5,72,256]{2,1,0:T(8,128)S(1)}, f32[5,72,256]{2,1,0:T(8,128)}, u32[]{:S(2)}) copy-start(f32[5,72,256]{2,1,0:T(8,128)} %copy-done.5) | copy-start | bytes 1105924
  62.2 26.0 %copy-start.8 = (f32[8,256]{1,0:T(8,128)S(1)}, f32[8,256]{1,0:T(8,128)}, u32[]{:S(2)}) copy-start(f32[8,256]{1,0:T(8,128)} %get-tuple-element.35.first.second.delta0) | copy-start | bytes 24580
  62.2 26.0 %copy-start.9 = (s32[24]{0:T(128)S(1)}, s32[24]{0:T(128)}, u32[]{:S(2)}) copy-start(s32[24]{0:T(128)} %get-tuple-element.27.ctl) | copy-start | bytes 292
  62.2 26.0 %copy-start.10 = (f32[8,256]{1,0:T(8,128)S(1)}, f32[8,256]{1,0:T(8,128)}, u32[]{:S(2)}) copy-start(f32[8,256]{1,0:T(8,128)} %get-tuple-element.42.delta1) | copy-start | bytes 24580
  67.1 30.2 %copy-start = (f32[2,3,256,256]{3,2,1,0:T(8,128)S(1)}, f32[2,3,256,256]{3,2,1,0:T(8,128)}, u32[]{:S(2)}) copy-start(f32[2,3,256,256]{3,2,1,0:T(8,128)} %get-tuple-element.48.state) | copy-start | bytes 4718596
  67.1 30.2 %copy-start.2 = (f32[5,72,256]{2,1,0:T(8,128)S(1)}, f32[5,72,256]{2,1,0:T(8,128)}, u32[]{:S(2)}) copy-start(f32[5,72,256]{2,1,0:T(8,128)} %copy-done.1) | copy-start | bytes 1105924
  67.1 30.2 %copy-start.4 = (f32[5,72,256]{2,1,0:T(8,128)S(1)}, f32[5,72,256]{2,1,0:T(8,128)}, u32[]{:S(2)}) copy-start(f32[5,72,256]{2,1,0:T(8,128)} %copy-done.3) | copy-start | bytes 1105924
  67.1 29.5 %collective-permute-start.3 = (f32[3,128,256]{2,1,0:T(8,128)}, f32[3,128,256]{2,1,0:T(8,128)S(1)}, u32[]{:S(2)}, u32[]{:S(2)}) collective-permute-start(f32[3,128,256]{2,1,0:T(8,128)} %get-tuple-element.41), channel_id=1, source_target_pairs={{0,2},{2,4},{4,6},{6,8},{8,10},{10,12},{12,14},{14,0},{1,3},{3,5},... | collective-permute-start | bytes 1179656 | tf_op jit(solution)/shard_map/ppermute | solution.py:39
  67.9 20.4 %collective-permute-start.4 = (f32[5,72,256]{2,1,0:T(8,128)S(1)}, f32[5,72,256]{2,1,0:T(8,128)S(1)}, u32[]{:S(2)}, u32[]{:S(2)}) collective-permute-start(f32[5,72,256]{2,1,0:T(8,128)S(1)} %copy-done.15), channel_id=1, source_target_pairs={{0,2},{2,4},{4,6},{6,8},{8,10},{10,12},{12,14},{14,0},{1,3},{3,5},... | collective-permute-start | bytes 1105928 | tf_op jit(solution)/shard_map/ppermute | solution.py:39
  88.3 1.0 copy-start.7
  89.3 0.7 copy-start.11
  97.2 12.1 %collective-permute-start.5 = (f32[3,128,256]{2,1,0:T(8,128)S(1)}, f32[3,128,256]{2,1,0:T(8,128)S(1)}, u32[]{:S(2)}, u32[]{:S(2)}) collective-permute-start(f32[3,128,256]{2,1,0:T(8,128)S(1)} %shard_map.74), channel_id=1, source_target_pairs={{0,2},{2,4},{4,6},{6,8},{8,10},{10,12},{12,14},{14,0},{1,3},{3,5},... | collective-permute-start | bytes 1179656 | tf_op jit(solution)/shard_map/ppermute | solution.py:39

commit v20 on v19

--- a/solution.py
+++ b/solution.py
@@ -20,7 +20,7 @@
 WET_FIRST, WET_SECOND = 16, 19
 CONTROLS = 24
 EARLY = 144
-PIECES = ((0, 72), (72, 144))
+PIECES = ((0, 80), (80, 144))
 AGAIN = 16
 LATE = TILE - EARLY + 16
 CHUNKS = 8
@@ -573,14 +573,14 @@
 
 
 def repeat_first(
-    ctl, delta0, delta1, delta2, low, high, late_in, state, out, work, other, tile, late, sems
+    ctl, delta0, delta1, delta2, low, high, late_in, staying, out, work, other, tile, late, sems
 ):
     rest = out.at[1 - ctl[MOVE + 1]]
     again = ctl[MOVE] == ctl[MOVE + 1]
 
     @pl.when(again)
     def _():
-        wait_all(start_all(((state.at[1 - ctl[MOVE]], tile),), sems))
+        wait_all(start_all(((staying, tile),), sems))
 
     @pl.when(jnp.logical_not(again))
     def _():
@@ -669,20 +669,27 @@
     )
 
 
+def last_update(moving, ctl, got, ground, columns, state, manning, rate, order, *rest):
+    del order
+    slot = ctl[MOVE] if moving else 1 - ctl[MOVE]
+    update(STEPS - 1, ctl, got, ground, columns, state, manning, rate, *rest, slots=(slot,))
+
+
 def update(
-    step, ctl, got_in, ground_in, columns_in, state_in, manning_in, rate_in, *rest, passing=None
+    step, ctl, got_in, ground_in, columns_in, state_in, manning_in, rate_in, *rest,
+    passing=None, slots=(0, 1),
 ):
     more = step + 1 < STEPS
     fresh_out, first_out, second_out, delta_out = rest[:4]
     rest = rest[4:]
     state, manning, rate, fresh, got, ground, columns, first, second, delta_keep, sems = rest
-    out, columns_out = late_first, late_second = first, second
+    out, columns_out = first, second
     small = start_all(
         ((got_in, got), (ground_in, ground), (columns_in, columns)), sems, 5 * PARTS
     )
     size = 2 * TILE // PARTS
     parts = [
-        (slot, slice(k * size, (k + 1) * size)) for slot in range(2) for k in range(PARTS // 2)
+        (slot, slice(k * size, (k + 1) * size)) for slot in slots for k in range(PARTS // 2)
     ]
     incoming = []
     for index, (slot, rows) in enumerate(parts):
@@ -711,7 +718,7 @@
     fix = column_fix(got, ground, columns)
     facing = jnp.where(upper > 0, ctl[SLOT_LOW], 1 - ctl[SLOT_LOW])
     begin = pl.multiple_of((1 - upper) * LANES, LANES)
-    target = (1 - upper) * (LANES - 1)
+    goal = (1 - upper) * (LANES - 1)
     lane = lax.broadcasted_iota(jnp.int32, (size, LANES), 1)
     total = jnp.zeros((ROWS, TILE), jnp.float32)
     for index, (slot, part_rows) in enumerate(parts):
@@ -725,10 +732,10 @@
         def _(slot=slot, part_rows=part_rows):
             for field in range(3):
                 turned = pltpu.roll(
-                    fix[part_rows], lax.rem(target + LANES - field, LANES), 1
+                    fix[part_rows], lax.rem(goal + LANES - field, LANES), 1
                 )
                 rate[slot, field, part_rows, pl.ds(begin, LANES)] += jnp.where(
-                    lane == target, turned, 0.0
+                    lane == goal, turned, 0.0
                 )
 
         wet_now = flag(ctl, WET + 2 * step + slot)
@@ -755,10 +762,9 @@
         if more:
             best = jnp.where(flag(ctl, WET + 2 * step + 2 + slot), best, 0.0)
             total = jnp.maximum(total, best)
+        target = fresh_out.at[slot, :, part_rows] if more else fresh_out.at[:, part_rows]
         outgoing += start_all(
-            ((fresh.at[slot, :, part_rows], fresh_out.at[slot, :, part_rows]),),
-            sems,
-            3 * PARTS + index,
+            ((fresh.at[slot, :, part_rows], target),), sems, 3 * PARTS + index
         )
         if passing and index == PARTS // 2:
             passing.middle()
@@ -766,10 +772,9 @@
         messages(ctl, fresh, None, jnp.max(total, keepdims=True), out, columns_out)
         outgoing += start_all(((out, first_out), (columns_out, second_out)), sems, 4 * PARTS)
     else:
-        late_rows(fresh.at[ctl[MOVE]], late_first)
-        outgoing += start_all(((late_first, first_out),), sems, 4 * PARTS)
-        late_rows(fresh.at[1 - ctl[MOVE]], late_second)
-        outgoing += start_all(((late_second, second_out),), sems, 4 * PARTS + 1)
+        second[...] = jnp.zeros_like(second)
+        late_rows(fresh.at[slots[0]], first)
+        outgoing += start_all(((first, first_out), (second, second_out)), sems, 4 * PARTS)
     wait_all(outgoing)
 
 
@@ -855,7 +860,9 @@
         got = spread(out)
         ground = got if step == 0 else ground
         scratch = [whole, part, whole, pltpu.SemaphoreType.DMA((3 * CHUNKS,))]
-        piece_scratch = [buffer(piece_shapes[0]), pltpu.SemaphoreType.DMA((2,))]
+        piece_scratch = [
+            [buffer(piece), pltpu.SemaphoreType.DMA((2,))] for piece in piece_shapes
+        ]
         if step == 1:
             rate, leaving = call(
                 rates_and_leaving,
@@ -863,7 +870,7 @@
                 (hbm(),) * 2,
                 [smem()] + [hbm()] * 5,
                 16 << 20,
-                scratch + piece_scratch,
+                scratch + piece_scratch[0],
             )(ctl, state, bed, state_first, manning, early_first[0])
             early_second = [shifted(leaving, "xb", 1)]
         elif step == 2:
@@ -879,36 +886,33 @@
             )(rate, got, leaving[0])
             early_first = [shifted(held, "xb", 1)]
         more = step + 1 < STEPS
-        if more:
-            shapes = f32(8 * devices, TILE), f32(8, TILE)
-        else:
-            shapes = late_shape, late_shape
+        shapes = (f32(8 * devices, TILE) if more else late_shape), f32(8, TILE)
         passing = step == 1
+        work = [
+            whole,
+            part,
+            whole,
+            whole,
+            pltpu.VMEM(got.shape, jnp.float32),
+            pltpu.VMEM(ground.shape, jnp.float32),
+            pltpu.VMEM((8, TILE), jnp.float32),
+            buffer(shapes[0]),
+            buffer(shapes[1]),
+            buffer(delta_shape),
+            pltpu.SemaphoreType.DMA((5 * PARTS + 4,)),
+        ]
+        operands = ctl, got, ground, columns, state, manning, rate
+        if not more:
+            break
         outs = call(
             functools.partial(update_and_leaving if passing else update, step),
             (shape,) + shapes + (delta_shape,) + ((piece_shapes[1],) if passing else ()),
             (hbm(),) * (5 if passing else 4),
             [smem()] + [hbm()] * (9 if passing else 6),
             8 << 20,
-            [
-                whole,
-                part,
-                whole,
-                whole,
-                pltpu.VMEM(got.shape, jnp.float32),
-                pltpu.VMEM(ground.shape, jnp.float32),
-                pltpu.VMEM((8, TILE), jnp.float32),
-                buffer(shapes[0]),
-                buffer(shapes[1]),
-                buffer(delta_shape),
-                pltpu.SemaphoreType.DMA((5 * PARTS + 4,)),
-            ]
-            + (piece_scratch if passing else []),
+            work + (piece_scratch[1] if passing else []),
             moved=10,
-        )(
-            ctl, got, ground, columns, state, manning, rate,
-            *((state_first, bed, early_first[1]) if passing else ())
-        )
+        )(*operands, *((state_first, bed, early_first[1]) if passing else ()))
         state, out, columns, delta, *passed = outs
         deltas.append(delta)
         if step == 0:
@@ -918,7 +922,21 @@
             early_first.append(shifted(held, "xb", 1))
         elif step == 1:
             early_second.append(shifted(passed[0], "xb", 1))
-    late_first, late_second = out, columns
+
+    def finish_step(moving, order):
+        return call(
+            functools.partial(last_update, moving),
+            (tile_shape,) + shapes + (delta_shape,),
+            (hbm(),) * 4,
+            [smem()] + [hbm()] * 7,
+            8 << 20,
+            work,
+            moved=10,
+        )(*operands, order)
+
+    _, late_first, _, delta = finish_step(True, early_second[1])
+    staying, late_second, _, _ = finish_step(False, delta)
+    deltas.append(delta)
     room = 16 << 20
     late_arrived = shifted(late_first, "xb", 1)
     second, late_second = call(
@@ -953,7 +971,7 @@
             pltpu.SemaphoreType.DMA((3,)),
         ],
         room=room,
-    )(ctl, *deltas, *early_first, late_arrived, state)
+    )(ctl, *deltas, *early_first, late_arrived, staying)
     return call(
         finish,
         shape,

time: 112 us -> 99.1 us (0.88)
  waiting for transfers between devices: 38.6 us -> 16.4 us
  Pallas kernels: 46.4 us -> 55.5 us
    ppermute x6, waiting for transfers between devices: 32.2 us -> 10.1 us  [shifted(): return lax.ppermute(value, axis, pairs)]
    pallas_call x0 -> x2, Pallas kernels: none -> 7.78 us  [finish_step(): call(functools.partial(last_update, moving), (tile_shape,) + shapes + (de...]
    pallas_call x1, Pallas kernels: 1.52 us -> 7.43 us  [body(): call(repeat_first, shape, hbm(), [smem()] + [vmem()] * 3 + [anywhere()] *...]
    pallas_call x3 -> x2, Pallas kernels: 14.7 us -> 10.1 us  [body(): call(functools.partial(update_and_leaving if passing else update, step),...]
    all_to_all x3, starting transfers between devices: 17.3 us -> 19 us  [spread(): lax.all_to_all(fast, ('xb', 'yb'), split_axis=0, concat_axis=0, tiled=True)]
    unnamed x32 -> x34, local copies, waits for them, and re-layouts: 5.38 us -> 4.9 us
  transfers between devices with their start and end apart: 9 -> 9, of which waited for: 6 -> 6; matrix products, arithmetic and copies ran while one was open for 0% -> 0% of each run, Pallas kernels for 32% -> 47%
where the time goes in v20:
time: 99.1 us; the launch traced here: 98.3 us
  Pallas kernels  55.5 us (56%)
  starting transfers between devices  21.2 us (21%)
  waiting for transfers between devices  16.4 us (17%)
  local copies, waits for them, and re-layouts  4.9 us (5%)
    all_to_all x3, starting transfers between devices, spread(): lax.all_to_all(fast, ('xb', 'yb'), split_axis=0, concat_axis=0, tiled=True)  19 us
    pallas_call x2, Pallas kernels, body(): call(functools.partial(update_and_leaving if passing else update, step),...  10.1 us
    ppermute x6, waiting for transfers between devices, shifted(): return lax.ppermute(value, axis, pairs)  10.1 us
    pallas_call x2, Pallas kernels, finish_step(): call(functools.partial(last_update, moving), (tile_shape,) + shapes + (de...  7.78 us
    pallas_call x1, Pallas kernels, body(): call(repeat_first, shape, hbm(), [smem()] + [vmem()] * 3 + [anywhere()] *...  7.43 us
    pallas_call x1, Pallas kernels, body(): call(repeat_second, (early_state, late_shape), (anywhere(), vmem()), [sme...  6.64 us
    all_to_all x3, waiting for transfers between devices, spread(): lax.all_to_all(fast, ('xb', 'yb'), split_axis=0, concat_axis=0, tiled=True)  6.32 us
    pallas_call x1, Pallas kernels, body(): call(rates_and_leaving, (shape, piece_shapes[0]), (hbm(),) * 2, [smem()]...  5.98 us
  transfers between devices with their start and end apart: 9, of which 6 were waited for; matrix products, arithmetic and copies ran while one was open for 0% of the time, Pallas kernels for 47%

profile of v20, /device:TPU:0, one launch (start us, length us, event | category | flops | bytes accessed | tf_op | source)
XLA Modules:
  0.0 98.3 jit_solution(15722207932703251687)
XLA Ops:
  0.0 3.6 %shard_map.64 = (f32[128,384]{1,0:T(8,128)}, f32[8,256]{1,0:T(8,128)}, s32[24]{0:T(128)}, f32[5,80,256]{2,1,0:T(8,128)}, f32[5,64,256]{2,1,0:T(8,128)}) custom-call(f32[2,3,256,256]{3,2,1,0:T(8,128)} %state_first.3, f32[2,256,256]{2,1,0:T(8,128)} %bed_in.9, f32[2,256,256]{2,1,0:T(8,128)} %manning.3, s32[4,32]{1,0:T(4,128)} %bitcast.19, s32[3,32]{1,0:T(4,128)} %wet_in.1, ...), custom_call_target="tpu_custom_call" | custom-call | flops 4194304 | bytes 4194304 | tf_op jit(solution)/shard_map/pallas_call | solution.py:835
  3.6 7.4 %all-to-all-start = ((f32[16,8,384]{2,1,0:T(8,128)}), f32[16,8,384]{2,1,0:T(8,128)S(1)}, u32[]{:S(2)}, u32[]{:S(2)}) async-start(f32[16,8,384]{2,1,0:T(8,128)} %bitcast.16), calls=%async_computation | async-start | bytes 393216 | tf_op jit(solution)/shard_map/all_to_all | solution.py:817
  11.0 6.0 %shard_map.65.rate_in.first = f32[2,3,256,256]{3,2,1,0:T(8,128)} custom-call(s32[24]{0:T(128)} %get-tuple-element.27.ctl, f32[2,3,256,256]{3,2,1,0:T(8,128)} %state_first.3, f32[2,256,256]{2,1,0:T(8,128)} %bed_in.9), custom_call_target="tpu_custom_call" | custom-call | flops 16777216 | bytes 4194304 | tf_op jit(solution)/shard_map/pallas_call | solution.py:881
  16.9 3.0 %all-to-all-done = f32[16,8,384]{2,1,0:T(8,128)S(1)} async-done(((f32[16,8,384]{2,1,0:T(8,128)}), f32[16,8,384]{2,1,0:T(8,128)S(1)}, u32[]{:S(2)}, u32[]{:S(2)}) %all-to-all-start) | async-done | bytes 196640 | tf_op jit(solution)/shard_map/all_to_all | solution.py:817
  20.0 0.7 copy-done.14
  20.6 5.0 %shard_map.66 = (f32[2,3,256,256]{3,2,1,0:T(8,128)}, f32[128,256]{1,0:T(8,128)}, f32[8,256]{1,0:T(8,128)}, f32[8,256]{1,0:T(8,128)}) custom-call(s32[24]{0:T(128)} %get-tuple-element.27.ctl, f32[128,384]{1,0:T(8,128)} %bitcast.8, f32[128,384]{1,0:T(8,128)} %bitcast.9, f32[8,256]{1,0:T(8,128)} %get-tuple-element.29.columns_in, ...), custom_call_target="tpu_custom_call" | custom-call | flops 8388608 | bytes 10485760 | tf_op jit(solution)/shard_map/pallas_call | solution.py:907
  25.6 0.6 collective-permute-start.1
  26.3 6.1 %all-to-all-start.1 = ((f32[16,8,256]{2,1,0:T(8,128)}), f32[16,8,256]{2,1,0:T(8,128)S(1)}, u32[]{:S(2)}, u32[]{:S(2)}) async-start(f32[16,8,256]{2,1,0:T(8,128)} %bitcast.17), calls=%async_computation.1 | async-start | bytes 262144 | tf_op jit(solution)/shard_map/all_to_all | solution.py:817
  32.4 3.6 %collective-permute-done.arrived.low = f32[5,80,256]{2,1,0:T(8,128)S(1)} collective-permute-done((f32[5,80,256]{2,1,0:T(8,128)}, f32[5,80,256]{2,1,0:T(8,128)S(1)}, u32[]{:S(2)}, u32[]{:S(2)}) %collective-permute-start) | collective-permute-done | bytes 409632 | tf_op jit(solution)/shard_map/ppermute | solution.py:39
  35.9 0.8 copy-done.2
  36.7 6.0 %shard_map.68 = (f32[2,3,256,256]{3,2,1,0:T(8,128)}, f32[5,80,256]{2,1,0:T(8,128)}) custom-call(s32[24]{0:T(128)} %get-tuple-element.27.ctl, f32[2,3,256,256]{3,2,1,0:T(8,128)} %get-tuple-element.32.state_in, f32[2,256,256]{2,1,0:T(8,128)} %bed_in.9, f32[2,3,256,256]{3,2,1,0:T(8,128)} %state_first.3, f32[2,256,256]{2,1,0:T(8,128)} %manning.3, ...), custom_call_target="tpu_custom_call" | custom-call | flops 16777216 | bytes 4194304 | tf_op jit(solution)/shard_map/pallas_call | solution.py:867
  42.8 1.2 %all-to-all-done.1 = f32[16,8,256]{2,1,0:T(8,128)S(1)} async-done(((f32[16,8,256]{2,1,0:T(8,128)}), f32[16,8,256]{2,1,0:T(8,128)S(1)}, u32[]{:S(2)}, u32[]{:S(2)}) %all-to-all-start.1) | async-done | bytes 131104 | tf_op jit(solution)/shard_map/all_to_all | solution.py:817
  44.0 0.6 copy-done.16
  44.6 0.2 copy-done.4
  44.8 5.1 %shard_map.70 = (f32[2,3,256,256]{3,2,1,0:T(8,128)}, f32[128,256]{1,0:T(8,128)}, f32[8,256]{1,0:T(8,128)}, f32[8,256]{1,0:T(8,128)}, f32[5,64,256]{2,1,0:T(8,128)}) custom-call(s32[24]{0:T(128)} %get-tuple-element.27.ctl, f32[128,256]{1,0:T(8,128)} %bitcast.15, f32[128,384]{1,0:T(8,128)} %bitcast.10, f32[8,256]{1,0:T(8,128)} %get-tuple-element.31.columns_in, ...), custom_call_target="tpu_custom_call" | custom-call | flops 8388608 | bytes 10485760 | tf_op jit(solution)/shard_map/pallas_call | solution.py:907
  49.9 0.6 collective-permute-start.3
  50.5 5.5 %all-to-all-start.2 = ((f32[16,8,256]{2,1,0:T(8,128)}), f32[16,8,256]{2,1,0:T(8,128)S(1)}, u32[]{:S(2)}, u32[]{:S(2)}) async-start(f32[16,8,256]{2,1,0:T(8,128)} %bitcast.18), calls=%async_computation.2 | async-start | bytes 262144 | tf_op jit(solution)/shard_map/all_to_all | solution.py:817
  56.1 0.8 copy-done
  56.8 6.0 %shard_map.71.rate = f32[2,3,256,256]{3,2,1,0:T(8,128)} custom-call(s32[24]{0:T(128)} %get-tuple-element.27.ctl, f32[2,3,256,256]{3,2,1,0:T(8,128)} %get-tuple-element.39.state_in.state, f32[2,256,256]{2,1,0:T(8,128)} %bed_in.9, f32[5,80,256]{2,1,0:T(8,128)} %copy-done), custom_call_target="tpu_custom_call" | custom-call | flops 16777216 | bytes 4194304 | tf_op jit(solution)/shard_map/pallas_call | solution.py:877
  62.8 2.1 %all-to-all-done.2 = f32[16,8,256]{2,1,0:T(8,128)S(1)} async-done(((f32[16,8,256]{2,1,0:T(8,128)}), f32[16,8,256]{2,1,0:T(8,128)S(1)}, u32[]{:S(2)}, u32[]{:S(2)}) %all-to-all-start.2) | async-done | bytes 131104 | tf_op jit(solution)/shard_map/all_to_all | solution.py:817
  64.9 0.6 copy-done.15
  65.7 4.0 %shard_map.72 = (f32[3,256,256]{2,1,0:T(8,128)}, f32[3,128,256]{2,1,0:T(8,128)}, f32[8,256]{1,0:T(8,128)}, f32[8,256]{1,0:T(8,128)}) custom-call(s32[24]{0:T(128)} %get-tuple-element.27.ctl, f32[128,256]{1,0:T(8,128)} %bitcast.13, f32[128,384]{1,0:T(8,128)} %bitcast.11, f32[8,256]{1,0:T(8,128)} %get-tuple-element.38.columns, ...), custom_call_target="tpu_custom_call" | custom-call | flops 8388608 | bytes 10485760 | tf_op jit(solution)/shard_map/pallas_call | solution.py:927
  69.7 0.5 collective-permute-start.4
  70.2 3.8 %shard_map.73 = (f32[3,256,256]{2,1,0:T(8,128)}, f32[3,128,256]{2,1,0:T(8,128)}, f32[8,256]{1,0:T(8,128)}, f32[8,256]{1,0:T(8,128)}) custom-call(s32[24]{0:T(128)} %get-tuple-element.27.ctl, f32[128,256]{1,0:T(8,128)} %bitcast.14, f32[128,384]{1,0:T(8,128)} %bitcast.12, f32[8,256]{1,0:T(8,128)} %get-tuple-element.38.columns, ...), custom_call_target="tpu_custom_call" | custom-call | flops 8388608 | bytes 10485760 | tf_op jit(solution)/shard_map/pallas_call | solution.py:927
  74.1 1.1 %copy-done.9 = f32[3,128,256]{2,1,0:T(8,128)S(1)} copy-done((f32[3,128,256]{2,1,0:T(8,128)S(1)}, f32[3,128,256]{2,1,0:T(8,128)}, u32[]{:S(2)}) %copy-start.9) | copy-done | bytes 393240
  75.2 6.6 %shard_map.74 = (f32[3,144,256]{2,1,0:T(8,128)S(1)}, f32[3,128,256]{2,1,0:T(8,128)S(1)}) custom-call(s32[24]{0:T(128)S(1)} %copy-done.12, f32[8,256]{1,0:T(8,128)S(1)} %copy-done.10, f32[8,256]{1,0:T(8,128)S(1)} %copy-done.13, f32[8,256]{1,0:T(8,128)S(1)} %copy-done.11, f32[5,80,256]{2,1,0:T(8,128)S(1)} %copy-done.1, f32[5,64,256]{2,1,0:T(8,128)S(1)} %copy-done.7, ...), custom_call_target="tpu_custom_call" | custom-call | flops 8388608 | bytes 4194304 | tf_op jit(solution)/shard_map/pallas_call | solution.py:942
  81.8 1.6 %collective-permute-done.4.arrived.late_in = f32[3,128,256]{2,1,0:T(8,128)S(1)} collective-permute-done((f32[3,128,256]{2,1,0:T(8,128)}, f32[3,128,256]{2,1,0:T(8,128)S(1)}, u32[]{:S(2)}, u32[]{:S(2)}) %collective-permute-start.4) | collective-permute-done | bytes 393248 | tf_op jit(solution)/shard_map/ppermute | solution.py:39
  83.5 0.6 shard_map.75
  84.1 0.4 collective-permute-start.5
  84.5 7.4 %shard_map.76.before = f32[2,3,256,256]{3,2,1,0:T(8,128)} custom-call(s32[24]{0:T(128)S(1)} %copy-done.12, f32[8,256]{1,0:T(8,128)S(1)} %copy-done.10, f32[8,256]{1,0:T(8,128)S(1)} %copy-done.13, f32[8,256]{1,0:T(8,128)S(1)} %copy-done.11, f32[5,80,256]{2,1,0:T(8,128)S(1)} %copy-done.3, f32[5,64,256]{2,1,0:T(8,128)S(1)} %copy-done.5, ...), custom_call_target="tpu_custom_call" | custom-call | flops 8388608 | bytes 4194304 | tf_op jit(solution)/shard_map/pallas_call | solution.py:960
  91.9 4.9 %collective-permute-done.5.late = f32[3,128,256]{2,1,0:T(8,128)S(1)} collective-permute-done((f32[3,128,256]{2,1,0:T(8,128)S(1)}, f32[3,128,256]{2,1,0:T(8,128)S(1)}, u32[]{:S(2)}, u32[]{:S(2)}) %collective-permute-start.5) | collective-permute-done | bytes 393248 | tf_op jit(solution)/shard_map/ppermute | solution.py:39
  96.8 1.5 %shard_map.77 = f32[2,3,256,256]{3,2,1,0:T(8,128)} custom-call(s32[24]{0:T(128)S(1)} %copy-done.12, f32[3,128,256]{2,1,0:T(8,128)S(1)} %collective-permute-done.5.late, f32[3,144,256]{2,1,0:T(8,128)S(1)} %get-tuple-element.47.order.early, f32[2,3,256,256]{3,2,1,0:T(8,128)} %shard_map.76.before), custom_call_target="tpu_custom_call", output_to_operand_aliasing={{}: (3, {})} | custom-call | flops 1048576 | bytes 4194304 | tf_op jit(solution)/shard_map/pallas_call | solution.py:975
  (34 shorter events, 0.2 us)
Async XLA Ops:
  3.6 16.4 %all-to-all-start = ((f32[16,8,384]{2,1,0:T(8,128)}), f32[16,8,384]{2,1,0:T(8,128)S(1)}, u32[]{:S(2)}, u32[]{:S(2)}) async-start(f32[16,8,384]{2,1,0:T(8,128)} %bitcast.16), calls=%async_computation | async-start | bytes 393216 | tf_op jit(solution)/shard_map/all_to_all | solution.py:817
  20.0 0.7 copy-start.14
  20.6 15.3 %collective-permute-start = (f32[5,80,256]{2,1,0:T(8,128)}, f32[5,80,256]{2,1,0:T(8,128)S(1)}, u32[]{:S(2)}, u32[]{:S(2)}) collective-permute-start(f32[5,80,256]{2,1,0:T(8,128)} %shard_map.67), channel_id=1, source_target_pairs={{0,2},{2,4},{4,6},{6,8},{8,10},{10,12},{12,14},{14,0},{1,3},{3,5},... | collective-permute-start | bytes 1228808 | tf_op jit(solution)/shard_map/ppermute | solution.py:39
  25.6 18.3 %collective-permute-start.1 = (f32[5,64,256]{2,1,0:T(8,128)}, f32[5,64,256]{2,1,0:T(8,128)S(1)}, u32[]{:S(2)}, u32[]{:S(2)}) collective-permute-start(f32[5,64,256]{2,1,0:T(8,128)} %shard_map.69), channel_id=1, source_target_pairs={{0,2},{2,4},{4,6},{6,8},{8,10},{10,12},{12,14},{14,0},{1,3},{3,5},... | collective-permute-start | bytes 983048 | tf_op jit(solution)/shard_map/ppermute | solution.py:39
  26.3 17.7 %all-to-all-start.1 = ((f32[16,8,256]{2,1,0:T(8,128)}), f32[16,8,256]{2,1,0:T(8,128)S(1)}, u32[]{:S(2)}, u32[]{:S(2)}) async-start(f32[16,8,256]{2,1,0:T(8,128)} %bitcast.17), calls=%async_computation.1 | async-start | bytes 262144 | tf_op jit(solution)/shard_map/all_to_all | solution.py:817
  35.9 0.8 copy-start.2
  42.7 13.4 %collective-permute-start.2 = (f32[5,80,256]{2,1,0:T(8,128)}, f32[5,80,256]{2,1,0:T(8,128)S(1)}, u32[]{:S(2)}, u32[]{:S(2)}) collective-permute-start(f32[5,80,256]{2,1,0:T(8,128)} %get-tuple-element.40), channel_id=1, source_target_pairs={{0,2},{2,4},{4,6},{6,8},{8,10},{10,12},{12,14},{14,0},{1,3},{3,5},... | collective-permute-start | bytes 1228808 | tf_op jit(solution)/shard_map/ppermute | solution.py:39
  44.0 0.6 copy-start.16
  44.0 0.8 copy-start.4
  49.9 15.0 %collective-permute-start.3 = (f32[5,64,256]{2,1,0:T(8,128)}, f32[5,64,256]{2,1,0:T(8,128)S(1)}, u32[]{:S(2)}, u32[]{:S(2)}) collective-permute-start(f32[5,64,256]{2,1,0:T(8,128)} %get-tuple-element.41), channel_id=1, source_target_pairs={{0,2},{2,4},{4,6},{6,8},{8,10},{10,12},{12,14},{14,0},{1,3},{3,5},... | collective-permute-start | bytes 983048 | tf_op jit(solution)/shard_map/ppermute | solution.py:39
  50.5 14.4 %all-to-all-start.2 = ((f32[16,8,256]{2,1,0:T(8,128)}), f32[16,8,256]{2,1,0:T(8,128)S(1)}, u32[]{:S(2)}, u32[]{:S(2)}) async-start(f32[16,8,256]{2,1,0:T(8,128)} %bitcast.18), calls=%async_computation.2 | async-start | bytes 262144 | tf_op jit(solution)/shard_map/all_to_all | solution.py:817
  56.1 0.8 copy-start
  64.9 0.6 copy-start.15
  64.9 0.8 copy-start.6
  69.7 13.8 %collective-permute-start.4 = (f32[3,128,256]{2,1,0:T(8,128)}, f32[3,128,256]{2,1,0:T(8,128)S(1)}, u32[]{:S(2)}, u32[]{:S(2)}) collective-permute-start(f32[3,128,256]{2,1,0:T(8,128)} %get-tuple-element.42), channel_id=1, source_target_pairs={{0,2},{2,4},{4,6},{6,8},{8,10},{10,12},{12,14},{14,0},{1,3},{3,5},... | collective-permute-start | bytes 1179656 | tf_op jit(solution)/shard_map/ppermute | solution.py:39
  70.2 3.9 %copy-start.1 = (f32[5,80,256]{2,1,0:T(8,128)S(1)}, f32[5,80,256]{2,1,0:T(8,128)}, u32[]{:S(2)}) copy-start(f32[5,80,256]{2,1,0:T(8,128)} %copy-done) | copy-start | bytes 1228804
  70.2 3.9 %copy-start.7 = (f32[5,64,256]{2,1,0:T(8,128)S(1)}, f32[5,64,256]{2,1,0:T(8,128)}, u32[]{:S(2)}) copy-start(f32[5,64,256]{2,1,0:T(8,128)} %copy-done.6) | copy-start | bytes 983044
  70.2 3.9 %copy-start.10 = (f32[8,256]{1,0:T(8,128)S(1)}, f32[8,256]{1,0:T(8,128)}, u32[]{:S(2)}) copy-start(f32[8,256]{1,0:T(8,128)} %get-tuple-element.35.first.second.delta0) | copy-start | bytes 24580
  70.2 3.9 %copy-start.11 = (f32[8,256]{1,0:T(8,128)S(1)}, f32[8,256]{1,0:T(8,128)}, u32[]{:S(2)}) copy-start(f32[8,256]{1,0:T(8,128)} %get-tuple-element.44.order.delta2) | copy-start | bytes 24580
  70.2 3.9 %copy-start.12 = (s32[24]{0:T(128)S(1)}, s32[24]{0:T(128)}, u32[]{:S(2)}) copy-start(s32[24]{0:T(128)} %get-tuple-element.27.ctl) | copy-start | bytes 292
  70.2 3.9 %copy-start.13 = (f32[8,256]{1,0:T(8,128)S(1)}, f32[8,256]{1,0:T(8,128)}, u32[]{:S(2)}) copy-start(f32[8,256]{1,0:T(8,128)} %get-tuple-element.43.delta1) | copy-start | bytes 24580
  74.0 10.4 %copy-start.3 = (f32[5,80,256]{2,1,0:T(8,128)S(1)}, f32[5,80,256]{2,1,0:T(8,128)}, u32[]{:S(2)}) copy-start(f32[5,80,256]{2,1,0:T(8,128)} %copy-done.2) | copy-start | bytes 1228804
  74.0 10.4 %copy-start.5 = (f32[5,64,256]{2,1,0:T(8,128)S(1)}, f32[5,64,256]{2,1,0:T(8,128)}, u32[]{:S(2)}) copy-start(f32[5,64,256]{2,1,0:T(8,128)} %copy-done.4) | copy-start | bytes 983044
  74.0 10.4 %copy-start.8 = (f32[3,256,256]{2,1,0:T(8,128)S(1)}, f32[3,256,256]{2,1,0:T(8,128)}, u32[]{:S(2)}) copy-start(f32[3,256,256]{2,1,0:T(8,128)} %get-tuple-element.48.staying) | copy-start | bytes 2359300
  74.1 1.1 %copy-start.9 = (f32[3,128,256]{2,1,0:T(8,128)S(1)}, f32[3,128,256]{2,1,0:T(8,128)}, u32[]{:S(2)}) copy-start(f32[3,128,256]{2,1,0:T(8,128)} %get-tuple-element.45.late) | copy-start | bytes 1179652
  84.1 12.7 %collective-permute-start.5 = (f32[3,128,256]{2,1,0:T(8,128)S(1)}, f32[3,128,256]{2,1,0:T(8,128)S(1)}, u32[]{:S(2)}, u32[]{:S(2)}) collective-permute-start(f32[3,128,256]{2,1,0:T(8,128)S(1)} %shard_map.75), channel_id=1, source_target_pairs={{0,2},{2,4},{4,6},{6,8},{8,10},{10,12},{12,14},{14,0},{1,3},{3,5},... | collective-permute-start | bytes 1179656 | tf_op jit(solution)/shard_map/ppermute | solution.py:39

commit v21 on v20

--- a/solution.py
+++ b/solution.py
@@ -19,9 +19,9 @@
 SLOT_LOW, WALL_WEST, WALL_EAST, WALL_OUTER, WET, MOVE = 0, 1, 3, 5, 7, 13
 WET_FIRST, WET_SECOND = 16, 19
 CONTROLS = 24
-EARLY = 144
-PIECES = ((0, 80), (80, 144))
-AGAIN = 16
+EARLY = 160
+PIECES = ((0, 72), (72, 160))
+AGAIN = 32
 LATE = TILE - EARLY + 16
 CHUNKS = 8
 PARTS = 8
@@ -147,9 +147,9 @@
 
 
 def opening(
-    state_in, bed_in, manning_in, neighbours_in, wet_in, moves_in,
-    out, columns, ctl, leaving_low, leaving_high,
-    state, bed, manning, neighbours, wet, moves, sems,
+    state_in, bed_in, neighbours_in, wet_in, moves_in,
+    out, columns, ctl,
+    state, bed, neighbours, wet, moves, sems,
 ):
     copies = start_all(
         (
@@ -177,8 +177,6 @@
         for slot in range(2):
             ctl[WET + 2 * step + slot] = wet[step, first + slot]
         ctl[MOVE + step] = moves[step, device]
-    moving = moves[0, device]
-    rough = start_all(((manning_in.at[moving, 0:EARLY], manning),), sems, 6)
     count = lax.axis_size("xb")
     upper = lax.axis_index("yb")
     column = lax.axis_index("xb")
@@ -193,20 +191,9 @@
         ctl[WET_FIRST + step] = wet[step, tile_first]
         ctl[WET_SECOND + step] = wet[step, tile_second]
 
-    wait_all(copies[3:] + rough)
-    early = []
-    for (begin, end), leaving in zip(PIECES, (leaving_low, leaving_high)):
-        early += start_all(
-            (
-                (state.at[moving, :, begin:end], leaving.at[0:3]),
-                (bed.at[moving, begin:end], leaving.at[3]),
-                (manning.at[begin:end], leaving.at[4]),
-            ),
-            sems,
-            7 + len(early),
-        )
     total = jnp.zeros((ROWS, TILE), jnp.float32)
     for slot in range(2):
+        copies[3 + slot].wait()
 
         def group(index, best, slot=slot):
             rows = pl.ds(pl.multiple_of(index * ROWS, ROWS), ROWS)
@@ -215,12 +202,42 @@
 
         best = lax.fori_loop(0, TILE // ROWS, group, jnp.zeros((ROWS, TILE), jnp.float32))
         total = jnp.maximum(total, jnp.where(wet[0, first + slot] > 0, best, 0.0))
+    copies[5].wait()
     messages(ctl, state, bed, jnp.max(total, keepdims=True), out, columns)
-    wait_all(early)
 
 
 def hold(first, second, leaving, same):
     del first, second, leaving, same
+
+
+class Splitting:
+    def __init__(self, ctl, state_in, bed_in, manning_in, leaving, buffer, sems):
+        slot = ctl[MOVE]
+        rows = slice(0, EARLY)
+        pairs = (
+            (state_in.at[slot, :, rows], buffer.at[0:3]),
+            (bed_in.at[slot, rows], buffer.at[3]),
+            (manning_in.at[slot, rows], buffer.at[4]),
+        )
+        self.incoming = [
+            pltpu.make_async_copy(src, dst, sems.at[k]) for k, (src, dst) in enumerate(pairs)
+        ]
+        self.outgoing = [
+            pltpu.make_async_copy(buffer.at[:, begin:end], piece, sems.at[3 + k])
+            for k, ((begin, end), piece) in enumerate(zip(PIECES, leaving))
+        ]
+
+    def start(self):
+        for copy in self.incoming:
+            copy.start()
+
+    def middle(self):
+        wait_all(self.incoming)
+        for copy in self.outgoing:
+            copy.start()
+
+    def end(self):
+        wait_all(self.outgoing)
 
 
 class Passing:
@@ -254,6 +271,15 @@
 
     def end(self):
         self.outgoing.wait()
+
+
+def rates_and_splitting(
+    ctl, state_in, bed_in, manning_in, rate_out, leaving_low, leaving_high,
+    state, bed, rate, sems, buffer, moving,
+):
+    leaving = leaving_low, leaving_high
+    splitting = Splitting(ctl, state_in, bed_in, manning_in, leaving, buffer, moving)
+    rates(ctl, state_in, bed_in, rate_out, state, bed, rate, sems, splitting)
 
 
 def rates_and_leaving(
@@ -832,27 +858,25 @@
         return pltpu.VMEM(like.shape, jnp.float32)
 
     piece_shapes = tuple(f32(5, end - begin, TILE) for begin, end in PIECES)
-    out, columns, ctl, *leaving = call(
+    out, columns, ctl = call(
         opening,
         (
             f32(8 * devices, TILE + LANES),
             f32(8, TILE),
             jax.ShapeDtypeStruct((CONTROLS,), jnp.int32),
-        )
-        + piece_shapes,
-        (vmem(), vmem(), smem(), hbm(), hbm()),
-        [hbm()] * 6,
+        ),
+        (vmem(), vmem(), smem()),
+        [hbm()] * 5,
         4 << 20,
         [
             whole,
             part,
-            pltpu.VMEM((EARLY, TILE), jnp.float32),
             pltpu.SMEM(neighbours.shape[::-1], jnp.int32),
             pltpu.SMEM(wet.shape, jnp.int32),
             pltpu.SMEM(moves.shape, jnp.int32),
-            pltpu.SemaphoreType.DMA((13,)),
+            pltpu.SemaphoreType.DMA((6,)),
         ],
-    )(state, bed, manning, neighbours.T, wet, moves)
+    )(state, bed, neighbours.T, wet, moves)
     state_first = state
     ground = None
     deltas = []
@@ -878,9 +902,14 @@
                 ctl, state, bed, early_second[0]
             )
         else:
-            rate = call(rates, shape, hbm(), [smem(), hbm(), hbm()], 16 << 20, scratch)(
-                ctl, state, bed
-            )
+            rate, *leaving = call(
+                rates_and_splitting,
+                (shape,) + piece_shapes,
+                (hbm(),) * 3,
+                [smem()] + [hbm()] * 3,
+                16 << 20,
+                scratch + [buffer(early_shape), pltpu.SemaphoreType.DMA((5,))],
+            )(ctl, state, bed, manning)
             held = call(
                 hold, piece_shapes[0], hbm(), [hbm()] * 3, 1 << 10, aliases={2: 0}
             )(rate, got, leaving[0])

time: 99.1 us -> 118 us (1.19)
  waiting for transfers between devices: 16.4 us -> 44.3 us
  Pallas kernels: 55.5 us -> 47 us
    ppermute x6, waiting for transfers between devices: 10.1 us -> 41.3 us  [shifted(): return lax.ppermute(value, axis, pairs)]
    pallas_call x1, Pallas kernels: 7.43 us -> 1.51 us  [body(): call(repeat_first, shape, hbm(), [smem()] + [vmem()] * 3 + [anywhere()] *...]
    all_to_all x3, waiting for transfers between devices: 6.32 us -> 2.97 us  [spread(): lax.all_to_all(fast, ('xb', 'yb'), split_axis=0, concat_axis=0, tiled=True)]
    pallas_call x1, Pallas kernels: 6.64 us -> 5.09 us  [body(): call(repeat_second, (early_state, late_shape), (anywhere(), vmem()), [sme...]
    ppermute x6, starting transfers between devices: 2.2 us -> 0.84 us  [shifted(): return lax.ppermute(value, axis, pairs)]
    unnamed x34 -> x36, local copies, waits for them, and re-layouts: 4.9 us -> 4.87 us
  transfers between devices with their start and end apart: 9 -> 9, of which waited for: 6 -> 4; matrix products, arithmetic and copies ran while one was open for 0% -> 0% of each run, Pallas kernels for 47% -> 24%
where the time goes in v21:
time: 118 us; the launch traced here: 117 us
  Pallas kernels  47 us (40%)
  waiting for transfers between devices  44.3 us (38%)
  starting transfers between devices  20.9 us (18%)
  local copies, waits for them, and re-layouts  4.87 us (4%)
    ppermute x6, waiting for transfers between devices, shifted(): return lax.ppermute(value, axis, pairs)  41.3 us
    all_to_all x3, starting transfers between devices, spread(): lax.all_to_all(fast, ('xb', 'yb'), split_axis=0, concat_axis=0, tiled=True)  20.1 us
    pallas_call x2, Pallas kernels, body(): call(functools.partial(update_and_leaving if passing else update, step),...  9.89 us
    pallas_call x2, Pallas kernels, finish_step(): call(functools.partial(last_update, moving), (tile_shape,) + shapes + (de...  7.76 us
    pallas_call x1, Pallas kernels, body(): call(rates_and_splitting, (shape,) + piece_shapes, (hbm(),) * 3, [smem()]...  6.02 us
    pallas_call x1, Pallas kernels, body(): call(rates_and_leaving, (shape, piece_shapes[0]), (hbm(),) * 2, [smem()]...  5.98 us
    pallas_call x1, Pallas kernels, body(): call(rates_after, shape, hbm(), [smem()] + [hbm()] * 3, 16 << 20, scratch)  5.96 us
    pallas_call x1, Pallas kernels, body(): call(repeat_second, (early_state, late_shape), (anywhere(), vmem()), [sme...  5.09 us
  transfers between devices with their start and end apart: 9, of which 4 were waited for; matrix products, arithmetic and copies ran while one was open for 0% of the time, Pallas kernels for 24%

profile of v21, /device:TPU:0, one launch (start us, length us, event | category | flops | bytes accessed | tf_op | source)
XLA Modules:
  0.0 117.5 jit_solution(1924871758580947934)
XLA Ops:
  0.0 2.7 %shard_map.64 = (f32[128,384]{1,0:T(8,128)}, f32[8,256]{1,0:T(8,128)}, s32[24]{0:T(128)}) custom-call(f32[2,3,256,256]{3,2,1,0:T(8,128)} %state_first.3, f32[2,256,256]{2,1,0:T(8,128)} %bed_in.9, s32[4,32]{1,0:T(4,128)} %bitcast.18, s32[3,32]{1,0:T(4,128)} %wet_in.1, s32[3,16]{1,0:T(4,128)} %moves_in.1), custom_call_target="tpu_custom_call" | custom-call | flops 4194304 | bytes 4194304 | tf_op jit(solution)/shard_map/pallas_call | solution.py:861
  2.7 7.4 %all-to-all-start = ((f32[16,8,384]{2,1,0:T(8,128)}), f32[16,8,384]{2,1,0:T(8,128)S(1)}, u32[]{:S(2)}, u32[]{:S(2)}) async-start(f32[16,8,384]{2,1,0:T(8,128)} %bitcast.16), calls=%async_computation | async-start | bytes 393216 | tf_op jit(solution)/shard_map/all_to_all | solution.py:843
  10.1 6.0 %shard_map.65 = (f32[2,3,256,256]{3,2,1,0:T(8,128)}, f32[5,72,256]{2,1,0:T(8,128)}, f32[5,88,256]{2,1,0:T(8,128)}) custom-call(s32[24]{0:T(128)} %get-tuple-element.28.ctl, f32[2,3,256,256]{3,2,1,0:T(8,128)} %state_first.3, f32[2,256,256]{2,1,0:T(8,128)} %bed_in.9, f32[2,256,256]{2,1,0:T(8,128)} %manning.3), custom_call_target="tpu_custom_call" | custom-call | flops 16777216 | bytes 4194304 | tf_op jit(solution)/shard_map/pallas_call | solution.py:905
  16.1 3.0 %all-to-all-done = f32[16,8,384]{2,1,0:T(8,128)S(1)} async-done(((f32[16,8,384]{2,1,0:T(8,128)}), f32[16,8,384]{2,1,0:T(8,128)S(1)}, u32[]{:S(2)}, u32[]{:S(2)}) %all-to-all-start) | async-done | bytes 196640 | tf_op jit(solution)/shard_map/all_to_all | solution.py:843
  19.1 0.7 copy-done.14
  19.8 4.9 %shard_map.66 = (f32[2,3,256,256]{3,2,1,0:T(8,128)}, f32[128,256]{1,0:T(8,128)}, f32[8,256]{1,0:T(8,128)}, f32[8,256]{1,0:T(8,128)}) custom-call(s32[24]{0:T(128)} %get-tuple-element.28.ctl, f32[128,384]{1,0:T(8,128)} %bitcast.7, f32[128,384]{1,0:T(8,128)} %bitcast.8, f32[8,256]{1,0:T(8,128)} %get-tuple-element.30.columns_in, ...), custom_call_target="tpu_custom_call" | custom-call | flops 8388608 | bytes 10485760 | tf_op jit(solution)/shard_map/pallas_call | solution.py:936
  24.7 0.5 collective-permute-start
  25.3 6.1 %all-to-all-start.1 = ((f32[16,8,256]{2,1,0:T(8,128)}), f32[16,8,256]{2,1,0:T(8,128)S(1)}, u32[]{:S(2)}, u32[]{:S(2)}) async-start(f32[16,8,256]{2,1,0:T(8,128)} %bitcast.3), calls=%async_computation.1 | async-start | bytes 262144 | tf_op jit(solution)/shard_map/all_to_all | solution.py:843
  31.4 17.3 %collective-permute-done.arrived.low = f32[5,72,256]{2,1,0:T(8,128)S(1)} collective-permute-done((f32[5,72,256]{2,1,0:T(8,128)}, f32[5,72,256]{2,1,0:T(8,128)S(1)}, u32[]{:S(2)}, u32[]{:S(2)}) %collective-permute-start) | collective-permute-done | bytes 368672 | tf_op jit(solution)/shard_map/ppermute | solution.py:39
  48.7 0.7 copy-done.4
  49.4 6.0 %shard_map.68 = (f32[2,3,256,256]{3,2,1,0:T(8,128)}, f32[5,72,256]{2,1,0:T(8,128)}) custom-call(s32[24]{0:T(128)} %get-tuple-element.28.ctl, f32[2,3,256,256]{3,2,1,0:T(8,128)} %get-tuple-element.34.state_in, f32[2,256,256]{2,1,0:T(8,128)} %bed_in.9, f32[2,3,256,256]{3,2,1,0:T(8,128)} %state_first.3, f32[2,256,256]{2,1,0:T(8,128)} %manning.3, ...), custom_call_target="tpu_custom_call" | custom-call | flops 16777216 | bytes 4194304 | tf_op jit(solution)/shard_map/pallas_call | solution.py:891
  55.5 0.6 copy-done.16
  56.1 0.2 copy-done.2
  56.3 5.0 %shard_map.70 = (f32[2,3,256,256]{3,2,1,0:T(8,128)}, f32[128,256]{1,0:T(8,128)}, f32[8,256]{1,0:T(8,128)}, f32[8,256]{1,0:T(8,128)}, f32[5,88,256]{2,1,0:T(8,128)}) custom-call(s32[24]{0:T(128)} %get-tuple-element.28.ctl, f32[128,256]{1,0:T(8,128)} %bitcast.15, f32[128,384]{1,0:T(8,128)} %bitcast.10, f32[8,256]{1,0:T(8,128)} %get-tuple-element.33.columns_in, ...), custom_call_target="tpu_custom_call" | custom-call | flops 8388608 | bytes 10485760 | tf_op jit(solution)/shard_map/pallas_call | solution.py:936
  61.3 0.1 collective-permute-start.3
  61.4 0.1 collective-permute-start.2
  61.4 6.6 %all-to-all-start.2 = ((f32[16,8,256]{2,1,0:T(8,128)}), f32[16,8,256]{2,1,0:T(8,128)S(1)}, u32[]{:S(2)}, u32[]{:S(2)}) async-start(f32[16,8,256]{2,1,0:T(8,128)} %bitcast.17), calls=%async_computation.2 | async-start | bytes 262144 | tf_op jit(solution)/shard_map/all_to_all | solution.py:843
  68.0 15.4 %collective-permute-done.2.order.low = f32[5,72,256]{2,1,0:T(8,128)S(1)} collective-permute-done((f32[5,72,256]{2,1,0:T(8,128)S(1)}, f32[5,72,256]{2,1,0:T(8,128)S(1)}, u32[]{:S(2)}, u32[]{:S(2)}) %collective-permute-start.2) | collective-permute-done | bytes 368672 | tf_op jit(solution)/shard_map/ppermute | solution.py:39
  83.4 0.7 copy-done.6
  84.1 6.0 %shard_map.71.rate = f32[2,3,256,256]{3,2,1,0:T(8,128)} custom-call(s32[24]{0:T(128)} %get-tuple-element.28.ctl, f32[2,3,256,256]{3,2,1,0:T(8,128)} %get-tuple-element.41.state_in.state, f32[2,256,256]{2,1,0:T(8,128)} %bed_in.9, f32[5,72,256]{2,1,0:T(8,128)} %copy-done.6), custom_call_target="tpu_custom_call" | custom-call | flops 16777216 | bytes 4194304 | tf_op jit(solution)/shard_map/pallas_call | solution.py:901
  90.1 0.6 copy-done.15
  90.7 0.2 copy-done
  90.9 3.9 %shard_map.72 = (f32[3,256,256]{2,1,0:T(8,128)}, f32[3,112,256]{2,1,0:T(8,128)}, f32[8,256]{1,0:T(8,128)}, f32[8,256]{1,0:T(8,128)}) custom-call(s32[24]{0:T(128)} %get-tuple-element.28.ctl, f32[128,256]{1,0:T(8,128)} %bitcast.13, f32[128,384]{1,0:T(8,128)} %bitcast.11, f32[8,256]{1,0:T(8,128)} %get-tuple-element.40.columns, ...), custom_call_target="tpu_custom_call" | custom-call | flops 8388608 | bytes 10485760 | tf_op jit(solution)/shard_map/pallas_call | solution.py:956
  94.9 0.1 collective-permute-start.4
  95.0 3.8 %shard_map.73 = (f32[3,256,256]{2,1,0:T(8,128)}, f32[3,112,256]{2,1,0:T(8,128)}, f32[8,256]{1,0:T(8,128)}, f32[8,256]{1,0:T(8,128)}) custom-call(s32[24]{0:T(128)} %get-tuple-element.28.ctl, f32[128,256]{1,0:T(8,128)} %bitcast.14, f32[128,384]{1,0:T(8,128)} %bitcast.12, f32[8,256]{1,0:T(8,128)} %get-tuple-element.40.columns, ...), custom_call_target="tpu_custom_call" | custom-call | flops 8388608 | bytes 10485760 | tf_op jit(solution)/shard_map/pallas_call | solution.py:956
  98.9 1.1 copy-done.9
  100.0 5.1 %shard_map.74 = (f32[3,160,256]{2,1,0:T(8,128)S(1)}, f32[3,112,256]{2,1,0:T(8,128)S(1)}) custom-call(s32[24]{0:T(128)S(1)} %copy-done.12, f32[8,256]{1,0:T(8,128)S(1)} %copy-done.10, f32[8,256]{1,0:T(8,128)S(1)} %copy-done.13, f32[8,256]{1,0:T(8,128)S(1)} %copy-done.11, f32[5,72,256]{2,1,0:T(8,128)S(1)} %copy-done.7, f32[5,88,256]{2,1,0:T(8,128)S(1)} %copy-done.1, ...), custom_call_target="tpu_custom_call" | custom-call | flops 8388608 | bytes 4194304 | tf_op jit(solution)/shard_map/pallas_call | solution.py:971
  105.1 0.6 shard_map.75
  105.7 0.1 collective-permute-start.5
  105.8 1.5 %shard_map.76.before = f32[2,3,256,256]{3,2,1,0:T(8,128)} custom-call(s32[24]{0:T(128)S(1)} %copy-done.12, f32[8,256]{1,0:T(8,128)S(1)} %copy-done.10, f32[8,256]{1,0:T(8,128)S(1)} %copy-done.13, f32[8,256]{1,0:T(8,128)S(1)} %copy-done.11, f32[5,72,256]{2,1,0:T(8,128)S(1)} %copy-done.5, f32[5,88,256]{2,1,0:T(8,128)S(1)} %copy-done.3, ...), custom_call_target="tpu_custom_call" | custom-call | flops 8388608 | bytes 4194304 | tf_op jit(solution)/shard_map/pallas_call | solution.py:989
  107.3 8.6 %collective-permute-done.5.late = f32[3,112,256]{2,1,0:T(8,128)S(1)} collective-permute-done((f32[3,112,256]{2,1,0:T(8,128)S(1)}, f32[3,112,256]{2,1,0:T(8,128)S(1)}, u32[]{:S(2)}, u32[]{:S(2)}) %collective-permute-start.5) | collective-permute-done | bytes 344096 | tf_op jit(solution)/shard_map/ppermute | solution.py:39
  115.9 1.5 %shard_map.77 = f32[2,3,256,256]{3,2,1,0:T(8,128)} custom-call(s32[24]{0:T(128)S(1)} %copy-done.12, f32[3,112,256]{2,1,0:T(8,128)S(1)} %collective-permute-done.5.late, f32[3,160,256]{2,1,0:T(8,128)S(1)} %get-tuple-element.49.order.early, f32[2,3,256,256]{3,2,1,0:T(8,128)} %shard_map.76.before), custom_call_target="tpu_custom_call", output_to_operand_aliasing={{}: (3, {})} | custom-call | flops 1048576 | bytes 4194304 | tf_op jit(solution)/shard_map/pallas_call | solution.py:1004
  (36 shorter events, 0.1 us)
Async XLA Ops:
  2.7 16.4 %all-to-all-start = ((f32[16,8,384]{2,1,0:T(8,128)}), f32[16,8,384]{2,1,0:T(8,128)S(1)}, u32[]{:S(2)}, u32[]{:S(2)}) async-start(f32[16,8,384]{2,1,0:T(8,128)} %bitcast.16), calls=%async_computation | async-start | bytes 393216 | tf_op jit(solution)/shard_map/all_to_all | solution.py:843
  19.1 0.7 copy-start.14
  24.7 30.8 %collective-permute-start.1 = (f32[5,88,256]{2,1,0:T(8,128)}, f32[5,88,256]{2,1,0:T(8,128)S(1)}, u32[]{:S(2)}, u32[]{:S(2)}) collective-permute-start(f32[5,88,256]{2,1,0:T(8,128)} %shard_map.69), channel_id=1, source_target_pairs={{0,2},{2,4},{4,6},{6,8},{8,10},{10,12},{12,14},{14,0},{1,3},{3,5},... | collective-permute-start | bytes 1351688 | tf_op jit(solution)/shard_map/ppermute | solution.py:39
  24.7 24.0 %collective-permute-start = (f32[5,72,256]{2,1,0:T(8,128)}, f32[5,72,256]{2,1,0:T(8,128)S(1)}, u32[]{:S(2)}, u32[]{:S(2)}) collective-permute-start(f32[5,72,256]{2,1,0:T(8,128)} %shard_map.67), channel_id=1, source_target_pairs={{0,2},{2,4},{4,6},{6,8},{8,10},{10,12},{12,14},{14,0},{1,3},{3,5},... | collective-permute-start | bytes 1105928 | tf_op jit(solution)/shard_map/ppermute | solution.py:39
  25.3 30.1 %all-to-all-start.1 = ((f32[16,8,256]{2,1,0:T(8,128)}), f32[16,8,256]{2,1,0:T(8,128)S(1)}, u32[]{:S(2)}, u32[]{:S(2)}) async-start(f32[16,8,256]{2,1,0:T(8,128)} %bitcast.3), calls=%async_computation.1 | async-start | bytes 262144 | tf_op jit(solution)/shard_map/all_to_all | solution.py:843
  48.7 0.7 copy-start.4
  55.4 0.6 copy-start.16
  55.5 0.8 copy-start.2
  56.3 5.1 %copy-start.17 = (f32[5,72,256]{2,1,0:T(8,128)S(1)}, f32[5,72,256]{2,1,0:T(8,128)}, u32[]{:S(2)}) copy-start(f32[5,72,256]{2,1,0:T(8,128)} %get-tuple-element.42) | copy-start | bytes 1105924
  61.3 28.8 %collective-permute-start.3 = (f32[5,88,256]{2,1,0:T(8,128)}, f32[5,88,256]{2,1,0:T(8,128)S(1)}, u32[]{:S(2)}, u32[]{:S(2)}) collective-permute-start(f32[5,88,256]{2,1,0:T(8,128)} %get-tuple-element.43), channel_id=1, source_target_pairs={{0,2},{2,4},{4,6},{6,8},{8,10},{10,12},{12,14},{14,0},{1,3},{3,5},... | collective-permute-start | bytes 1351688 | tf_op jit(solution)/shard_map/ppermute | solution.py:39
  61.4 22.0 %collective-permute-start.2 = (f32[5,72,256]{2,1,0:T(8,128)S(1)}, f32[5,72,256]{2,1,0:T(8,128)S(1)}, u32[]{:S(2)}, u32[]{:S(2)}) collective-permute-start(f32[5,72,256]{2,1,0:T(8,128)S(1)} %copy-done.17), channel_id=1, source_target_pairs={{0,2},{2,4},{4,6},{6,8},{8,10},{10,12},{12,14},{14,0},{1,3},{3,5},... | collective-permute-start | bytes 1105928 | tf_op jit(solution)/shard_map/ppermute | solution.py:39
  61.4 28.6 %all-to-all-start.2 = ((f32[16,8,256]{2,1,0:T(8,128)}), f32[16,8,256]{2,1,0:T(8,128)S(1)}, u32[]{:S(2)}, u32[]{:S(2)}) async-start(f32[16,8,256]{2,1,0:T(8,128)} %bitcast.17), calls=%async_computation.2 | async-start | bytes 262144 | tf_op jit(solution)/shard_map/all_to_all | solution.py:843
  83.4 0.7 copy-start.6
  90.1 0.6 copy-start.15
  90.1 0.8 copy-start
  94.9 10.2 %collective-permute-start.4 = (f32[3,112,256]{2,1,0:T(8,128)}, f32[3,112,256]{2,1,0:T(8,128)S(1)}, u32[]{:S(2)}, u32[]{:S(2)}) collective-permute-start(f32[3,112,256]{2,1,0:T(8,128)} %get-tuple-element.44), channel_id=1, source_target_pairs={{0,2},{2,4},{4,6},{6,8},{8,10},{10,12},{12,14},{14,0},{1,3},{3,5},... | collective-permute-start | bytes 1032200 | tf_op jit(solution)/shard_map/ppermute | solution.py:39
  94.9 3.9 %copy-start.1 = (f32[5,88,256]{2,1,0:T(8,128)S(1)}, f32[5,88,256]{2,1,0:T(8,128)}, u32[]{:S(2)}) copy-start(f32[5,88,256]{2,1,0:T(8,128)} %copy-done) | copy-start | bytes 1351684
  94.9 3.9 %copy-start.7 = (f32[5,72,256]{2,1,0:T(8,128)S(1)}, f32[5,72,256]{2,1,0:T(8,128)}, u32[]{:S(2)}) copy-start(f32[5,72,256]{2,1,0:T(8,128)} %copy-done.6) | copy-start | bytes 1105924
  94.9 3.9 %copy-start.10 = (f32[8,256]{1,0:T(8,128)S(1)}, f32[8,256]{1,0:T(8,128)}, u32[]{:S(2)}) copy-start(f32[8,256]{1,0:T(8,128)} %get-tuple-element.37.first.second.delta0) | copy-start | bytes 24580
  94.9 3.9 %copy-start.11 = (f32[8,256]{1,0:T(8,128)S(1)}, f32[8,256]{1,0:T(8,128)}, u32[]{:S(2)}) copy-start(f32[8,256]{1,0:T(8,128)} %get-tuple-element.46.order.delta2) | copy-start | bytes 24580
  95.0 3.9 %copy-start.12 = (s32[24]{0:T(128)S(1)}, s32[24]{0:T(128)}, u32[]{:S(2)}) copy-start(s32[24]{0:T(128)} %get-tuple-element.28.ctl) | copy-start | bytes 292
  95.0 3.9 %copy-start.13 = (f32[8,256]{1,0:T(8,128)S(1)}, f32[8,256]{1,0:T(8,128)}, u32[]{:S(2)}) copy-start(f32[8,256]{1,0:T(8,128)} %get-tuple-element.45.delta1) | copy-start | bytes 24580
  98.8 6.9 %copy-start.3 = (f32[5,88,256]{2,1,0:T(8,128)S(1)}, f32[5,88,256]{2,1,0:T(8,128)}, u32[]{:S(2)}) copy-start(f32[5,88,256]{2,1,0:T(8,128)} %copy-done.2) | copy-start | bytes 1351684
  98.8 6.9 %copy-start.5 = (f32[5,72,256]{2,1,0:T(8,128)S(1)}, f32[5,72,256]{2,1,0:T(8,128)}, u32[]{:S(2)}) copy-start(f32[5,72,256]{2,1,0:T(8,128)} %copy-done.4) | copy-start | bytes 1105924
  98.8 6.9 %copy-start.8 = (f32[3,256,256]{2,1,0:T(8,128)S(1)}, f32[3,256,256]{2,1,0:T(8,128)}, u32[]{:S(2)}) copy-start(f32[3,256,256]{2,1,0:T(8,128)} %get-tuple-element.50.staying) | copy-start | bytes 2359300
  98.9 1.1 copy-start.9
  105.7 10.2 %collective-permute-start.5 = (f32[3,112,256]{2,1,0:T(8,128)S(1)}, f32[3,112,256]{2,1,0:T(8,128)S(1)}, u32[]{:S(2)}, u32[]{:S(2)}) collective-permute-start(f32[3,112,256]{2,1,0:T(8,128)S(1)} %shard_map.75), channel_id=1, source_target_pairs={{0,2},{2,4},{4,6},{6,8},{8,10},{10,12},{12,14},{14,0},{1,3},{3,5},... | collective-permute-start | bytes 1032200 | tf_op jit(solution)/shard_map/ppermute | solution.py:39

commit v22 on v21

--- a/solution.py
+++ b/solution.py
@@ -20,7 +20,7 @@
 WET_FIRST, WET_SECOND = 16, 19
 CONTROLS = 24
 EARLY = 160
-PIECES = ((0, 72), (72, 160))
+PIECES = ((0, 80), (80, 160))
 AGAIN = 32
 LATE = TILE - EARLY + 16
 CHUNKS = 8

time: 118 us -> 104 us (0.88)
  waiting for transfers between devices: 44.3 us -> 16.2 us
  starting transfers between devices: 20.9 us -> 31.1 us
  Pallas kernels: 47 us -> 51.2 us
    ppermute x6, waiting for transfers between devices: 41.3 us -> 9.06 us  [shifted(): return lax.ppermute(value, axis, pairs)]
    ppermute x6, starting transfers between devices: 0.84 us -> 12.8 us  [shifted(): return lax.ppermute(value, axis, pairs)]
    pallas_call x1, Pallas kernels: 1.51 us -> 5.82 us  [body(): call(repeat_first, shape, hbm(), [smem()] + [vmem()] * 3 + [anywhere()] *...]
    all_to_all x3, waiting for transfers between devices: 2.97 us -> 7.11 us  [spread(): lax.all_to_all(fast, ('xb', 'yb'), split_axis=0, concat_axis=0, tiled=True)]
    all_to_all x3, starting transfers between devices: 20.1 us -> 18.3 us  [spread(): lax.all_to_all(fast, ('xb', 'yb'), split_axis=0, concat_axis=0, tiled=True)]
    unnamed x36 -> x34, local copies, waits for them, and re-layouts: 4.87 us -> 4.92 us
  transfers between devices with their start and end apart: 9 -> 9, of which waited for: 4 -> 6; matrix products, arithmetic and copies ran while one was open for 0% -> 0% of each run, Pallas kernels for 24% -> 41%
where the time goes in v22:
time: 104 us
  Pallas kernels  51.2 us (49%)
  starting transfers between devices  31.1 us (30%)
  waiting for transfers between devices  16.2 us (16%)
  local copies, waits for them, and re-layouts  4.92 us (5%)
    all_to_all x3, starting transfers between devices, spread(): lax.all_to_all(fast, ('xb', 'yb'), split_axis=0, concat_axis=0, tiled=True)  18.3 us
    ppermute x6, starting transfers between devices, shifted(): return lax.ppermute(value, axis, pairs)  12.8 us
    pallas_call x2, Pallas kernels, body(): call(functools.partial(update_and_leaving if passing else update, step),...  9.75 us
    ppermute x6, waiting for transfers between devices, shifted(): return lax.ppermute(value, axis, pairs)  9.06 us
    pallas_call x2, Pallas kernels, finish_step(): call(functools.partial(last_update, moving), (tile_shape,) + shapes + (de...  7.78 us
    all_to_all x3, waiting for transfers between devices, spread(): lax.all_to_all(fast, ('xb', 'yb'), split_axis=0, concat_axis=0, tiled=True)  7.11 us
    pallas_call x1, Pallas kernels, body(): call(rates_and_splitting, (shape,) + piece_shapes, (hbm(),) * 3, [smem()]...  6.02 us
    pallas_call x1, Pallas kernels, body(): call(rates_and_leaving, (shape, piece_shapes[0]), (hbm(),) * 2, [smem()]...  5.98 us
  transfers between devices with their start and end apart: 9, of which 6 were waited for; matrix products, arithmetic and copies ran while one was open for 0% of the time, Pallas kernels for 41%

profile of v22, /device:TPU:0, one launch (start us, length us, event | category | flops | bytes accessed | tf_op | source)
XLA Modules:
  0.0 103.7 jit_solution(13614495198476659827)
XLA Ops:
  0.0 2.7 %shard_map.64 = (f32[128,384]{1,0:T(8,128)}, f32[8,256]{1,0:T(8,128)}, s32[24]{0:T(128)}) custom-call(f32[2,3,256,256]{3,2,1,0:T(8,128)} %state_first.3, f32[2,256,256]{2,1,0:T(8,128)} %bed_in.9, s32[4,32]{1,0:T(4,128)} %bitcast.19, s32[3,32]{1,0:T(4,128)} %wet_in.1, s32[3,16]{1,0:T(4,128)} %moves_in.1), custom_call_target="tpu_custom_call" | custom-call | flops 4194304 | bytes 4194304 | tf_op jit(solution)/shard_map/pallas_call | solution.py:861
  2.7 7.4 %all-to-all-start = ((f32[16,8,384]{2,1,0:T(8,128)}), f32[16,8,384]{2,1,0:T(8,128)S(1)}, u32[]{:S(2)}, u32[]{:S(2)}) async-start(f32[16,8,384]{2,1,0:T(8,128)} %bitcast.16), calls=%async_computation | async-start | bytes 393216 | tf_op jit(solution)/shard_map/all_to_all | solution.py:843
  10.1 6.0 %shard_map.65 = (f32[2,3,256,256]{3,2,1,0:T(8,128)}, f32[5,80,256]{2,1,0:T(8,128)}, f32[5,80,256]{2,1,0:T(8,128)}) custom-call(s32[24]{0:T(128)} %get-tuple-element.28.ctl, f32[2,3,256,256]{3,2,1,0:T(8,128)} %state_first.3, f32[2,256,256]{2,1,0:T(8,128)} %bed_in.9, f32[2,256,256]{2,1,0:T(8,128)} %manning.3), custom_call_target="tpu_custom_call" | custom-call | flops 16777216 | bytes 4194304 | tf_op jit(solution)/shard_map/pallas_call | solution.py:905
  16.1 3.0 %all-to-all-done = f32[16,8,384]{2,1,0:T(8,128)S(1)} async-done(((f32[16,8,384]{2,1,0:T(8,128)}), f32[16,8,384]{2,1,0:T(8,128)S(1)}, u32[]{:S(2)}, u32[]{:S(2)}) %all-to-all-start) | async-done | bytes 196640 | tf_op jit(solution)/shard_map/all_to_all | solution.py:843
  19.1 0.7 copy-done.14
  19.7 4.9 %shard_map.66 = (f32[2,3,256,256]{3,2,1,0:T(8,128)}, f32[128,256]{1,0:T(8,128)}, f32[8,256]{1,0:T(8,128)}, f32[8,256]{1,0:T(8,128)}) custom-call(s32[24]{0:T(128)} %get-tuple-element.28.ctl, f32[128,384]{1,0:T(8,128)} %bitcast.8, f32[128,384]{1,0:T(8,128)} %bitcast.9, f32[8,256]{1,0:T(8,128)} %get-tuple-element.30.columns_in, ...), custom_call_target="tpu_custom_call" | custom-call | flops 8388608 | bytes 10485760 | tf_op jit(solution)/shard_map/pallas_call | solution.py:936
  24.6 0.6 collective-permute-start.1
  25.3 6.1 %all-to-all-start.1 = ((f32[16,8,256]{2,1,0:T(8,128)}), f32[16,8,256]{2,1,0:T(8,128)S(1)}, u32[]{:S(2)}, u32[]{:S(2)}) async-start(f32[16,8,256]{2,1,0:T(8,128)} %bitcast.17), calls=%async_computation.1 | async-start | bytes 262144 | tf_op jit(solution)/shard_map/all_to_all | solution.py:843
  31.4 3.7 %collective-permute-done.arrived.low = f32[5,80,256]{2,1,0:T(8,128)S(1)} collective-permute-done((f32[5,80,256]{2,1,0:T(8,128)}, f32[5,80,256]{2,1,0:T(8,128)S(1)}, u32[]{:S(2)}, u32[]{:S(2)}) %collective-permute-start) | collective-permute-done | bytes 409632 | tf_op jit(solution)/shard_map/ppermute | solution.py:39
  35.1 0.8 copy-done.4
  35.8 6.0 %shard_map.68 = (f32[2,3,256,256]{3,2,1,0:T(8,128)}, f32[5,80,256]{2,1,0:T(8,128)}) custom-call(s32[24]{0:T(128)} %get-tuple-element.28.ctl, f32[2,3,256,256]{3,2,1,0:T(8,128)} %get-tuple-element.34.state_in, f32[2,256,256]{2,1,0:T(8,128)} %bed_in.9, f32[2,3,256,256]{3,2,1,0:T(8,128)} %state_first.3, f32[2,256,256]{2,1,0:T(8,128)} %manning.3, ...), custom_call_target="tpu_custom_call" | custom-call | flops 16777216 | bytes 4194304 | tf_op jit(solution)/shard_map/pallas_call | solution.py:891
  41.9 3.0 %all-to-all-done.1 = f32[16,8,256]{2,1,0:T(8,128)S(1)} async-done(((f32[16,8,256]{2,1,0:T(8,128)}), f32[16,8,256]{2,1,0:T(8,128)S(1)}, u32[]{:S(2)}, u32[]{:S(2)}) %all-to-all-start.1) | async-done | bytes 131104 | tf_op jit(solution)/shard_map/all_to_all | solution.py:843
  44.9 0.6 copy-done.16
  45.7 4.9 %shard_map.70 = (f32[2,3,256,256]{3,2,1,0:T(8,128)}, f32[128,256]{1,0:T(8,128)}, f32[8,256]{1,0:T(8,128)}, f32[8,256]{1,0:T(8,128)}, f32[5,80,256]{2,1,0:T(8,128)}) custom-call(s32[24]{0:T(128)} %get-tuple-element.28.ctl, f32[128,256]{1,0:T(8,128)} %bitcast.15, f32[128,384]{1,0:T(8,128)} %bitcast.10, f32[8,256]{1,0:T(8,128)} %get-tuple-element.33.columns_in, ...), custom_call_target="tpu_custom_call" | custom-call | flops 8388608 | bytes 10485760 | tf_op jit(solution)/shard_map/pallas_call | solution.py:936
  50.5 9.6 %collective-permute-start.3 = (f32[5,80,256]{2,1,0:T(8,128)}, f32[5,80,256]{2,1,0:T(8,128)S(1)}, u32[]{:S(2)}, u32[]{:S(2)}) collective-permute-start(f32[5,80,256]{2,1,0:T(8,128)} %get-tuple-element.43), channel_id=1, source_target_pairs={{0,2},{2,4},{4,6},{6,8},{8,10},{10,12},{12,14},{14,0},{1,3},{3,5},... | collective-permute-start | bytes 1228808 | tf_op jit(solution)/shard_map/ppermute | solution.py:39
  60.2 4.8 %all-to-all-start.2 = ((f32[16,8,256]{2,1,0:T(8,128)}), f32[16,8,256]{2,1,0:T(8,128)S(1)}, u32[]{:S(2)}, u32[]{:S(2)}) async-start(f32[16,8,256]{2,1,0:T(8,128)} %bitcast.18), calls=%async_computation.2 | async-start | bytes 262144 | tf_op jit(solution)/shard_map/all_to_all | solution.py:843
  65.0 0.8 copy-done
  65.8 6.0 %shard_map.71.rate = f32[2,3,256,256]{3,2,1,0:T(8,128)} custom-call(s32[24]{0:T(128)} %get-tuple-element.28.ctl, f32[2,3,256,256]{3,2,1,0:T(8,128)} %get-tuple-element.41.state_in.state, f32[2,256,256]{2,1,0:T(8,128)} %bed_in.9, f32[5,80,256]{2,1,0:T(8,128)} %copy-done), custom_call_target="tpu_custom_call" | custom-call | flops 16777216 | bytes 4194304 | tf_op jit(solution)/shard_map/pallas_call | solution.py:901
  71.7 1.2 %all-to-all-done.2 = f32[16,8,256]{2,1,0:T(8,128)S(1)} async-done(((f32[16,8,256]{2,1,0:T(8,128)}), f32[16,8,256]{2,1,0:T(8,128)S(1)}, u32[]{:S(2)}, u32[]{:S(2)}) %all-to-all-start.2) | async-done | bytes 131104 | tf_op jit(solution)/shard_map/all_to_all | solution.py:843
  72.9 0.6 copy-done.15
  73.6 0.2 copy-done.2
  73.7 3.7 %shard_map.72 = (f32[3,256,256]{2,1,0:T(8,128)}, f32[3,112,256]{2,1,0:T(8,128)}, f32[8,256]{1,0:T(8,128)}, f32[8,256]{1,0:T(8,128)}) custom-call(s32[24]{0:T(128)} %get-tuple-element.28.ctl, f32[128,256]{1,0:T(8,128)} %bitcast.13, f32[128,384]{1,0:T(8,128)} %bitcast.11, f32[8,256]{1,0:T(8,128)} %get-tuple-element.40.columns, ...), custom_call_target="tpu_custom_call" | custom-call | flops 8388608 | bytes 10485760 | tf_op jit(solution)/shard_map/pallas_call | solution.py:956
  77.4 1.1 %collective-permute-start.4 = (f32[3,112,256]{2,1,0:T(8,128)}, f32[3,112,256]{2,1,0:T(8,128)S(1)}, u32[]{:S(2)}, u32[]{:S(2)}) collective-permute-start(f32[3,112,256]{2,1,0:T(8,128)} %get-tuple-element.44), channel_id=1, source_target_pairs={{0,2},{2,4},{4,6},{6,8},{8,10},{10,12},{12,14},{14,0},{1,3},{3,5},... | collective-permute-start | bytes 1032200 | tf_op jit(solution)/shard_map/ppermute | solution.py:39
  78.6 4.1 %shard_map.73 = (f32[3,256,256]{2,1,0:T(8,128)}, f32[3,112,256]{2,1,0:T(8,128)}, f32[8,256]{1,0:T(8,128)}, f32[8,256]{1,0:T(8,128)}) custom-call(s32[24]{0:T(128)} %get-tuple-element.28.ctl, f32[128,256]{1,0:T(8,128)} %bitcast.14, f32[128,384]{1,0:T(8,128)} %bitcast.12, f32[8,256]{1,0:T(8,128)} %get-tuple-element.40.columns, ...), custom_call_target="tpu_custom_call" | custom-call | flops 8388608 | bytes 10485760 | tf_op jit(solution)/shard_map/pallas_call | solution.py:956
  82.8 1.1 %copy-done.9 = f32[3,112,256]{2,1,0:T(8,128)S(1)} copy-done((f32[3,112,256]{2,1,0:T(8,128)S(1)}, f32[3,112,256]{2,1,0:T(8,128)}, u32[]{:S(2)}) %copy-start.9) | copy-done | bytes 344088
  83.9 5.1 %shard_map.74 = (f32[3,160,256]{2,1,0:T(8,128)S(1)}, f32[3,112,256]{2,1,0:T(8,128)S(1)}) custom-call(s32[24]{0:T(128)S(1)} %copy-done.12, f32[8,256]{1,0:T(8,128)S(1)} %copy-done.10, f32[8,256]{1,0:T(8,128)S(1)} %copy-done.13, f32[8,256]{1,0:T(8,128)S(1)} %copy-done.11, f32[5,80,256]{2,1,0:T(8,128)S(1)} %copy-done.1, f32[5,80,256]{2,1,0:T(8,128)S(1)} %copy-done.3, ...), custom_call_target="tpu_custom_call" | custom-call | flops 8388608 | bytes 4194304 | tf_op jit(solution)/shard_map/pallas_call | solution.py:971
  89.0 1.0 %collective-permute-done.4.arrived.late_in = f32[3,112,256]{2,1,0:T(8,128)S(1)} collective-permute-done((f32[3,112,256]{2,1,0:T(8,128)}, f32[3,112,256]{2,1,0:T(8,128)S(1)}, u32[]{:S(2)}, u32[]{:S(2)}) %collective-permute-start.4) | collective-permute-done | bytes 344096 | tf_op jit(solution)/shard_map/ppermute | solution.py:39
  90.0 0.6 shard_map.75
  90.6 1.4 %collective-permute-start.5 = (f32[3,112,256]{2,1,0:T(8,128)S(1)}, f32[3,112,256]{2,1,0:T(8,128)S(1)}, u32[]{:S(2)}, u32[]{:S(2)}) collective-permute-start(f32[3,112,256]{2,1,0:T(8,128)S(1)} %shard_map.75), channel_id=1, source_target_pairs={{0,2},{2,4},{4,6},{6,8},{8,10},{10,12},{12,14},{14,0},{1,3},{3,5},... | collective-permute-start | bytes 1032200 | tf_op jit(solution)/shard_map/ppermute | solution.py:39
  92.0 5.8 %shard_map.76.before = f32[2,3,256,256]{3,2,1,0:T(8,128)} custom-call(s32[24]{0:T(128)S(1)} %copy-done.12, f32[8,256]{1,0:T(8,128)S(1)} %copy-done.10, f32[8,256]{1,0:T(8,128)S(1)} %copy-done.13, f32[8,256]{1,0:T(8,128)S(1)} %copy-done.11, f32[5,80,256]{2,1,0:T(8,128)S(1)} %copy-done.5, f32[5,80,256]{2,1,0:T(8,128)S(1)} %copy-done.7, ...), custom_call_target="tpu_custom_call" | custom-call | flops 8388608 | bytes 4194304 | tf_op jit(solution)/shard_map/pallas_call | solution.py:989
  97.8 4.3 %collective-permute-done.5.late = f32[3,112,256]{2,1,0:T(8,128)S(1)} collective-permute-done((f32[3,112,256]{2,1,0:T(8,128)S(1)}, f32[3,112,256]{2,1,0:T(8,128)S(1)}, u32[]{:S(2)}, u32[]{:S(2)}) %collective-permute-start.5) | collective-permute-done | bytes 344096 | tf_op jit(solution)/shard_map/ppermute | solution.py:39
  102.1 1.5 %shard_map.77 = f32[2,3,256,256]{3,2,1,0:T(8,128)} custom-call(s32[24]{0:T(128)S(1)} %copy-done.12, f32[3,112,256]{2,1,0:T(8,128)S(1)} %collective-permute-done.5.late, f32[3,160,256]{2,1,0:T(8,128)S(1)} %get-tuple-element.49.order.early, f32[2,3,256,256]{3,2,1,0:T(8,128)} %shard_map.76.before), custom_call_target="tpu_custom_call", output_to_operand_aliasing={{}: (3, {})} | custom-call | flops 1048576 | bytes 4194304 | tf_op jit(solution)/shard_map/pallas_call | solution.py:1004
  (34 shorter events, 0.3 us)
Async XLA Ops:
  2.7 16.4 %all-to-all-start = ((f32[16,8,384]{2,1,0:T(8,128)}), f32[16,8,384]{2,1,0:T(8,128)S(1)}, u32[]{:S(2)}, u32[]{:S(2)}) async-start(f32[16,8,384]{2,1,0:T(8,128)} %bitcast.16), calls=%async_computation | async-start | bytes 393216 | tf_op jit(solution)/shard_map/all_to_all | solution.py:843
  19.1 0.7 copy-start.14
  19.7 15.3 %collective-permute-start = (f32[5,80,256]{2,1,0:T(8,128)}, f32[5,80,256]{2,1,0:T(8,128)S(1)}, u32[]{:S(2)}, u32[]{:S(2)}) collective-permute-start(f32[5,80,256]{2,1,0:T(8,128)} %shard_map.67), channel_id=1, source_target_pairs={{0,2},{2,4},{4,6},{6,8},{8,10},{10,12},{12,14},{14,0},{1,3},{3,5},... | collective-permute-start | bytes 1228808 | tf_op jit(solution)/shard_map/ppermute | solution.py:39
  24.6 20.2 %collective-permute-start.1 = (f32[5,80,256]{2,1,0:T(8,128)}, f32[5,80,256]{2,1,0:T(8,128)S(1)}, u32[]{:S(2)}, u32[]{:S(2)}) collective-permute-start(f32[5,80,256]{2,1,0:T(8,128)} %shard_map.69), channel_id=1, source_target_pairs={{0,2},{2,4},{4,6},{6,8},{8,10},{10,12},{12,14},{14,0},{1,3},{3,5},... | collective-permute-start | bytes 1228808 | tf_op jit(solution)/shard_map/ppermute | solution.py:39
  25.3 19.6 %all-to-all-start.1 = ((f32[16,8,256]{2,1,0:T(8,128)}), f32[16,8,256]{2,1,0:T(8,128)S(1)}, u32[]{:S(2)}, u32[]{:S(2)}) async-start(f32[16,8,256]{2,1,0:T(8,128)} %bitcast.17), calls=%async_computation.1 | async-start | bytes 262144 | tf_op jit(solution)/shard_map/all_to_all | solution.py:843
  35.1 0.8 copy-start.4
  41.8 23.2 %collective-permute-start.2 = (f32[5,80,256]{2,1,0:T(8,128)}, f32[5,80,256]{2,1,0:T(8,128)S(1)}, u32[]{:S(2)}, u32[]{:S(2)}) collective-permute-start(f32[5,80,256]{2,1,0:T(8,128)} %get-tuple-element.42), channel_id=1, source_target_pairs={{0,2},{2,4},{4,6},{6,8},{8,10},{10,12},{12,14},{14,0},{1,3},{3,5},... | collective-permute-start | bytes 1228808 | tf_op jit(solution)/shard_map/ppermute | solution.py:39
  44.9 0.7 copy-start.16
  44.9 0.8 copy-start.6
  50.5 22.4 %collective-permute-start.3 = (f32[5,80,256]{2,1,0:T(8,128)}, f32[5,80,256]{2,1,0:T(8,128)S(1)}, u32[]{:S(2)}, u32[]{:S(2)}) collective-permute-start(f32[5,80,256]{2,1,0:T(8,128)} %get-tuple-element.43), channel_id=1, source_target_pairs={{0,2},{2,4},{4,6},{6,8},{8,10},{10,12},{12,14},{14,0},{1,3},{3,5},... | collective-permute-start | bytes 1228808 | tf_op jit(solution)/shard_map/ppermute | solution.py:39
  60.2 12.8 %all-to-all-start.2 = ((f32[16,8,256]{2,1,0:T(8,128)}), f32[16,8,256]{2,1,0:T(8,128)S(1)}, u32[]{:S(2)}, u32[]{:S(2)}) async-start(f32[16,8,256]{2,1,0:T(8,128)} %bitcast.18), calls=%async_computation.2 | async-start | bytes 262144 | tf_op jit(solution)/shard_map/all_to_all | solution.py:843
  65.0 0.8 copy-start
  72.9 0.7 copy-start.15
  72.9 0.8 copy-start.2
  77.4 12.6 %collective-permute-start.4 = (f32[3,112,256]{2,1,0:T(8,128)}, f32[3,112,256]{2,1,0:T(8,128)S(1)}, u32[]{:S(2)}, u32[]{:S(2)}) collective-permute-start(f32[3,112,256]{2,1,0:T(8,128)} %get-tuple-element.44), channel_id=1, source_target_pairs={{0,2},{2,4},{4,6},{6,8},{8,10},{10,12},{12,14},{14,0},{1,3},{3,5},... | collective-permute-start | bytes 1032200 | tf_op jit(solution)/shard_map/ppermute | solution.py:39
  78.5 4.2 %copy-start.1 = (f32[5,80,256]{2,1,0:T(8,128)S(1)}, f32[5,80,256]{2,1,0:T(8,128)}, u32[]{:S(2)}) copy-start(f32[5,80,256]{2,1,0:T(8,128)} %copy-done) | copy-start | bytes 1228804
  78.5 4.2 %copy-start.3 = (f32[5,80,256]{2,1,0:T(8,128)S(1)}, f32[5,80,256]{2,1,0:T(8,128)}, u32[]{:S(2)}) copy-start(f32[5,80,256]{2,1,0:T(8,128)} %copy-done.2) | copy-start | bytes 1228804
  78.5 4.2 %copy-start.10 = (f32[8,256]{1,0:T(8,128)S(1)}, f32[8,256]{1,0:T(8,128)}, u32[]{:S(2)}) copy-start(f32[8,256]{1,0:T(8,128)} %get-tuple-element.37.first.second.delta0) | copy-start | bytes 24580
  78.5 4.2 %copy-start.11 = (f32[8,256]{1,0:T(8,128)S(1)}, f32[8,256]{1,0:T(8,128)}, u32[]{:S(2)}) copy-start(f32[8,256]{1,0:T(8,128)} %get-tuple-element.46.order.delta2) | copy-start | bytes 24580
  78.5 4.2 %copy-start.12 = (s32[24]{0:T(128)S(1)}, s32[24]{0:T(128)}, u32[]{:S(2)}) copy-start(s32[24]{0:T(128)} %get-tuple-element.28.ctl) | copy-start | bytes 292
  78.6 4.2 %copy-start.13 = (f32[8,256]{1,0:T(8,128)S(1)}, f32[8,256]{1,0:T(8,128)}, u32[]{:S(2)}) copy-start(f32[8,256]{1,0:T(8,128)} %get-tuple-element.45.delta1) | copy-start | bytes 24580
  82.7 9.3 %copy-start.5 = (f32[5,80,256]{2,1,0:T(8,128)S(1)}, f32[5,80,256]{2,1,0:T(8,128)}, u32[]{:S(2)}) copy-start(f32[5,80,256]{2,1,0:T(8,128)} %copy-done.4) | copy-start | bytes 1228804
  82.7 9.3 %copy-start.7 = (f32[5,80,256]{2,1,0:T(8,128)S(1)}, f32[5,80,256]{2,1,0:T(8,128)}, u32[]{:S(2)}) copy-start(f32[5,80,256]{2,1,0:T(8,128)} %copy-done.6) | copy-start | bytes 1228804
  82.7 9.3 %copy-start.8 = (f32[3,256,256]{2,1,0:T(8,128)S(1)}, f32[3,256,256]{2,1,0:T(8,128)}, u32[]{:S(2)}) copy-start(f32[3,256,256]{2,1,0:T(8,128)} %get-tuple-element.50.staying) | copy-start | bytes 2359300
  82.8 1.1 %copy-start.9 = (f32[3,112,256]{2,1,0:T(8,128)S(1)}, f32[3,112,256]{2,1,0:T(8,128)}, u32[]{:S(2)}) copy-start(f32[3,112,256]{2,1,0:T(8,128)} %get-tuple-element.47.late) | copy-start | bytes 1032196
  90.6 11.6 %collective-permute-start.5 = (f32[3,112,256]{2,1,0:T(8,128)S(1)}, f32[3,112,256]{2,1,0:T(8,128)S(1)}, u32[]{:S(2)}, u32[]{:S(2)}) collective-permute-start(f32[3,112,256]{2,1,0:T(8,128)S(1)} %shard_map.75), channel_id=1, source_target_pairs={{0,2},{2,4},{4,6},{6,8},{8,10},{10,12},{12,14},{14,0},{1,3},{3,5},... | collective-permute-start | bytes 1032200 | tf_op jit(solution)/shard_map/ppermute | solution.py:39

commit v23 on v22

--- a/solution.py
+++ b/solution.py
@@ -19,8 +19,8 @@
 SLOT_LOW, WALL_WEST, WALL_EAST, WALL_OUTER, WET, MOVE = 0, 1, 3, 5, 7, 13
 WET_FIRST, WET_SECOND = 16, 19
 CONTROLS = 24
-EARLY = 160
-PIECES = ((0, 80), (80, 160))
+EARLY = 128
+PIECES = ((0, 64), (64, 128))
 AGAIN = 32
 LATE = TILE - EARLY + 16
 CHUNKS = 8

time: 104 us -> 98.6 us (0.948)
  starting transfers between devices: 31.1 us -> 21.2 us
  waiting for transfers between devices: 16.2 us -> 22.2 us
  Pallas kernels: 51.2 us -> 49.7 us
    ppermute x6, starting transfers between devices: 12.8 us -> 2.43 us  [shifted(): return lax.ppermute(value, axis, pairs)]
    ppermute x6, waiting for transfers between devices: 9.06 us -> 15.8 us  [shifted(): return lax.ppermute(value, axis, pairs)]
  transfers between devices with their start and end apart: 9 -> 9, of which waited for: 6 -> 6; matrix products, arithmetic and copies ran while one was open for 0% -> 0% of each run, Pallas kernels for 41% -> 42%
where the time goes in v23:
time: 98.6 us; the launch traced here: 98.3 us
  Pallas kernels  49.7 us (50%)
  waiting for transfers between devices  22.2 us (23%)
  starting transfers between devices  21.2 us (22%)
  local copies, waits for them, and re-layouts  4.86 us (5%)
    all_to_all x3, starting transfers between devices, spread(): lax.all_to_all(fast, ('xb', 'yb'), split_axis=0, concat_axis=0, tiled=True)  18.8 us
    ppermute x6, waiting for transfers between devices, shifted(): return lax.ppermute(value, axis, pairs)  15.8 us
    pallas_call x2, Pallas kernels, body(): call(functools.partial(update_and_leaving if passing else update, step),...  9.79 us
    pallas_call x2, Pallas kernels, finish_step(): call(functools.partial(last_update, moving), (tile_shape,) + shapes + (de...  7.84 us
    all_to_all x3, waiting for transfers between devices, spread(): lax.all_to_all(fast, ('xb', 'yb'), split_axis=0, concat_axis=0, tiled=True)  6.45 us
    pallas_call x1, Pallas kernels, body(): call(rates_and_splitting, (shape,) + piece_shapes, (hbm(),) * 3, [smem()]...  6.02 us
    pallas_call x1, Pallas kernels, body(): call(rates_and_leaving, (shape, piece_shapes[0]), (hbm(),) * 2, [smem()]...  5.98 us
    pallas_call x1, Pallas kernels, body(): call(rates_after, shape, hbm(), [smem()] + [hbm()] * 3, 16 << 20, scratch)  5.96 us
  transfers between devices with their start and end apart: 9, of which 6 were waited for; matrix products, arithmetic and copies ran while one was open for 0% of the time, Pallas kernels for 42%

profile of v23, /device:TPU:0, one launch (start us, length us, event | category | flops | bytes accessed | tf_op | source)
XLA Modules:
  0.0 98.3 jit_solution(13099394222423705064)
XLA Ops:
  0.0 2.7 %shard_map.64 = (f32[128,384]{1,0:T(8,128)}, f32[8,256]{1,0:T(8,128)}, s32[24]{0:T(128)}) custom-call(f32[2,3,256,256]{3,2,1,0:T(8,128)} %state_first.3, f32[2,256,256]{2,1,0:T(8,128)} %bed_in.9, s32[4,32]{1,0:T(4,128)} %bitcast.19, s32[3,32]{1,0:T(4,128)} %wet_in.1, s32[3,16]{1,0:T(4,128)} %moves_in.1), custom_call_target="tpu_custom_call" | custom-call | flops 4194304 | bytes 4194304 | tf_op jit(solution)/shard_map/pallas_call | solution.py:861
  2.7 7.4 %all-to-all-start = ((f32[16,8,384]{2,1,0:T(8,128)}), f32[16,8,384]{2,1,0:T(8,128)S(1)}, u32[]{:S(2)}, u32[]{:S(2)}) async-start(f32[16,8,384]{2,1,0:T(8,128)} %bitcast.16), calls=%async_computation | async-start | bytes 393216 | tf_op jit(solution)/shard_map/all_to_all | solution.py:843
  10.1 6.0 %shard_map.65 = (f32[2,3,256,256]{3,2,1,0:T(8,128)}, f32[5,64,256]{2,1,0:T(8,128)}, f32[5,64,256]{2,1,0:T(8,128)}) custom-call(s32[24]{0:T(128)} %get-tuple-element.28.ctl, f32[2,3,256,256]{3,2,1,0:T(8,128)} %state_first.3, f32[2,256,256]{2,1,0:T(8,128)} %bed_in.9, f32[2,256,256]{2,1,0:T(8,128)} %manning.3), custom_call_target="tpu_custom_call" | custom-call | flops 16777216 | bytes 4194304 | tf_op jit(solution)/shard_map/pallas_call | solution.py:905
  16.1 3.0 %all-to-all-done = f32[16,8,384]{2,1,0:T(8,128)S(1)} async-done(((f32[16,8,384]{2,1,0:T(8,128)}), f32[16,8,384]{2,1,0:T(8,128)S(1)}, u32[]{:S(2)}, u32[]{:S(2)}) %all-to-all-start) | async-done | bytes 196640 | tf_op jit(solution)/shard_map/all_to_all | solution.py:843
  19.1 0.7 copy-done.14
  19.8 4.9 %shard_map.66 = (f32[2,3,256,256]{3,2,1,0:T(8,128)}, f32[128,256]{1,0:T(8,128)}, f32[8,256]{1,0:T(8,128)}, f32[8,256]{1,0:T(8,128)}) custom-call(s32[24]{0:T(128)} %get-tuple-element.28.ctl, f32[128,384]{1,0:T(8,128)} %bitcast.8, f32[128,384]{1,0:T(8,128)} %bitcast.9, f32[8,256]{1,0:T(8,128)} %get-tuple-element.30.columns_in, ...), custom_call_target="tpu_custom_call" | custom-call | flops 8388608 | bytes 10485760 | tf_op jit(solution)/shard_map/pallas_call | solution.py:936
  24.7 0.6 collective-permute-start.1
  25.3 6.1 %all-to-all-start.1 = ((f32[16,8,256]{2,1,0:T(8,128)}), f32[16,8,256]{2,1,0:T(8,128)S(1)}, u32[]{:S(2)}, u32[]{:S(2)}) async-start(f32[16,8,256]{2,1,0:T(8,128)} %bitcast.17), calls=%async_computation.1 | async-start | bytes 262144 | tf_op jit(solution)/shard_map/all_to_all | solution.py:843
  31.4 1.9 %collective-permute-done.arrived.low = f32[5,64,256]{2,1,0:T(8,128)S(1)} collective-permute-done((f32[5,64,256]{2,1,0:T(8,128)}, f32[5,64,256]{2,1,0:T(8,128)S(1)}, u32[]{:S(2)}, u32[]{:S(2)}) %collective-permute-start) | collective-permute-done | bytes 327712 | tf_op jit(solution)/shard_map/ppermute | solution.py:39
  33.3 0.7 copy-done
  34.0 6.0 %shard_map.68 = (f32[2,3,256,256]{3,2,1,0:T(8,128)}, f32[5,64,256]{2,1,0:T(8,128)}) custom-call(s32[24]{0:T(128)} %get-tuple-element.28.ctl, f32[2,3,256,256]{3,2,1,0:T(8,128)} %get-tuple-element.34.state_in, f32[2,256,256]{2,1,0:T(8,128)} %bed_in.9, f32[2,3,256,256]{3,2,1,0:T(8,128)} %state_first.3, f32[2,256,256]{2,1,0:T(8,128)} %manning.3, ...), custom_call_target="tpu_custom_call" | custom-call | flops 16777216 | bytes 4194304 | tf_op jit(solution)/shard_map/pallas_call | solution.py:891
  40.1 1.2 %all-to-all-done.1 = f32[16,8,256]{2,1,0:T(8,128)S(1)} async-done(((f32[16,8,256]{2,1,0:T(8,128)}), f32[16,8,256]{2,1,0:T(8,128)S(1)}, u32[]{:S(2)}, u32[]{:S(2)}) %all-to-all-start.1) | async-done | bytes 131104 | tf_op jit(solution)/shard_map/all_to_all | solution.py:843
  41.4 0.6 copy-done.16
  42.0 0.1 copy-done.2
  42.1 4.9 %shard_map.70 = (f32[2,3,256,256]{3,2,1,0:T(8,128)}, f32[128,256]{1,0:T(8,128)}, f32[8,256]{1,0:T(8,128)}, f32[8,256]{1,0:T(8,128)}, f32[5,64,256]{2,1,0:T(8,128)}) custom-call(s32[24]{0:T(128)} %get-tuple-element.28.ctl, f32[128,256]{1,0:T(8,128)} %bitcast.15, f32[128,384]{1,0:T(8,128)} %bitcast.10, f32[8,256]{1,0:T(8,128)} %get-tuple-element.33.columns_in, ...), custom_call_target="tpu_custom_call" | custom-call | flops 8388608 | bytes 10485760 | tf_op jit(solution)/shard_map/pallas_call | solution.py:936
  47.1 0.8 collective-permute-start.3
  47.9 5.3 %all-to-all-start.2 = ((f32[16,8,256]{2,1,0:T(8,128)}), f32[16,8,256]{2,1,0:T(8,128)S(1)}, u32[]{:S(2)}, u32[]{:S(2)}) async-start(f32[16,8,256]{2,1,0:T(8,128)} %bitcast.18), calls=%async_computation.2 | async-start | bytes 262144 | tf_op jit(solution)/shard_map/all_to_all | solution.py:843
  53.2 0.7 copy-done.4
  54.0 6.0 %shard_map.71.rate = f32[2,3,256,256]{3,2,1,0:T(8,128)} custom-call(s32[24]{0:T(128)} %get-tuple-element.28.ctl, f32[2,3,256,256]{3,2,1,0:T(8,128)} %get-tuple-element.41.state_in.state, f32[2,256,256]{2,1,0:T(8,128)} %bed_in.9, f32[5,64,256]{2,1,0:T(8,128)} %copy-done.4), custom_call_target="tpu_custom_call" | custom-call | flops 16777216 | bytes 4194304 | tf_op jit(solution)/shard_map/pallas_call | solution.py:901
  59.9 2.2 %all-to-all-done.2 = f32[16,8,256]{2,1,0:T(8,128)S(1)} async-done(((f32[16,8,256]{2,1,0:T(8,128)}), f32[16,8,256]{2,1,0:T(8,128)S(1)}, u32[]{:S(2)}, u32[]{:S(2)}) %all-to-all-start.2) | async-done | bytes 131104 | tf_op jit(solution)/shard_map/all_to_all | solution.py:843
  62.2 0.6 copy-done.15
  62.8 0.1 copy-done.6
  63.0 4.0 %shard_map.72 = (f32[3,256,256]{2,1,0:T(8,128)}, f32[3,144,256]{2,1,0:T(8,128)}, f32[8,256]{1,0:T(8,128)}, f32[8,256]{1,0:T(8,128)}) custom-call(s32[24]{0:T(128)} %get-tuple-element.28.ctl, f32[128,256]{1,0:T(8,128)} %bitcast.13, f32[128,384]{1,0:T(8,128)} %bitcast.11, f32[8,256]{1,0:T(8,128)} %get-tuple-element.40.columns, ...), custom_call_target="tpu_custom_call" | custom-call | flops 8388608 | bytes 10485760 | tf_op jit(solution)/shard_map/pallas_call | solution.py:956
  67.0 0.8 collective-permute-start.4
  67.8 3.8 %shard_map.73 = (f32[3,256,256]{2,1,0:T(8,128)}, f32[3,144,256]{2,1,0:T(8,128)}, f32[8,256]{1,0:T(8,128)}, f32[8,256]{1,0:T(8,128)}) custom-call(s32[24]{0:T(128)} %get-tuple-element.28.ctl, f32[128,256]{1,0:T(8,128)} %bitcast.14, f32[128,384]{1,0:T(8,128)} %bitcast.12, f32[8,256]{1,0:T(8,128)} %get-tuple-element.40.columns, ...), custom_call_target="tpu_custom_call" | custom-call | flops 8388608 | bytes 10485760 | tf_op jit(solution)/shard_map/pallas_call | solution.py:956
  71.8 1.1 %copy-done.9 = f32[3,144,256]{2,1,0:T(8,128)S(1)} copy-done((f32[3,144,256]{2,1,0:T(8,128)S(1)}, f32[3,144,256]{2,1,0:T(8,128)}, u32[]{:S(2)}) %copy-start.9) | copy-done | bytes 442392
  72.9 4.3 %shard_map.74 = (f32[3,128,256]{2,1,0:T(8,128)S(1)}, f32[3,144,256]{2,1,0:T(8,128)S(1)}) custom-call(s32[24]{0:T(128)S(1)} %copy-done.12, f32[8,256]{1,0:T(8,128)S(1)} %copy-done.10, f32[8,256]{1,0:T(8,128)S(1)} %copy-done.13, f32[8,256]{1,0:T(8,128)S(1)} %copy-done.11, f32[5,64,256]{2,1,0:T(8,128)S(1)} %copy-done.5, f32[5,64,256]{2,1,0:T(8,128)S(1)} %copy-done.7, ...), custom_call_target="tpu_custom_call" | custom-call | flops 8388608 | bytes 4194304 | tf_op jit(solution)/shard_map/pallas_call | solution.py:971
  77.1 5.0 %collective-permute-done.4.arrived.late_in = f32[3,144,256]{2,1,0:T(8,128)S(1)} collective-permute-done((f32[3,144,256]{2,1,0:T(8,128)}, f32[3,144,256]{2,1,0:T(8,128)S(1)}, u32[]{:S(2)}, u32[]{:S(2)}) %collective-permute-start.4) | collective-permute-done | bytes 442400 | tf_op jit(solution)/shard_map/ppermute | solution.py:39
  82.1 0.6 shard_map.75
  82.8 5.1 %shard_map.76.before = f32[2,3,256,256]{3,2,1,0:T(8,128)} custom-call(s32[24]{0:T(128)S(1)} %copy-done.12, f32[8,256]{1,0:T(8,128)S(1)} %copy-done.10, f32[8,256]{1,0:T(8,128)S(1)} %copy-done.13, f32[8,256]{1,0:T(8,128)S(1)} %copy-done.11, f32[5,64,256]{2,1,0:T(8,128)S(1)} %copy-done.1, f32[5,64,256]{2,1,0:T(8,128)S(1)} %copy-done.3, ...), custom_call_target="tpu_custom_call" | custom-call | flops 8388608 | bytes 4194304 | tf_op jit(solution)/shard_map/pallas_call | solution.py:989
  87.9 8.9 %collective-permute-done.5.late = f32[3,144,256]{2,1,0:T(8,128)S(1)} collective-permute-done((f32[3,144,256]{2,1,0:T(8,128)S(1)}, f32[3,144,256]{2,1,0:T(8,128)S(1)}, u32[]{:S(2)}, u32[]{:S(2)}) %collective-permute-start.5) | collective-permute-done | bytes 442400 | tf_op jit(solution)/shard_map/ppermute | solution.py:39
  96.8 1.5 %shard_map.77 = f32[2,3,256,256]{3,2,1,0:T(8,128)} custom-call(s32[24]{0:T(128)S(1)} %copy-done.12, f32[3,144,256]{2,1,0:T(8,128)S(1)} %collective-permute-done.5.late, f32[3,128,256]{2,1,0:T(8,128)S(1)} %get-tuple-element.49.order.early, f32[2,3,256,256]{3,2,1,0:T(8,128)} %shard_map.76.before), custom_call_target="tpu_custom_call", output_to_operand_aliasing={{}: (3, {})} | custom-call | flops 1048576 | bytes 4194304 | tf_op jit(solution)/shard_map/pallas_call | solution.py:1004
  (34 shorter events, 0.2 us)
Async XLA Ops:
  2.7 16.4 %all-to-all-start = ((f32[16,8,384]{2,1,0:T(8,128)}), f32[16,8,384]{2,1,0:T(8,128)S(1)}, u32[]{:S(2)}, u32[]{:S(2)}) async-start(f32[16,8,384]{2,1,0:T(8,128)} %bitcast.16), calls=%async_computation | async-start | bytes 393216 | tf_op jit(solution)/shard_map/all_to_all | solution.py:843
  19.1 0.7 copy-start.14
  19.8 13.5 %collective-permute-start = (f32[5,64,256]{2,1,0:T(8,128)}, f32[5,64,256]{2,1,0:T(8,128)S(1)}, u32[]{:S(2)}, u32[]{:S(2)}) collective-permute-start(f32[5,64,256]{2,1,0:T(8,128)} %shard_map.67), channel_id=1, source_target_pairs={{0,2},{2,4},{4,6},{6,8},{8,10},{10,12},{12,14},{14,0},{1,3},{3,5},... | collective-permute-start | bytes 983048 | tf_op jit(solution)/shard_map/ppermute | solution.py:39
  24.7 16.7 %collective-permute-start.1 = (f32[5,64,256]{2,1,0:T(8,128)}, f32[5,64,256]{2,1,0:T(8,128)S(1)}, u32[]{:S(2)}, u32[]{:S(2)}) collective-permute-start(f32[5,64,256]{2,1,0:T(8,128)} %shard_map.69), channel_id=1, source_target_pairs={{0,2},{2,4},{4,6},{6,8},{8,10},{10,12},{12,14},{14,0},{1,3},{3,5},... | collective-permute-start | bytes 983048 | tf_op jit(solution)/shard_map/ppermute | solution.py:39
  25.3 16.1 %all-to-all-start.1 = ((f32[16,8,256]{2,1,0:T(8,128)}), f32[16,8,256]{2,1,0:T(8,128)S(1)}, u32[]{:S(2)}, u32[]{:S(2)}) async-start(f32[16,8,256]{2,1,0:T(8,128)} %bitcast.17), calls=%async_computation.1 | async-start | bytes 262144 | tf_op jit(solution)/shard_map/all_to_all | solution.py:843
  33.3 0.8 copy-start
  40.0 13.2 %collective-permute-start.2 = (f32[5,64,256]{2,1,0:T(8,128)}, f32[5,64,256]{2,1,0:T(8,128)S(1)}, u32[]{:S(2)}, u32[]{:S(2)}) collective-permute-start(f32[5,64,256]{2,1,0:T(8,128)} %get-tuple-element.42), channel_id=1, source_target_pairs={{0,2},{2,4},{4,6},{6,8},{8,10},{10,12},{12,14},{14,0},{1,3},{3,5},... | collective-permute-start | bytes 983048 | tf_op jit(solution)/shard_map/ppermute | solution.py:39
  41.4 0.7 copy-start.16
  41.4 0.8 copy-start.2
  47.1 15.1 %collective-permute-start.3 = (f32[5,64,256]{2,1,0:T(8,128)}, f32[5,64,256]{2,1,0:T(8,128)S(1)}, u32[]{:S(2)}, u32[]{:S(2)}) collective-permute-start(f32[5,64,256]{2,1,0:T(8,128)} %get-tuple-element.43), channel_id=1, source_target_pairs={{0,2},{2,4},{4,6},{6,8},{8,10},{10,12},{12,14},{14,0},{1,3},{3,5},... | collective-permute-start | bytes 983048 | tf_op jit(solution)/shard_map/ppermute | solution.py:39
  47.9 14.3 %all-to-all-start.2 = ((f32[16,8,256]{2,1,0:T(8,128)}), f32[16,8,256]{2,1,0:T(8,128)S(1)}, u32[]{:S(2)}, u32[]{:S(2)}) async-start(f32[16,8,256]{2,1,0:T(8,128)} %bitcast.18), calls=%async_computation.2 | async-start | bytes 262144 | tf_op jit(solution)/shard_map/all_to_all | solution.py:843
  53.2 0.7 copy-start.4
  62.2 0.7 copy-start.15
  62.2 0.8 copy-start.6
  67.0 15.1 %collective-permute-start.4 = (f32[3,144,256]{2,1,0:T(8,128)}, f32[3,144,256]{2,1,0:T(8,128)S(1)}, u32[]{:S(2)}, u32[]{:S(2)}) collective-permute-start(f32[3,144,256]{2,1,0:T(8,128)} %get-tuple-element.44), channel_id=1, source_target_pairs={{0,2},{2,4},{4,6},{6,8},{8,10},{10,12},{12,14},{14,0},{1,3},{3,5},... | collective-permute-start | bytes 1327112 | tf_op jit(solution)/shard_map/ppermute | solution.py:39
  67.8 3.9 %copy-start.5 = (f32[5,64,256]{2,1,0:T(8,128)S(1)}, f32[5,64,256]{2,1,0:T(8,128)}, u32[]{:S(2)}) copy-start(f32[5,64,256]{2,1,0:T(8,128)} %copy-done.4) | copy-start | bytes 983044
  67.8 3.9 %copy-start.7 = (f32[5,64,256]{2,1,0:T(8,128)S(1)}, f32[5,64,256]{2,1,0:T(8,128)}, u32[]{:S(2)}) copy-start(f32[5,64,256]{2,1,0:T(8,128)} %copy-done.6) | copy-start | bytes 983044
  67.8 3.9 %copy-start.10 = (f32[8,256]{1,0:T(8,128)S(1)}, f32[8,256]{1,0:T(8,128)}, u32[]{:S(2)}) copy-start(f32[8,256]{1,0:T(8,128)} %get-tuple-element.37.first.second.delta0) | copy-start | bytes 24580
  67.8 3.9 %copy-start.11 = (f32[8,256]{1,0:T(8,128)S(1)}, f32[8,256]{1,0:T(8,128)}, u32[]{:S(2)}) copy-start(f32[8,256]{1,0:T(8,128)} %get-tuple-element.46.order.delta2) | copy-start | bytes 24580
  67.8 3.9 %copy-start.12 = (s32[24]{0:T(128)S(1)}, s32[24]{0:T(128)}, u32[]{:S(2)}) copy-start(s32[24]{0:T(128)} %get-tuple-element.28.ctl) | copy-start | bytes 292
  67.8 3.9 %copy-start.13 = (f32[8,256]{1,0:T(8,128)S(1)}, f32[8,256]{1,0:T(8,128)}, u32[]{:S(2)}) copy-start(f32[8,256]{1,0:T(8,128)} %get-tuple-element.45.delta1) | copy-start | bytes 24580
  71.7 11.1 %copy-start.1 = (f32[5,64,256]{2,1,0:T(8,128)S(1)}, f32[5,64,256]{2,1,0:T(8,128)}, u32[]{:S(2)}) copy-start(f32[5,64,256]{2,1,0:T(8,128)} %copy-done) | copy-start | bytes 983044
  71.7 11.1 %copy-start.3 = (f32[5,64,256]{2,1,0:T(8,128)S(1)}, f32[5,64,256]{2,1,0:T(8,128)}, u32[]{:S(2)}) copy-start(f32[5,64,256]{2,1,0:T(8,128)} %copy-done.2) | copy-start | bytes 983044
  71.7 11.1 %copy-start.8 = (f32[3,256,256]{2,1,0:T(8,128)S(1)}, f32[3,256,256]{2,1,0:T(8,128)}, u32[]{:S(2)}) copy-start(f32[3,256,256]{2,1,0:T(8,128)} %get-tuple-element.50.staying) | copy-start | bytes 2359300
  71.8 1.1 %copy-start.9 = (f32[3,144,256]{2,1,0:T(8,128)S(1)}, f32[3,144,256]{2,1,0:T(8,128)}, u32[]{:S(2)}) copy-start(f32[3,144,256]{2,1,0:T(8,128)} %get-tuple-element.47.late) | copy-start | bytes 1327108
  82.7 14.1 %collective-permute-start.5 = (f32[3,144,256]{2,1,0:T(8,128)S(1)}, f32[3,144,256]{2,1,0:T(8,128)S(1)}, u32[]{:S(2)}, u32[]{:S(2)}) collective-permute-start(f32[3,144,256]{2,1,0:T(8,128)S(1)} %shard_map.75), channel_id=1, source_target_pairs={{0,2},{2,4},{4,6},{6,8},{8,10},{10,12},{12,14},{14,0},{1,3},{3,5},... | collective-permute-start | bytes 1327112 | tf_op jit(solution)/shard_map/ppermute | solution.py:39

commit v24 on v23

--- a/solution.py
+++ b/solution.py
@@ -19,13 +19,13 @@
 SLOT_LOW, WALL_WEST, WALL_EAST, WALL_OUTER, WET, MOVE = 0, 1, 3, 5, 7, 13
 WET_FIRST, WET_SECOND = 16, 19
 CONTROLS = 24
-EARLY = 128
-PIECES = ((0, 64), (64, 128))
-AGAIN = 32
+EARLY = 144
+PIECES = ((0, 80), (80, 144))
+AGAIN = 48
 LATE = TILE - EARLY + 16
 CHUNKS = 8
 PARTS = 8
-STRIP = 16
+STRIP = 32
 TOP = 6
 SCALE = 0.5 / SPACING
 SLOPE = GRAVITY / (2.0 * SPACING)

time: 98.6 us -> 98.7 us (level)
  Pallas kernels: 49.7 us -> 43.6 us
  waiting for transfers between devices: 22.2 us -> 27.8 us
    pallas_call x1, Pallas kernels: 5.1 us -> 1.51 us  [body(): call(repeat_first, shape, hbm(), [smem()] + [vmem()] * 3 + [anywhere()] *...]
    ppermute x6, waiting for transfers between devices: 15.8 us -> 19.3 us  [shifted(): return lax.ppermute(value, axis, pairs)]
    all_to_all x3, waiting for transfers between devices: 6.45 us -> 8.5 us  [spread(): lax.all_to_all(fast, ('xb', 'yb'), split_axis=0, concat_axis=0, tiled=True)]
  transfers between devices with their start and end apart: 9 -> 9, of which waited for: 6 -> 6; matrix products, arithmetic and copies ran while one was open for 0% -> 0% of each run, Pallas kernels for 42% -> 36%
where the time goes in v24:
time: 98.7 us; the launch traced here: 97.9 us
  Pallas kernels  43.6 us (44%)
  waiting for transfers between devices  27.8 us (28%)
  starting transfers between devices  21.2 us (21%)
  local copies, waits for them, and re-layouts  4.89 us (5%)
    ppermute x6, waiting for transfers between devices, shifted(): return lax.ppermute(value, axis, pairs)  19.3 us
    all_to_all x3, starting transfers between devices, spread(): lax.all_to_all(fast, ('xb', 'yb'), split_axis=0, concat_axis=0, tiled=True)  18.9 us
    pallas_call x2, Pallas kernels, body(): call(functools.partial(update_and_leaving if passing else update, step),...  9.86 us
    all_to_all x3, waiting for transfers between devices, spread(): lax.all_to_all(fast, ('xb', 'yb'), split_axis=0, concat_axis=0, tiled=True)  8.5 us
    pallas_call x2, Pallas kernels, finish_step(): call(functools.partial(last_update, moving), (tile_shape,) + shapes + (de...  7.77 us
    pallas_call x1, Pallas kernels, body(): call(rates_and_splitting, (shape,) + piece_shapes, (hbm(),) * 3, [smem()]...  5.31 us
    pallas_call x1, Pallas kernels, body(): call(rates_and_leaving, (shape, piece_shapes[0]), (hbm(),) * 2, [smem()]...  5.27 us
    pallas_call x1, Pallas kernels, body(): call(rates_after, shape, hbm(), [smem()] + [hbm()] * 3, 16 << 20, scratch)  5.25 us
  transfers between devices with their start and end apart: 9, of which 6 were waited for; matrix products, arithmetic and copies ran while one was open for 0% of the time, Pallas kernels for 36%

profile of v24, /device:TPU:0, one launch (start us, length us, event | category | flops | bytes accessed | tf_op | source)
XLA Modules:
  0.0 97.9 jit_solution(1795512047445623300)
XLA Ops:
  0.0 2.7 %shard_map.64 = (f32[128,384]{1,0:T(8,128)}, f32[8,256]{1,0:T(8,128)}, s32[24]{0:T(128)}) custom-call(f32[2,3,256,256]{3,2,1,0:T(8,128)} %state_first.3, f32[2,256,256]{2,1,0:T(8,128)} %bed_in.9, s32[4,32]{1,0:T(4,128)} %bitcast.19, s32[3,32]{1,0:T(4,128)} %wet_in.1, s32[3,16]{1,0:T(4,128)} %moves_in.1), custom_call_target="tpu_custom_call" | custom-call | flops 4194304 | bytes 4194304 | tf_op jit(solution)/shard_map/pallas_call | solution.py:861
  2.7 7.4 %all-to-all-start = ((f32[16,8,384]{2,1,0:T(8,128)}), f32[16,8,384]{2,1,0:T(8,128)S(1)}, u32[]{:S(2)}, u32[]{:S(2)}) async-start(f32[16,8,384]{2,1,0:T(8,128)} %bitcast.16), calls=%async_computation | async-start | bytes 393216 | tf_op jit(solution)/shard_map/all_to_all | solution.py:843
  10.1 5.3 %shard_map.65 = (f32[2,3,256,256]{3,2,1,0:T(8,128)}, f32[5,80,256]{2,1,0:T(8,128)}, f32[5,64,256]{2,1,0:T(8,128)}) custom-call(s32[24]{0:T(128)} %get-tuple-element.28.ctl, f32[2,3,256,256]{3,2,1,0:T(8,128)} %state_first.3, f32[2,256,256]{2,1,0:T(8,128)} %bed_in.9, f32[2,256,256]{2,1,0:T(8,128)} %manning.3), custom_call_target="tpu_custom_call" | custom-call | flops 16777216 | bytes 4194304 | tf_op jit(solution)/shard_map/pallas_call | solution.py:905
  15.4 3.7 %all-to-all-done = f32[16,8,384]{2,1,0:T(8,128)S(1)} async-done(((f32[16,8,384]{2,1,0:T(8,128)}), f32[16,8,384]{2,1,0:T(8,128)S(1)}, u32[]{:S(2)}, u32[]{:S(2)}) %all-to-all-start) | async-done | bytes 196640 | tf_op jit(solution)/shard_map/all_to_all | solution.py:843
  19.1 0.7 copy-done.14
  19.8 4.9 %shard_map.66 = (f32[2,3,256,256]{3,2,1,0:T(8,128)}, f32[128,256]{1,0:T(8,128)}, f32[8,256]{1,0:T(8,128)}, f32[8,256]{1,0:T(8,128)}) custom-call(s32[24]{0:T(128)} %get-tuple-element.28.ctl, f32[128,384]{1,0:T(8,128)} %bitcast.8, f32[128,384]{1,0:T(8,128)} %bitcast.9, f32[8,256]{1,0:T(8,128)} %get-tuple-element.30.columns_in, ...), custom_call_target="tpu_custom_call" | custom-call | flops 8388608 | bytes 10485760 | tf_op jit(solution)/shard_map/pallas_call | solution.py:936
  24.7 0.6 collective-permute-start.1
  25.3 6.1 %all-to-all-start.1 = ((f32[16,8,256]{2,1,0:T(8,128)}), f32[16,8,256]{2,1,0:T(8,128)S(1)}, u32[]{:S(2)}, u32[]{:S(2)}) async-start(f32[16,8,256]{2,1,0:T(8,128)} %bitcast.17), calls=%async_computation.1 | async-start | bytes 262144 | tf_op jit(solution)/shard_map/all_to_all | solution.py:843
  31.4 3.7 %collective-permute-done.arrived.low = f32[5,80,256]{2,1,0:T(8,128)S(1)} collective-permute-done((f32[5,80,256]{2,1,0:T(8,128)}, f32[5,80,256]{2,1,0:T(8,128)S(1)}, u32[]{:S(2)}, u32[]{:S(2)}) %collective-permute-start) | collective-permute-done | bytes 409632 | tf_op jit(solution)/shard_map/ppermute | solution.py:39
  35.1 0.8 copy-done.2
  35.9 5.3 %shard_map.68 = (f32[2,3,256,256]{3,2,1,0:T(8,128)}, f32[5,80,256]{2,1,0:T(8,128)}) custom-call(s32[24]{0:T(128)} %get-tuple-element.28.ctl, f32[2,3,256,256]{3,2,1,0:T(8,128)} %get-tuple-element.34.state_in, f32[2,256,256]{2,1,0:T(8,128)} %bed_in.9, f32[2,3,256,256]{3,2,1,0:T(8,128)} %state_first.3, f32[2,256,256]{2,1,0:T(8,128)} %manning.3, ...), custom_call_target="tpu_custom_call" | custom-call | flops 16777216 | bytes 4194304 | tf_op jit(solution)/shard_map/pallas_call | solution.py:891
  41.2 1.9 %all-to-all-done.1 = f32[16,8,256]{2,1,0:T(8,128)S(1)} async-done(((f32[16,8,256]{2,1,0:T(8,128)}), f32[16,8,256]{2,1,0:T(8,128)S(1)}, u32[]{:S(2)}, u32[]{:S(2)}) %all-to-all-start.1) | async-done | bytes 131104 | tf_op jit(solution)/shard_map/all_to_all | solution.py:843
  43.1 0.7 copy-done.16
  43.8 0.1 copy-done.4
  43.9 5.0 %shard_map.70 = (f32[2,3,256,256]{3,2,1,0:T(8,128)}, f32[128,256]{1,0:T(8,128)}, f32[8,256]{1,0:T(8,128)}, f32[8,256]{1,0:T(8,128)}, f32[5,64,256]{2,1,0:T(8,128)}) custom-call(s32[24]{0:T(128)} %get-tuple-element.28.ctl, f32[128,256]{1,0:T(8,128)} %bitcast.15, f32[128,384]{1,0:T(8,128)} %bitcast.10, f32[8,256]{1,0:T(8,128)} %get-tuple-element.33.columns_in, ...), custom_call_target="tpu_custom_call" | custom-call | flops 8388608 | bytes 10485760 | tf_op jit(solution)/shard_map/pallas_call | solution.py:936
  48.9 0.8 collective-permute-start.3
  49.7 5.4 %all-to-all-start.2 = ((f32[16,8,256]{2,1,0:T(8,128)}), f32[16,8,256]{2,1,0:T(8,128)S(1)}, u32[]{:S(2)}, u32[]{:S(2)}) async-start(f32[16,8,256]{2,1,0:T(8,128)} %bitcast.18), calls=%async_computation.2 | async-start | bytes 262144 | tf_op jit(solution)/shard_map/all_to_all | solution.py:843
  55.1 0.8 copy-done
  55.9 5.3 %shard_map.71.rate = f32[2,3,256,256]{3,2,1,0:T(8,128)} custom-call(s32[24]{0:T(128)} %get-tuple-element.28.ctl, f32[2,3,256,256]{3,2,1,0:T(8,128)} %get-tuple-element.41.state_in.state, f32[2,256,256]{2,1,0:T(8,128)} %bed_in.9, f32[5,80,256]{2,1,0:T(8,128)} %copy-done), custom_call_target="tpu_custom_call" | custom-call | flops 16777216 | bytes 4194304 | tf_op jit(solution)/shard_map/pallas_call | solution.py:901
  61.1 2.9 %all-to-all-done.2 = f32[16,8,256]{2,1,0:T(8,128)S(1)} async-done(((f32[16,8,256]{2,1,0:T(8,128)}), f32[16,8,256]{2,1,0:T(8,128)S(1)}, u32[]{:S(2)}, u32[]{:S(2)}) %all-to-all-start.2) | async-done | bytes 131104 | tf_op jit(solution)/shard_map/all_to_all | solution.py:843
  64.0 0.7 copy-done.15
  64.7 0.1 copy-done.6
  64.8 3.7 %shard_map.72 = (f32[3,256,256]{2,1,0:T(8,128)}, f32[3,128,256]{2,1,0:T(8,128)}, f32[8,256]{1,0:T(8,128)}, f32[8,256]{1,0:T(8,128)}) custom-call(s32[24]{0:T(128)} %get-tuple-element.28.ctl, f32[128,256]{1,0:T(8,128)} %bitcast.13, f32[128,384]{1,0:T(8,128)} %bitcast.11, f32[8,256]{1,0:T(8,128)} %get-tuple-element.40.columns, ...), custom_call_target="tpu_custom_call" | custom-call | flops 8388608 | bytes 10485760 | tf_op jit(solution)/shard_map/pallas_call | solution.py:956
  68.5 0.8 collective-permute-start.4
  69.3 4.1 %shard_map.73 = (f32[3,256,256]{2,1,0:T(8,128)}, f32[3,128,256]{2,1,0:T(8,128)}, f32[8,256]{1,0:T(8,128)}, f32[8,256]{1,0:T(8,128)}) custom-call(s32[24]{0:T(128)} %get-tuple-element.28.ctl, f32[128,256]{1,0:T(8,128)} %bitcast.14, f32[128,384]{1,0:T(8,128)} %bitcast.12, f32[8,256]{1,0:T(8,128)} %get-tuple-element.40.columns, ...), custom_call_target="tpu_custom_call" | custom-call | flops 8388608 | bytes 10485760 | tf_op jit(solution)/shard_map/pallas_call | solution.py:956
  73.5 1.1 %copy-done.9 = f32[3,128,256]{2,1,0:T(8,128)S(1)} copy-done((f32[3,128,256]{2,1,0:T(8,128)S(1)}, f32[3,128,256]{2,1,0:T(8,128)}, u32[]{:S(2)}) %copy-start.9) | copy-done | bytes 393240
  74.6 3.8 %shard_map.74 = (f32[3,144,256]{2,1,0:T(8,128)S(1)}, f32[3,128,256]{2,1,0:T(8,128)S(1)}) custom-call(s32[24]{0:T(128)S(1)} %copy-done.12, f32[8,256]{1,0:T(8,128)S(1)} %copy-done.10, f32[8,256]{1,0:T(8,128)S(1)} %copy-done.13, f32[8,256]{1,0:T(8,128)S(1)} %copy-done.11, f32[5,80,256]{2,1,0:T(8,128)S(1)} %copy-done.1, f32[5,64,256]{2,1,0:T(8,128)S(1)} %copy-done.7, ...), custom_call_target="tpu_custom_call" | custom-call | flops 8388608 | bytes 4194304 | tf_op jit(solution)/shard_map/pallas_call | solution.py:971
  78.4 4.1 %collective-permute-done.4.arrived.late_in = f32[3,128,256]{2,1,0:T(8,128)S(1)} collective-permute-done((f32[3,128,256]{2,1,0:T(8,128)}, f32[3,128,256]{2,1,0:T(8,128)S(1)}, u32[]{:S(2)}, u32[]{:S(2)}) %collective-permute-start.4) | collective-permute-done | bytes 393248 | tf_op jit(solution)/shard_map/ppermute | solution.py:39
  82.6 0.6 shard_map.75
  83.3 1.5 %shard_map.76.before = f32[2,3,256,256]{3,2,1,0:T(8,128)} custom-call(s32[24]{0:T(128)S(1)} %copy-done.12, f32[8,256]{1,0:T(8,128)S(1)} %copy-done.10, f32[8,256]{1,0:T(8,128)S(1)} %copy-done.13, f32[8,256]{1,0:T(8,128)S(1)} %copy-done.11, f32[5,80,256]{2,1,0:T(8,128)S(1)} %copy-done.3, f32[5,64,256]{2,1,0:T(8,128)S(1)} %copy-done.5, ...), custom_call_target="tpu_custom_call" | custom-call | flops 8388608 | bytes 4194304 | tf_op jit(solution)/shard_map/pallas_call | solution.py:989
  84.8 11.4 %collective-permute-done.5.late = f32[3,128,256]{2,1,0:T(8,128)S(1)} collective-permute-done((f32[3,128,256]{2,1,0:T(8,128)S(1)}, f32[3,128,256]{2,1,0:T(8,128)S(1)}, u32[]{:S(2)}, u32[]{:S(2)}) %collective-permute-start.5) | collective-permute-done | bytes 393248 | tf_op jit(solution)/shard_map/ppermute | solution.py:39
  96.2 1.5 %shard_map.77 = f32[2,3,256,256]{3,2,1,0:T(8,128)} custom-call(s32[24]{0:T(128)S(1)} %copy-done.12, f32[3,128,256]{2,1,0:T(8,128)S(1)} %collective-permute-done.5.late, f32[3,144,256]{2,1,0:T(8,128)S(1)} %get-tuple-element.49.order.early, f32[2,3,256,256]{3,2,1,0:T(8,128)} %shard_map.76.before), custom_call_target="tpu_custom_call", output_to_operand_aliasing={{}: (3, {})} | custom-call | flops 1048576 | bytes 4194304 | tf_op jit(solution)/shard_map/pallas_call | solution.py:1004
  (34 shorter events, 0.2 us)
Async XLA Ops:
  2.7 16.4 %all-to-all-start = ((f32[16,8,384]{2,1,0:T(8,128)}), f32[16,8,384]{2,1,0:T(8,128)S(1)}, u32[]{:S(2)}, u32[]{:S(2)}) async-start(f32[16,8,384]{2,1,0:T(8,128)} %bitcast.16), calls=%async_computation | async-start | bytes 393216 | tf_op jit(solution)/shard_map/all_to_all | solution.py:843
  19.1 0.7 copy-start.14
  19.8 15.3 %collective-permute-start = (f32[5,80,256]{2,1,0:T(8,128)}, f32[5,80,256]{2,1,0:T(8,128)S(1)}, u32[]{:S(2)}, u32[]{:S(2)}) collective-permute-start(f32[5,80,256]{2,1,0:T(8,128)} %shard_map.67), channel_id=1, source_target_pairs={{0,2},{2,4},{4,6},{6,8},{8,10},{10,12},{12,14},{14,0},{1,3},{3,5},... | collective-permute-start | bytes 1228808 | tf_op jit(solution)/shard_map/ppermute | solution.py:39
  24.7 18.5 %collective-permute-start.1 = (f32[5,64,256]{2,1,0:T(8,128)}, f32[5,64,256]{2,1,0:T(8,128)S(1)}, u32[]{:S(2)}, u32[]{:S(2)}) collective-permute-start(f32[5,64,256]{2,1,0:T(8,128)} %shard_map.69), channel_id=1, source_target_pairs={{0,2},{2,4},{4,6},{6,8},{8,10},{10,12},{12,14},{14,0},{1,3},{3,5},... | collective-permute-start | bytes 983048 | tf_op jit(solution)/shard_map/ppermute | solution.py:39
  25.3 17.8 %all-to-all-start.1 = ((f32[16,8,256]{2,1,0:T(8,128)}), f32[16,8,256]{2,1,0:T(8,128)S(1)}, u32[]{:S(2)}, u32[]{:S(2)}) async-start(f32[16,8,256]{2,1,0:T(8,128)} %bitcast.17), calls=%async_computation.1 | async-start | bytes 262144 | tf_op jit(solution)/shard_map/all_to_all | solution.py:843
  35.1 0.8 copy-start.2
  41.2 13.9 %collective-permute-start.2 = (f32[5,80,256]{2,1,0:T(8,128)}, f32[5,80,256]{2,1,0:T(8,128)S(1)}, u32[]{:S(2)}, u32[]{:S(2)}) collective-permute-start(f32[5,80,256]{2,1,0:T(8,128)} %get-tuple-element.42), channel_id=1, source_target_pairs={{0,2},{2,4},{4,6},{6,8},{8,10},{10,12},{12,14},{14,0},{1,3},{3,5},... | collective-permute-start | bytes 1228808 | tf_op jit(solution)/shard_map/ppermute | solution.py:39
  43.1 0.7 copy-start.16
  43.1 0.8 copy-start.4
  48.9 15.1 %collective-permute-start.3 = (f32[5,64,256]{2,1,0:T(8,128)}, f32[5,64,256]{2,1,0:T(8,128)S(1)}, u32[]{:S(2)}, u32[]{:S(2)}) collective-permute-start(f32[5,64,256]{2,1,0:T(8,128)} %get-tuple-element.43), channel_id=1, source_target_pairs={{0,2},{2,4},{4,6},{6,8},{8,10},{10,12},{12,14},{14,0},{1,3},{3,5},... | collective-permute-start | bytes 983048 | tf_op jit(solution)/shard_map/ppermute | solution.py:39
  49.7 14.3 %all-to-all-start.2 = ((f32[16,8,256]{2,1,0:T(8,128)}), f32[16,8,256]{2,1,0:T(8,128)S(1)}, u32[]{:S(2)}, u32[]{:S(2)}) async-start(f32[16,8,256]{2,1,0:T(8,128)} %bitcast.18), calls=%async_computation.2 | async-start | bytes 262144 | tf_op jit(solution)/shard_map/all_to_all | solution.py:843
  55.1 0.8 copy-start
  64.0 0.7 copy-start.15
  64.0 0.8 copy-start.6
  68.5 14.1 %collective-permute-start.4 = (f32[3,128,256]{2,1,0:T(8,128)}, f32[3,128,256]{2,1,0:T(8,128)S(1)}, u32[]{:S(2)}, u32[]{:S(2)}) collective-permute-start(f32[3,128,256]{2,1,0:T(8,128)} %get-tuple-element.44), channel_id=1, source_target_pairs={{0,2},{2,4},{4,6},{6,8},{8,10},{10,12},{12,14},{14,0},{1,3},{3,5},... | collective-permute-start | bytes 1179656 | tf_op jit(solution)/shard_map/ppermute | solution.py:39
  69.3 4.2 %copy-start.1 = (f32[5,80,256]{2,1,0:T(8,128)S(1)}, f32[5,80,256]{2,1,0:T(8,128)}, u32[]{:S(2)}) copy-start(f32[5,80,256]{2,1,0:T(8,128)} %copy-done) | copy-start | bytes 1228804
  69.3 4.2 %copy-start.7 = (f32[5,64,256]{2,1,0:T(8,128)S(1)}, f32[5,64,256]{2,1,0:T(8,128)}, u32[]{:S(2)}) copy-start(f32[5,64,256]{2,1,0:T(8,128)} %copy-done.6) | copy-start | bytes 983044
  69.3 4.2 %copy-start.10 = (f32[8,256]{1,0:T(8,128)S(1)}, f32[8,256]{1,0:T(8,128)}, u32[]{:S(2)}) copy-start(f32[8,256]{1,0:T(8,128)} %get-tuple-element.37.first.second.delta0) | copy-start | bytes 24580
  69.3 4.2 %copy-start.11 = (f32[8,256]{1,0:T(8,128)S(1)}, f32[8,256]{1,0:T(8,128)}, u32[]{:S(2)}) copy-start(f32[8,256]{1,0:T(8,128)} %get-tuple-element.46.order.delta2) | copy-start | bytes 24580
  69.3 4.2 %copy-start.12 = (s32[24]{0:T(128)S(1)}, s32[24]{0:T(128)}, u32[]{:S(2)}) copy-start(s32[24]{0:T(128)} %get-tuple-element.28.ctl) | copy-start | bytes 292
  69.3 4.2 %copy-start.13 = (f32[8,256]{1,0:T(8,128)S(1)}, f32[8,256]{1,0:T(8,128)}, u32[]{:S(2)}) copy-start(f32[8,256]{1,0:T(8,128)} %get-tuple-element.45.delta1) | copy-start | bytes 24580
  73.4 9.8 %copy-start.3 = (f32[5,80,256]{2,1,0:T(8,128)S(1)}, f32[5,80,256]{2,1,0:T(8,128)}, u32[]{:S(2)}) copy-start(f32[5,80,256]{2,1,0:T(8,128)} %copy-done.2) | copy-start | bytes 1228804
  73.4 9.8 %copy-start.5 = (f32[5,64,256]{2,1,0:T(8,128)S(1)}, f32[5,64,256]{2,1,0:T(8,128)}, u32[]{:S(2)}) copy-start(f32[5,64,256]{2,1,0:T(8,128)} %copy-done.4) | copy-start | bytes 983044
  73.4 9.8 %copy-start.8 = (f32[3,256,256]{2,1,0:T(8,128)S(1)}, f32[3,256,256]{2,1,0:T(8,128)}, u32[]{:S(2)}) copy-start(f32[3,256,256]{2,1,0:T(8,128)} %get-tuple-element.50.staying) | copy-start | bytes 2359300
  73.5 1.1 %copy-start.9 = (f32[3,128,256]{2,1,0:T(8,128)S(1)}, f32[3,128,256]{2,1,0:T(8,128)}, u32[]{:S(2)}) copy-start(f32[3,128,256]{2,1,0:T(8,128)} %get-tuple-element.47.late) | copy-start | bytes 1179652
  83.2 13.1 %collective-permute-start.5 = (f32[3,128,256]{2,1,0:T(8,128)S(1)}, f32[3,128,256]{2,1,0:T(8,128)S(1)}, u32[]{:S(2)}, u32[]{:S(2)}) collective-permute-start(f32[3,128,256]{2,1,0:T(8,128)S(1)} %shard_map.75), channel_id=1, source_target_pairs={{0,2},{2,4},{4,6},{6,8},{8,10},{10,12},{12,14},{14,0},{1,3},{3,5},... | collective-permute-start | bytes 1179656 | tf_op jit(solution)/shard_map/ppermute | solution.py:39

commit v25 on v24

--- a/solution.py
+++ b/solution.py
@@ -23,6 +23,7 @@
 PIECES = ((0, 80), (80, 144))
 AGAIN = 48
 LATE = TILE - EARLY + 16
+HALF = LATE // 2
 CHUNKS = 8
 PARTS = 8
 STRIP = 32
@@ -562,12 +563,12 @@
         late[field, 16:, :] = tile[field, EARLY:, :]
 
 
-def merge(late, early, tile):
+def merge(late, rest, early, tile):
     for field in range(3):
-        merge_field(field, late, early, tile)
-
-
-def merge_field(field, late, early, tile):
+        merge_field(field, late, rest, early, tile)
+
+
+def merge_field(field, late, rest, early, tile):
     row = sublanes()
     lane = lax.broadcasted_iota(jnp.int32, (8, LANES), 1)
     first = late[field, 0:8, :]
@@ -589,19 +590,23 @@
         if block == EARLY // 8 - 1:
             value = jnp.where(row < 5, value, first)
         tile[field, rows, :] = value
-    tile[field, EARLY:, :] = late[field, 16:, :]
-
-
-def repeat_second(ctl, delta0, delta1, delta2, low, high, late, out, late_out, work, tile, sems):
-    near = start_all(((late, late_out),), sems, 2)
+    tile[field, EARLY : TILE - HALF, :] = late[field, 16:, :]
+    tile[field, TILE - HALF :, :] = rest[field]
+
+
+def repeat_second(
+    ctl, delta0, delta1, delta2, low, high, late, rest, out, late_out, rest_out, work, tile, sems
+):
+    near = start_all(((late, late_out), (rest, rest_out)), sems, 2)
     repeat_steps(ctl, WET_SECOND, (delta0, delta1, delta2), (low, high), work, tile, sems)
     wait_all(start_all(((tile, out),), sems) + near)
 
 
 def repeat_first(
-    ctl, delta0, delta1, delta2, low, high, late_in, staying, out, work, other, tile, late, sems
+    ctl, delta0, delta1, delta2, low, high, late_in, rest_in, staying, out,
+    work, other, tile, late, rest, sems,
 ):
-    rest = out.at[1 - ctl[MOVE + 1]]
+    kept = out.at[1 - ctl[MOVE + 1]]
     again = ctl[MOVE] == ctl[MOVE + 1]
 
     @pl.when(again)
@@ -610,19 +615,19 @@
 
     @pl.when(jnp.logical_not(again))
     def _():
-        copies = start_all(((late_in, late),), sems, 2)
+        copies = start_all(((late_in, late), (rest_in, rest)), sems, 2)
         repeat_steps(ctl, WET_FIRST, (delta0, delta1, delta2), (low, high), work, other, sems)
         wait_all(copies)
-        merge(late, other, tile)
-
-    wait_all(start_all(((tile, rest),), sems))
-
-
-def finish(ctl, late, early, before, out, tile, sems):
+        merge(late, rest, other, tile)
+
+    wait_all(start_all(((tile, kept),), sems))
+
+
+def finish(ctl, late, rest, early, before, out, tile, sems):
     del before
     copies = []
     for field in range(3):
-        merge_field(field, late, early, tile)
+        merge_field(field, late, rest, early, tile)
         copies += start_all(
             ((tile.at[field], out.at[ctl[MOVE + 1], field]),), sems, field
         )
@@ -798,9 +803,10 @@
         messages(ctl, fresh, None, jnp.max(total, keepdims=True), out, columns_out)
         outgoing += start_all(((out, first_out), (columns_out, second_out)), sems, 4 * PARTS)
     else:
-        second[...] = jnp.zeros_like(second)
         late_rows(fresh.at[slots[0]], first)
-        outgoing += start_all(((first, first_out), (second, second_out)), sems, 4 * PARTS)
+        outgoing += start_all(
+            ((first.at[:, :HALF], first_out), (first.at[:, HALF:], second_out)), sems, 4 * PARTS
+        )
     wait_all(outgoing)
 
 
@@ -852,6 +858,7 @@
     early_shape = f32(5, EARLY, TILE)
     early_state = f32(3, EARLY, TILE)
     late_shape = f32(3, LATE, TILE)
+    half_shape = f32(3, HALF, TILE)
     delta_shape = f32(8, TILE)
 
     def buffer(like):
@@ -915,7 +922,7 @@
             )(rate, got, leaving[0])
             early_first = [shifted(held, "xb", 1)]
         more = step + 1 < STEPS
-        shapes = (f32(8 * devices, TILE) if more else late_shape), f32(8, TILE)
+        shapes = (f32(8 * devices, TILE), f32(8, TILE)) if more else (half_shape,) * 2
         passing = step == 1
         work = [
             whole,
@@ -925,7 +932,7 @@
             pltpu.VMEM(got.shape, jnp.float32),
             pltpu.VMEM(ground.shape, jnp.float32),
             pltpu.VMEM((8, TILE), jnp.float32),
-            buffer(shapes[0]),
+            buffer(shapes[0] if more else late_shape),
             buffer(shapes[1]),
             buffer(delta_shape),
             pltpu.SemaphoreType.DMA((5 * PARTS + 4,)),
@@ -963,54 +970,64 @@
             moved=10,
         )(*operands, order)
 
-    _, late_first, _, delta = finish_step(True, early_second[1])
-    staying, late_second, _, _ = finish_step(False, delta)
+    _, late_first, rest_first, delta = finish_step(True, early_second[1])
+    staying, late_second, rest_second, _ = finish_step(False, delta)
     deltas.append(delta)
     room = 16 << 20
     late_arrived = shifted(late_first, "xb", 1)
-    second, late_second = call(
+    rest_first = call(hold, half_shape, hbm(), [hbm()] * 3, 1 << 10, aliases={2: 0})(
+        staying, staying, rest_first
+    )
+    rest_arrived = shifted(rest_first, "xb", 1)
+    second, late_second, rest_second = call(
         repeat_second,
-        (early_state, late_shape),
-        (anywhere(), vmem()),
-        [smem()] + [vmem()] * 3 + [anywhere()] * 3,
+        (early_state, half_shape, half_shape),
+        (anywhere(), vmem(), vmem()),
+        [smem()] + [vmem()] * 3 + [anywhere()] * 4,
         8 << 20,
-        [buffer(early_shape), buffer(early_state), pltpu.SemaphoreType.DMA((3,))],
+        [buffer(early_shape), buffer(early_state), pltpu.SemaphoreType.DMA((4,))],
         room=room,
-    )(ctl, *deltas, *early_second, late_second)
-    leaving = call(
-        second_late,
-        late_shape,
-        vmem(),
-        [smem(), vmem(), vmem(), anywhere()],
-        1 << 10,
-        room=room,
-    )(ctl, late_arrived, late_second, second)
-    late_next = shifted(leaving, "xb", 1)
+    )(ctl, *deltas, *early_second, late_second, rest_second)
+
+    def pass_late(arrived, own):
+        leaving = call(
+            second_late,
+            half_shape,
+            vmem(),
+            [smem(), vmem(), vmem(), anywhere()],
+            1 << 10,
+            room=room,
+        )(ctl, arrived, own, second)
+        return shifted(leaving, "xb", 1)
+
+    late_next = pass_late(late_arrived, late_second)
+    rest_next = pass_late(rest_arrived, rest_second)
     final = call(
         repeat_first,
         shape,
         hbm(),
-        [smem()] + [vmem()] * 3 + [anywhere()] * 4,
+        [smem()] + [vmem()] * 3 + [anywhere()] * 5,
         8 << 20,
         [
             buffer(early_shape),
             buffer(early_state),
             buffer(tile_shape),
-            buffer(late_shape),
-            pltpu.SemaphoreType.DMA((3,)),
+            buffer(half_shape),
+            buffer(half_shape),
+            pltpu.SemaphoreType.DMA((4,)),
         ],
         room=room,
-    )(ctl, *deltas, *early_first, late_arrived, staying)
+    )(ctl, *deltas, *early_first, late_arrived, rest_arrived, staying)
     return call(
         finish,
         shape,
         hbm(),
-        [smem(), vmem(), vmem(), hbm()],
+        [smem(), vmem(), vmem(), vmem(), hbm()],
         1 << 20,
         [buffer(tile_shape), pltpu.SemaphoreType.DMA((3,))],
-        {3: 0},
+        {4: 0},
         room=room,
-    )(ctl, late_next, second, final)
+    )(ctl, late_next, rest_next, second, final)
 
 
 def solution(mesh):

time: 98.7 us -> 98.6 us (level)
  starting transfers between devices: 21.2 us -> 22.9 us
  waiting for transfers between devices: 27.8 us -> 26.3 us
  local copies, waits for them, and re-layouts: 4.89 us -> 3.8 us
    ppermute x6 -> x8, starting transfers between devices: 2.33 us -> 4.15 us  [shifted(): return lax.ppermute(value, axis, pairs)]
    ppermute x6 -> x8, waiting for transfers between devices: 19.3 us -> 18.1 us  [shifted(): return lax.ppermute(value, axis, pairs)]
    unnamed x34 -> x38, local copies, waits for them, and re-layouts: 4.89 us -> 3.8 us
    pallas_call x3 -> x5, Pallas kernels: 5.94 us -> 6.82 us  [the longest x1 4.17 us: body(): call(repeat_second, (early_state, half_shape, half_shape), (anywhere(), v...]
  transfers between devices with their start and end apart: 9 -> 11, of which waited for: 6 -> 8; matrix products, arithmetic and copies ran while one was open for 0% -> 0% of each run, Pallas kernels for 36% -> 33%
where the time goes in v25:
time: 98.6 us; the launch traced here: 98 us
  Pallas kernels  44.4 us (45%)
  waiting for transfers between devices  26.3 us (27%)
  starting transfers between devices  22.9 us (23%)
  local copies, waits for them, and re-layouts  3.8 us (4%)
    all_to_all x3, starting transfers between devices, spread(): lax.all_to_all(fast, ('xb', 'yb'), split_axis=0, concat_axis=0, tiled=True)  18.8 us
    ppermute x8, waiting for transfers between devices, shifted(): return lax.ppermute(value, axis, pairs)  18.1 us
    pallas_call x2, Pallas kernels, body(): call(functools.partial(update_and_leaving if passing else update, step),...  9.87 us
    all_to_all x3, waiting for transfers between devices, spread(): lax.all_to_all(fast, ('xb', 'yb'), split_axis=0, concat_axis=0, tiled=True)  8.27 us
    pallas_call x2, Pallas kernels, finish_step(): call(functools.partial(last_update, moving), (tile_shape,) + shapes + (de...  7.66 us
    pallas_call x1, Pallas kernels, body(): call(rates_and_splitting, (shape,) + piece_shapes, (hbm(),) * 3, [smem()]...  5.31 us
    pallas_call x1, Pallas kernels, body(): call(rates_and_leaving, (shape, piece_shapes[0]), (hbm(),) * 2, [smem()]...  5.27 us
    pallas_call x1, Pallas kernels, body(): call(rates_after, shape, hbm(), [smem()] + [hbm()] * 3, 16 << 20, scratch)  5.25 us
  transfers between devices with their start and end apart: 11, of which 8 were waited for; matrix products, arithmetic and copies ran while one was open for 0% of the time, Pallas kernels for 33%

profile of v25, /device:TPU:0, one launch (start us, length us, event | category | flops | bytes accessed | tf_op | source)
XLA Modules:
  0.0 98.0 jit_solution(16175263181050396968)
XLA Ops:
  0.0 2.7 %shard_map.64 = (f32[128,384]{1,0:T(8,128)}, f32[8,256]{1,0:T(8,128)}, s32[24]{0:T(128)}) custom-call(f32[2,3,256,256]{3,2,1,0:T(8,128)} %state_first.3, f32[2,256,256]{2,1,0:T(8,128)} %bed_in.9, s32[4,32]{1,0:T(4,128)} %bitcast.19, s32[3,32]{1,0:T(4,128)} %wet_in.1, s32[3,16]{1,0:T(4,128)} %moves_in.1), custom_call_target="tpu_custom_call" | custom-call | flops 4194304 | bytes 4194304 | tf_op jit(solution)/shard_map/pallas_call | solution.py:868
  2.7 7.4 %all-to-all-start = ((f32[16,8,384]{2,1,0:T(8,128)}), f32[16,8,384]{2,1,0:T(8,128)S(1)}, u32[]{:S(2)}, u32[]{:S(2)}) async-start(f32[16,8,384]{2,1,0:T(8,128)} %bitcast.16), calls=%async_computation | async-start | bytes 393216 | tf_op jit(solution)/shard_map/all_to_all | solution.py:849
  10.1 5.3 %shard_map.65 = (f32[2,3,256,256]{3,2,1,0:T(8,128)}, f32[5,80,256]{2,1,0:T(8,128)}, f32[5,64,256]{2,1,0:T(8,128)}) custom-call(s32[24]{0:T(128)} %get-tuple-element.31.ctl, f32[2,3,256,256]{3,2,1,0:T(8,128)} %state_first.3, f32[2,256,256]{2,1,0:T(8,128)} %bed_in.9, f32[2,256,256]{2,1,0:T(8,128)} %manning.3), custom_call_target="tpu_custom_call" | custom-call | flops 16777216 | bytes 4194304 | tf_op jit(solution)/shard_map/pallas_call | solution.py:912
  15.4 3.7 %all-to-all-done = f32[16,8,384]{2,1,0:T(8,128)S(1)} async-done(((f32[16,8,384]{2,1,0:T(8,128)}), f32[16,8,384]{2,1,0:T(8,128)S(1)}, u32[]{:S(2)}, u32[]{:S(2)}) %all-to-all-start) | async-done | bytes 196640 | tf_op jit(solution)/shard_map/all_to_all | solution.py:849
  19.1 0.7 copy-done.15
  19.8 4.9 %shard_map.66 = (f32[2,3,256,256]{3,2,1,0:T(8,128)}, f32[128,256]{1,0:T(8,128)}, f32[8,256]{1,0:T(8,128)}, f32[8,256]{1,0:T(8,128)}) custom-call(s32[24]{0:T(128)} %get-tuple-element.31.ctl, f32[128,384]{1,0:T(8,128)} %bitcast.8, f32[128,384]{1,0:T(8,128)} %bitcast.9, f32[8,256]{1,0:T(8,128)} %get-tuple-element.33.columns_in, ...), custom_call_target="tpu_custom_call" | custom-call | flops 8388608 | bytes 10485760 | tf_op jit(solution)/shard_map/pallas_call | solution.py:943
  24.7 0.6 collective-permute-start.1
  25.3 6.1 %all-to-all-start.1 = ((f32[16,8,256]{2,1,0:T(8,128)}), f32[16,8,256]{2,1,0:T(8,128)S(1)}, u32[]{:S(2)}, u32[]{:S(2)}) async-start(f32[16,8,256]{2,1,0:T(8,128)} %bitcast.17), calls=%async_computation.1 | async-start | bytes 262144 | tf_op jit(solution)/shard_map/all_to_all | solution.py:849
  31.4 3.7 %collective-permute-done.arrived.low = f32[5,80,256]{2,1,0:T(8,128)S(1)} collective-permute-done((f32[5,80,256]{2,1,0:T(8,128)}, f32[5,80,256]{2,1,0:T(8,128)S(1)}, u32[]{:S(2)}, u32[]{:S(2)}) %collective-permute-start) | collective-permute-done | bytes 409632 | tf_op jit(solution)/shard_map/ppermute | solution.py:40
  35.1 0.8 copy-done.3
  35.9 5.3 %shard_map.68 = (f32[2,3,256,256]{3,2,1,0:T(8,128)}, f32[5,80,256]{2,1,0:T(8,128)}) custom-call(s32[24]{0:T(128)} %get-tuple-element.31.ctl, f32[2,3,256,256]{3,2,1,0:T(8,128)} %get-tuple-element.37.state_in, f32[2,256,256]{2,1,0:T(8,128)} %bed_in.9, f32[2,3,256,256]{3,2,1,0:T(8,128)} %state_first.3, f32[2,256,256]{2,1,0:T(8,128)} %manning.3, ...), custom_call_target="tpu_custom_call" | custom-call | flops 16777216 | bytes 4194304 | tf_op jit(solution)/shard_map/pallas_call | solution.py:898
  41.2 1.9 %all-to-all-done.1 = f32[16,8,256]{2,1,0:T(8,128)S(1)} async-done(((f32[16,8,256]{2,1,0:T(8,128)}), f32[16,8,256]{2,1,0:T(8,128)S(1)}, u32[]{:S(2)}, u32[]{:S(2)}) %all-to-all-start.1) | async-done | bytes 131104 | tf_op jit(solution)/shard_map/all_to_all | solution.py:849
  43.1 0.7 copy-done.17
  43.9 5.0 %shard_map.70 = (f32[2,3,256,256]{3,2,1,0:T(8,128)}, f32[128,256]{1,0:T(8,128)}, f32[8,256]{1,0:T(8,128)}, f32[8,256]{1,0:T(8,128)}, f32[5,64,256]{2,1,0:T(8,128)}) custom-call(s32[24]{0:T(128)} %get-tuple-element.31.ctl, f32[128,256]{1,0:T(8,128)} %bitcast.15, f32[128,384]{1,0:T(8,128)} %bitcast.10, f32[8,256]{1,0:T(8,128)} %get-tuple-element.36.columns_in, ...), custom_call_target="tpu_custom_call" | custom-call | flops 8388608 | bytes 10485760 | tf_op jit(solution)/shard_map/pallas_call | solution.py:943
  48.9 0.9 collective-permute-start.3
  49.8 5.3 %all-to-all-start.2 = ((f32[16,8,256]{2,1,0:T(8,128)}), f32[16,8,256]{2,1,0:T(8,128)S(1)}, u32[]{:S(2)}, u32[]{:S(2)}) async-start(f32[16,8,256]{2,1,0:T(8,128)} %bitcast.18), calls=%async_computation.2 | async-start | bytes 262144 | tf_op jit(solution)/shard_map/all_to_all | solution.py:849
  55.1 0.8 copy-done.1
  55.9 5.3 %shard_map.71.rate = f32[2,3,256,256]{3,2,1,0:T(8,128)} custom-call(s32[24]{0:T(128)} %get-tuple-element.31.ctl, f32[2,3,256,256]{3,2,1,0:T(8,128)} %get-tuple-element.44.state_in.state, f32[2,256,256]{2,1,0:T(8,128)} %bed_in.9, f32[5,80,256]{2,1,0:T(8,128)} %copy-done.1), custom_call_target="tpu_custom_call" | custom-call | flops 16777216 | bytes 4194304 | tf_op jit(solution)/shard_map/pallas_call | solution.py:908
  61.1 2.7 %all-to-all-done.2 = f32[16,8,256]{2,1,0:T(8,128)S(1)} async-done(((f32[16,8,256]{2,1,0:T(8,128)}), f32[16,8,256]{2,1,0:T(8,128)S(1)}, u32[]{:S(2)}, u32[]{:S(2)}) %all-to-all-start.2) | async-done | bytes 131104 | tf_op jit(solution)/shard_map/all_to_all | solution.py:849
  63.8 0.7 copy-done.16
  64.6 3.7 %shard_map.72 = (f32[3,256,256]{2,1,0:T(8,128)}, f32[3,64,256]{2,1,0:T(8,128)}, f32[3,64,256]{2,1,0:T(8,128)}, f32[8,256]{1,0:T(8,128)}) custom-call(s32[24]{0:T(128)} %get-tuple-element.31.ctl, f32[128,256]{1,0:T(8,128)} %bitcast.13, f32[128,384]{1,0:T(8,128)} %bitcast.11, f32[8,256]{1,0:T(8,128)} %get-tuple-element.43.columns, ...), custom_call_target="tpu_custom_call" | custom-call | flops 8388608 | bytes 10485760 | tf_op jit(solution)/shard_map/pallas_call | solution.py:963
  68.3 4.0 %shard_map.73 = (f32[3,256,256]{2,1,0:T(8,128)}, f32[3,64,256]{2,1,0:T(8,128)}, f32[3,64,256]{2,1,0:T(8,128)}, f32[8,256]{1,0:T(8,128)}) custom-call(s32[24]{0:T(128)} %get-tuple-element.31.ctl, f32[128,256]{1,0:T(8,128)} %bitcast.14, f32[128,384]{1,0:T(8,128)} %bitcast.12, f32[8,256]{1,0:T(8,128)} %get-tuple-element.43.columns, ...), custom_call_target="tpu_custom_call" | custom-call | flops 8388608 | bytes 10485760 | tf_op jit(solution)/shard_map/pallas_call | solution.py:963
  72.4 0.8 collective-permute-start.6
  73.2 1.6 %collective-permute-start.4 = (f32[3,64,256]{2,1,0:T(8,128)S(1)}, f32[3,64,256]{2,1,0:T(8,128)S(1)}, u32[]{:S(2)}, u32[]{:S(2)}) collective-permute-start(f32[3,64,256]{2,1,0:T(8,128)S(1)} %copy-done.18), channel_id=1, source_target_pairs={{0,2},{2,4},{4,6},{6,8},{8,10},{10,12},{12,14},{14,0},{1,3},{3,5},... | collective-permute-start | bytes 589832 | tf_op jit(solution)/shard_map/ppermute | solution.py:40
  74.9 4.2 %shard_map.74 = (f32[3,144,256]{2,1,0:T(8,128)S(1)}, f32[3,64,256]{2,1,0:T(8,128)S(1)}, f32[3,64,256]{2,1,0:T(8,128)S(1)}) custom-call(s32[24]{0:T(128)S(1)} %copy-done.13, f32[8,256]{1,0:T(8,128)S(1)} %copy-done.11, f32[8,256]{1,0:T(8,128)S(1)} %copy-done.14, f32[8,256]{1,0:T(8,128)S(1)} %copy-done.12, f32[5,80,256]{2,1,0:T(8,128)S(1)} %copy-done.2, ...), custom_call_target="tpu_custom_call" | custom-call | flops 8388608 | bytes 4194304 | tf_op jit(solution)/shard_map/pallas_call | solution.py:982
  79.1 4.0 %collective-permute-done.6.arrived.rest_in = f32[3,64,256]{2,1,0:T(8,128)S(1)} collective-permute-done((f32[3,64,256]{2,1,0:T(8,128)}, f32[3,64,256]{2,1,0:T(8,128)S(1)}, u32[]{:S(2)}, u32[]{:S(2)}) %collective-permute-start.6) | collective-permute-done | bytes 196640 | tf_op jit(solution)/shard_map/ppermute | solution.py:40
  83.1 0.6 shard_map.77
  83.7 2.7 %collective-permute-done.4.arrived.late_in = f32[3,64,256]{2,1,0:T(8,128)S(1)} collective-permute-done((f32[3,64,256]{2,1,0:T(8,128)S(1)}, f32[3,64,256]{2,1,0:T(8,128)S(1)}, u32[]{:S(2)}, u32[]{:S(2)}) %collective-permute-start.4) | collective-permute-done | bytes 196640 | tf_op jit(solution)/shard_map/ppermute | solution.py:40
  87.1 1.5 %shard_map.78.before = f32[2,3,256,256]{3,2,1,0:T(8,128)} custom-call(s32[24]{0:T(128)S(1)} %copy-done.13, f32[8,256]{1,0:T(8,128)S(1)} %copy-done.11, f32[8,256]{1,0:T(8,128)S(1)} %copy-done.14, f32[8,256]{1,0:T(8,128)S(1)} %copy-done.12, f32[5,80,256]{2,1,0:T(8,128)S(1)} %copy-done.4, f32[5,64,256]{2,1,0:T(8,128)S(1)} %copy-done.6, ...), custom_call_target="tpu_custom_call" | custom-call | flops 8388608 | bytes 4194304 | tf_op jit(solution)/shard_map/pallas_call | solution.py:1005
  88.7 3.7 %collective-permute-done.7.rest = f32[3,64,256]{2,1,0:T(8,128)S(1)} collective-permute-done((f32[3,64,256]{2,1,0:T(8,128)S(1)}, f32[3,64,256]{2,1,0:T(8,128)S(1)}, u32[]{:S(2)}, u32[]{:S(2)}) %collective-permute-start.7) | collective-permute-done | bytes 196640 | tf_op jit(solution)/shard_map/ppermute | solution.py:40
  92.4 3.9 %collective-permute-done.5.late = f32[3,64,256]{2,1,0:T(8,128)S(1)} collective-permute-done((f32[3,64,256]{2,1,0:T(8,128)S(1)}, f32[3,64,256]{2,1,0:T(8,128)S(1)}, u32[]{:S(2)}, u32[]{:S(2)}) %collective-permute-start.5) | collective-permute-done | bytes 196640 | tf_op jit(solution)/shard_map/ppermute | solution.py:40
  96.3 1.5 %shard_map.79 = f32[2,3,256,256]{3,2,1,0:T(8,128)} custom-call(s32[24]{0:T(128)S(1)} %copy-done.13, f32[3,64,256]{2,1,0:T(8,128)S(1)} %collective-permute-done.5.late, f32[3,64,256]{2,1,0:T(8,128)S(1)} %collective-permute-done.7.rest, f32[3,144,256]{2,1,0:T(8,128)S(1)} %get-tuple-element.53.order.early, ...), custom_call_target="tpu_custom_call", output_to_operand_aliasing={{}: (4, {})} | custom-call | flops 1048576 | bytes 4194304 | tf_op jit(solution)/shard_map/pallas_call | solution.py:1021
  (44 shorter events, 1.0 us)
Async XLA Ops:
  2.7 16.4 %all-to-all-start = ((f32[16,8,384]{2,1,0:T(8,128)}), f32[16,8,384]{2,1,0:T(8,128)S(1)}, u32[]{:S(2)}, u32[]{:S(2)}) async-start(f32[16,8,384]{2,1,0:T(8,128)} %bitcast.16), calls=%async_computation | async-start | bytes 393216 | tf_op jit(solution)/shard_map/all_to_all | solution.py:849
  19.1 0.7 copy-start.15
  19.8 15.3 %collective-permute-start = (f32[5,80,256]{2,1,0:T(8,128)}, f32[5,80,256]{2,1,0:T(8,128)S(1)}, u32[]{:S(2)}, u32[]{:S(2)}) collective-permute-start(f32[5,80,256]{2,1,0:T(8,128)} %shard_map.67), channel_id=1, source_target_pairs={{0,2},{2,4},{4,6},{6,8},{8,10},{10,12},{12,14},{14,0},{1,3},{3,5},... | collective-permute-start | bytes 1228808 | tf_op jit(solution)/shard_map/ppermute | solution.py:40
  24.7 18.5 %collective-permute-start.1 = (f32[5,64,256]{2,1,0:T(8,128)}, f32[5,64,256]{2,1,0:T(8,128)S(1)}, u32[]{:S(2)}, u32[]{:S(2)}) collective-permute-start(f32[5,64,256]{2,1,0:T(8,128)} %shard_map.69), channel_id=1, source_target_pairs={{0,2},{2,4},{4,6},{6,8},{8,10},{10,12},{12,14},{14,0},{1,3},{3,5},... | collective-permute-start | bytes 983048 | tf_op jit(solution)/shard_map/ppermute | solution.py:40
  25.3 17.8 %all-to-all-start.1 = ((f32[16,8,256]{2,1,0:T(8,128)}), f32[16,8,256]{2,1,0:T(8,128)S(1)}, u32[]{:S(2)}, u32[]{:S(2)}) async-start(f32[16,8,256]{2,1,0:T(8,128)} %bitcast.17), calls=%async_computation.1 | async-start | bytes 262144 | tf_op jit(solution)/shard_map/all_to_all | solution.py:849
  35.1 0.8 copy-start.3
  41.1 13.9 %collective-permute-start.2 = (f32[5,80,256]{2,1,0:T(8,128)}, f32[5,80,256]{2,1,0:T(8,128)S(1)}, u32[]{:S(2)}, u32[]{:S(2)}) collective-permute-start(f32[5,80,256]{2,1,0:T(8,128)} %get-tuple-element.45), channel_id=1, source_target_pairs={{0,2},{2,4},{4,6},{6,8},{8,10},{10,12},{12,14},{14,0},{1,3},{3,5},... | collective-permute-start | bytes 1228808 | tf_op jit(solution)/shard_map/ppermute | solution.py:40
  43.1 0.7 copy-start.17
  43.1 0.8 copy-start.5
  48.9 14.9 %collective-permute-start.3 = (f32[5,64,256]{2,1,0:T(8,128)}, f32[5,64,256]{2,1,0:T(8,128)S(1)}, u32[]{:S(2)}, u32[]{:S(2)}) collective-permute-start(f32[5,64,256]{2,1,0:T(8,128)} %get-tuple-element.46), channel_id=1, source_target_pairs={{0,2},{2,4},{4,6},{6,8},{8,10},{10,12},{12,14},{14,0},{1,3},{3,5},... | collective-permute-start | bytes 983048 | tf_op jit(solution)/shard_map/ppermute | solution.py:40
  49.8 14.0 %all-to-all-start.2 = ((f32[16,8,256]{2,1,0:T(8,128)}), f32[16,8,256]{2,1,0:T(8,128)S(1)}, u32[]{:S(2)}, u32[]{:S(2)}) async-start(f32[16,8,256]{2,1,0:T(8,128)} %bitcast.18), calls=%async_computation.2 | async-start | bytes 262144 | tf_op jit(solution)/shard_map/all_to_all | solution.py:849
  55.1 0.8 copy-start.1
  63.8 0.7 copy-start.16
  63.8 0.8 copy-start.7
  72.3 0.9 copy-start.18
  72.3 2.6 %copy-start.2 = (f32[5,80,256]{2,1,0:T(8,128)S(1)}, f32[5,80,256]{2,1,0:T(8,128)}, u32[]{:S(2)}) copy-start(f32[5,80,256]{2,1,0:T(8,128)} %copy-done.1) | copy-start | bytes 1228804
  72.3 2.5 %copy-start.8 = (f32[5,64,256]{2,1,0:T(8,128)S(1)}, f32[5,64,256]{2,1,0:T(8,128)}, u32[]{:S(2)}) copy-start(f32[5,64,256]{2,1,0:T(8,128)} %copy-done.7) | copy-start | bytes 983044
  72.3 2.5 %copy-start.9 = (f32[3,64,256]{2,1,0:T(8,128)S(1)}, f32[3,64,256]{2,1,0:T(8,128)}, u32[]{:S(2)}) copy-start(f32[3,64,256]{2,1,0:T(8,128)} %get-tuple-element.50.late) | copy-start | bytes 589828
  72.3 2.5 %copy-start.10 = (f32[3,64,256]{2,1,0:T(8,128)S(1)}, f32[3,64,256]{2,1,0:T(8,128)}, u32[]{:S(2)}) copy-start(f32[3,64,256]{2,1,0:T(8,128)} %get-tuple-element.51.rest) | copy-start | bytes 589828
  72.3 2.5 %copy-start.11 = (f32[8,256]{1,0:T(8,128)S(1)}, f32[8,256]{1,0:T(8,128)}, u32[]{:S(2)}) copy-start(f32[8,256]{1,0:T(8,128)} %get-tuple-element.40.first.second.delta0) | copy-start | bytes 24580
  72.3 2.5 %copy-start.12 = (f32[8,256]{1,0:T(8,128)S(1)}, f32[8,256]{1,0:T(8,128)}, u32[]{:S(2)}) copy-start(f32[8,256]{1,0:T(8,128)} %get-tuple-element.49.order.delta2) | copy-start | bytes 24580
  72.3 2.5 %copy-start.13 = (s32[24]{0:T(128)S(1)}, s32[24]{0:T(128)}, u32[]{:S(2)}) copy-start(s32[24]{0:T(128)} %get-tuple-element.31.ctl) | copy-start | bytes 292
  72.3 2.5 %copy-start.14 = (f32[8,256]{1,0:T(8,128)S(1)}, f32[8,256]{1,0:T(8,128)}, u32[]{:S(2)}) copy-start(f32[8,256]{1,0:T(8,128)} %get-tuple-element.48.delta1) | copy-start | bytes 24580
  72.4 10.7 %collective-permute-start.6 = (f32[3,64,256]{2,1,0:T(8,128)}, f32[3,64,256]{2,1,0:T(8,128)S(1)}, u32[]{:S(2)}, u32[]{:S(2)}) collective-permute-start(f32[3,64,256]{2,1,0:T(8,128)} %shard_map.76), channel_id=1, source_target_pairs={{0,2},{2,4},{4,6},{6,8},{8,10},{10,12},{12,14},{14,0},{1,3},{3,5},... | collective-permute-start | bytes 589832 | tf_op jit(solution)/shard_map/ppermute | solution.py:40
  73.2 13.3 %collective-permute-start.4 = (f32[3,64,256]{2,1,0:T(8,128)S(1)}, f32[3,64,256]{2,1,0:T(8,128)S(1)}, u32[]{:S(2)}, u32[]{:S(2)}) collective-permute-start(f32[3,64,256]{2,1,0:T(8,128)S(1)} %copy-done.18), channel_id=1, source_target_pairs={{0,2},{2,4},{4,6},{6,8},{8,10},{10,12},{12,14},{14,0},{1,3},{3,5},... | collective-permute-start | bytes 589832 | tf_op jit(solution)/shard_map/ppermute | solution.py:40
  74.9 12.2 %copy-start = (f32[3,256,256]{2,1,0:T(8,128)S(1)}, f32[3,256,256]{2,1,0:T(8,128)}, u32[]{:S(2)}) copy-start(f32[3,256,256]{2,1,0:T(8,128)} %get-tuple-element.54.first.second.staying) | copy-start | bytes 2359300
  74.9 12.2 %copy-start.4 = (f32[5,80,256]{2,1,0:T(8,128)S(1)}, f32[5,80,256]{2,1,0:T(8,128)}, u32[]{:S(2)}) copy-start(f32[5,80,256]{2,1,0:T(8,128)} %copy-done.3) | copy-start | bytes 1228804
  74.9 12.2 %copy-start.6 = (f32[5,64,256]{2,1,0:T(8,128)S(1)}, f32[5,64,256]{2,1,0:T(8,128)}, u32[]{:S(2)}) copy-start(f32[5,64,256]{2,1,0:T(8,128)} %copy-done.5) | copy-start | bytes 983044
  83.6 8.8 %collective-permute-start.7 = (f32[3,64,256]{2,1,0:T(8,128)S(1)}, f32[3,64,256]{2,1,0:T(8,128)S(1)}, u32[]{:S(2)}, u32[]{:S(2)}) collective-permute-start(f32[3,64,256]{2,1,0:T(8,128)S(1)} %shard_map.77), channel_id=1, source_target_pairs={{0,2},{2,4},{4,6},{6,8},{8,10},{10,12},{12,14},{14,0},{1,3},{3,5},... | collective-permute-start | bytes 589832 | tf_op jit(solution)/shard_map/ppermute | solution.py:40
  87.0 9.2 %collective-permute-start.5 = (f32[3,64,256]{2,1,0:T(8,128)S(1)}, f32[3,64,256]{2,1,0:T(8,128)S(1)}, u32[]{:S(2)}, u32[]{:S(2)}) collective-permute-start(f32[3,64,256]{2,1,0:T(8,128)S(1)} %shard_map.75), channel_id=1, source_target_pairs={{0,2},{2,4},{4,6},{6,8},{8,10},{10,12},{12,14},{14,0},{1,3},{3,5},... | collective-permute-start | bytes 589832 | tf_op jit(solution)/shard_map/ppermute | solution.py:40

commit v26 on v25

--- a/solution.py
+++ b/solution.py
@@ -700,10 +700,10 @@
     )
 
 
-def last_update(moving, ctl, got, ground, columns, state, manning, rate, order, *rest):
+def last_update(ctl, got, ground, columns, state, manning, rate, order, *rest):
     del order
-    slot = ctl[MOVE] if moving else 1 - ctl[MOVE]
-    update(STEPS - 1, ctl, got, ground, columns, state, manning, rate, *rest, slots=(slot,))
+    slots = ctl[MOVE], 1 - ctl[MOVE]
+    update(STEPS - 1, ctl, got, ground, columns, state, manning, rate, *rest, slots=slots)
 
 
 def update(
@@ -711,8 +711,8 @@
     passing=None, slots=(0, 1),
 ):
     more = step + 1 < STEPS
-    fresh_out, first_out, second_out, delta_out = rest[:4]
-    rest = rest[4:]
+    fresh_out, *lines_to, delta_out = rest[: 4 if more else 6]
+    rest = rest[4 if more else 6 :]
     state, manning, rate, fresh, got, ground, columns, first, second, delta_keep, sems = rest
     out, columns_out = first, second
     small = start_all(
@@ -793,20 +793,34 @@
         if more:
             best = jnp.where(flag(ctl, WET + 2 * step + 2 + slot), best, 0.0)
             total = jnp.maximum(total, best)
-        target = fresh_out.at[slot, :, part_rows] if more else fresh_out.at[:, part_rows]
-        outgoing += start_all(
-            ((fresh.at[slot, :, part_rows], target),), sems, 3 * PARTS + index
-        )
+        if more:
+            outgoing += start_all(
+                ((fresh.at[slot, :, part_rows], fresh_out.at[slot, :, part_rows]),),
+                sems,
+                3 * PARTS + index,
+            )
+        elif index >= PARTS // 2:
+            outgoing += start_all(
+                ((fresh.at[slot, :, part_rows], fresh_out.at[:, part_rows]),),
+                sems,
+                3 * PARTS + index,
+            )
+        if not more and part_rows.stop == TILE:
+            late, low, high = (
+                (first, *lines_to[:2]) if index < PARTS // 2 else (second, *lines_to[2:])
+            )
+            late_rows(fresh.at[slot], late)
+            outgoing += start_all(
+                ((late.at[:, :HALF], low), (late.at[:, HALF:], high)),
+                sems,
+                4 * PARTS + (0 if index < PARTS // 2 else 2),
+            )
         if passing and index == PARTS // 2:
             passing.middle()
     if more:
         messages(ctl, fresh, None, jnp.max(total, keepdims=True), out, columns_out)
-        outgoing += start_all(((out, first_out), (columns_out, second_out)), sems, 4 * PARTS)
-    else:
-        late_rows(fresh.at[slots[0]], first)
-        outgoing += start_all(
-            ((first.at[:, :HALF], first_out), (first.at[:, HALF:], second_out)), sems, 4 * PARTS
-        )
+        pairs = zip((out, columns_out), lines_to)
+        outgoing += start_all(tuple(pairs), sems, 4 * PARTS)
     wait_all(outgoing)
 
 
@@ -922,7 +936,7 @@
             )(rate, got, leaving[0])
             early_first = [shifted(held, "xb", 1)]
         more = step + 1 < STEPS
-        shapes = (f32(8 * devices, TILE), f32(8, TILE)) if more else (half_shape,) * 2
+        shapes = (f32(8 * devices, TILE), f32(8, TILE)) if more else (half_shape,) * 4
         passing = step == 1
         work = [
             whole,
@@ -933,7 +947,7 @@
             pltpu.VMEM(ground.shape, jnp.float32),
             pltpu.VMEM((8, TILE), jnp.float32),
             buffer(shapes[0] if more else late_shape),
-            buffer(shapes[1]),
+            buffer(shapes[1] if more else late_shape),
             buffer(delta_shape),
             pltpu.SemaphoreType.DMA((5 * PARTS + 4,)),
         ]
@@ -959,25 +973,18 @@
         elif step == 1:
             early_second.append(shifted(passed[0], "xb", 1))
 
-    def finish_step(moving, order):
-        return call(
-            functools.partial(last_update, moving),
-            (tile_shape,) + shapes + (delta_shape,),
-            (hbm(),) * 4,
-            [smem()] + [hbm()] * 7,
-            8 << 20,
-            work,
-            moved=10,
-        )(*operands, order)
-
-    _, late_first, rest_first, delta = finish_step(True, early_second[1])
-    staying, late_second, rest_second, _ = finish_step(False, delta)
+    staying, late_first, rest_first, late_second, rest_second, delta = call(
+        last_update,
+        (tile_shape,) + shapes + (delta_shape,),
+        (hbm(),) * 6,
+        [smem()] + [hbm()] * 7,
+        8 << 20,
+        work,
+        moved=10,
+    )(*operands, early_second[1])
     deltas.append(delta)
     room = 16 << 20
     late_arrived = shifted(late_first, "xb", 1)
-    rest_first = call(hold, half_shape, hbm(), [hbm()] * 3, 1 << 10, aliases={2: 0})(
-        staying, staying, rest_first
-    )
     rest_arrived = shifted(rest_first, "xb", 1)
     second, late_second, rest_second = call(
         repeat_second,

time: 98.6 us -> 96 us (0.974)
  waiting for transfers between devices: 26.3 us -> 19.6 us
  local copies, waits for them, and re-layouts: 3.8 us -> 7.29 us
    ppermute x8, waiting for transfers between devices: 18.1 us -> 11 us  [shifted(): return lax.ppermute(value, axis, pairs)]
    unnamed x38 -> x36, local copies, waits for them, and re-layouts: 3.8 us -> 7.29 us
    pallas_call x1, Pallas kernels: 1.52 us -> 4.95 us  [body(): call(repeat_first, shape, hbm(), [smem()] + [vmem()] * 3 + [anywhere()] *...]
    pallas_call x3 -> x1, Pallas kernels: 7.66 us -> 4.75 us  [body(): call(last_update, (tile_shape,) + shapes + (delta_shape,), (hbm(),) * 6,...]
  transfers between devices with their start and end apart: 11 -> 11, of which waited for: 8 -> 8; matrix products, arithmetic and copies ran while one was open for 0% -> 0% of each run, Pallas kernels for 33% -> 38%
where the time goes in v26:
time: 96 us; the launch traced here: 95.4 us
  Pallas kernels  44.9 us (47%)
  starting transfers between devices  23.2 us (24%)
  waiting for transfers between devices  19.6 us (20%)
  local copies, waits for them, and re-layouts  7.29 us (8%)
    all_to_all x3, starting transfers between devices, spread(): lax.all_to_all(fast, ('xb', 'yb'), split_axis=0, concat_axis=0, tiled=True)  18.8 us
    ppermute x8, waiting for transfers between devices, shifted(): return lax.ppermute(value, axis, pairs)  11 us
    pallas_call x2, Pallas kernels, body(): call(functools.partial(update_and_leaving if passing else update, step),...  9.84 us
    all_to_all x3, waiting for transfers between devices, spread(): lax.all_to_all(fast, ('xb', 'yb'), split_axis=0, concat_axis=0, tiled=True)  8.64 us
    unnamed x36, local copies, waits for them, and re-layouts  7.29 us
    pallas_call x1, Pallas kernels, body(): call(rates_and_splitting, (shape,) + piece_shapes, (hbm(),) * 3, [smem()]...  5.31 us
    pallas_call x1, Pallas kernels, body(): call(rates_and_leaving, (shape, piece_shapes[0]), (hbm(),) * 2, [smem()]...  5.27 us
    pallas_call x1, Pallas kernels, body(): call(rates_after, shape, hbm(), [smem()] + [hbm()] * 3, 16 << 20, scratch)  5.25 us
  transfers between devices with their start and end apart: 11, of which 8 were waited for; matrix products, arithmetic and copies ran while one was open for 0% of the time, Pallas kernels for 38%

profile of v26, /device:TPU:0, one launch (start us, length us, event | category | flops | bytes accessed | tf_op | source)
XLA Modules:
  0.0 95.4 jit_solution(4262585178183980192)
XLA Ops:
  0.0 2.7 %shard_map.64 = (f32[128,384]{1,0:T(8,128)}, f32[8,256]{1,0:T(8,128)}, s32[24]{0:T(128)}) custom-call(f32[2,3,256,256]{3,2,1,0:T(8,128)} %state_first.3, f32[2,256,256]{2,1,0:T(8,128)} %bed_in.9, s32[4,32]{1,0:T(4,128)} %bitcast.17, s32[3,32]{1,0:T(4,128)} %wet_in.1, s32[3,16]{1,0:T(4,128)} %moves_in.1), custom_call_target="tpu_custom_call" | custom-call | flops 4194304 | bytes 4194304 | tf_op jit(solution)/shard_map/pallas_call | solution.py:882
  2.7 7.4 %all-to-all-start = ((f32[16,8,384]{2,1,0:T(8,128)}), f32[16,8,384]{2,1,0:T(8,128)S(1)}, u32[]{:S(2)}, u32[]{:S(2)}) async-start(f32[16,8,384]{2,1,0:T(8,128)} %bitcast.14), calls=%async_computation | async-start | bytes 393216 | tf_op jit(solution)/shard_map/all_to_all | solution.py:863
  10.1 5.3 %shard_map.65 = (f32[2,3,256,256]{3,2,1,0:T(8,128)}, f32[5,80,256]{2,1,0:T(8,128)}, f32[5,64,256]{2,1,0:T(8,128)}) custom-call(s32[24]{0:T(128)} %get-tuple-element.31.ctl, f32[2,3,256,256]{3,2,1,0:T(8,128)} %state_first.3, f32[2,256,256]{2,1,0:T(8,128)} %bed_in.9, f32[2,256,256]{2,1,0:T(8,128)} %manning.1), custom_call_target="tpu_custom_call" | custom-call | flops 16777216 | bytes 4194304 | tf_op jit(solution)/shard_map/pallas_call | solution.py:926
  15.4 3.7 %all-to-all-done = f32[16,8,384]{2,1,0:T(8,128)S(1)} async-done(((f32[16,8,384]{2,1,0:T(8,128)}), f32[16,8,384]{2,1,0:T(8,128)S(1)}, u32[]{:S(2)}, u32[]{:S(2)}) %all-to-all-start) | async-done | bytes 196640 | tf_op jit(solution)/shard_map/all_to_all | solution.py:863
  19.1 0.7 copy-done.15
  19.8 5.0 %shard_map.66 = (f32[2,3,256,256]{3,2,1,0:T(8,128)}, f32[128,256]{1,0:T(8,128)}, f32[8,256]{1,0:T(8,128)}, f32[8,256]{1,0:T(8,128)}) custom-call(s32[24]{0:T(128)} %get-tuple-element.31.ctl, f32[128,384]{1,0:T(8,128)} %bitcast.8, f32[128,384]{1,0:T(8,128)} %bitcast.9, f32[8,256]{1,0:T(8,128)} %get-tuple-element.33.columns_in, ...), custom_call_target="tpu_custom_call" | custom-call | flops 8388608 | bytes 10485760 | tf_op jit(solution)/shard_map/pallas_call | solution.py:957
  24.8 0.6 collective-permute-start.1
  25.4 6.1 %all-to-all-start.1 = ((f32[16,8,256]{2,1,0:T(8,128)}), f32[16,8,256]{2,1,0:T(8,128)S(1)}, u32[]{:S(2)}, u32[]{:S(2)}) async-start(f32[16,8,256]{2,1,0:T(8,128)} %bitcast.15), calls=%async_computation.1 | async-start | bytes 262144 | tf_op jit(solution)/shard_map/all_to_all | solution.py:863
  31.5 3.6 %collective-permute-done.arrived.low = f32[5,80,256]{2,1,0:T(8,128)S(1)} collective-permute-done((f32[5,80,256]{2,1,0:T(8,128)}, f32[5,80,256]{2,1,0:T(8,128)S(1)}, u32[]{:S(2)}, u32[]{:S(2)}) %collective-permute-start) | collective-permute-done | bytes 409632 | tf_op jit(solution)/shard_map/ppermute | solution.py:40
  35.1 0.8 copy-done.2
  35.9 5.3 %shard_map.68 = (f32[2,3,256,256]{3,2,1,0:T(8,128)}, f32[5,80,256]{2,1,0:T(8,128)}) custom-call(s32[24]{0:T(128)} %get-tuple-element.31.ctl, f32[2,3,256,256]{3,2,1,0:T(8,128)} %get-tuple-element.37.state_in, f32[2,256,256]{2,1,0:T(8,128)} %bed_in.9, f32[2,3,256,256]{3,2,1,0:T(8,128)} %state_first.3, f32[2,256,256]{2,1,0:T(8,128)} %manning.1, ...), custom_call_target="tpu_custom_call" | custom-call | flops 16777216 | bytes 4194304 | tf_op jit(solution)/shard_map/pallas_call | solution.py:912
  41.2 1.9 %all-to-all-done.1 = f32[16,8,256]{2,1,0:T(8,128)S(1)} async-done(((f32[16,8,256]{2,1,0:T(8,128)}), f32[16,8,256]{2,1,0:T(8,128)S(1)}, u32[]{:S(2)}, u32[]{:S(2)}) %all-to-all-start.1) | async-done | bytes 131104 | tf_op jit(solution)/shard_map/all_to_all | solution.py:863
  43.1 0.7 copy-done.16
  43.9 4.9 %shard_map.70 = (f32[2,3,256,256]{3,2,1,0:T(8,128)}, f32[128,256]{1,0:T(8,128)}, f32[8,256]{1,0:T(8,128)}, f32[8,256]{1,0:T(8,128)}, f32[5,64,256]{2,1,0:T(8,128)}) custom-call(s32[24]{0:T(128)} %get-tuple-element.31.ctl, f32[128,256]{1,0:T(8,128)} %bitcast.12, f32[128,384]{1,0:T(8,128)} %bitcast.10, f32[8,256]{1,0:T(8,128)} %get-tuple-element.36.columns_in, ...), custom_call_target="tpu_custom_call" | custom-call | flops 8388608 | bytes 10485760 | tf_op jit(solution)/shard_map/pallas_call | solution.py:957
  48.8 0.8 collective-permute-start.3
  49.6 5.3 %all-to-all-start.2 = ((f32[16,8,256]{2,1,0:T(8,128)}), f32[16,8,256]{2,1,0:T(8,128)S(1)}, u32[]{:S(2)}, u32[]{:S(2)}) async-start(f32[16,8,256]{2,1,0:T(8,128)} %bitcast.16), calls=%async_computation.2 | async-start | bytes 262144 | tf_op jit(solution)/shard_map/all_to_all | solution.py:863
  55.0 0.8 copy-done
  55.7 5.3 %shard_map.71.rate = f32[2,3,256,256]{3,2,1,0:T(8,128)} custom-call(s32[24]{0:T(128)} %get-tuple-element.31.ctl, f32[2,3,256,256]{3,2,1,0:T(8,128)} %get-tuple-element.44.state_in.state, f32[2,256,256]{2,1,0:T(8,128)} %bed_in.9, f32[5,80,256]{2,1,0:T(8,128)} %copy-done), custom_call_target="tpu_custom_call" | custom-call | flops 16777216 | bytes 4194304 | tf_op jit(solution)/shard_map/pallas_call | solution.py:922
  61.0 3.0 %all-to-all-done.2 = f32[16,8,256]{2,1,0:T(8,128)S(1)} async-done(((f32[16,8,256]{2,1,0:T(8,128)}), f32[16,8,256]{2,1,0:T(8,128)S(1)}, u32[]{:S(2)}, u32[]{:S(2)}) %all-to-all-start.2) | async-done | bytes 131104 | tf_op jit(solution)/shard_map/all_to_all | solution.py:863
  64.0 0.7 copy-done.17
  64.8 4.7 %shard_map.72 = (f32[3,256,256]{2,1,0:T(8,128)}, f32[3,64,256]{2,1,0:T(8,128)}, f32[3,64,256]{2,1,0:T(8,128)}, f32[3,64,256]{2,1,0:T(8,128)}, f32[3,64,256]{2,1,0:T(8,128)}, /*index=5*/f32[8,256]{1,0:T(8,128)}) custom-call(s32[24]{0:T(128)} %get-tuple-element.31.ctl, f32[128,256]{1,0:T(8,128)} %bitcast.13, f32[128,384]{1,0:T(8,128)} %bitcast.11, ...), custom_call_target="tpu_custom_call" | custom-call | flops 8388608 | bytes 10485760 | tf_op jit(solution)/shard_map/pallas_call | solution.py:976
  69.6 0.8 collective-permute-start.4
  70.4 1.7 %collective-permute-start.6 = (f32[3,64,256]{2,1,0:T(8,128)}, f32[3,64,256]{2,1,0:T(8,128)S(1)}, u32[]{:S(2)}, u32[]{:S(2)}) collective-permute-start(f32[3,64,256]{2,1,0:T(8,128)} %get-tuple-element.54), channel_id=1, source_target_pairs={{0,2},{2,4},{4,6},{6,8},{8,10},{10,12},{12,14},{14,0},{1,3},{3,5},... | collective-permute-start | bytes 589832 | tf_op jit(solution)/shard_map/ppermute | solution.py:40
  72.1 1.0 %copy-done.7 = f32[5,64,256]{2,1,0:T(8,128)S(1)} copy-done((f32[5,64,256]{2,1,0:T(8,128)S(1)}, f32[5,64,256]{2,1,0:T(8,128)}, u32[]{:S(2)}) %copy-start.7) | copy-done | bytes 327704
  73.1 0.9 copy-done.9
  74.0 0.9 copy-done.10
  74.9 0.7 copy-done.14
  75.6 4.2 %shard_map.73 = (f32[3,144,256]{2,1,0:T(8,128)S(1)}, f32[3,64,256]{2,1,0:T(8,128)S(1)}, f32[3,64,256]{2,1,0:T(8,128)S(1)}) custom-call(s32[24]{0:T(128)S(1)} %copy-done.12, f32[8,256]{1,0:T(8,128)S(1)} %copy-done.11, f32[8,256]{1,0:T(8,128)S(1)} %copy-done.13, f32[8,256]{1,0:T(8,128)S(1)} %copy-done.14, f32[5,80,256]{2,1,0:T(8,128)S(1)} %copy-done.1, ...), custom_call_target="tpu_custom_call" | custom-call | flops 8388608 | bytes 4194304 | tf_op jit(solution)/shard_map/pallas_call | solution.py:989
  81.2 2.6 %collective-permute-done.6.arrived.rest_in = f32[3,64,256]{2,1,0:T(8,128)S(1)} collective-permute-done((f32[3,64,256]{2,1,0:T(8,128)}, f32[3,64,256]{2,1,0:T(8,128)S(1)}, u32[]{:S(2)}, u32[]{:S(2)}) %collective-permute-start.6) | collective-permute-done | bytes 196640 | tf_op jit(solution)/shard_map/ppermute | solution.py:40
  84.4 5.0 %shard_map.76.before = f32[2,3,256,256]{3,2,1,0:T(8,128)} custom-call(s32[24]{0:T(128)S(1)} %copy-done.12, f32[8,256]{1,0:T(8,128)S(1)} %copy-done.11, f32[8,256]{1,0:T(8,128)S(1)} %copy-done.13, f32[8,256]{1,0:T(8,128)S(1)} %copy-done.14, f32[5,80,256]{2,1,0:T(8,128)S(1)} %copy-done.3, f32[5,64,256]{2,1,0:T(8,128)S(1)} %copy-done.5, ...), custom_call_target="tpu_custom_call" | custom-call | flops 8388608 | bytes 4194304 | tf_op jit(solution)/shard_map/pallas_call | solution.py:1012
  89.9 3.8 %collective-permute-done.7.rest = f32[3,64,256]{2,1,0:T(8,128)S(1)} collective-permute-done((f32[3,64,256]{2,1,0:T(8,128)S(1)}, f32[3,64,256]{2,1,0:T(8,128)S(1)}, u32[]{:S(2)}, u32[]{:S(2)}) %collective-permute-start.7) | collective-permute-done | bytes 196640 | tf_op jit(solution)/shard_map/ppermute | solution.py:40
  93.7 1.5 %shard_map.77 = f32[2,3,256,256]{3,2,1,0:T(8,128)} custom-call(s32[24]{0:T(128)S(1)} %copy-done.12, f32[3,64,256]{2,1,0:T(8,128)S(1)} %collective-permute-done.5.late, f32[3,64,256]{2,1,0:T(8,128)S(1)} %collective-permute-done.7.rest, f32[3,144,256]{2,1,0:T(8,128)S(1)} %get-tuple-element.53.order.early, ...), custom_call_target="tpu_custom_call", output_to_operand_aliasing={{}: (4, {})} | custom-call | flops 1048576 | bytes 4194304 | tf_op jit(solution)/shard_map/pallas_call | solution.py:1028
  (40 shorter events, 2.8 us)
Async XLA Ops:
  2.7 16.4 %all-to-all-start = ((f32[16,8,384]{2,1,0:T(8,128)}), f32[16,8,384]{2,1,0:T(8,128)S(1)}, u32[]{:S(2)}, u32[]{:S(2)}) async-start(f32[16,8,384]{2,1,0:T(8,128)} %bitcast.14), calls=%async_computation | async-start | bytes 393216 | tf_op jit(solution)/shard_map/all_to_all | solution.py:863
  19.1 0.7 copy-start.15
  19.8 15.3 %collective-permute-start = (f32[5,80,256]{2,1,0:T(8,128)}, f32[5,80,256]{2,1,0:T(8,128)S(1)}, u32[]{:S(2)}, u32[]{:S(2)}) collective-permute-start(f32[5,80,256]{2,1,0:T(8,128)} %shard_map.67), channel_id=1, source_target_pairs={{0,2},{2,4},{4,6},{6,8},{8,10},{10,12},{12,14},{14,0},{1,3},{3,5},... | collective-permute-start | bytes 1228808 | tf_op jit(solution)/shard_map/ppermute | solution.py:40
  24.8 18.4 %collective-permute-start.1 = (f32[5,64,256]{2,1,0:T(8,128)}, f32[5,64,256]{2,1,0:T(8,128)S(1)}, u32[]{:S(2)}, u32[]{:S(2)}) collective-permute-start(f32[5,64,256]{2,1,0:T(8,128)} %shard_map.69), channel_id=1, source_target_pairs={{0,2},{2,4},{4,6},{6,8},{8,10},{10,12},{12,14},{14,0},{1,3},{3,5},... | collective-permute-start | bytes 983048 | tf_op jit(solution)/shard_map/ppermute | solution.py:40
  25.4 17.8 %all-to-all-start.1 = ((f32[16,8,256]{2,1,0:T(8,128)}), f32[16,8,256]{2,1,0:T(8,128)S(1)}, u32[]{:S(2)}, u32[]{:S(2)}) async-start(f32[16,8,256]{2,1,0:T(8,128)} %bitcast.15), calls=%async_computation.1 | async-start | bytes 262144 | tf_op jit(solution)/shard_map/all_to_all | solution.py:863
  35.1 0.8 copy-start.2
  41.1 13.8 %collective-permute-start.2 = (f32[5,80,256]{2,1,0:T(8,128)}, f32[5,80,256]{2,1,0:T(8,128)S(1)}, u32[]{:S(2)}, u32[]{:S(2)}) collective-permute-start(f32[5,80,256]{2,1,0:T(8,128)} %get-tuple-element.45), channel_id=1, source_target_pairs={{0,2},{2,4},{4,6},{6,8},{8,10},{10,12},{12,14},{14,0},{1,3},{3,5},... | collective-permute-start | bytes 1228808 | tf_op jit(solution)/shard_map/ppermute | solution.py:40
  43.1 0.7 copy-start.16
  43.1 0.8 copy-start.4
  48.8 15.2 %collective-permute-start.3 = (f32[5,64,256]{2,1,0:T(8,128)}, f32[5,64,256]{2,1,0:T(8,128)S(1)}, u32[]{:S(2)}, u32[]{:S(2)}) collective-permute-start(f32[5,64,256]{2,1,0:T(8,128)} %get-tuple-element.46), channel_id=1, source_target_pairs={{0,2},{2,4},{4,6},{6,8},{8,10},{10,12},{12,14},{14,0},{1,3},{3,5},... | collective-permute-start | bytes 983048 | tf_op jit(solution)/shard_map/ppermute | solution.py:40
  49.6 14.4 %all-to-all-start.2 = ((f32[16,8,256]{2,1,0:T(8,128)}), f32[16,8,256]{2,1,0:T(8,128)S(1)}, u32[]{:S(2)}, u32[]{:S(2)}) async-start(f32[16,8,256]{2,1,0:T(8,128)} %bitcast.16), calls=%async_computation.2 | async-start | bytes 262144 | tf_op jit(solution)/shard_map/all_to_all | solution.py:863
  55.0 0.8 copy-start
  64.0 0.7 copy-start.17
  64.0 0.8 copy-start.6
  64.8 7.3 %copy-start.1 = (f32[5,80,256]{2,1,0:T(8,128)S(1)}, f32[5,80,256]{2,1,0:T(8,128)}, u32[]{:S(2)}) copy-start(f32[5,80,256]{2,1,0:T(8,128)} %copy-done) | copy-start | bytes 1228804
  64.8 7.3 %copy-start.11 = (f32[8,256]{1,0:T(8,128)S(1)}, f32[8,256]{1,0:T(8,128)}, u32[]{:S(2)}) copy-start(f32[8,256]{1,0:T(8,128)} %get-tuple-element.40.first.second.delta0) | copy-start | bytes 24580
  64.8 7.3 %copy-start.12 = (s32[24]{0:T(128)S(1)}, s32[24]{0:T(128)}, u32[]{:S(2)}) copy-start(s32[24]{0:T(128)} %get-tuple-element.31.ctl) | copy-start | bytes 292
  64.8 7.3 %copy-start.13 = (f32[8,256]{1,0:T(8,128)S(1)}, f32[8,256]{1,0:T(8,128)}, u32[]{:S(2)}) copy-start(f32[8,256]{1,0:T(8,128)} %get-tuple-element.48.delta1) | copy-start | bytes 24580
  69.6 10.7 %collective-permute-start.4 = (f32[3,64,256]{2,1,0:T(8,128)}, f32[3,64,256]{2,1,0:T(8,128)S(1)}, u32[]{:S(2)}, u32[]{:S(2)}) collective-permute-start(f32[3,64,256]{2,1,0:T(8,128)} %get-tuple-element.47), channel_id=1, source_target_pairs={{0,2},{2,4},{4,6},{6,8},{8,10},{10,12},{12,14},{14,0},{1,3},{3,5},... | collective-permute-start | bytes 589832 | tf_op jit(solution)/shard_map/ppermute | solution.py:40
  70.4 13.3 %collective-permute-start.6 = (f32[3,64,256]{2,1,0:T(8,128)}, f32[3,64,256]{2,1,0:T(8,128)S(1)}, u32[]{:S(2)}, u32[]{:S(2)}) collective-permute-start(f32[3,64,256]{2,1,0:T(8,128)} %get-tuple-element.54), channel_id=1, source_target_pairs={{0,2},{2,4},{4,6},{6,8},{8,10},{10,12},{12,14},{14,0},{1,3},{3,5},... | collective-permute-start | bytes 589832 | tf_op jit(solution)/shard_map/ppermute | solution.py:40
  72.1 1.0 %copy-start.7 = (f32[5,64,256]{2,1,0:T(8,128)S(1)}, f32[5,64,256]{2,1,0:T(8,128)}, u32[]{:S(2)}) copy-start(f32[5,64,256]{2,1,0:T(8,128)} %copy-done.6) | copy-start | bytes 983044
  73.1 0.9 copy-start.9
  74.0 0.9 copy-start.10
  74.9 0.7 copy-start.14
  75.6 8.7 %copy-start.3 = (f32[5,80,256]{2,1,0:T(8,128)S(1)}, f32[5,80,256]{2,1,0:T(8,128)}, u32[]{:S(2)}) copy-start(f32[5,80,256]{2,1,0:T(8,128)} %copy-done.2) | copy-start | bytes 1228804
  75.6 8.8 %copy-start.5 = (f32[5,64,256]{2,1,0:T(8,128)S(1)}, f32[5,64,256]{2,1,0:T(8,128)}, u32[]{:S(2)}) copy-start(f32[5,64,256]{2,1,0:T(8,128)} %copy-done.4) | copy-start | bytes 983044
  75.6 8.8 %copy-start.8 = (f32[3,256,256]{2,1,0:T(8,128)S(1)}, f32[3,256,256]{2,1,0:T(8,128)}, u32[]{:S(2)}) copy-start(f32[3,256,256]{2,1,0:T(8,128)} %get-tuple-element.56.staying) | copy-start | bytes 2359300
  80.9 9.0 %collective-permute-start.5 = (f32[3,64,256]{2,1,0:T(8,128)S(1)}, f32[3,64,256]{2,1,0:T(8,128)S(1)}, u32[]{:S(2)}, u32[]{:S(2)}) collective-permute-start(f32[3,64,256]{2,1,0:T(8,128)S(1)} %shard_map.74), channel_id=1, source_target_pairs={{0,2},{2,4},{4,6},{6,8},{8,10},{10,12},{12,14},{14,0},{1,3},{3,5},... | collective-permute-start | bytes 589832 | tf_op jit(solution)/shard_map/ppermute | solution.py:40
  84.3 9.4 %collective-permute-start.7 = (f32[3,64,256]{2,1,0:T(8,128)S(1)}, f32[3,64,256]{2,1,0:T(8,128)S(1)}, u32[]{:S(2)}, u32[]{:S(2)}) collective-permute-start(f32[3,64,256]{2,1,0:T(8,128)S(1)} %shard_map.75), channel_id=1, source_target_pairs={{0,2},{2,4},{4,6},{6,8},{8,10},{10,12},{12,14},{14,0},{1,3},{3,5},... | collective-permute-start | bytes 589832 | tf_op jit(solution)/shard_map/ppermute | solution.py:40

commit v27 on v26

--- a/solution.py
+++ b/solution.py
@@ -25,7 +25,7 @@
 LATE = TILE - EARLY + 16
 HALF = LATE // 2
 CHUNKS = 8
-PARTS = 8
+PARTS = 4
 STRIP = 32
 TOP = 6
 SCALE = 0.5 / SPACING
@@ -990,10 +990,9 @@
         repeat_second,
         (early_state, half_shape, half_shape),
         (anywhere(), vmem(), vmem()),
-        [smem()] + [vmem()] * 3 + [anywhere()] * 4,
+        [smem()] + [vmem()] * 3 + [hbm()] * 4,
         8 << 20,
         [buffer(early_shape), buffer(early_state), pltpu.SemaphoreType.DMA((4,))],
-        room=room,
     )(ctl, *deltas, *early_second, late_second, rest_second)
 
     def pass_late(arrived, own):

time: 96 us -> 97.1 us (1.011)
  waiting for transfers between devices: 19.6 us -> 23.5 us
  Pallas kernels: 44.9 us -> 42.9 us
    ppermute x8, waiting for transfers between devices: 11 us -> 15.2 us  [shifted(): return lax.ppermute(value, axis, pairs)]
    pallas_call x1, Pallas kernels: 4.95 us -> 1.52 us  [body(): call(repeat_first, shape, hbm(), [smem()] + [vmem()] * 3 + [anywhere()] *...]
    pallas_call x1, Pallas kernels: 4.16 us -> 6.41 us  [body(): call(repeat_second, (early_state, half_shape, half_shape), (anywhere(), v...]
  transfers between devices with their start and end apart: 11 -> 11, of which waited for: 8 -> 8; matrix products, arithmetic and copies ran while one was open for 0% -> 0% of each run, Pallas kernels for 38% -> 35%
where the time goes in v27:
time: 97.1 us; the launch traced here: 96.4 us
  Pallas kernels  42.9 us (44%)
  waiting for transfers between devices  23.5 us (24%)
  starting transfers between devices  22.9 us (24%)
  local copies, waits for them, and re-layouts  6.65 us (7%)
    all_to_all x3, starting transfers between devices, spread(): lax.all_to_all(fast, ('xb', 'yb'), split_axis=0, concat_axis=0, tiled=True)  18.8 us
    ppermute x8, waiting for transfers between devices, shifted(): return lax.ppermute(value, axis, pairs)  15.2 us
    pallas_call x2, Pallas kernels, body(): call(functools.partial(update_and_leaving if passing else update, step),...  9.26 us
    all_to_all x3, waiting for transfers between devices, spread(): lax.all_to_all(fast, ('xb', 'yb'), split_axis=0, concat_axis=0, tiled=True)  8.32 us
    unnamed x36, local copies, waits for them, and re-layouts  6.65 us
    pallas_call x1, Pallas kernels, body(): call(repeat_second, (early_state, half_shape, half_shape), (anywhere(), v...  6.41 us
    pallas_call x1, Pallas kernels, body(): call(rates_and_splitting, (shape,) + piece_shapes, (hbm(),) * 3, [smem()]...  5.31 us
    pallas_call x1, Pallas kernels, body(): call(rates_and_leaving, (shape, piece_shapes[0]), (hbm(),) * 2, [smem()]...  5.27 us
  transfers between devices with their start and end apart: 11, of which 8 were waited for; matrix products, arithmetic and copies ran while one was open for 0% of the time, Pallas kernels for 35%

profile of v27, /device:TPU:0, one launch (start us, length us, event | category | flops | bytes accessed | tf_op | source)
XLA Modules:
  0.0 96.4 jit_solution(11297330237180557793)
XLA Ops:
  0.0 2.7 %shard_map.64 = (f32[128,384]{1,0:T(8,128)}, f32[8,256]{1,0:T(8,128)}, s32[24]{0:T(128)}) custom-call(f32[2,3,256,256]{3,2,1,0:T(8,128)} %state_first.3, f32[2,256,256]{2,1,0:T(8,128)} %bed_in.9, s32[4,32]{1,0:T(4,128)} %bitcast.17, s32[3,32]{1,0:T(4,128)} %wet_in.1, s32[3,16]{1,0:T(4,128)} %moves_in.1), custom_call_target="tpu_custom_call" | custom-call | flops 4194304 | bytes 4194304 | tf_op jit(solution)/shard_map/pallas_call | solution.py:882
  2.7 7.4 %all-to-all-start = ((f32[16,8,384]{2,1,0:T(8,128)}), f32[16,8,384]{2,1,0:T(8,128)S(1)}, u32[]{:S(2)}, u32[]{:S(2)}) async-start(f32[16,8,384]{2,1,0:T(8,128)} %bitcast.14), calls=%async_computation | async-start | bytes 393216 | tf_op jit(solution)/shard_map/all_to_all | solution.py:863
  10.1 5.3 %shard_map.65 = (f32[2,3,256,256]{3,2,1,0:T(8,128)}, f32[5,80,256]{2,1,0:T(8,128)}, f32[5,64,256]{2,1,0:T(8,128)}) custom-call(s32[24]{0:T(128)} %get-tuple-element.31.ctl, f32[2,3,256,256]{3,2,1,0:T(8,128)} %state_first.3, f32[2,256,256]{2,1,0:T(8,128)} %bed_in.9, f32[2,256,256]{2,1,0:T(8,128)} %manning.1), custom_call_target="tpu_custom_call" | custom-call | flops 16777216 | bytes 4194304 | tf_op jit(solution)/shard_map/pallas_call | solution.py:926
  15.4 3.7 %all-to-all-done = f32[16,8,384]{2,1,0:T(8,128)S(1)} async-done(((f32[16,8,384]{2,1,0:T(8,128)}), f32[16,8,384]{2,1,0:T(8,128)S(1)}, u32[]{:S(2)}, u32[]{:S(2)}) %all-to-all-start) | async-done | bytes 196640 | tf_op jit(solution)/shard_map/all_to_all | solution.py:863
  19.1 0.7 copy-done.13
  19.8 4.6 %shard_map.66 = (f32[2,3,256,256]{3,2,1,0:T(8,128)}, f32[128,256]{1,0:T(8,128)}, f32[8,256]{1,0:T(8,128)}, f32[8,256]{1,0:T(8,128)}) custom-call(s32[24]{0:T(128)} %get-tuple-element.31.ctl, f32[128,384]{1,0:T(8,128)} %bitcast.8, f32[128,384]{1,0:T(8,128)} %bitcast.9, f32[8,256]{1,0:T(8,128)} %get-tuple-element.33.columns_in, ...), custom_call_target="tpu_custom_call" | custom-call | flops 8388608 | bytes 10485760 | tf_op jit(solution)/shard_map/pallas_call | solution.py:957
  25.0 6.1 %all-to-all-start.1 = ((f32[16,8,256]{2,1,0:T(8,128)}), f32[16,8,256]{2,1,0:T(8,128)S(1)}, u32[]{:S(2)}, u32[]{:S(2)}) async-start(f32[16,8,256]{2,1,0:T(8,128)} %bitcast.15), calls=%async_computation.1 | async-start | bytes 262144 | tf_op jit(solution)/shard_map/all_to_all | solution.py:863
  31.2 4.0 %collective-permute-done.arrived.low = f32[5,80,256]{2,1,0:T(8,128)S(1)} collective-permute-done((f32[5,80,256]{2,1,0:T(8,128)}, f32[5,80,256]{2,1,0:T(8,128)S(1)}, u32[]{:S(2)}, u32[]{:S(2)}) %collective-permute-start) | collective-permute-done | bytes 409632 | tf_op jit(solution)/shard_map/ppermute | solution.py:40
  35.1 0.8 copy-done.2
  35.9 5.3 %shard_map.68 = (f32[2,3,256,256]{3,2,1,0:T(8,128)}, f32[5,80,256]{2,1,0:T(8,128)}) custom-call(s32[24]{0:T(128)} %get-tuple-element.31.ctl, f32[2,3,256,256]{3,2,1,0:T(8,128)} %get-tuple-element.37.state_in, f32[2,256,256]{2,1,0:T(8,128)} %bed_in.9, f32[2,3,256,256]{3,2,1,0:T(8,128)} %state_first.3, f32[2,256,256]{2,1,0:T(8,128)} %manning.1, ...), custom_call_target="tpu_custom_call" | custom-call | flops 16777216 | bytes 4194304 | tf_op jit(solution)/shard_map/pallas_call | solution.py:912
  41.3 1.9 %all-to-all-done.1 = f32[16,8,256]{2,1,0:T(8,128)S(1)} async-done(((f32[16,8,256]{2,1,0:T(8,128)}), f32[16,8,256]{2,1,0:T(8,128)S(1)}, u32[]{:S(2)}, u32[]{:S(2)}) %all-to-all-start.1) | async-done | bytes 131104 | tf_op jit(solution)/shard_map/all_to_all | solution.py:863
  43.1 0.6 copy-done.16
  43.9 4.6 %shard_map.70 = (f32[2,3,256,256]{3,2,1,0:T(8,128)}, f32[128,256]{1,0:T(8,128)}, f32[8,256]{1,0:T(8,128)}, f32[8,256]{1,0:T(8,128)}, f32[5,64,256]{2,1,0:T(8,128)}) custom-call(s32[24]{0:T(128)} %get-tuple-element.31.ctl, f32[128,256]{1,0:T(8,128)} %bitcast.12, f32[128,384]{1,0:T(8,128)} %bitcast.10, f32[8,256]{1,0:T(8,128)} %get-tuple-element.36.columns_in, ...), custom_call_target="tpu_custom_call" | custom-call | flops 8388608 | bytes 10485760 | tf_op jit(solution)/shard_map/pallas_call | solution.py:957
  48.5 0.8 collective-permute-start.3
  49.4 5.3 %all-to-all-start.2 = ((f32[16,8,256]{2,1,0:T(8,128)}), f32[16,8,256]{2,1,0:T(8,128)S(1)}, u32[]{:S(2)}, u32[]{:S(2)}) async-start(f32[16,8,256]{2,1,0:T(8,128)} %bitcast.16), calls=%async_computation.2 | async-start | bytes 262144 | tf_op jit(solution)/shard_map/all_to_all | solution.py:863
  54.7 0.8 copy-done.14
  55.5 5.3 %shard_map.71.rate = f32[2,3,256,256]{3,2,1,0:T(8,128)} custom-call(s32[24]{0:T(128)} %get-tuple-element.31.ctl, f32[2,3,256,256]{3,2,1,0:T(8,128)} %get-tuple-element.44.state_in.state, f32[2,256,256]{2,1,0:T(8,128)} %bed_in.9, f32[5,80,256]{2,1,0:T(8,128)} %copy-done.14), custom_call_target="tpu_custom_call" | custom-call | flops 16777216 | bytes 4194304 | tf_op jit(solution)/shard_map/pallas_call | solution.py:922
  60.7 2.8 %all-to-all-done.2 = f32[16,8,256]{2,1,0:T(8,128)S(1)} async-done(((f32[16,8,256]{2,1,0:T(8,128)}), f32[16,8,256]{2,1,0:T(8,128)S(1)}, u32[]{:S(2)}, u32[]{:S(2)}) %all-to-all-start.2) | async-done | bytes 131104 | tf_op jit(solution)/shard_map/all_to_all | solution.py:863
  63.5 0.6 copy-done.17
  64.3 4.6 %shard_map.72 = (f32[3,256,256]{2,1,0:T(8,128)}, f32[3,64,256]{2,1,0:T(8,128)}, f32[3,64,256]{2,1,0:T(8,128)}, f32[3,64,256]{2,1,0:T(8,128)}, f32[3,64,256]{2,1,0:T(8,128)}, /*index=5*/f32[8,256]{1,0:T(8,128)}) custom-call(s32[24]{0:T(128)} %get-tuple-element.31.ctl, f32[128,256]{1,0:T(8,128)} %bitcast.13, f32[128,384]{1,0:T(8,128)} %bitcast.11, ...), custom_call_target="tpu_custom_call" | custom-call | flops 8388608 | bytes 10485760 | tf_op jit(solution)/shard_map/pallas_call | solution.py:976
  68.9 0.9 collective-permute-start.4
  69.7 1.6 %collective-permute-start.6 = (f32[3,64,256]{2,1,0:T(8,128)}, f32[3,64,256]{2,1,0:T(8,128)S(1)}, u32[]{:S(2)}, u32[]{:S(2)}) collective-permute-start(f32[3,64,256]{2,1,0:T(8,128)} %get-tuple-element.54), channel_id=1, source_target_pairs={{0,2},{2,4},{4,6},{6,8},{8,10},{10,12},{12,14},{14,0},{1,3},{3,5},... | collective-permute-start | bytes 589832 | tf_op jit(solution)/shard_map/ppermute | solution.py:40
  71.4 6.4 %shard_map.73 = (f32[3,144,256]{2,1,0:T(8,128)}, f32[3,64,256]{2,1,0:T(8,128)}, f32[3,64,256]{2,1,0:T(8,128)}) custom-call(s32[24]{0:T(128)} %get-tuple-element.31.ctl, f32[8,256]{1,0:T(8,128)} %get-tuple-element.40.first.second.delta0, f32[8,256]{1,0:T(8,128)} %get-tuple-element.48.delta1, f32[8,256]{1,0:T(8,128)} %get-tuple-element.49.delta2, ...), custom_call_target="tpu_custom_call" | custom-call | flops 8388608 | bytes 4194304 | tf_op jit(solution)/shard_map/pallas_call | solution.py:989
  77.8 1.8 %collective-permute-done.4.arrived.late_in = f32[3,64,256]{2,1,0:T(8,128)S(1)} collective-permute-done((f32[3,64,256]{2,1,0:T(8,128)}, f32[3,64,256]{2,1,0:T(8,128)S(1)}, u32[]{:S(2)}, u32[]{:S(2)}) %collective-permute-start.4) | collective-permute-done | bytes 196640 | tf_op jit(solution)/shard_map/ppermute | solution.py:40
  79.6 1.0 %copy-done = f32[3,144,256]{2,1,0:T(8,128)S(1)} copy-done((f32[3,144,256]{2,1,0:T(8,128)S(1)}, f32[3,144,256]{2,1,0:T(8,128)}, u32[]{:S(2)}) %copy-start) | copy-done | bytes 442392
  80.6 0.9 copy-done.8
  82.2 0.8 collective-permute-done.6.arrived.rest_in
  83.0 0.9 copy-done.7
  84.6 1.5 %shard_map.76.before = f32[2,3,256,256]{3,2,1,0:T(8,128)} custom-call(s32[24]{0:T(128)S(1)} %copy-done.10, f32[8,256]{1,0:T(8,128)S(1)} %copy-done.9, f32[8,256]{1,0:T(8,128)S(1)} %copy-done.11, f32[8,256]{1,0:T(8,128)S(1)} %copy-done.12, f32[5,80,256]{2,1,0:T(8,128)S(1)} %copy-done.3, f32[5,64,256]{2,1,0:T(8,128)S(1)} %copy-done.5, ...), custom_call_target="tpu_custom_call" | custom-call | flops 8388608 | bytes 4194304 | tf_op jit(solution)/shard_map/pallas_call | solution.py:1011
  86.1 5.9 %collective-permute-done.5.late = f32[3,64,256]{2,1,0:T(8,128)S(1)} collective-permute-done((f32[3,64,256]{2,1,0:T(8,128)S(1)}, f32[3,64,256]{2,1,0:T(8,128)S(1)}, u32[]{:S(2)}, u32[]{:S(2)}) %collective-permute-start.5) | collective-permute-done | bytes 196640 | tf_op jit(solution)/shard_map/ppermute | solution.py:40
  92.0 2.7 %collective-permute-done.7.rest = f32[3,64,256]{2,1,0:T(8,128)S(1)} collective-permute-done((f32[3,64,256]{2,1,0:T(8,128)S(1)}, f32[3,64,256]{2,1,0:T(8,128)S(1)}, u32[]{:S(2)}, u32[]{:S(2)}) %collective-permute-start.7) | collective-permute-done | bytes 196640 | tf_op jit(solution)/shard_map/ppermute | solution.py:40
  94.7 1.5 %shard_map.77 = f32[2,3,256,256]{3,2,1,0:T(8,128)} custom-call(s32[24]{0:T(128)S(1)} %copy-done.10, f32[3,64,256]{2,1,0:T(8,128)S(1)} %collective-permute-done.5.late, f32[3,64,256]{2,1,0:T(8,128)S(1)} %collective-permute-done.7.rest, f32[3,144,256]{2,1,0:T(8,128)S(1)} %copy-done.1, f32[2,3,256,256]{3,2,1,0:T(8,128)} %shard_map.76.before), custom_call_target="tpu_custom_call", output_to_operand_aliasing={{}: (4, {})} | custom-call | flops 1048576 | bytes 4194304 | tf_op jit(solution)/shard_map/pallas_call | solution.py:1027
  (40 shorter events, 2.2 us)
Async XLA Ops:
  2.7 16.4 %all-to-all-start = ((f32[16,8,384]{2,1,0:T(8,128)}), f32[16,8,384]{2,1,0:T(8,128)S(1)}, u32[]{:S(2)}, u32[]{:S(2)}) async-start(f32[16,8,384]{2,1,0:T(8,128)} %bitcast.14), calls=%async_computation | async-start | bytes 393216 | tf_op jit(solution)/shard_map/all_to_all | solution.py:863
  19.1 0.7 copy-start.13
  19.8 15.4 %collective-permute-start = (f32[5,80,256]{2,1,0:T(8,128)}, f32[5,80,256]{2,1,0:T(8,128)S(1)}, u32[]{:S(2)}, u32[]{:S(2)}) collective-permute-start(f32[5,80,256]{2,1,0:T(8,128)} %shard_map.67), channel_id=1, source_target_pairs={{0,2},{2,4},{4,6},{6,8},{8,10},{10,12},{12,14},{14,0},{1,3},{3,5},... | collective-permute-start | bytes 1228808 | tf_op jit(solution)/shard_map/ppermute | solution.py:40
  24.4 18.7 %collective-permute-start.1 = (f32[5,64,256]{2,1,0:T(8,128)}, f32[5,64,256]{2,1,0:T(8,128)S(1)}, u32[]{:S(2)}, u32[]{:S(2)}) collective-permute-start(f32[5,64,256]{2,1,0:T(8,128)} %shard_map.69), channel_id=1, source_target_pairs={{0,2},{2,4},{4,6},{6,8},{8,10},{10,12},{12,14},{14,0},{1,3},{3,5},... | collective-permute-start | bytes 983048 | tf_op jit(solution)/shard_map/ppermute | solution.py:40
  25.0 18.1 %all-to-all-start.1 = ((f32[16,8,256]{2,1,0:T(8,128)}), f32[16,8,256]{2,1,0:T(8,128)S(1)}, u32[]{:S(2)}, u32[]{:S(2)}) async-start(f32[16,8,256]{2,1,0:T(8,128)} %bitcast.15), calls=%async_computation.1 | async-start | bytes 262144 | tf_op jit(solution)/shard_map/all_to_all | solution.py:863
  35.1 0.8 copy-start.2
  41.2 13.5 %collective-permute-start.2 = (f32[5,80,256]{2,1,0:T(8,128)}, f32[5,80,256]{2,1,0:T(8,128)S(1)}, u32[]{:S(2)}, u32[]{:S(2)}) collective-permute-start(f32[5,80,256]{2,1,0:T(8,128)} %get-tuple-element.45), channel_id=1, source_target_pairs={{0,2},{2,4},{4,6},{6,8},{8,10},{10,12},{12,14},{14,0},{1,3},{3,5},... | collective-permute-start | bytes 1228808 | tf_op jit(solution)/shard_map/ppermute | solution.py:40
  43.1 0.6 copy-start.16
  43.1 0.8 copy-start.4
  48.5 15.0 %collective-permute-start.3 = (f32[5,64,256]{2,1,0:T(8,128)}, f32[5,64,256]{2,1,0:T(8,128)S(1)}, u32[]{:S(2)}, u32[]{:S(2)}) collective-permute-start(f32[5,64,256]{2,1,0:T(8,128)} %get-tuple-element.46), channel_id=1, source_target_pairs={{0,2},{2,4},{4,6},{6,8},{8,10},{10,12},{12,14},{14,0},{1,3},{3,5},... | collective-permute-start | bytes 983048 | tf_op jit(solution)/shard_map/ppermute | solution.py:40
  49.4 14.2 %all-to-all-start.2 = ((f32[16,8,256]{2,1,0:T(8,128)}), f32[16,8,256]{2,1,0:T(8,128)S(1)}, u32[]{:S(2)}, u32[]{:S(2)}) async-start(f32[16,8,256]{2,1,0:T(8,128)} %bitcast.16), calls=%async_computation.2 | async-start | bytes 262144 | tf_op jit(solution)/shard_map/all_to_all | solution.py:863
  54.7 0.8 copy-start.14
  63.5 0.7 copy-start.17
  63.5 0.8 copy-start.15
  64.3 15.3 %copy-start.10 = (s32[24]{0:T(128)S(1)}, s32[24]{0:T(128)}, u32[]{:S(2)}) copy-start(s32[24]{0:T(128)} %get-tuple-element.31.ctl) | copy-start | bytes 292
  68.9 10.7 %collective-permute-start.4 = (f32[3,64,256]{2,1,0:T(8,128)}, f32[3,64,256]{2,1,0:T(8,128)S(1)}, u32[]{:S(2)}, u32[]{:S(2)}) collective-permute-start(f32[3,64,256]{2,1,0:T(8,128)} %get-tuple-element.47), channel_id=1, source_target_pairs={{0,2},{2,4},{4,6},{6,8},{8,10},{10,12},{12,14},{14,0},{1,3},{3,5},... | collective-permute-start | bytes 589832 | tf_op jit(solution)/shard_map/ppermute | solution.py:40
  69.7 13.2 %collective-permute-start.6 = (f32[3,64,256]{2,1,0:T(8,128)}, f32[3,64,256]{2,1,0:T(8,128)S(1)}, u32[]{:S(2)}, u32[]{:S(2)}) collective-permute-start(f32[3,64,256]{2,1,0:T(8,128)} %get-tuple-element.54), channel_id=1, source_target_pairs={{0,2},{2,4},{4,6},{6,8},{8,10},{10,12},{12,14},{14,0},{1,3},{3,5},... | collective-permute-start | bytes 589832 | tf_op jit(solution)/shard_map/ppermute | solution.py:40
  71.3 13.2 %copy-start.3 = (f32[5,80,256]{2,1,0:T(8,128)S(1)}, f32[5,80,256]{2,1,0:T(8,128)}, u32[]{:S(2)}) copy-start(f32[5,80,256]{2,1,0:T(8,128)} %copy-done.2) | copy-start | bytes 1228804
  71.3 13.2 %copy-start.5 = (f32[5,64,256]{2,1,0:T(8,128)S(1)}, f32[5,64,256]{2,1,0:T(8,128)}, u32[]{:S(2)}) copy-start(f32[5,64,256]{2,1,0:T(8,128)} %copy-done.4) | copy-start | bytes 983044
  71.3 13.2 %copy-start.9 = (f32[8,256]{1,0:T(8,128)S(1)}, f32[8,256]{1,0:T(8,128)}, u32[]{:S(2)}) copy-start(f32[8,256]{1,0:T(8,128)} %get-tuple-element.40.first.second.delta0) | copy-start | bytes 24580
  71.3 13.2 %copy-start.11 = (f32[8,256]{1,0:T(8,128)S(1)}, f32[8,256]{1,0:T(8,128)}, u32[]{:S(2)}) copy-start(f32[8,256]{1,0:T(8,128)} %get-tuple-element.48.delta1) | copy-start | bytes 24580
  71.4 13.2 %copy-start.12 = (f32[8,256]{1,0:T(8,128)S(1)}, f32[8,256]{1,0:T(8,128)}, u32[]{:S(2)}) copy-start(f32[8,256]{1,0:T(8,128)} %get-tuple-element.49.delta2) | copy-start | bytes 24580
  79.6 1.0 %copy-start = (f32[3,144,256]{2,1,0:T(8,128)S(1)}, f32[3,144,256]{2,1,0:T(8,128)}, u32[]{:S(2)}) copy-start(f32[3,144,256]{2,1,0:T(8,128)} %get-tuple-element.53.order.early) | copy-start | bytes 1327108
  80.6 0.9 copy-start.8
  81.5 3.1 %copy-start.6 = (f32[3,256,256]{2,1,0:T(8,128)S(1)}, f32[3,256,256]{2,1,0:T(8,128)}, u32[]{:S(2)}) copy-start(f32[3,256,256]{2,1,0:T(8,128)} %get-tuple-element.56.staying) | copy-start | bytes 2359300
  82.1 9.9 %collective-permute-start.5 = (f32[3,64,256]{2,1,0:T(8,128)S(1)}, f32[3,64,256]{2,1,0:T(8,128)S(1)}, u32[]{:S(2)}, u32[]{:S(2)}) collective-permute-start(f32[3,64,256]{2,1,0:T(8,128)S(1)} %shard_map.74), channel_id=1, source_target_pairs={{0,2},{2,4},{4,6},{6,8},{8,10},{10,12},{12,14},{14,0},{1,3},{3,5},... | collective-permute-start | bytes 589832 | tf_op jit(solution)/shard_map/ppermute | solution.py:40
  83.0 0.9 copy-start.7
  84.5 10.3 %collective-permute-start.7 = (f32[3,64,256]{2,1,0:T(8,128)S(1)}, f32[3,64,256]{2,1,0:T(8,128)S(1)}, u32[]{:S(2)}, u32[]{:S(2)}) collective-permute-start(f32[3,64,256]{2,1,0:T(8,128)S(1)} %shard_map.75), channel_id=1, source_target_pairs={{0,2},{2,4},{4,6},{6,8},{8,10},{10,12},{12,14},{14,0},{1,3},{3,5},... | collective-permute-start | bytes 589832 | tf_op jit(solution)/shard_map/ppermute | solution.py:40
  84.6 10.1 %copy-start.1 = (f32[3,144,256]{2,1,0:T(8,128)S(1)}, f32[3,144,256]{2,1,0:T(8,128)}, u32[]{:S(2)}) copy-start(f32[3,144,256]{2,1,0:T(8,128)} %get-tuple-element.53.order.early) | copy-start | bytes 1327108

commit v28 on v26

--- a/solution.py
+++ b/solution.py
@@ -25,7 +25,7 @@
 LATE = TILE - EARLY + 16
 HALF = LATE // 2
 CHUNKS = 8
-PARTS = 8
+PARTS = 4
 STRIP = 32
 TOP = 6
 SCALE = 0.5 / SPACING

time: 96 us -> 95.4 us (level)
  transfers between devices with their start and end apart: 11 -> 11, of which waited for: 8 -> 8; matrix products, arithmetic and copies ran while one was open for 0% -> 0% of each run, Pallas kernels for 38% -> 37%
where the time goes in v28:
time: 95.4 us; the launch traced here: 94.7 us
  Pallas kernels  44.1 us (46%)
  starting transfers between devices  23.2 us (24%)
  waiting for transfers between devices  19.8 us (21%)
  local copies, waits for them, and re-layouts  7.29 us (8%)
    all_to_all x3, starting transfers between devices, spread(): lax.all_to_all(fast, ('xb', 'yb'), split_axis=0, concat_axis=0, tiled=True)  18.8 us
    ppermute x8, waiting for transfers between devices, shifted(): return lax.ppermute(value, axis, pairs)  11.4 us
    pallas_call x2, Pallas kernels, body(): call(functools.partial(update_and_leaving if passing else update, step),...  9.23 us
    all_to_all x3, waiting for transfers between devices, spread(): lax.all_to_all(fast, ('xb', 'yb'), split_axis=0, concat_axis=0, tiled=True)  8.36 us
    unnamed x36, local copies, waits for them, and re-layouts  7.29 us
    pallas_call x1, Pallas kernels, body(): call(rates_and_splitting, (shape,) + piece_shapes, (hbm(),) * 3, [smem()]...  5.31 us
    pallas_call x1, Pallas kernels, body(): call(rates_and_leaving, (shape, piece_shapes[0]), (hbm(),) * 2, [smem()]...  5.27 us
    pallas_call x1, Pallas kernels, body(): call(rates_after, shape, hbm(), [smem()] + [hbm()] * 3, 16 << 20, scratch)  5.25 us
  transfers between devices with their start and end apart: 11, of which 8 were waited for; matrix products, arithmetic and copies ran while one was open for 0% of the time, Pallas kernels for 37%

profile of v28, /device:TPU:0, one launch (start us, length us, event | category | flops | bytes accessed | tf_op | source)
XLA Modules:
  0.0 94.7 jit_solution(13942216832378431767)
XLA Ops:
  0.0 2.7 %shard_map.64 = (f32[128,384]{1,0:T(8,128)}, f32[8,256]{1,0:T(8,128)}, s32[24]{0:T(128)}) custom-call(f32[2,3,256,256]{3,2,1,0:T(8,128)} %state_first.3, f32[2,256,256]{2,1,0:T(8,128)} %bed_in.9, s32[4,32]{1,0:T(4,128)} %bitcast.17, s32[3,32]{1,0:T(4,128)} %wet_in.1, s32[3,16]{1,0:T(4,128)} %moves_in.1), custom_call_target="tpu_custom_call" | custom-call | flops 4194304 | bytes 4194304 | tf_op jit(solution)/shard_map/pallas_call | solution.py:882
  2.7 7.4 %all-to-all-start = ((f32[16,8,384]{2,1,0:T(8,128)}), f32[16,8,384]{2,1,0:T(8,128)S(1)}, u32[]{:S(2)}, u32[]{:S(2)}) async-start(f32[16,8,384]{2,1,0:T(8,128)} %bitcast.14), calls=%async_computation | async-start | bytes 393216 | tf_op jit(solution)/shard_map/all_to_all | solution.py:863
  10.1 5.3 %shard_map.65 = (f32[2,3,256,256]{3,2,1,0:T(8,128)}, f32[5,80,256]{2,1,0:T(8,128)}, f32[5,64,256]{2,1,0:T(8,128)}) custom-call(s32[24]{0:T(128)} %get-tuple-element.31.ctl, f32[2,3,256,256]{3,2,1,0:T(8,128)} %state_first.3, f32[2,256,256]{2,1,0:T(8,128)} %bed_in.9, f32[2,256,256]{2,1,0:T(8,128)} %manning.1), custom_call_target="tpu_custom_call" | custom-call | flops 16777216 | bytes 4194304 | tf_op jit(solution)/shard_map/pallas_call | solution.py:926
  15.4 3.7 %all-to-all-done = f32[16,8,384]{2,1,0:T(8,128)S(1)} async-done(((f32[16,8,384]{2,1,0:T(8,128)}), f32[16,8,384]{2,1,0:T(8,128)S(1)}, u32[]{:S(2)}, u32[]{:S(2)}) %all-to-all-start) | async-done | bytes 196640 | tf_op jit(solution)/shard_map/all_to_all | solution.py:863
  19.1 0.7 copy-done.15
  19.8 4.6 %shard_map.66 = (f32[2,3,256,256]{3,2,1,0:T(8,128)}, f32[128,256]{1,0:T(8,128)}, f32[8,256]{1,0:T(8,128)}, f32[8,256]{1,0:T(8,128)}) custom-call(s32[24]{0:T(128)} %get-tuple-element.31.ctl, f32[128,384]{1,0:T(8,128)} %bitcast.8, f32[128,384]{1,0:T(8,128)} %bitcast.9, f32[8,256]{1,0:T(8,128)} %get-tuple-element.33.columns_in, ...), custom_call_target="tpu_custom_call" | custom-call | flops 8388608 | bytes 10485760 | tf_op jit(solution)/shard_map/pallas_call | solution.py:957
  24.4 0.6 collective-permute-start.1
  25.0 6.1 %all-to-all-start.1 = ((f32[16,8,256]{2,1,0:T(8,128)}), f32[16,8,256]{2,1,0:T(8,128)S(1)}, u32[]{:S(2)}, u32[]{:S(2)}) async-start(f32[16,8,256]{2,1,0:T(8,128)} %bitcast.15), calls=%async_computation.1 | async-start | bytes 262144 | tf_op jit(solution)/shard_map/all_to_all | solution.py:863
  31.1 4.0 %collective-permute-done.arrived.low = f32[5,80,256]{2,1,0:T(8,128)S(1)} collective-permute-done((f32[5,80,256]{2,1,0:T(8,128)}, f32[5,80,256]{2,1,0:T(8,128)S(1)}, u32[]{:S(2)}, u32[]{:S(2)}) %collective-permute-start) | collective-permute-done | bytes 409632 | tf_op jit(solution)/shard_map/ppermute | solution.py:40
  35.1 0.8 copy-done.2
  35.9 5.3 %shard_map.68 = (f32[2,3,256,256]{3,2,1,0:T(8,128)}, f32[5,80,256]{2,1,0:T(8,128)}) custom-call(s32[24]{0:T(128)} %get-tuple-element.31.ctl, f32[2,3,256,256]{3,2,1,0:T(8,128)} %get-tuple-element.37.state_in, f32[2,256,256]{2,1,0:T(8,128)} %bed_in.9, f32[2,3,256,256]{3,2,1,0:T(8,128)} %state_first.3, f32[2,256,256]{2,1,0:T(8,128)} %manning.1, ...), custom_call_target="tpu_custom_call" | custom-call | flops 16777216 | bytes 4194304 | tf_op jit(solution)/shard_map/pallas_call | solution.py:912
  41.2 1.9 %all-to-all-done.1 = f32[16,8,256]{2,1,0:T(8,128)S(1)} async-done(((f32[16,8,256]{2,1,0:T(8,128)}), f32[16,8,256]{2,1,0:T(8,128)S(1)}, u32[]{:S(2)}, u32[]{:S(2)}) %all-to-all-start.1) | async-done | bytes 131104 | tf_op jit(solution)/shard_map/all_to_all | solution.py:863
  43.1 0.7 copy-done.16
  43.9 4.6 %shard_map.70 = (f32[2,3,256,256]{3,2,1,0:T(8,128)}, f32[128,256]{1,0:T(8,128)}, f32[8,256]{1,0:T(8,128)}, f32[8,256]{1,0:T(8,128)}, f32[5,64,256]{2,1,0:T(8,128)}) custom-call(s32[24]{0:T(128)} %get-tuple-element.31.ctl, f32[128,256]{1,0:T(8,128)} %bitcast.12, f32[128,384]{1,0:T(8,128)} %bitcast.10, f32[8,256]{1,0:T(8,128)} %get-tuple-element.36.columns_in, ...), custom_call_target="tpu_custom_call" | custom-call | flops 8388608 | bytes 10485760 | tf_op jit(solution)/shard_map/pallas_call | solution.py:957
  48.5 0.8 collective-permute-start.3
  49.4 5.3 %all-to-all-start.2 = ((f32[16,8,256]{2,1,0:T(8,128)}), f32[16,8,256]{2,1,0:T(8,128)S(1)}, u32[]{:S(2)}, u32[]{:S(2)}) async-start(f32[16,8,256]{2,1,0:T(8,128)} %bitcast.16), calls=%async_computation.2 | async-start | bytes 262144 | tf_op jit(solution)/shard_map/all_to_all | solution.py:863
  54.7 0.8 copy-done
  55.5 5.3 %shard_map.71.rate = f32[2,3,256,256]{3,2,1,0:T(8,128)} custom-call(s32[24]{0:T(128)} %get-tuple-element.31.ctl, f32[2,3,256,256]{3,2,1,0:T(8,128)} %get-tuple-element.44.state_in.state, f32[2,256,256]{2,1,0:T(8,128)} %bed_in.9, f32[5,80,256]{2,1,0:T(8,128)} %copy-done), custom_call_target="tpu_custom_call" | custom-call | flops 16777216 | bytes 4194304 | tf_op jit(solution)/shard_map/pallas_call | solution.py:922
  60.7 2.8 %all-to-all-done.2 = f32[16,8,256]{2,1,0:T(8,128)S(1)} async-done(((f32[16,8,256]{2,1,0:T(8,128)}), f32[16,8,256]{2,1,0:T(8,128)S(1)}, u32[]{:S(2)}, u32[]{:S(2)}) %all-to-all-start.2) | async-done | bytes 131104 | tf_op jit(solution)/shard_map/all_to_all | solution.py:863
  63.6 0.7 copy-done.17
  64.3 4.6 %shard_map.72 = (f32[3,256,256]{2,1,0:T(8,128)}, f32[3,64,256]{2,1,0:T(8,128)}, f32[3,64,256]{2,1,0:T(8,128)}, f32[3,64,256]{2,1,0:T(8,128)}, f32[3,64,256]{2,1,0:T(8,128)}, /*index=5*/f32[8,256]{1,0:T(8,128)}) custom-call(s32[24]{0:T(128)} %get-tuple-element.31.ctl, f32[128,256]{1,0:T(8,128)} %bitcast.13, f32[128,384]{1,0:T(8,128)} %bitcast.11, ...), custom_call_target="tpu_custom_call" | custom-call | flops 8388608 | bytes 10485760 | tf_op jit(solution)/shard_map/pallas_call | solution.py:976
  68.9 0.8 collective-permute-start.4
  69.8 1.7 %collective-permute-start.6 = (f32[3,64,256]{2,1,0:T(8,128)}, f32[3,64,256]{2,1,0:T(8,128)S(1)}, u32[]{:S(2)}, u32[]{:S(2)}) collective-permute-start(f32[3,64,256]{2,1,0:T(8,128)} %get-tuple-element.54), channel_id=1, source_target_pairs={{0,2},{2,4},{4,6},{6,8},{8,10},{10,12},{12,14},{14,0},{1,3},{3,5},... | collective-permute-start | bytes 589832 | tf_op jit(solution)/shard_map/ppermute | solution.py:40
  71.4 1.0 %copy-done.7 = f32[5,64,256]{2,1,0:T(8,128)S(1)} copy-done((f32[5,64,256]{2,1,0:T(8,128)S(1)}, f32[5,64,256]{2,1,0:T(8,128)}, u32[]{:S(2)}) %copy-start.7) | copy-done | bytes 327704
  72.4 0.9 copy-done.9
  73.3 0.9 copy-done.10
  74.3 0.7 copy-done.14
  75.0 4.2 %shard_map.73 = (f32[3,144,256]{2,1,0:T(8,128)S(1)}, f32[3,64,256]{2,1,0:T(8,128)S(1)}, f32[3,64,256]{2,1,0:T(8,128)S(1)}) custom-call(s32[24]{0:T(128)S(1)} %copy-done.12, f32[8,256]{1,0:T(8,128)S(1)} %copy-done.11, f32[8,256]{1,0:T(8,128)S(1)} %copy-done.13, f32[8,256]{1,0:T(8,128)S(1)} %copy-done.14, f32[5,80,256]{2,1,0:T(8,128)S(1)} %copy-done.1, ...), custom_call_target="tpu_custom_call" | custom-call | flops 8388608 | bytes 4194304 | tf_op jit(solution)/shard_map/pallas_call | solution.py:989
  80.5 2.6 %collective-permute-done.6.arrived.rest_in = f32[3,64,256]{2,1,0:T(8,128)S(1)} collective-permute-done((f32[3,64,256]{2,1,0:T(8,128)}, f32[3,64,256]{2,1,0:T(8,128)S(1)}, u32[]{:S(2)}, u32[]{:S(2)}) %collective-permute-start.6) | collective-permute-done | bytes 196640 | tf_op jit(solution)/shard_map/ppermute | solution.py:40
  83.7 5.0 %shard_map.76.before = f32[2,3,256,256]{3,2,1,0:T(8,128)} custom-call(s32[24]{0:T(128)S(1)} %copy-done.12, f32[8,256]{1,0:T(8,128)S(1)} %copy-done.11, f32[8,256]{1,0:T(8,128)S(1)} %copy-done.13, f32[8,256]{1,0:T(8,128)S(1)} %copy-done.14, f32[5,80,256]{2,1,0:T(8,128)S(1)} %copy-done.3, f32[5,64,256]{2,1,0:T(8,128)S(1)} %copy-done.5, ...), custom_call_target="tpu_custom_call" | custom-call | flops 8388608 | bytes 4194304 | tf_op jit(solution)/shard_map/pallas_call | solution.py:1012
  89.3 3.8 %collective-permute-done.7.rest = f32[3,64,256]{2,1,0:T(8,128)S(1)} collective-permute-done((f32[3,64,256]{2,1,0:T(8,128)S(1)}, f32[3,64,256]{2,1,0:T(8,128)S(1)}, u32[]{:S(2)}, u32[]{:S(2)}) %collective-permute-start.7) | collective-permute-done | bytes 196640 | tf_op jit(solution)/shard_map/ppermute | solution.py:40
  93.0 1.5 %shard_map.77 = f32[2,3,256,256]{3,2,1,0:T(8,128)} custom-call(s32[24]{0:T(128)S(1)} %copy-done.12, f32[3,64,256]{2,1,0:T(8,128)S(1)} %collective-permute-done.5.late, f32[3,64,256]{2,1,0:T(8,128)S(1)} %collective-permute-done.7.rest, f32[3,144,256]{2,1,0:T(8,128)S(1)} %get-tuple-element.53.order.early, ...), custom_call_target="tpu_custom_call", output_to_operand_aliasing={{}: (4, {})} | custom-call | flops 1048576 | bytes 4194304 | tf_op jit(solution)/shard_map/pallas_call | solution.py:1028
  (40 shorter events, 2.9 us)
Async XLA Ops:
  2.7 16.4 %all-to-all-start = ((f32[16,8,384]{2,1,0:T(8,128)}), f32[16,8,384]{2,1,0:T(8,128)S(1)}, u32[]{:S(2)}, u32[]{:S(2)}) async-start(f32[16,8,384]{2,1,0:T(8,128)} %bitcast.14), calls=%async_computation | async-start | bytes 393216 | tf_op jit(solution)/shard_map/all_to_all | solution.py:863
  19.1 0.7 copy-start.15
  19.8 15.4 %collective-permute-start = (f32[5,80,256]{2,1,0:T(8,128)}, f32[5,80,256]{2,1,0:T(8,128)S(1)}, u32[]{:S(2)}, u32[]{:S(2)}) collective-permute-start(f32[5,80,256]{2,1,0:T(8,128)} %shard_map.67), channel_id=1, source_target_pairs={{0,2},{2,4},{4,6},{6,8},{8,10},{10,12},{12,14},{14,0},{1,3},{3,5},... | collective-permute-start | bytes 1228808 | tf_op jit(solution)/shard_map/ppermute | solution.py:40
  24.4 18.7 %collective-permute-start.1 = (f32[5,64,256]{2,1,0:T(8,128)}, f32[5,64,256]{2,1,0:T(8,128)S(1)}, u32[]{:S(2)}, u32[]{:S(2)}) collective-permute-start(f32[5,64,256]{2,1,0:T(8,128)} %shard_map.69), channel_id=1, source_target_pairs={{0,2},{2,4},{4,6},{6,8},{8,10},{10,12},{12,14},{14,0},{1,3},{3,5},... | collective-permute-start | bytes 983048 | tf_op jit(solution)/shard_map/ppermute | solution.py:40
  25.0 18.1 %all-to-all-start.1 = ((f32[16,8,256]{2,1,0:T(8,128)}), f32[16,8,256]{2,1,0:T(8,128)S(1)}, u32[]{:S(2)}, u32[]{:S(2)}) async-start(f32[16,8,256]{2,1,0:T(8,128)} %bitcast.15), calls=%async_computation.1 | async-start | bytes 262144 | tf_op jit(solution)/shard_map/all_to_all | solution.py:863
  35.1 0.8 copy-start.2
  41.2 13.5 %collective-permute-start.2 = (f32[5,80,256]{2,1,0:T(8,128)}, f32[5,80,256]{2,1,0:T(8,128)S(1)}, u32[]{:S(2)}, u32[]{:S(2)}) collective-permute-start(f32[5,80,256]{2,1,0:T(8,128)} %get-tuple-element.45), channel_id=1, source_target_pairs={{0,2},{2,4},{4,6},{6,8},{8,10},{10,12},{12,14},{14,0},{1,3},{3,5},... | collective-permute-start | bytes 1228808 | tf_op jit(solution)/shard_map/ppermute | solution.py:40
  43.1 0.7 copy-start.16
  43.1 0.8 copy-start.4
  48.5 15.0 %collective-permute-start.3 = (f32[5,64,256]{2,1,0:T(8,128)}, f32[5,64,256]{2,1,0:T(8,128)S(1)}, u32[]{:S(2)}, u32[]{:S(2)}) collective-permute-start(f32[5,64,256]{2,1,0:T(8,128)} %get-tuple-element.46), channel_id=1, source_target_pairs={{0,2},{2,4},{4,6},{6,8},{8,10},{10,12},{12,14},{14,0},{1,3},{3,5},... | collective-permute-start | bytes 983048 | tf_op jit(solution)/shard_map/ppermute | solution.py:40
  49.4 14.2 %all-to-all-start.2 = ((f32[16,8,256]{2,1,0:T(8,128)}), f32[16,8,256]{2,1,0:T(8,128)S(1)}, u32[]{:S(2)}, u32[]{:S(2)}) async-start(f32[16,8,256]{2,1,0:T(8,128)} %bitcast.16), calls=%async_computation.2 | async-start | bytes 262144 | tf_op jit(solution)/shard_map/all_to_all | solution.py:863
  54.7 0.8 copy-start
  63.5 0.7 copy-start.17
  63.5 0.8 copy-start.6
  64.3 7.1 %copy-start.1 = (f32[5,80,256]{2,1,0:T(8,128)S(1)}, f32[5,80,256]{2,1,0:T(8,128)}, u32[]{:S(2)}) copy-start(f32[5,80,256]{2,1,0:T(8,128)} %copy-done) | copy-start | bytes 1228804
  64.3 7.1 %copy-start.11 = (f32[8,256]{1,0:T(8,128)S(1)}, f32[8,256]{1,0:T(8,128)}, u32[]{:S(2)}) copy-start(f32[8,256]{1,0:T(8,128)} %get-tuple-element.40.first.second.delta0) | copy-start | bytes 24580
  64.3 7.1 %copy-start.12 = (s32[24]{0:T(128)S(1)}, s32[24]{0:T(128)}, u32[]{:S(2)}) copy-start(s32[24]{0:T(128)} %get-tuple-element.31.ctl) | copy-start | bytes 292
  64.3 7.1 %copy-start.13 = (f32[8,256]{1,0:T(8,128)S(1)}, f32[8,256]{1,0:T(8,128)}, u32[]{:S(2)}) copy-start(f32[8,256]{1,0:T(8,128)} %get-tuple-element.48.delta1) | copy-start | bytes 24580
  68.9 10.7 %collective-permute-start.4 = (f32[3,64,256]{2,1,0:T(8,128)}, f32[3,64,256]{2,1,0:T(8,128)S(1)}, u32[]{:S(2)}, u32[]{:S(2)}) collective-permute-start(f32[3,64,256]{2,1,0:T(8,128)} %get-tuple-element.47), channel_id=1, source_target_pairs={{0,2},{2,4},{4,6},{6,8},{8,10},{10,12},{12,14},{14,0},{1,3},{3,5},... | collective-permute-start | bytes 589832 | tf_op jit(solution)/shard_map/ppermute | solution.py:40
  69.8 13.3 %collective-permute-start.6 = (f32[3,64,256]{2,1,0:T(8,128)}, f32[3,64,256]{2,1,0:T(8,128)S(1)}, u32[]{:S(2)}, u32[]{:S(2)}) collective-permute-start(f32[3,64,256]{2,1,0:T(8,128)} %get-tuple-element.54), channel_id=1, source_target_pairs={{0,2},{2,4},{4,6},{6,8},{8,10},{10,12},{12,14},{14,0},{1,3},{3,5},... | collective-permute-start | bytes 589832 | tf_op jit(solution)/shard_map/ppermute | solution.py:40
  71.4 1.0 %copy-start.7 = (f32[5,64,256]{2,1,0:T(8,128)S(1)}, f32[5,64,256]{2,1,0:T(8,128)}, u32[]{:S(2)}) copy-start(f32[5,64,256]{2,1,0:T(8,128)} %copy-done.6) | copy-start | bytes 983044
  72.4 0.9 copy-start.9
  73.3 0.9 copy-start.10
  74.3 0.7 copy-start.14
  74.9 8.7 %copy-start.3 = (f32[5,80,256]{2,1,0:T(8,128)S(1)}, f32[5,80,256]{2,1,0:T(8,128)}, u32[]{:S(2)}) copy-start(f32[5,80,256]{2,1,0:T(8,128)} %copy-done.2) | copy-start | bytes 1228804
  75.0 8.8 %copy-start.5 = (f32[5,64,256]{2,1,0:T(8,128)S(1)}, f32[5,64,256]{2,1,0:T(8,128)}, u32[]{:S(2)}) copy-start(f32[5,64,256]{2,1,0:T(8,128)} %copy-done.4) | copy-start | bytes 983044
  75.0 8.8 %copy-start.8 = (f32[3,256,256]{2,1,0:T(8,128)S(1)}, f32[3,256,256]{2,1,0:T(8,128)}, u32[]{:S(2)}) copy-start(f32[3,256,256]{2,1,0:T(8,128)} %get-tuple-element.56.staying) | copy-start | bytes 2359300
  80.2 9.1 %collective-permute-start.5 = (f32[3,64,256]{2,1,0:T(8,128)S(1)}, f32[3,64,256]{2,1,0:T(8,128)S(1)}, u32[]{:S(2)}, u32[]{:S(2)}) collective-permute-start(f32[3,64,256]{2,1,0:T(8,128)S(1)} %shard_map.74), channel_id=1, source_target_pairs={{0,2},{2,4},{4,6},{6,8},{8,10},{10,12},{12,14},{14,0},{1,3},{3,5},... | collective-permute-start | bytes 589832 | tf_op jit(solution)/shard_map/ppermute | solution.py:40
  83.6 9.4 %collective-permute-start.7 = (f32[3,64,256]{2,1,0:T(8,128)S(1)}, f32[3,64,256]{2,1,0:T(8,128)S(1)}, u32[]{:S(2)}, u32[]{:S(2)}) collective-permute-start(f32[3,64,256]{2,1,0:T(8,128)S(1)} %shard_map.75), channel_id=1, source_target_pairs={{0,2},{2,4},{4,6},{6,8},{8,10},{10,12},{12,14},{14,0},{1,3},{3,5},... | collective-permute-start | bytes 589832 | tf_op jit(solution)/shard_map/ppermute | solution.py:40

commit v29 on v28

--- a/solution.py
+++ b/solution.py
@@ -20,7 +20,7 @@
 WET_FIRST, WET_SECOND = 16, 19
 CONTROLS = 24
 EARLY = 144
-PIECES = ((0, 80), (80, 144))
+PIECES = ((0, 72), (72, 144))
 AGAIN = 48
 LATE = TILE - EARLY + 16
 HALF = LATE // 2
@@ -591,7 +591,8 @@
             value = jnp.where(row < 5, value, first)
         tile[field, rows, :] = value
     tile[field, EARLY : TILE - HALF, :] = late[field, 16:, :]
-    tile[field, TILE - HALF :, :] = rest[field]
+    if rest is not None:
+        tile[field, TILE - HALF :, :] = rest[field]
 
 
 def repeat_second(
@@ -623,15 +624,20 @@
     wait_all(start_all(((tile, kept),), sems))
 
 
-def finish(ctl, late, rest, early, before, out, tile, sems):
+def finish_late(ctl, late, early, before, out, tile, sems):
     del before
     copies = []
     for field in range(3):
-        merge_field(field, late, rest, early, tile)
+        merge_field(field, late, None, early, tile)
         copies += start_all(
-            ((tile.at[field], out.at[ctl[MOVE + 1], field]),), sems, field
+            ((tile.at[field], out.at[ctl[MOVE + 1], field, 0 : TILE - HALF]),), sems, field
         )
     wait_all(copies)
+
+
+def finish_rest(ctl, rest, before, out, sems):
+    del before
+    wait_all(start_all(((rest, out.at[ctl[MOVE + 1], :, TILE - HALF :]),), sems))
 
 
 def second_late(ctl, arrived, own, order, leaving):
@@ -1025,16 +1031,26 @@
         ],
         room=room,
     )(ctl, *deltas, *early_first, late_arrived, rest_arrived, staying)
-    return call(
-        finish,
+    final = call(
+        finish_late,
         shape,
         hbm(),
-        [smem(), vmem(), vmem(), vmem(), hbm()],
+        [smem(), vmem(), vmem(), hbm()],
         1 << 20,
-        [buffer(tile_shape), pltpu.SemaphoreType.DMA((3,))],
-        {4: 0},
+        [pltpu.VMEM((3, TILE - HALF, TILE), jnp.float32), pltpu.SemaphoreType.DMA((3,))],
+        {3: 0},
         room=room,
-    )(ctl, late_next, rest_next, second, final)
+    )(ctl, late_next, second, final)
+    return call(
+        finish_rest,
+        shape,
+        hbm(),
+        [smem(), vmem(), hbm()],
+        1 << 20,
+        [pltpu.SemaphoreType.DMA((1,))],
+        {2: 0},
+        room=room,
+    )(ctl, rest_next, final)
 
 
 def solution(mesh):

time: 95.4 us -> 102 us (1.069)
  starting transfers between devices: 23.2 us -> 32.1 us
  waiting for transfers between devices: 19.8 us -> 16.1 us
  Pallas kernels: 44.1 us -> 45.3 us
    all_to_all x3, starting transfers between devices: 18.8 us -> 24.4 us  [spread(): lax.all_to_all(fast, ('xb', 'yb'), split_axis=0, concat_axis=0, tiled=True)]
    ppermute x8, waiting for transfers between devices: 11.4 us -> 7.59 us  [shifted(): return lax.ppermute(value, axis, pairs)]
    ppermute x8, starting transfers between devices: 4.38 us -> 7.73 us  [shifted(): return lax.ppermute(value, axis, pairs)]
    pallas_call x1 -> x2, Pallas kernels: 1.53 us -> 2.69 us  [the longest x1 1.46 us: body(): call(finish_late, shape, hbm(), [smem(), vmem(), vmem(), hbm()], 1 << 20,...]
  transfers between devices with their start and end apart: 11 -> 11, of which waited for: 8 -> 7; matrix products, arithmetic and copies ran while one was open for 0% -> 0% of each run, Pallas kernels for 37% -> 36%
where the time goes in v29:
time: 102 us; the launch traced here: 101 us
  Pallas kernels  45.3 us (44%)
  starting transfers between devices  32.1 us (31%)
  waiting for transfers between devices  16.1 us (16%)
  local copies, waits for them, and re-layouts  7.27 us (7%)
    all_to_all x3, starting transfers between devices, spread(): lax.all_to_all(fast, ('xb', 'yb'), split_axis=0, concat_axis=0, tiled=True)  24.4 us
    pallas_call x2, Pallas kernels, body(): call(functools.partial(update_and_leaving if passing else update, step),...  9.23 us
    all_to_all x3, waiting for transfers between devices, spread(): lax.all_to_all(fast, ('xb', 'yb'), split_axis=0, concat_axis=0, tiled=True)  8.46 us
    ppermute x8, starting transfers between devices, shifted(): return lax.ppermute(value, axis, pairs)  7.73 us
    ppermute x8, waiting for transfers between devices, shifted(): return lax.ppermute(value, axis, pairs)  7.59 us
    unnamed x36, local copies, waits for them, and re-layouts  7.27 us
    pallas_call x1, Pallas kernels, body(): call(rates_and_splitting, (shape,) + piece_shapes, (hbm(),) * 3, [smem()]...  5.31 us
    pallas_call x1, Pallas kernels, body(): call(rates_and_leaving, (shape, piece_shapes[0]), (hbm(),) * 2, [smem()]...  5.27 us
  transfers between devices with their start and end apart: 11, of which 7 were waited for; matrix products, arithmetic and copies ran while one was open for 0% of the time, Pallas kernels for 36%

profile of v29, /device:TPU:0, one launch (start us, length us, event | category | flops | bytes accessed | tf_op | source)
XLA Modules:
  0.0 101.1 jit_solution(12871542173970384349)
XLA Ops:
  0.0 2.7 %shard_map.64 = (f32[128,384]{1,0:T(8,128)}, f32[8,256]{1,0:T(8,128)}, s32[24]{0:T(128)}) custom-call(f32[2,3,256,256]{3,2,1,0:T(8,128)} %state_first.3, f32[2,256,256]{2,1,0:T(8,128)} %bed_in.9, s32[4,32]{1,0:T(4,128)} %bitcast.17, s32[3,32]{1,0:T(4,128)} %wet_in.1, s32[3,16]{1,0:T(4,128)} %moves_in.1), custom_call_target="tpu_custom_call" | custom-call | flops 4194304 | bytes 4194304 | tf_op jit(solution)/shard_map/pallas_call | solution.py:888
  2.7 7.4 %all-to-all-start = ((f32[16,8,384]{2,1,0:T(8,128)}), f32[16,8,384]{2,1,0:T(8,128)S(1)}, u32[]{:S(2)}, u32[]{:S(2)}) async-start(f32[16,8,384]{2,1,0:T(8,128)} %bitcast.14), calls=%async_computation | async-start | bytes 393216 | tf_op jit(solution)/shard_map/all_to_all | solution.py:869
  10.1 5.3 %shard_map.65 = (f32[2,3,256,256]{3,2,1,0:T(8,128)}, f32[5,72,256]{2,1,0:T(8,128)}, f32[5,72,256]{2,1,0:T(8,128)}) custom-call(s32[24]{0:T(128)} %get-tuple-element.31.ctl, f32[2,3,256,256]{3,2,1,0:T(8,128)} %state_first.3, f32[2,256,256]{2,1,0:T(8,128)} %bed_in.9, f32[2,256,256]{2,1,0:T(8,128)} %manning.1), custom_call_target="tpu_custom_call" | custom-call | flops 16777216 | bytes 4194304 | tf_op jit(solution)/shard_map/pallas_call | solution.py:932
  15.4 3.7 %all-to-all-done = f32[16,8,384]{2,1,0:T(8,128)S(1)} async-done(((f32[16,8,384]{2,1,0:T(8,128)}), f32[16,8,384]{2,1,0:T(8,128)S(1)}, u32[]{:S(2)}, u32[]{:S(2)}) %all-to-all-start) | async-done | bytes 196640 | tf_op jit(solution)/shard_map/all_to_all | solution.py:869
  19.1 0.7 copy-done.15
  19.8 4.6 %shard_map.66 = (f32[2,3,256,256]{3,2,1,0:T(8,128)}, f32[128,256]{1,0:T(8,128)}, f32[8,256]{1,0:T(8,128)}, f32[8,256]{1,0:T(8,128)}) custom-call(s32[24]{0:T(128)} %get-tuple-element.31.ctl, f32[128,384]{1,0:T(8,128)} %bitcast.8, f32[128,384]{1,0:T(8,128)} %bitcast.9, f32[8,256]{1,0:T(8,128)} %get-tuple-element.33.columns_in, ...), custom_call_target="tpu_custom_call" | custom-call | flops 8388608 | bytes 10485760 | tf_op jit(solution)/shard_map/pallas_call | solution.py:963
  25.0 6.1 %all-to-all-start.1 = ((f32[16,8,256]{2,1,0:T(8,128)}), f32[16,8,256]{2,1,0:T(8,128)S(1)}, u32[]{:S(2)}, u32[]{:S(2)}) async-start(f32[16,8,256]{2,1,0:T(8,128)} %bitcast.15), calls=%async_computation.1 | async-start | bytes 262144 | tf_op jit(solution)/shard_map/all_to_all | solution.py:869
  31.1 3.0 %collective-permute-done.arrived.low = f32[5,72,256]{2,1,0:T(8,128)S(1)} collective-permute-done((f32[5,72,256]{2,1,0:T(8,128)}, f32[5,72,256]{2,1,0:T(8,128)S(1)}, u32[]{:S(2)}, u32[]{:S(2)}) %collective-permute-start) | collective-permute-done | bytes 368672 | tf_op jit(solution)/shard_map/ppermute | solution.py:40
  34.2 0.7 copy-done
  34.9 5.3 %shard_map.68 = (f32[2,3,256,256]{3,2,1,0:T(8,128)}, f32[5,72,256]{2,1,0:T(8,128)}) custom-call(s32[24]{0:T(128)} %get-tuple-element.31.ctl, f32[2,3,256,256]{3,2,1,0:T(8,128)} %get-tuple-element.37.state_in, f32[2,256,256]{2,1,0:T(8,128)} %bed_in.9, f32[2,3,256,256]{3,2,1,0:T(8,128)} %state_first.3, f32[2,256,256]{2,1,0:T(8,128)} %manning.1, ...), custom_call_target="tpu_custom_call" | custom-call | flops 16777216 | bytes 4194304 | tf_op jit(solution)/shard_map/pallas_call | solution.py:918
  40.2 2.9 %all-to-all-done.1 = f32[16,8,256]{2,1,0:T(8,128)S(1)} async-done(((f32[16,8,256]{2,1,0:T(8,128)}), f32[16,8,256]{2,1,0:T(8,128)S(1)}, u32[]{:S(2)}, u32[]{:S(2)}) %all-to-all-start.1) | async-done | bytes 131104 | tf_op jit(solution)/shard_map/all_to_all | solution.py:869
  43.9 4.6 %shard_map.70 = (f32[2,3,256,256]{3,2,1,0:T(8,128)}, f32[128,256]{1,0:T(8,128)}, f32[8,256]{1,0:T(8,128)}, f32[8,256]{1,0:T(8,128)}, f32[5,72,256]{2,1,0:T(8,128)}) custom-call(s32[24]{0:T(128)} %get-tuple-element.31.ctl, f32[128,256]{1,0:T(8,128)} %bitcast.12, f32[128,384]{1,0:T(8,128)} %bitcast.10, f32[8,256]{1,0:T(8,128)} %get-tuple-element.36.columns_in, ...), custom_call_target="tpu_custom_call" | custom-call | flops 8388608 | bytes 10485760 | tf_op jit(solution)/shard_map/pallas_call | solution.py:963
  48.5 0.8 collective-permute-start.3
  49.4 10.9 %all-to-all-start.2 = ((f32[16,8,256]{2,1,0:T(8,128)}), f32[16,8,256]{2,1,0:T(8,128)S(1)}, u32[]{:S(2)}, u32[]{:S(2)}) async-start(f32[16,8,256]{2,1,0:T(8,128)} %bitcast.16), calls=%async_computation.2 | async-start | bytes 262144 | tf_op jit(solution)/shard_map/all_to_all | solution.py:869
  60.3 0.7 copy-done.4
  61.1 5.3 %shard_map.71.rate = f32[2,3,256,256]{3,2,1,0:T(8,128)} custom-call(s32[24]{0:T(128)} %get-tuple-element.31.ctl, f32[2,3,256,256]{3,2,1,0:T(8,128)} %get-tuple-element.44.state_in.state, f32[2,256,256]{2,1,0:T(8,128)} %bed_in.9, f32[5,72,256]{2,1,0:T(8,128)} %copy-done.4), custom_call_target="tpu_custom_call" | custom-call | flops 16777216 | bytes 4194304 | tf_op jit(solution)/shard_map/pallas_call | solution.py:928
  66.3 1.9 %all-to-all-done.2 = f32[16,8,256]{2,1,0:T(8,128)S(1)} async-done(((f32[16,8,256]{2,1,0:T(8,128)}), f32[16,8,256]{2,1,0:T(8,128)S(1)}, u32[]{:S(2)}, u32[]{:S(2)}) %all-to-all-start.2) | async-done | bytes 131104 | tf_op jit(solution)/shard_map/all_to_all | solution.py:869
  69.0 4.6 %shard_map.72 = (f32[3,256,256]{2,1,0:T(8,128)}, f32[3,64,256]{2,1,0:T(8,128)}, f32[3,64,256]{2,1,0:T(8,128)}, f32[3,64,256]{2,1,0:T(8,128)}, f32[3,64,256]{2,1,0:T(8,128)}, /*index=5*/f32[8,256]{1,0:T(8,128)}) custom-call(s32[24]{0:T(128)} %get-tuple-element.31.ctl, f32[128,256]{1,0:T(8,128)} %bitcast.13, f32[128,384]{1,0:T(8,128)} %bitcast.11, ...), custom_call_target="tpu_custom_call" | custom-call | flops 8388608 | bytes 10485760 | tf_op jit(solution)/shard_map/pallas_call | solution.py:982
  73.7 1.7 %collective-permute-start.6 = (f32[3,64,256]{2,1,0:T(8,128)}, f32[3,64,256]{2,1,0:T(8,128)S(1)}, u32[]{:S(2)}, u32[]{:S(2)}) collective-permute-start(f32[3,64,256]{2,1,0:T(8,128)} %get-tuple-element.54), channel_id=1, source_target_pairs={{0,2},{2,4},{4,6},{6,8},{8,10},{10,12},{12,14},{14,0},{1,3},{3,5},... | collective-permute-start | bytes 589832 | tf_op jit(solution)/shard_map/ppermute | solution.py:40
  75.4 3.4 %collective-permute-start.4 = (f32[3,64,256]{2,1,0:T(8,128)}, f32[3,64,256]{2,1,0:T(8,128)S(1)}, u32[]{:S(2)}, u32[]{:S(2)}) collective-permute-start(f32[3,64,256]{2,1,0:T(8,128)} %get-tuple-element.47), channel_id=1, source_target_pairs={{0,2},{2,4},{4,6},{6,8},{8,10},{10,12},{12,14},{14,0},{1,3},{3,5},... | collective-permute-start | bytes 589832 | tf_op jit(solution)/shard_map/ppermute | solution.py:40
  78.8 1.0 copy-done.7
  79.8 0.9 copy-done.9
  80.7 0.9 copy-done.10
  81.7 0.7 copy-done.14
  82.4 4.2 %shard_map.73 = (f32[3,144,256]{2,1,0:T(8,128)S(1)}, f32[3,64,256]{2,1,0:T(8,128)S(1)}, f32[3,64,256]{2,1,0:T(8,128)S(1)}) custom-call(s32[24]{0:T(128)S(1)} %copy-done.12, f32[8,256]{1,0:T(8,128)S(1)} %copy-done.11, f32[8,256]{1,0:T(8,128)S(1)} %copy-done.13, f32[8,256]{1,0:T(8,128)S(1)} %copy-done.14, f32[5,72,256]{2,1,0:T(8,128)S(1)} %copy-done.5, ...), custom_call_target="tpu_custom_call" | custom-call | flops 8388608 | bytes 4194304 | tf_op jit(solution)/shard_map/pallas_call | solution.py:995
  87.2 1.1 %collective-permute-done.4.arrived.rest_in = f32[3,64,256]{2,1,0:T(8,128)S(1)} collective-permute-done((f32[3,64,256]{2,1,0:T(8,128)}, f32[3,64,256]{2,1,0:T(8,128)S(1)}, u32[]{:S(2)}, u32[]{:S(2)}) %collective-permute-start.4) | collective-permute-done | bytes 196640 | tf_op jit(solution)/shard_map/ppermute | solution.py:40
  88.9 1.0 collective-permute-start.5
  89.8 4.9 %shard_map.76.before = f32[2,3,256,256]{3,2,1,0:T(8,128)} custom-call(s32[24]{0:T(128)S(1)} %copy-done.12, f32[8,256]{1,0:T(8,128)S(1)} %copy-done.11, f32[8,256]{1,0:T(8,128)S(1)} %copy-done.13, f32[8,256]{1,0:T(8,128)S(1)} %copy-done.14, f32[5,72,256]{2,1,0:T(8,128)S(1)} %copy-done.1, f32[5,72,256]{2,1,0:T(8,128)S(1)} %copy-done.3, ...), custom_call_target="tpu_custom_call" | custom-call | flops 8388608 | bytes 4194304 | tf_op jit(solution)/shard_map/pallas_call | solution.py:1018
  94.8 2.3 %collective-permute-done.7.late = f32[3,64,256]{2,1,0:T(8,128)S(1)} collective-permute-done((f32[3,64,256]{2,1,0:T(8,128)S(1)}, f32[3,64,256]{2,1,0:T(8,128)S(1)}, u32[]{:S(2)}, u32[]{:S(2)}) %collective-permute-start.7) | collective-permute-done | bytes 196640 | tf_op jit(solution)/shard_map/ppermute | solution.py:40
  97.1 1.5 %shard_map.77.before = f32[2,3,256,256]{3,2,1,0:T(8,128)} custom-call(s32[24]{0:T(128)S(1)} %copy-done.12, f32[3,64,256]{2,1,0:T(8,128)S(1)} %collective-permute-done.7.late, f32[3,144,256]{2,1,0:T(8,128)S(1)} %get-tuple-element.53.order.early, f32[2,3,256,256]{3,2,1,0:T(8,128)} %shard_map.76.before), custom_call_target="tpu_custom_call", output_to_operand_aliasing={{}: (3, {})} | custom-call | flops 1048576 | bytes 4194304 | tf_op jit(solution)/shard_map/pallas_call | solution.py:1034
  98.6 1.2 %collective-permute-done.5.rest = f32[3,64,256]{2,1,0:T(8,128)S(1)} collective-permute-done((f32[3,64,256]{2,1,0:T(8,128)S(1)}, f32[3,64,256]{2,1,0:T(8,128)S(1)}, u32[]{:S(2)}, u32[]{:S(2)}) %collective-permute-start.5) | collective-permute-done | bytes 196640 | tf_op jit(solution)/shard_map/ppermute | solution.py:40
  99.7 1.2 %shard_map.78 = f32[2,3,256,256]{3,2,1,0:T(8,128)} custom-call(s32[24]{0:T(128)S(1)} %copy-done.12, f32[3,64,256]{2,1,0:T(8,128)S(1)} %collective-permute-done.5.rest, f32[2,3,256,256]{3,2,1,0:T(8,128)} %shard_map.77.before), custom_call_target="tpu_custom_call", output_to_operand_aliasing={{}: (2, {})} | custom-call | flops 1048576 | bytes 4194304 | tf_op jit(solution)/shard_map/pallas_call | solution.py:1044
  (41 shorter events, 3.6 us)
Async XLA Ops:
  2.7 16.4 %all-to-all-start = ((f32[16,8,384]{2,1,0:T(8,128)}), f32[16,8,384]{2,1,0:T(8,128)S(1)}, u32[]{:S(2)}, u32[]{:S(2)}) async-start(f32[16,8,384]{2,1,0:T(8,128)} %bitcast.14), calls=%async_computation | async-start | bytes 393216 | tf_op jit(solution)/shard_map/all_to_all | solution.py:869
  19.1 0.7 copy-start.15
  19.8 14.4 %collective-permute-start = (f32[5,72,256]{2,1,0:T(8,128)}, f32[5,72,256]{2,1,0:T(8,128)S(1)}, u32[]{:S(2)}, u32[]{:S(2)}) collective-permute-start(f32[5,72,256]{2,1,0:T(8,128)} %shard_map.67), channel_id=1, source_target_pairs={{0,2},{2,4},{4,6},{6,8},{8,10},{10,12},{12,14},{14,0},{1,3},{3,5},... | collective-permute-start | bytes 1105928 | tf_op jit(solution)/shard_map/ppermute | solution.py:40
  24.4 18.7 %collective-permute-start.1 = (f32[5,72,256]{2,1,0:T(8,128)}, f32[5,72,256]{2,1,0:T(8,128)S(1)}, u32[]{:S(2)}, u32[]{:S(2)}) collective-permute-start(f32[5,72,256]{2,1,0:T(8,128)} %shard_map.69), channel_id=1, source_target_pairs={{0,2},{2,4},{4,6},{6,8},{8,10},{10,12},{12,14},{14,0},{1,3},{3,5},... | collective-permute-start | bytes 1105928 | tf_op jit(solution)/shard_map/ppermute | solution.py:40
  25.0 18.1 %all-to-all-start.1 = ((f32[16,8,256]{2,1,0:T(8,128)}), f32[16,8,256]{2,1,0:T(8,128)S(1)}, u32[]{:S(2)}, u32[]{:S(2)}) async-start(f32[16,8,256]{2,1,0:T(8,128)} %bitcast.15), calls=%async_computation.1 | async-start | bytes 262144 | tf_op jit(solution)/shard_map/all_to_all | solution.py:869
  34.2 0.7 copy-start
  40.2 20.1 %collective-permute-start.2 = (f32[5,72,256]{2,1,0:T(8,128)}, f32[5,72,256]{2,1,0:T(8,128)S(1)}, u32[]{:S(2)}, u32[]{:S(2)}) collective-permute-start(f32[5,72,256]{2,1,0:T(8,128)} %get-tuple-element.45), channel_id=1, source_target_pairs={{0,2},{2,4},{4,6},{6,8},{8,10},{10,12},{12,14},{14,0},{1,3},{3,5},... | collective-permute-start | bytes 1105928 | tf_op jit(solution)/shard_map/ppermute | solution.py:40
  43.1 0.7 copy-start.16
  43.1 0.8 copy-start.2
  48.5 19.7 %collective-permute-start.3 = (f32[5,72,256]{2,1,0:T(8,128)}, f32[5,72,256]{2,1,0:T(8,128)S(1)}, u32[]{:S(2)}, u32[]{:S(2)}) collective-permute-start(f32[5,72,256]{2,1,0:T(8,128)} %get-tuple-element.46), channel_id=1, source_target_pairs={{0,2},{2,4},{4,6},{6,8},{8,10},{10,12},{12,14},{14,0},{1,3},{3,5},... | collective-permute-start | bytes 1105928 | tf_op jit(solution)/shard_map/ppermute | solution.py:40
  49.4 18.9 %all-to-all-start.2 = ((f32[16,8,256]{2,1,0:T(8,128)}), f32[16,8,256]{2,1,0:T(8,128)S(1)}, u32[]{:S(2)}, u32[]{:S(2)}) async-start(f32[16,8,256]{2,1,0:T(8,128)} %bitcast.16), calls=%async_computation.2 | async-start | bytes 262144 | tf_op jit(solution)/shard_map/all_to_all | solution.py:869
  60.3 0.7 copy-start.4
  68.2 0.7 copy-start.17
  68.2 0.8 copy-start.6
  69.0 9.8 %copy-start.5 = (f32[5,72,256]{2,1,0:T(8,128)S(1)}, f32[5,72,256]{2,1,0:T(8,128)}, u32[]{:S(2)}) copy-start(f32[5,72,256]{2,1,0:T(8,128)} %copy-done.4) | copy-start | bytes 1105924
  69.0 9.8 %copy-start.11 = (f32[8,256]{1,0:T(8,128)S(1)}, f32[8,256]{1,0:T(8,128)}, u32[]{:S(2)}) copy-start(f32[8,256]{1,0:T(8,128)} %get-tuple-element.40.first.second.delta0) | copy-start | bytes 24580
  69.0 9.8 %copy-start.12 = (s32[24]{0:T(128)S(1)}, s32[24]{0:T(128)}, u32[]{:S(2)}) copy-start(s32[24]{0:T(128)} %get-tuple-element.31.ctl) | copy-start | bytes 292
  69.0 9.8 %copy-start.13 = (f32[8,256]{1,0:T(8,128)S(1)}, f32[8,256]{1,0:T(8,128)}, u32[]{:S(2)}) copy-start(f32[8,256]{1,0:T(8,128)} %get-tuple-element.48.delta1) | copy-start | bytes 24580
  73.7 12.9 %collective-permute-start.6 = (f32[3,64,256]{2,1,0:T(8,128)}, f32[3,64,256]{2,1,0:T(8,128)S(1)}, u32[]{:S(2)}, u32[]{:S(2)}) collective-permute-start(f32[3,64,256]{2,1,0:T(8,128)} %get-tuple-element.54), channel_id=1, source_target_pairs={{0,2},{2,4},{4,6},{6,8},{8,10},{10,12},{12,14},{14,0},{1,3},{3,5},... | collective-permute-start | bytes 589832 | tf_op jit(solution)/shard_map/ppermute | solution.py:40
  75.4 12.9 %collective-permute-start.4 = (f32[3,64,256]{2,1,0:T(8,128)}, f32[3,64,256]{2,1,0:T(8,128)S(1)}, u32[]{:S(2)}, u32[]{:S(2)}) collective-permute-start(f32[3,64,256]{2,1,0:T(8,128)} %get-tuple-element.47), channel_id=1, source_target_pairs={{0,2},{2,4},{4,6},{6,8},{8,10},{10,12},{12,14},{14,0},{1,3},{3,5},... | collective-permute-start | bytes 589832 | tf_op jit(solution)/shard_map/ppermute | solution.py:40
  78.8 1.0 copy-start.7
  79.8 0.9 copy-start.9
  80.7 0.9 copy-start.10
  81.7 0.7 copy-start.14
  82.4 7.5 %copy-start.1 = (f32[5,72,256]{2,1,0:T(8,128)S(1)}, f32[5,72,256]{2,1,0:T(8,128)}, u32[]{:S(2)}) copy-start(f32[5,72,256]{2,1,0:T(8,128)} %copy-done) | copy-start | bytes 1105924
  82.4 7.5 %copy-start.3 = (f32[5,72,256]{2,1,0:T(8,128)S(1)}, f32[5,72,256]{2,1,0:T(8,128)}, u32[]{:S(2)}) copy-start(f32[5,72,256]{2,1,0:T(8,128)} %copy-done.2) | copy-start | bytes 1105924
  82.4 7.5 %copy-start.8 = (f32[3,256,256]{2,1,0:T(8,128)S(1)}, f32[3,256,256]{2,1,0:T(8,128)}, u32[]{:S(2)}) copy-start(f32[3,256,256]{2,1,0:T(8,128)} %get-tuple-element.56.staying) | copy-start | bytes 2359300
  87.1 10.0 %collective-permute-start.7 = (f32[3,64,256]{2,1,0:T(8,128)S(1)}, f32[3,64,256]{2,1,0:T(8,128)S(1)}, u32[]{:S(2)}, u32[]{:S(2)}) collective-permute-start(f32[3,64,256]{2,1,0:T(8,128)S(1)} %shard_map.75), channel_id=1, source_target_pairs={{0,2},{2,4},{4,6},{6,8},{8,10},{10,12},{12,14},{14,0},{1,3},{3,5},... | collective-permute-start | bytes 589832 | tf_op jit(solution)/shard_map/ppermute | solution.py:40
  88.9 10.9 %collective-permute-start.5 = (f32[3,64,256]{2,1,0:T(8,128)S(1)}, f32[3,64,256]{2,1,0:T(8,128)S(1)}, u32[]{:S(2)}, u32[]{:S(2)}) collective-permute-start(f32[3,64,256]{2,1,0:T(8,128)S(1)} %shard_map.74), channel_id=1, source_target_pairs={{0,2},{2,4},{4,6},{6,8},{8,10},{10,12},{12,14},{14,0},{1,3},{3,5},... | collective-permute-start | bytes 589832 | tf_op jit(solution)/shard_map/ppermute | solution.py:40

commit v30 on v29

--- a/solution.py
+++ b/solution.py
@@ -12,7 +12,7 @@
 ROOT_G = GRAVITY**0.5
 SPACING = 5.0
 COURANT = 0.2
-ROWS = 32
+ROWS = 64
 LANES = 128
 TILE = 256
 VMEM_BYTES = 60 * 1024 * 1024
@@ -20,7 +20,7 @@
 WET_FIRST, WET_SECOND = 16, 19
 CONTROLS = 24
 EARLY = 144
-PIECES = ((0, 72), (72, 144))
+PIECES = ((0, 80), (80, 144))
 AGAIN = 48
 LATE = TILE - EARLY + 16
 HALF = LATE // 2

time: 102 us -> 94.9 us (0.930)
  starting transfers between devices: 32.1 us -> 23.2 us
  waiting for transfers between devices: 16.1 us -> 21.8 us
  Pallas kernels: 45.3 us -> 41.5 us
    ppermute x8, waiting for transfers between devices: 7.59 us -> 13.4 us  [shifted(): return lax.ppermute(value, axis, pairs)]
    all_to_all x3, starting transfers between devices: 24.4 us -> 18.8 us  [spread(): lax.all_to_all(fast, ('xb', 'yb'), split_axis=0, concat_axis=0, tiled=True)]
    pallas_call x1, Pallas kernels: 4.95 us -> 1.52 us  [body(): call(repeat_first, shape, hbm(), [smem()] + [vmem()] * 3 + [anywhere()] *...]
    ppermute x8, starting transfers between devices: 7.73 us -> 4.41 us  [shifted(): return lax.ppermute(value, axis, pairs)]
  transfers between devices with their start and end apart: 11 -> 11, of which waited for: 7 -> 8; matrix products, arithmetic and copies ran while one was open for 0% -> 0% of each run, Pallas kernels for 36% -> 35%
where the time goes in v30:
time: 94.9 us; the launch traced here: 94.2 us
  Pallas kernels  41.5 us (44%)
  starting transfers between devices  23.2 us (24%)
  waiting for transfers between devices  21.8 us (23%)
  local copies, waits for them, and re-layouts  7.29 us (8%)
    all_to_all x3, starting transfers between devices, spread(): lax.all_to_all(fast, ('xb', 'yb'), split_axis=0, concat_axis=0, tiled=True)  18.8 us
    ppermute x8, waiting for transfers between devices, shifted(): return lax.ppermute(value, axis, pairs)  13.4 us
    pallas_call x2, Pallas kernels, body(): call(functools.partial(update_and_leaving if passing else update, step),...  9.05 us
    all_to_all x3, waiting for transfers between devices, spread(): lax.all_to_all(fast, ('xb', 'yb'), split_axis=0, concat_axis=0, tiled=True)  8.36 us
    unnamed x36, local copies, waits for them, and re-layouts  7.29 us
    pallas_call x1, Pallas kernels, body(): call(rates_and_splitting, (shape,) + piece_shapes, (hbm(),) * 3, [smem()]...  5.31 us
    pallas_call x1, Pallas kernels, body(): call(rates_and_leaving, (shape, piece_shapes[0]), (hbm(),) * 2, [smem()]...  5.27 us
    pallas_call x1, Pallas kernels, body(): call(rates_after, shape, hbm(), [smem()] + [hbm()] * 3, 16 << 20, scratch)  5.25 us
  transfers between devices with their start and end apart: 11, of which 8 were waited for; matrix products, arithmetic and copies ran while one was open for 0% of the time, Pallas kernels for 35%

profile of v30, /device:TPU:0, one launch (start us, length us, event | category | flops | bytes accessed | tf_op | source)
XLA Modules:
  0.0 94.2 jit_solution(12382231181986937799)
XLA Ops:
  0.0 2.7 %shard_map.64 = (f32[128,384]{1,0:T(8,128)}, f32[8,256]{1,0:T(8,128)}, s32[24]{0:T(128)}) custom-call(f32[2,3,256,256]{3,2,1,0:T(8,128)} %state_first.3, f32[2,256,256]{2,1,0:T(8,128)} %bed_in.9, s32[4,32]{1,0:T(4,128)} %bitcast.17, s32[3,32]{1,0:T(4,128)} %wet_in.1, s32[3,16]{1,0:T(4,128)} %moves_in.1), custom_call_target="tpu_custom_call" | custom-call | flops 4194304 | bytes 4194304 | tf_op jit(solution)/shard_map/pallas_call | solution.py:888
  2.7 7.4 %all-to-all-start = ((f32[16,8,384]{2,1,0:T(8,128)}), f32[16,8,384]{2,1,0:T(8,128)S(1)}, u32[]{:S(2)}, u32[]{:S(2)}) async-start(f32[16,8,384]{2,1,0:T(8,128)} %bitcast.14), calls=%async_computation | async-start | bytes 393216 | tf_op jit(solution)/shard_map/all_to_all | solution.py:869
  10.1 5.3 %shard_map.65 = (f32[2,3,256,256]{3,2,1,0:T(8,128)}, f32[5,80,256]{2,1,0:T(8,128)}, f32[5,64,256]{2,1,0:T(8,128)}) custom-call(s32[24]{0:T(128)} %get-tuple-element.31.ctl, f32[2,3,256,256]{3,2,1,0:T(8,128)} %state_first.3, f32[2,256,256]{2,1,0:T(8,128)} %bed_in.9, f32[2,256,256]{2,1,0:T(8,128)} %manning.1), custom_call_target="tpu_custom_call" | custom-call | flops 16777216 | bytes 4194304 | tf_op jit(solution)/shard_map/pallas_call | solution.py:932
  15.4 3.7 %all-to-all-done = f32[16,8,384]{2,1,0:T(8,128)S(1)} async-done(((f32[16,8,384]{2,1,0:T(8,128)}), f32[16,8,384]{2,1,0:T(8,128)S(1)}, u32[]{:S(2)}, u32[]{:S(2)}) %all-to-all-start) | async-done | bytes 196640 | tf_op jit(solution)/shard_map/all_to_all | solution.py:869
  19.1 0.7 copy-done.15
  19.8 4.5 %shard_map.66 = (f32[2,3,256,256]{3,2,1,0:T(8,128)}, f32[128,256]{1,0:T(8,128)}, f32[8,256]{1,0:T(8,128)}, f32[8,256]{1,0:T(8,128)}) custom-call(s32[24]{0:T(128)} %get-tuple-element.31.ctl, f32[128,384]{1,0:T(8,128)} %bitcast.8, f32[128,384]{1,0:T(8,128)} %bitcast.9, f32[8,256]{1,0:T(8,128)} %get-tuple-element.33.columns_in, ...), custom_call_target="tpu_custom_call" | custom-call | flops 8388608 | bytes 10485760 | tf_op jit(solution)/shard_map/pallas_call | solution.py:963
  24.9 6.1 %all-to-all-start.1 = ((f32[16,8,256]{2,1,0:T(8,128)}), f32[16,8,256]{2,1,0:T(8,128)S(1)}, u32[]{:S(2)}, u32[]{:S(2)}) async-start(f32[16,8,256]{2,1,0:T(8,128)} %bitcast.15), calls=%async_computation.1 | async-start | bytes 262144 | tf_op jit(solution)/shard_map/all_to_all | solution.py:869
  31.0 4.1 %collective-permute-done.arrived.low = f32[5,80,256]{2,1,0:T(8,128)S(1)} collective-permute-done((f32[5,80,256]{2,1,0:T(8,128)}, f32[5,80,256]{2,1,0:T(8,128)S(1)}, u32[]{:S(2)}, u32[]{:S(2)}) %collective-permute-start) | collective-permute-done | bytes 409632 | tf_op jit(solution)/shard_map/ppermute | solution.py:40
  35.1 0.8 copy-done.2
  35.9 5.3 %shard_map.68 = (f32[2,3,256,256]{3,2,1,0:T(8,128)}, f32[5,80,256]{2,1,0:T(8,128)}) custom-call(s32[24]{0:T(128)} %get-tuple-element.31.ctl, f32[2,3,256,256]{3,2,1,0:T(8,128)} %get-tuple-element.37.state_in, f32[2,256,256]{2,1,0:T(8,128)} %bed_in.9, f32[2,3,256,256]{3,2,1,0:T(8,128)} %state_first.3, f32[2,256,256]{2,1,0:T(8,128)} %manning.1, ...), custom_call_target="tpu_custom_call" | custom-call | flops 16777216 | bytes 4194304 | tf_op jit(solution)/shard_map/pallas_call | solution.py:918
  41.2 1.9 %all-to-all-done.1 = f32[16,8,256]{2,1,0:T(8,128)S(1)} async-done(((f32[16,8,256]{2,1,0:T(8,128)}), f32[16,8,256]{2,1,0:T(8,128)S(1)}, u32[]{:S(2)}, u32[]{:S(2)}) %all-to-all-start.1) | async-done | bytes 131104 | tf_op jit(solution)/shard_map/all_to_all | solution.py:869
  43.1 0.7 copy-done.16
  43.9 4.5 %shard_map.70 = (f32[2,3,256,256]{3,2,1,0:T(8,128)}, f32[128,256]{1,0:T(8,128)}, f32[8,256]{1,0:T(8,128)}, f32[8,256]{1,0:T(8,128)}, f32[5,64,256]{2,1,0:T(8,128)}) custom-call(s32[24]{0:T(128)} %get-tuple-element.31.ctl, f32[128,256]{1,0:T(8,128)} %bitcast.12, f32[128,384]{1,0:T(8,128)} %bitcast.10, f32[8,256]{1,0:T(8,128)} %get-tuple-element.36.columns_in, ...), custom_call_target="tpu_custom_call" | custom-call | flops 8388608 | bytes 10485760 | tf_op jit(solution)/shard_map/pallas_call | solution.py:963
  48.4 0.8 collective-permute-start.3
  49.3 5.3 %all-to-all-start.2 = ((f32[16,8,256]{2,1,0:T(8,128)}), f32[16,8,256]{2,1,0:T(8,128)S(1)}, u32[]{:S(2)}, u32[]{:S(2)}) async-start(f32[16,8,256]{2,1,0:T(8,128)} %bitcast.16), calls=%async_computation.2 | async-start | bytes 262144 | tf_op jit(solution)/shard_map/all_to_all | solution.py:869
  54.6 0.8 copy-done
  55.4 5.3 %shard_map.71.rate = f32[2,3,256,256]{3,2,1,0:T(8,128)} custom-call(s32[24]{0:T(128)} %get-tuple-element.31.ctl, f32[2,3,256,256]{3,2,1,0:T(8,128)} %get-tuple-element.44.state_in.state, f32[2,256,256]{2,1,0:T(8,128)} %bed_in.9, f32[5,80,256]{2,1,0:T(8,128)} %copy-done), custom_call_target="tpu_custom_call" | custom-call | flops 16777216 | bytes 4194304 | tf_op jit(solution)/shard_map/pallas_call | solution.py:928
  60.6 2.8 %all-to-all-done.2 = f32[16,8,256]{2,1,0:T(8,128)S(1)} async-done(((f32[16,8,256]{2,1,0:T(8,128)}), f32[16,8,256]{2,1,0:T(8,128)S(1)}, u32[]{:S(2)}, u32[]{:S(2)}) %all-to-all-start.2) | async-done | bytes 131104 | tf_op jit(solution)/shard_map/all_to_all | solution.py:869
  64.2 4.5 %shard_map.72 = (f32[3,256,256]{2,1,0:T(8,128)}, f32[3,64,256]{2,1,0:T(8,128)}, f32[3,64,256]{2,1,0:T(8,128)}, f32[3,64,256]{2,1,0:T(8,128)}, f32[3,64,256]{2,1,0:T(8,128)}, /*index=5*/f32[8,256]{1,0:T(8,128)}) custom-call(s32[24]{0:T(128)} %get-tuple-element.31.ctl, f32[128,256]{1,0:T(8,128)} %bitcast.13, f32[128,384]{1,0:T(8,128)} %bitcast.11, ...), custom_call_target="tpu_custom_call" | custom-call | flops 8388608 | bytes 10485760 | tf_op jit(solution)/shard_map/pallas_call | solution.py:982
  68.7 0.9 collective-permute-start.6
  69.6 1.6 %collective-permute-start.4 = (f32[3,64,256]{2,1,0:T(8,128)}, f32[3,64,256]{2,1,0:T(8,128)S(1)}, u32[]{:S(2)}, u32[]{:S(2)}) collective-permute-start(f32[3,64,256]{2,1,0:T(8,128)} %get-tuple-element.47), channel_id=1, source_target_pairs={{0,2},{2,4},{4,6},{6,8},{8,10},{10,12},{12,14},{14,0},{1,3},{3,5},... | collective-permute-start | bytes 589832 | tf_op jit(solution)/shard_map/ppermute | solution.py:40
  71.3 1.0 %copy-done.7 = f32[5,64,256]{2,1,0:T(8,128)S(1)} copy-done((f32[5,64,256]{2,1,0:T(8,128)S(1)}, f32[5,64,256]{2,1,0:T(8,128)}, u32[]{:S(2)}) %copy-start.7) | copy-done | bytes 327704
  72.2 0.9 copy-done.9
  73.2 0.9 copy-done.10
  74.1 0.7 copy-done.14
  74.8 4.2 %shard_map.73 = (f32[3,144,256]{2,1,0:T(8,128)S(1)}, f32[3,64,256]{2,1,0:T(8,128)S(1)}, f32[3,64,256]{2,1,0:T(8,128)S(1)}) custom-call(s32[24]{0:T(128)S(1)} %copy-done.12, f32[8,256]{1,0:T(8,128)S(1)} %copy-done.11, f32[8,256]{1,0:T(8,128)S(1)} %copy-done.13, f32[8,256]{1,0:T(8,128)S(1)} %copy-done.14, f32[5,80,256]{2,1,0:T(8,128)S(1)} %copy-done.1, ...), custom_call_target="tpu_custom_call" | custom-call | flops 8388608 | bytes 4194304 | tf_op jit(solution)/shard_map/pallas_call | solution.py:995
  80.3 2.6 %collective-permute-done.4.arrived.rest_in = f32[3,64,256]{2,1,0:T(8,128)S(1)} collective-permute-done((f32[3,64,256]{2,1,0:T(8,128)}, f32[3,64,256]{2,1,0:T(8,128)S(1)}, u32[]{:S(2)}, u32[]{:S(2)}) %collective-permute-start.4) | collective-permute-done | bytes 196640 | tf_op jit(solution)/shard_map/ppermute | solution.py:40
  83.5 1.5 %shard_map.76.before = f32[2,3,256,256]{3,2,1,0:T(8,128)} custom-call(s32[24]{0:T(128)S(1)} %copy-done.12, f32[8,256]{1,0:T(8,128)S(1)} %copy-done.11, f32[8,256]{1,0:T(8,128)S(1)} %copy-done.13, f32[8,256]{1,0:T(8,128)S(1)} %copy-done.14, f32[5,80,256]{2,1,0:T(8,128)S(1)} %copy-done.3, f32[5,64,256]{2,1,0:T(8,128)S(1)} %copy-done.5, ...), custom_call_target="tpu_custom_call" | custom-call | flops 8388608 | bytes 4194304 | tf_op jit(solution)/shard_map/pallas_call | solution.py:1018
  85.1 3.9 %collective-permute-done.7.late = f32[3,64,256]{2,1,0:T(8,128)S(1)} collective-permute-done((f32[3,64,256]{2,1,0:T(8,128)S(1)}, f32[3,64,256]{2,1,0:T(8,128)S(1)}, u32[]{:S(2)}, u32[]{:S(2)}) %collective-permute-start.7) | collective-permute-done | bytes 196640 | tf_op jit(solution)/shard_map/ppermute | solution.py:40
  89.0 1.5 %shard_map.77.before = f32[2,3,256,256]{3,2,1,0:T(8,128)} custom-call(s32[24]{0:T(128)S(1)} %copy-done.12, f32[3,64,256]{2,1,0:T(8,128)S(1)} %collective-permute-done.7.late, f32[3,144,256]{2,1,0:T(8,128)S(1)} %get-tuple-element.53.order.early, f32[2,3,256,256]{3,2,1,0:T(8,128)} %shard_map.76.before), custom_call_target="tpu_custom_call", output_to_operand_aliasing={{}: (3, {})} | custom-call | flops 1048576 | bytes 4194304 | tf_op jit(solution)/shard_map/pallas_call | solution.py:1034
  90.4 2.4 %collective-permute-done.5.rest = f32[3,64,256]{2,1,0:T(8,128)S(1)} collective-permute-done((f32[3,64,256]{2,1,0:T(8,128)S(1)}, f32[3,64,256]{2,1,0:T(8,128)S(1)}, u32[]{:S(2)}, u32[]{:S(2)}) %collective-permute-start.5) | collective-permute-done | bytes 196640 | tf_op jit(solution)/shard_map/ppermute | solution.py:40
  92.8 1.2 %shard_map.78 = f32[2,3,256,256]{3,2,1,0:T(8,128)} custom-call(s32[24]{0:T(128)S(1)} %copy-done.12, f32[3,64,256]{2,1,0:T(8,128)S(1)} %collective-permute-done.5.rest, f32[2,3,256,256]{3,2,1,0:T(8,128)} %shard_map.77.before), custom_call_target="tpu_custom_call", output_to_operand_aliasing={{}: (2, {})} | custom-call | flops 1048576 | bytes 4194304 | tf_op jit(solution)/shard_map/pallas_call | solution.py:1044
  (41 shorter events, 3.6 us)
Async XLA Ops:
  2.7 16.4 %all-to-all-start = ((f32[16,8,384]{2,1,0:T(8,128)}), f32[16,8,384]{2,1,0:T(8,128)S(1)}, u32[]{:S(2)}, u32[]{:S(2)}) async-start(f32[16,8,384]{2,1,0:T(8,128)} %bitcast.14), calls=%async_computation | async-start | bytes 393216 | tf_op jit(solution)/shard_map/all_to_all | solution.py:869
  19.1 0.7 copy-start.15
  19.8 15.4 %collective-permute-start = (f32[5,80,256]{2,1,0:T(8,128)}, f32[5,80,256]{2,1,0:T(8,128)S(1)}, u32[]{:S(2)}, u32[]{:S(2)}) collective-permute-start(f32[5,80,256]{2,1,0:T(8,128)} %shard_map.67), channel_id=1, source_target_pairs={{0,2},{2,4},{4,6},{6,8},{8,10},{10,12},{12,14},{14,0},{1,3},{3,5},... | collective-permute-start | bytes 1228808 | tf_op jit(solution)/shard_map/ppermute | solution.py:40
  24.3 18.8 %collective-permute-start.1 = (f32[5,64,256]{2,1,0:T(8,128)}, f32[5,64,256]{2,1,0:T(8,128)S(1)}, u32[]{:S(2)}, u32[]{:S(2)}) collective-permute-start(f32[5,64,256]{2,1,0:T(8,128)} %shard_map.69), channel_id=1, source_target_pairs={{0,2},{2,4},{4,6},{6,8},{8,10},{10,12},{12,14},{14,0},{1,3},{3,5},... | collective-permute-start | bytes 983048 | tf_op jit(solution)/shard_map/ppermute | solution.py:40
  24.9 18.2 %all-to-all-start.1 = ((f32[16,8,256]{2,1,0:T(8,128)}), f32[16,8,256]{2,1,0:T(8,128)S(1)}, u32[]{:S(2)}, u32[]{:S(2)}) async-start(f32[16,8,256]{2,1,0:T(8,128)} %bitcast.15), calls=%async_computation.1 | async-start | bytes 262144 | tf_op jit(solution)/shard_map/all_to_all | solution.py:869
  35.1 0.8 copy-start.2
  41.2 13.4 %collective-permute-start.2 = (f32[5,80,256]{2,1,0:T(8,128)}, f32[5,80,256]{2,1,0:T(8,128)S(1)}, u32[]{:S(2)}, u32[]{:S(2)}) collective-permute-start(f32[5,80,256]{2,1,0:T(8,128)} %get-tuple-element.45), channel_id=1, source_target_pairs={{0,2},{2,4},{4,6},{6,8},{8,10},{10,12},{12,14},{14,0},{1,3},{3,5},... | collective-permute-start | bytes 1228808 | tf_op jit(solution)/shard_map/ppermute | solution.py:40
  43.1 0.7 copy-start.16
  43.1 0.8 copy-start.4
  48.4 15.0 %collective-permute-start.3 = (f32[5,64,256]{2,1,0:T(8,128)}, f32[5,64,256]{2,1,0:T(8,128)S(1)}, u32[]{:S(2)}, u32[]{:S(2)}) collective-permute-start(f32[5,64,256]{2,1,0:T(8,128)} %get-tuple-element.46), channel_id=1, source_target_pairs={{0,2},{2,4},{4,6},{6,8},{8,10},{10,12},{12,14},{14,0},{1,3},{3,5},... | collective-permute-start | bytes 983048 | tf_op jit(solution)/shard_map/ppermute | solution.py:40
  49.3 14.2 %all-to-all-start.2 = ((f32[16,8,256]{2,1,0:T(8,128)}), f32[16,8,256]{2,1,0:T(8,128)S(1)}, u32[]{:S(2)}, u32[]{:S(2)}) async-start(f32[16,8,256]{2,1,0:T(8,128)} %bitcast.16), calls=%async_computation.2 | async-start | bytes 262144 | tf_op jit(solution)/shard_map/all_to_all | solution.py:869
  54.6 0.8 copy-start
  63.4 0.7 copy-start.17
  63.5 0.8 copy-start.6
  64.2 7.0 %copy-start.1 = (f32[5,80,256]{2,1,0:T(8,128)S(1)}, f32[5,80,256]{2,1,0:T(8,128)}, u32[]{:S(2)}) copy-start(f32[5,80,256]{2,1,0:T(8,128)} %copy-done) | copy-start | bytes 1228804
  64.2 7.0 %copy-start.11 = (f32[8,256]{1,0:T(8,128)S(1)}, f32[8,256]{1,0:T(8,128)}, u32[]{:S(2)}) copy-start(f32[8,256]{1,0:T(8,128)} %get-tuple-element.40.first.second.delta0) | copy-start | bytes 24580
  64.2 7.0 %copy-start.12 = (s32[24]{0:T(128)S(1)}, s32[24]{0:T(128)}, u32[]{:S(2)}) copy-start(s32[24]{0:T(128)} %get-tuple-element.31.ctl) | copy-start | bytes 292
  64.2 7.0 %copy-start.13 = (f32[8,256]{1,0:T(8,128)S(1)}, f32[8,256]{1,0:T(8,128)}, u32[]{:S(2)}) copy-start(f32[8,256]{1,0:T(8,128)} %get-tuple-element.48.delta1) | copy-start | bytes 24580
  68.7 10.7 %collective-permute-start.6 = (f32[3,64,256]{2,1,0:T(8,128)}, f32[3,64,256]{2,1,0:T(8,128)S(1)}, u32[]{:S(2)}, u32[]{:S(2)}) collective-permute-start(f32[3,64,256]{2,1,0:T(8,128)} %get-tuple-element.54), channel_id=1, source_target_pairs={{0,2},{2,4},{4,6},{6,8},{8,10},{10,12},{12,14},{14,0},{1,3},{3,5},... | collective-permute-start | bytes 589832 | tf_op jit(solution)/shard_map/ppermute | solution.py:40
  69.6 13.3 %collective-permute-start.4 = (f32[3,64,256]{2,1,0:T(8,128)}, f32[3,64,256]{2,1,0:T(8,128)S(1)}, u32[]{:S(2)}, u32[]{:S(2)}) collective-permute-start(f32[3,64,256]{2,1,0:T(8,128)} %get-tuple-element.47), channel_id=1, source_target_pairs={{0,2},{2,4},{4,6},{6,8},{8,10},{10,12},{12,14},{14,0},{1,3},{3,5},... | collective-permute-start | bytes 589832 | tf_op jit(solution)/shard_map/ppermute | solution.py:40
  71.2 1.0 %copy-start.7 = (f32[5,64,256]{2,1,0:T(8,128)S(1)}, f32[5,64,256]{2,1,0:T(8,128)}, u32[]{:S(2)}) copy-start(f32[5,64,256]{2,1,0:T(8,128)} %copy-done.6) | copy-start | bytes 983044
  72.2 0.9 copy-start.9
  73.1 0.9 copy-start.10
  74.1 0.7 copy-start.14
  74.8 8.7 %copy-start.3 = (f32[5,80,256]{2,1,0:T(8,128)S(1)}, f32[5,80,256]{2,1,0:T(8,128)}, u32[]{:S(2)}) copy-start(f32[5,80,256]{2,1,0:T(8,128)} %copy-done.2) | copy-start | bytes 1228804
  74.8 8.8 %copy-start.5 = (f32[5,64,256]{2,1,0:T(8,128)S(1)}, f32[5,64,256]{2,1,0:T(8,128)}, u32[]{:S(2)}) copy-start(f32[5,64,256]{2,1,0:T(8,128)} %copy-done.4) | copy-start | bytes 983044
  74.8 8.8 %copy-start.8 = (f32[3,256,256]{2,1,0:T(8,128)S(1)}, f32[3,256,256]{2,1,0:T(8,128)}, u32[]{:S(2)}) copy-start(f32[3,256,256]{2,1,0:T(8,128)} %get-tuple-element.56.staying) | copy-start | bytes 2359300
  80.0 9.0 %collective-permute-start.7 = (f32[3,64,256]{2,1,0:T(8,128)S(1)}, f32[3,64,256]{2,1,0:T(8,128)S(1)}, u32[]{:S(2)}, u32[]{:S(2)}) collective-permute-start(f32[3,64,256]{2,1,0:T(8,128)S(1)} %shard_map.75), channel_id=1, source_target_pairs={{0,2},{2,4},{4,6},{6,8},{8,10},{10,12},{12,14},{14,0},{1,3},{3,5},... | collective-permute-start | bytes 589832 | tf_op jit(solution)/shard_map/ppermute | solution.py:40
  83.4 9.4 %collective-permute-start.5 = (f32[3,64,256]{2,1,0:T(8,128)S(1)}, f32[3,64,256]{2,1,0:T(8,128)S(1)}, u32[]{:S(2)}, u32[]{:S(2)}) collective-permute-start(f32[3,64,256]{2,1,0:T(8,128)S(1)} %shard_map.74), channel_id=1, source_target_pairs={{0,2},{2,4},{4,6},{6,8},{8,10},{10,12},{12,14},{14,0},{1,3},{3,5},... | collective-permute-start | bytes 589832 | tf_op jit(solution)/shard_map/ppermute | solution.py:40

commit v31 on v30

--- a/solution.py
+++ b/solution.py
@@ -19,9 +19,9 @@
 SLOT_LOW, WALL_WEST, WALL_EAST, WALL_OUTER, WET, MOVE = 0, 1, 3, 5, 7, 13
 WET_FIRST, WET_SECOND = 16, 19
 CONTROLS = 24
-EARLY = 144
-PIECES = ((0, 80), (80, 144))
-AGAIN = 48
+EARLY = 128
+PIECES = ((0, 64), (64, 128))
+AGAIN = 64
 LATE = TILE - EARLY + 16
 HALF = LATE // 2
 CHUNKS = 8

time: 94.9 us -> 94.3 us (level)
  no operation moved by 1% of the time
where the time goes in v31:
time: 94.3 us; the launch traced here: 93.6 us
  Pallas kernels  41.2 us (44%)
  starting transfers between devices  22.9 us (24%)
  waiting for transfers between devices  21.9 us (23%)
  local copies, waits for them, and re-layouts  7.23 us (8%)
    all_to_all x3, starting transfers between devices, spread(): lax.all_to_all(fast, ('xb', 'yb'), split_axis=0, concat_axis=0, tiled=True)  18.8 us
    ppermute x8, waiting for transfers between devices, shifted(): return lax.ppermute(value, axis, pairs)  13.4 us
    pallas_call x2, Pallas kernels, body(): call(functools.partial(update_and_leaving if passing else update, step),...  9.06 us
    all_to_all x3, waiting for transfers between devices, spread(): lax.all_to_all(fast, ('xb', 'yb'), split_axis=0, concat_axis=0, tiled=True)  8.5 us
    unnamed x36, local copies, waits for them, and re-layouts  7.23 us
    pallas_call x1, Pallas kernels, body(): call(rates_and_splitting, (shape,) + piece_shapes, (hbm(),) * 3, [smem()]...  5.31 us
    pallas_call x1, Pallas kernels, body(): call(rates_and_leaving, (shape, piece_shapes[0]), (hbm(),) * 2, [smem()]...  5.27 us
    pallas_call x1, Pallas kernels, body(): call(rates_after, shape, hbm(), [smem()] + [hbm()] * 3, 16 << 20, scratch)  5.25 us
  transfers between devices with their start and end apart: 11, of which 8 were waited for; matrix products, arithmetic and copies ran while one was open for 0% of the time, Pallas kernels for 35%

profile of v31, /device:TPU:0, one launch (start us, length us, event | category | flops | bytes accessed | tf_op | source)
XLA Modules:
  0.0 93.6 jit_solution(14414297834791584635)
XLA Ops:
  0.0 2.7 %shard_map.64 = (f32[128,384]{1,0:T(8,128)}, f32[8,256]{1,0:T(8,128)}, s32[24]{0:T(128)}) custom-call(f32[2,3,256,256]{3,2,1,0:T(8,128)} %state_first.3, f32[2,256,256]{2,1,0:T(8,128)} %bed_in.9, s32[4,32]{1,0:T(4,128)} %bitcast.17, s32[3,32]{1,0:T(4,128)} %wet_in.1, s32[3,16]{1,0:T(4,128)} %moves_in.1), custom_call_target="tpu_custom_call" | custom-call | flops 4194304 | bytes 4194304 | tf_op jit(solution)/shard_map/pallas_call | solution.py:888
  2.7 7.4 %all-to-all-start = ((f32[16,8,384]{2,1,0:T(8,128)}), f32[16,8,384]{2,1,0:T(8,128)S(1)}, u32[]{:S(2)}, u32[]{:S(2)}) async-start(f32[16,8,384]{2,1,0:T(8,128)} %bitcast.14), calls=%async_computation | async-start | bytes 393216 | tf_op jit(solution)/shard_map/all_to_all | solution.py:869
  10.1 5.3 %shard_map.65 = (f32[2,3,256,256]{3,2,1,0:T(8,128)}, f32[5,64,256]{2,1,0:T(8,128)}, f32[5,64,256]{2,1,0:T(8,128)}) custom-call(s32[24]{0:T(128)} %get-tuple-element.31.ctl, f32[2,3,256,256]{3,2,1,0:T(8,128)} %state_first.3, f32[2,256,256]{2,1,0:T(8,128)} %bed_in.9, f32[2,256,256]{2,1,0:T(8,128)} %manning.1), custom_call_target="tpu_custom_call" | custom-call | flops 16777216 | bytes 4194304 | tf_op jit(solution)/shard_map/pallas_call | solution.py:932
  15.4 3.7 %all-to-all-done = f32[16,8,384]{2,1,0:T(8,128)S(1)} async-done(((f32[16,8,384]{2,1,0:T(8,128)}), f32[16,8,384]{2,1,0:T(8,128)S(1)}, u32[]{:S(2)}, u32[]{:S(2)}) %all-to-all-start) | async-done | bytes 196640 | tf_op jit(solution)/shard_map/all_to_all | solution.py:869
  19.1 0.7 copy-done.15
  19.7 4.5 %shard_map.66 = (f32[2,3,256,256]{3,2,1,0:T(8,128)}, f32[128,256]{1,0:T(8,128)}, f32[8,256]{1,0:T(8,128)}, f32[8,256]{1,0:T(8,128)}) custom-call(s32[24]{0:T(128)} %get-tuple-element.31.ctl, f32[128,384]{1,0:T(8,128)} %bitcast.8, f32[128,384]{1,0:T(8,128)} %bitcast.9, f32[8,256]{1,0:T(8,128)} %get-tuple-element.33.columns_in, ...), custom_call_target="tpu_custom_call" | custom-call | flops 8388608 | bytes 10485760 | tf_op jit(solution)/shard_map/pallas_call | solution.py:963
  24.9 6.1 %all-to-all-start.1 = ((f32[16,8,256]{2,1,0:T(8,128)}), f32[16,8,256]{2,1,0:T(8,128)S(1)}, u32[]{:S(2)}, u32[]{:S(2)}) async-start(f32[16,8,256]{2,1,0:T(8,128)} %bitcast.15), calls=%async_computation.1 | async-start | bytes 262144 | tf_op jit(solution)/shard_map/all_to_all | solution.py:869
  31.0 2.2 %collective-permute-done.arrived.low = f32[5,64,256]{2,1,0:T(8,128)S(1)} collective-permute-done((f32[5,64,256]{2,1,0:T(8,128)}, f32[5,64,256]{2,1,0:T(8,128)S(1)}, u32[]{:S(2)}, u32[]{:S(2)}) %collective-permute-start) | collective-permute-done | bytes 327712 | tf_op jit(solution)/shard_map/ppermute | solution.py:40
  33.3 0.7 copy-done
  34.0 5.3 %shard_map.68 = (f32[2,3,256,256]{3,2,1,0:T(8,128)}, f32[5,64,256]{2,1,0:T(8,128)}) custom-call(s32[24]{0:T(128)} %get-tuple-element.31.ctl, f32[2,3,256,256]{3,2,1,0:T(8,128)} %get-tuple-element.37.state_in, f32[2,256,256]{2,1,0:T(8,128)} %bed_in.9, f32[2,3,256,256]{3,2,1,0:T(8,128)} %state_first.3, f32[2,256,256]{2,1,0:T(8,128)} %manning.1, ...), custom_call_target="tpu_custom_call" | custom-call | flops 16777216 | bytes 4194304 | tf_op jit(solution)/shard_map/pallas_call | solution.py:918
  39.4 2.0 %all-to-all-done.1 = f32[16,8,256]{2,1,0:T(8,128)S(1)} async-done(((f32[16,8,256]{2,1,0:T(8,128)}), f32[16,8,256]{2,1,0:T(8,128)S(1)}, u32[]{:S(2)}, u32[]{:S(2)}) %all-to-all-start.1) | async-done | bytes 131104 | tf_op jit(solution)/shard_map/all_to_all | solution.py:869
  42.1 4.5 %shard_map.70 = (f32[2,3,256,256]{3,2,1,0:T(8,128)}, f32[128,256]{1,0:T(8,128)}, f32[8,256]{1,0:T(8,128)}, f32[8,256]{1,0:T(8,128)}, f32[5,64,256]{2,1,0:T(8,128)}) custom-call(s32[24]{0:T(128)} %get-tuple-element.31.ctl, f32[128,256]{1,0:T(8,128)} %bitcast.12, f32[128,384]{1,0:T(8,128)} %bitcast.10, f32[8,256]{1,0:T(8,128)} %get-tuple-element.36.columns_in, ...), custom_call_target="tpu_custom_call" | custom-call | flops 8388608 | bytes 10485760 | tf_op jit(solution)/shard_map/pallas_call | solution.py:963
  46.7 0.8 collective-permute-start.3
  47.5 5.3 %all-to-all-start.2 = ((f32[16,8,256]{2,1,0:T(8,128)}), f32[16,8,256]{2,1,0:T(8,128)S(1)}, u32[]{:S(2)}, u32[]{:S(2)}) async-start(f32[16,8,256]{2,1,0:T(8,128)} %bitcast.16), calls=%async_computation.2 | async-start | bytes 262144 | tf_op jit(solution)/shard_map/all_to_all | solution.py:869
  52.8 0.7 copy-done.4
  53.6 5.3 %shard_map.71.rate = f32[2,3,256,256]{3,2,1,0:T(8,128)} custom-call(s32[24]{0:T(128)} %get-tuple-element.31.ctl, f32[2,3,256,256]{3,2,1,0:T(8,128)} %get-tuple-element.44.state_in.state, f32[2,256,256]{2,1,0:T(8,128)} %bed_in.9, f32[5,64,256]{2,1,0:T(8,128)} %copy-done.4), custom_call_target="tpu_custom_call" | custom-call | flops 16777216 | bytes 4194304 | tf_op jit(solution)/shard_map/pallas_call | solution.py:928
  58.8 2.8 %all-to-all-done.2 = f32[16,8,256]{2,1,0:T(8,128)S(1)} async-done(((f32[16,8,256]{2,1,0:T(8,128)}), f32[16,8,256]{2,1,0:T(8,128)S(1)}, u32[]{:S(2)}, u32[]{:S(2)}) %all-to-all-start.2) | async-done | bytes 131104 | tf_op jit(solution)/shard_map/all_to_all | solution.py:869
  62.4 4.5 %shard_map.72 = (f32[3,256,256]{2,1,0:T(8,128)}, f32[3,72,256]{2,1,0:T(8,128)}, f32[3,72,256]{2,1,0:T(8,128)}, f32[3,72,256]{2,1,0:T(8,128)}, f32[3,72,256]{2,1,0:T(8,128)}, /*index=5*/f32[8,256]{1,0:T(8,128)}) custom-call(s32[24]{0:T(128)} %get-tuple-element.31.ctl, f32[128,256]{1,0:T(8,128)} %bitcast.13, f32[128,384]{1,0:T(8,128)} %bitcast.11, ...), custom_call_target="tpu_custom_call" | custom-call | flops 8388608 | bytes 10485760 | tf_op jit(solution)/shard_map/pallas_call | solution.py:982
  67.0 0.8 collective-permute-start.6
  67.7 1.7 %collective-permute-start.4 = (f32[3,72,256]{2,1,0:T(8,128)}, f32[3,72,256]{2,1,0:T(8,128)S(1)}, u32[]{:S(2)}, u32[]{:S(2)}) collective-permute-start(f32[3,72,256]{2,1,0:T(8,128)} %get-tuple-element.47), channel_id=1, source_target_pairs={{0,2},{2,4},{4,6},{6,8},{8,10},{10,12},{12,14},{14,0},{1,3},{3,5},... | collective-permute-start | bytes 663560 | tf_op jit(solution)/shard_map/ppermute | solution.py:40
  69.4 1.0 %copy-done.7 = f32[5,64,256]{2,1,0:T(8,128)S(1)} copy-done((f32[5,64,256]{2,1,0:T(8,128)S(1)}, f32[5,64,256]{2,1,0:T(8,128)}, u32[]{:S(2)}) %copy-start.7) | copy-done | bytes 327704
  70.4 0.9 copy-done.9
  71.3 0.9 copy-done.10
  72.3 0.7 copy-done.14
  73.0 3.8 %shard_map.73 = (f32[3,128,256]{2,1,0:T(8,128)S(1)}, f32[3,72,256]{2,1,0:T(8,128)S(1)}, f32[3,72,256]{2,1,0:T(8,128)S(1)}) custom-call(s32[24]{0:T(128)S(1)} %copy-done.12, f32[8,256]{1,0:T(8,128)S(1)} %copy-done.11, f32[8,256]{1,0:T(8,128)S(1)} %copy-done.13, f32[8,256]{1,0:T(8,128)S(1)} %copy-done.14, f32[5,64,256]{2,1,0:T(8,128)S(1)} %copy-done.5, ...), custom_call_target="tpu_custom_call" | custom-call | flops 8388608 | bytes 4194304 | tf_op jit(solution)/shard_map/pallas_call | solution.py:995
  76.8 1.4 %collective-permute-done.6.arrived.late_in = f32[3,72,256]{2,1,0:T(8,128)S(1)} collective-permute-done((f32[3,72,256]{2,1,0:T(8,128)}, f32[3,72,256]{2,1,0:T(8,128)S(1)}, u32[]{:S(2)}, u32[]{:S(2)}) %collective-permute-start.6) | collective-permute-done | bytes 221216 | tf_op jit(solution)/shard_map/ppermute | solution.py:40
  78.8 3.3 %collective-permute-done.4.arrived.rest_in = f32[3,72,256]{2,1,0:T(8,128)S(1)} collective-permute-done((f32[3,72,256]{2,1,0:T(8,128)}, f32[3,72,256]{2,1,0:T(8,128)S(1)}, u32[]{:S(2)}, u32[]{:S(2)}) %collective-permute-start.4) | collective-permute-done | bytes 221216 | tf_op jit(solution)/shard_map/ppermute | solution.py:40
  82.8 1.5 %shard_map.76.before = f32[2,3,256,256]{3,2,1,0:T(8,128)} custom-call(s32[24]{0:T(128)S(1)} %copy-done.12, f32[8,256]{1,0:T(8,128)S(1)} %copy-done.11, f32[8,256]{1,0:T(8,128)S(1)} %copy-done.13, f32[8,256]{1,0:T(8,128)S(1)} %copy-done.14, f32[5,64,256]{2,1,0:T(8,128)S(1)} %copy-done.1, f32[5,64,256]{2,1,0:T(8,128)S(1)} %copy-done.3, ...), custom_call_target="tpu_custom_call" | custom-call | flops 8388608 | bytes 4194304 | tf_op jit(solution)/shard_map/pallas_call | solution.py:1018
  84.3 3.2 %collective-permute-done.7.late = f32[3,72,256]{2,1,0:T(8,128)S(1)} collective-permute-done((f32[3,72,256]{2,1,0:T(8,128)S(1)}, f32[3,72,256]{2,1,0:T(8,128)S(1)}, u32[]{:S(2)}, u32[]{:S(2)}) %collective-permute-start.7) | collective-permute-done | bytes 221216 | tf_op jit(solution)/shard_map/ppermute | solution.py:40
  87.5 1.4 %shard_map.77.before = f32[2,3,256,256]{3,2,1,0:T(8,128)} custom-call(s32[24]{0:T(128)S(1)} %copy-done.12, f32[3,72,256]{2,1,0:T(8,128)S(1)} %collective-permute-done.7.late, f32[3,128,256]{2,1,0:T(8,128)S(1)} %get-tuple-element.53.order.early, f32[2,3,256,256]{3,2,1,0:T(8,128)} %shard_map.76.before), custom_call_target="tpu_custom_call", output_to_operand_aliasing={{}: (3, {})} | custom-call | flops 1048576 | bytes 4194304 | tf_op jit(solution)/shard_map/pallas_call | solution.py:1034
  89.0 3.2 %collective-permute-done.5.rest = f32[3,72,256]{2,1,0:T(8,128)S(1)} collective-permute-done((f32[3,72,256]{2,1,0:T(8,128)S(1)}, f32[3,72,256]{2,1,0:T(8,128)S(1)}, u32[]{:S(2)}, u32[]{:S(2)}) %collective-permute-start.5) | collective-permute-done | bytes 221216 | tf_op jit(solution)/shard_map/ppermute | solution.py:40
  92.2 1.2 %shard_map.78 = f32[2,3,256,256]{3,2,1,0:T(8,128)} custom-call(s32[24]{0:T(128)S(1)} %copy-done.12, f32[3,72,256]{2,1,0:T(8,128)S(1)} %collective-permute-done.5.rest, f32[2,3,256,256]{3,2,1,0:T(8,128)} %shard_map.77.before), custom_call_target="tpu_custom_call", output_to_operand_aliasing={{}: (2, {})} | custom-call | flops 1048576 | bytes 4194304 | tf_op jit(solution)/shard_map/pallas_call | solution.py:1044
  (41 shorter events, 3.5 us)
Async XLA Ops:
  2.7 16.4 %all-to-all-start = ((f32[16,8,384]{2,1,0:T(8,128)}), f32[16,8,384]{2,1,0:T(8,128)S(1)}, u32[]{:S(2)}, u32[]{:S(2)}) async-start(f32[16,8,384]{2,1,0:T(8,128)} %bitcast.14), calls=%async_computation | async-start | bytes 393216 | tf_op jit(solution)/shard_map/all_to_all | solution.py:869
  19.1 0.7 copy-start.15
  19.7 13.5 %collective-permute-start = (f32[5,64,256]{2,1,0:T(8,128)}, f32[5,64,256]{2,1,0:T(8,128)S(1)}, u32[]{:S(2)}, u32[]{:S(2)}) collective-permute-start(f32[5,64,256]{2,1,0:T(8,128)} %shard_map.67), channel_id=1, source_target_pairs={{0,2},{2,4},{4,6},{6,8},{8,10},{10,12},{12,14},{14,0},{1,3},{3,5},... | collective-permute-start | bytes 983048 | tf_op jit(solution)/shard_map/ppermute | solution.py:40
  24.3 17.1 %collective-permute-start.1 = (f32[5,64,256]{2,1,0:T(8,128)}, f32[5,64,256]{2,1,0:T(8,128)S(1)}, u32[]{:S(2)}, u32[]{:S(2)}) collective-permute-start(f32[5,64,256]{2,1,0:T(8,128)} %shard_map.69), channel_id=1, source_target_pairs={{0,2},{2,4},{4,6},{6,8},{8,10},{10,12},{12,14},{14,0},{1,3},{3,5},... | collective-permute-start | bytes 983048 | tf_op jit(solution)/shard_map/ppermute | solution.py:40
  24.9 16.4 %all-to-all-start.1 = ((f32[16,8,256]{2,1,0:T(8,128)}), f32[16,8,256]{2,1,0:T(8,128)S(1)}, u32[]{:S(2)}, u32[]{:S(2)}) async-start(f32[16,8,256]{2,1,0:T(8,128)} %bitcast.15), calls=%async_computation.1 | async-start | bytes 262144 | tf_op jit(solution)/shard_map/all_to_all | solution.py:869
  33.3 0.7 copy-start
  39.3 13.5 %collective-permute-start.2 = (f32[5,64,256]{2,1,0:T(8,128)}, f32[5,64,256]{2,1,0:T(8,128)S(1)}, u32[]{:S(2)}, u32[]{:S(2)}) collective-permute-start(f32[5,64,256]{2,1,0:T(8,128)} %get-tuple-element.45), channel_id=1, source_target_pairs={{0,2},{2,4},{4,6},{6,8},{8,10},{10,12},{12,14},{14,0},{1,3},{3,5},... | collective-permute-start | bytes 983048 | tf_op jit(solution)/shard_map/ppermute | solution.py:40
  41.3 0.7 copy-start.16
  41.3 0.8 copy-start.2
  46.7 15.0 %collective-permute-start.3 = (f32[5,64,256]{2,1,0:T(8,128)}, f32[5,64,256]{2,1,0:T(8,128)S(1)}, u32[]{:S(2)}, u32[]{:S(2)}) collective-permute-start(f32[5,64,256]{2,1,0:T(8,128)} %get-tuple-element.46), channel_id=1, source_target_pairs={{0,2},{2,4},{4,6},{6,8},{8,10},{10,12},{12,14},{14,0},{1,3},{3,5},... | collective-permute-start | bytes 983048 | tf_op jit(solution)/shard_map/ppermute | solution.py:40
  47.5 14.2 %all-to-all-start.2 = ((f32[16,8,256]{2,1,0:T(8,128)}), f32[16,8,256]{2,1,0:T(8,128)S(1)}, u32[]{:S(2)}, u32[]{:S(2)}) async-start(f32[16,8,256]{2,1,0:T(8,128)} %bitcast.16), calls=%async_computation.2 | async-start | bytes 262144 | tf_op jit(solution)/shard_map/all_to_all | solution.py:869
  52.8 0.7 copy-start.4
  61.7 0.6 copy-start.17
  61.7 0.8 copy-start.6
  62.4 7.0 %copy-start.5 = (f32[5,64,256]{2,1,0:T(8,128)S(1)}, f32[5,64,256]{2,1,0:T(8,128)}, u32[]{:S(2)}) copy-start(f32[5,64,256]{2,1,0:T(8,128)} %copy-done.4) | copy-start | bytes 983044
  62.4 7.0 %copy-start.11 = (f32[8,256]{1,0:T(8,128)S(1)}, f32[8,256]{1,0:T(8,128)}, u32[]{:S(2)}) copy-start(f32[8,256]{1,0:T(8,128)} %get-tuple-element.40.first.second.delta0) | copy-start | bytes 24580
  62.4 7.0 %copy-start.12 = (s32[24]{0:T(128)S(1)}, s32[24]{0:T(128)}, u32[]{:S(2)}) copy-start(s32[24]{0:T(128)} %get-tuple-element.31.ctl) | copy-start | bytes 292
  62.4 7.0 %copy-start.13 = (f32[8,256]{1,0:T(8,128)S(1)}, f32[8,256]{1,0:T(8,128)}, u32[]{:S(2)}) copy-start(f32[8,256]{1,0:T(8,128)} %get-tuple-element.48.delta1) | copy-start | bytes 24580
  67.0 11.2 %collective-permute-start.6 = (f32[3,72,256]{2,1,0:T(8,128)}, f32[3,72,256]{2,1,0:T(8,128)S(1)}, u32[]{:S(2)}, u32[]{:S(2)}) collective-permute-start(f32[3,72,256]{2,1,0:T(8,128)} %get-tuple-element.54), channel_id=1, source_target_pairs={{0,2},{2,4},{4,6},{6,8},{8,10},{10,12},{12,14},{14,0},{1,3},{3,5},... | collective-permute-start | bytes 663560 | tf_op jit(solution)/shard_map/ppermute | solution.py:40
  67.7 14.4 %collective-permute-start.4 = (f32[3,72,256]{2,1,0:T(8,128)}, f32[3,72,256]{2,1,0:T(8,128)S(1)}, u32[]{:S(2)}, u32[]{:S(2)}) collective-permute-start(f32[3,72,256]{2,1,0:T(8,128)} %get-tuple-element.47), channel_id=1, source_target_pairs={{0,2},{2,4},{4,6},{6,8},{8,10},{10,12},{12,14},{14,0},{1,3},{3,5},... | collective-permute-start | bytes 663560 | tf_op jit(solution)/shard_map/ppermute | solution.py:40
  69.4 1.0 %copy-start.7 = (f32[5,64,256]{2,1,0:T(8,128)S(1)}, f32[5,64,256]{2,1,0:T(8,128)}, u32[]{:S(2)}) copy-start(f32[5,64,256]{2,1,0:T(8,128)} %copy-done.6) | copy-start | bytes 983044
  70.4 0.9 copy-start.9
  71.3 0.9 copy-start.10
  72.3 0.7 copy-start.14
  73.0 9.8 %copy-start.1 = (f32[5,64,256]{2,1,0:T(8,128)S(1)}, f32[5,64,256]{2,1,0:T(8,128)}, u32[]{:S(2)}) copy-start(f32[5,64,256]{2,1,0:T(8,128)} %copy-done) | copy-start | bytes 983044
  73.0 9.8 %copy-start.3 = (f32[5,64,256]{2,1,0:T(8,128)S(1)}, f32[5,64,256]{2,1,0:T(8,128)}, u32[]{:S(2)}) copy-start(f32[5,64,256]{2,1,0:T(8,128)} %copy-done.2) | copy-start | bytes 983044
  73.0 9.8 %copy-start.8 = (f32[3,256,256]{2,1,0:T(8,128)S(1)}, f32[3,256,256]{2,1,0:T(8,128)}, u32[]{:S(2)}) copy-start(f32[3,256,256]{2,1,0:T(8,128)} %get-tuple-element.56.staying) | copy-start | bytes 2359300
  78.8 8.8 %collective-permute-start.7 = (f32[3,72,256]{2,1,0:T(8,128)S(1)}, f32[3,72,256]{2,1,0:T(8,128)S(1)}, u32[]{:S(2)}, u32[]{:S(2)}) collective-permute-start(f32[3,72,256]{2,1,0:T(8,128)S(1)} %shard_map.75), channel_id=1, source_target_pairs={{0,2},{2,4},{4,6},{6,8},{8,10},{10,12},{12,14},{14,0},{1,3},{3,5},... | collective-permute-start | bytes 663560 | tf_op jit(solution)/shard_map/ppermute | solution.py:40
  82.7 9.5 %collective-permute-start.5 = (f32[3,72,256]{2,1,0:T(8,128)S(1)}, f32[3,72,256]{2,1,0:T(8,128)S(1)}, u32[]{:S(2)}, u32[]{:S(2)}) collective-permute-start(f32[3,72,256]{2,1,0:T(8,128)S(1)} %shard_map.74), channel_id=1, source_target_pairs={{0,2},{2,4},{4,6},{6,8},{8,10},{10,12},{12,14},{14,0},{1,3},{3,5},... | collective-permute-start | bytes 663560 | tf_op jit(solution)/shard_map/ppermute | solution.py:40

commit v32 on v31

--- a/solution.py
+++ b/solution.py
@@ -938,8 +938,14 @@
                 scratch + [buffer(early_shape), pltpu.SemaphoreType.DMA((5,))],
             )(ctl, state, bed, manning)
             held = call(
-                hold, piece_shapes[0], hbm(), [hbm()] * 3, 1 << 10, aliases={2: 0}
-            )(rate, got, leaving[0])
+                hold,
+                piece_shapes[0],
+                hbm(),
+                [anywhere(), anywhere(), hbm()],
+                1 << 10,
+                aliases={2: 0},
+                room=1 << 20,
+            )(got, got, leaving[0])
             early_first = [shifted(held, "xb", 1)]
         more = step + 1 < STEPS
         shapes = (f32(8 * devices, TILE), f32(8, TILE)) if more else (half_shape,) * 4

time: 94.3 us -> 95.3 us (1.011)
  local copies, waits for them, and re-layouts: 7.23 us -> 8.34 us
    unnamed x36 -> x42, local copies, waits for them, and re-layouts: 7.23 us -> 8.34 us
where the time goes in v32:
time: 95.3 us; the launch traced here: 94.7 us
  Pallas kernels  41.2 us (43%)
  starting transfers between devices  22.8 us (24%)
  waiting for transfers between devices  21.9 us (23%)
  local copies, waits for them, and re-layouts  8.34 us (9%)
    all_to_all x3, starting transfers between devices, spread(): lax.all_to_all(fast, ('xb', 'yb'), split_axis=0, concat_axis=0, tiled=True)  18.8 us
    ppermute x8, waiting for transfers between devices, shifted(): return lax.ppermute(value, axis, pairs)  13.4 us
    pallas_call x2, Pallas kernels, body(): call(functools.partial(update_and_leaving if passing else update, step),...  9.08 us
    all_to_all x3, waiting for transfers between devices, spread(): lax.all_to_all(fast, ('xb', 'yb'), split_axis=0, concat_axis=0, tiled=True)  8.49 us
    unnamed x42, local copies, waits for them, and re-layouts  8.34 us
    pallas_call x1, Pallas kernels, body(): call(rates_and_splitting, (shape,) + piece_shapes, (hbm(),) * 3, [smem()]...  5.31 us
    pallas_call x1, Pallas kernels, body(): call(rates_and_leaving, (shape, piece_shapes[0]), (hbm(),) * 2, [smem()]...  5.27 us
    pallas_call x1, Pallas kernels, body(): call(rates_after, shape, hbm(), [smem()] + [hbm()] * 3, 16 << 20, scratch)  5.25 us
  transfers between devices with their start and end apart: 11, of which 8 were waited for; matrix products, arithmetic and copies ran while one was open for 0% of the time, Pallas kernels for 35%

profile of v32, /device:TPU:0, one launch (start us, length us, event | category | flops | bytes accessed | tf_op | source)
XLA Modules:
  0.0 94.7 jit_solution(9864230218221182811)
XLA Ops:
  0.0 2.7 %shard_map.64 = (f32[128,384]{1,0:T(8,128)}, f32[8,256]{1,0:T(8,128)}, s32[24]{0:T(128)}) custom-call(f32[2,3,256,256]{3,2,1,0:T(8,128)} %state_first.3, f32[2,256,256]{2,1,0:T(8,128)} %bed_in.9, s32[4,32]{1,0:T(4,128)} %bitcast.18, s32[3,32]{1,0:T(4,128)} %wet_in.1, s32[3,16]{1,0:T(4,128)} %moves_in.1), custom_call_target="tpu_custom_call" | custom-call | flops 4194304 | bytes 4194304 | tf_op jit(solution)/shard_map/pallas_call | solution.py:888
  2.7 7.4 %all-to-all-start = ((f32[16,8,384]{2,1,0:T(8,128)}), f32[16,8,384]{2,1,0:T(8,128)S(1)}, u32[]{:S(2)}, u32[]{:S(2)}) async-start(f32[16,8,384]{2,1,0:T(8,128)} %bitcast.15), calls=%async_computation | async-start | bytes 393216 | tf_op jit(solution)/shard_map/all_to_all | solution.py:869
  10.1 5.3 %shard_map.65 = (f32[2,3,256,256]{3,2,1,0:T(8,128)}, f32[5,64,256]{2,1,0:T(8,128)}, f32[5,64,256]{2,1,0:T(8,128)}) custom-call(s32[24]{0:T(128)} %get-tuple-element.31.ctl, f32[2,3,256,256]{3,2,1,0:T(8,128)} %state_first.3, f32[2,256,256]{2,1,0:T(8,128)} %bed_in.9, f32[2,256,256]{2,1,0:T(8,128)} %manning.1), custom_call_target="tpu_custom_call" | custom-call | flops 16777216 | bytes 4194304 | tf_op jit(solution)/shard_map/pallas_call | solution.py:932
  15.4 3.7 %all-to-all-done = f32[16,8,384]{2,1,0:T(8,128)S(1)} async-done(((f32[16,8,384]{2,1,0:T(8,128)}), f32[16,8,384]{2,1,0:T(8,128)S(1)}, u32[]{:S(2)}, u32[]{:S(2)}) %all-to-all-start) | async-done | bytes 196640 | tf_op jit(solution)/shard_map/all_to_all | solution.py:869
  19.1 1.0 %copy-done.10 = f32[5,64,256]{2,1,0:T(8,128)S(1)} copy-done((f32[5,64,256]{2,1,0:T(8,128)S(1)}, f32[5,64,256]{2,1,0:T(8,128)}, u32[]{:S(2)}) %copy-start.10) | copy-done | bytes 327704
  20.1 0.7 copy-done.11
  20.9 4.5 %shard_map.66 = (f32[2,3,256,256]{3,2,1,0:T(8,128)}, f32[128,256]{1,0:T(8,128)}, f32[8,256]{1,0:T(8,128)}, f32[8,256]{1,0:T(8,128)}) custom-call(s32[24]{0:T(128)} %get-tuple-element.31.ctl, f32[128,384]{1,0:T(8,128)} %bitcast.9, f32[128,384]{1,0:T(8,128)} %bitcast.10, f32[8,256]{1,0:T(8,128)} %get-tuple-element.33.columns_in, ...), custom_call_target="tpu_custom_call" | custom-call | flops 8388608 | bytes 10485760 | tf_op jit(solution)/shard_map/pallas_call | solution.py:969
  26.0 6.1 %all-to-all-start.1 = ((f32[16,8,256]{2,1,0:T(8,128)}), f32[16,8,256]{2,1,0:T(8,128)S(1)}, u32[]{:S(2)}, u32[]{:S(2)}) async-start(f32[16,8,256]{2,1,0:T(8,128)} %bitcast.16), calls=%async_computation.1 | async-start | bytes 262144 | tf_op jit(solution)/shard_map/all_to_all | solution.py:869
  32.1 2.2 %collective-permute-done.arrived.low = f32[5,64,256]{2,1,0:T(8,128)S(1)} collective-permute-done((f32[5,64,256]{2,1,0:T(8,128)}, f32[5,64,256]{2,1,0:T(8,128)S(1)}, u32[]{:S(2)}, u32[]{:S(2)}) %collective-permute-start) | collective-permute-done | bytes 327712 | tf_op jit(solution)/shard_map/ppermute | solution.py:40
  34.4 0.7 copy-done.1
  35.1 5.3 %shard_map.68 = (f32[2,3,256,256]{3,2,1,0:T(8,128)}, f32[5,64,256]{2,1,0:T(8,128)}) custom-call(s32[24]{0:T(128)} %get-tuple-element.31.ctl, f32[2,3,256,256]{3,2,1,0:T(8,128)} %get-tuple-element.37.state_in, f32[2,256,256]{2,1,0:T(8,128)} %bed_in.9, f32[2,3,256,256]{3,2,1,0:T(8,128)} %state_first.3, f32[2,256,256]{2,1,0:T(8,128)} %manning.1, ...), custom_call_target="tpu_custom_call" | custom-call | flops 16777216 | bytes 4194304 | tf_op jit(solution)/shard_map/pallas_call | solution.py:918
  40.5 2.0 %all-to-all-done.1 = f32[16,8,256]{2,1,0:T(8,128)S(1)} async-done(((f32[16,8,256]{2,1,0:T(8,128)}), f32[16,8,256]{2,1,0:T(8,128)S(1)}, u32[]{:S(2)}, u32[]{:S(2)}) %all-to-all-start.1) | async-done | bytes 131104 | tf_op jit(solution)/shard_map/all_to_all | solution.py:869
  43.2 4.5 %shard_map.70 = (f32[2,3,256,256]{3,2,1,0:T(8,128)}, f32[128,256]{1,0:T(8,128)}, f32[8,256]{1,0:T(8,128)}, f32[8,256]{1,0:T(8,128)}, f32[5,64,256]{2,1,0:T(8,128)}) custom-call(s32[24]{0:T(128)} %get-tuple-element.31.ctl, f32[128,256]{1,0:T(8,128)} %bitcast.13, f32[128,384]{1,0:T(8,128)} %bitcast.11, f32[8,256]{1,0:T(8,128)} %get-tuple-element.36.columns_in, ...), custom_call_target="tpu_custom_call" | custom-call | flops 8388608 | bytes 10485760 | tf_op jit(solution)/shard_map/pallas_call | solution.py:969
  47.8 0.8 collective-permute-start.3
  48.6 5.3 %all-to-all-start.2 = ((f32[16,8,256]{2,1,0:T(8,128)}), f32[16,8,256]{2,1,0:T(8,128)S(1)}, u32[]{:S(2)}, u32[]{:S(2)}) async-start(f32[16,8,256]{2,1,0:T(8,128)} %bitcast.17), calls=%async_computation.2 | async-start | bytes 262144 | tf_op jit(solution)/shard_map/all_to_all | solution.py:869
  54.0 0.7 copy-done.5
  54.7 5.3 %shard_map.71.rate = f32[2,3,256,256]{3,2,1,0:T(8,128)} custom-call(s32[24]{0:T(128)} %get-tuple-element.31.ctl, f32[2,3,256,256]{3,2,1,0:T(8,128)} %get-tuple-element.44.state_in.state, f32[2,256,256]{2,1,0:T(8,128)} %bed_in.9, f32[5,64,256]{2,1,0:T(8,128)} %copy-done.5), custom_call_target="tpu_custom_call" | custom-call | flops 16777216 | bytes 4194304 | tf_op jit(solution)/shard_map/pallas_call | solution.py:928
  60.0 2.8 %all-to-all-done.2 = f32[16,8,256]{2,1,0:T(8,128)S(1)} async-done(((f32[16,8,256]{2,1,0:T(8,128)}), f32[16,8,256]{2,1,0:T(8,128)S(1)}, u32[]{:S(2)}, u32[]{:S(2)}) %all-to-all-start.2) | async-done | bytes 131104 | tf_op jit(solution)/shard_map/all_to_all | solution.py:869
  63.5 4.5 %shard_map.72 = (f32[3,256,256]{2,1,0:T(8,128)}, f32[3,72,256]{2,1,0:T(8,128)}, f32[3,72,256]{2,1,0:T(8,128)}, f32[3,72,256]{2,1,0:T(8,128)}, f32[3,72,256]{2,1,0:T(8,128)}, /*index=5*/f32[8,256]{1,0:T(8,128)}) custom-call(s32[24]{0:T(128)} %get-tuple-element.31.ctl, f32[128,256]{1,0:T(8,128)} %bitcast.14, f32[128,384]{1,0:T(8,128)} %bitcast.12, ...), custom_call_target="tpu_custom_call" | custom-call | flops 8388608 | bytes 10485760 | tf_op jit(solution)/shard_map/pallas_call | solution.py:988
  68.0 0.8 collective-permute-start.6
  68.8 1.6 %collective-permute-start.4 = (f32[3,72,256]{2,1,0:T(8,128)}, f32[3,72,256]{2,1,0:T(8,128)S(1)}, u32[]{:S(2)}, u32[]{:S(2)}) collective-permute-start(f32[3,72,256]{2,1,0:T(8,128)} %get-tuple-element.47), channel_id=1, source_target_pairs={{0,2},{2,4},{4,6},{6,8},{8,10},{10,12},{12,14},{14,0},{1,3},{3,5},... | collective-permute-start | bytes 663560 | tf_op jit(solution)/shard_map/ppermute | solution.py:40
  70.5 1.0 %copy-done.8 = f32[5,64,256]{2,1,0:T(8,128)S(1)} copy-done((f32[5,64,256]{2,1,0:T(8,128)S(1)}, f32[5,64,256]{2,1,0:T(8,128)}, u32[]{:S(2)}) %copy-start.8) | copy-done | bytes 327704
  71.4 0.9 copy-done.12
  72.4 0.9 copy-done.13
  74.0 3.8 %shard_map.73 = (f32[3,128,256]{2,1,0:T(8,128)S(1)}, f32[3,72,256]{2,1,0:T(8,128)S(1)}, f32[3,72,256]{2,1,0:T(8,128)S(1)}) custom-call(s32[24]{0:T(128)S(1)} %copy-done.15, f32[8,256]{1,0:T(8,128)S(1)} %copy-done.14, f32[8,256]{1,0:T(8,128)S(1)} %copy-done.16, f32[8,256]{1,0:T(8,128)S(1)} %copy-done.17, f32[5,64,256]{2,1,0:T(8,128)S(1)} %copy-done.6, ...), custom_call_target="tpu_custom_call" | custom-call | flops 8388608 | bytes 4194304 | tf_op jit(solution)/shard_map/pallas_call | solution.py:1001
  77.8 1.5 %collective-permute-done.6.arrived.late_in = f32[3,72,256]{2,1,0:T(8,128)S(1)} collective-permute-done((f32[3,72,256]{2,1,0:T(8,128)}, f32[3,72,256]{2,1,0:T(8,128)S(1)}, u32[]{:S(2)}, u32[]{:S(2)}) %collective-permute-start.6) | collective-permute-done | bytes 221216 | tf_op jit(solution)/shard_map/ppermute | solution.py:40
  79.9 3.2 %collective-permute-done.4.arrived.rest_in = f32[3,72,256]{2,1,0:T(8,128)S(1)} collective-permute-done((f32[3,72,256]{2,1,0:T(8,128)}, f32[3,72,256]{2,1,0:T(8,128)S(1)}, u32[]{:S(2)}, u32[]{:S(2)}) %collective-permute-start.4) | collective-permute-done | bytes 221216 | tf_op jit(solution)/shard_map/ppermute | solution.py:40
  83.8 1.5 %shard_map.76.before = f32[2,3,256,256]{3,2,1,0:T(8,128)} custom-call(s32[24]{0:T(128)S(1)} %copy-done.15, f32[8,256]{1,0:T(8,128)S(1)} %copy-done.14, f32[8,256]{1,0:T(8,128)S(1)} %copy-done.16, f32[8,256]{1,0:T(8,128)S(1)} %copy-done.18, f32[5,64,256]{2,1,0:T(8,128)S(1)} %copy-done.2, f32[5,64,256]{2,1,0:T(8,128)S(1)} %copy-done.4, ...), custom_call_target="tpu_custom_call" | custom-call | flops 8388608 | bytes 4194304 | tf_op jit(solution)/shard_map/pallas_call | solution.py:1024
  85.3 3.5 %collective-permute-done.7.late = f32[3,72,256]{2,1,0:T(8,128)S(1)} collective-permute-done((f32[3,72,256]{2,1,0:T(8,128)S(1)}, f32[3,72,256]{2,1,0:T(8,128)S(1)}, u32[]{:S(2)}, u32[]{:S(2)}) %collective-permute-start.7) | collective-permute-done | bytes 221216 | tf_op jit(solution)/shard_map/ppermute | solution.py:40
  88.8 1.4 %shard_map.77.before = f32[2,3,256,256]{3,2,1,0:T(8,128)} custom-call(s32[24]{0:T(128)S(1)} %copy-done.15, f32[3,72,256]{2,1,0:T(8,128)S(1)} %collective-permute-done.7.late, f32[3,128,256]{2,1,0:T(8,128)S(1)} %get-tuple-element.53.order.early, f32[2,3,256,256]{3,2,1,0:T(8,128)} %shard_map.76.before), custom_call_target="tpu_custom_call", output_to_operand_aliasing={{}: (3, {})} | custom-call | flops 1048576 | bytes 4194304 | tf_op jit(solution)/shard_map/pallas_call | solution.py:1040
  90.3 3.0 %collective-permute-done.5.rest = f32[3,72,256]{2,1,0:T(8,128)S(1)} collective-permute-done((f32[3,72,256]{2,1,0:T(8,128)S(1)}, f32[3,72,256]{2,1,0:T(8,128)S(1)}, u32[]{:S(2)}, u32[]{:S(2)}) %collective-permute-start.5) | collective-permute-done | bytes 221216 | tf_op jit(solution)/shard_map/ppermute | solution.py:40
  93.3 1.2 %shard_map.78 = f32[2,3,256,256]{3,2,1,0:T(8,128)} custom-call(s32[24]{0:T(128)S(1)} %copy-done.15, f32[3,72,256]{2,1,0:T(8,128)S(1)} %collective-permute-done.5.rest, f32[2,3,256,256]{3,2,1,0:T(8,128)} %shard_map.77.before), custom_call_target="tpu_custom_call", output_to_operand_aliasing={{}: (2, {})} | custom-call | flops 1048576 | bytes 4194304 | tf_op jit(solution)/shard_map/pallas_call | solution.py:1050
  (47 shorter events, 4.2 us)
Async XLA Ops:
  2.7 16.4 %all-to-all-start = ((f32[16,8,384]{2,1,0:T(8,128)}), f32[16,8,384]{2,1,0:T(8,128)S(1)}, u32[]{:S(2)}, u32[]{:S(2)}) async-start(f32[16,8,384]{2,1,0:T(8,128)} %bitcast.15), calls=%async_computation | async-start | bytes 393216 | tf_op jit(solution)/shard_map/all_to_all | solution.py:869
  19.1 1.8 %copy-start = (f32[16,8,384]{2,1,0:T(8,128)}, f32[16,8,384]{2,1,0:T(8,128)S(1)}, u32[]{:S(2)}) copy-start(f32[16,8,384]{2,1,0:T(8,128)S(1)} %all-to-all-done) | copy-start | bytes 589828
  19.1 1.0 %copy-start.10 = (f32[5,64,256]{2,1,0:T(8,128)S(1)}, f32[5,64,256]{2,1,0:T(8,128)}, u32[]{:S(2)}) copy-start(f32[5,64,256]{2,1,0:T(8,128)} %get-tuple-element.38.leaving) | copy-start | bytes 983044
  20.1 0.7 copy-start.11
  20.9 13.5 %collective-permute-start = (f32[5,64,256]{2,1,0:T(8,128)}, f32[5,64,256]{2,1,0:T(8,128)S(1)}, u32[]{:S(2)}, u32[]{:S(2)}) collective-permute-start(f32[5,64,256]{2,1,0:T(8,128)} %copy-done.11), channel_id=1, source_target_pairs={{0,2},{2,4},{4,6},{6,8},{8,10},{10,12},{12,14},{14,0},{1,3},{3,5},... | collective-permute-start | bytes 983048 | tf_op jit(solution)/shard_map/ppermute | solution.py:40
  25.4 17.0 %collective-permute-start.1 = (f32[5,64,256]{2,1,0:T(8,128)}, f32[5,64,256]{2,1,0:T(8,128)S(1)}, u32[]{:S(2)}, u32[]{:S(2)}) collective-permute-start(f32[5,64,256]{2,1,0:T(8,128)} %shard_map.69), channel_id=1, source_target_pairs={{0,2},{2,4},{4,6},{6,8},{8,10},{10,12},{12,14},{14,0},{1,3},{3,5},... | collective-permute-start | bytes 983048 | tf_op jit(solution)/shard_map/ppermute | solution.py:40
  26.0 16.4 %all-to-all-start.1 = ((f32[16,8,256]{2,1,0:T(8,128)}), f32[16,8,256]{2,1,0:T(8,128)S(1)}, u32[]{:S(2)}, u32[]{:S(2)}) async-start(f32[16,8,256]{2,1,0:T(8,128)} %bitcast.16), calls=%async_computation.1 | async-start | bytes 262144 | tf_op jit(solution)/shard_map/all_to_all | solution.py:869
  34.4 0.7 copy-start.1
  40.4 13.5 %collective-permute-start.2 = (f32[5,64,256]{2,1,0:T(8,128)}, f32[5,64,256]{2,1,0:T(8,128)S(1)}, u32[]{:S(2)}, u32[]{:S(2)}) collective-permute-start(f32[5,64,256]{2,1,0:T(8,128)} %get-tuple-element.45), channel_id=1, source_target_pairs={{0,2},{2,4},{4,6},{6,8},{8,10},{10,12},{12,14},{14,0},{1,3},{3,5},... | collective-permute-start | bytes 983048 | tf_op jit(solution)/shard_map/ppermute | solution.py:40
  42.5 0.6 copy-start.19
  42.5 0.8 copy-start.3
  47.8 15.0 %collective-permute-start.3 = (f32[5,64,256]{2,1,0:T(8,128)}, f32[5,64,256]{2,1,0:T(8,128)S(1)}, u32[]{:S(2)}, u32[]{:S(2)}) collective-permute-start(f32[5,64,256]{2,1,0:T(8,128)} %get-tuple-element.46), channel_id=1, source_target_pairs={{0,2},{2,4},{4,6},{6,8},{8,10},{10,12},{12,14},{14,0},{1,3},{3,5},... | collective-permute-start | bytes 983048 | tf_op jit(solution)/shard_map/ppermute | solution.py:40
  48.6 14.2 %all-to-all-start.2 = ((f32[16,8,256]{2,1,0:T(8,128)}), f32[16,8,256]{2,1,0:T(8,128)S(1)}, u32[]{:S(2)}, u32[]{:S(2)}) async-start(f32[16,8,256]{2,1,0:T(8,128)} %bitcast.17), calls=%async_computation.2 | async-start | bytes 262144 | tf_op jit(solution)/shard_map/all_to_all | solution.py:869
  53.9 0.7 copy-start.5
  62.8 0.6 copy-start.20
  62.8 0.8 copy-start.7
  63.5 6.9 %copy-start.6 = (f32[5,64,256]{2,1,0:T(8,128)S(1)}, f32[5,64,256]{2,1,0:T(8,128)}, u32[]{:S(2)}) copy-start(f32[5,64,256]{2,1,0:T(8,128)} %copy-done.5) | copy-start | bytes 983044
  63.5 6.9 %copy-start.14 = (f32[8,256]{1,0:T(8,128)S(1)}, f32[8,256]{1,0:T(8,128)}, u32[]{:S(2)}) copy-start(f32[8,256]{1,0:T(8,128)} %get-tuple-element.40.first.second.delta0) | copy-start | bytes 24580
  63.5 6.9 %copy-start.15 = (s32[24]{0:T(128)S(1)}, s32[24]{0:T(128)}, u32[]{:S(2)}) copy-start(s32[24]{0:T(128)} %get-tuple-element.31.ctl) | copy-start | bytes 292
  63.5 6.9 %copy-start.16 = (f32[8,256]{1,0:T(8,128)S(1)}, f32[8,256]{1,0:T(8,128)}, u32[]{:S(2)}) copy-start(f32[8,256]{1,0:T(8,128)} %get-tuple-element.48.delta1) | copy-start | bytes 24580
  68.0 11.2 %collective-permute-start.6 = (f32[3,72,256]{2,1,0:T(8,128)}, f32[3,72,256]{2,1,0:T(8,128)S(1)}, u32[]{:S(2)}, u32[]{:S(2)}) collective-permute-start(f32[3,72,256]{2,1,0:T(8,128)} %get-tuple-element.54), channel_id=1, source_target_pairs={{0,2},{2,4},{4,6},{6,8},{8,10},{10,12},{12,14},{14,0},{1,3},{3,5},... | collective-permute-start | bytes 663560 | tf_op jit(solution)/shard_map/ppermute | solution.py:40
  68.8 14.3 %collective-permute-start.4 = (f32[3,72,256]{2,1,0:T(8,128)}, f32[3,72,256]{2,1,0:T(8,128)S(1)}, u32[]{:S(2)}, u32[]{:S(2)}) collective-permute-start(f32[3,72,256]{2,1,0:T(8,128)} %get-tuple-element.47), channel_id=1, source_target_pairs={{0,2},{2,4},{4,6},{6,8},{8,10},{10,12},{12,14},{14,0},{1,3},{3,5},... | collective-permute-start | bytes 663560 | tf_op jit(solution)/shard_map/ppermute | solution.py:40
  70.5 1.0 %copy-start.8 = (f32[5,64,256]{2,1,0:T(8,128)S(1)}, f32[5,64,256]{2,1,0:T(8,128)}, u32[]{:S(2)}) copy-start(f32[5,64,256]{2,1,0:T(8,128)} %copy-done.7) | copy-start | bytes 983044
  71.4 0.9 copy-start.12
  72.4 0.9 copy-start.13
  73.3 0.7 copy-start.17
  74.0 9.8 %copy-start.2 = (f32[5,64,256]{2,1,0:T(8,128)S(1)}, f32[5,64,256]{2,1,0:T(8,128)}, u32[]{:S(2)}) copy-start(f32[5,64,256]{2,1,0:T(8,128)} %copy-done.1) | copy-start | bytes 983044
  74.0 9.8 %copy-start.4 = (f32[5,64,256]{2,1,0:T(8,128)S(1)}, f32[5,64,256]{2,1,0:T(8,128)}, u32[]{:S(2)}) copy-start(f32[5,64,256]{2,1,0:T(8,128)} %copy-done.3) | copy-start | bytes 983044
  74.0 9.8 %copy-start.9 = (f32[3,256,256]{2,1,0:T(8,128)S(1)}, f32[3,256,256]{2,1,0:T(8,128)}, u32[]{:S(2)}) copy-start(f32[3,256,256]{2,1,0:T(8,128)} %get-tuple-element.56.staying) | copy-start | bytes 2359300
  74.0 9.8 %copy-start.18 = (f32[8,256]{1,0:T(8,128)S(1)}, f32[8,256]{1,0:T(8,128)}, u32[]{:S(2)}) copy-start(f32[8,256]{1,0:T(8,128)} %get-tuple-element.49.delta2) | copy-start | bytes 24580
  79.9 8.9 %collective-permute-start.7 = (f32[3,72,256]{2,1,0:T(8,128)S(1)}, f32[3,72,256]{2,1,0:T(8,128)S(1)}, u32[]{:S(2)}, u32[]{:S(2)}) collective-permute-start(f32[3,72,256]{2,1,0:T(8,128)S(1)} %shard_map.75), channel_id=1, source_target_pairs={{0,2},{2,4},{4,6},{6,8},{8,10},{10,12},{12,14},{14,0},{1,3},{3,5},... | collective-permute-start | bytes 663560 | tf_op jit(solution)/shard_map/ppermute | solution.py:40
  83.7 9.6 %collective-permute-start.5 = (f32[3,72,256]{2,1,0:T(8,128)S(1)}, f32[3,72,256]{2,1,0:T(8,128)S(1)}, u32[]{:S(2)}, u32[]{:S(2)}) collective-permute-start(f32[3,72,256]{2,1,0:T(8,128)S(1)} %shard_map.74), channel_id=1, source_target_pairs={{0,2},{2,4},{4,6},{6,8},{8,10},{10,12},{12,14},{14,0},{1,3},{3,5},... | collective-permute-start | bytes 663560 | tf_op jit(solution)/shard_map/ppermute | solution.py:40

commit v33 on v31

--- a/solution.py
+++ b/solution.py
@@ -12,7 +12,7 @@
 ROOT_G = GRAVITY**0.5
 SPACING = 5.0
 COURANT = 0.2
-ROWS = 64
+ROWS = 128
 LANES = 128
 TILE = 256
 VMEM_BYTES = 60 * 1024 * 1024

time: 94.3 us -> 94.3 us (level)
  no operation moved by 1% of the time
where the time goes in v33:
time: 94.3 us; the launch traced here: 93.7 us
  Pallas kernels  41.3 us (44%)
  starting transfers between devices  22.9 us (24%)
  waiting for transfers between devices  21.8 us (23%)
  local copies, waits for them, and re-layouts  7.23 us (8%)
    all_to_all x3, starting transfers between devices, spread(): lax.all_to_all(fast, ('xb', 'yb'), split_axis=0, concat_axis=0, tiled=True)  18.9 us
    ppermute x8, waiting for transfers between devices, shifted(): return lax.ppermute(value, axis, pairs)  13.4 us
    pallas_call x2, Pallas kernels, body(): call(functools.partial(update_and_leaving if passing else update, step),...  9.15 us
    all_to_all x3, waiting for transfers between devices, spread(): lax.all_to_all(fast, ('xb', 'yb'), split_axis=0, concat_axis=0, tiled=True)  8.5 us
    unnamed x36, local copies, waits for them, and re-layouts  7.23 us
    pallas_call x1, Pallas kernels, body(): call(rates_and_splitting, (shape,) + piece_shapes, (hbm(),) * 3, [smem()]...  5.31 us
    pallas_call x1, Pallas kernels, body(): call(rates_and_leaving, (shape, piece_shapes[0]), (hbm(),) * 2, [smem()]...  5.27 us
    pallas_call x1, Pallas kernels, body(): call(rates_after, shape, hbm(), [smem()] + [hbm()] * 3, 16 << 20, scratch)  5.25 us
  transfers between devices with their start and end apart: 11, of which 8 were waited for; matrix products, arithmetic and copies ran while one was open for 0% of the time, Pallas kernels for 35%

profile of v33, /device:TPU:0, one launch (start us, length us, event | category | flops | bytes accessed | tf_op | source)
XLA Modules:
  0.0 93.7 jit_solution(6865402481461539811)
XLA Ops:
  0.0 2.7 %shard_map.64 = (f32[128,384]{1,0:T(8,128)}, f32[8,256]{1,0:T(8,128)}, s32[24]{0:T(128)}) custom-call(f32[2,3,256,256]{3,2,1,0:T(8,128)} %state_first.3, f32[2,256,256]{2,1,0:T(8,128)} %bed_in.9, s32[4,32]{1,0:T(4,128)} %bitcast.17, s32[3,32]{1,0:T(4,128)} %wet_in.1, s32[3,16]{1,0:T(4,128)} %moves_in.1), custom_call_target="tpu_custom_call" | custom-call | flops 4194304 | bytes 4194304 | tf_op jit(solution)/shard_map/pallas_call | solution.py:888
  2.7 7.4 %all-to-all-start = ((f32[16,8,384]{2,1,0:T(8,128)}), f32[16,8,384]{2,1,0:T(8,128)S(1)}, u32[]{:S(2)}, u32[]{:S(2)}) async-start(f32[16,8,384]{2,1,0:T(8,128)} %bitcast.14), calls=%async_computation | async-start | bytes 393216 | tf_op jit(solution)/shard_map/all_to_all | solution.py:869
  10.1 5.3 %shard_map.65 = (f32[2,3,256,256]{3,2,1,0:T(8,128)}, f32[5,64,256]{2,1,0:T(8,128)}, f32[5,64,256]{2,1,0:T(8,128)}) custom-call(s32[24]{0:T(128)} %get-tuple-element.31.ctl, f32[2,3,256,256]{3,2,1,0:T(8,128)} %state_first.3, f32[2,256,256]{2,1,0:T(8,128)} %bed_in.9, f32[2,256,256]{2,1,0:T(8,128)} %manning.1), custom_call_target="tpu_custom_call" | custom-call | flops 16777216 | bytes 4194304 | tf_op jit(solution)/shard_map/pallas_call | solution.py:932
  15.4 3.7 %all-to-all-done = f32[16,8,384]{2,1,0:T(8,128)S(1)} async-done(((f32[16,8,384]{2,1,0:T(8,128)}), f32[16,8,384]{2,1,0:T(8,128)S(1)}, u32[]{:S(2)}, u32[]{:S(2)}) %all-to-all-start) | async-done | bytes 196640 | tf_op jit(solution)/shard_map/all_to_all | solution.py:869
  19.1 0.7 copy-done.15
  19.8 4.6 %shard_map.66 = (f32[2,3,256,256]{3,2,1,0:T(8,128)}, f32[128,256]{1,0:T(8,128)}, f32[8,256]{1,0:T(8,128)}, f32[8,256]{1,0:T(8,128)}) custom-call(s32[24]{0:T(128)} %get-tuple-element.31.ctl, f32[128,384]{1,0:T(8,128)} %bitcast.8, f32[128,384]{1,0:T(8,128)} %bitcast.9, f32[8,256]{1,0:T(8,128)} %get-tuple-element.33.columns_in, ...), custom_call_target="tpu_custom_call" | custom-call | flops 8388608 | bytes 10485760 | tf_op jit(solution)/shard_map/pallas_call | solution.py:963
  24.9 6.1 %all-to-all-start.1 = ((f32[16,8,256]{2,1,0:T(8,128)}), f32[16,8,256]{2,1,0:T(8,128)S(1)}, u32[]{:S(2)}, u32[]{:S(2)}) async-start(f32[16,8,256]{2,1,0:T(8,128)} %bitcast.15), calls=%async_computation.1 | async-start | bytes 262144 | tf_op jit(solution)/shard_map/all_to_all | solution.py:869
  31.1 2.2 %collective-permute-done.arrived.low = f32[5,64,256]{2,1,0:T(8,128)S(1)} collective-permute-done((f32[5,64,256]{2,1,0:T(8,128)}, f32[5,64,256]{2,1,0:T(8,128)S(1)}, u32[]{:S(2)}, u32[]{:S(2)}) %collective-permute-start) | collective-permute-done | bytes 327712 | tf_op jit(solution)/shard_map/ppermute | solution.py:40
  33.3 0.7 copy-done
  34.0 5.3 %shard_map.68 = (f32[2,3,256,256]{3,2,1,0:T(8,128)}, f32[5,64,256]{2,1,0:T(8,128)}) custom-call(s32[24]{0:T(128)} %get-tuple-element.31.ctl, f32[2,3,256,256]{3,2,1,0:T(8,128)} %get-tuple-element.37.state_in, f32[2,256,256]{2,1,0:T(8,128)} %bed_in.9, f32[2,3,256,256]{3,2,1,0:T(8,128)} %state_first.3, f32[2,256,256]{2,1,0:T(8,128)} %manning.1, ...), custom_call_target="tpu_custom_call" | custom-call | flops 16777216 | bytes 4194304 | tf_op jit(solution)/shard_map/pallas_call | solution.py:918
  39.4 2.0 %all-to-all-done.1 = f32[16,8,256]{2,1,0:T(8,128)S(1)} async-done(((f32[16,8,256]{2,1,0:T(8,128)}), f32[16,8,256]{2,1,0:T(8,128)S(1)}, u32[]{:S(2)}, u32[]{:S(2)}) %all-to-all-start.1) | async-done | bytes 131104 | tf_op jit(solution)/shard_map/all_to_all | solution.py:869
  42.1 4.6 %shard_map.70 = (f32[2,3,256,256]{3,2,1,0:T(8,128)}, f32[128,256]{1,0:T(8,128)}, f32[8,256]{1,0:T(8,128)}, f32[8,256]{1,0:T(8,128)}, f32[5,64,256]{2,1,0:T(8,128)}) custom-call(s32[24]{0:T(128)} %get-tuple-element.31.ctl, f32[128,256]{1,0:T(8,128)} %bitcast.12, f32[128,384]{1,0:T(8,128)} %bitcast.10, f32[8,256]{1,0:T(8,128)} %get-tuple-element.36.columns_in, ...), custom_call_target="tpu_custom_call" | custom-call | flops 8388608 | bytes 10485760 | tf_op jit(solution)/shard_map/pallas_call | solution.py:963
  46.7 0.8 collective-permute-start.3
  47.5 5.4 %all-to-all-start.2 = ((f32[16,8,256]{2,1,0:T(8,128)}), f32[16,8,256]{2,1,0:T(8,128)S(1)}, u32[]{:S(2)}, u32[]{:S(2)}) async-start(f32[16,8,256]{2,1,0:T(8,128)} %bitcast.16), calls=%async_computation.2 | async-start | bytes 262144 | tf_op jit(solution)/shard_map/all_to_all | solution.py:869
  52.9 0.7 copy-done.4
  53.6 5.3 %shard_map.71.rate = f32[2,3,256,256]{3,2,1,0:T(8,128)} custom-call(s32[24]{0:T(128)} %get-tuple-element.31.ctl, f32[2,3,256,256]{3,2,1,0:T(8,128)} %get-tuple-element.44.state_in.state, f32[2,256,256]{2,1,0:T(8,128)} %bed_in.9, f32[5,64,256]{2,1,0:T(8,128)} %copy-done.4), custom_call_target="tpu_custom_call" | custom-call | flops 16777216 | bytes 4194304 | tf_op jit(solution)/shard_map/pallas_call | solution.py:928
  58.9 2.8 %all-to-all-done.2 = f32[16,8,256]{2,1,0:T(8,128)S(1)} async-done(((f32[16,8,256]{2,1,0:T(8,128)}), f32[16,8,256]{2,1,0:T(8,128)S(1)}, u32[]{:S(2)}, u32[]{:S(2)}) %all-to-all-start.2) | async-done | bytes 131104 | tf_op jit(solution)/shard_map/all_to_all | solution.py:869
  62.5 4.5 %shard_map.72 = (f32[3,256,256]{2,1,0:T(8,128)}, f32[3,72,256]{2,1,0:T(8,128)}, f32[3,72,256]{2,1,0:T(8,128)}, f32[3,72,256]{2,1,0:T(8,128)}, f32[3,72,256]{2,1,0:T(8,128)}, /*index=5*/f32[8,256]{1,0:T(8,128)}) custom-call(s32[24]{0:T(128)} %get-tuple-element.31.ctl, f32[128,256]{1,0:T(8,128)} %bitcast.13, f32[128,384]{1,0:T(8,128)} %bitcast.11, ...), custom_call_target="tpu_custom_call" | custom-call | flops 8388608 | bytes 10485760 | tf_op jit(solution)/shard_map/pallas_call | solution.py:982
  67.0 0.8 collective-permute-start.6
  67.8 1.6 %collective-permute-start.4 = (f32[3,72,256]{2,1,0:T(8,128)}, f32[3,72,256]{2,1,0:T(8,128)S(1)}, u32[]{:S(2)}, u32[]{:S(2)}) collective-permute-start(f32[3,72,256]{2,1,0:T(8,128)} %get-tuple-element.47), channel_id=1, source_target_pairs={{0,2},{2,4},{4,6},{6,8},{8,10},{10,12},{12,14},{14,0},{1,3},{3,5},... | collective-permute-start | bytes 663560 | tf_op jit(solution)/shard_map/ppermute | solution.py:40
  69.5 1.0 %copy-done.7 = f32[5,64,256]{2,1,0:T(8,128)S(1)} copy-done((f32[5,64,256]{2,1,0:T(8,128)S(1)}, f32[5,64,256]{2,1,0:T(8,128)}, u32[]{:S(2)}) %copy-start.7) | copy-done | bytes 327704
  70.5 0.9 copy-done.9
  71.4 0.9 copy-done.10
  72.3 0.7 copy-done.14
  73.0 3.8 %shard_map.73 = (f32[3,128,256]{2,1,0:T(8,128)S(1)}, f32[3,72,256]{2,1,0:T(8,128)S(1)}, f32[3,72,256]{2,1,0:T(8,128)S(1)}) custom-call(s32[24]{0:T(128)S(1)} %copy-done.12, f32[8,256]{1,0:T(8,128)S(1)} %copy-done.11, f32[8,256]{1,0:T(8,128)S(1)} %copy-done.13, f32[8,256]{1,0:T(8,128)S(1)} %copy-done.14, f32[5,64,256]{2,1,0:T(8,128)S(1)} %copy-done.5, ...), custom_call_target="tpu_custom_call" | custom-call | flops 8388608 | bytes 4194304 | tf_op jit(solution)/shard_map/pallas_call | solution.py:995
  76.9 1.4 %collective-permute-done.6.arrived.late_in = f32[3,72,256]{2,1,0:T(8,128)S(1)} collective-permute-done((f32[3,72,256]{2,1,0:T(8,128)}, f32[3,72,256]{2,1,0:T(8,128)S(1)}, u32[]{:S(2)}, u32[]{:S(2)}) %collective-permute-start.6) | collective-permute-done | bytes 221216 | tf_op jit(solution)/shard_map/ppermute | solution.py:40
  78.9 3.3 %collective-permute-done.4.arrived.rest_in = f32[3,72,256]{2,1,0:T(8,128)S(1)} collective-permute-done((f32[3,72,256]{2,1,0:T(8,128)}, f32[3,72,256]{2,1,0:T(8,128)S(1)}, u32[]{:S(2)}, u32[]{:S(2)}) %collective-permute-start.4) | collective-permute-done | bytes 221216 | tf_op jit(solution)/shard_map/ppermute | solution.py:40
  82.8 1.5 %shard_map.76.before = f32[2,3,256,256]{3,2,1,0:T(8,128)} custom-call(s32[24]{0:T(128)S(1)} %copy-done.12, f32[8,256]{1,0:T(8,128)S(1)} %copy-done.11, f32[8,256]{1,0:T(8,128)S(1)} %copy-done.13, f32[8,256]{1,0:T(8,128)S(1)} %copy-done.14, f32[5,64,256]{2,1,0:T(8,128)S(1)} %copy-done.1, f32[5,64,256]{2,1,0:T(8,128)S(1)} %copy-done.3, ...), custom_call_target="tpu_custom_call" | custom-call | flops 8388608 | bytes 4194304 | tf_op jit(solution)/shard_map/pallas_call | solution.py:1018
  84.4 3.2 %collective-permute-done.7.late = f32[3,72,256]{2,1,0:T(8,128)S(1)} collective-permute-done((f32[3,72,256]{2,1,0:T(8,128)S(1)}, f32[3,72,256]{2,1,0:T(8,128)S(1)}, u32[]{:S(2)}, u32[]{:S(2)}) %collective-permute-start.7) | collective-permute-done | bytes 221216 | tf_op jit(solution)/shard_map/ppermute | solution.py:40
  87.6 1.4 %shard_map.77.before = f32[2,3,256,256]{3,2,1,0:T(8,128)} custom-call(s32[24]{0:T(128)S(1)} %copy-done.12, f32[3,72,256]{2,1,0:T(8,128)S(1)} %collective-permute-done.7.late, f32[3,128,256]{2,1,0:T(8,128)S(1)} %get-tuple-element.53.order.early, f32[2,3,256,256]{3,2,1,0:T(8,128)} %shard_map.76.before), custom_call_target="tpu_custom_call", output_to_operand_aliasing={{}: (3, {})} | custom-call | flops 1048576 | bytes 4194304 | tf_op jit(solution)/shard_map/pallas_call | solution.py:1034
  89.1 3.2 %collective-permute-done.5.rest = f32[3,72,256]{2,1,0:T(8,128)S(1)} collective-permute-done((f32[3,72,256]{2,1,0:T(8,128)S(1)}, f32[3,72,256]{2,1,0:T(8,128)S(1)}, u32[]{:S(2)}, u32[]{:S(2)}) %collective-permute-start.5) | collective-permute-done | bytes 221216 | tf_op jit(solution)/shard_map/ppermute | solution.py:40
  92.3 1.2 %shard_map.78 = f32[2,3,256,256]{3,2,1,0:T(8,128)} custom-call(s32[24]{0:T(128)S(1)} %copy-done.12, f32[3,72,256]{2,1,0:T(8,128)S(1)} %collective-permute-done.5.rest, f32[2,3,256,256]{3,2,1,0:T(8,128)} %shard_map.77.before), custom_call_target="tpu_custom_call", output_to_operand_aliasing={{}: (2, {})} | custom-call | flops 1048576 | bytes 4194304 | tf_op jit(solution)/shard_map/pallas_call | solution.py:1044
  (41 shorter events, 3.5 us)
Async XLA Ops:
  2.7 16.4 %all-to-all-start = ((f32[16,8,384]{2,1,0:T(8,128)}), f32[16,8,384]{2,1,0:T(8,128)S(1)}, u32[]{:S(2)}, u32[]{:S(2)}) async-start(f32[16,8,384]{2,1,0:T(8,128)} %bitcast.14), calls=%async_computation | async-start | bytes 393216 | tf_op jit(solution)/shard_map/all_to_all | solution.py:869
  19.1 0.7 copy-start.15
  19.8 13.5 %collective-permute-start = (f32[5,64,256]{2,1,0:T(8,128)}, f32[5,64,256]{2,1,0:T(8,128)S(1)}, u32[]{:S(2)}, u32[]{:S(2)}) collective-permute-start(f32[5,64,256]{2,1,0:T(8,128)} %shard_map.67), channel_id=1, source_target_pairs={{0,2},{2,4},{4,6},{6,8},{8,10},{10,12},{12,14},{14,0},{1,3},{3,5},... | collective-permute-start | bytes 983048 | tf_op jit(solution)/shard_map/ppermute | solution.py:40
  24.4 17.0 %collective-permute-start.1 = (f32[5,64,256]{2,1,0:T(8,128)}, f32[5,64,256]{2,1,0:T(8,128)S(1)}, u32[]{:S(2)}, u32[]{:S(2)}) collective-permute-start(f32[5,64,256]{2,1,0:T(8,128)} %shard_map.69), channel_id=1, source_target_pairs={{0,2},{2,4},{4,6},{6,8},{8,10},{10,12},{12,14},{14,0},{1,3},{3,5},... | collective-permute-start | bytes 983048 | tf_op jit(solution)/shard_map/ppermute | solution.py:40
  24.9 16.4 %all-to-all-start.1 = ((f32[16,8,256]{2,1,0:T(8,128)}), f32[16,8,256]{2,1,0:T(8,128)S(1)}, u32[]{:S(2)}, u32[]{:S(2)}) async-start(f32[16,8,256]{2,1,0:T(8,128)} %bitcast.15), calls=%async_computation.1 | async-start | bytes 262144 | tf_op jit(solution)/shard_map/all_to_all | solution.py:869
  33.3 0.7 copy-start
  39.3 13.6 %collective-permute-start.2 = (f32[5,64,256]{2,1,0:T(8,128)}, f32[5,64,256]{2,1,0:T(8,128)S(1)}, u32[]{:S(2)}, u32[]{:S(2)}) collective-permute-start(f32[5,64,256]{2,1,0:T(8,128)} %get-tuple-element.45), channel_id=1, source_target_pairs={{0,2},{2,4},{4,6},{6,8},{8,10},{10,12},{12,14},{14,0},{1,3},{3,5},... | collective-permute-start | bytes 983048 | tf_op jit(solution)/shard_map/ppermute | solution.py:40
  41.4 0.7 copy-start.16
  41.4 0.8 copy-start.2
  46.7 15.0 %collective-permute-start.3 = (f32[5,64,256]{2,1,0:T(8,128)}, f32[5,64,256]{2,1,0:T(8,128)S(1)}, u32[]{:S(2)}, u32[]{:S(2)}) collective-permute-start(f32[5,64,256]{2,1,0:T(8,128)} %get-tuple-element.46), channel_id=1, source_target_pairs={{0,2},{2,4},{4,6},{6,8},{8,10},{10,12},{12,14},{14,0},{1,3},{3,5},... | collective-permute-start | bytes 983048 | tf_op jit(solution)/shard_map/ppermute | solution.py:40
  47.5 14.2 %all-to-all-start.2 = ((f32[16,8,256]{2,1,0:T(8,128)}), f32[16,8,256]{2,1,0:T(8,128)S(1)}, u32[]{:S(2)}, u32[]{:S(2)}) async-start(f32[16,8,256]{2,1,0:T(8,128)} %bitcast.16), calls=%async_computation.2 | async-start | bytes 262144 | tf_op jit(solution)/shard_map/all_to_all | solution.py:869
  52.9 0.7 copy-start.4
  61.7 0.6 copy-start.17
  61.7 0.8 copy-start.6
  62.5 7.0 %copy-start.5 = (f32[5,64,256]{2,1,0:T(8,128)S(1)}, f32[5,64,256]{2,1,0:T(8,128)}, u32[]{:S(2)}) copy-start(f32[5,64,256]{2,1,0:T(8,128)} %copy-done.4) | copy-start | bytes 983044
  62.5 7.0 %copy-start.11 = (f32[8,256]{1,0:T(8,128)S(1)}, f32[8,256]{1,0:T(8,128)}, u32[]{:S(2)}) copy-start(f32[8,256]{1,0:T(8,128)} %get-tuple-element.40.first.second.delta0) | copy-start | bytes 24580
  62.5 7.0 %copy-start.12 = (s32[24]{0:T(128)S(1)}, s32[24]{0:T(128)}, u32[]{:S(2)}) copy-start(s32[24]{0:T(128)} %get-tuple-element.31.ctl) | copy-start | bytes 292
  62.5 7.0 %copy-start.13 = (f32[8,256]{1,0:T(8,128)S(1)}, f32[8,256]{1,0:T(8,128)}, u32[]{:S(2)}) copy-start(f32[8,256]{1,0:T(8,128)} %get-tuple-element.48.delta1) | copy-start | bytes 24580
  67.0 11.2 %collective-permute-start.6 = (f32[3,72,256]{2,1,0:T(8,128)}, f32[3,72,256]{2,1,0:T(8,128)S(1)}, u32[]{:S(2)}, u32[]{:S(2)}) collective-permute-start(f32[3,72,256]{2,1,0:T(8,128)} %get-tuple-element.54), channel_id=1, source_target_pairs={{0,2},{2,4},{4,6},{6,8},{8,10},{10,12},{12,14},{14,0},{1,3},{3,5},... | collective-permute-start | bytes 663560 | tf_op jit(solution)/shard_map/ppermute | solution.py:40
  67.8 14.3 %collective-permute-start.4 = (f32[3,72,256]{2,1,0:T(8,128)}, f32[3,72,256]{2,1,0:T(8,128)S(1)}, u32[]{:S(2)}, u32[]{:S(2)}) collective-permute-start(f32[3,72,256]{2,1,0:T(8,128)} %get-tuple-element.47), channel_id=1, source_target_pairs={{0,2},{2,4},{4,6},{6,8},{8,10},{10,12},{12,14},{14,0},{1,3},{3,5},... | collective-permute-start | bytes 663560 | tf_op jit(solution)/shard_map/ppermute | solution.py:40
  69.5 1.0 %copy-start.7 = (f32[5,64,256]{2,1,0:T(8,128)S(1)}, f32[5,64,256]{2,1,0:T(8,128)}, u32[]{:S(2)}) copy-start(f32[5,64,256]{2,1,0:T(8,128)} %copy-done.6) | copy-start | bytes 983044
  70.5 0.9 copy-start.9
  71.4 0.9 copy-start.10
  72.3 0.7 copy-start.14
  73.0 9.8 %copy-start.1 = (f32[5,64,256]{2,1,0:T(8,128)S(1)}, f32[5,64,256]{2,1,0:T(8,128)}, u32[]{:S(2)}) copy-start(f32[5,64,256]{2,1,0:T(8,128)} %copy-done) | copy-start | bytes 983044
  73.0 9.8 %copy-start.3 = (f32[5,64,256]{2,1,0:T(8,128)S(1)}, f32[5,64,256]{2,1,0:T(8,128)}, u32[]{:S(2)}) copy-start(f32[5,64,256]{2,1,0:T(8,128)} %copy-done.2) | copy-start | bytes 983044
  73.0 9.8 %copy-start.8 = (f32[3,256,256]{2,1,0:T(8,128)S(1)}, f32[3,256,256]{2,1,0:T(8,128)}, u32[]{:S(2)}) copy-start(f32[3,256,256]{2,1,0:T(8,128)} %get-tuple-element.56.staying) | copy-start | bytes 2359300
  78.8 8.8 %collective-permute-start.7 = (f32[3,72,256]{2,1,0:T(8,128)S(1)}, f32[3,72,256]{2,1,0:T(8,128)S(1)}, u32[]{:S(2)}, u32[]{:S(2)}) collective-permute-start(f32[3,72,256]{2,1,0:T(8,128)S(1)} %shard_map.75), channel_id=1, source_target_pairs={{0,2},{2,4},{4,6},{6,8},{8,10},{10,12},{12,14},{14,0},{1,3},{3,5},... | collective-permute-start | bytes 663560 | tf_op jit(solution)/shard_map/ppermute | solution.py:40
  82.7 9.5 %collective-permute-start.5 = (f32[3,72,256]{2,1,0:T(8,128)S(1)}, f32[3,72,256]{2,1,0:T(8,128)S(1)}, u32[]{:S(2)}, u32[]{:S(2)}) collective-permute-start(f32[3,72,256]{2,1,0:T(8,128)S(1)} %shard_map.74), channel_id=1, source_target_pairs={{0,2},{2,4},{4,6},{6,8},{8,10},{10,12},{12,14},{14,0},{1,3},{3,5},... | collective-permute-start | bytes 663560 | tf_op jit(solution)/shard_map/ppermute | solution.py:40
